TPU v7x, 32 devices: a whole 2x2x4 slice. The times are simulated.
32 devices in a mesh: rows: 8 (over y, x, core), rep: 4 (over z).
Axes of the slice: x: 2, y: 2, z: 4, core: 2. Of those that a mesh axis runs over, the one named last changes fastest.
Arguments:
- node_feats: bfloat16 [8192, 256], P('rows'), may hold values from -6 to 6
- weight: bfloat16 [256, 256], replicated, may hold values from -0.375 to 0.375
- cotangent: bfloat16 [8192, 256], P('rows'), may hold values from -6 to 6
- tile_values: bfloat16 [8, 5, 32, 128, 128], P('rows', None, 'rep'), may hold values from -1 to 1, as said below
- tile_coords: int32 [2, 8, 5, 32], P(None, 'rows', None, 'rep'), may hold values from 0 to 7, as said below
- tile_counts: int32 [8, 5], P('rows'), may hold values from 0 to 32, as said below
Outputs:
- activated: bfloat16 [8192, 256], P('rows')
- input_grad: bfloat16 [8192, 256], P('rows')
- weight_grad: float32 [256, 256], replicated
Inputs may be any that keep to these rules, and one draw needn't show every extreme that they name: tile_counts[r, d] = tile_counts[(r + d - 2) mod 8, 4 - d]; tile_counts[r, 2] = 32. tile_coords[0, r, d, k] = tile_coords[1, s, 4 - d, k] and tile_coords[1, r, d, k] = tile_coords[0, s, 4 - d, k] with s = (r + d - 2) mod 8, for d other than 2; for d = 2, slots 2m and 2m + 1 hold swapped coordinates. tile_values[r, d, k] is the transpose of tile_values[s, 4 - d, k] with s as above for d other than 2; for d = 2, slot 2m + 1 is the transpose of slot 2m.
All inputs are finite; a program needn't handle non-finite values.
Results may differ from a plain program's by a relative error of at most 0.006.
Values may be sent and summed in bfloat16 or wider, within the bound.
No kernel may reach another device: no remote copies, remote signals or barrier semaphores. Data moves between devices by JAX's collectives and lax.ppermute only.
A program may use at most 64 MiB of HBM per device.

v0:
```python
import jax
import jax.numpy as jnp
from jax import lax
from jax.sharding import PartitionSpec as P


def extended_2(block, sides, width):
    for axis, dim in sides:
        count = lax.axis_size(axis)
        forward = [(i, i + 1) for i in range(count - 1)]
        forward.append((count - 1, 0))
        backward = [(target, source) for source, target in forward]
        low = lax.ppermute(
            lax.slice_in_dim(block, block.shape[dim] - width, None, axis=dim), axis, forward
        )
        high = lax.ppermute(lax.slice_in_dim(block, 0, width, axis=dim), axis, backward)
        block = jnp.concatenate([low, block, high], axis=dim)
    return block


def silu_slope(value):
    sig = jax.nn.sigmoid(value)
    return sig * (1.0 + value * (1.0 - sig))


def offset_terms(panel, values, rows_idx, cols_idx, live):
    blocks = panel.shape[0]
    picked = panel[cols_idx]
    product = jnp.einsum("kuv,kvf->kuf", values, picked, preferred_element_type=jnp.float32)
    place = (
        (rows_idx[:, None] == jnp.arange(blocks, dtype=jnp.int32)[None, :]) & live[:, None]
    ).astype(jnp.float32)
    return jnp.einsum("kb,kuf->buf", place, product, precision=lax.Precision.HIGHEST)


def widen_margin(pair):
    return extended_2(pair, (("rows", 0),), pair.shape[0] // 2)


def propagate(source, values, rows_idx, cols_idx, counts):
    reach = values.shape[0]
    slots_dev = values.shape[1]
    tile = values.shape[-1]
    hops = reach // 2
    local_rows = source.shape[0]
    width = source.shape[1]
    blocks = local_rows // tile
    first_slot = lax.axis_index("rep") * slots_dev
    live = (first_slot + jnp.arange(slots_dev, dtype=jnp.int32))[None, :] < counts[:, None]
    total = jnp.zeros((blocks, tile, width), jnp.float32)
    before = source
    after = source
    lower_panels = []
    upper_panels = []
    for level in range(hops):
        extended = widen_margin(jnp.concatenate([after, before], axis=0))
        before = extended[:local_rows]
        after = extended[3 * local_rows :]
        lower_panels.append(before)
        upper_panels.append(after)
    ordered = lower_panels[::-1] + [source] + upper_panels
    for step in range(reach):
        total = total + offset_terms(
            ordered[step].reshape(blocks, tile, width),
            values[step],
            rows_idx[step],
            cols_idx[step],
            live[step],
        )
    return total.reshape(local_rows, width)


def per_device(node_feats, weight, cotangent, tile_values, tile_coords, tile_counts):
    values = tile_values[0]
    rows_idx = tile_coords[0, 0]
    cols_idx = tile_coords[1, 0]
    counts = tile_counts[0]
    scale = (node_feats.shape[0] * lax.axis_size("rows")) ** (-0.5)
    contract = (((0,), (0,)), ((), ()))
    transformed = jnp.dot(node_feats, weight, preferred_element_type=jnp.float32).astype(
        jnp.bfloat16
    )
    agg_part = propagate(transformed, values, rows_idx, cols_idx, counts)
    aggregated = lax.psum(agg_part, "rep")
    activated = jax.nn.silu(aggregated).astype(jnp.bfloat16)
    adjoint = (cotangent.astype(jnp.float32) * silu_slope(aggregated)).astype(jnp.bfloat16)
    back_part = propagate(adjoint, values, rows_idx, cols_idx, counts)
    back_sum = lax.psum(back_part, "rep").astype(jnp.bfloat16)
    grad_terms = (
        lax.dot_general(node_feats, back_sum, contract, preferred_element_type=jnp.float32) * scale
    )
    weight_grad = lax.psum(grad_terms, "rows")
    input_grad = jnp.dot(back_sum, weight.T, preferred_element_type=jnp.float32).astype(
        jnp.bfloat16
    )
    return (activated, input_grad, weight_grad)


def solution(mesh):
    return jax.shard_map(
        per_device,
        mesh=mesh,
        in_specs=(
            P("rows", None),
            P(),
            P("rows", None),
            P("rows", None, "rep", None, None),
            P(None, "rows", None, "rep"),
            P("rows", None),
        ),
        out_specs=(P("rows", None), P("rows", None), P()),
        check_vma=False,
    )
```

profile of v0, /device:TPU:1, one launch (start us, length us, event | category | flops | bytes accessed | tf_op | source)
XLA Modules:
  0.0 253.9 jit_solution(16300250117851149329)
XLA Ops:
  7.2 1.0 copy-done
  8.2 2.0 convolution_convert_fusion.1
  10.2 2.6 %collective-permute-start = (bf16[1024,256]{1,0:T(8,128)(2,1)}, bf16[1024,256]{1,0:T(8,128)(2,1)}, u32[]{:S(2)}, u32[]{:S(2)}) collective-permute-start(bf16[1024,256]{1,0:T(8,128)(2,1)} %convolution_convert_fusion.1), channel_id=1, source_target_pairs={{0,4},{4,8},{8,12},{12,16},{16,20},{20,24},{24,28},{28,0},{1,5},{5... | collective-permute-start | bytes 1572872 | tf_op jit(solution)/shard_map/ppermute | solution.py:13
  12.8 0.7 fusion.89
  13.5 0.7 slice_bitcast_fusion.5
  14.3 1.6 gather_fusion.2
  16.4 1.4 copy.15
  17.8 6.1 %collective-permute-done = bf16[1024,256]{1,0:T(8,128)(2,1)} collective-permute-done((bf16[1024,256]{1,0:T(8,128)(2,1)}, bf16[1024,256]{1,0:T(8,128)(2,1)}, u32[]{:S(2)}, u32[]{:S(2)}) %collective-permute-start) | collective-permute-done | bytes 524320 | tf_op jit(solution)/shard_map/ppermute | solution.py:13
  23.9 1.6 gather_fusion.1
  25.5 2.5 collective-permute-start.1
  28.4 1.4 copy.14
  29.8 1.6 gather_fusion.3
  31.8 1.4 copy.16
  33.2 3.2 %collective-permute-done.1 = bf16[1024,256]{1,0:T(8,128)(2,1)} collective-permute-done((bf16[1024,256]{1,0:T(8,128)(2,1)}, bf16[1024,256]{1,0:T(8,128)(2,1)}, u32[]{:S(2)}, u32[]{:S(2)}) %collective-permute-start.1) | collective-permute-done | bytes 524320 | tf_op jit(solution)/shard_map/ppermute | solution.py:13
  36.5 1.6 gather_fusion
  38.4 1.4 copy.13
  39.8 3.0 %collective-permute-done.3 = bf16[1024,256]{1,0:T(8,128)(2,1)} collective-permute-done((bf16[1024,256]{1,0:T(8,128)(2,1)}, bf16[1024,256]{1,0:T(8,128)(2,1)}, u32[]{:S(2)}, u32[]{:S(2)}) %collective-permute-start.3) | collective-permute-done | bytes 524320 | tf_op jit(solution)/shard_map/ppermute | solution.py:16
  42.8 1.6 gather_fusion.4
  44.8 1.4 copy.17
  46.2 1.9 fusion.11
  49.9 0.6 copy-done.7
  51.2 0.6 copy-done.9
  52.4 1.3 copy.10
  53.8 53.4 %all-reduce.4.cloned.1.call-done = f32[1024,256]{1,0:T(8,128)} async-done(((f32[1024,256]{1,0:T(8,128)}), f32[1024,256]{1,0:T(8,128)}) %all-reduce.4.cloned.1.call-update) | async-done | bytes 1048592 | tf_op jit(solution)/shard_map/psum | solution.py:84
  107.2 2.5 multiply_convert_fusion
  109.6 1.5 collective-permute-start.4
  111.2 1.4 gather_fusion.7
  112.5 1.4 fusion.21
  113.9 1.4 copy.20
  115.3 5.7 %collective-permute-done.4 = bf16[1024,256]{1,0:T(8,128)(2,1)} collective-permute-done((bf16[1024,256]{1,0:T(8,128)(2,1)S(1)}, bf16[1024,256]{1,0:T(8,128)(2,1)}, u32[]{:S(2)}, u32[]{:S(2)}) %collective-permute-start.4) | collective-permute-done | bytes 524320 | tf_op jit(solution)/shard_map/ppermute | solution.py:13
  121.1 2.4 gather_fusion.6
  123.5 2.6 %collective-permute-start.5 = (bf16[1024,256]{1,0:T(8,128)(2,1)}, bf16[1024,256]{1,0:T(8,128)(2,1)}, u32[]{:S(2)}, u32[]{:S(2)}) collective-permute-start(bf16[1024,256]{1,0:T(8,128)(2,1)} %collective-permute-done.4), channel_id=1, source_target_pairs={{0,4},{4,8},{8,12},{12,16},{16,20},{20,24},{24,28},{28,0},{1,5},{5... | collective-permute-start | bytes 1572872 | tf_op jit(solution)/shard_map/ppermute | solution.py:13
  126.1 1.4 fusion.25
  127.5 1.4 copy.19
  128.9 1.6 gather_fusion.8
  130.9 1.4 copy.21
  132.5 1.6 gather_fusion.5
  134.5 1.4 copy.18
  135.9 2.8 %fusion.5 = f32[8,128,256]{2,0,1:T(8,128)} fusion(f32[8,256,128]{1,0,2:T(8,128)} %copy.18, s32[8]{0:T(128)S(1)} %get-tuple-element.15, pred[8]{0:T(512)(128)(4,1)S(1)} %get-tuple-element.25), kind=kOutput, calls=%fused_computation.26 | convolution fusion | flops 25165952 | bytes 2097192 | tf_op jit(solution)/shard_map/kb,kuf->buf/dot_general | solution.py:33
  138.7 3.0 %collective-permute-done.7 = bf16[1024,256]{1,0:T(8,128)(2,1)} collective-permute-done((bf16[1024,256]{1,0:T(8,128)(2,1)}, bf16[1024,256]{1,0:T(8,128)(2,1)}, u32[]{:S(2)}, u32[]{:S(2)}) %collective-permute-start.7) | collective-permute-done | bytes 524320 | tf_op jit(solution)/shard_map/ppermute | solution.py:16
  141.7 1.6 gather_fusion.9
  143.7 1.4 copy.22
  145.1 1.9 convolution_add_fusion.3
  150.4 40.0 %all-reduce.7 = bf16[1024,256]{1,0:T(8,128)(2,1)S(1)} all-reduce(f32[1024,256]{1,0:T(8,128)S(1)} %bitcast.147), channel_id=1, replica_groups=mesh['rows'=8,'rep'=4] {'rep'}, use_global_device_ids=true, to_apply=%region_1.2 | all-reduce | flops 262144 | bytes 1572864 | tf_op jit(solution)/shard_map/psum | solution.py:88
  190.4 1.0 fusion
  191.5 1.1 convolution_convert_fusion
  192.6 52.7 %all-reduce.6.cloned.1.call-done = f32[256,256]{0,1:T(8,128)} async-done(((f32[256,256]{0,1:T(8,128)}), f32[256,256]{0,1:T(8,128)}) %all-reduce.6.cloned.1.call-update) | async-done | bytes 262160 | tf_op jit(solution)/shard_map/psum | solution.py:92
  245.3 1.8 copy.12
  (58 shorter events, 9.8 us)
Async XLA Ops:
  7.2 1.0 copy-start
  7.2 8.8 %copy-start.1 = (bf16[1,5,8,128,128]{4,3,2,1,0:T(8,128)(2,1)S(1)}, bf16[1,5,8,128,128]{4,3,2,1,0:T(8,128)(2,1)}, u32[]{:S(2)}) copy-start(bf16[1,5,8,128,128]{4,3,2,1,0:T(8,128)(2,1)} %param.9) | copy-start | bytes 3932164
  7.2 100.0 %all-reduce.4.cloned.1.call-start = ((), (), s32[]{:S(2)}) async-start(), calls=%async_computation | async-start | bytes 2097152 | tf_op jit(solution)/shard_map/psum | solution.py:84
  10.2 13.7 %collective-permute-start = (bf16[1024,256]{1,0:T(8,128)(2,1)}, bf16[1024,256]{1,0:T(8,128)(2,1)}, u32[]{:S(2)}, u32[]{:S(2)}) collective-permute-start(bf16[1024,256]{1,0:T(8,128)(2,1)} %convolution_convert_fusion.1), channel_id=1, source_target_pairs={{0,4},{4,8},{8,12},{12,16},{16,20},{20,24},{24,28},{28,0},{1,5},{5... | collective-permute-start | bytes 1572872 | tf_op jit(solution)/shard_map/ppermute | solution.py:13
  12.8 17.0 %collective-permute-start.2 = (bf16[1024,256]{1,0:T(8,128)(2,1)}, bf16[1024,256]{1,0:T(8,128)(2,1)}, u32[]{:S(2)}, u32[]{:S(2)}) collective-permute-start(bf16[1024,256]{1,0:T(8,128)(2,1)} %convolution_convert_fusion.1), channel_id=1, source_target_pairs={{4,0},{8,4},{12,8},{16,12},{20,16},{24,20},{28,24},{0,28},{5,1},{9... | collective-permute-start | bytes 1572872 | tf_op jit(solution)/shard_map/ppermute | solution.py:16
  14.3 2.0 copy-start.12
  25.5 10.9 %collective-permute-start.1 = (bf16[1024,256]{1,0:T(8,128)(2,1)}, bf16[1024,256]{1,0:T(8,128)(2,1)}, u32[]{:S(2)}, u32[]{:S(2)}) collective-permute-start(bf16[1024,256]{1,0:T(8,128)(2,1)} %collective-permute-done), channel_id=1, source_target_pairs={{0,4},{4,8},{8,12},{12,16},{16,20},{20,24},{24,28},{28,0},{1,5},{5... | collective-permute-start | bytes 1572872 | tf_op jit(solution)/shard_map/ppermute | solution.py:13
  31.4 11.4 %collective-permute-start.3 = (bf16[1024,256]{1,0:T(8,128)(2,1)}, bf16[1024,256]{1,0:T(8,128)(2,1)}, u32[]{:S(2)}, u32[]{:S(2)}) collective-permute-start(bf16[1024,256]{1,0:T(8,128)(2,1)} %collective-permute-done.2), channel_id=1, source_target_pairs={{4,0},{8,4},{12,8},{16,12},{20,16},{24,20},{28,24},{0,28},{5,1},{9... | collective-permute-start | bytes 1572872 | tf_op jit(solution)/shard_map/ppermute | solution.py:16
  46.2 1.9 copy-start.6
  48.1 1.2 copy-start.3
  49.3 1.2 copy-start.7
  50.6 1.2 copy-start.9
  52.4 54.8 %copy-start.10 = (bf16[1024,256]{1,0:T(8,128)(2,1)S(1)}, bf16[1024,256]{1,0:T(8,128)(2,1)}, u32[]{:S(2)}) copy-start(bf16[1024,256]{1,0:T(8,128)(2,1)} %param.8) | copy-start | bytes 1572868
  53.7 191.6 %all-reduce.6.cloned.1.call-start = ((), (), s32[]{:S(2)}) async-start(), calls=%async_computation.1 | async-start | bytes 524288 | tf_op jit(solution)/shard_map/psum | solution.py:92
  109.6 11.5 %collective-permute-start.4 = (bf16[1024,256]{1,0:T(8,128)(2,1)S(1)}, bf16[1024,256]{1,0:T(8,128)(2,1)}, u32[]{:S(2)}, u32[]{:S(2)}) collective-permute-start(bf16[1024,256]{1,0:T(8,128)(2,1)S(1)} %get-tuple-element.9), channel_id=1, source_target_pairs={{0,4},{4,8},{8,12},{12,16},{16,20},{20,24},{24,28},{28,0},{1,5},{5... | collective-permute-start | bytes 1572872 | tf_op jit(solution)/shard_map/ppermute | solution.py:13
  111.2 17.7 %collective-permute-start.6 = (bf16[1024,256]{1,0:T(8,128)(2,1)S(1)}, bf16[1024,256]{1,0:T(8,128)(2,1)}, u32[]{:S(2)}, u32[]{:S(2)}) collective-permute-start(bf16[1024,256]{1,0:T(8,128)(2,1)S(1)} %get-tuple-element.9), channel_id=1, source_target_pairs={{4,0},{8,4},{12,8},{16,12},{20,16},{24,20},{28,24},{0,28},{5,1},{9... | collective-permute-start | bytes 1572872 | tf_op jit(solution)/shard_map/ppermute | solution.py:16
  123.5 9.0 %collective-permute-start.5 = (bf16[1024,256]{1,0:T(8,128)(2,1)}, bf16[1024,256]{1,0:T(8,128)(2,1)}, u32[]{:S(2)}, u32[]{:S(2)}) collective-permute-start(bf16[1024,256]{1,0:T(8,128)(2,1)} %collective-permute-done.4), channel_id=1, source_target_pairs={{0,4},{4,8},{8,12},{12,16},{16,20},{20,24},{24,28},{28,0},{1,5},{5... | collective-permute-start | bytes 1572872 | tf_op jit(solution)/shard_map/ppermute | solution.py:13
  132.2 9.4 %collective-permute-start.7 = (bf16[1024,256]{1,0:T(8,128)(2,1)}, bf16[1024,256]{1,0:T(8,128)(2,1)}, u32[]{:S(2)}, u32[]{:S(2)}) collective-permute-start(bf16[1024,256]{1,0:T(8,128)(2,1)} %collective-permute-done.6), channel_id=1, source_target_pairs={{4,0},{8,4},{12,8},{16,12},{20,16},{24,20},{28,24},{0,28},{5,1},{9... | collective-permute-start | bytes 1572872 | tf_op jit(solution)/shard_map/ppermute | solution.py:16
  143.6 1.4 copy-start.4
  145.1 1.9 copy-start.2
  147.0 1.2 copy-start.5
  148.2 1.2 copy-start.8
  150.4 41.1 %copy-start.11 = (bf16[256,256]{1,0:T(8,128)(2,1)S(1)}, bf16[256,256]{1,0:T(8,128)(2,1)}, u32[]{:S(2)}) copy-start(bf16[256,256]{1,0:T(8,128)(2,1)} %param.7) | copy-start | bytes 393220
Sparse Core Ops, SparseCore 0:
  53.8 53.2 all-reduce.3
  191.6 53.6 all-reduce.5
where the time goes:
time: 256 us; the launch traced here: 254 us
  waiting for transfers between devices  127 us (50%)
  blocking collectives  40 us (16%)
  local copies, waits for them, and re-layouts  38.9 us (15%)
  matrix products  20.5 us (8%)
  between operations  14.4 us (6%)
  starting transfers between devices  9.4 us (4%)
  other arithmetic  3.3 us (1%)
    psum x1, waiting for transfers between devices, per_device(): aggregated = lax.psum(agg_part, 'rep')  53.4 us
    psum x1, waiting for transfers between devices, per_device(): weight_grad = lax.psum(grad_terms, 'rows')  52.7 us
    psum x1, blocking collectives, per_device(): back_sum = lax.psum(back_part, 'rep').astype(jnp.bfloat16)  40 us
    gather x10, local copies, waits for them, and re-layouts, offset_terms(): picked = panel[cols_idx]  16.7 us
    ppermute x4, waiting for transfers between devices, extended_2(): lax.ppermute(lax.slice_in_dim(block, block.shape[dim] - width, None, axis...  15.3 us
    dot_general x10, local copies, waits for them, and re-layouts, offset_terms(): jnp.einsum('kuv,kvf->kuf', values, picked, preferred_element_type=jnp.flo...  13.9 us
    dot_general x10, matrix products, offset_terms(): jnp.einsum('kb,kuf->buf', place, product, precision=lax.Precision.HIGHEST)  10.8 us
    ppermute x4, starting transfers between devices, extended_2(): lax.ppermute(lax.slice_in_dim(block, block.shape[dim] - width, None, axis...  9.25 us
  transfers between devices with their start and end apart: 10, of which 8 were waited for; matrix products, arithmetic and copies ran while one was open for 14% of the time, Pallas kernels for 0%

commit v1 on v0

v1 whole, which is shorter than its diff:
```python
import functools

import jax
import jax.numpy as jnp
from jax import lax
from jax.experimental import pallas as pl
from jax.experimental.pallas import tpu as pltpu
from jax.sharding import PartitionSpec as P

AXES = ("rows", "rep")


def route(shape, move):
    chips, reps = shape
    pairs = []
    for c in range(chips):
        for j in range(2):
            for z in range(reps):
                to = move(c, j, z)
                if to is not None:
                    target = ((to[0] % chips) * 2 + to[1]) * reps + to[2]
                    pairs.append(((c * 2 + j) * reps + z, target))
    return pairs


def tile_kernel(blocks, dsel_ref, meta_a_ref, meta_b_ref, own_ref, first_ref, second_ref, *refs):
    panels = refs[:5]
    out_ref = refs[5]
    acc_ref = refs[6]
    tile = own_ref.shape[-1]
    slots = own_ref.shape[1]
    mine = dsel_ref[5] == 1
    acc_ref[...] = jnp.zeros_like(acc_ref)
    for i in range(5):
        d = dsel_ref[i]
        for k in range(slots):
            for use_first in (False, True):
                if use_first:
                    values = first_ref[d, k]
                    meta = meta_b_ref
                else:
                    values = jnp.where(mine, own_ref[d, k], second_ref[d, k])
                    meta = meta_a_ref
                row = pl.multiple_of(meta[0, d * slots + k] * tile, tile)
                col = pl.multiple_of(meta[1, d * slots + k] * tile, tile)
                prod = jnp.dot(
                    values, panels[i][pl.ds(col, tile), :], preferred_element_type=jnp.float32
                )
                acc_ref[pl.ds(row, tile), :] += prod
    out_ref[...] = acc_ref[: blocks * tile, :].astype(out_ref.dtype)


def tile_product(dsel, meta_a, meta_b, own, first, second, panels):
    rows, width = panels[0].shape
    tile = own.shape[-1]
    blocks = rows // tile
    smem = pl.BlockSpec(memory_space=pltpu.SMEM)
    vmem = pl.BlockSpec(memory_space=pltpu.VMEM)
    count = own.shape[0] * own.shape[1] * 2
    return pl.pallas_call(
        functools.partial(tile_kernel, blocks),
        out_shape=jax.ShapeDtypeStruct((rows, width), jnp.bfloat16),
        in_specs=[smem] * 3 + [vmem] * 8,
        out_specs=vmem,
        scratch_shapes=[pltpu.VMEM(((blocks + 1) * tile, width), jnp.float32)],
        compiler_params=pltpu.CompilerParams(vmem_limit_bytes=32 * 1024 * 1024),
        cost_estimate=pl.CostEstimate(
            flops=2 * count * tile * tile * width,
            bytes_accessed=count * tile * tile * 3 + 6 * rows * width * 2,
            transcendentals=0,
        ),
        name="tile_product",
    )(dsel, meta_a, meta_b, own, first, second, *panels)


def middle_kernel(near_ref, far_ref, w_near_ref, w_far_ref, cot_ref, act_ref, adj_ref):
    agg = jnp.dot(near_ref[...], w_near_ref[...], preferred_element_type=jnp.float32)
    agg += jnp.dot(far_ref[...], w_far_ref[...], preferred_element_type=jnp.float32)
    sig = jax.nn.sigmoid(agg)
    act_ref[...] = (agg * sig).astype(act_ref.dtype)
    slope = sig * (1.0 + agg * (1.0 - sig))
    adj_ref[...] = (cot_ref[...].astype(jnp.float32) * slope).astype(adj_ref.dtype)


def middle(near, far, w_near, w_far, cot):
    vmem = pl.BlockSpec(memory_space=pltpu.VMEM)
    rows, width = near.shape
    out = jax.ShapeDtypeStruct((rows, width), jnp.bfloat16)
    return pl.pallas_call(
        middle_kernel,
        out_shape=(out, out),
        in_specs=[vmem] * 5,
        out_specs=(vmem, vmem),
        compiler_params=pltpu.CompilerParams(vmem_limit_bytes=32 * 1024 * 1024),
        cost_estimate=pl.CostEstimate(
            flops=4 * rows * width * width,
            bytes_accessed=10 * rows * width,
            transcendentals=rows * width,
        ),
        name="middle",
    )(near, far, w_near, w_far, cot)


def final_kernel(flag_ref, self_ref, one_ref, two_ref, w_near_ref, w_far_ref, out_ref):
    mine = flag_ref[0] == 1
    near = jnp.where(mine, self_ref[...], one_ref[...])
    far = jnp.where(mine, one_ref[...], two_ref[...])
    dims = (((1,), (1,)), ((), ()))
    total = lax.dot_general(near, w_near_ref[...], dims, preferred_element_type=jnp.float32)
    total += lax.dot_general(far, w_far_ref[...], dims, preferred_element_type=jnp.float32)
    out_ref[...] = total.astype(out_ref.dtype)


def final(flag, own, one, two, w_near, w_far):
    smem = pl.BlockSpec(memory_space=pltpu.SMEM)
    vmem = pl.BlockSpec(memory_space=pltpu.VMEM)
    rows = own.shape[0]
    wide = w_near.shape[0]
    return pl.pallas_call(
        final_kernel,
        out_shape=jax.ShapeDtypeStruct((rows, wide), jnp.bfloat16),
        in_specs=[smem] + [vmem] * 5,
        out_specs=vmem,
        compiler_params=pltpu.CompilerParams(vmem_limit_bytes=32 * 1024 * 1024),
        cost_estimate=pl.CostEstimate(
            flops=2 * rows * wide * wide, bytes_accessed=8 * rows * wide, transcendentals=0
        ),
        name="final",
    )(flag, own, one, two, w_near, w_far)


def per_device(node_feats, weight, cotangent, tile_values, tile_coords, tile_counts):
    groups = lax.axis_size("rows")
    reps = lax.axis_size("rep")
    shape = (groups // 2, reps)
    r = lax.axis_index("rows")
    z = lax.axis_index("rep")
    j = r % 2
    p = z % 2
    a = z // 2
    home = j == p
    scale = (node_feats.shape[0] * groups) ** (-0.5)
    half = node_feats.shape[1] // 2

    def send(value, move):
        return lax.ppermute(value, AXES, route(shape, move))

    def split(value):
        low, high = value[:, :half], value[:, half:]
        return jnp.where(j == 0, low, high), jnp.where(j == 0, high, low)

    def sibling(c, j, z):
        return (c, 1 - j, z)

    def across(c, j, z):
        return (c, j, (z + reps // 2) % reps)

    own = tile_values[0]
    slots = own.shape[1]
    slot_ids = z * slots + jnp.arange(slots, dtype=jnp.int32)
    blocks = node_feats.shape[0] // own.shape[-1]
    live = slot_ids[None, :] < tile_counts[0][:, None]
    meta = jnp.stack([jnp.where(live, tile_coords[0, 0], blocks), tile_coords[1, 0]])
    meta = meta.reshape(2, -1)

    def to_home(c, j, z):
        return (c, 1 - j, z) if j == z % 2 else (c, j, z ^ 1)

    def forward_x(c, j, z):
        return (c + 1, j, z) if j == z % 2 or z % 2 == 0 else (c - 1, j, z)

    def forward_x_cross(c, j, z):
        to = forward_x(c, j, z)
        return (to[0], 1 - j, to[2])

    mine, yours = split(node_feats)
    swapped = send(yours, sibling)
    one = send(mine, forward_x)
    two = send(yours, forward_x_cross)
    first = send(own, to_home)
    meta_b = send(meta, to_home)
    meta_far = send(meta, lambda c, j, z: None if j == z % 2 else (c, 1 - j, z ^ 1))
    group_half = jnp.where(home, mine, swapped)
    right = send(group_half, lambda c, j, z: (c - 1, j, z))
    second = send(first, lambda c, j, z: (c, 1 - j, z) if j == z % 2 else None)
    meta_a = jnp.where(home, meta, meta_far)
    cot_mine, cot_yours = split(cotangent)
    cot = jnp.where(home, cot_mine, send(cot_yours, sibling))

    d_other = jnp.where(p == 0, 3, 1)
    d_third = jnp.where(p == 0, 1, 3)
    flag = home.astype(jnp.int32)
    dsel = jnp.stack(
        [
            jnp.where(home, 2, d_other),
            jnp.where(home, d_other, 2),
            jnp.where(home, 0, d_third),
            jnp.where(home, d_third, 0),
            jnp.asarray(4),
            flag,
        ]
    ).astype(jnp.int32)
    part = tile_product(
        dsel, meta_a, meta_b, own, first, second, [mine, swapped, one, two, right]
    )

    def join(value):
        other = send(value, across)
        return (value.astype(jnp.float32) + other.astype(jnp.float32)).astype(jnp.bfloat16)

    near = join(part)
    far = send(near, sibling)
    w_cols, _ = split(weight)
    w_near = jnp.where(j == 0, w_cols[:half], w_cols[half:])
    w_far = jnp.where(j == 0, w_cols[half:], w_cols[:half])
    act, adj = middle(near, far, w_near, w_far, cot)

    dsel_back = jnp.stack([jnp.asarray(2), d_other, jnp.asarray(0), jnp.asarray(4), d_third, flag])
    dsel_back = dsel_back.astype(jnp.int32)
    left = send(adj, lambda c, j, z: (c + 1, j, z))
    right = send(adj, lambda c, j, z: (c - 1, j, z))
    third = send(adj, lambda c, j, z: (c + 1 if z % 2 else c - 1, j, z ^ 1))
    other = send(adj, lambda c, j, z: (c, j, z ^ 1))
    back_part = tile_product(
        dsel_back, meta_a, meta_b, own, first, second, [adj, other, left, right, third]
    )

    def deliver(value):
        one = send(value, lambda c, j, z: (c, j, z ^ 1) if j == z % 2 else (c, 1 - j, z))
        two = send(value, lambda c, j, z: None if j == z % 2 else (c, 1 - j, z ^ 1))
        return one, two

    act_one, act_two = deliver(act)
    act_near = jnp.where(home, act, act_one)
    act_far = jnp.where(home, act_one, act_two)
    activated = jnp.concatenate(
        [jnp.where(j == 0, act_near, act_far), jnp.where(j == 0, act_far, act_near)], axis=1
    )

    contract = (((0,), (0,)), ((), ()))
    grad = lax.dot_general(
        jnp.where(a == j, near, far), adj, contract, preferred_element_type=jnp.float32
    )
    grad = grad + send(grad, lambda c, j, z: (c, j, z ^ 1))
    step = 1
    while step < shape[0]:
        grad = grad + send(grad, lambda c, j, z, s=step: (c ^ s, j, z))
        step *= 2
    grad = grad * scale
    grad_across = send(grad, across)
    tall = jnp.concatenate(
        [jnp.where(a == 0, grad, grad_across), jnp.where(a == 0, grad_across, grad)], axis=0
    )
    tall_far = send(tall, sibling)
    weight_grad = jnp.concatenate(
        [jnp.where(j == 0, tall, tall_far), jnp.where(j == 0, tall_far, tall)], axis=1
    )

    back = join(back_part)
    back_one, back_two = deliver(back)
    w_cols, w_rest = split(weight)
    input_grad = final(flag[None], back, back_one, back_two, w_cols, w_rest)
    return (activated, input_grad, weight_grad)


def solution(mesh):
    return jax.shard_map(
        per_device,
        mesh=mesh,
        in_specs=(
            P("rows", None),
            P(),
            P("rows", None),
            P("rows", None, "rep", None, None),
            P(None, "rows", None, "rep"),
            P("rows", None),
        ),
        out_specs=(P("rows", None), P("rows", None), P()),
        check_vma=False,
    )
```

time: 256 us -> 124 us (0.48)
  waiting for transfers between devices: 127 us -> 60.4 us
  blocking collectives: 40 us -> 0 us
  local copies, waits for them, and re-layouts: 38.9 us -> 3.47 us
  starting transfers between devices: 9.4 us -> 43.6 us
  matrix products: 20.5 us -> 0.27 us
  between operations: 14.4 us -> 0.94 us
  Pallas kernels: 0 us -> 6.59 us
  other arithmetic: 3.3 us -> 7.91 us
    psum x2 -> x0, waiting for transfers between devices: 106 us -> none  [the longest x1 53.4 us: per_device(): aggregated = lax.psum(agg_part, 'rep')]
    psum x1 -> x0, blocking collectives: 40 us -> none  [per_device(): back_sum = lax.psum(back_part, 'rep').astype(jnp.bfloat16)]
    ppermute x8 -> x25, waiting for transfers between devices: 21.3 us -> 60.4 us  [send(): return lax.ppermute(value, AXES, route(shape, move))]
    ppermute x8 -> x25, starting transfers between devices: 9.32 us -> 43.6 us  [send(): return lax.ppermute(value, AXES, route(shape, move))]
    dot_general x23 -> x1, matrix products: 20.5 us -> 0.27 us  [per_device(): lax.dot_general(jnp.where(a == j, near, far), adj, contract, preferred_el...]
    gather x10 -> x0, local copies, waits for them, and re-layouts: 16.7 us -> none  [offset_terms(): picked = panel[cols_idx]]
    dot_general x10 -> x0, local copies, waits for them, and re-layouts: 13.9 us -> none  [offset_terms(): jnp.einsum('kuv,kvf->kuf', values, picked, preferred_element_type=jnp.flo...]
    pallas_call x0 -> x4, Pallas kernels: none -> 6.59 us  [the longest x2 5.02 us: tile_product(): pl.pallas_call(functools.partial(tile_kernel, blocks), out_shape=jax.Shap...]
  transfers between devices with their start and end apart: 10 -> 25, of which waited for: 8 -> 12; matrix products, arithmetic and copies ran while one was open for 14% -> 8% of each run, Pallas kernels for 0% -> 2%
where the time goes in v1:
time: 124 us; the launch traced here: 123 us
  waiting for transfers between devices  60.4 us (49%)
  starting transfers between devices  43.6 us (35%)
  other arithmetic  7.91 us (6%)
  Pallas kernels  6.59 us (5%)
  local copies, waits for them, and re-layouts  3.47 us (3%)
    ppermute x25, waiting for transfers between devices, send(): return lax.ppermute(value, AXES, route(shape, move))  60.4 us
    ppermute x25, starting transfers between devices, send(): return lax.ppermute(value, AXES, route(shape, move))  43.6 us
    pallas_call x2, Pallas kernels, tile_product(): pl.pallas_call(functools.partial(tile_kernel, blocks), out_shape=jax.Shap...  5.02 us
    select_n x3, other arithmetic, split(): return (jnp.where(j == 0, low, high), jnp.where(j == 0, high, low))  2.51 us
  transfers between devices with their start and end apart: 25, of which 12 were waited for; matrix products, arithmetic and copies ran while one was open for 8% of the time, Pallas kernels for 2%

profile of v1, /device:TPU:1, one launch (start us, length us, event | category | flops | bytes accessed | tf_op | source)
XLA Modules:
  0.0 123.2 jit_solution(10635303379354950536)
XLA Ops:
  0.6 2.2 %collective-permute-start.2 = (bf16[5,8,128,128]{3,2,1,0:T(8,128)(2,1)}, bf16[5,8,128,128]{3,2,1,0:T(8,128)(2,1)S(1)}, u32[]{:S(2)}, u32[]{:S(2)}) collective-permute-start(bf16[5,8,128,128]{3,2,1,0:T(8,128)(2,1)} %bitcast.12), channel_id=1, source_target_pairs={{0,4},{1,0},{2,6},{3,2},{4,5},{5,1},{6,7},{7,3},{8,12},{9,8},{10,1... | collective-permute-start | bytes 3932168 | tf_op jit(solution)/shard_map/ppermute | solution.py:146
  2.8 14.9 %collective-permute-done.2.first_ref = bf16[5,8,128,128]{3,2,1,0:T(8,128)(2,1)S(1)} collective-permute-done((bf16[5,8,128,128]{3,2,1,0:T(8,128)(2,1)}, bf16[5,8,128,128]{3,2,1,0:T(8,128)(2,1)S(1)}, u32[]{:S(2)}, u32[]{:S(2)}) %collective-permute-start.2) | collective-permute-done | bytes 1310752 | tf_op jit(solution)/shard_map/ppermute | solution.py:146
  17.7 1.3 %collective-permute-start.3 = (bf16[5,8,128,128]{3,2,1,0:T(8,128)(2,1)S(1)}, bf16[5,8,128,128]{3,2,1,0:T(8,128)(2,1)}, u32[]{:S(2)}, u32[]{:S(2)}) collective-permute-start(bf16[5,8,128,128]{3,2,1,0:T(8,128)(2,1)S(1)} %collective-permute-done.2.first_ref), channel_id=1, source_target_pairs={{0,4},{2,6},{5,1},{7,3},{8,12},{10,14},{13,9},{15,11},{16,20},{18,... | collective-permute-start | bytes 3932168 | tf_op jit(solution)/shard_map/ppermute | solution.py:146
  19.0 1.8 %broadcast_select_fusion.6 = bf16[1024,128]{1,0:T(8,128)(2,1)} fusion(pred[]{:T(512)S(6)} %eq.13, bf16[1024,256]{1,0:T(8,128)(2,1)} %param.6), kind=kLoop, calls=%fused_computation.14 | loop fusion | flops 131072 | bytes 786433 | tf_op jit(solution)/shard_map/jit(_where)/select_n | solution.py:150
  20.8 2.9 %collective-permute-start.4 = (bf16[1024,128]{1,0:T(8,128)(2,1)}, bf16[1024,128]{1,0:T(8,128)(2,1)S(1)}, u32[]{:S(2)}, u32[]{:S(2)}) collective-permute-start(bf16[1024,128]{1,0:T(8,128)(2,1)} %broadcast_select_fusion.6), channel_id=1, source_target_pairs={{0,4},{1,5},{2,6},{3,7},{4,0},{5,1},{6,2},{7,3},{8,12},{9,13},{10,... | collective-permute-start | bytes 786440 | tf_op jit(solution)/shard_map/ppermute | solution.py:146
  23.7 1.5 %collective-permute-start.6 = (bf16[1024,128]{1,0:T(8,128)(2,1)}, bf16[1024,128]{1,0:T(8,128)(2,1)S(1)}, u32[]{:S(2)}, u32[]{:S(2)}) collective-permute-start(bf16[1024,128]{1,0:T(8,128)(2,1)} %broadcast_select_fusion.6), channel_id=1, source_target_pairs={{0,12},{1,29},{2,14},{3,31},{4,8},{5,9},{6,10},{7,11},{8,20},{9,5}... | collective-permute-start | bytes 786440 | tf_op jit(solution)/shard_map/ppermute | solution.py:146
  25.3 0.7 slice_reduce_fusion.1
  26.2 0.7 lt.39
  27.1 1.8 %broadcast_select_fusion.2 = (bf16[1024,128]{1,0:T(8,128)(2,1)}, bf16[1024,128]{1,0:T(8,128)(2,1)S(1)}) fusion(bf16[1024,128]{1,0:T(8,128)(2,1)S(1)} %collective-permute-done.4.refs_1_, pred[]{:T(512)S(6)} %eq.14, bf16[1024,256]{1,0:T(8,128)(2,1)} %param.6, pred[]{:T(512)S(6)} %eq.13), kind=kLoop, calls=%fused_computation.10 | loop fusion | flops 262144 | bytes 1310722 | tf_op jit(solution)/shard_map/jit(_where)/select_n | solution.py:183
  28.9 1.2 collective-permute-start.5
  30.1 1.2 collective-permute-start.7
  31.2 2.8 %collective-permute-start = (s32[2,40]{1,0:T(2,128)S(1)}, s32[2,40]{1,0:T(2,128)S(1)}, u32[]{:S(2)}, u32[]{:S(2)}) collective-permute-start(s32[2,40]{1,0:T(2,128)S(1)} %pad_add_fusion), channel_id=1, source_target_pairs={{1,4},{3,6},{4,1},{6,3},{9,12},{11,14},{12,9},{14,11},{17,20},{19,... | collective-permute-start | bytes 968 | tf_op jit(solution)/shard_map/ppermute | solution.py:146
  34.2 2.3 %collective-permute-done = s32[2,40]{1,0:T(2,128)S(1)} collective-permute-done((s32[2,40]{1,0:T(2,128)S(1)}, s32[2,40]{1,0:T(2,128)S(1)}, u32[]{:S(2)}, u32[]{:S(2)}) %collective-permute-start) | collective-permute-done | bytes 352 | tf_op jit(solution)/shard_map/ppermute | solution.py:146
  36.5 1.1 collective-permute-done.1.meta_b_ref
  37.7 1.1 collective-permute-done.5.refs_2_
  38.8 5.4 %collective-permute-done.7.refs_4_ = bf16[1024,128]{1,0:T(8,128)(2,1)} collective-permute-done((bf16[1024,128]{1,0:T(8,128)(2,1)}, bf16[1024,128]{1,0:T(8,128)(2,1)}, u32[]{:S(2)}, u32[]{:S(2)}) %collective-permute-start.7) | collective-permute-done | bytes 262176 | tf_op jit(solution)/shard_map/ppermute | solution.py:146
  44.2 2.6 %tile_product.2 = bf16[1024,128]{1,0:T(8,128)(2,1)S(1)} custom-call(s32[6]{0:T(128)S(1)} %stack.42.dsel_ref, s32[2,40]{1,0:T(2,128)S(1)} %broadcast_select_fusion.16.meta_a_ref, s32[2,40]{1,0:T(2,128)S(1)} %collective-permute-done.1.meta_b_ref, bf16[5,8,128,128]{3,2,1,0:T(8,128)(2,1)S(1)} %bitcast.13, ...), custom_call_target="tpu_custom_call" | custom-call | flops 335544320 | bytes 5505024 | tf_op jit(solution)/shard_map/tile_product/pallas_call | solution.py:60
  46.8 2.4 %collective-permute-start.8 = (bf16[1024,128]{1,0:T(8,128)(2,1)S(1)}, bf16[1024,128]{1,0:T(8,128)(2,1)S(1)}, u32[]{:S(2)}, u32[]{:S(2)}) collective-permute-start(bf16[1024,128]{1,0:T(8,128)(2,1)S(1)} %tile_product.2), channel_id=1, source_target_pairs={{0,2},{1,3},{2,0},{3,1},{4,6},{5,7},{6,4},{7,5},{8,10},{9,11},{10,... | collective-permute-start | bytes 786440 | tf_op jit(solution)/shard_map/ppermute | solution.py:146
  49.2 0.7 broadcast_select_fusion.5
  49.9 1.3 %collective-permute-start.10 = (bf16[1024,128]{1,0:T(8,128)(2,1)}, bf16[1024,128]{1,0:T(8,128)(2,1)S(1)}, u32[]{:S(2)}, u32[]{:S(2)}) collective-permute-start(bf16[1024,128]{1,0:T(8,128)(2,1)} %broadcast_select_fusion.5), channel_id=1, source_target_pairs={{0,4},{1,5},{2,6},{3,7},{4,0},{5,1},{6,2},{7,3},{8,12},{9,13},{10,... | collective-permute-start | bytes 786440 | tf_op jit(solution)/shard_map/ppermute | solution.py:146
  51.3 10.1 %collective-permute-done.8 = bf16[1024,128]{1,0:T(8,128)(2,1)S(1)} collective-permute-done((bf16[1024,128]{1,0:T(8,128)(2,1)S(1)}, bf16[1024,128]{1,0:T(8,128)(2,1)S(1)}, u32[]{:S(2)}, u32[]{:S(2)}) %collective-permute-start.8) | collective-permute-done | bytes 262176 | tf_op jit(solution)/shard_map/ppermute | solution.py:146
  61.4 0.6 collective-permute-start.9
  62.0 0.6 broadcast_select_fusion.14
  62.6 1.1 select_select_fusion.cot_ref
  63.7 0.7 copy-done.3
  64.5 0.8 copy-done.4
  66.0 3.7 %collective-permute-done.20 = f32[128,128]{1,0:T(8,128)S(1)} collective-permute-done((f32[128,128]{1,0:T(8,128)S(1)}, f32[128,128]{1,0:T(8,128)S(1)}, u32[]{:S(2)}, u32[]{:S(2)}) %collective-permute-start.20) | collective-permute-done | bytes 65568 | tf_op jit(solution)/shard_map/ppermute | solution.py:146
  69.7 1.6 %collective-permute-start.21 = (f32[128,128]{1,0:T(8,128)S(1)}, f32[128,128]{1,0:T(8,128)S(1)}, u32[]{:S(2)}, u32[]{:S(2)}) collective-permute-start(f32[128,128]{1,0:T(8,128)S(1)} %add.39), channel_id=1, source_target_pairs={{0,8},{1,9},{2,10},{3,11},{4,12},{5,13},{6,14},{7,15},{8,0},{9,1},... | collective-permute-start | bytes 196616 | tf_op jit(solution)/shard_map/ppermute | solution.py:146
  71.2 1.7 %collective-permute-done.21 = f32[128,128]{1,0:T(8,128)S(1)} collective-permute-done((f32[128,128]{1,0:T(8,128)S(1)}, f32[128,128]{1,0:T(8,128)S(1)}, u32[]{:S(2)}, u32[]{:S(2)}) %collective-permute-start.21) | collective-permute-done | bytes 65568 | tf_op jit(solution)/shard_map/ppermute | solution.py:146
  72.9 0.8 collective-permute-start.22
  73.7 2.3 %collective-permute-done.22 = f32[128,128]{1,0:T(8,128)S(1)} collective-permute-done((f32[128,128]{1,0:T(8,128)S(1)}, f32[128,128]{1,0:T(8,128)S(1)}, u32[]{:S(2)}, u32[]{:S(2)}) %collective-permute-start.22) | collective-permute-done | bytes 65568 | tf_op jit(solution)/shard_map/ppermute | solution.py:146
  76.1 2.1 %collective-permute-start.23 = (f32[128,128]{1,0:T(8,128)S(1)}, f32[128,128]{1,0:T(8,128)S(1)}, u32[]{:S(2)}, u32[]{:S(2)}) collective-permute-start(f32[128,128]{1,0:T(8,128)S(1)} %add_multiply_fusion), channel_id=1, source_target_pairs={{0,2},{1,3},{2,0},{3,1},{4,6},{5,7},{6,4},{7,5},{8,10},{9,11},{10,... | collective-permute-start | bytes 196616 | tf_op jit(solution)/shard_map/ppermute | solution.py:146
  78.3 1.5 %collective-permute-start.14 = (bf16[1024,128]{1,0:T(8,128)(2,1)S(1)}, bf16[1024,128]{1,0:T(8,128)(2,1)S(1)}, u32[]{:S(2)}, u32[]{:S(2)}) collective-permute-start(bf16[1024,128]{1,0:T(8,128)(2,1)S(1)} %get-tuple-element.6.refs_0_), channel_id=1, source_target_pairs={{0,8},{1,9},{2,10},{3,11},{4,12},{5,13},{6,14},{7,15},{8,16},{9,17... | collective-permute-start | bytes 786440 | tf_op jit(solution)/shard_map/ppermute | solution.py:146
  79.8 0.9 collective-permute-start.15
  80.7 1.3 %collective-permute-start.16 = (bf16[1024,128]{1,0:T(8,128)(2,1)S(1)}, bf16[1024,128]{1,0:T(8,128)(2,1)S(1)}, u32[]{:S(2)}, u32[]{:S(2)}) collective-permute-start(bf16[1024,128]{1,0:T(8,128)(2,1)S(1)} %get-tuple-element.6.refs_0_), channel_id=1, source_target_pairs={{0,25},{1,8},{2,27},{3,10},{4,29},{5,12},{6,31},{7,14},{8,1},{9,16... | collective-permute-start | bytes 786440 | tf_op jit(solution)/shard_map/ppermute | solution.py:146
  81.9 3.9 %collective-permute-start.11 = (bf16[1024,128]{1,0:T(8,128)(2,1)}, bf16[1024,128]{1,0:T(8,128)(2,1)S(1)}, u32[]{:S(2)}, u32[]{:S(2)}) collective-permute-start(bf16[1024,128]{1,0:T(8,128)(2,1)} %copy-done.1), channel_id=1, source_target_pairs={{0,1},{1,5},{2,3},{3,7},{4,0},{5,4},{6,2},{7,6},{8,9},{9,13},{10,1... | collective-permute-start | bytes 786440 | tf_op jit(solution)/shard_map/ppermute | solution.py:146
  85.9 2.5 %collective-permute-start.12 = (bf16[1024,128]{1,0:T(8,128)(2,1)}, bf16[1024,128]{1,0:T(8,128)(2,1)S(1)}, u32[]{:S(2)}, u32[]{:S(2)}) collective-permute-start(bf16[1024,128]{1,0:T(8,128)(2,1)} %copy-done.1), channel_id=1, source_target_pairs={{1,4},{3,6},{4,1},{6,3},{9,12},{11,14},{12,9},{14,11},{17,20},{19,... | collective-permute-start | bytes 786440 | tf_op jit(solution)/shard_map/ppermute | solution.py:146
  88.5 7.9 %collective-permute-start.24 = (f32[256,128]{1,0:T(8,128)S(1)}, f32[256,128]{1,0:T(8,128)S(1)}, u32[]{:S(2)}, u32[]{:S(2)}) collective-permute-start(f32[256,128]{1,0:T(8,128)S(1)} %pad_maximum_fusion.2), channel_id=1, source_target_pairs={{0,4},{1,5},{2,6},{3,7},{4,0},{5,1},{6,2},{7,3},{8,12},{9,13},{10,... | collective-permute-start | bytes 393224 | tf_op jit(solution)/shard_map/ppermute | solution.py:146
  96.4 2.5 %tile_product.3 = bf16[1024,128]{1,0:T(8,128)(2,1)S(1)} custom-call(s32[6]{0:T(128)S(1)} %stack.47.dsel_ref, s32[2,40]{1,0:T(2,128)S(1)} %broadcast_select_fusion.16.meta_a_ref, s32[2,40]{1,0:T(2,128)S(1)} %collective-permute-done.1.meta_b_ref, bf16[5,8,128,128]{3,2,1,0:T(8,128)(2,1)S(1)} %bitcast.14, ...), custom_call_target="tpu_custom_call" | custom-call | flops 335544320 | bytes 5505024 | tf_op jit(solution)/shard_map/tile_product/pallas_call | solution.py:60
  98.8 0.4 collective-permute-start.17
  99.3 0.9 pad_maximum_fusion
  100.1 12.7 %collective-permute-done.17 = bf16[1024,128]{1,0:T(8,128)(2,1)S(1)} collective-permute-done((bf16[1024,128]{1,0:T(8,128)(2,1)S(1)}, bf16[1024,128]{1,0:T(8,128)(2,1)S(1)}, u32[]{:S(2)}, u32[]{:S(2)}) %collective-permute-start.17) | collective-permute-done | bytes 262176 | tf_op jit(solution)/shard_map/ppermute | solution.py:146
  112.9 1.4 %collective-permute-start.18 = (bf16[1024,128]{1,0:T(8,128)(2,1)S(1)}, bf16[1024,128]{1,0:T(8,128)(2,1)S(1)}, u32[]{:S(2)}, u32[]{:S(2)}) collective-permute-start(bf16[1024,128]{1,0:T(8,128)(2,1)S(1)} %add_convert_fusion.self_ref), channel_id=1, source_target_pairs={{0,1},{1,5},{2,3},{3,7},{4,0},{5,4},{6,2},{7,6},{8,9},{9,13},{10,1... | collective-permute-start | bytes 786440 | tf_op jit(solution)/shard_map/ppermute | solution.py:146
  114.3 1.9 %collective-permute-start.19 = (bf16[1024,128]{1,0:T(8,128)(2,1)S(1)}, bf16[1024,128]{1,0:T(8,128)(2,1)S(1)}, u32[]{:S(2)}, u32[]{:S(2)}) collective-permute-start(bf16[1024,128]{1,0:T(8,128)(2,1)S(1)} %add_convert_fusion.self_ref), channel_id=1, source_target_pairs={{1,4},{3,6},{4,1},{6,3},{9,12},{11,14},{12,9},{14,11},{17,20},{19,... | collective-permute-start | bytes 786440 | tf_op jit(solution)/shard_map/ppermute | solution.py:146
  116.2 0.7 pad_maximum_fusion.1
  117.0 1.2 collective-permute-done.18.one_ref
  118.2 3.8 %collective-permute-done.19.two_ref = bf16[1024,128]{1,0:T(8,128)(2,1)S(1)} collective-permute-done((bf16[1024,128]{1,0:T(8,128)(2,1)S(1)}, bf16[1024,128]{1,0:T(8,128)(2,1)S(1)}, u32[]{:S(2)}, u32[]{:S(2)}) %collective-permute-start.19) | collective-permute-done | bytes 262176 | tf_op jit(solution)/shard_map/ppermute | solution.py:146
  122.0 1.2 final.1
  (51 shorter events, 1.6 us)
Async XLA Ops:
  0.6 43.6 %copy-start = (bf16[1,5,8,128,128]{4,3,2,1,0:T(8,128)(2,1)S(1)}, bf16[1,5,8,128,128]{4,3,2,1,0:T(8,128)(2,1)}, u32[]{:S(2)}) copy-start(bf16[1,5,8,128,128]{4,3,2,1,0:T(8,128)(2,1)} %param.9) | copy-start | bytes 3932164
  0.6 17.1 %collective-permute-start.2 = (bf16[5,8,128,128]{3,2,1,0:T(8,128)(2,1)}, bf16[5,8,128,128]{3,2,1,0:T(8,128)(2,1)S(1)}, u32[]{:S(2)}, u32[]{:S(2)}) collective-permute-start(bf16[5,8,128,128]{3,2,1,0:T(8,128)(2,1)} %bitcast.12), channel_id=1, source_target_pairs={{0,4},{1,0},{2,6},{3,2},{4,5},{5,1},{6,7},{7,3},{8,12},{9,8},{10,1... | collective-permute-start | bytes 3932168 | tf_op jit(solution)/shard_map/ppermute | solution.py:146
  17.7 26.5 %collective-permute-start.3 = (bf16[5,8,128,128]{3,2,1,0:T(8,128)(2,1)S(1)}, bf16[5,8,128,128]{3,2,1,0:T(8,128)(2,1)}, u32[]{:S(2)}, u32[]{:S(2)}) collective-permute-start(bf16[5,8,128,128]{3,2,1,0:T(8,128)(2,1)S(1)} %collective-permute-done.2.first_ref), channel_id=1, source_target_pairs={{0,4},{2,6},{5,1},{7,3},{8,12},{10,14},{13,9},{15,11},{16,20},{18,... | collective-permute-start | bytes 3932168 | tf_op jit(solution)/shard_map/ppermute | solution.py:146
  20.8 6.3 %collective-permute-start.4 = (bf16[1024,128]{1,0:T(8,128)(2,1)}, bf16[1024,128]{1,0:T(8,128)(2,1)S(1)}, u32[]{:S(2)}, u32[]{:S(2)}) collective-permute-start(bf16[1024,128]{1,0:T(8,128)(2,1)} %broadcast_select_fusion.6), channel_id=1, source_target_pairs={{0,4},{1,5},{2,6},{3,7},{4,0},{5,1},{6,2},{7,3},{8,12},{9,13},{10,... | collective-permute-start | bytes 786440 | tf_op jit(solution)/shard_map/ppermute | solution.py:146
  23.7 13.9 %collective-permute-start.6 = (bf16[1024,128]{1,0:T(8,128)(2,1)}, bf16[1024,128]{1,0:T(8,128)(2,1)S(1)}, u32[]{:S(2)}, u32[]{:S(2)}) collective-permute-start(bf16[1024,128]{1,0:T(8,128)(2,1)} %broadcast_select_fusion.6), channel_id=1, source_target_pairs={{0,12},{1,29},{2,14},{3,31},{4,8},{5,9},{6,10},{7,11},{8,20},{9,5}... | collective-permute-start | bytes 786440 | tf_op jit(solution)/shard_map/ppermute | solution.py:146
  28.9 9.9 %collective-permute-start.5 = (bf16[1024,128]{1,0:T(8,128)(2,1)S(1)}, bf16[1024,128]{1,0:T(8,128)(2,1)}, u32[]{:S(2)}, u32[]{:S(2)}) collective-permute-start(bf16[1024,128]{1,0:T(8,128)(2,1)S(1)} %get-tuple-element.10.refs_0_), channel_id=1, source_target_pairs={{0,8},{1,25},{2,10},{3,27},{4,12},{5,13},{6,14},{7,15},{8,16},{9,1... | collective-permute-start | bytes 786440 | tf_op jit(solution)/shard_map/ppermute | solution.py:146
  30.1 14.2 %collective-permute-start.7 = (bf16[1024,128]{1,0:T(8,128)(2,1)}, bf16[1024,128]{1,0:T(8,128)(2,1)}, u32[]{:S(2)}, u32[]{:S(2)}) collective-permute-start(bf16[1024,128]{1,0:T(8,128)(2,1)} %get-tuple-element.9), channel_id=1, source_target_pairs={{0,24},{1,25},{2,26},{3,27},{4,28},{5,29},{6,30},{7,31},{8,0},{9,1... | collective-permute-start | bytes 786440 | tf_op jit(solution)/shard_map/ppermute | solution.py:146
  31.2 5.3 %collective-permute-start = (s32[2,40]{1,0:T(2,128)S(1)}, s32[2,40]{1,0:T(2,128)S(1)}, u32[]{:S(2)}, u32[]{:S(2)}) collective-permute-start(s32[2,40]{1,0:T(2,128)S(1)} %pad_add_fusion), channel_id=1, source_target_pairs={{1,4},{3,6},{4,1},{6,3},{9,12},{11,14},{12,9},{14,11},{17,20},{19,... | collective-permute-start | bytes 968 | tf_op jit(solution)/shard_map/ppermute | solution.py:146
  36.5 1.1 collective-permute-start.1
  36.5 12.7 %copy-start.5 = (bf16[1024,256]{1,0:T(8,128)(2,1)S(1)}, bf16[1024,256]{1,0:T(8,128)(2,1)}, u32[]{:S(2)}) copy-start(bf16[1024,256]{1,0:T(8,128)(2,1)} %param.8) | copy-start | bytes 1572868
  36.5 14.7 %copy-start.6 = (bf16[256,256]{1,0:T(8,128)(2,1)S(1)}, bf16[256,256]{1,0:T(8,128)(2,1)}, u32[]{:S(2)}) copy-start(bf16[256,256]{1,0:T(8,128)(2,1)} %param.7) | copy-start | bytes 393220
  46.8 14.5 %collective-permute-start.8 = (bf16[1024,128]{1,0:T(8,128)(2,1)S(1)}, bf16[1024,128]{1,0:T(8,128)(2,1)S(1)}, u32[]{:S(2)}, u32[]{:S(2)}) collective-permute-start(bf16[1024,128]{1,0:T(8,128)(2,1)S(1)} %tile_product.2), channel_id=1, source_target_pairs={{0,2},{1,3},{2,0},{3,1},{4,6},{5,7},{6,4},{7,5},{8,10},{9,11},{10,... | collective-permute-start | bytes 786440 | tf_op jit(solution)/shard_map/ppermute | solution.py:146
  49.9 12.7 %collective-permute-start.10 = (bf16[1024,128]{1,0:T(8,128)(2,1)}, bf16[1024,128]{1,0:T(8,128)(2,1)S(1)}, u32[]{:S(2)}, u32[]{:S(2)}) collective-permute-start(bf16[1024,128]{1,0:T(8,128)(2,1)} %broadcast_select_fusion.5), channel_id=1, source_target_pairs={{0,4},{1,5},{2,6},{3,7},{4,0},{5,1},{6,2},{7,3},{8,12},{9,13},{10,... | collective-permute-start | bytes 786440 | tf_op jit(solution)/shard_map/ppermute | solution.py:146
  61.4 2.3 %collective-permute-start.9 = (bf16[1024,128]{1,0:T(8,128)(2,1)S(1)}, bf16[1024,128]{1,0:T(8,128)(2,1)S(1)}, u32[]{:S(2)}, u32[]{:S(2)}) collective-permute-start(bf16[1024,128]{1,0:T(8,128)(2,1)S(1)} %add_convert_fusion.1.near_ref), channel_id=1, source_target_pairs={{0,4},{1,5},{2,6},{3,7},{4,0},{5,1},{6,2},{7,3},{8,12},{9,13},{10,... | collective-permute-start | bytes 786440 | tf_op jit(solution)/shard_map/ppermute | solution.py:146
  63.7 0.8 copy-start.3
  64.5 0.8 copy-start.4
  65.6 7.3 %copy-start.1 = (bf16[1024,128]{1,0:T(8,128)(2,1)}, bf16[1024,128]{1,0:T(8,128)(2,1)S(1)}, u32[]{:S(2)}) copy-start(bf16[1024,128]{1,0:T(8,128)(2,1)S(1)} %get-tuple-element.5) | copy-start | bytes 786436
  65.9 3.8 %collective-permute-start.20 = (f32[128,128]{1,0:T(8,128)S(1)}, f32[128,128]{1,0:T(8,128)S(1)}, u32[]{:S(2)}, u32[]{:S(2)}) collective-permute-start(f32[128,128]{1,0:T(8,128)S(1)} %fusion), channel_id=1, source_target_pairs={{0,1},{1,0},{2,3},{3,2},{4,5},{5,4},{6,7},{7,6},{8,9},{9,8},{10,11... | collective-permute-start | bytes 196616 | tf_op jit(solution)/shard_map/ppermute | solution.py:146
  69.7 3.2 %collective-permute-start.21 = (f32[128,128]{1,0:T(8,128)S(1)}, f32[128,128]{1,0:T(8,128)S(1)}, u32[]{:S(2)}, u32[]{:S(2)}) collective-permute-start(f32[128,128]{1,0:T(8,128)S(1)} %add.39), channel_id=1, source_target_pairs={{0,8},{1,9},{2,10},{3,11},{4,12},{5,13},{6,14},{7,15},{8,0},{9,1},... | collective-permute-start | bytes 196616 | tf_op jit(solution)/shard_map/ppermute | solution.py:146
  72.9 3.2 %collective-permute-start.22 = (f32[128,128]{1,0:T(8,128)S(1)}, f32[128,128]{1,0:T(8,128)S(1)}, u32[]{:S(2)}, u32[]{:S(2)}) collective-permute-start(f32[128,128]{1,0:T(8,128)S(1)} %add.40), channel_id=1, source_target_pairs={{0,16},{1,17},{2,18},{3,19},{4,20},{5,21},{6,22},{7,23},{8,24},{9,... | collective-permute-start | bytes 196616 | tf_op jit(solution)/shard_map/ppermute | solution.py:146
  73.7 12.2 %collective-permute-start.13 = (bf16[1024,128]{1,0:T(8,128)(2,1)S(1)}, bf16[1024,128]{1,0:T(8,128)(2,1)S(1)}, u32[]{:S(2)}, u32[]{:S(2)}) collective-permute-start(bf16[1024,128]{1,0:T(8,128)(2,1)S(1)} %get-tuple-element.6.refs_0_), channel_id=1, source_target_pairs={{0,1},{1,0},{2,3},{3,2},{4,5},{5,4},{6,7},{7,6},{8,9},{9,8},{10,11... | collective-permute-start | bytes 786440 | tf_op jit(solution)/shard_map/ppermute | solution.py:146
  76.1 5.8 %collective-permute-start.23 = (f32[128,128]{1,0:T(8,128)S(1)}, f32[128,128]{1,0:T(8,128)S(1)}, u32[]{:S(2)}, u32[]{:S(2)}) collective-permute-start(f32[128,128]{1,0:T(8,128)S(1)} %add_multiply_fusion), channel_id=1, source_target_pairs={{0,2},{1,3},{2,0},{3,1},{4,6},{5,7},{6,4},{7,5},{8,10},{9,11},{10,... | collective-permute-start | bytes 196616 | tf_op jit(solution)/shard_map/ppermute | solution.py:146
  78.3 10.1 %collective-permute-start.14 = (bf16[1024,128]{1,0:T(8,128)(2,1)S(1)}, bf16[1024,128]{1,0:T(8,128)(2,1)S(1)}, u32[]{:S(2)}, u32[]{:S(2)}) collective-permute-start(bf16[1024,128]{1,0:T(8,128)(2,1)S(1)} %get-tuple-element.6.refs_0_), channel_id=1, source_target_pairs={{0,8},{1,9},{2,10},{3,11},{4,12},{5,13},{6,14},{7,15},{8,16},{9,17... | collective-permute-start | bytes 786440 | tf_op jit(solution)/shard_map/ppermute | solution.py:146
  79.8 16.6 %collective-permute-start.15 = (bf16[1024,128]{1,0:T(8,128)(2,1)S(1)}, bf16[1024,128]{1,0:T(8,128)(2,1)S(1)}, u32[]{:S(2)}, u32[]{:S(2)}) collective-permute-start(bf16[1024,128]{1,0:T(8,128)(2,1)S(1)} %get-tuple-element.6.refs_0_), channel_id=1, source_target_pairs={{0,24},{1,25},{2,26},{3,27},{4,28},{5,29},{6,30},{7,31},{8,0},{9,1... | collective-permute-start | bytes 786440 | tf_op jit(solution)/shard_map/ppermute | solution.py:146
  80.7 15.7 %collective-permute-start.16 = (bf16[1024,128]{1,0:T(8,128)(2,1)S(1)}, bf16[1024,128]{1,0:T(8,128)(2,1)S(1)}, u32[]{:S(2)}, u32[]{:S(2)}) collective-permute-start(bf16[1024,128]{1,0:T(8,128)(2,1)S(1)} %get-tuple-element.6.refs_0_), channel_id=1, source_target_pairs={{0,25},{1,8},{2,27},{3,10},{4,29},{5,12},{6,31},{7,14},{8,1},{9,16... | collective-permute-start | bytes 786440 | tf_op jit(solution)/shard_map/ppermute | solution.py:146
  81.9 17.3 %collective-permute-start.11 = (bf16[1024,128]{1,0:T(8,128)(2,1)}, bf16[1024,128]{1,0:T(8,128)(2,1)S(1)}, u32[]{:S(2)}, u32[]{:S(2)}) collective-permute-start(bf16[1024,128]{1,0:T(8,128)(2,1)} %copy-done.1), channel_id=1, source_target_pairs={{0,1},{1,5},{2,3},{3,7},{4,0},{5,4},{6,2},{7,6},{8,9},{9,13},{10,1... | collective-permute-start | bytes 786440 | tf_op jit(solution)/shard_map/ppermute | solution.py:146
  85.9 13.3 %collective-permute-start.12 = (bf16[1024,128]{1,0:T(8,128)(2,1)}, bf16[1024,128]{1,0:T(8,128)(2,1)S(1)}, u32[]{:S(2)}, u32[]{:S(2)}) collective-permute-start(bf16[1024,128]{1,0:T(8,128)(2,1)} %copy-done.1), channel_id=1, source_target_pairs={{1,4},{3,6},{4,1},{6,3},{9,12},{11,14},{12,9},{14,11},{17,20},{19,... | collective-permute-start | bytes 786440 | tf_op jit(solution)/shard_map/ppermute | solution.py:146
  88.4 10.8 %copy-start.2 = (bf16[1024,128]{1,0:T(8,128)(2,1)S(1)}, bf16[1024,128]{1,0:T(8,128)(2,1)}, u32[]{:S(2)}) copy-start(bf16[1024,128]{1,0:T(8,128)(2,1)} %copy-done.1) | copy-start | bytes 786436
  88.5 27.7 %collective-permute-start.24 = (f32[256,128]{1,0:T(8,128)S(1)}, f32[256,128]{1,0:T(8,128)S(1)}, u32[]{:S(2)}, u32[]{:S(2)}) collective-permute-start(f32[256,128]{1,0:T(8,128)S(1)} %pad_maximum_fusion.2), channel_id=1, source_target_pairs={{0,4},{1,5},{2,6},{3,7},{4,0},{5,1},{6,2},{7,3},{8,12},{9,13},{10,... | collective-permute-start | bytes 393224 | tf_op jit(solution)/shard_map/ppermute | solution.py:146
  98.8 14.0 %collective-permute-start.17 = (bf16[1024,128]{1,0:T(8,128)(2,1)S(1)}, bf16[1024,128]{1,0:T(8,128)(2,1)S(1)}, u32[]{:S(2)}, u32[]{:S(2)}) collective-permute-start(bf16[1024,128]{1,0:T(8,128)(2,1)S(1)} %tile_product.3), channel_id=1, source_target_pairs={{0,2},{1,3},{2,0},{3,1},{4,6},{5,7},{6,4},{7,5},{8,10},{9,11},{10,... | collective-permute-start | bytes 786440 | tf_op jit(solution)/shard_map/ppermute | solution.py:146
  112.9 5.3 %collective-permute-start.18 = (bf16[1024,128]{1,0:T(8,128)(2,1)S(1)}, bf16[1024,128]{1,0:T(8,128)(2,1)S(1)}, u32[]{:S(2)}, u32[]{:S(2)}) collective-permute-start(bf16[1024,128]{1,0:T(8,128)(2,1)S(1)} %add_convert_fusion.self_ref), channel_id=1, source_target_pairs={{0,1},{1,5},{2,3},{3,7},{4,0},{5,4},{6,2},{7,6},{8,9},{9,13},{10,1... | collective-permute-start | bytes 786440 | tf_op jit(solution)/shard_map/ppermute | solution.py:146
  114.3 7.7 %collective-permute-start.19 = (bf16[1024,128]{1,0:T(8,128)(2,1)S(1)}, bf16[1024,128]{1,0:T(8,128)(2,1)S(1)}, u32[]{:S(2)}, u32[]{:S(2)}) collective-permute-start(bf16[1024,128]{1,0:T(8,128)(2,1)S(1)} %add_convert_fusion.self_ref), channel_id=1, source_target_pairs={{1,4},{3,6},{4,1},{6,3},{9,12},{11,14},{12,9},{14,11},{17,20},{19,... | collective-permute-start | bytes 786440 | tf_op jit(solution)/shard_map/ppermute | solution.py:146

commit v2 on v1

v2 whole, which is shorter than its diff:
```python
import functools

import jax
import jax.numpy as jnp
from jax import lax
from jax.experimental import pallas as pl
from jax.experimental.pallas import tpu as pltpu
from jax.sharding import PartitionSpec as P

AXES = ("rows", "rep")


def route(shape, move):
    chips, reps = shape
    pairs = []
    for c in range(chips):
        for j in range(2):
            for z in range(reps):
                to = move(c, j, z)
                if to is not None:
                    target = ((to[0] % chips) * 2 + to[1]) * reps + to[2]
                    pairs.append(((c * 2 + j) * reps + z, target))
    return pairs


def place():
    r = lax.axis_index("rows")
    z = lax.axis_index("rep")
    return r % 2, z, z % 2


def halves_kernel(x_ref, cot_ref, *refs):
    outs, sems = refs[:4], refs[4]
    j, _, _ = place()
    half = outs[0].shape[1]
    near = pl.ds(pl.multiple_of(j * half, half), half)
    far = pl.ds(pl.multiple_of((1 - j) * half, half), half)
    parts = ((x_ref, near), (x_ref, far), (cot_ref, near), (cot_ref, far))
    copies = []
    for i, (source, cols) in enumerate(parts):
        copy = pltpu.make_async_copy(source.at[:, cols], outs[i], sems.at[i])
        copy.start()
        copies.append(copy)
    for copy in copies:
        copy.wait()


def halves(feats, cot):
    rows, width = feats.shape
    part = jax.ShapeDtypeStruct((rows, width // 2), feats.dtype)
    vmem = pl.BlockSpec(memory_space=pltpu.VMEM)
    return pl.pallas_call(
        halves_kernel,
        out_shape=(part,) * 4,
        in_specs=[pl.BlockSpec(memory_space=pl.ANY)] * 2,
        out_specs=(vmem,) * 4,
        scratch_shapes=[pltpu.SemaphoreType.DMA((4,))],
        compiler_params=pltpu.CompilerParams(vmem_limit_bytes=16 * 1024 * 1024),
        name="halves",
    )(feats, cot)


def slots_kernel(dead, coords_ref, counts_ref, out_ref):
    _, z, _ = place()
    _, reach, slots = coords_ref.shape
    for d in range(reach):
        for k in range(slots):
            live = z * slots + k < counts_ref[d]
            out_ref[0, d * slots + k] = jnp.where(live, coords_ref[0, d, k], dead)
            out_ref[1, d * slots + k] = coords_ref[1, d, k]


def slot_blocks(coords, counts, dead):
    smem = pl.BlockSpec(memory_space=pltpu.SMEM)
    return pl.pallas_call(
        functools.partial(slots_kernel, dead),
        out_shape=jax.ShapeDtypeStruct((2, coords.shape[1] * coords.shape[2]), jnp.int32),
        in_specs=[smem, smem],
        out_specs=smem,
        name="slot_blocks",
    )(coords, counts)


def tile_kernel(blocks, dsel_ref, meta_a_ref, meta_b_ref, own_ref, first_ref, second_ref, *refs):
    panels, out_ref, acc_ref = refs[:-2], refs[-2], refs[-1]
    tile = own_ref.shape[-1]
    slots = own_ref.shape[1]
    j, _, p = place()
    home = j == p
    acc_ref[...] = jnp.zeros_like(acc_ref)
    for i in range(5):
        d = dsel_ref[i]
        for k in range(slots):
            for use_first in (False, True):
                if use_first:
                    values = first_ref[d, k]
                    meta = meta_b_ref
                else:
                    values = jnp.where(home, own_ref[d, k], second_ref[d, k])
                    meta = meta_a_ref
                row = pl.multiple_of(meta[0, d * slots + k] * tile, tile)
                col = pl.multiple_of(meta[1, d * slots + k] * tile, tile)
                source = panels[i][pl.ds(col, tile), :]
                if i == 4 and len(panels) == 6:
                    source = jnp.where(home, source, panels[5][pl.ds(col, tile), :])
                prod = jnp.dot(values, source, preferred_element_type=jnp.float32)
                acc_ref[pl.ds(row, tile), :] += prod
    out_ref[...] = acc_ref[: blocks * tile, :].astype(out_ref.dtype)


def tile_product(dsel, meta_a, meta_b, own, first, second, panels):
    rows, width = panels[0].shape
    tile = own.shape[-1]
    blocks = rows // tile
    smem = pl.BlockSpec(memory_space=pltpu.SMEM)
    vmem = pl.BlockSpec(memory_space=pltpu.VMEM)
    count = own.shape[0] * own.shape[1] * 2
    return pl.pallas_call(
        functools.partial(tile_kernel, blocks),
        out_shape=jax.ShapeDtypeStruct((rows, width), jnp.bfloat16),
        in_specs=[smem] * 3 + [vmem] * (3 + len(panels)),
        out_specs=vmem,
        scratch_shapes=[pltpu.VMEM(((blocks + 1) * tile, width), jnp.float32)],
        compiler_params=pltpu.CompilerParams(vmem_limit_bytes=32 * 1024 * 1024),
        cost_estimate=pl.CostEstimate(
            flops=2 * count * tile * tile * width,
            bytes_accessed=count * tile * tile * 3 + 6 * rows * width * 2,
            transcendentals=0,
        ),
        name="tile_product",
    )(dsel, meta_a, meta_b, own, first, second, *panels)


def middle_kernel(near_ref, far_ref, w_ref, cot_ref, cot_swap_ref, act_ref, adj_ref):
    j, _, p = place()
    half = near_ref.shape[1]
    near = pl.multiple_of(j * half, half)
    far = pl.multiple_of((1 - j) * half, half)
    cols = pl.ds(near, half)
    agg = jnp.dot(
        near_ref[...], w_ref[pl.ds(near, half), cols], preferred_element_type=jnp.float32
    )
    agg += jnp.dot(far_ref[...], w_ref[pl.ds(far, half), cols], preferred_element_type=jnp.float32)
    sig = jax.nn.sigmoid(agg)
    act_ref[...] = (agg * sig).astype(act_ref.dtype)
    slope = sig * (1.0 + agg * (1.0 - sig))
    cot = jnp.where(j == p, cot_ref[...], cot_swap_ref[...])
    adj_ref[...] = (cot.astype(jnp.float32) * slope).astype(adj_ref.dtype)


def middle(near, far, weight, cot, cot_swap):
    vmem = pl.BlockSpec(memory_space=pltpu.VMEM)
    rows, width = near.shape
    out = jax.ShapeDtypeStruct((rows, width), jnp.bfloat16)
    return pl.pallas_call(
        middle_kernel,
        out_shape=(out, out),
        in_specs=[vmem] * 5,
        out_specs=(vmem, vmem),
        compiler_params=pltpu.CompilerParams(vmem_limit_bytes=32 * 1024 * 1024),
        cost_estimate=pl.CostEstimate(
            flops=4 * rows * width * width,
            bytes_accessed=10 * rows * width,
            transcendentals=rows * width,
        ),
        name="middle",
    )(near, far, weight, cot, cot_swap)


def grad_kernel(scale, near_ref, far_ref, adj_ref, after_ref, out_ref):
    j, z, _ = place()
    lhs = jnp.where(z // 2 == j, near_ref[...], far_ref[...])
    dims = (((0,), (0,)), ((), ()))
    out_ref[...] = scale * lax.dot_general(
        lhs, adj_ref[...], dims, preferred_element_type=jnp.float32
    )


def grad_block(scale, near, far, adj, after):
    vmem = pl.BlockSpec(memory_space=pltpu.VMEM)
    rows, width = near.shape
    return pl.pallas_call(
        functools.partial(grad_kernel, scale),
        out_shape=jax.ShapeDtypeStruct((width, width), jnp.float32),
        in_specs=[vmem] * 3 + [pl.BlockSpec(memory_space=pl.ANY)],
        out_specs=vmem,
        compiler_params=pltpu.CompilerParams(vmem_limit_bytes=16 * 1024 * 1024),
        cost_estimate=pl.CostEstimate(
            flops=2 * rows * width * width, bytes_accessed=8 * rows * width, transcendentals=0
        ),
        name="grad_block",
    )(near, far, adj, after)


def final_kernel(self_ref, one_ref, two_ref, w_ref, out_ref):
    j, _, p = place()
    half = self_ref.shape[1]
    near = jnp.where(j == p, self_ref[...], one_ref[...])
    far = jnp.where(j == p, one_ref[...], two_ref[...])
    w_near = w_ref[:, pl.ds(pl.multiple_of(j * half, half), half)]
    w_far = w_ref[:, pl.ds(pl.multiple_of((1 - j) * half, half), half)]
    dims = (((1,), (1,)), ((), ()))
    total = lax.dot_general(near, w_near, dims, preferred_element_type=jnp.float32)
    total += lax.dot_general(far, w_far, dims, preferred_element_type=jnp.float32)
    out_ref[...] = total.astype(out_ref.dtype)


def final(own, one, two, weight):
    vmem = pl.BlockSpec(memory_space=pltpu.VMEM)
    rows = own.shape[0]
    wide = weight.shape[0]
    return pl.pallas_call(
        final_kernel,
        out_shape=jax.ShapeDtypeStruct((rows, wide), jnp.bfloat16),
        in_specs=[vmem] * 4,
        out_specs=vmem,
        compiler_params=pltpu.CompilerParams(vmem_limit_bytes=32 * 1024 * 1024),
        cost_estimate=pl.CostEstimate(
            flops=2 * rows * wide * wide, bytes_accessed=8 * rows * wide, transcendentals=0
        ),
        name="final",
    )(own, one, two, weight)


def per_device(node_feats, weight, cotangent, tile_values, tile_coords, tile_counts):
    groups = lax.axis_size("rows")
    reps = lax.axis_size("rep")
    shape = (groups // 2, reps)
    j, z, p = place()
    a = z // 2
    home = j == p
    scale = (node_feats.shape[0] * groups) ** (-0.5)

    def send(value, move):
        return lax.ppermute(value, AXES, route(shape, move))

    def sibling(c, j, z):
        return (c, 1 - j, z)

    def across(c, j, z):
        return (c, j, (z + reps // 2) % reps)

    def sibling_across(c, j, z):
        return (c, 1 - j, (z + reps // 2) % reps)

    own = tile_values[0]
    blocks = node_feats.shape[0] // own.shape[-1]

    def to_home(c, j, z):
        return (c, 1 - j, z) if j == z % 2 else (c, j, z ^ 1)

    def forward_x(c, j, z):
        return (c + 1, j, z) if j == z % 2 or z % 2 == 0 else (c - 1, j, z)

    def forward_x_cross(c, j, z):
        to = forward_x(c, j, z)
        return (to[0], 1 - j, to[2])

    first = send(own, to_home)
    mine, yours, cot, cot_yours = halves(node_feats, cotangent)
    one = send(mine, forward_x)
    two = send(yours, forward_x_cross)
    right = send(mine, lambda c, j, z: (c - 1, j, z) if j == z % 2 else None)
    right_cross = send(yours, lambda c, j, z: (c - 1, 1 - j, z) if j == z % 2 else None)
    swapped = send(yours, sibling)
    coords, counts, swapped = lax.optimization_barrier((tile_coords, tile_counts, swapped))
    meta = slot_blocks(coords[:, 0], counts[0], blocks)
    meta_b = send(meta, to_home)
    meta_far = send(meta, lambda c, j, z: None if j == z % 2 else (c, 1 - j, z ^ 1))
    cot_swap = send(cot_yours, sibling)
    first, one, two, right, right_cross, swapped, meta_b, meta_far = lax.optimization_barrier(
        (first, one, two, right, right_cross, swapped, meta_b, meta_far)
    )
    second = send(first, lambda c, j, z: (c, 1 - j, z) if j == z % 2 else None)
    meta_a = jnp.where(home, meta, meta_far)

    d_other = jnp.where(p == 0, 3, 1)
    d_third = jnp.where(p == 0, 1, 3)
    dsel = jnp.stack(
        [
            jnp.where(home, 2, d_other),
            jnp.where(home, d_other, 2),
            jnp.where(home, 0, d_third),
            jnp.where(home, d_third, 0),
            jnp.asarray(4),
        ]
    ).astype(jnp.int32)
    part = tile_product(
        dsel, meta_a, meta_b, own, first, second, [mine, swapped, one, two, right, right_cross]
    )

    def join(value):
        other = send(value, across)
        return (value.astype(jnp.float32) + other.astype(jnp.float32)).astype(jnp.bfloat16)

    near = join(part)
    far = send(near, sibling)
    act, adj = middle(near, far, weight, cot, cot_swap)

    dsel_back = jnp.stack([jnp.asarray(2), d_other, jnp.asarray(0), jnp.asarray(4), d_third])
    dsel_back = dsel_back.astype(jnp.int32)
    left = send(adj, lambda c, j, z: (c + 1, j, z))
    right = send(adj, lambda c, j, z: (c - 1, j, z))
    third = send(adj, lambda c, j, z: (c + 1 if z % 2 else c - 1, j, z ^ 1))
    other = send(adj, lambda c, j, z: (c, j, z ^ 1))
    back_part = tile_product(
        dsel_back, meta_a, meta_b, own, first, second, [adj, other, left, right, third]
    )

    def deliver(value):
        one = send(value, lambda c, j, z: (c, j, z ^ 1) if j == z % 2 else (c, 1 - j, z))
        two = send(value, lambda c, j, z: None if j == z % 2 else (c, 1 - j, z ^ 1))
        return one, two

    act_one, act_two = deliver(act)
    act_near = jnp.where(home, act, act_one)
    act_far = jnp.where(home, act_one, act_two)
    activated = jnp.concatenate(
        [jnp.where(j == 0, act_near, act_far), jnp.where(j == 0, act_far, act_near)], axis=1
    )

    back = join(back_part)
    back_one, back_two = deliver(back)
    input_grad = final(back, back_one, back_two, weight)

    grad = grad_block(scale, near, far, adj, other)
    step = 1
    while step < shape[0]:
        flips = [step] if step * 2 >= shape[0] else [step, 2 * step, 3 * step]
        got = [send(grad, lambda c, j, z, s=s: (c ^ s, j, z)) for s in flips]
        grad = grad + got[0]
        if len(got) == 3:
            grad = grad + (got[1] + got[2])
        step *= 2 if len(flips) == 1 else 4
    grad = grad + send(grad, lambda c, j, z: (c, j, z ^ 1))
    grad_across = send(grad, across)
    grad_sib = send(grad, sibling)
    grad_sib_across = send(grad, sibling_across)
    tall = jnp.concatenate(
        [jnp.where(a == 0, grad, grad_across), jnp.where(a == 0, grad_across, grad)], axis=0
    )
    tall_far = jnp.concatenate(
        [
            jnp.where(a == 0, grad_sib, grad_sib_across),
            jnp.where(a == 0, grad_sib_across, grad_sib),
        ],
        axis=0,
    )
    weight_grad = jnp.concatenate(
        [jnp.where(j == 0, tall, tall_far), jnp.where(j == 0, tall_far, tall)], axis=1
    )
    return (activated, input_grad, weight_grad)


def solution(mesh):
    return jax.shard_map(
        per_device,
        mesh=mesh,
        in_specs=(
            P("rows", None),
            P(),
            P("rows", None),
            P("rows", None, "rep", None, None),
            P(None, "rows", None, "rep"),
            P("rows", None),
        ),
        out_specs=(P("rows", None), P("rows", None), P()),
        check_vma=False,
    )
```

time: 124 us -> 112 us (0.903)
  waiting for transfers between devices: 60.4 us -> 47.3 us
  local copies, waits for them, and re-layouts: 3.47 us -> 14.2 us
  other arithmetic: 7.91 us -> 2.69 us
  starting transfers between devices: 43.6 us -> 38.7 us
    ppermute x25 -> x28, waiting for transfers between devices: 60.4 us -> 47.3 us  [send(): return lax.ppermute(value, AXES, route(shape, move))]
    unnamed x14 -> x42, local copies, waits for them, and re-layouts: 1.54 us -> 12.7 us
    select_n x7 -> x1, other arithmetic: 6.04 us -> 0.01 us  [per_device(): jnp.where(a == 0, grad_sib, grad_sib_across)]
    ppermute x25 -> x28, starting transfers between devices: 43.6 us -> 38.7 us  [send(): return lax.ppermute(value, AXES, route(shape, move))]
    pallas_call x0 -> x3, Pallas kernels: none -> 1.94 us  [the longest x1 1.44 us: slot_blocks(): pl.pallas_call(functools.partial(slots_kernel, dead), out_shape=jax.Shape...]
  transfers between devices with their start and end apart: 25 -> 28, of which waited for: 12 -> 12; matrix products, arithmetic and copies ran while one was open for 8% -> 4% of each run, Pallas kernels for 2% -> 4%
where the time goes in v2:
time: 112 us; the launch traced here: 111 us
  waiting for transfers between devices  47.3 us (42%)
  starting transfers between devices  38.7 us (35%)
  local copies, waits for them, and re-layouts  14.2 us (13%)
  Pallas kernels  7.48 us (7%)
  other arithmetic  2.69 us (2%)
    ppermute x28, waiting for transfers between devices, send(): return lax.ppermute(value, AXES, route(shape, move))  47.3 us
    ppermute x28, starting transfers between devices, send(): return lax.ppermute(value, AXES, route(shape, move))  38.7 us
    unnamed x42, local copies, waits for them, and re-layouts  12.7 us
    pallas_call x2, Pallas kernels, tile_product(): pl.pallas_call(functools.partial(tile_kernel, blocks), out_shape=jax.Shap...  3.94 us
  transfers between devices with their start and end apart: 28, of which 12 were waited for; matrix products, arithmetic and copies ran while one was open for 4% of the time, Pallas kernels for 4%

profile of v2, /device:TPU:1, one launch (start us, length us, event | category | flops | bytes accessed | tf_op | source)
XLA Modules:
  0.0 111.4 jit_solution(2953312344869333738)
XLA Ops:
  0.6 2.2 %collective-permute-start.1 = (bf16[5,8,128,128]{3,2,1,0:T(8,128)(2,1)}, bf16[5,8,128,128]{3,2,1,0:T(8,128)(2,1)S(1)}, u32[]{:S(2)}, u32[]{:S(2)}) collective-permute-start(bf16[5,8,128,128]{3,2,1,0:T(8,128)(2,1)} %bitcast.11), channel_id=1, source_target_pairs={{0,4},{1,0},{2,6},{3,2},{4,5},{5,1},{6,7},{7,3},{8,12},{9,8},{10,1... | collective-permute-start | bytes 3932168 | tf_op jit(solution)/shard_map/ppermute | solution.py:235
  2.8 1.0 copy-done.4
  3.9 1.0 copy-done.5
  5.8 0.7 copy-done.19
  6.5 1.2 %collective-permute-start.2 = (bf16[1024,128]{1,0:T(8,128)(2,1)S(1)}, bf16[1024,128]{1,0:T(8,128)(2,1)S(1)}, u32[]{:S(2)}, u32[]{:S(2)}) collective-permute-start(bf16[1024,128]{1,0:T(8,128)(2,1)S(1)} %get-tuple-element.23.refs_0_), channel_id=1, source_target_pairs={{0,8},{1,25},{2,10},{3,27},{4,12},{5,13},{6,14},{7,15},{8,16},{9,1... | collective-permute-start | bytes 786440 | tf_op jit(solution)/shard_map/ppermute | solution.py:235
  7.8 1.9 %collective-permute-start.3 = (bf16[1024,128]{1,0:T(8,128)(2,1)S(1)}, bf16[1024,128]{1,0:T(8,128)(2,1)S(1)}, u32[]{:S(2)}, u32[]{:S(2)}) collective-permute-start(bf16[1024,128]{1,0:T(8,128)(2,1)S(1)} %get-tuple-element.20), channel_id=1, source_target_pairs={{0,12},{1,29},{2,14},{3,31},{4,8},{5,9},{6,10},{7,11},{8,20},{9,5}... | collective-permute-start | bytes 786440 | tf_op jit(solution)/shard_map/ppermute | solution.py:235
  10.3 1.3 %collective-permute-start.5 = (bf16[1024,128]{1,0:T(8,128)(2,1)S(1)}, bf16[1024,128]{1,0:T(8,128)(2,1)S(1)}, u32[]{:S(2)}, u32[]{:S(2)}) collective-permute-start(bf16[1024,128]{1,0:T(8,128)(2,1)S(1)} %get-tuple-element.20), channel_id=1, source_target_pairs={{0,28},{2,30},{5,25},{7,27},{8,4},{10,6},{13,1},{15,3},{16,12},{18... | collective-permute-start | bytes 786440 | tf_op jit(solution)/shard_map/ppermute | solution.py:235
  12.9 1.4 %slot_blocks.1 = s32[2,40]{1,0:T(2,128)} custom-call(s32[2,5,8]{2,1,0:T(8,128)} %copy.10.coords_ref, s32[5]{0:T(128)} %bitcast.15), custom_call_target="tpu_custom_call" | custom-call | tf_op jit(solution)/shard_map/slot_blocks/pallas_call | solution.py:75
  14.8 3.7 %collective-permute-start.6 = (s32[2,40]{1,0:T(2,128)}, s32[2,40]{1,0:T(2,128)S(1)}, u32[]{:S(2)}, u32[]{:S(2)}) collective-permute-start(s32[2,40]{1,0:T(2,128)} %slot_blocks.1), channel_id=1, source_target_pairs={{0,4},{1,0},{2,6},{3,2},{4,5},{5,1},{6,7},{7,3},{8,12},{9,8},{10,1... | collective-permute-start | bytes 968 | tf_op jit(solution)/shard_map/ppermute | solution.py:235
  18.5 2.6 %collective-permute-done.3.refs_3_ = bf16[1024,128]{1,0:T(8,128)(2,1)S(1)} collective-permute-done((bf16[1024,128]{1,0:T(8,128)(2,1)S(1)}, bf16[1024,128]{1,0:T(8,128)(2,1)S(1)}, u32[]{:S(2)}, u32[]{:S(2)}) %collective-permute-start.3) | collective-permute-done | bytes 262176 | tf_op jit(solution)/shard_map/ppermute | solution.py:235
  21.1 0.7 copy-done.7
  21.8 3.2 %collective-permute-start.7 = (s32[2,40]{1,0:T(2,128)}, s32[2,40]{1,0:T(2,128)S(1)}, u32[]{:S(2)}, u32[]{:S(2)}) collective-permute-start(s32[2,40]{1,0:T(2,128)} %slot_blocks.1), channel_id=1, source_target_pairs={{1,4},{3,6},{4,1},{6,3},{9,12},{11,14},{12,9},{14,11},{17,20},{19,... | collective-permute-start | bytes 968 | tf_op jit(solution)/shard_map/ppermute | solution.py:235
  25.8 1.0 collective-permute-done.5.refs_5_
  27.5 1.3 %collective-permute-start.8 = (bf16[5,8,128,128]{3,2,1,0:T(8,128)(2,1)S(1)}, bf16[5,8,128,128]{3,2,1,0:T(8,128)(2,1)S(1)}, u32[]{:S(2)}, u32[]{:S(2)}) collective-permute-start(bf16[5,8,128,128]{3,2,1,0:T(8,128)(2,1)S(1)} %collective-permute-done.1.first_ref), channel_id=1, source_target_pairs={{0,4},{2,6},{5,1},{7,3},{8,12},{10,14},{13,9},{15,11},{16,20},{18,... | collective-permute-start | bytes 3932168 | tf_op jit(solution)/shard_map/ppermute | solution.py:235
  28.9 3.5 %collective-permute-done.8.second_ref = bf16[5,8,128,128]{3,2,1,0:T(8,128)(2,1)S(1)} collective-permute-done((bf16[5,8,128,128]{3,2,1,0:T(8,128)(2,1)S(1)}, bf16[5,8,128,128]{3,2,1,0:T(8,128)(2,1)S(1)}, u32[]{:S(2)}, u32[]{:S(2)}) %collective-permute-start.8) | collective-permute-done | bytes 1310752 | tf_op jit(solution)/shard_map/ppermute | solution.py:235
  32.4 1.3 %copy-done = bf16[1,5,8,128,128]{4,3,2,1,0:T(8,128)(2,1)S(1)} copy-done((bf16[1,5,8,128,128]{4,3,2,1,0:T(8,128)(2,1)S(1)}, bf16[1,5,8,128,128]{4,3,2,1,0:T(8,128)(2,1)}, u32[]{:S(2)}) %copy-start) | copy-done | bytes 1310744
  33.7 0.9 copy-done.8
  34.7 0.9 copy-done.10
  35.6 0.9 copy-done.12
  36.6 1.7 %tile_product.2 = bf16[1024,128]{1,0:T(8,128)(2,1)S(1)} custom-call(s32[5]{0:T(128)S(1)} %stack.28.dsel_ref, s32[2,40]{1,0:T(2,128)S(1)} %broadcast_select_fusion.8.meta_a_ref, s32[2,40]{1,0:T(2,128)S(1)} %collective-permute-done.6.meta_b_ref, bf16[5,8,128,128]{3,2,1,0:T(8,128)(2,1)S(1)} %bitcast.12, ...), custom_call_target="tpu_custom_call" | custom-call | flops 335544320 | bytes 5505024 | tf_op jit(solution)/shard_map/tile_product/pallas_call | solution.py:118
  38.4 2.4 %collective-permute-start.9 = (bf16[1024,128]{1,0:T(8,128)(2,1)S(1)}, bf16[1024,128]{1,0:T(8,128)(2,1)S(1)}, u32[]{:S(2)}, u32[]{:S(2)}) collective-permute-start(bf16[1024,128]{1,0:T(8,128)(2,1)S(1)} %tile_product.2), channel_id=1, source_target_pairs={{0,2},{1,3},{2,0},{3,1},{4,6},{5,7},{6,4},{7,5},{8,10},{9,11},{10,... | collective-permute-start | bytes 786440 | tf_op jit(solution)/shard_map/ppermute | solution.py:235
  41.2 11.5 %collective-permute-done.9 = bf16[1024,128]{1,0:T(8,128)(2,1)S(1)} collective-permute-done((bf16[1024,128]{1,0:T(8,128)(2,1)S(1)}, bf16[1024,128]{1,0:T(8,128)(2,1)S(1)}, u32[]{:S(2)}, u32[]{:S(2)}) %collective-permute-start.9) | collective-permute-done | bytes 262176 | tf_op jit(solution)/shard_map/ppermute | solution.py:235
  52.8 1.0 collective-permute-start.10
  53.8 1.2 %collective-permute-done.10.far_ref = bf16[1024,128]{1,0:T(8,128)(2,1)S(1)} collective-permute-done((bf16[1024,128]{1,0:T(8,128)(2,1)S(1)}, bf16[1024,128]{1,0:T(8,128)(2,1)S(1)}, u32[]{:S(2)}, u32[]{:S(2)}) %collective-permute-start.10) | collective-permute-done | bytes 262176 | tf_op jit(solution)/shard_map/ppermute | solution.py:235
  55.6 1.4 %collective-permute-start.15 = (bf16[1024,128]{1,0:T(8,128)(2,1)S(1)}, bf16[1024,128]{1,0:T(8,128)(2,1)S(1)}, u32[]{:S(2)}, u32[]{:S(2)}) collective-permute-start(bf16[1024,128]{1,0:T(8,128)(2,1)S(1)} %get-tuple-element.36.refs_0_.adj_ref), channel_id=1, source_target_pairs={{0,8},{1,9},{2,10},{3,11},{4,12},{5,13},{6,14},{7,15},{8,16},{9,17... | collective-permute-start | bytes 786440 | tf_op jit(solution)/shard_map/ppermute | solution.py:235
  57.0 1.0 collective-permute-start.16
  58.0 1.2 %collective-permute-start.17 = (bf16[1024,128]{1,0:T(8,128)(2,1)S(1)}, bf16[1024,128]{1,0:T(8,128)(2,1)}, u32[]{:S(2)}, u32[]{:S(2)}) collective-permute-start(bf16[1024,128]{1,0:T(8,128)(2,1)S(1)} %get-tuple-element.36.refs_0_.adj_ref), channel_id=1, source_target_pairs={{0,25},{1,8},{2,27},{3,10},{4,29},{5,12},{6,31},{7,14},{8,1},{9,16... | collective-permute-start | bytes 786440 | tf_op jit(solution)/shard_map/ppermute | solution.py:235
  59.2 3.7 %collective-permute-done.14.refs_1_.after_ref = bf16[1024,128]{1,0:T(8,128)(2,1)S(1)} collective-permute-done((bf16[1024,128]{1,0:T(8,128)(2,1)S(1)}, bf16[1024,128]{1,0:T(8,128)(2,1)S(1)}, u32[]{:S(2)}, u32[]{:S(2)}) %collective-permute-start.14) | collective-permute-done | bytes 262176 | tf_op jit(solution)/shard_map/ppermute | solution.py:235
  63.2 1.3 %collective-permute-start.21 = (f32[128,128]{1,0:T(8,128)S(1)}, f32[128,128]{1,0:T(8,128)S(1)}, u32[]{:S(2)}, u32[]{:S(2)}) collective-permute-start(f32[128,128]{1,0:T(8,128)S(1)} %grad_block.1), channel_id=1, source_target_pairs={{0,8},{1,9},{2,10},{3,11},{4,12},{5,13},{6,14},{7,15},{8,0},{9,1},... | collective-permute-start | bytes 196616 | tf_op jit(solution)/shard_map/ppermute | solution.py:235
  64.7 0.7 copy-done.17
  65.4 1.2 %collective-permute-start.23 = (f32[128,128]{1,0:T(8,128)S(1)}, f32[128,128]{1,0:T(8,128)}, u32[]{:S(2)}, u32[]{:S(2)}) collective-permute-start(f32[128,128]{1,0:T(8,128)S(1)} %grad_block.1), channel_id=1, source_target_pairs={{0,24},{1,25},{2,26},{3,27},{4,28},{5,29},{6,30},{7,31},{8,16},{9,... | collective-permute-start | bytes 196616 | tf_op jit(solution)/shard_map/ppermute | solution.py:235
  66.7 7.9 %collective-permute-done.16.refs_3_ = bf16[1024,128]{1,0:T(8,128)(2,1)} collective-permute-done((bf16[1024,128]{1,0:T(8,128)(2,1)S(1)}, bf16[1024,128]{1,0:T(8,128)(2,1)}, u32[]{:S(2)}, u32[]{:S(2)}) %collective-permute-start.16) | collective-permute-done | bytes 262176 | tf_op jit(solution)/shard_map/ppermute | solution.py:235
  74.6 2.6 %collective-permute-start.12 = (bf16[1024,128]{1,0:T(8,128)(2,1)}, bf16[1024,128]{1,0:T(8,128)(2,1)S(1)}, u32[]{:S(2)}, u32[]{:S(2)}) collective-permute-start(bf16[1024,128]{1,0:T(8,128)(2,1)} %copy-done.15), channel_id=1, source_target_pairs={{0,1},{1,5},{2,3},{3,7},{4,0},{5,4},{6,2},{7,6},{8,9},{9,13},{10,1... | collective-permute-start | bytes 786440 | tf_op jit(solution)/shard_map/ppermute | solution.py:235
  77.2 3.0 %collective-permute-start.13 = (bf16[1024,128]{1,0:T(8,128)(2,1)}, bf16[1024,128]{1,0:T(8,128)(2,1)S(1)}, u32[]{:S(2)}, u32[]{:S(2)}) collective-permute-start(bf16[1024,128]{1,0:T(8,128)(2,1)} %copy-done.15), channel_id=1, source_target_pairs={{1,4},{3,6},{4,1},{6,3},{9,12},{11,14},{12,9},{14,11},{17,20},{19,... | collective-permute-start | bytes 786440 | tf_op jit(solution)/shard_map/ppermute | solution.py:235
  80.2 1.3 %copy-done.3 = bf16[5,8,128,128]{3,2,1,0:T(8,128)(2,1)S(1)} copy-done((bf16[5,8,128,128]{3,2,1,0:T(8,128)(2,1)S(1)}, bf16[5,8,128,128]{3,2,1,0:T(8,128)(2,1)}, u32[]{:S(2)}) %copy-start.3) | copy-done | bytes 1310744
  81.6 0.9 copy-done.18
  82.5 2.2 %tile_product.3 = bf16[1024,128]{1,0:T(8,128)(2,1)S(1)} custom-call(s32[5]{0:T(128)S(1)} %stack.31.dsel_ref, s32[2,40]{1,0:T(2,128)S(1)} %broadcast_select_fusion.8.meta_a_ref, s32[2,40]{1,0:T(2,128)S(1)} %collective-permute-done.6.meta_b_ref, bf16[5,8,128,128]{3,2,1,0:T(8,128)(2,1)S(1)} %bitcast.13, ...), custom_call_target="tpu_custom_call" | custom-call | flops 335544320 | bytes 5505024 | tf_op jit(solution)/shard_map/tile_product/pallas_call | solution.py:118
  84.7 2.1 %collective-permute-start.18 = (bf16[1024,128]{1,0:T(8,128)(2,1)S(1)}, bf16[1024,128]{1,0:T(8,128)(2,1)S(1)}, u32[]{:S(2)}, u32[]{:S(2)}) collective-permute-start(bf16[1024,128]{1,0:T(8,128)(2,1)S(1)} %tile_product.3), channel_id=1, source_target_pairs={{0,2},{1,3},{2,0},{3,1},{4,6},{5,7},{6,4},{7,5},{8,10},{9,11},{10,... | collective-permute-start | bytes 786440 | tf_op jit(solution)/shard_map/ppermute | solution.py:235
  86.8 0.9 add_add_fusion
  87.9 5.8 %collective-permute-done.24 = f32[128,128]{1,0:T(8,128)S(1)} collective-permute-done((f32[128,128]{1,0:T(8,128)S(1)}, f32[128,128]{1,0:T(8,128)S(1)}, u32[]{:S(2)}, u32[]{:S(2)}) %collective-permute-start.24) | collective-permute-done | bytes 65568 | tf_op jit(solution)/shard_map/ppermute | solution.py:235
  93.7 0.9 pad_maximum_fusion
  94.6 2.6 %collective-permute-start.26 = (f32[128,128]{1,0:T(8,128)S(1)}, f32[128,128]{1,0:T(8,128)S(1)}, u32[]{:S(2)}, u32[]{:S(2)}) collective-permute-start(f32[128,128]{1,0:T(8,128)S(1)} %add.33), channel_id=1, source_target_pairs={{0,4},{1,5},{2,6},{3,7},{4,0},{5,1},{6,2},{7,3},{8,12},{9,13},{10,... | collective-permute-start | bytes 196616 | tf_op jit(solution)/shard_map/ppermute | solution.py:235
  97.3 4.7 %collective-permute-done.25 = f32[128,128]{1,0:T(8,128)S(1)} collective-permute-done((f32[128,128]{1,0:T(8,128)S(1)}, f32[128,128]{1,0:T(8,128)S(1)}, u32[]{:S(2)}, u32[]{:S(2)}) %collective-permute-start.25) | collective-permute-done | bytes 65568 | tf_op jit(solution)/shard_map/ppermute | solution.py:235
  102.5 1.9 %collective-permute-start.20 = (bf16[1024,128]{1,0:T(8,128)(2,1)S(1)}, bf16[1024,128]{1,0:T(8,128)(2,1)S(1)}, u32[]{:S(2)}, u32[]{:S(2)}) collective-permute-start(bf16[1024,128]{1,0:T(8,128)(2,1)S(1)} %add_convert_fusion.self_ref), channel_id=1, source_target_pairs={{1,4},{3,6},{4,1},{6,3},{9,12},{11,14},{12,9},{14,11},{17,20},{19,... | collective-permute-start | bytes 786440 | tf_op jit(solution)/shard_map/ppermute | solution.py:235
  104.5 0.7 pad_maximum_fusion.1
  105.2 2.2 %collective-permute-done.19.one_ref = bf16[1024,128]{1,0:T(8,128)(2,1)S(1)} collective-permute-done((bf16[1024,128]{1,0:T(8,128)(2,1)S(1)}, bf16[1024,128]{1,0:T(8,128)(2,1)S(1)}, u32[]{:S(2)}, u32[]{:S(2)}) %collective-permute-start.19) | collective-permute-done | bytes 262176 | tf_op jit(solution)/shard_map/ppermute | solution.py:235
  107.4 2.8 %collective-permute-done.20.two_ref = bf16[1024,128]{1,0:T(8,128)(2,1)S(1)} collective-permute-done((bf16[1024,128]{1,0:T(8,128)(2,1)S(1)}, bf16[1024,128]{1,0:T(8,128)(2,1)S(1)}, u32[]{:S(2)}, u32[]{:S(2)}) %collective-permute-start.20) | collective-permute-done | bytes 262176 | tf_op jit(solution)/shard_map/ppermute | solution.py:235
  110.2 1.2 %final.1 = bf16[1024,256]{1,0:T(8,128)(2,1)} custom-call(bf16[1024,128]{1,0:T(8,128)(2,1)S(1)} %add_convert_fusion.self_ref, bf16[1024,128]{1,0:T(8,128)(2,1)S(1)} %collective-permute-done.19.one_ref, bf16[1024,128]{1,0:T(8,128)(2,1)S(1)} %collective-permute-done.20.two_ref, bf16[256,256]{1,0:T(8,128)(2,1)S(1)} %copy-done.6), custom_call_target="tpu_custom_call" | custom-call | flops 134217728 | bytes 2097152 | tf_op jit(solution)/shard_map/final/pallas_call | solution.py:212
  (72 shorter events, 7.5 us)
Async XLA Ops:
  0.6 26.9 %collective-permute-start.1 = (bf16[5,8,128,128]{3,2,1,0:T(8,128)(2,1)}, bf16[5,8,128,128]{3,2,1,0:T(8,128)(2,1)S(1)}, u32[]{:S(2)}, u32[]{:S(2)}) collective-permute-start(bf16[5,8,128,128]{3,2,1,0:T(8,128)(2,1)} %bitcast.11), channel_id=1, source_target_pairs={{0,4},{1,0},{2,6},{3,2},{4,5},{5,1},{6,7},{7,3},{8,12},{9,8},{10,1... | collective-permute-start | bytes 3932168 | tf_op jit(solution)/shard_map/ppermute | solution.py:235
  2.8 1.0 copy-start.4
  3.9 1.0 copy-start.5
  5.8 0.7 copy-start.19
  6.5 3.8 %collective-permute-start = (bf16[1024,128]{1,0:T(8,128)(2,1)S(1)}, bf16[1024,128]{1,0:T(8,128)(2,1)S(1)}, u32[]{:S(2)}, u32[]{:S(2)}) collective-permute-start(bf16[1024,128]{1,0:T(8,128)(2,1)S(1)} %get-tuple-element.20), channel_id=1, source_target_pairs={{0,4},{1,5},{2,6},{3,7},{4,0},{5,1},{6,2},{7,3},{8,12},{9,13},{10,... | collective-permute-start | bytes 786440 | tf_op jit(solution)/shard_map/ppermute | solution.py:235
  6.5 8.3 %collective-permute-start.2 = (bf16[1024,128]{1,0:T(8,128)(2,1)S(1)}, bf16[1024,128]{1,0:T(8,128)(2,1)S(1)}, u32[]{:S(2)}, u32[]{:S(2)}) collective-permute-start(bf16[1024,128]{1,0:T(8,128)(2,1)S(1)} %get-tuple-element.23.refs_0_), channel_id=1, source_target_pairs={{0,8},{1,25},{2,10},{3,27},{4,12},{5,13},{6,14},{7,15},{8,16},{9,1... | collective-permute-start | bytes 786440 | tf_op jit(solution)/shard_map/ppermute | solution.py:235
  7.8 13.3 %collective-permute-start.3 = (bf16[1024,128]{1,0:T(8,128)(2,1)S(1)}, bf16[1024,128]{1,0:T(8,128)(2,1)S(1)}, u32[]{:S(2)}, u32[]{:S(2)}) collective-permute-start(bf16[1024,128]{1,0:T(8,128)(2,1)S(1)} %get-tuple-element.20), channel_id=1, source_target_pairs={{0,12},{1,29},{2,14},{3,31},{4,8},{5,9},{6,10},{7,11},{8,20},{9,5}... | collective-permute-start | bytes 786440 | tf_op jit(solution)/shard_map/ppermute | solution.py:235
  9.6 15.4 %collective-permute-start.4 = (bf16[1024,128]{1,0:T(8,128)(2,1)S(1)}, bf16[1024,128]{1,0:T(8,128)(2,1)S(1)}, u32[]{:S(2)}, u32[]{:S(2)}) collective-permute-start(bf16[1024,128]{1,0:T(8,128)(2,1)S(1)} %get-tuple-element.23.refs_0_), channel_id=1, source_target_pairs={{0,24},{2,26},{5,29},{7,31},{8,0},{10,2},{13,5},{15,7},{16,8},{18,... | collective-permute-start | bytes 786440 | tf_op jit(solution)/shard_map/ppermute | solution.py:235
  10.3 16.4 %collective-permute-start.5 = (bf16[1024,128]{1,0:T(8,128)(2,1)S(1)}, bf16[1024,128]{1,0:T(8,128)(2,1)S(1)}, u32[]{:S(2)}, u32[]{:S(2)}) collective-permute-start(bf16[1024,128]{1,0:T(8,128)(2,1)S(1)} %get-tuple-element.20), channel_id=1, source_target_pairs={{0,28},{2,30},{5,25},{7,27},{8,4},{10,6},{13,1},{15,3},{16,12},{18... | collective-permute-start | bytes 786440 | tf_op jit(solution)/shard_map/ppermute | solution.py:235
  14.8 12.7 %collective-permute-start.6 = (s32[2,40]{1,0:T(2,128)}, s32[2,40]{1,0:T(2,128)S(1)}, u32[]{:S(2)}, u32[]{:S(2)}) collective-permute-start(s32[2,40]{1,0:T(2,128)} %slot_blocks.1), channel_id=1, source_target_pairs={{0,4},{1,0},{2,6},{3,2},{4,5},{5,1},{6,7},{7,3},{8,12},{9,8},{10,1... | collective-permute-start | bytes 968 | tf_op jit(solution)/shard_map/ppermute | solution.py:235
  21.1 0.7 copy-start.7
  21.8 5.7 %collective-permute-start.7 = (s32[2,40]{1,0:T(2,128)}, s32[2,40]{1,0:T(2,128)S(1)}, u32[]{:S(2)}, u32[]{:S(2)}) collective-permute-start(s32[2,40]{1,0:T(2,128)} %slot_blocks.1), channel_id=1, source_target_pairs={{1,4},{3,6},{4,1},{6,3},{9,12},{11,14},{12,9},{14,11},{17,20},{19,... | collective-permute-start | bytes 968 | tf_op jit(solution)/shard_map/ppermute | solution.py:235
  25.1 0.7 copy-start.9
  26.8 0.7 copy-start.11
  27.5 4.9 %collective-permute-start.8 = (bf16[5,8,128,128]{3,2,1,0:T(8,128)(2,1)S(1)}, bf16[5,8,128,128]{3,2,1,0:T(8,128)(2,1)S(1)}, u32[]{:S(2)}, u32[]{:S(2)}) collective-permute-start(bf16[5,8,128,128]{3,2,1,0:T(8,128)(2,1)S(1)} %collective-permute-done.1.first_ref), channel_id=1, source_target_pairs={{0,4},{2,6},{5,1},{7,3},{8,12},{10,14},{13,9},{15,11},{16,20},{18,... | collective-permute-start | bytes 3932168 | tf_op jit(solution)/shard_map/ppermute | solution.py:235
  32.4 1.3 %copy-start = (bf16[1,5,8,128,128]{4,3,2,1,0:T(8,128)(2,1)S(1)}, bf16[1,5,8,128,128]{4,3,2,1,0:T(8,128)(2,1)}, u32[]{:S(2)}) copy-start(bf16[1,5,8,128,128]{4,3,2,1,0:T(8,128)(2,1)} %param.9) | copy-start | bytes 3932164
  33.7 0.9 copy-start.8
  34.7 0.9 copy-start.10
  35.6 0.9 copy-start.12
  36.6 1.8 %copy-start.2 = (bf16[5,8,128,128]{3,2,1,0:T(8,128)(2,1)}, bf16[5,8,128,128]{3,2,1,0:T(8,128)(2,1)S(1)}, u32[]{:S(2)}) copy-start(bf16[5,8,128,128]{3,2,1,0:T(8,128)(2,1)S(1)} %collective-permute-done.8.second_ref) | copy-start | bytes 3932164
  36.6 4.1 %copy-start.20 = (bf16[1024,128]{1,0:T(8,128)(2,1)S(1)}, bf16[1024,128]{1,0:T(8,128)(2,1)}, u32[]{:S(2)}) copy-start(bf16[1024,128]{1,0:T(8,128)(2,1)} %copy-done.19) | copy-start | bytes 786436
  36.6 18.4 %copy-start.6 = (bf16[256,256]{1,0:T(8,128)(2,1)S(1)}, bf16[256,256]{1,0:T(8,128)(2,1)}, u32[]{:S(2)}) copy-start(bf16[256,256]{1,0:T(8,128)(2,1)} %w_ref.3) | copy-start | bytes 393220
  36.6 18.4 %copy-start.14 = (bf16[1024,128]{1,0:T(8,128)(2,1)S(1)}, bf16[1024,128]{1,0:T(8,128)(2,1)}, u32[]{:S(2)}) copy-start(bf16[1024,128]{1,0:T(8,128)(2,1)} %copy-done.13) | copy-start | bytes 786436
  38.4 14.4 %collective-permute-start.9 = (bf16[1024,128]{1,0:T(8,128)(2,1)S(1)}, bf16[1024,128]{1,0:T(8,128)(2,1)S(1)}, u32[]{:S(2)}, u32[]{:S(2)}) collective-permute-start(bf16[1024,128]{1,0:T(8,128)(2,1)S(1)} %tile_product.2), channel_id=1, source_target_pairs={{0,2},{1,3},{2,0},{3,1},{4,6},{5,7},{6,4},{7,5},{8,10},{9,11},{10,... | collective-permute-start | bytes 786440 | tf_op jit(solution)/shard_map/ppermute | solution.py:235
  40.7 13.1 %collective-permute-start.11 = (bf16[1024,128]{1,0:T(8,128)(2,1)S(1)}, bf16[1024,128]{1,0:T(8,128)(2,1)S(1)}, u32[]{:S(2)}, u32[]{:S(2)}) collective-permute-start(bf16[1024,128]{1,0:T(8,128)(2,1)S(1)} %copy-done.20), channel_id=1, source_target_pairs={{0,4},{1,5},{2,6},{3,7},{4,0},{5,1},{6,2},{7,3},{8,12},{9,13},{10,... | collective-permute-start | bytes 786440 | tf_op jit(solution)/shard_map/ppermute | solution.py:235
  52.8 27.4 %copy-start.1 = (bf16[1,5,8,128,128]{4,3,2,1,0:T(8,128)(2,1)S(1)}, bf16[1,5,8,128,128]{4,3,2,1,0:T(8,128)(2,1)}, u32[]{:S(2)}) copy-start(bf16[1,5,8,128,128]{4,3,2,1,0:T(8,128)(2,1)} %param.9) | copy-start | bytes 3932164
  52.8 2.2 %collective-permute-start.10 = (bf16[1024,128]{1,0:T(8,128)(2,1)S(1)}, bf16[1024,128]{1,0:T(8,128)(2,1)S(1)}, u32[]{:S(2)}, u32[]{:S(2)}) collective-permute-start(bf16[1024,128]{1,0:T(8,128)(2,1)S(1)} %add_convert_fusion.1.near_ref), channel_id=1, source_target_pairs={{0,4},{1,5},{2,6},{3,7},{4,0},{5,1},{6,2},{7,3},{8,12},{9,13},{10,... | collective-permute-start | bytes 786440 | tf_op jit(solution)/shard_map/ppermute | solution.py:235
  55.3 9.4 %copy-start.15 = (bf16[1024,128]{1,0:T(8,128)(2,1)}, bf16[1024,128]{1,0:T(8,128)(2,1)S(1)}, u32[]{:S(2)}) copy-start(bf16[1024,128]{1,0:T(8,128)(2,1)S(1)} %get-tuple-element.35) | copy-start | bytes 786436
  55.4 7.6 %collective-permute-start.14 = (bf16[1024,128]{1,0:T(8,128)(2,1)S(1)}, bf16[1024,128]{1,0:T(8,128)(2,1)S(1)}, u32[]{:S(2)}, u32[]{:S(2)}) collective-permute-start(bf16[1024,128]{1,0:T(8,128)(2,1)S(1)} %get-tuple-element.36.refs_0_.adj_ref), channel_id=1, source_target_pairs={{0,1},{1,0},{2,3},{3,2},{4,5},{5,4},{6,7},{7,6},{8,9},{9,8},{10,11... | collective-permute-start | bytes 786440 | tf_op jit(solution)/shard_map/ppermute | solution.py:235
  55.6 9.1 %collective-permute-start.15 = (bf16[1024,128]{1,0:T(8,128)(2,1)S(1)}, bf16[1024,128]{1,0:T(8,128)(2,1)S(1)}, u32[]{:S(2)}, u32[]{:S(2)}) collective-permute-start(bf16[1024,128]{1,0:T(8,128)(2,1)S(1)} %get-tuple-element.36.refs_0_.adj_ref), channel_id=1, source_target_pairs={{0,8},{1,9},{2,10},{3,11},{4,12},{5,13},{6,14},{7,15},{8,16},{9,17... | collective-permute-start | bytes 786440 | tf_op jit(solution)/shard_map/ppermute | solution.py:235
  57.0 17.5 %collective-permute-start.16 = (bf16[1024,128]{1,0:T(8,128)(2,1)S(1)}, bf16[1024,128]{1,0:T(8,128)(2,1)}, u32[]{:S(2)}, u32[]{:S(2)}) collective-permute-start(bf16[1024,128]{1,0:T(8,128)(2,1)S(1)} %get-tuple-element.36.refs_0_.adj_ref), channel_id=1, source_target_pairs={{0,24},{1,25},{2,26},{3,27},{4,28},{5,29},{6,30},{7,31},{8,0},{9,1... | collective-permute-start | bytes 786440 | tf_op jit(solution)/shard_map/ppermute | solution.py:235
  58.0 19.2 %collective-permute-start.17 = (bf16[1024,128]{1,0:T(8,128)(2,1)S(1)}, bf16[1024,128]{1,0:T(8,128)(2,1)}, u32[]{:S(2)}, u32[]{:S(2)}) collective-permute-start(bf16[1024,128]{1,0:T(8,128)(2,1)S(1)} %get-tuple-element.36.refs_0_.adj_ref), channel_id=1, source_target_pairs={{0,25},{1,8},{2,27},{3,10},{4,29},{5,12},{6,31},{7,14},{8,1},{9,16... | collective-permute-start | bytes 786440 | tf_op jit(solution)/shard_map/ppermute | solution.py:235
  63.2 21.5 %collective-permute-start.21 = (f32[128,128]{1,0:T(8,128)S(1)}, f32[128,128]{1,0:T(8,128)S(1)}, u32[]{:S(2)}, u32[]{:S(2)}) collective-permute-start(f32[128,128]{1,0:T(8,128)S(1)} %grad_block.1), channel_id=1, source_target_pairs={{0,8},{1,9},{2,10},{3,11},{4,12},{5,13},{6,14},{7,15},{8,0},{9,1},... | collective-permute-start | bytes 196616 | tf_op jit(solution)/shard_map/ppermute | solution.py:235
  64.5 22.3 %collective-permute-start.22 = (f32[128,128]{1,0:T(8,128)S(1)}, f32[128,128]{1,0:T(8,128)S(1)}, u32[]{:S(2)}, u32[]{:S(2)}) collective-permute-start(f32[128,128]{1,0:T(8,128)S(1)} %grad_block.1), channel_id=1, source_target_pairs={{0,16},{1,17},{2,18},{3,19},{4,20},{5,21},{6,22},{7,23},{8,24},{9,... | collective-permute-start | bytes 196616 | tf_op jit(solution)/shard_map/ppermute | solution.py:235
  64.7 0.7 copy-start.17
  65.4 21.4 %collective-permute-start.23 = (f32[128,128]{1,0:T(8,128)S(1)}, f32[128,128]{1,0:T(8,128)}, u32[]{:S(2)}, u32[]{:S(2)}) collective-permute-start(f32[128,128]{1,0:T(8,128)S(1)} %grad_block.1), channel_id=1, source_target_pairs={{0,24},{1,25},{2,26},{3,27},{4,28},{5,29},{6,30},{7,31},{8,16},{9,... | collective-permute-start | bytes 196616 | tf_op jit(solution)/shard_map/ppermute | solution.py:235
  74.6 13.2 %collective-permute-start.12 = (bf16[1024,128]{1,0:T(8,128)(2,1)}, bf16[1024,128]{1,0:T(8,128)(2,1)S(1)}, u32[]{:S(2)}, u32[]{:S(2)}) collective-permute-start(bf16[1024,128]{1,0:T(8,128)(2,1)} %copy-done.15), channel_id=1, source_target_pairs={{0,1},{1,5},{2,3},{3,7},{4,0},{5,4},{6,2},{7,6},{8,9},{9,13},{10,1... | collective-permute-start | bytes 786440 | tf_op jit(solution)/shard_map/ppermute | solution.py:235
  77.2 10.5 %collective-permute-start.13 = (bf16[1024,128]{1,0:T(8,128)(2,1)}, bf16[1024,128]{1,0:T(8,128)(2,1)S(1)}, u32[]{:S(2)}, u32[]{:S(2)}) collective-permute-start(bf16[1024,128]{1,0:T(8,128)(2,1)} %copy-done.15), channel_id=1, source_target_pairs={{1,4},{3,6},{4,1},{6,3},{9,12},{11,14},{12,9},{14,11},{17,20},{19,... | collective-permute-start | bytes 786440 | tf_op jit(solution)/shard_map/ppermute | solution.py:235
  80.2 1.3 %copy-start.3 = (bf16[5,8,128,128]{3,2,1,0:T(8,128)(2,1)S(1)}, bf16[5,8,128,128]{3,2,1,0:T(8,128)(2,1)}, u32[]{:S(2)}) copy-start(bf16[5,8,128,128]{3,2,1,0:T(8,128)(2,1)} %copy-done.2) | copy-start | bytes 3932164
  81.5 0.9 copy-start.18
  82.5 5.3 %copy-start.16 = (bf16[1024,128]{1,0:T(8,128)(2,1)S(1)}, bf16[1024,128]{1,0:T(8,128)(2,1)}, u32[]{:S(2)}) copy-start(bf16[1024,128]{1,0:T(8,128)(2,1)} %copy-done.15) | copy-start | bytes 786436
  84.7 17.3 %collective-permute-start.18 = (bf16[1024,128]{1,0:T(8,128)(2,1)S(1)}, bf16[1024,128]{1,0:T(8,128)(2,1)S(1)}, u32[]{:S(2)}, u32[]{:S(2)}) collective-permute-start(bf16[1024,128]{1,0:T(8,128)(2,1)S(1)} %tile_product.3), channel_id=1, source_target_pairs={{0,2},{1,3},{2,0},{3,1},{4,6},{5,7},{6,4},{7,5},{8,10},{9,11},{10,... | collective-permute-start | bytes 786440 | tf_op jit(solution)/shard_map/ppermute | solution.py:235
  87.7 5.9 %collective-permute-start.24 = (f32[128,128]{1,0:T(8,128)S(1)}, f32[128,128]{1,0:T(8,128)S(1)}, u32[]{:S(2)}, u32[]{:S(2)}) collective-permute-start(f32[128,128]{1,0:T(8,128)S(1)} %add_add_fusion), channel_id=1, source_target_pairs={{0,1},{1,0},{2,3},{3,2},{4,5},{5,4},{6,7},{7,6},{8,9},{9,8},{10,11... | collective-permute-start | bytes 196616 | tf_op jit(solution)/shard_map/ppermute | solution.py:235
  93.6 8.4 %collective-permute-start.25 = (f32[128,128]{1,0:T(8,128)S(1)}, f32[128,128]{1,0:T(8,128)S(1)}, u32[]{:S(2)}, u32[]{:S(2)}) collective-permute-start(f32[128,128]{1,0:T(8,128)S(1)} %add.33), channel_id=1, source_target_pairs={{0,2},{1,3},{2,0},{3,1},{4,6},{5,7},{6,4},{7,5},{8,10},{9,11},{10,... | collective-permute-start | bytes 196616 | tf_op jit(solution)/shard_map/ppermute | solution.py:235
  94.6 9.8 %collective-permute-start.26 = (f32[128,128]{1,0:T(8,128)S(1)}, f32[128,128]{1,0:T(8,128)S(1)}, u32[]{:S(2)}, u32[]{:S(2)}) collective-permute-start(f32[128,128]{1,0:T(8,128)S(1)} %add.33), channel_id=1, source_target_pairs={{0,4},{1,5},{2,6},{3,7},{4,0},{5,1},{6,2},{7,3},{8,12},{9,13},{10,... | collective-permute-start | bytes 196616 | tf_op jit(solution)/shard_map/ppermute | solution.py:235
  97.1 7.3 %collective-permute-start.27 = (f32[128,128]{1,0:T(8,128)S(1)}, f32[128,128]{1,0:T(8,128)S(1)}, u32[]{:S(2)}, u32[]{:S(2)}) collective-permute-start(f32[128,128]{1,0:T(8,128)S(1)} %add.33), channel_id=1, source_target_pairs={{0,6},{1,7},{2,4},{3,5},{4,2},{5,3},{6,0},{7,1},{8,14},{9,15},{10,... | collective-permute-start | bytes 196616 | tf_op jit(solution)/shard_map/ppermute | solution.py:235
  102.1 5.3 %collective-permute-start.19 = (bf16[1024,128]{1,0:T(8,128)(2,1)S(1)}, bf16[1024,128]{1,0:T(8,128)(2,1)S(1)}, u32[]{:S(2)}, u32[]{:S(2)}) collective-permute-start(bf16[1024,128]{1,0:T(8,128)(2,1)S(1)} %add_convert_fusion.self_ref), channel_id=1, source_target_pairs={{0,1},{1,5},{2,3},{3,7},{4,0},{5,4},{6,2},{7,6},{8,9},{9,13},{10,1... | collective-permute-start | bytes 786440 | tf_op jit(solution)/shard_map/ppermute | solution.py:235
  102.5 7.7 %collective-permute-start.20 = (bf16[1024,128]{1,0:T(8,128)(2,1)S(1)}, bf16[1024,128]{1,0:T(8,128)(2,1)S(1)}, u32[]{:S(2)}, u32[]{:S(2)}) collective-permute-start(bf16[1024,128]{1,0:T(8,128)(2,1)S(1)} %add_convert_fusion.self_ref), channel_id=1, source_target_pairs={{1,4},{3,6},{4,1},{6,3},{9,12},{11,14},{12,9},{14,11},{17,20},{19,... | collective-permute-start | bytes 786440 | tf_op jit(solution)/shard_map/ppermute | solution.py:235
  (1 other events, 0.7 us)

commit v3 on v2

v3 whole, which is shorter than its diff:
```python
import functools

import jax
import jax.numpy as jnp
from jax import lax
from jax.experimental import pallas as pl
from jax.experimental.pallas import tpu as pltpu
from jax.sharding import PartitionSpec as P

AXES = ("rows", "rep")


def route(shape, move):
    chips, reps = shape
    pairs = []
    for c in range(chips):
        for j in range(2):
            for z in range(reps):
                to = move(c, j, z)
                if to is not None:
                    target = ((to[0] % chips) * 2 + to[1]) * reps + to[2]
                    pairs.append(((c * 2 + j) * reps + z, target))
    return pairs


def place():
    r = lax.axis_index("rows")
    z = lax.axis_index("rep")
    return r % 2, z, z % 2


def halves_kernel(x_ref, near_ref, far_ref, sems):
    j, _, _ = place()
    half = near_ref.shape[1]
    copies = []
    for i, out in enumerate((near_ref, far_ref)):
        start = pl.multiple_of((j if i == 0 else 1 - j) * half, half)
        copy = pltpu.make_async_copy(x_ref.at[:, pl.ds(start, half)], out, sems.at[i])
        copy.start()
        copies.append(copy)
    for copy in copies:
        copy.wait()


def halves(value):
    rows, width = value.shape
    part = jax.ShapeDtypeStruct((rows, width // 2), value.dtype)
    hbm = pl.BlockSpec(memory_space=pltpu.HBM)
    return pl.pallas_call(
        halves_kernel,
        out_shape=(part, part),
        in_specs=[hbm],
        out_specs=(hbm, hbm),
        scratch_shapes=[pltpu.SemaphoreType.DMA((2,))],
        compiler_params=pltpu.CompilerParams(vmem_limit_bytes=1024 * 1024),
        name="halves",
    )(value)


def pick_kernel(home_ref, away_ref, out_ref, sem):
    j, _, p = place()

    @pl.when(j == p)
    def _():
        copy = pltpu.make_async_copy(home_ref, out_ref, sem)
        copy.start()
        copy.wait()

    @pl.when(j != p)
    def _():
        copy = pltpu.make_async_copy(away_ref, out_ref, sem)
        copy.start()
        copy.wait()


def pick(home, away):
    hbm = pl.BlockSpec(memory_space=pltpu.HBM)
    return pl.pallas_call(
        pick_kernel,
        out_shape=jax.ShapeDtypeStruct(home.shape, home.dtype),
        in_specs=[hbm, hbm],
        out_specs=hbm,
        scratch_shapes=[pltpu.SemaphoreType.DMA],
        compiler_params=pltpu.CompilerParams(vmem_limit_bytes=1024 * 1024),
        name="pick",
    )(home, away)


def slots_kernel(dead, coords_ref, counts_ref, out_ref):
    _, z, _ = place()
    _, reach, slots = coords_ref.shape
    for d in range(reach):
        for k in range(slots):
            live = z * slots + k < counts_ref[d]
            out_ref[0, d * slots + k] = jnp.where(live, coords_ref[0, d, k], dead)
            out_ref[1, d * slots + k] = coords_ref[1, d, k]


def slot_blocks(coords, counts, dead):
    smem = pl.BlockSpec(memory_space=pltpu.SMEM)
    return pl.pallas_call(
        functools.partial(slots_kernel, dead),
        out_shape=jax.ShapeDtypeStruct((2, coords.shape[1] * coords.shape[2]), jnp.int32),
        in_specs=[smem, smem],
        out_specs=smem,
        compiler_params=pltpu.CompilerParams(vmem_limit_bytes=1024 * 1024),
        name="slot_blocks",
    )(coords, counts)


def offset_of(kind):
    j, _, p = place()
    home = j == p
    near, far = jnp.where(p == 0, 3, 1), jnp.where(p == 0, 1, 3)
    return {
        "self": 2,
        "left": 0,
        "right": 4,
        "near": near,
        "far": far,
        "mine": jnp.where(home, 2, near),
        "swapped": jnp.where(home, near, 2),
        "one": jnp.where(home, 0, far),
        "two": jnp.where(home, far, 0),
    }[kind]


def tile_kernel(kinds, sets, summed, *refs):
    refs = list(refs)
    metas = [refs.pop(0) for _ in range(sum(len(s) for s in sets))]
    tiles = [refs.pop(0) for _ in range(sum(len(s) for s in sets))]
    panels = [refs.pop(0) for _ in kinds]
    before = refs.pop(0) if summed else None
    out_ref, acc_ref, tile_buf, panel_buf, tile_sems, panel_sems = refs
    slots, tile = tile_buf.shape[2], tile_buf.shape[-1]
    rows = out_ref.shape[0]
    j, _, p = place()
    home = j == p
    offsets = [offset_of(kind) for kind in kinds]

    def tile_copy(ref, i, s):
        return pltpu.make_async_copy(ref.at[offsets[i]], tile_buf.at[i, s], tile_sems.at[i, s])

    def panel_copy(i):
        return pltpu.make_async_copy(panels[i], panel_buf.at[i], panel_sems.at[i])

    for i in range(len(kinds)):
        panel_copy(i).start()
        at = 0
        for s, members in enumerate(sets):
            if len(members) == 1:
                tile_copy(tiles[at], i, s).start()
            else:

                @pl.when(home)
                def _(ref=tiles[at], i=i, s=s):
                    tile_copy(ref, i, s).start()

                @pl.when(jnp.logical_not(home))
                def _(ref=tiles[at + 1], i=i, s=s):
                    tile_copy(ref, i, s).start()

            at += len(members)
    if summed:
        acc_ref[:rows, :] = before[...]
    else:
        acc_ref[...] = jnp.zeros_like(acc_ref)
    for i in range(len(kinds)):
        d = offsets[i]
        panel_copy(i).wait()
        at = 0
        for s, members in enumerate(sets):
            tile_copy(tiles[at], i, s).wait()
            for k in range(slots):
                row = metas[at][0, d * slots + k]
                col = metas[at][1, d * slots + k]
                if len(members) == 2:
                    row = jnp.where(home, row, metas[at + 1][0, d * slots + k])
                    col = jnp.where(home, col, metas[at + 1][1, d * slots + k])
                row = pl.multiple_of(row * tile, tile)
                col = pl.multiple_of(col * tile, tile)
                prod = jnp.dot(
                    tile_buf[i, s, k],
                    panel_buf[i, pl.ds(col, tile), :],
                    preferred_element_type=jnp.float32,
                )
                acc_ref[pl.ds(row, tile), :] += prod
            at += len(members)
    out_ref[...] = acc_ref[:rows, :].astype(out_ref.dtype)


def tile_product(named, sets, dtype, before=None):
    kinds = [kind for kind, _ in named]
    panels = [panel for _, panel in named]
    metas = [meta for members in sets for meta, _ in members]
    tiles = [values for members in sets for _, values in members]
    rows, width = panels[0].shape
    _, slots, tile, _ = tiles[0].shape
    smem = pl.BlockSpec(memory_space=pltpu.SMEM)
    vmem = pl.BlockSpec(memory_space=pltpu.VMEM)
    hbm = pl.BlockSpec(memory_space=pltpu.HBM)
    anywhere = pl.BlockSpec(memory_space=pl.ANY)
    count = len(kinds) * len(sets) * slots
    summed = before is not None
    return pl.pallas_call(
        functools.partial(tile_kernel, kinds, [[0] * len(m) for m in sets], summed),
        out_shape=jax.ShapeDtypeStruct((rows, width), dtype),
        in_specs=[smem] * len(metas)
        + [hbm] * len(tiles)
        + [anywhere] * len(panels)
        + [vmem] * summed,
        out_specs=vmem,
        scratch_shapes=[
            pltpu.VMEM((rows + tile, width), jnp.float32),
            pltpu.VMEM((len(kinds), len(sets), slots, tile, tile), tiles[0].dtype),
            pltpu.VMEM((len(kinds), rows, width), panels[0].dtype),
            pltpu.SemaphoreType.DMA((len(kinds), len(sets))),
            pltpu.SemaphoreType.DMA((len(kinds),)),
        ],
        compiler_params=pltpu.CompilerParams(vmem_limit_bytes=8 * 1024 * 1024),
        cost_estimate=pl.CostEstimate(
            flops=2 * count * tile * tile * width,
            bytes_accessed=count * tile * tile * 2 + len(kinds) * rows * width * 2,
            transcendentals=0,
        ),
        name="tile_product",
    )(*metas, *tiles, *panels, *([before] if summed else []))


def middle_kernel(near_ref, far_ref, w_ref, cot_ref, cot_swap_ref, act_ref, adj_ref):
    j, _, p = place()
    half = near_ref.shape[1]
    near = pl.multiple_of(j * half, half)
    far = pl.multiple_of((1 - j) * half, half)
    cols = pl.ds(near, half)
    agg = jnp.dot(
        near_ref[...], w_ref[pl.ds(near, half), cols], preferred_element_type=jnp.float32
    )
    agg += jnp.dot(far_ref[...], w_ref[pl.ds(far, half), cols], preferred_element_type=jnp.float32)
    sig = jax.nn.sigmoid(agg)
    act_ref[...] = (agg * sig).astype(act_ref.dtype)
    slope = sig * (1.0 + agg * (1.0 - sig))
    cot = jnp.where(j == p, cot_ref[...], cot_swap_ref[...])
    adj_ref[...] = (cot.astype(jnp.float32) * slope).astype(adj_ref.dtype)


def middle(near, far, weight, cot, cot_swap):
    vmem = pl.BlockSpec(memory_space=pltpu.VMEM)
    rows, width = near.shape
    out = jax.ShapeDtypeStruct((rows, width), jnp.bfloat16)
    return pl.pallas_call(
        middle_kernel,
        out_shape=(out, out),
        in_specs=[vmem] * 5,
        out_specs=(vmem, vmem),
        compiler_params=pltpu.CompilerParams(vmem_limit_bytes=8 * 1024 * 1024),
        cost_estimate=pl.CostEstimate(
            flops=4 * rows * width * width,
            bytes_accessed=10 * rows * width,
            transcendentals=rows * width,
        ),
        name="middle",
    )(near, far, weight, cot, cot_swap)


def grad_kernel(scale, near_ref, far_ref, adj_ref, after_ref, out_ref):
    j, _, _ = place()
    half = near_ref.shape[1]
    dims = (((0,), (0,)), ((), ()))
    for i, ref in enumerate((near_ref, far_ref)):
        start = pl.multiple_of((j if i == 0 else 1 - j) * half, half)
        out_ref[pl.ds(start, half), :] = scale * lax.dot_general(
            ref[...], adj_ref[...], dims, preferred_element_type=jnp.float32
        )


def grad_block(scale, near, far, adj, after):
    vmem = pl.BlockSpec(memory_space=pltpu.VMEM)
    rows, width = near.shape
    return pl.pallas_call(
        functools.partial(grad_kernel, scale),
        out_shape=jax.ShapeDtypeStruct((2 * width, width), jnp.float32),
        in_specs=[vmem] * 3 + [pl.BlockSpec(memory_space=pl.ANY)],
        out_specs=vmem,
        compiler_params=pltpu.CompilerParams(vmem_limit_bytes=8 * 1024 * 1024),
        cost_estimate=pl.CostEstimate(
            flops=4 * rows * width * width, bytes_accessed=8 * rows * width, transcendentals=0
        ),
        name="grad_block",
    )(near, far, adj, after)


def add_kernel(first_ref, second_ref, after_ref, out_ref):
    out_ref[...] = first_ref[...] + second_ref[...]


def add_after(first, second, after):
    vmem = pl.BlockSpec(memory_space=pltpu.VMEM)
    return pl.pallas_call(
        add_kernel,
        out_shape=jax.ShapeDtypeStruct(first.shape, first.dtype),
        in_specs=[vmem, vmem, pl.BlockSpec(memory_space=pl.ANY)],
        out_specs=vmem,
        compiler_params=pltpu.CompilerParams(vmem_limit_bytes=1024 * 1024),
        name="add_after",
    )(first, second, after)


def final_kernel(self_ref, one_ref, two_ref, w_ref, out_ref):
    j, _, p = place()
    half = self_ref.shape[1]
    near = jnp.where(j == p, self_ref[...], one_ref[...])
    far = jnp.where(j == p, one_ref[...], two_ref[...])
    w_near = w_ref[:, pl.ds(pl.multiple_of(j * half, half), half)]
    w_far = w_ref[:, pl.ds(pl.multiple_of((1 - j) * half, half), half)]
    dims = (((1,), (1,)), ((), ()))
    total = lax.dot_general(near, w_near, dims, preferred_element_type=jnp.float32)
    total += lax.dot_general(far, w_far, dims, preferred_element_type=jnp.float32)
    out_ref[...] = total.astype(out_ref.dtype)


def final(own, one, two, weight):
    vmem = pl.BlockSpec(memory_space=pltpu.VMEM)
    rows = own.shape[0]
    wide = weight.shape[0]
    return pl.pallas_call(
        final_kernel,
        out_shape=jax.ShapeDtypeStruct((rows, wide), jnp.bfloat16),
        in_specs=[vmem] * 4,
        out_specs=vmem,
        compiler_params=pltpu.CompilerParams(vmem_limit_bytes=8 * 1024 * 1024),
        cost_estimate=pl.CostEstimate(
            flops=2 * rows * wide * wide, bytes_accessed=8 * rows * wide, transcendentals=0
        ),
        name="final",
    )(own, one, two, weight)


def per_device(node_feats, weight, cotangent, tile_values, tile_coords, tile_counts):
    groups = lax.axis_size("rows")
    reps = lax.axis_size("rep")
    shape = (groups // 2, reps)
    j, z, p = place()
    home = j == p
    scale = (node_feats.shape[0] * groups) ** (-0.5)

    def send(value, move):
        return lax.ppermute(value, AXES, route(shape, move))

    def sibling(c, j, z):
        return (c, 1 - j, z)

    def across(c, j, z):
        return (c, j, (z + reps // 2) % reps)

    own = tile_values[0]
    blocks = node_feats.shape[0] // own.shape[-1]

    def to_home(c, j, z):
        return (c, 1 - j, z) if j == z % 2 else (c, j, z ^ 1)

    def forward_x(c, j, z):
        return (c + 1, j, z) if j == z % 2 or z % 2 == 0 else (c - 1, j, z)

    def forward_x_cross(c, j, z):
        to = forward_x(c, j, z)
        return (to[0], 1 - j, to[2])

    first = send(own, to_home)
    mine, yours = halves(node_feats)
    one = send(mine, forward_x)
    two = send(yours, forward_x_cross)
    swapped = send(yours, sibling)
    right = send(pick(mine, swapped), lambda c, j, z: (c - 1, j, z))
    coords, counts, swapped = lax.optimization_barrier((tile_coords, tile_counts, swapped))
    meta = slot_blocks(coords[:, 0], counts[0], blocks)
    meta_b = send(meta, to_home)
    meta_far = send(meta, lambda c, j, z: None if j == z % 2 else (c, 1 - j, z ^ 1))
    first, one, two, right, meta_b, meta_far = lax.optimization_barrier(
        (first, one, two, right, meta_b, meta_far)
    )
    second = send(first, lambda c, j, z: (c, 1 - j, z) if j == z % 2 else None)

    set_first = [(meta_b, first)]
    set_rest = [(meta, own), (meta_far, second)]
    panels = [("mine", mine), ("swapped", swapped), ("one", one), ("two", two), ("right", right)]
    part = tile_product(panels, [set_first], jnp.float32)
    part = tile_product(panels, [set_rest], jnp.bfloat16, part)

    def join(value):
        other = send(value, across)
        return (value.astype(jnp.float32) + other.astype(jnp.float32)).astype(jnp.bfloat16)

    near = join(part)
    far = send(near, sibling)
    cot, cot_yours = halves(cotangent)
    act, adj = middle(near, far, weight, cot, send(cot_yours, sibling))

    left = send(adj, lambda c, j, z: (c + 1, j, z))
    right = send(adj, lambda c, j, z: (c - 1, j, z))
    third = send(adj, lambda c, j, z: (c + 1 if z % 2 else c - 1, j, z ^ 1))
    other = send(adj, lambda c, j, z: (c, j, z ^ 1))
    back_part = tile_product([("self", adj), ("near", other)], [set_first, set_rest], jnp.float32)
    far_panels = [("left", left), ("right", right), ("far", third)]
    back_part = tile_product(far_panels, [set_first, set_rest], jnp.bfloat16, back_part)

    def deliver(value):
        one = send(value, lambda c, j, z: (c, j, z ^ 1) if j == z % 2 else (c, 1 - j, z))
        two = send(value, lambda c, j, z: None if j == z % 2 else (c, 1 - j, z ^ 1))
        return one, two

    act_one, act_two = deliver(act)
    act_near = jnp.where(home, act, act_one)
    act_far = jnp.where(home, act_one, act_two)
    activated = jnp.concatenate(
        [jnp.where(j == 0, act_near, act_far), jnp.where(j == 0, act_far, act_near)], axis=1
    )

    back = join(back_part)
    back_one, back_two = deliver(back)
    input_grad = final(back, back_one, back_two, weight)

    grad = grad_block(scale, near, far, adj, other)
    grad = add_after(grad, send(grad, lambda c, j, z: (c, j, z ^ 1)), back_part)
    step = 1
    while step < shape[0]:
        flips = [step] if step * 2 >= shape[0] else [step, 2 * step, 3 * step]
        got = [send(grad, lambda c, j, z, s=s: (c ^ s, j, z)) for s in flips]
        grad = grad + got[0]
        if len(got) == 3:
            grad = grad + (got[1] + got[2])
        step *= 2 if len(flips) == 1 else 4
    rest = send(grad, sibling)
    weight_grad = jnp.concatenate(
        [jnp.where(j == 0, grad, rest), jnp.where(j == 0, rest, grad)], axis=1
    )
    return (activated, input_grad, weight_grad)


def solution(mesh):
    return jax.shard_map(
        per_device,
        mesh=mesh,
        in_specs=(
            P("rows", None),
            P(),
            P("rows", None),
            P("rows", None, "rep", None, None),
            P(None, "rows", None, "rep"),
            P("rows", None),
        ),
        out_specs=(P("rows", None), P("rows", None), P()),
        check_vma=False,
    )
```

time: 112 us -> 95.6 us (0.85)
  local copies, waits for them, and re-layouts: 14.2 us -> 3.1 us
  waiting for transfers between devices: 47.3 us -> 38.3 us
  Pallas kernels: 7.48 us -> 12.9 us
  starting transfers between devices: 38.7 us -> 37.3 us
    unnamed x42 -> x20, local copies, waits for them, and re-layouts: 12.7 us -> 3.09 us
    ppermute x28 -> x25, waiting for transfers between devices: 47.3 us -> 38.3 us  [send(): return lax.ppermute(value, AXES, route(shape, move))]
    pallas_call x3 -> x8, Pallas kernels: 4.17 us -> 8.94 us  [the longest x4 8.67 us: tile_product(): pl.pallas_call(functools.partial(tile_kernel, kinds, [[0] * len(m) for m...]
    ppermute x28 -> x25, starting transfers between devices: 38.7 us -> 37.3 us  [send(): return lax.ppermute(value, AXES, route(shape, move))]
  transfers between devices with their start and end apart: 28 -> 25, of which waited for: 12 -> 13; matrix products, arithmetic and copies ran while one was open for 4% -> 3% of each run, Pallas kernels for 4% -> 9%
where the time goes in v3:
time: 95.6 us; the launch traced here: 95.3 us
  waiting for transfers between devices  38.3 us (40%)
  starting transfers between devices  37.3 us (39%)
  Pallas kernels  12.9 us (13%)
  local copies, waits for them, and re-layouts  3.1 us (3%)
  other arithmetic  2.85 us (3%)
    ppermute x25, waiting for transfers between devices, send(): return lax.ppermute(value, AXES, route(shape, move))  38.3 us
    ppermute x25, starting transfers between devices, send(): return lax.ppermute(value, AXES, route(shape, move))  37.3 us
    pallas_call x4, Pallas kernels, tile_product(): pl.pallas_call(functools.partial(tile_kernel, kinds, [[0] * len(m) for m...  8.67 us
    unnamed x20, local copies, waits for them, and re-layouts  3.09 us
  transfers between devices with their start and end apart: 25, of which 13 were waited for; matrix products, arithmetic and copies ran while one was open for 3% of the time, Pallas kernels for 9%

profile of v3, /device:TPU:1, one launch (start us, length us, event | category | flops | bytes accessed | tf_op | source)
XLA Modules:
  0.0 95.3 jit_solution(11296896837397874515)
XLA Ops:
  0.6 2.2 %collective-permute-start.1 = (bf16[5,8,128,128]{3,2,1,0:T(8,128)(2,1)}, bf16[5,8,128,128]{3,2,1,0:T(8,128)(2,1)S(1)}, u32[]{:S(2)}, u32[]{:S(2)}) collective-permute-start(bf16[5,8,128,128]{3,2,1,0:T(8,128)(2,1)} %bitcast.5), channel_id=1, source_target_pairs={{0,4},{1,0},{2,6},{3,2},{4,5},{5,1},{6,7},{7,3},{8,12},{9,8},{10,1... | collective-permute-start | bytes 3932168 | tf_op jit(solution)/shard_map/ppermute | solution.py:348
  2.8 1.0 %copy-done.3 = bf16[1024,256]{1,0:T(8,128)(2,1)S(1)} copy-done((bf16[1024,256]{1,0:T(8,128)(2,1)S(1)}, bf16[1024,256]{1,0:T(8,128)(2,1)}, u32[]{:S(2)}) %copy-start.3) | copy-done | bytes 524312
  4.1 1.3 %collective-permute-start.2 = (bf16[1024,128]{1,0:T(8,128)(2,1)S(1)}, bf16[1024,128]{1,0:T(8,128)(2,1)S(1)}, u32[]{:S(2)}, u32[]{:S(2)}) collective-permute-start(bf16[1024,128]{1,0:T(8,128)(2,1)S(1)} %get-tuple-element.21.home_ref.refs_2_.refs_4_), channel_id=1, source_target_pairs={{0,8},{1,25},{2,10},{3,27},{4,12},{5,13},{6,14},{7,15},{8,16},{9,1... | collective-permute-start | bytes 786440 | tf_op jit(solution)/shard_map/ppermute | solution.py:348
  5.3 1.8 %collective-permute-start.3 = (bf16[1024,128]{1,0:T(8,128)(2,1)S(1)}, bf16[1024,128]{1,0:T(8,128)(2,1)S(1)}, u32[]{:S(2)}, u32[]{:S(2)}) collective-permute-start(bf16[1024,128]{1,0:T(8,128)(2,1)S(1)} %get-tuple-element.18), channel_id=1, source_target_pairs={{0,12},{1,29},{2,14},{3,31},{4,8},{5,9},{6,10},{7,11},{8,20},{9,5}... | collective-permute-start | bytes 786440 | tf_op jit(solution)/shard_map/ppermute | solution.py:348
  7.2 1.2 %collective-permute-start.4 = (bf16[1024,128]{1,0:T(8,128)(2,1)S(1)}, bf16[1024,128]{1,0:T(8,128)(2,1)S(1)}, u32[]{:S(2)}, u32[]{:S(2)}) collective-permute-start(bf16[1024,128]{1,0:T(8,128)(2,1)S(1)} %pick.1), channel_id=1, source_target_pairs={{0,24},{1,25},{2,26},{3,27},{4,28},{5,29},{6,30},{7,31},{8,0},{9,1... | collective-permute-start | bytes 786440 | tf_op jit(solution)/shard_map/ppermute | solution.py:348
  8.4 1.3 %slot_blocks.1.refs_0_.refs_1_ = s32[2,40]{1,0:T(2,128)S(1)} custom-call(s32[2,5,8]{2,1,0:T(8,128)S(1)} %copy.10.coords_ref, s32[5]{0:T(128)S(1)} %bitcast.9), custom_call_target="tpu_custom_call" | custom-call | tf_op jit(solution)/shard_map/slot_blocks/pallas_call | solution.py:101
  9.8 1.7 %collective-permute-start.5 = (s32[2,40]{1,0:T(2,128)S(1)}, s32[2,40]{1,0:T(2,128)S(1)}, u32[]{:S(2)}, u32[]{:S(2)}) collective-permute-start(s32[2,40]{1,0:T(2,128)S(1)} %slot_blocks.1.refs_0_.refs_1_), channel_id=1, source_target_pairs={{0,4},{1,0},{2,6},{3,2},{4,5},{5,1},{6,7},{7,3},{8,12},{9,8},{10,1... | collective-permute-start | bytes 968 | tf_op jit(solution)/shard_map/ppermute | solution.py:348
  11.5 1.0 %collective-permute-done.2.refs_4_.refs_6_ = bf16[1024,128]{1,0:T(8,128)(2,1)S(1)} collective-permute-done((bf16[1024,128]{1,0:T(8,128)(2,1)S(1)}, bf16[1024,128]{1,0:T(8,128)(2,1)S(1)}, u32[]{:S(2)}, u32[]{:S(2)}) %collective-permute-start.2) | collective-permute-done | bytes 262176 | tf_op jit(solution)/shard_map/ppermute | solution.py:348
  12.5 3.8 %collective-permute-start.6 = (s32[2,40]{1,0:T(2,128)S(1)}, s32[2,40]{1,0:T(2,128)S(1)}, u32[]{:S(2)}, u32[]{:S(2)}) collective-permute-start(s32[2,40]{1,0:T(2,128)S(1)} %slot_blocks.1.refs_0_.refs_1_), channel_id=1, source_target_pairs={{1,4},{3,6},{4,1},{6,3},{9,12},{11,14},{12,9},{14,11},{17,20},{19,... | collective-permute-start | bytes 968 | tf_op jit(solution)/shard_map/ppermute | solution.py:348
  16.2 3.3 %collective-permute-done.3.refs_5_.refs_7_ = bf16[1024,128]{1,0:T(8,128)(2,1)S(1)} collective-permute-done((bf16[1024,128]{1,0:T(8,128)(2,1)S(1)}, bf16[1024,128]{1,0:T(8,128)(2,1)S(1)}, u32[]{:S(2)}, u32[]{:S(2)}) %collective-permute-start.3) | collective-permute-done | bytes 262176 | tf_op jit(solution)/shard_map/ppermute | solution.py:348
  19.6 4.2 %collective-permute-done.4.refs_6_.refs_8_ = bf16[1024,128]{1,0:T(8,128)(2,1)S(1)} collective-permute-done((bf16[1024,128]{1,0:T(8,128)(2,1)S(1)}, bf16[1024,128]{1,0:T(8,128)(2,1)S(1)}, u32[]{:S(2)}, u32[]{:S(2)}) %collective-permute-start.4) | collective-permute-done | bytes 262176 | tf_op jit(solution)/shard_map/ppermute | solution.py:348
  23.8 1.3 %collective-permute-start.7 = (bf16[5,8,128,128]{3,2,1,0:T(8,128)(2,1)S(1)}, bf16[5,8,128,128]{3,2,1,0:T(8,128)(2,1)S(1)}, u32[]{:S(2)}, u32[]{:S(2)}) collective-permute-start(bf16[5,8,128,128]{3,2,1,0:T(8,128)(2,1)S(1)} %collective-permute-done.1.refs_1_.refs_3_), channel_id=1, source_target_pairs={{0,4},{2,6},{5,1},{7,3},{8,12},{10,14},{13,9},{15,11},{16,20},{18,... | collective-permute-start | bytes 3932168 | tf_op jit(solution)/shard_map/ppermute | solution.py:348
  25.0 2.1 %tile_product.4.refs_9_ = f32[1024,128]{1,0:T(8,128)S(1)} custom-call(s32[2,40]{1,0:T(2,128)S(1)} %collective-permute-done.5.refs_0_, bf16[5,8,128,128]{3,2,1,0:T(8,128)(2,1)S(1)} %collective-permute-done.1.refs_1_.refs_3_, bf16[1024,128]{1,0:T(8,128)(2,1)S(1)} %get-tuple-element.21.home_ref.refs_2_.refs_4_, ...), custom_call_target="tpu_custom_call" | custom-call | flops 167772160 | bytes 2621440 | tf_op jit(solution)/shard_map/tile_product/pallas_call | solution.py:205
  27.2 1.7 %collective-permute-done.7.refs_3_.refs_5_ = bf16[5,8,128,128]{3,2,1,0:T(8,128)(2,1)S(1)} collective-permute-done((bf16[5,8,128,128]{3,2,1,0:T(8,128)(2,1)S(1)}, bf16[5,8,128,128]{3,2,1,0:T(8,128)(2,1)S(1)}, u32[]{:S(2)}, u32[]{:S(2)}) %collective-permute-start.7) | collective-permute-done | bytes 1310752 | tf_op jit(solution)/shard_map/ppermute | solution.py:348
  28.8 2.1 %tile_product.5 = bf16[1024,128]{1,0:T(8,128)(2,1)S(1)} custom-call(s32[2,40]{1,0:T(2,128)S(1)} %slot_blocks.1.refs_0_.refs_1_, s32[2,40]{1,0:T(2,128)S(1)} %collective-permute-done.6.refs_1_.refs_2_, bf16[5,8,128,128]{3,2,1,0:T(8,128)(2,1)S(1)} %bitcast.6, bf16[5,8,128,128]{3,2,1,0:T(8,128)(2,1)S(1)} %collective-permute-done.7.refs_3_.refs_5_, ...), custom_call_target="tpu_custom_call" | custom-call | flops 167772160 | bytes 2621440 | tf_op jit(solution)/shard_map/tile_product/pallas_call | solution.py:205
  31.0 2.4 %collective-permute-start.8 = (bf16[1024,128]{1,0:T(8,128)(2,1)S(1)}, bf16[1024,128]{1,0:T(8,128)(2,1)S(1)}, u32[]{:S(2)}, u32[]{:S(2)}) collective-permute-start(bf16[1024,128]{1,0:T(8,128)(2,1)S(1)} %tile_product.5), channel_id=1, source_target_pairs={{0,2},{1,3},{2,0},{3,1},{4,6},{5,7},{6,4},{7,5},{8,10},{9,11},{10,... | collective-permute-start | bytes 786440 | tf_op jit(solution)/shard_map/ppermute | solution.py:348
  33.5 0.5 collective-permute-start.10
  34.0 11.3 %collective-permute-done.8 = bf16[1024,128]{1,0:T(8,128)(2,1)S(1)} collective-permute-done((bf16[1024,128]{1,0:T(8,128)(2,1)S(1)}, bf16[1024,128]{1,0:T(8,128)(2,1)S(1)}, u32[]{:S(2)}, u32[]{:S(2)}) %collective-permute-start.8) | collective-permute-done | bytes 262176 | tf_op jit(solution)/shard_map/ppermute | solution.py:348
  45.4 1.0 %collective-permute-start.9 = (bf16[1024,128]{1,0:T(8,128)(2,1)S(1)}, bf16[1024,128]{1,0:T(8,128)(2,1)S(1)}, u32[]{:S(2)}, u32[]{:S(2)}) collective-permute-start(bf16[1024,128]{1,0:T(8,128)(2,1)S(1)} %add_convert_fusion.1.near_ref), channel_id=1, source_target_pairs={{0,4},{1,5},{2,6},{3,7},{4,0},{5,1},{6,2},{7,3},{8,12},{9,13},{10,... | collective-permute-start | bytes 786440 | tf_op jit(solution)/shard_map/ppermute | solution.py:348
  46.4 1.2 %collective-permute-done.9.far_ref = bf16[1024,128]{1,0:T(8,128)(2,1)S(1)} collective-permute-done((bf16[1024,128]{1,0:T(8,128)(2,1)S(1)}, bf16[1024,128]{1,0:T(8,128)(2,1)S(1)}, u32[]{:S(2)}, u32[]{:S(2)}) %collective-permute-start.9) | collective-permute-done | bytes 262176 | tf_op jit(solution)/shard_map/ppermute | solution.py:348
  47.6 1.1 %middle.1 = (bf16[1024,128]{1,0:T(8,128)(2,1)}, bf16[1024,128]{1,0:T(8,128)(2,1)S(1)}) custom-call(bf16[1024,128]{1,0:T(8,128)(2,1)S(1)} %add_convert_fusion.1.near_ref, bf16[1024,128]{1,0:T(8,128)(2,1)S(1)} %collective-permute-done.9.far_ref, bf16[256,256]{1,0:T(8,128)(2,1)S(1)} %copy-done.5, bf16[1024,128]{1,0:T(8,128)(2,1)S(1)} %get-tuple-element.29.cot_ref, ...), custom_call_target="tpu_custom_call" | custom-call | flops 67108864 | bytes 1310720 | tf_op jit(solution)/shard_map/middle/pallas_call | solution.py:251
  48.9 1.4 %collective-permute-start.13 = (bf16[1024,128]{1,0:T(8,128)(2,1)S(1)}, bf16[1024,128]{1,0:T(8,128)(2,1)S(1)}, u32[]{:S(2)}, u32[]{:S(2)}) collective-permute-start(bf16[1024,128]{1,0:T(8,128)(2,1)S(1)} %get-tuple-element.32.refs_6_.adj_ref), channel_id=1, source_target_pairs={{0,8},{1,9},{2,10},{3,11},{4,12},{5,13},{6,14},{7,15},{8,16},{9,17... | collective-permute-start | bytes 786440 | tf_op jit(solution)/shard_map/ppermute | solution.py:348
  50.3 1.0 %collective-permute-start.14 = (bf16[1024,128]{1,0:T(8,128)(2,1)S(1)}, bf16[1024,128]{1,0:T(8,128)(2,1)}, u32[]{:S(2)}, u32[]{:S(2)}) collective-permute-start(bf16[1024,128]{1,0:T(8,128)(2,1)S(1)} %get-tuple-element.32.refs_6_.adj_ref), channel_id=1, source_target_pairs={{0,24},{1,25},{2,26},{3,27},{4,28},{5,29},{6,30},{7,31},{8,0},{9,1... | collective-permute-start | bytes 786440 | tf_op jit(solution)/shard_map/ppermute | solution.py:348
  51.3 1.2 %collective-permute-start.15 = (bf16[1024,128]{1,0:T(8,128)(2,1)S(1)}, bf16[1024,128]{1,0:T(8,128)(2,1)}, u32[]{:S(2)}, u32[]{:S(2)}) collective-permute-start(bf16[1024,128]{1,0:T(8,128)(2,1)S(1)} %get-tuple-element.32.refs_6_.adj_ref), channel_id=1, source_target_pairs={{0,25},{1,8},{2,27},{3,10},{4,29},{5,12},{6,31},{7,14},{8,1},{9,16... | collective-permute-start | bytes 786440 | tf_op jit(solution)/shard_map/ppermute | solution.py:348
  52.5 1.5 %collective-permute-start.11 = (bf16[1024,128]{1,0:T(8,128)(2,1)}, bf16[1024,128]{1,0:T(8,128)(2,1)}, u32[]{:S(2)}, u32[]{:S(2)}) collective-permute-start(bf16[1024,128]{1,0:T(8,128)(2,1)} %get-tuple-element.31), channel_id=1, source_target_pairs={{0,1},{1,5},{2,3},{3,7},{4,0},{5,4},{6,2},{7,6},{8,9},{9,13},{10,1... | collective-permute-start | bytes 786440 | tf_op jit(solution)/shard_map/ppermute | solution.py:348
  54.0 2.2 %collective-permute-done.16.refs_7_.after_ref = bf16[1024,128]{1,0:T(8,128)(2,1)S(1)} collective-permute-done((bf16[1024,128]{1,0:T(8,128)(2,1)S(1)}, bf16[1024,128]{1,0:T(8,128)(2,1)S(1)}, u32[]{:S(2)}, u32[]{:S(2)}) %collective-permute-start.16) | collective-permute-done | bytes 262176 | tf_op jit(solution)/shard_map/ppermute | solution.py:348
  56.2 4.0 %collective-permute-start.12 = (bf16[1024,128]{1,0:T(8,128)(2,1)}, bf16[1024,128]{1,0:T(8,128)(2,1)}, u32[]{:S(2)}, u32[]{:S(2)}) collective-permute-start(bf16[1024,128]{1,0:T(8,128)(2,1)} %get-tuple-element.31), channel_id=1, source_target_pairs={{1,4},{3,6},{4,1},{6,3},{9,12},{11,14},{12,9},{14,11},{17,20},{19,... | collective-permute-start | bytes 786440 | tf_op jit(solution)/shard_map/ppermute | solution.py:348
  60.2 0.3 grad_block.1.first_ref
  60.6 0.7 copy-done.6
  61.3 1.3 %copy-done.2 = bf16[5,8,128,128]{3,2,1,0:T(8,128)(2,1)S(1)} copy-done((bf16[5,8,128,128]{3,2,1,0:T(8,128)(2,1)S(1)}, bf16[5,8,128,128]{3,2,1,0:T(8,128)(2,1)}, u32[]{:S(2)}) %copy-start.2) | copy-done | bytes 1310744
  62.6 1.8 %tile_product.6.refs_9_ = f32[1024,128]{1,0:T(8,128)S(1)} custom-call(s32[2,40]{1,0:T(2,128)S(1)} %collective-permute-done.5.refs_0_, s32[2,40]{1,0:T(2,128)S(1)} %slot_blocks.1.refs_0_.refs_1_, s32[2,40]{1,0:T(2,128)S(1)} %collective-permute-done.6.refs_1_.refs_2_, bf16[5,8,128,128]{3,2,1,0:T(8,128)(2,1)S(1)} %collective-permute-done.1.refs_1_.refs_3_, ...), custom_call_target="tpu_custom_call" | custom-call | flops 134217728 | bytes 1572864 | tf_op jit(solution)/shard_map/tile_product/pallas_call | solution.py:205
  64.4 3.1 %collective-permute-done.14.refs_7_ = bf16[1024,128]{1,0:T(8,128)(2,1)} collective-permute-done((bf16[1024,128]{1,0:T(8,128)(2,1)S(1)}, bf16[1024,128]{1,0:T(8,128)(2,1)}, u32[]{:S(2)}, u32[]{:S(2)}) %collective-permute-start.14) | collective-permute-done | bytes 262176 | tf_op jit(solution)/shard_map/ppermute | solution.py:348
  67.6 2.7 %tile_product.7.after_ref = bf16[1024,128]{1,0:T(8,128)(2,1)S(1)} custom-call(s32[2,40]{1,0:T(2,128)S(1)} %collective-permute-done.5.refs_0_, s32[2,40]{1,0:T(2,128)S(1)} %slot_blocks.1.refs_0_.refs_1_, s32[2,40]{1,0:T(2,128)S(1)} %collective-permute-done.6.refs_1_.refs_2_, bf16[5,8,128,128]{3,2,1,0:T(8,128)(2,1)S(1)} %collective-permute-done.1.refs_1_.refs_3_, ...), custom_call_target="tpu_custom_call" | custom-call | flops 201326592 | bytes 2359296 | tf_op jit(solution)/shard_map/tile_product/pallas_call | solution.py:205
  70.2 3.2 %collective-permute-start.17 = (bf16[1024,128]{1,0:T(8,128)(2,1)S(1)}, bf16[1024,128]{1,0:T(8,128)(2,1)S(1)}, u32[]{:S(2)}, u32[]{:S(2)}) collective-permute-start(bf16[1024,128]{1,0:T(8,128)(2,1)S(1)} %tile_product.7.after_ref), channel_id=1, source_target_pairs={{0,2},{1,3},{2,0},{3,1},{4,6},{5,7},{6,4},{7,5},{8,10},{9,11},{10,... | collective-permute-start | bytes 786440 | tf_op jit(solution)/shard_map/ppermute | solution.py:348
  73.4 1.3 %collective-permute-start.21 = (f32[256,128]{1,0:T(8,128)S(1)}, f32[256,128]{1,0:T(8,128)S(1)}, u32[]{:S(2)}, u32[]{:S(2)}) collective-permute-start(f32[256,128]{1,0:T(8,128)S(1)} %add_after.1), channel_id=1, source_target_pairs={{0,8},{1,9},{2,10},{3,11},{4,12},{5,13},{6,14},{7,15},{8,0},{9,1},... | collective-permute-start | bytes 393224 | tf_op jit(solution)/shard_map/ppermute | solution.py:348
  74.7 1.2 %collective-permute-start.22 = (f32[256,128]{1,0:T(8,128)S(1)}, f32[256,128]{1,0:T(8,128)S(1)}, u32[]{:S(2)}, u32[]{:S(2)}) collective-permute-start(f32[256,128]{1,0:T(8,128)S(1)} %add_after.1), channel_id=1, source_target_pairs={{0,16},{1,17},{2,18},{3,19},{4,20},{5,21},{6,22},{7,23},{8,24},{9,... | collective-permute-start | bytes 393224 | tf_op jit(solution)/shard_map/ppermute | solution.py:348
  76.2 1.1 %broadcast_select_fusion.3 = (bf16[1024,128]{1,0:T(8,128)(2,1)S(1)}, bf16[1024,128]{1,0:T(8,128)(2,1)S(1)}) fusion(pred[]{:T(512)S(6)} %eq.12, bf16[1024,128]{1,0:T(8,128)(2,1)} %get-tuple-element.31, bf16[1024,128]{1,0:T(8,128)(2,1)} %collective-permute-done.11, pred[]{:T(512)S(6)} %eq.13, bf16[1024,128]{1,0:T(8,128)(2,1)} %collective-permute-done.12), kind=kLoop, calls=%fused_computation.7 | loop fusion | flops 524288 | bytes 1310722 | tf_op jit(solution)/shard_map/jit(_where)/select_n | solution.py:416
  77.2 0.9 pad_maximum_fusion
  78.1 0.7 collective-permute-done.22
  78.8 3.2 %collective-permute-done.23 = f32[256,128]{1,0:T(8,128)S(1)} collective-permute-done((f32[256,128]{1,0:T(8,128)S(1)}, f32[256,128]{1,0:T(8,128)S(1)}, u32[]{:S(2)}, u32[]{:S(2)}) %collective-permute-start.23) | collective-permute-done | bytes 131104 | tf_op jit(solution)/shard_map/ppermute | solution.py:348
  82.1 2.4 %collective-permute-start.24 = (f32[256,128]{1,0:T(8,128)S(1)}, f32[256,128]{1,0:T(8,128)S(1)}, u32[]{:S(2)}, u32[]{:S(2)}) collective-permute-start(f32[256,128]{1,0:T(8,128)S(1)} %add_add_fusion), channel_id=1, source_target_pairs={{0,4},{1,5},{2,6},{3,7},{4,0},{5,1},{6,2},{7,3},{8,12},{9,13},{10,... | collective-permute-start | bytes 393224 | tf_op jit(solution)/shard_map/ppermute | solution.py:348
  84.5 1.3 %collective-permute-done.17 = bf16[1024,128]{1,0:T(8,128)(2,1)S(1)} collective-permute-done((bf16[1024,128]{1,0:T(8,128)(2,1)S(1)}, bf16[1024,128]{1,0:T(8,128)(2,1)S(1)}, u32[]{:S(2)}, u32[]{:S(2)}) %collective-permute-start.17) | collective-permute-done | bytes 262176 | tf_op jit(solution)/shard_map/ppermute | solution.py:348
  85.8 0.6 collective-permute-start.18
  86.4 1.9 %collective-permute-start.19 = (bf16[1024,128]{1,0:T(8,128)(2,1)S(1)}, bf16[1024,128]{1,0:T(8,128)(2,1)S(1)}, u32[]{:S(2)}, u32[]{:S(2)}) collective-permute-start(bf16[1024,128]{1,0:T(8,128)(2,1)S(1)} %add_convert_fusion.self_ref), channel_id=1, source_target_pairs={{1,4},{3,6},{4,1},{6,3},{9,12},{11,14},{12,9},{14,11},{17,20},{19,... | collective-permute-start | bytes 786440 | tf_op jit(solution)/shard_map/ppermute | solution.py:348
  88.4 0.7 pad_maximum_fusion.1
  89.1 2.0 %collective-permute-done.18.one_ref = bf16[1024,128]{1,0:T(8,128)(2,1)S(1)} collective-permute-done((bf16[1024,128]{1,0:T(8,128)(2,1)S(1)}, bf16[1024,128]{1,0:T(8,128)(2,1)S(1)}, u32[]{:S(2)}, u32[]{:S(2)}) %collective-permute-start.18) | collective-permute-done | bytes 262176 | tf_op jit(solution)/shard_map/ppermute | solution.py:348
  91.1 3.0 %collective-permute-done.19.two_ref = bf16[1024,128]{1,0:T(8,128)(2,1)S(1)} collective-permute-done((bf16[1024,128]{1,0:T(8,128)(2,1)S(1)}, bf16[1024,128]{1,0:T(8,128)(2,1)S(1)}, u32[]{:S(2)}, u32[]{:S(2)}) %collective-permute-start.19) | collective-permute-done | bytes 262176 | tf_op jit(solution)/shard_map/ppermute | solution.py:348
  94.1 1.2 %final.1 = bf16[1024,256]{1,0:T(8,128)(2,1)} custom-call(bf16[1024,128]{1,0:T(8,128)(2,1)S(1)} %add_convert_fusion.self_ref, bf16[1024,128]{1,0:T(8,128)(2,1)S(1)} %collective-permute-done.18.one_ref, bf16[1024,128]{1,0:T(8,128)(2,1)S(1)} %collective-permute-done.19.two_ref, bf16[256,256]{1,0:T(8,128)(2,1)S(1)} %copy-done.5), custom_call_target="tpu_custom_call" | custom-call | flops 134217728 | bytes 2097152 | tf_op jit(solution)/shard_map/final/pallas_call | solution.py:326
  (43 shorter events, 1.1 us)
Async XLA Ops:
  0.6 7.8 %copy-start.8 = (s32[1,5]{1,0:T(1,128)S(1)}, s32[1,5]{1,0:T(1,128)}, u32[]{:S(2)}) copy-start(s32[1,5]{1,0:T(1,128)} %param.11) | copy-start | bytes 64
  0.6 23.1 %collective-permute-start.1 = (bf16[5,8,128,128]{3,2,1,0:T(8,128)(2,1)}, bf16[5,8,128,128]{3,2,1,0:T(8,128)(2,1)S(1)}, u32[]{:S(2)}, u32[]{:S(2)}) collective-permute-start(bf16[5,8,128,128]{3,2,1,0:T(8,128)(2,1)} %bitcast.5), channel_id=1, source_target_pairs={{0,4},{1,0},{2,6},{3,2},{4,5},{5,1},{6,7},{7,3},{8,12},{9,8},{10,1... | collective-permute-start | bytes 3932168 | tf_op jit(solution)/shard_map/ppermute | solution.py:348
  2.8 1.0 %copy-start.3 = (bf16[1024,256]{1,0:T(8,128)(2,1)S(1)}, bf16[1024,256]{1,0:T(8,128)(2,1)}, u32[]{:S(2)}) copy-start(bf16[1024,256]{1,0:T(8,128)(2,1)} %x_ref.2) | copy-start | bytes 1572868
  3.9 4.5 %copy-start.9 = (s32[2,1,5,8]{3,1,2,0:T(1,128)S(1)}, s32[2,1,5,8]{3,1,2,0:T(1,128)}, u32[]{:S(2)}) copy-start(s32[2,1,5,8]{3,1,2,0:T(1,128)} %param.10) | copy-start | bytes 964
  4.0 3.2 %collective-permute-start = (bf16[1024,128]{1,0:T(8,128)(2,1)S(1)}, bf16[1024,128]{1,0:T(8,128)(2,1)S(1)}, u32[]{:S(2)}, u32[]{:S(2)}) collective-permute-start(bf16[1024,128]{1,0:T(8,128)(2,1)S(1)} %get-tuple-element.18), channel_id=1, source_target_pairs={{0,4},{1,5},{2,6},{3,7},{4,0},{5,1},{6,2},{7,3},{8,12},{9,13},{10,... | collective-permute-start | bytes 786440 | tf_op jit(solution)/shard_map/ppermute | solution.py:348
  4.1 8.4 %collective-permute-start.2 = (bf16[1024,128]{1,0:T(8,128)(2,1)S(1)}, bf16[1024,128]{1,0:T(8,128)(2,1)S(1)}, u32[]{:S(2)}, u32[]{:S(2)}) collective-permute-start(bf16[1024,128]{1,0:T(8,128)(2,1)S(1)} %get-tuple-element.21.home_ref.refs_2_.refs_4_), channel_id=1, source_target_pairs={{0,8},{1,25},{2,10},{3,27},{4,12},{5,13},{6,14},{7,15},{8,16},{9,1... | collective-permute-start | bytes 786440 | tf_op jit(solution)/shard_map/ppermute | solution.py:348
  5.3 14.2 %collective-permute-start.3 = (bf16[1024,128]{1,0:T(8,128)(2,1)S(1)}, bf16[1024,128]{1,0:T(8,128)(2,1)S(1)}, u32[]{:S(2)}, u32[]{:S(2)}) collective-permute-start(bf16[1024,128]{1,0:T(8,128)(2,1)S(1)} %get-tuple-element.18), channel_id=1, source_target_pairs={{0,12},{1,29},{2,14},{3,31},{4,8},{5,9},{6,10},{7,11},{8,20},{9,5}... | collective-permute-start | bytes 786440 | tf_op jit(solution)/shard_map/ppermute | solution.py:348
  7.2 16.6 %collective-permute-start.4 = (bf16[1024,128]{1,0:T(8,128)(2,1)S(1)}, bf16[1024,128]{1,0:T(8,128)(2,1)S(1)}, u32[]{:S(2)}, u32[]{:S(2)}) collective-permute-start(bf16[1024,128]{1,0:T(8,128)(2,1)S(1)} %pick.1), channel_id=1, source_target_pairs={{0,24},{1,25},{2,26},{3,27},{4,28},{5,29},{6,30},{7,31},{8,0},{9,1... | collective-permute-start | bytes 786440 | tf_op jit(solution)/shard_map/ppermute | solution.py:348
  9.8 19.1 %copy-start = (bf16[1,5,8,128,128]{4,3,2,1,0:T(8,128)(2,1)S(1)}, bf16[1,5,8,128,128]{4,3,2,1,0:T(8,128)(2,1)}, u32[]{:S(2)}) copy-start(bf16[1,5,8,128,128]{4,3,2,1,0:T(8,128)(2,1)} %param.9) | copy-start | bytes 3932164
  9.8 9.8 %collective-permute-start.5 = (s32[2,40]{1,0:T(2,128)S(1)}, s32[2,40]{1,0:T(2,128)S(1)}, u32[]{:S(2)}, u32[]{:S(2)}) collective-permute-start(s32[2,40]{1,0:T(2,128)S(1)} %slot_blocks.1.refs_0_.refs_1_), channel_id=1, source_target_pairs={{0,4},{1,0},{2,6},{3,2},{4,5},{5,1},{6,7},{7,3},{8,12},{9,8},{10,1... | collective-permute-start | bytes 968 | tf_op jit(solution)/shard_map/ppermute | solution.py:348
  12.5 7.1 %collective-permute-start.6 = (s32[2,40]{1,0:T(2,128)S(1)}, s32[2,40]{1,0:T(2,128)S(1)}, u32[]{:S(2)}, u32[]{:S(2)}) collective-permute-start(s32[2,40]{1,0:T(2,128)S(1)} %slot_blocks.1.refs_0_.refs_1_), channel_id=1, source_target_pairs={{1,4},{3,6},{4,1},{6,3},{9,12},{11,14},{12,9},{14,11},{17,20},{19,... | collective-permute-start | bytes 968 | tf_op jit(solution)/shard_map/ppermute | solution.py:348
  23.8 5.1 %collective-permute-start.7 = (bf16[5,8,128,128]{3,2,1,0:T(8,128)(2,1)S(1)}, bf16[5,8,128,128]{3,2,1,0:T(8,128)(2,1)S(1)}, u32[]{:S(2)}, u32[]{:S(2)}) collective-permute-start(bf16[5,8,128,128]{3,2,1,0:T(8,128)(2,1)S(1)} %collective-permute-done.1.refs_1_.refs_3_), channel_id=1, source_target_pairs={{0,4},{2,6},{5,1},{7,3},{8,12},{10,14},{13,9},{15,11},{16,20},{18,... | collective-permute-start | bytes 3932168 | tf_op jit(solution)/shard_map/ppermute | solution.py:348
  27.2 6.2 %copy-start.4 = (bf16[1024,256]{1,0:T(8,128)(2,1)S(1)}, bf16[1024,256]{1,0:T(8,128)(2,1)}, u32[]{:S(2)}) copy-start(bf16[1024,256]{1,0:T(8,128)(2,1)} %x_ref.3) | copy-start | bytes 1572868
  28.8 2.1 %copy-start.1 = (bf16[5,8,128,128]{3,2,1,0:T(8,128)(2,1)}, bf16[5,8,128,128]{3,2,1,0:T(8,128)(2,1)S(1)}, u32[]{:S(2)}) copy-start(bf16[5,8,128,128]{3,2,1,0:T(8,128)(2,1)S(1)} %collective-permute-done.7.refs_3_.refs_5_) | copy-start | bytes 3932164
  31.0 16.6 %copy-start.5 = (bf16[256,256]{1,0:T(8,128)(2,1)S(1)}, bf16[256,256]{1,0:T(8,128)(2,1)}, u32[]{:S(2)}) copy-start(bf16[256,256]{1,0:T(8,128)(2,1)} %w_ref.3) | copy-start | bytes 393220
  31.0 14.4 %collective-permute-start.8 = (bf16[1024,128]{1,0:T(8,128)(2,1)S(1)}, bf16[1024,128]{1,0:T(8,128)(2,1)S(1)}, u32[]{:S(2)}, u32[]{:S(2)}) collective-permute-start(bf16[1024,128]{1,0:T(8,128)(2,1)S(1)} %tile_product.5), channel_id=1, source_target_pairs={{0,2},{1,3},{2,0},{3,1},{4,6},{5,7},{6,4},{7,5},{8,10},{9,11},{10,... | collective-permute-start | bytes 786440 | tf_op jit(solution)/shard_map/ppermute | solution.py:348
  33.5 12.9 %collective-permute-start.10 = (bf16[1024,128]{1,0:T(8,128)(2,1)S(1)}, bf16[1024,128]{1,0:T(8,128)(2,1)S(1)}, u32[]{:S(2)}, u32[]{:S(2)}) collective-permute-start(bf16[1024,128]{1,0:T(8,128)(2,1)S(1)} %get-tuple-element.30), channel_id=1, source_target_pairs={{0,4},{1,5},{2,6},{3,7},{4,0},{5,1},{6,2},{7,3},{8,12},{9,13},{10,... | collective-permute-start | bytes 786440 | tf_op jit(solution)/shard_map/ppermute | solution.py:348
  45.4 2.2 %collective-permute-start.9 = (bf16[1024,128]{1,0:T(8,128)(2,1)S(1)}, bf16[1024,128]{1,0:T(8,128)(2,1)S(1)}, u32[]{:S(2)}, u32[]{:S(2)}) collective-permute-start(bf16[1024,128]{1,0:T(8,128)(2,1)S(1)} %add_convert_fusion.1.near_ref), channel_id=1, source_target_pairs={{0,4},{1,5},{2,6},{3,7},{4,0},{5,1},{6,2},{7,3},{8,12},{9,13},{10,... | collective-permute-start | bytes 786440 | tf_op jit(solution)/shard_map/ppermute | solution.py:348
  48.7 7.5 %collective-permute-start.16 = (bf16[1024,128]{1,0:T(8,128)(2,1)S(1)}, bf16[1024,128]{1,0:T(8,128)(2,1)S(1)}, u32[]{:S(2)}, u32[]{:S(2)}) collective-permute-start(bf16[1024,128]{1,0:T(8,128)(2,1)S(1)} %get-tuple-element.32.refs_6_.adj_ref), channel_id=1, source_target_pairs={{0,1},{1,0},{2,3},{3,2},{4,5},{5,4},{6,7},{7,6},{8,9},{9,8},{10,11... | collective-permute-start | bytes 786440 | tf_op jit(solution)/shard_map/ppermute | solution.py:348
  48.9 11.7 %collective-permute-start.13 = (bf16[1024,128]{1,0:T(8,128)(2,1)S(1)}, bf16[1024,128]{1,0:T(8,128)(2,1)S(1)}, u32[]{:S(2)}, u32[]{:S(2)}) collective-permute-start(bf16[1024,128]{1,0:T(8,128)(2,1)S(1)} %get-tuple-element.32.refs_6_.adj_ref), channel_id=1, source_target_pairs={{0,8},{1,9},{2,10},{3,11},{4,12},{5,13},{6,14},{7,15},{8,16},{9,17... | collective-permute-start | bytes 786440 | tf_op jit(solution)/shard_map/ppermute | solution.py:348
  50.3 17.3 %collective-permute-start.14 = (bf16[1024,128]{1,0:T(8,128)(2,1)S(1)}, bf16[1024,128]{1,0:T(8,128)(2,1)}, u32[]{:S(2)}, u32[]{:S(2)}) collective-permute-start(bf16[1024,128]{1,0:T(8,128)(2,1)S(1)} %get-tuple-element.32.refs_6_.adj_ref), channel_id=1, source_target_pairs={{0,24},{1,25},{2,26},{3,27},{4,28},{5,29},{6,30},{7,31},{8,0},{9,1... | collective-permute-start | bytes 786440 | tf_op jit(solution)/shard_map/ppermute | solution.py:348
  51.3 16.3 %collective-permute-start.15 = (bf16[1024,128]{1,0:T(8,128)(2,1)S(1)}, bf16[1024,128]{1,0:T(8,128)(2,1)}, u32[]{:S(2)}, u32[]{:S(2)}) collective-permute-start(bf16[1024,128]{1,0:T(8,128)(2,1)S(1)} %get-tuple-element.32.refs_6_.adj_ref), channel_id=1, source_target_pairs={{0,25},{1,8},{2,27},{3,10},{4,29},{5,12},{6,31},{7,14},{8,1},{9,16... | collective-permute-start | bytes 786440 | tf_op jit(solution)/shard_map/ppermute | solution.py:348
  52.5 23.5 %collective-permute-start.11 = (bf16[1024,128]{1,0:T(8,128)(2,1)}, bf16[1024,128]{1,0:T(8,128)(2,1)}, u32[]{:S(2)}, u32[]{:S(2)}) collective-permute-start(bf16[1024,128]{1,0:T(8,128)(2,1)} %get-tuple-element.31), channel_id=1, source_target_pairs={{0,1},{1,5},{2,3},{3,7},{4,0},{5,4},{6,2},{7,6},{8,9},{9,13},{10,1... | collective-permute-start | bytes 786440 | tf_op jit(solution)/shard_map/ppermute | solution.py:348
  56.2 19.9 %collective-permute-start.12 = (bf16[1024,128]{1,0:T(8,128)(2,1)}, bf16[1024,128]{1,0:T(8,128)(2,1)}, u32[]{:S(2)}, u32[]{:S(2)}) collective-permute-start(bf16[1024,128]{1,0:T(8,128)(2,1)} %get-tuple-element.31), channel_id=1, source_target_pairs={{1,4},{3,6},{4,1},{6,3},{9,12},{11,14},{12,9},{14,11},{17,20},{19,... | collective-permute-start | bytes 786440 | tf_op jit(solution)/shard_map/ppermute | solution.py:348
  60.6 0.7 copy-start.6
  61.3 12.1 %collective-permute-start.20 = (f32[256,128]{1,0:T(8,128)S(1)}, f32[256,128]{1,0:T(8,128)S(1)}, u32[]{:S(2)}, u32[]{:S(2)}) collective-permute-start(f32[256,128]{1,0:T(8,128)S(1)} %grad_block.1.first_ref), channel_id=1, source_target_pairs={{0,1},{1,0},{2,3},{3,2},{4,5},{5,4},{6,7},{7,6},{8,9},{9,8},{10,11... | collective-permute-start | bytes 393224 | tf_op jit(solution)/shard_map/ppermute | solution.py:348
  61.3 1.3 %copy-start.2 = (bf16[5,8,128,128]{3,2,1,0:T(8,128)(2,1)S(1)}, bf16[5,8,128,128]{3,2,1,0:T(8,128)(2,1)}, u32[]{:S(2)}) copy-start(bf16[5,8,128,128]{3,2,1,0:T(8,128)(2,1)} %copy-done.1) | copy-start | bytes 3932164
  62.6 4.9 %copy-start.7 = (bf16[1024,128]{1,0:T(8,128)(2,1)S(1)}, bf16[1024,128]{1,0:T(8,128)(2,1)}, u32[]{:S(2)}) copy-start(bf16[1024,128]{1,0:T(8,128)(2,1)} %copy-done.6) | copy-start | bytes 786436
  70.2 15.5 %collective-permute-start.17 = (bf16[1024,128]{1,0:T(8,128)(2,1)S(1)}, bf16[1024,128]{1,0:T(8,128)(2,1)S(1)}, u32[]{:S(2)}, u32[]{:S(2)}) collective-permute-start(bf16[1024,128]{1,0:T(8,128)(2,1)S(1)} %tile_product.7.after_ref), channel_id=1, source_target_pairs={{0,2},{1,3},{2,0},{3,1},{4,6},{5,7},{6,4},{7,5},{8,10},{9,11},{10,... | collective-permute-start | bytes 786440 | tf_op jit(solution)/shard_map/ppermute | solution.py:348
  73.4 4.7 %collective-permute-start.21 = (f32[256,128]{1,0:T(8,128)S(1)}, f32[256,128]{1,0:T(8,128)S(1)}, u32[]{:S(2)}, u32[]{:S(2)}) collective-permute-start(f32[256,128]{1,0:T(8,128)S(1)} %add_after.1), channel_id=1, source_target_pairs={{0,8},{1,9},{2,10},{3,11},{4,12},{5,13},{6,14},{7,15},{8,0},{9,1},... | collective-permute-start | bytes 393224 | tf_op jit(solution)/shard_map/ppermute | solution.py:348
  74.7 4.1 %collective-permute-start.22 = (f32[256,128]{1,0:T(8,128)S(1)}, f32[256,128]{1,0:T(8,128)S(1)}, u32[]{:S(2)}, u32[]{:S(2)}) collective-permute-start(f32[256,128]{1,0:T(8,128)S(1)} %add_after.1), channel_id=1, source_target_pairs={{0,16},{1,17},{2,18},{3,19},{4,20},{5,21},{6,22},{7,23},{8,24},{9,... | collective-permute-start | bytes 393224 | tf_op jit(solution)/shard_map/ppermute | solution.py:348
  76.0 6.1 %collective-permute-start.23 = (f32[256,128]{1,0:T(8,128)S(1)}, f32[256,128]{1,0:T(8,128)S(1)}, u32[]{:S(2)}, u32[]{:S(2)}) collective-permute-start(f32[256,128]{1,0:T(8,128)S(1)} %add_after.1), channel_id=1, source_target_pairs={{0,24},{1,25},{2,26},{3,27},{4,28},{5,29},{6,30},{7,31},{8,16},{9,... | collective-permute-start | bytes 393224 | tf_op jit(solution)/shard_map/ppermute | solution.py:348
  82.1 6.2 %collective-permute-start.24 = (f32[256,128]{1,0:T(8,128)S(1)}, f32[256,128]{1,0:T(8,128)S(1)}, u32[]{:S(2)}, u32[]{:S(2)}) collective-permute-start(f32[256,128]{1,0:T(8,128)S(1)} %add_add_fusion), channel_id=1, source_target_pairs={{0,4},{1,5},{2,6},{3,7},{4,0},{5,1},{6,2},{7,3},{8,12},{9,13},{10,... | collective-permute-start | bytes 393224 | tf_op jit(solution)/shard_map/ppermute | solution.py:348
  85.8 5.3 %collective-permute-start.18 = (bf16[1024,128]{1,0:T(8,128)(2,1)S(1)}, bf16[1024,128]{1,0:T(8,128)(2,1)S(1)}, u32[]{:S(2)}, u32[]{:S(2)}) collective-permute-start(bf16[1024,128]{1,0:T(8,128)(2,1)S(1)} %add_convert_fusion.self_ref), channel_id=1, source_target_pairs={{0,1},{1,5},{2,3},{3,7},{4,0},{5,4},{6,2},{7,6},{8,9},{9,13},{10,1... | collective-permute-start | bytes 786440 | tf_op jit(solution)/shard_map/ppermute | solution.py:348
  86.4 7.7 %collective-permute-start.19 = (bf16[1024,128]{1,0:T(8,128)(2,1)S(1)}, bf16[1024,128]{1,0:T(8,128)(2,1)S(1)}, u32[]{:S(2)}, u32[]{:S(2)}) collective-permute-start(bf16[1024,128]{1,0:T(8,128)(2,1)S(1)} %add_convert_fusion.self_ref), channel_id=1, source_target_pairs={{1,4},{3,6},{4,1},{6,3},{9,12},{11,14},{12,9},{14,11},{17,20},{19,... | collective-permute-start | bytes 786440 | tf_op jit(solution)/shard_map/ppermute | solution.py:348

commit v4 on v3

v4 whole, which is shorter than its diff:
```python
import functools

import jax
import jax.numpy as jnp
from jax import lax
from jax.experimental import pallas as pl
from jax.experimental.pallas import tpu as pltpu
from jax.sharding import PartitionSpec as P

AXES = ("rows", "rep")


def cut(rows):
    first = rows * 5 // 16 // 16 * 16
    return first, rows - first


def route(shape, move):
    chips, reps = shape
    pairs = []
    for c in range(chips):
        for j in range(2):
            for z in range(reps):
                to = move(c, j, z)
                if to is not None:
                    target = ((to[0] % chips) * 2 + to[1]) * reps + to[2]
                    pairs.append(((c * 2 + j) * reps + z, target))
    return pairs


def place():
    r = lax.axis_index("rows")
    z = lax.axis_index("rep")
    return r % 2, z, z % 2


def halves_kernel(x_ref, near_ref, far_ref, sems):
    j, _, _ = place()
    half = near_ref.shape[1]
    copies = []
    for i, out in enumerate((near_ref, far_ref)):
        start = pl.multiple_of((j if i == 0 else 1 - j) * half, half)
        copy = pltpu.make_async_copy(x_ref.at[:, pl.ds(start, half)], out, sems.at[i])
        copy.start()
        copies.append(copy)
    for copy in copies:
        copy.wait()


def halves(value):
    rows, width = value.shape
    part = jax.ShapeDtypeStruct((rows, width // 2), value.dtype)
    hbm = pl.BlockSpec(memory_space=pltpu.HBM)
    return pl.pallas_call(
        halves_kernel,
        out_shape=(part, part),
        in_specs=[hbm],
        out_specs=(hbm, hbm),
        scratch_shapes=[pltpu.SemaphoreType.DMA((2,))],
        compiler_params=pltpu.CompilerParams(vmem_limit_bytes=1024 * 1024),
        name="halves",
    )(value)


def pick_kernel(mine_ref, swapped_ref, *refs):
    outs, sems = refs[:3], refs[3]
    rows, rest = outs[0].shape[0], outs[1].shape[0]
    j, _, p = place()

    def copies(own, other):
        return [
            pltpu.make_async_copy(own.at[pl.ds(0, rows), :], outs[0], sems.at[0]),
            pltpu.make_async_copy(own.at[pl.ds(rows, rest), :], outs[1], sems.at[1]),
            pltpu.make_async_copy(other, outs[2], sems.at[2]),
        ]

    @pl.when(j == p)
    def _():
        for copy in copies(mine_ref, swapped_ref):
            copy.start()
        for copy in copies(mine_ref, swapped_ref):
            copy.wait()

    @pl.when(j != p)
    def _():
        for copy in copies(swapped_ref, mine_ref):
            copy.start()
        for copy in copies(swapped_ref, mine_ref):
            copy.wait()


def pick(mine, swapped):
    hbm = pl.BlockSpec(memory_space=pltpu.HBM)
    rows, width = mine.shape
    shapes = [jax.ShapeDtypeStruct((n, width), mine.dtype) for n in (*cut(rows), rows)]
    return pl.pallas_call(
        pick_kernel,
        out_shape=tuple(shapes),
        in_specs=[hbm, hbm],
        out_specs=(hbm, hbm, hbm),
        scratch_shapes=[pltpu.SemaphoreType.DMA((3,))],
        compiler_params=pltpu.CompilerParams(vmem_limit_bytes=1024 * 1024),
        name="pick",
    )(mine, swapped)


def slots_kernel(dead, coords_ref, counts_ref, out_ref):
    _, z, _ = place()
    _, reach, slots = coords_ref.shape
    for d in range(reach):
        for k in range(slots):
            live = z * slots + k < counts_ref[d]
            out_ref[0, d * slots + k] = jnp.where(live, coords_ref[0, d, k], dead)
            out_ref[1, d * slots + k] = coords_ref[1, d, k]


def slot_blocks(coords, counts, dead):
    smem = pl.BlockSpec(memory_space=pltpu.SMEM)
    return pl.pallas_call(
        functools.partial(slots_kernel, dead),
        out_shape=jax.ShapeDtypeStruct((2, coords.shape[1] * coords.shape[2]), jnp.int32),
        in_specs=[smem, smem],
        out_specs=smem,
        compiler_params=pltpu.CompilerParams(vmem_limit_bytes=1024 * 1024),
        name="slot_blocks",
    )(coords, counts)


def offset_of(kind):
    _, _, p = place()
    even = (lax.axis_index("rows") // 2) % 2 == 0
    return {
        "self": 2,
        "near": jnp.where(p == 0, 3, 1),
        "far": jnp.where(p == 0, 1, 3),
        "direct": jnp.where(even, 4, 0),
        "second": jnp.where(even, 0, 4),
    }[kind]


def tile_kernel(kinds, pieces, sets, outs, summed, waits, *refs):
    refs = list(refs)
    metas = [refs.pop(0) for _ in range(sum(sets))]
    tiles = [refs.pop(0) for _ in range(sum(sets))]
    panels = [[refs.pop(0) for _ in range(count)] for count in pieces]
    before = refs.pop(0) if summed else None
    refs = refs[waits:]
    out_refs = [refs.pop(0) for _ in range(outs)]
    acc_ref, tile_buf, panel_buf, tile_sems, panel_sems = refs
    slots, tile = tile_buf.shape[2], tile_buf.shape[-1]
    rows = panel_buf.shape[1]
    j, _, p = place()
    home = j == p
    offsets = [offset_of(kind) for kind in kinds]

    def tile_copy(ref, i, s):
        return pltpu.make_async_copy(ref.at[offsets[i]], tile_buf.at[i, s], tile_sems.at[i, s])

    def panel_copies(i):
        starts = (0, panels[i][0].shape[0])
        return [
            pltpu.make_async_copy(
                ref, panel_buf.at[i, pl.ds(starts[n], ref.shape[0]), :], panel_sems.at[i, n]
            )
            for n, ref in enumerate(panels[i])
        ]

    for i in range(len(kinds)):
        for copy in panel_copies(i):
            copy.start()
        at = 0
        for s, members in enumerate(sets):
            if members == 1:
                tile_copy(tiles[at], i, s).start()
            else:

                @pl.when(home)
                def _(ref=tiles[at], i=i, s=s):
                    tile_copy(ref, i, s).start()

                @pl.when(jnp.logical_not(home))
                def _(ref=tiles[at + 1], i=i, s=s):
                    tile_copy(ref, i, s).start()

            at += members
    if summed:
        acc_ref[:rows, :] = before[...]
    else:
        acc_ref[...] = jnp.zeros_like(acc_ref)
    for i in range(len(kinds)):
        d = offsets[i]
        for copy in panel_copies(i):
            copy.wait()
        at = 0
        for s, members in enumerate(sets):
            tile_copy(tiles[at], i, s).wait()
            for k in range(slots):
                row = metas[at][0, d * slots + k]
                col = metas[at][1, d * slots + k]
                if members == 2:
                    row = jnp.where(home, row, metas[at + 1][0, d * slots + k])
                    col = jnp.where(home, col, metas[at + 1][1, d * slots + k])
                row = pl.multiple_of(row * tile, tile)
                col = pl.multiple_of(col * tile, tile)
                prod = jnp.dot(
                    tile_buf[i, s, k],
                    panel_buf[i, pl.ds(col, tile), :],
                    preferred_element_type=jnp.float32,
                )
                acc_ref[pl.ds(row, tile), :] += prod
            at += members
    start = 0
    for out_ref in out_refs:
        size = out_ref.shape[0]
        out_ref[...] = acc_ref[start : start + size, :].astype(out_ref.dtype)
        start += size


def tile_product(named, sets, dtype, outs=1, before=None, after=()):
    kinds = [kind for kind, _ in named]
    pieces = [len(panel) for _, panel in named]
    panels = [piece for _, panel in named for piece in panel]
    metas = [meta for members in sets for meta, _ in members]
    tiles = [values for members in sets for _, values in members]
    width = panels[0].shape[1]
    rows = sum(piece.shape[0] for piece in named[0][1])
    _, slots, tile, _ = tiles[0].shape
    smem = pl.BlockSpec(memory_space=pltpu.SMEM)
    vmem = pl.BlockSpec(memory_space=pltpu.VMEM)
    hbm = pl.BlockSpec(memory_space=pltpu.HBM)
    anywhere = pl.BlockSpec(memory_space=pl.ANY)
    count = len(kinds) * len(sets) * slots
    summed = before is not None
    return pl.pallas_call(
        functools.partial(tile_kernel, kinds, pieces, [len(m) for m in sets], outs, summed, len(after)),
        out_shape=tuple(
            jax.ShapeDtypeStruct((n, width), dtype) for n in (cut(rows) if outs == 2 else [rows])
        ),
        in_specs=[smem] * len(metas)
        + [hbm] * len(tiles)
        + [anywhere] * len(panels)
        + [vmem] * summed
        + [anywhere] * len(after),
        out_specs=(vmem,) * outs,
        scratch_shapes=[
            pltpu.VMEM((rows + tile, width), jnp.float32),
            pltpu.VMEM((len(kinds), len(sets), slots, tile, tile), tiles[0].dtype),
            pltpu.VMEM((len(kinds), rows, width), panels[0].dtype),
            pltpu.SemaphoreType.DMA((len(kinds), len(sets))),
            pltpu.SemaphoreType.DMA((len(kinds), 2)),
        ],
        compiler_params=pltpu.CompilerParams(vmem_limit_bytes=8 * 1024 * 1024),
        cost_estimate=pl.CostEstimate(
            flops=2 * count * tile * tile * width,
            bytes_accessed=count * tile * tile * 2 + len(kinds) * rows * width * 2,
            transcendentals=0,
        ),
        name="tile_product",
    )(*metas, *tiles, *panels, *([before] if summed else []), *after)


def middle_kernel(chunk, near_ref, far_ref, w_ref, cot_ref, swap_ref, *refs):
    j, _, p = place()
    rows, half = near_ref.shape
    near = pl.multiple_of(j * half, half)
    far = pl.multiple_of((1 - j) * half, half)
    cols = pl.ds(near, half)
    agg = jnp.dot(
        near_ref[...], w_ref[pl.ds(near, half), cols], preferred_element_type=jnp.float32
    )
    agg += jnp.dot(far_ref[...], w_ref[pl.ds(far, half), cols], preferred_element_type=jnp.float32)
    sig = jax.nn.sigmoid(agg)
    slope = sig * (1.0 + agg * (1.0 - sig))
    start = cot_ref.shape[0] - rows if chunk else 0
    mine = pl.ds(start, rows)
    cot = jnp.where(j == p, cot_ref[mine, :], swap_ref[mine, :]).astype(jnp.float32)
    act = (agg * sig).astype(jnp.bfloat16)
    adj = (cot * slope).astype(jnp.bfloat16)
    if chunk == 0:
        act_ref, adj_ref = refs
        act_ref[...] = act
        adj_ref[...] = adj
    else:
        act_first_ref, adj_first_ref, _, act_ref, adj_ref, whole_ref = refs
        act_ref[:start, :] = act_first_ref[...]
        act_ref[start:, :] = act
        adj_ref[...] = adj
        whole_ref[:start, :] = adj_first_ref[...]
        whole_ref[start:, :] = adj


def middle(near, far, weight, cot, cot_swap, first=None):
    vmem = pl.BlockSpec(memory_space=pltpu.VMEM)
    rows, width = near.shape
    part = jax.ShapeDtypeStruct((rows, width), jnp.bfloat16)
    whole = jax.ShapeDtypeStruct(cot.shape, jnp.bfloat16)
    return pl.pallas_call(
        functools.partial(middle_kernel, 0 if first is None else 1),
        out_shape=(part, part) if first is None else (whole, part, whole),
        in_specs=[vmem] * 5 + ([vmem, vmem, pl.BlockSpec(memory_space=pl.ANY)] if first else []),
        out_specs=(vmem,) * (2 if first is None else 3),
        compiler_params=pltpu.CompilerParams(vmem_limit_bytes=8 * 1024 * 1024),
        cost_estimate=pl.CostEstimate(flops=1, bytes_accessed=1, transcendentals=0),
        name="middle",
    )(near, far, weight, cot, cot_swap, *(first or ()))


def grad_kernel(scale, near_a, near_b, far_a, far_b, adj_ref, after_ref, out_ref):
    j, _, _ = place()
    cut_at, half = near_a.shape
    dims = (((0,), (0,)), ((), ()))
    for i, refs in enumerate(((near_a, near_b), (far_a, far_b))):
        start = pl.multiple_of((j if i == 0 else 1 - j) * half, half)
        total = jnp.zeros((half, half), jnp.float32)
        for n, ref in enumerate(refs):
            adj = adj_ref[cut_at:, :] if n else adj_ref[:cut_at, :]
            total += lax.dot_general(ref[...], adj, dims, preferred_element_type=jnp.float32)
        out_ref[pl.ds(start, half), :] = scale * total


def grad_block(scale, nears, fars, adj, after):
    vmem = pl.BlockSpec(memory_space=pltpu.VMEM)
    rows, width = adj.shape
    return pl.pallas_call(
        functools.partial(grad_kernel, scale),
        out_shape=jax.ShapeDtypeStruct((2 * width, width), jnp.float32),
        in_specs=[vmem] * 5 + [pl.BlockSpec(memory_space=pl.ANY)],
        out_specs=vmem,
        compiler_params=pltpu.CompilerParams(vmem_limit_bytes=8 * 1024 * 1024),
        cost_estimate=pl.CostEstimate(
            flops=4 * rows * width * width, bytes_accessed=8 * rows * width, transcendentals=0
        ),
        name="grad_block",
    )(*nears, *fars, adj, after)


def add_kernel(count, *refs):
    total = refs[0][...].astype(jnp.float32) + refs[1][...].astype(jnp.float32)
    if count == 4:
        total = total + (refs[2][...] + refs[3][...])
    refs[-1][...] = total.astype(refs[-1].dtype)


def add_after(values, *after):
    vmem = pl.BlockSpec(memory_space=pltpu.VMEM)
    return pl.pallas_call(
        functools.partial(add_kernel, len(values)),
        out_shape=jax.ShapeDtypeStruct(values[0].shape, values[0].dtype),
        in_specs=[vmem] * len(values) + [pl.BlockSpec(memory_space=pl.ANY)] * len(after),
        out_specs=vmem,
        compiler_params=pltpu.CompilerParams(vmem_limit_bytes=4 * 1024 * 1024),
        name="add_after",
    )(*values, *after)


def final_kernel(own_ref, one_ref, two_ref, w_ref, grad_ref, rest_ref, out_ref, grad_out_ref):
    j, _, p = place()
    half = own_ref.shape[1]
    near_cols = pl.ds(pl.multiple_of(j * half, half), half)
    far_cols = pl.ds(pl.multiple_of((1 - j) * half, half), half)
    grad_out_ref[:, near_cols] = grad_ref[...]
    grad_out_ref[:, far_cols] = rest_ref[...]
    near = jnp.where(j == p, own_ref[...], one_ref[...])
    far = jnp.where(j == p, one_ref[...], two_ref[...])
    dims = (((1,), (1,)), ((), ()))
    total = lax.dot_general(near, w_ref[:, near_cols], dims, preferred_element_type=jnp.float32)
    total += lax.dot_general(far, w_ref[:, far_cols], dims, preferred_element_type=jnp.float32)
    out_ref[...] = total.astype(out_ref.dtype)


def final(own, one, two, weight, grad, rest):
    vmem = pl.BlockSpec(memory_space=pltpu.VMEM)
    rows = own.shape[0]
    wide = weight.shape[0]
    return pl.pallas_call(
        final_kernel,
        out_shape=(
            jax.ShapeDtypeStruct((rows, wide), jnp.bfloat16),
            jax.ShapeDtypeStruct(weight.shape, jnp.float32),
        ),
        in_specs=[vmem] * 6,
        out_specs=(vmem, vmem),
        compiler_params=pltpu.CompilerParams(vmem_limit_bytes=8 * 1024 * 1024),
        cost_estimate=pl.CostEstimate(
            flops=2 * rows * wide * wide, bytes_accessed=8 * rows * wide, transcendentals=0
        ),
        name="final",
    )(own, one, two, weight, grad, rest)


def per_device(node_feats, weight, cotangent, tile_values, tile_coords, tile_counts):
    groups = lax.axis_size("rows")
    reps = lax.axis_size("rep")
    shape = (groups // 2, reps)
    j, z, p = place()
    home = j == p
    scale = (node_feats.shape[0] * groups) ** (-0.5)

    def send(value, move):
        return lax.ppermute(value, AXES, route(shape, move))

    def sibling(c, j, z):
        return (c, 1 - j, z)

    def across(c, j, z):
        return (c, j, (z + reps // 2) % reps)

    own = tile_values[0]
    blocks = node_feats.shape[0] // own.shape[-1]

    def to_home(c, j, z):
        return (c, 1 - j, z) if j == z % 2 else (c, j, z ^ 1)

    def to_direct(c, j, z):
        return (c ^ 1, j, z)

    def to_second(c, j, z):
        return (c ^ 2, j, z) if shape[0] == 4 else (c + 1 if c % 2 else c - 1, j, z)

    def hand_on(value, direct):
        return send(direct if shape[0] == 4 else value, to_second)

    first = send(own, to_home)
    mine, yours = halves(node_feats)
    swapped = send(yours, sibling)
    feats_a, feats_b, feats_other = pick(mine, swapped)
    feats = [feats_a, feats_b]
    direct = [send(value, to_direct) for value in feats]
    far = send(feats_other, lambda c, j, z: (c - 1 if z % 2 else c + 1, j, z))
    second = [hand_on(value, got) for value, got in zip(feats, direct)]
    coords, counts, feats_other = lax.optimization_barrier((tile_coords, tile_counts, feats_other))
    meta = slot_blocks(coords[:, 0], counts[0], blocks)
    meta_b = send(meta, to_home)
    meta_far = send(meta, lambda c, j, z: None if j == z % 2 else (c, 1 - j, z ^ 1))
    first, second, far, meta_b, meta_far = lax.optimization_barrier(
        (first, second, far, meta_b, meta_far)
    )
    other_first = send(first, lambda c, j, z: (c, 1 - j, z) if j == z % 2 else None)

    set_first = [(meta_b, first)]
    set_rest = [(meta, own), (meta_far, other_first)]
    panels = [
        ("self", feats),
        ("near", [feats_other]),
        ("direct", direct),
        ("second", second),
        ("far", [far]),
    ]
    (part,) = tile_product(panels, [set_first], jnp.float32)
    parts = tile_product(panels, [set_rest], jnp.bfloat16, 2, part)

    def join(value, other):
        return (value.astype(jnp.float32) + other.astype(jnp.float32)).astype(jnp.bfloat16)

    cot, cot_yours = halves(cotangent)
    cot_swap = send(cot_yours, sibling)

    def to_far(c, j, z):
        return (c + 1 if z % 2 else c - 1, j, z ^ 1)

    across_a, across_b = [send(value, across) for value in parts]
    near_a = join(parts[0], across_a)
    far_a = send(near_a, sibling)
    act_a, adj_a = middle(near_a, far_a, weight, cot, cot_swap)
    direct = [send(adj_a, to_direct)]
    far = [send(adj_a, to_far)]
    second = [hand_on(adj_a, direct[0])]
    near_b = add_after([parts[1], across_b], direct[0], far[0])
    far_b = send(near_b, sibling)
    act, adj_b, adj = middle(near_b, far_b, weight, cot, cot_swap, (act_a, adj_a, second[0]))
    direct.append(send(adj_b, to_direct))
    far.append(send(adj_b, to_far))
    second.append(hand_on(adj_b, direct[1]))
    other = send(adj, lambda c, j, z: (c, j, z ^ 1))
    panels = [("self", [adj]), ("near", [other])]
    (back_part,) = tile_product(panels, [set_first, set_rest], jnp.float32)
    panels = [("direct", direct), ("far", far), ("second", second)]
    grad = grad_block(scale, [near_a, near_b], [far_a, far_b], adj, other)
    grad_got = send(grad, lambda c, j, z: (c, j, z ^ 1))
    (back_part,) = tile_product(
        panels, [set_first, set_rest], jnp.bfloat16, 1, back_part, [grad_got]
    )

    def deliver(value):
        one = send(value, lambda c, j, z: (c, j, z ^ 1) if j == z % 2 else (c, 1 - j, z))
        two = send(value, lambda c, j, z: None if j == z % 2 else (c, 1 - j, z ^ 1))
        return one, two

    act_one, act_two = deliver(act)
    act_near = jnp.where(home, act, act_one)
    act_far = jnp.where(home, act_one, act_two)
    activated = jnp.concatenate(
        [jnp.where(j == 0, act_near, act_far), jnp.where(j == 0, act_far, act_near)], axis=1
    )

    back = join(back_part, send(back_part, across))
    back_one, back_two = deliver(back)

    grad = add_after([grad, grad_got], back_part)
    step = 1
    while step < shape[0]:
        flips = [step] if step * 2 >= shape[0] else [step, 2 * step, 3 * step]
        got = [send(grad, lambda c, j, z, s=s: (c ^ s, j, z)) for s in flips]
        grad = add_after([grad, *got], back)
        step *= 2 if len(flips) == 1 else 4
    grad_rest = send(grad, sibling)
    input_grad, weight_grad = final(back, back_one, back_two, weight, grad, grad_rest)
    return (activated, input_grad, weight_grad)


def solution(mesh):
    return jax.shard_map(
        per_device,
        mesh=mesh,
        in_specs=(
            P("rows", None),
            P(),
            P("rows", None),
            P("rows", None, "rep", None, None),
            P(None, "rows", None, "rep"),
            P("rows", None),
        ),
        out_specs=(P("rows", None), P("rows", None), P()),
        check_vma=False,
    )
```

time: 95.6 us -> 106 us (1.11)
  starting transfers between devices: 37.3 us -> 46.8 us
  Pallas kernels: 12.9 us -> 15.6 us
  other arithmetic: 2.85 us -> 1 us
  waiting for transfers between devices: 38.3 us -> 39.5 us
    ppermute x25 -> x32, starting transfers between devices: 37.3 us -> 46.8 us  [send(): return lax.ppermute(value, AXES, route(shape, move))]
    pallas_call x8 -> x11, Pallas kernels: 11 us -> 13.6 us  [the longest x4 11.4 us: tile_product(): pl.pallas_call(functools.partial(tile_kernel, kinds, pieces, [len(m) for...]
    unnamed x20 -> x10, local copies, waits for them, and re-layouts: 3.09 us -> 1.71 us
    ppermute x25 -> x32, waiting for transfers between devices: 38.3 us -> 39.5 us  [send(): return lax.ppermute(value, AXES, route(shape, move))]
  transfers between devices with their start and end apart: 25 -> 32, of which waited for: 13 -> 19; matrix products, arithmetic and copies ran while one was open for 3% -> 2% of each run, Pallas kernels for 9% -> 7%
where the time goes in v4:
time: 106 us
  starting transfers between devices  46.8 us (44%)
  waiting for transfers between devices  39.5 us (37%)
  Pallas kernels  15.6 us (15%)
  local copies, waits for them, and re-layouts  2.41 us (2%)
    ppermute x32, starting transfers between devices, send(): return lax.ppermute(value, AXES, route(shape, move))  46.8 us
    ppermute x32, waiting for transfers between devices, send(): return lax.ppermute(value, AXES, route(shape, move))  39.5 us
    pallas_call x4, Pallas kernels, tile_product(): pl.pallas_call(functools.partial(tile_kernel, kinds, pieces, [len(m) for...  11.4 us
  transfers between devices with their start and end apart: 32, of which 19 were waited for; matrix products, arithmetic and copies ran while one was open for 2% of the time, Pallas kernels for 7%

profile of v4, /device:TPU:1, one launch (start us, length us, event | category | flops | bytes accessed | tf_op | source)
XLA Modules:
  0.0 106.1 jit_solution(5824164311599194493)
XLA Ops:
  0.6 2.2 %collective-permute-start.1 = (bf16[5,8,128,128]{3,2,1,0:T(8,128)(2,1)}, bf16[5,8,128,128]{3,2,1,0:T(8,128)(2,1)S(1)}, u32[]{:S(2)}, u32[]{:S(2)}) collective-permute-start(bf16[5,8,128,128]{3,2,1,0:T(8,128)(2,1)} %bitcast.5), channel_id=1, source_target_pairs={{0,4},{1,0},{2,6},{3,2},{4,5},{5,1},{6,7},{7,3},{8,12},{9,8},{10,1... | collective-permute-start | bytes 3932168 | tf_op jit(solution)/shard_map/ppermute | solution.py:400
  2.8 1.0 copy-done.2
  4.1 1.5 %collective-permute-done.swapped_ref = bf16[1024,128]{1,0:T(8,128)(2,1)S(1)} collective-permute-done((bf16[1024,128]{1,0:T(8,128)(2,1)S(1)}, bf16[1024,128]{1,0:T(8,128)(2,1)S(1)}, u32[]{:S(2)}, u32[]{:S(2)}) %collective-permute-start) | collective-permute-done | bytes 262176 | tf_op jit(solution)/shard_map/ppermute | solution.py:400
  5.9 1.3 %collective-permute-start.4 = (bf16[704,128]{1,0:T(8,128)(2,1)S(1)}, bf16[704,128]{1,0:T(8,128)(2,1)S(1)}, u32[]{:S(2)}, u32[]{:S(2)}) collective-permute-start(bf16[704,128]{1,0:T(8,128)(2,1)S(1)} %get-tuple-element.34.refs_3_.refs_5_), channel_id=1, source_target_pairs={{0,8},{1,9},{2,10},{3,11},{4,12},{5,13},{6,14},{7,15},{8,0},{9,1},... | collective-permute-start | bytes 540680 | tf_op jit(solution)/shard_map/ppermute | solution.py:400
  7.5 4.5 %collective-permute-done.4.refs_6_.refs_8_ = bf16[704,128]{1,0:T(8,128)(2,1)S(1)} collective-permute-done((bf16[704,128]{1,0:T(8,128)(2,1)S(1)}, bf16[704,128]{1,0:T(8,128)(2,1)S(1)}, u32[]{:S(2)}, u32[]{:S(2)}) %collective-permute-start.4) | collective-permute-done | bytes 180256 | tf_op jit(solution)/shard_map/ppermute | solution.py:400
  12.0 1.2 %collective-permute-start.5 = (bf16[704,128]{1,0:T(8,128)(2,1)S(1)}, bf16[704,128]{1,0:T(8,128)(2,1)S(1)}, u32[]{:S(2)}, u32[]{:S(2)}) collective-permute-start(bf16[704,128]{1,0:T(8,128)(2,1)S(1)} %collective-permute-done.4.refs_6_.refs_8_), channel_id=1, source_target_pairs={{0,16},{1,17},{2,18},{3,19},{4,20},{5,21},{6,22},{7,23},{8,24},{9,... | collective-permute-start | bytes 540680 | tf_op jit(solution)/shard_map/ppermute | solution.py:400
  13.3 1.2 %collective-permute-start.2 = (bf16[320,128]{1,0:T(8,128)(2,1)S(1)}, bf16[320,128]{1,0:T(8,128)(2,1)S(1)}, u32[]{:S(2)}, u32[]{:S(2)}) collective-permute-start(bf16[320,128]{1,0:T(8,128)(2,1)S(1)} %get-tuple-element.33.refs_2_.refs_4_), channel_id=1, source_target_pairs={{0,8},{1,9},{2,10},{3,11},{4,12},{5,13},{6,14},{7,15},{8,0},{9,1},... | collective-permute-start | bytes 245768 | tf_op jit(solution)/shard_map/ppermute | solution.py:400
  14.5 5.0 %collective-permute-done.2.refs_5_.refs_7_ = bf16[320,128]{1,0:T(8,128)(2,1)S(1)} collective-permute-done((bf16[320,128]{1,0:T(8,128)(2,1)S(1)}, bf16[320,128]{1,0:T(8,128)(2,1)S(1)}, u32[]{:S(2)}, u32[]{:S(2)}) %collective-permute-start.2) | collective-permute-done | bytes 81952 | tf_op jit(solution)/shard_map/ppermute | solution.py:400
  19.4 1.2 %collective-permute-start.3 = (bf16[320,128]{1,0:T(8,128)(2,1)S(1)}, bf16[320,128]{1,0:T(8,128)(2,1)S(1)}, u32[]{:S(2)}, u32[]{:S(2)}) collective-permute-start(bf16[320,128]{1,0:T(8,128)(2,1)S(1)} %collective-permute-done.2.refs_5_.refs_7_), channel_id=1, source_target_pairs={{0,16},{1,17},{2,18},{3,19},{4,20},{5,21},{6,22},{7,23},{8,24},{9,... | collective-permute-start | bytes 245768 | tf_op jit(solution)/shard_map/ppermute | solution.py:400
  22.0 1.3 %slot_blocks.1.refs_0_.refs_1_ = s32[2,40]{1,0:T(2,128)S(1)} custom-call(s32[2,5,8]{2,1,0:T(8,128)S(1)} %copy.10.coords_ref, s32[5]{0:T(128)S(1)} %bitcast.9), custom_call_target="tpu_custom_call" | custom-call | tf_op jit(solution)/shard_map/slot_blocks/pallas_call | solution.py:119
  23.4 0.7 collective-permute-start.7
  24.1 1.2 %collective-permute-done.7.refs_0_ = s32[2,40]{1,0:T(2,128)S(1)} collective-permute-done((s32[2,40]{1,0:T(2,128)S(1)}, s32[2,40]{1,0:T(2,128)S(1)}, u32[]{:S(2)}, u32[]{:S(2)}) %collective-permute-start.7) | collective-permute-done | bytes 352 | tf_op jit(solution)/shard_map/ppermute | solution.py:400
  25.3 4.2 %collective-permute-start.8 = (s32[2,40]{1,0:T(2,128)S(1)}, s32[2,40]{1,0:T(2,128)S(1)}, u32[]{:S(2)}, u32[]{:S(2)}) collective-permute-start(s32[2,40]{1,0:T(2,128)S(1)} %slot_blocks.1.refs_0_.refs_1_), channel_id=1, source_target_pairs={{1,4},{3,6},{4,1},{6,3},{9,12},{11,14},{12,9},{14,11},{17,20},{19,... | collective-permute-start | bytes 968 | tf_op jit(solution)/shard_map/ppermute | solution.py:400
  29.5 1.2 %collective-permute-done.8.refs_1_.refs_2_ = s32[2,40]{1,0:T(2,128)S(1)} collective-permute-done((s32[2,40]{1,0:T(2,128)S(1)}, s32[2,40]{1,0:T(2,128)S(1)}, u32[]{:S(2)}, u32[]{:S(2)}) %collective-permute-start.8) | collective-permute-done | bytes 352 | tf_op jit(solution)/shard_map/ppermute | solution.py:400
  30.8 1.3 %collective-permute-start.9 = (bf16[5,8,128,128]{3,2,1,0:T(8,128)(2,1)S(1)}, bf16[5,8,128,128]{3,2,1,0:T(8,128)(2,1)S(1)}, u32[]{:S(2)}, u32[]{:S(2)}) collective-permute-start(bf16[5,8,128,128]{3,2,1,0:T(8,128)(2,1)S(1)} %collective-permute-done.1.refs_1_.refs_3_), channel_id=1, source_target_pairs={{0,4},{2,6},{5,1},{7,3},{8,12},{10,14},{13,9},{15,11},{16,20},{18,... | collective-permute-start | bytes 3932168 | tf_op jit(solution)/shard_map/ppermute | solution.py:400
  32.1 3.1 %tile_product.4.refs_12_ = f32[1024,128]{1,0:T(8,128)S(1)} custom-call(s32[2,40]{1,0:T(2,128)S(1)} %collective-permute-done.7.refs_0_, bf16[5,8,128,128]{3,2,1,0:T(8,128)(2,1)S(1)} %collective-permute-done.1.refs_1_.refs_3_, bf16[320,128]{1,0:T(8,128)(2,1)S(1)} %get-tuple-element.33.refs_2_.refs_4_, bf16[704,128]{1,0:T(8,128)(2,1)S(1)} %get-tuple-element.34.refs_3_.refs_5_, ...), custom_call_target="tpu_custom_call" | custom-call | flops 167772160 | bytes 2621440 | tf_op jit(solution)/shard_map/tile_product/pallas_call | solution.py:234
  35.7 3.1 %tile_product.5 = (bf16[320,128]{1,0:T(8,128)(2,1)S(1)}, bf16[704,128]{1,0:T(8,128)(2,1)S(1)}) custom-call(s32[2,40]{1,0:T(2,128)S(1)} %slot_blocks.1.refs_0_.refs_1_, s32[2,40]{1,0:T(2,128)S(1)} %collective-permute-done.8.refs_1_.refs_2_, bf16[5,8,128,128]{3,2,1,0:T(8,128)(2,1)S(1)} %bitcast.6, ...), custom_call_target="tpu_custom_call" | custom-call | flops 167772160 | bytes 2621440 | tf_op jit(solution)/shard_map/tile_product/pallas_call | solution.py:234
  38.9 2.4 %collective-permute-start.11 = (bf16[320,128]{1,0:T(8,128)(2,1)S(1)}, bf16[320,128]{1,0:T(8,128)(2,1)S(1)}, u32[]{:S(2)}, u32[]{:S(2)}) collective-permute-start(bf16[320,128]{1,0:T(8,128)(2,1)S(1)} %get-tuple-element.43), channel_id=1, source_target_pairs={{0,2},{1,3},{2,0},{3,1},{4,6},{5,7},{6,4},{7,5},{8,10},{9,11},{10,... | collective-permute-start | bytes 245768 | tf_op jit(solution)/shard_map/ppermute | solution.py:400
  41.4 1.1 %collective-permute-start.13 = (bf16[1024,128]{1,0:T(8,128)(2,1)S(1)}, bf16[1024,128]{1,0:T(8,128)(2,1)S(1)}, u32[]{:S(2)}, u32[]{:S(2)}) collective-permute-start(bf16[1024,128]{1,0:T(8,128)(2,1)S(1)} %get-tuple-element.45), channel_id=1, source_target_pairs={{0,4},{1,5},{2,6},{3,7},{4,0},{5,1},{6,2},{7,3},{8,12},{9,13},{10,... | collective-permute-start | bytes 786440 | tf_op jit(solution)/shard_map/ppermute | solution.py:400
  43.2 3.8 %collective-permute-start.12 = (bf16[320,128]{1,0:T(8,128)(2,1)S(1)}, bf16[320,128]{1,0:T(8,128)(2,1)S(1)}, u32[]{:S(2)}, u32[]{:S(2)}) collective-permute-start(bf16[320,128]{1,0:T(8,128)(2,1)S(1)} %add_convert_fusion.1.near_ref.near_a), channel_id=1, source_target_pairs={{0,4},{1,5},{2,6},{3,7},{4,0},{5,1},{6,2},{7,3},{8,12},{9,13},{10,... | collective-permute-start | bytes 245768 | tf_op jit(solution)/shard_map/ppermute | solution.py:400
  47.0 0.9 collective-permute-done.12.far_ref.far_a
  48.2 1.2 %collective-permute-start.14 = (bf16[320,128]{1,0:T(8,128)(2,1)S(1)}, bf16[320,128]{1,0:T(8,128)(2,1)S(1)}, u32[]{:S(2)}, u32[]{:S(2)}) collective-permute-start(bf16[320,128]{1,0:T(8,128)(2,1)S(1)} %get-tuple-element.46.refs_1_), channel_id=1, source_target_pairs={{0,8},{1,9},{2,10},{3,11},{4,12},{5,13},{6,14},{7,15},{8,0},{9,1},... | collective-permute-start | bytes 245768 | tf_op jit(solution)/shard_map/ppermute | solution.py:400
  49.4 4.0 %collective-permute-start.15 = (bf16[320,128]{1,0:T(8,128)(2,1)S(1)}, bf16[320,128]{1,0:T(8,128)(2,1)S(1)}, u32[]{:S(2)}, u32[]{:S(2)}) collective-permute-start(bf16[320,128]{1,0:T(8,128)(2,1)S(1)} %get-tuple-element.46.refs_1_), channel_id=1, source_target_pairs={{0,25},{1,8},{2,27},{3,10},{4,29},{5,12},{6,31},{7,14},{8,1},{9,16... | collective-permute-start | bytes 245768 | tf_op jit(solution)/shard_map/ppermute | solution.py:400
  53.9 2.3 %collective-permute-done.15.refs_3_.refs_8_ = bf16[320,128]{1,0:T(8,128)(2,1)S(1)} collective-permute-done((bf16[320,128]{1,0:T(8,128)(2,1)S(1)}, bf16[320,128]{1,0:T(8,128)(2,1)S(1)}, u32[]{:S(2)}, u32[]{:S(2)}) %collective-permute-start.15) | collective-permute-done | bytes 81952 | tf_op jit(solution)/shard_map/ppermute | solution.py:400
  56.3 0.9 collective-permute-start.16
  57.2 1.2 %collective-permute-start.17 = (bf16[320,128]{1,0:T(8,128)(2,1)S(1)}, bf16[320,128]{1,0:T(8,128)(2,1)S(1)}, u32[]{:S(2)}, u32[]{:S(2)}) collective-permute-start(bf16[320,128]{1,0:T(8,128)(2,1)S(1)} %collective-permute-done.14.refs_2_.refs_6_), channel_id=1, source_target_pairs={{0,16},{1,17},{2,18},{3,19},{4,20},{5,21},{6,22},{7,23},{8,24},{9,... | collective-permute-start | bytes 245768 | tf_op jit(solution)/shard_map/ppermute | solution.py:400
  58.4 2.8 %collective-permute-done.17.refs_2_.refs_10_ = bf16[320,128]{1,0:T(8,128)(2,1)S(1)} collective-permute-done((bf16[320,128]{1,0:T(8,128)(2,1)S(1)}, bf16[320,128]{1,0:T(8,128)(2,1)S(1)}, u32[]{:S(2)}, u32[]{:S(2)}) %collective-permute-start.17) | collective-permute-done | bytes 81952 | tf_op jit(solution)/shard_map/ppermute | solution.py:400
  61.5 2.4 %collective-permute-start.23 = (bf16[1024,128]{1,0:T(8,128)(2,1)S(1)}, bf16[1024,128]{1,0:T(8,128)(2,1)S(1)}, u32[]{:S(2)}, u32[]{:S(2)}) collective-permute-start(bf16[1024,128]{1,0:T(8,128)(2,1)S(1)} %get-tuple-element.50.refs_6_.adj_ref), channel_id=1, source_target_pairs={{0,1},{1,0},{2,3},{3,2},{4,5},{5,4},{6,7},{7,6},{8,9},{9,8},{10,11... | collective-permute-start | bytes 786440 | tf_op jit(solution)/shard_map/ppermute | solution.py:400
  63.9 1.2 %collective-permute-start.20 = (bf16[704,128]{1,0:T(8,128)(2,1)S(1)}, bf16[704,128]{1,0:T(8,128)(2,1)S(1)}, u32[]{:S(2)}, u32[]{:S(2)}) collective-permute-start(bf16[704,128]{1,0:T(8,128)(2,1)S(1)} %get-tuple-element.49), channel_id=1, source_target_pairs={{0,8},{1,9},{2,10},{3,11},{4,12},{5,13},{6,14},{7,15},{8,0},{9,1},... | collective-permute-start | bytes 540680 | tf_op jit(solution)/shard_map/ppermute | solution.py:400
  65.2 3.6 %collective-permute-done.20.refs_7_ = bf16[704,128]{1,0:T(8,128)(2,1)S(1)} collective-permute-done((bf16[704,128]{1,0:T(8,128)(2,1)S(1)}, bf16[704,128]{1,0:T(8,128)(2,1)S(1)}, u32[]{:S(2)}, u32[]{:S(2)}) %collective-permute-start.20) | collective-permute-done | bytes 180256 | tf_op jit(solution)/shard_map/ppermute | solution.py:400
  70.1 1.2 %collective-permute-start.24 = (f32[256,128]{1,0:T(8,128)S(1)}, f32[256,128]{1,0:T(8,128)S(1)}, u32[]{:S(2)}, u32[]{:S(2)}) collective-permute-start(f32[256,128]{1,0:T(8,128)S(1)} %grad_block.1.refs_0_), channel_id=1, source_target_pairs={{0,1},{1,0},{2,3},{3,2},{4,5},{5,4},{6,7},{7,6},{8,9},{9,8},{10,11... | collective-permute-start | bytes 393224 | tf_op jit(solution)/shard_map/ppermute | solution.py:400
  71.3 1.8 %tile_product.6.refs_12_ = f32[1024,128]{1,0:T(8,128)S(1)} custom-call(s32[2,40]{1,0:T(2,128)S(1)} %collective-permute-done.7.refs_0_, s32[2,40]{1,0:T(2,128)S(1)} %slot_blocks.1.refs_0_.refs_1_, s32[2,40]{1,0:T(2,128)S(1)} %collective-permute-done.8.refs_1_.refs_2_, bf16[5,8,128,128]{3,2,1,0:T(8,128)(2,1)S(1)} %collective-permute-done.1.refs_1_.refs_3_, ...), custom_call_target="tpu_custom_call" | custom-call | flops 134217728 | bytes 1572864 | tf_op jit(solution)/shard_map/tile_product/pallas_call | solution.py:234
  73.2 1.4 %collective-permute-done.21.refs_9_ = bf16[704,128]{1,0:T(8,128)(2,1)S(1)} collective-permute-done((bf16[704,128]{1,0:T(8,128)(2,1)S(1)}, bf16[704,128]{1,0:T(8,128)(2,1)S(1)}, u32[]{:S(2)}, u32[]{:S(2)}) %collective-permute-start.21) | collective-permute-done | bytes 180256 | tf_op jit(solution)/shard_map/ppermute | solution.py:400
  74.5 3.5 %collective-permute-done.22.refs_11_ = bf16[704,128]{1,0:T(8,128)(2,1)S(1)} collective-permute-done((bf16[704,128]{1,0:T(8,128)(2,1)S(1)}, bf16[704,128]{1,0:T(8,128)(2,1)S(1)}, u32[]{:S(2)}, u32[]{:S(2)}) %collective-permute-start.22) | collective-permute-done | bytes 180256 | tf_op jit(solution)/shard_map/ppermute | solution.py:400
  78.1 3.3 %tile_product.7.refs_2_ = bf16[1024,128]{1,0:T(8,128)(2,1)S(1)} custom-call(s32[2,40]{1,0:T(2,128)S(1)} %collective-permute-done.7.refs_0_, s32[2,40]{1,0:T(2,128)S(1)} %slot_blocks.1.refs_0_.refs_1_, s32[2,40]{1,0:T(2,128)S(1)} %collective-permute-done.8.refs_1_.refs_2_, bf16[5,8,128,128]{3,2,1,0:T(8,128)(2,1)S(1)} %collective-permute-done.1.refs_1_.refs_3_, ...), custom_call_target="tpu_custom_call" | custom-call | flops 201326592 | bytes 2359296 | tf_op jit(solution)/shard_map/tile_product/pallas_call | solution.py:234
  81.4 3.2 %collective-permute-start.25 = (bf16[1024,128]{1,0:T(8,128)(2,1)S(1)}, bf16[1024,128]{1,0:T(8,128)(2,1)S(1)}, u32[]{:S(2)}, u32[]{:S(2)}) collective-permute-start(bf16[1024,128]{1,0:T(8,128)(2,1)S(1)} %tile_product.7.refs_2_), channel_id=1, source_target_pairs={{0,2},{1,3},{2,0},{3,1},{4,6},{5,7},{6,4},{7,5},{8,10},{9,11},{10,... | collective-permute-start | bytes 786440 | tf_op jit(solution)/shard_map/ppermute | solution.py:400
  84.6 1.4 %collective-permute-start.18 = (bf16[1024,128]{1,0:T(8,128)(2,1)S(1)}, bf16[1024,128]{1,0:T(8,128)(2,1)S(1)}, u32[]{:S(2)}, u32[]{:S(2)}) collective-permute-start(bf16[1024,128]{1,0:T(8,128)(2,1)S(1)} %get-tuple-element.48), channel_id=1, source_target_pairs={{0,1},{1,5},{2,3},{3,7},{4,0},{5,4},{6,2},{7,6},{8,9},{9,13},{10,1... | collective-permute-start | bytes 786440 | tf_op jit(solution)/shard_map/ppermute | solution.py:400
  86.0 2.0 %collective-permute-start.19 = (bf16[1024,128]{1,0:T(8,128)(2,1)S(1)}, bf16[1024,128]{1,0:T(8,128)(2,1)S(1)}, u32[]{:S(2)}, u32[]{:S(2)}) collective-permute-start(bf16[1024,128]{1,0:T(8,128)(2,1)S(1)} %get-tuple-element.48), channel_id=1, source_target_pairs={{1,4},{3,6},{4,1},{6,3},{9,12},{11,14},{12,9},{14,11},{17,20},{19,... | collective-permute-start | bytes 786440 | tf_op jit(solution)/shard_map/ppermute | solution.py:400
  88.1 1.4 %collective-permute-start.28 = (f32[256,128]{1,0:T(8,128)S(1)}, f32[256,128]{1,0:T(8,128)S(1)}, u32[]{:S(2)}, u32[]{:S(2)}) collective-permute-start(f32[256,128]{1,0:T(8,128)S(1)} %add_after.4.refs_0_), channel_id=1, source_target_pairs={{0,8},{1,9},{2,10},{3,11},{4,12},{5,13},{6,14},{7,15},{8,0},{9,1},... | collective-permute-start | bytes 393224 | tf_op jit(solution)/shard_map/ppermute | solution.py:400
  89.4 0.7 collective-permute-start.29
  90.2 6.0 %collective-permute-done.25 = bf16[1024,128]{1,0:T(8,128)(2,1)S(1)} collective-permute-done((bf16[1024,128]{1,0:T(8,128)(2,1)S(1)}, bf16[1024,128]{1,0:T(8,128)(2,1)S(1)}, u32[]{:S(2)}, u32[]{:S(2)}) %collective-permute-start.25) | collective-permute-done | bytes 262176 | tf_op jit(solution)/shard_map/ppermute | solution.py:400
  96.3 0.9 collective-permute-start.26
  97.2 2.2 %collective-permute-start.27 = (bf16[1024,128]{1,0:T(8,128)(2,1)S(1)}, bf16[1024,128]{1,0:T(8,128)(2,1)S(1)}, u32[]{:S(2)}, u32[]{:S(2)}) collective-permute-start(bf16[1024,128]{1,0:T(8,128)(2,1)S(1)} %add_convert_fusion.refs_4_.own_ref), channel_id=1, source_target_pairs={{1,4},{3,6},{4,1},{6,3},{9,12},{11,14},{12,9},{14,11},{17,20},{19,... | collective-permute-start | bytes 786440 | tf_op jit(solution)/shard_map/ppermute | solution.py:400
  99.4 2.2 %collective-permute-done.30.refs_3_ = f32[256,128]{1,0:T(8,128)S(1)} collective-permute-done((f32[256,128]{1,0:T(8,128)S(1)}, f32[256,128]{1,0:T(8,128)S(1)}, u32[]{:S(2)}, u32[]{:S(2)}) %collective-permute-start.30) | collective-permute-done | bytes 131104 | tf_op jit(solution)/shard_map/ppermute | solution.py:400
  101.6 1.5 %collective-permute-start.31 = (f32[256,128]{1,0:T(8,128)S(1)}, f32[256,128]{1,0:T(8,128)S(1)}, u32[]{:S(2)}, u32[]{:S(2)}) collective-permute-start(f32[256,128]{1,0:T(8,128)S(1)} %add_after.5.grad_ref), channel_id=1, source_target_pairs={{0,4},{1,5},{2,6},{3,7},{4,0},{5,1},{6,2},{7,3},{8,12},{9,13},{10,... | collective-permute-start | bytes 393224 | tf_op jit(solution)/shard_map/ppermute | solution.py:400
  103.2 0.9 pad_maximum_fusion
  104.1 0.8 collective-permute-done.27.two_ref
  104.9 1.3 %final.1 = (bf16[1024,256]{1,0:T(8,128)(2,1)}, f32[256,256]{1,0:T(8,128)}) custom-call(bf16[1024,128]{1,0:T(8,128)(2,1)S(1)} %add_convert_fusion.refs_4_.own_ref, bf16[1024,128]{1,0:T(8,128)(2,1)S(1)} %collective-permute-done.26.one_ref, bf16[1024,128]{1,0:T(8,128)(2,1)S(1)} %collective-permute-done.27.two_ref, bf16[256,256]{1,0:T(8,128)(2,1)S(1)} %copy-done.1, ...), custom_call_target="tpu_custom_call" | custom-call | flops 134217728 | bytes 2097152 | tf_op jit(solution)/shard_map/final/pallas_call | solution.py:375
  (47 shorter events, 6.2 us)
Async XLA Ops:
  0.6 30.1 %collective-permute-start.1 = (bf16[5,8,128,128]{3,2,1,0:T(8,128)(2,1)}, bf16[5,8,128,128]{3,2,1,0:T(8,128)(2,1)S(1)}, u32[]{:S(2)}, u32[]{:S(2)}) collective-permute-start(bf16[5,8,128,128]{3,2,1,0:T(8,128)(2,1)} %bitcast.5), channel_id=1, source_target_pairs={{0,4},{1,0},{2,6},{3,2},{4,5},{5,1},{6,7},{7,3},{8,12},{9,8},{10,1... | collective-permute-start | bytes 3932168 | tf_op jit(solution)/shard_map/ppermute | solution.py:400
  2.8 1.0 copy-start.2
  4.0 1.6 %collective-permute-start = (bf16[1024,128]{1,0:T(8,128)(2,1)S(1)}, bf16[1024,128]{1,0:T(8,128)(2,1)S(1)}, u32[]{:S(2)}, u32[]{:S(2)}) collective-permute-start(bf16[1024,128]{1,0:T(8,128)(2,1)S(1)} %get-tuple-element.29), channel_id=1, source_target_pairs={{0,4},{1,5},{2,6},{3,7},{4,0},{5,1},{6,2},{7,3},{8,12},{9,13},{10,... | collective-permute-start | bytes 786440 | tf_op jit(solution)/shard_map/ppermute | solution.py:400
  5.9 6.1 %collective-permute-start.4 = (bf16[704,128]{1,0:T(8,128)(2,1)S(1)}, bf16[704,128]{1,0:T(8,128)(2,1)S(1)}, u32[]{:S(2)}, u32[]{:S(2)}) collective-permute-start(bf16[704,128]{1,0:T(8,128)(2,1)S(1)} %get-tuple-element.34.refs_3_.refs_5_), channel_id=1, source_target_pairs={{0,8},{1,9},{2,10},{3,11},{4,12},{5,13},{6,14},{7,15},{8,0},{9,1},... | collective-permute-start | bytes 540680 | tf_op jit(solution)/shard_map/ppermute | solution.py:400
  7.2 23.5 %collective-permute-start.6 = (bf16[1024,128]{1,0:T(8,128)(2,1)S(1)}, bf16[1024,128]{1,0:T(8,128)(2,1)S(1)}, u32[]{:S(2)}, u32[]{:S(2)}) collective-permute-start(bf16[1024,128]{1,0:T(8,128)(2,1)S(1)} %get-tuple-element.37.refs_4_.refs_6_), channel_id=1, source_target_pairs={{0,8},{1,25},{2,10},{3,27},{4,12},{5,29},{6,14},{7,31},{8,16},{9,1... | collective-permute-start | bytes 786440 | tf_op jit(solution)/shard_map/ppermute | solution.py:400
  12.0 18.8 %collective-permute-start.5 = (bf16[704,128]{1,0:T(8,128)(2,1)S(1)}, bf16[704,128]{1,0:T(8,128)(2,1)S(1)}, u32[]{:S(2)}, u32[]{:S(2)}) collective-permute-start(bf16[704,128]{1,0:T(8,128)(2,1)S(1)} %collective-permute-done.4.refs_6_.refs_8_), channel_id=1, source_target_pairs={{0,16},{1,17},{2,18},{3,19},{4,20},{5,21},{6,22},{7,23},{8,24},{9,... | collective-permute-start | bytes 540680 | tf_op jit(solution)/shard_map/ppermute | solution.py:400
  13.3 6.2 %collective-permute-start.2 = (bf16[320,128]{1,0:T(8,128)(2,1)S(1)}, bf16[320,128]{1,0:T(8,128)(2,1)S(1)}, u32[]{:S(2)}, u32[]{:S(2)}) collective-permute-start(bf16[320,128]{1,0:T(8,128)(2,1)S(1)} %get-tuple-element.33.refs_2_.refs_4_), channel_id=1, source_target_pairs={{0,8},{1,9},{2,10},{3,11},{4,12},{5,13},{6,14},{7,15},{8,0},{9,1},... | collective-permute-start | bytes 245768 | tf_op jit(solution)/shard_map/ppermute | solution.py:400
  19.4 11.3 %collective-permute-start.3 = (bf16[320,128]{1,0:T(8,128)(2,1)S(1)}, bf16[320,128]{1,0:T(8,128)(2,1)S(1)}, u32[]{:S(2)}, u32[]{:S(2)}) collective-permute-start(bf16[320,128]{1,0:T(8,128)(2,1)S(1)} %collective-permute-done.2.refs_5_.refs_7_), channel_id=1, source_target_pairs={{0,16},{1,17},{2,18},{3,19},{4,20},{5,21},{6,22},{7,23},{8,24},{9,... | collective-permute-start | bytes 245768 | tf_op jit(solution)/shard_map/ppermute | solution.py:400
  21.4 0.7 copy-start.4
  23.4 12.3 %copy-start = (bf16[1,5,8,128,128]{4,3,2,1,0:T(8,128)(2,1)S(1)}, bf16[1,5,8,128,128]{4,3,2,1,0:T(8,128)(2,1)}, u32[]{:S(2)}) copy-start(bf16[1,5,8,128,128]{4,3,2,1,0:T(8,128)(2,1)} %param.9) | copy-start | bytes 3932164
  23.4 1.9 %collective-permute-start.7 = (s32[2,40]{1,0:T(2,128)S(1)}, s32[2,40]{1,0:T(2,128)S(1)}, u32[]{:S(2)}, u32[]{:S(2)}) collective-permute-start(s32[2,40]{1,0:T(2,128)S(1)} %slot_blocks.1.refs_0_.refs_1_), channel_id=1, source_target_pairs={{0,4},{1,0},{2,6},{3,2},{4,5},{5,1},{6,7},{7,3},{8,12},{9,8},{10,1... | collective-permute-start | bytes 968 | tf_op jit(solution)/shard_map/ppermute | solution.py:400
  25.3 5.4 %collective-permute-start.8 = (s32[2,40]{1,0:T(2,128)S(1)}, s32[2,40]{1,0:T(2,128)S(1)}, u32[]{:S(2)}, u32[]{:S(2)}) collective-permute-start(s32[2,40]{1,0:T(2,128)S(1)} %slot_blocks.1.refs_0_.refs_1_), channel_id=1, source_target_pairs={{1,4},{3,6},{4,1},{6,3},{9,12},{11,14},{12,9},{14,11},{17,20},{19,... | collective-permute-start | bytes 968 | tf_op jit(solution)/shard_map/ppermute | solution.py:400
  30.8 4.9 %collective-permute-start.9 = (bf16[5,8,128,128]{3,2,1,0:T(8,128)(2,1)S(1)}, bf16[5,8,128,128]{3,2,1,0:T(8,128)(2,1)S(1)}, u32[]{:S(2)}, u32[]{:S(2)}) collective-permute-start(bf16[5,8,128,128]{3,2,1,0:T(8,128)(2,1)S(1)} %collective-permute-done.1.refs_1_.refs_3_), channel_id=1, source_target_pairs={{0,4},{2,6},{5,1},{7,3},{8,12},{10,14},{13,9},{15,11},{16,20},{18,... | collective-permute-start | bytes 3932168 | tf_op jit(solution)/shard_map/ppermute | solution.py:400
  35.2 6.0 %copy-start.3 = (bf16[1024,256]{1,0:T(8,128)(2,1)S(1)}, bf16[1024,256]{1,0:T(8,128)(2,1)}, u32[]{:S(2)}) copy-start(bf16[1024,256]{1,0:T(8,128)(2,1)} %x_ref.3) | copy-start | bytes 1572868
  35.2 12.7 %copy-start.1 = (bf16[256,256]{1,0:T(8,128)(2,1)S(1)}, bf16[256,256]{1,0:T(8,128)(2,1)}, u32[]{:S(2)}) copy-start(bf16[256,256]{1,0:T(8,128)(2,1)} %w_ref.5) | copy-start | bytes 393220
  38.9 4.3 %collective-permute-start.11 = (bf16[320,128]{1,0:T(8,128)(2,1)S(1)}, bf16[320,128]{1,0:T(8,128)(2,1)S(1)}, u32[]{:S(2)}, u32[]{:S(2)}) collective-permute-start(bf16[320,128]{1,0:T(8,128)(2,1)S(1)} %get-tuple-element.43), channel_id=1, source_target_pairs={{0,2},{1,3},{2,0},{3,1},{4,6},{5,7},{6,4},{7,5},{8,10},{9,11},{10,... | collective-permute-start | bytes 245768 | tf_op jit(solution)/shard_map/ppermute | solution.py:400
  41.4 5.6 %collective-permute-start.13 = (bf16[1024,128]{1,0:T(8,128)(2,1)S(1)}, bf16[1024,128]{1,0:T(8,128)(2,1)S(1)}, u32[]{:S(2)}, u32[]{:S(2)}) collective-permute-start(bf16[1024,128]{1,0:T(8,128)(2,1)S(1)} %get-tuple-element.45), channel_id=1, source_target_pairs={{0,4},{1,5},{2,6},{3,7},{4,0},{5,1},{6,2},{7,3},{8,12},{9,13},{10,... | collective-permute-start | bytes 786440 | tf_op jit(solution)/shard_map/ppermute | solution.py:400
  42.5 11.4 %collective-permute-start.10 = (bf16[704,128]{1,0:T(8,128)(2,1)S(1)}, bf16[704,128]{1,0:T(8,128)(2,1)S(1)}, u32[]{:S(2)}, u32[]{:S(2)}) collective-permute-start(bf16[704,128]{1,0:T(8,128)(2,1)S(1)} %get-tuple-element.42.refs_0_), channel_id=1, source_target_pairs={{0,2},{1,3},{2,0},{3,1},{4,6},{5,7},{6,4},{7,5},{8,10},{9,11},{10,... | collective-permute-start | bytes 540680 | tf_op jit(solution)/shard_map/ppermute | solution.py:400
  43.2 4.8 %collective-permute-start.12 = (bf16[320,128]{1,0:T(8,128)(2,1)S(1)}, bf16[320,128]{1,0:T(8,128)(2,1)S(1)}, u32[]{:S(2)}, u32[]{:S(2)}) collective-permute-start(bf16[320,128]{1,0:T(8,128)(2,1)S(1)} %add_convert_fusion.1.near_ref.near_a), channel_id=1, source_target_pairs={{0,4},{1,5},{2,6},{3,7},{4,0},{5,1},{6,2},{7,3},{8,12},{9,13},{10,... | collective-permute-start | bytes 245768 | tf_op jit(solution)/shard_map/ppermute | solution.py:400
  48.2 5.7 %collective-permute-start.14 = (bf16[320,128]{1,0:T(8,128)(2,1)S(1)}, bf16[320,128]{1,0:T(8,128)(2,1)S(1)}, u32[]{:S(2)}, u32[]{:S(2)}) collective-permute-start(bf16[320,128]{1,0:T(8,128)(2,1)S(1)} %get-tuple-element.46.refs_1_), channel_id=1, source_target_pairs={{0,8},{1,9},{2,10},{3,11},{4,12},{5,13},{6,14},{7,15},{8,0},{9,1},... | collective-permute-start | bytes 245768 | tf_op jit(solution)/shard_map/ppermute | solution.py:400
  49.4 6.8 %collective-permute-start.15 = (bf16[320,128]{1,0:T(8,128)(2,1)S(1)}, bf16[320,128]{1,0:T(8,128)(2,1)S(1)}, u32[]{:S(2)}, u32[]{:S(2)}) collective-permute-start(bf16[320,128]{1,0:T(8,128)(2,1)S(1)} %get-tuple-element.46.refs_1_), channel_id=1, source_target_pairs={{0,25},{1,8},{2,27},{3,10},{4,29},{5,12},{6,31},{7,14},{8,1},{9,16... | collective-permute-start | bytes 245768 | tf_op jit(solution)/shard_map/ppermute | solution.py:400
  56.3 5.0 %collective-permute-start.16 = (bf16[704,128]{1,0:T(8,128)(2,1)S(1)}, bf16[704,128]{1,0:T(8,128)(2,1)S(1)}, u32[]{:S(2)}, u32[]{:S(2)}) collective-permute-start(bf16[704,128]{1,0:T(8,128)(2,1)S(1)} %add_after.3.near_ref.near_b), channel_id=1, source_target_pairs={{0,4},{1,5},{2,6},{3,7},{4,0},{5,1},{6,2},{7,3},{8,12},{9,13},{10,... | collective-permute-start | bytes 540680 | tf_op jit(solution)/shard_map/ppermute | solution.py:400
  57.2 4.0 %collective-permute-start.17 = (bf16[320,128]{1,0:T(8,128)(2,1)S(1)}, bf16[320,128]{1,0:T(8,128)(2,1)S(1)}, u32[]{:S(2)}, u32[]{:S(2)}) collective-permute-start(bf16[320,128]{1,0:T(8,128)(2,1)S(1)} %collective-permute-done.14.refs_2_.refs_6_), channel_id=1, source_target_pairs={{0,16},{1,17},{2,18},{3,19},{4,20},{5,21},{6,22},{7,23},{8,24},{9,... | collective-permute-start | bytes 245768 | tf_op jit(solution)/shard_map/ppermute | solution.py:400
  61.5 8.2 %collective-permute-start.23 = (bf16[1024,128]{1,0:T(8,128)(2,1)S(1)}, bf16[1024,128]{1,0:T(8,128)(2,1)S(1)}, u32[]{:S(2)}, u32[]{:S(2)}) collective-permute-start(bf16[1024,128]{1,0:T(8,128)(2,1)S(1)} %get-tuple-element.50.refs_6_.adj_ref), channel_id=1, source_target_pairs={{0,1},{1,0},{2,3},{3,2},{4,5},{5,4},{6,7},{7,6},{8,9},{9,8},{10,11... | collective-permute-start | bytes 786440 | tf_op jit(solution)/shard_map/ppermute | solution.py:400
  63.9 4.9 %collective-permute-start.20 = (bf16[704,128]{1,0:T(8,128)(2,1)S(1)}, bf16[704,128]{1,0:T(8,128)(2,1)S(1)}, u32[]{:S(2)}, u32[]{:S(2)}) collective-permute-start(bf16[704,128]{1,0:T(8,128)(2,1)S(1)} %get-tuple-element.49), channel_id=1, source_target_pairs={{0,8},{1,9},{2,10},{3,11},{4,12},{5,13},{6,14},{7,15},{8,0},{9,1},... | collective-permute-start | bytes 540680 | tf_op jit(solution)/shard_map/ppermute | solution.py:400
  65.1 9.4 %collective-permute-start.21 = (bf16[704,128]{1,0:T(8,128)(2,1)S(1)}, bf16[704,128]{1,0:T(8,128)(2,1)S(1)}, u32[]{:S(2)}, u32[]{:S(2)}) collective-permute-start(bf16[704,128]{1,0:T(8,128)(2,1)S(1)} %get-tuple-element.49), channel_id=1, source_target_pairs={{0,25},{1,8},{2,27},{3,10},{4,29},{5,12},{6,31},{7,14},{8,1},{9,16... | collective-permute-start | bytes 540680 | tf_op jit(solution)/shard_map/ppermute | solution.py:400
  68.8 9.2 %collective-permute-start.22 = (bf16[704,128]{1,0:T(8,128)(2,1)S(1)}, bf16[704,128]{1,0:T(8,128)(2,1)S(1)}, u32[]{:S(2)}, u32[]{:S(2)}) collective-permute-start(bf16[704,128]{1,0:T(8,128)(2,1)S(1)} %collective-permute-done.20.refs_7_), channel_id=1, source_target_pairs={{0,16},{1,17},{2,18},{3,19},{4,20},{5,21},{6,22},{7,23},{8,24},{9,... | collective-permute-start | bytes 540680 | tf_op jit(solution)/shard_map/ppermute | solution.py:400
  70.1 7.9 %collective-permute-start.24 = (f32[256,128]{1,0:T(8,128)S(1)}, f32[256,128]{1,0:T(8,128)S(1)}, u32[]{:S(2)}, u32[]{:S(2)}) collective-permute-start(f32[256,128]{1,0:T(8,128)S(1)} %grad_block.1.refs_0_), channel_id=1, source_target_pairs={{0,1},{1,0},{2,3},{3,2},{4,5},{5,4},{6,7},{7,6},{8,9},{9,8},{10,11... | collective-permute-start | bytes 393224 | tf_op jit(solution)/shard_map/ppermute | solution.py:400
  81.4 14.8 %collective-permute-start.25 = (bf16[1024,128]{1,0:T(8,128)(2,1)S(1)}, bf16[1024,128]{1,0:T(8,128)(2,1)S(1)}, u32[]{:S(2)}, u32[]{:S(2)}) collective-permute-start(bf16[1024,128]{1,0:T(8,128)(2,1)S(1)} %tile_product.7.refs_2_), channel_id=1, source_target_pairs={{0,2},{1,3},{2,0},{3,1},{4,6},{5,7},{6,4},{7,5},{8,10},{9,11},{10,... | collective-permute-start | bytes 786440 | tf_op jit(solution)/shard_map/ppermute | solution.py:400
  84.6 18.5 %collective-permute-start.18 = (bf16[1024,128]{1,0:T(8,128)(2,1)S(1)}, bf16[1024,128]{1,0:T(8,128)(2,1)S(1)}, u32[]{:S(2)}, u32[]{:S(2)}) collective-permute-start(bf16[1024,128]{1,0:T(8,128)(2,1)S(1)} %get-tuple-element.48), channel_id=1, source_target_pairs={{0,1},{1,5},{2,3},{3,7},{4,0},{5,4},{6,2},{7,6},{8,9},{9,13},{10,1... | collective-permute-start | bytes 786440 | tf_op jit(solution)/shard_map/ppermute | solution.py:400
  86.0 17.1 %collective-permute-start.19 = (bf16[1024,128]{1,0:T(8,128)(2,1)S(1)}, bf16[1024,128]{1,0:T(8,128)(2,1)S(1)}, u32[]{:S(2)}, u32[]{:S(2)}) collective-permute-start(bf16[1024,128]{1,0:T(8,128)(2,1)S(1)} %get-tuple-element.48), channel_id=1, source_target_pairs={{1,4},{3,6},{4,1},{6,3},{9,12},{11,14},{12,9},{14,11},{17,20},{19,... | collective-permute-start | bytes 786440 | tf_op jit(solution)/shard_map/ppermute | solution.py:400
  88.1 8.2 %collective-permute-start.28 = (f32[256,128]{1,0:T(8,128)S(1)}, f32[256,128]{1,0:T(8,128)S(1)}, u32[]{:S(2)}, u32[]{:S(2)}) collective-permute-start(f32[256,128]{1,0:T(8,128)S(1)} %add_after.4.refs_0_), channel_id=1, source_target_pairs={{0,8},{1,9},{2,10},{3,11},{4,12},{5,13},{6,14},{7,15},{8,0},{9,1},... | collective-permute-start | bytes 393224 | tf_op jit(solution)/shard_map/ppermute | solution.py:400
  89.4 7.8 %collective-permute-start.29 = (f32[256,128]{1,0:T(8,128)S(1)}, f32[256,128]{1,0:T(8,128)S(1)}, u32[]{:S(2)}, u32[]{:S(2)}) collective-permute-start(f32[256,128]{1,0:T(8,128)S(1)} %add_after.4.refs_0_), channel_id=1, source_target_pairs={{0,16},{1,17},{2,18},{3,19},{4,20},{5,21},{6,22},{7,23},{8,24},{9,... | collective-permute-start | bytes 393224 | tf_op jit(solution)/shard_map/ppermute | solution.py:400
  96.2 5.4 %collective-permute-start.30 = (f32[256,128]{1,0:T(8,128)S(1)}, f32[256,128]{1,0:T(8,128)S(1)}, u32[]{:S(2)}, u32[]{:S(2)}) collective-permute-start(f32[256,128]{1,0:T(8,128)S(1)} %add_after.4.refs_0_), channel_id=1, source_target_pairs={{0,24},{1,25},{2,26},{3,27},{4,28},{5,29},{6,30},{7,31},{8,16},{9,... | collective-permute-start | bytes 393224 | tf_op jit(solution)/shard_map/ppermute | solution.py:400
  96.3 7.8 %collective-permute-start.26 = (bf16[1024,128]{1,0:T(8,128)(2,1)S(1)}, bf16[1024,128]{1,0:T(8,128)(2,1)S(1)}, u32[]{:S(2)}, u32[]{:S(2)}) collective-permute-start(bf16[1024,128]{1,0:T(8,128)(2,1)S(1)} %add_convert_fusion.refs_4_.own_ref), channel_id=1, source_target_pairs={{0,1},{1,5},{2,3},{3,7},{4,0},{5,4},{6,2},{7,6},{8,9},{9,13},{10,1... | collective-permute-start | bytes 786440 | tf_op jit(solution)/shard_map/ppermute | solution.py:400
  97.2 7.7 %collective-permute-start.27 = (bf16[1024,128]{1,0:T(8,128)(2,1)S(1)}, bf16[1024,128]{1,0:T(8,128)(2,1)S(1)}, u32[]{:S(2)}, u32[]{:S(2)}) collective-permute-start(bf16[1024,128]{1,0:T(8,128)(2,1)S(1)} %add_convert_fusion.refs_4_.own_ref), channel_id=1, source_target_pairs={{1,4},{3,6},{4,1},{6,3},{9,12},{11,14},{12,9},{14,11},{17,20},{19,... | collective-permute-start | bytes 786440 | tf_op jit(solution)/shard_map/ppermute | solution.py:400
  101.6 2.5 %collective-permute-start.31 = (f32[256,128]{1,0:T(8,128)S(1)}, f32[256,128]{1,0:T(8,128)S(1)}, u32[]{:S(2)}, u32[]{:S(2)}) collective-permute-start(f32[256,128]{1,0:T(8,128)S(1)} %add_after.5.grad_ref), channel_id=1, source_target_pairs={{0,4},{1,5},{2,6},{3,7},{4,0},{5,1},{6,2},{7,3},{8,12},{9,13},{10,... | collective-permute-start | bytes 393224 | tf_op jit(solution)/shard_map/ppermute | solution.py:400

commit v5 on v3

--- a/solution.py
+++ b/solution.py
@@ -8,6 +8,7 @@
 from jax.sharding import PartitionSpec as P
 
 AXES = ("rows", "rep")
+TOGETHER = 4
 
 
 def route(shape, move):
@@ -57,33 +58,42 @@
     )(value)
 
 
-def pick_kernel(home_ref, away_ref, out_ref, sem):
+def pick_kernel(mine_ref, swapped_ref, group_ref, other_ref, sems):
     j, _, p = place()
+
+    def copies(own, other):
+        return [
+            pltpu.make_async_copy(own, group_ref, sems.at[0]),
+            pltpu.make_async_copy(other, other_ref, sems.at[1]),
+        ]
 
     @pl.when(j == p)
     def _():
-        copy = pltpu.make_async_copy(home_ref, out_ref, sem)
-        copy.start()
-        copy.wait()
+        for copy in copies(mine_ref, swapped_ref):
+            copy.start()
+        for copy in copies(mine_ref, swapped_ref):
+            copy.wait()
 
     @pl.when(j != p)
     def _():
-        copy = pltpu.make_async_copy(away_ref, out_ref, sem)
-        copy.start()
-        copy.wait()
-
-
-def pick(home, away):
+        for copy in copies(swapped_ref, mine_ref):
+            copy.start()
+        for copy in copies(swapped_ref, mine_ref):
+            copy.wait()
+
+
+def pick(mine, swapped):
     hbm = pl.BlockSpec(memory_space=pltpu.HBM)
+    shape = jax.ShapeDtypeStruct(mine.shape, mine.dtype)
     return pl.pallas_call(
         pick_kernel,
-        out_shape=jax.ShapeDtypeStruct(home.shape, home.dtype),
+        out_shape=(shape, shape),
         in_specs=[hbm, hbm],
-        out_specs=hbm,
-        scratch_shapes=[pltpu.SemaphoreType.DMA],
+        out_specs=(hbm, hbm),
+        scratch_shapes=[pltpu.SemaphoreType.DMA((2,))],
         compiler_params=pltpu.CompilerParams(vmem_limit_bytes=1024 * 1024),
         name="pick",
-    )(home, away)
+    )(mine, swapped)
 
 
 def slots_kernel(dead, coords_ref, counts_ref, out_ref):
@@ -109,29 +119,24 @@
 
 
 def offset_of(kind):
-    j, _, p = place()
-    home = j == p
-    near, far = jnp.where(p == 0, 3, 1), jnp.where(p == 0, 1, 3)
+    _, _, p = place()
+    even = (lax.axis_index("rows") // 2) % 2 == 0
     return {
         "self": 2,
-        "left": 0,
-        "right": 4,
-        "near": near,
-        "far": far,
-        "mine": jnp.where(home, 2, near),
-        "swapped": jnp.where(home, near, 2),
-        "one": jnp.where(home, 0, far),
-        "two": jnp.where(home, far, 0),
+        "near": jnp.where(p == 0, 3, 1),
+        "far": jnp.where(p == 0, 1, 3),
+        "direct": jnp.where(even, 4, 0),
+        "second": jnp.where(even, 0, 4),
     }[kind]
 
 
-def tile_kernel(kinds, sets, summed, *refs):
+def tile_kernel(kinds, sets, summed, waits, *refs):
     refs = list(refs)
-    metas = [refs.pop(0) for _ in range(sum(len(s) for s in sets))]
-    tiles = [refs.pop(0) for _ in range(sum(len(s) for s in sets))]
+    metas = [refs.pop(0) for _ in range(sum(sets))]
+    tiles = [refs.pop(0) for _ in range(sum(sets))]
     panels = [refs.pop(0) for _ in kinds]
     before = refs.pop(0) if summed else None
-    out_ref, acc_ref, tile_buf, panel_buf, tile_sems, panel_sems = refs
+    out_ref, acc_ref, tile_buf, panel_buf, tile_sems, panel_sems = refs[waits:]
     slots, tile = tile_buf.shape[2], tile_buf.shape[-1]
     rows = out_ref.shape[0]
     j, _, p = place()
@@ -148,7 +153,7 @@
         panel_copy(i).start()
         at = 0
         for s, members in enumerate(sets):
-            if len(members) == 1:
+            if members == 1:
                 tile_copy(tiles[at], i, s).start()
             else:
 
@@ -160,7 +165,7 @@
                 def _(ref=tiles[at + 1], i=i, s=s):
                     tile_copy(ref, i, s).start()
 
-            at += len(members)
+            at += members
     if summed:
         acc_ref[:rows, :] = before[...]
     else:
@@ -171,25 +176,28 @@
         at = 0
         for s, members in enumerate(sets):
             tile_copy(tiles[at], i, s).wait()
-            for k in range(slots):
-                row = metas[at][0, d * slots + k]
-                col = metas[at][1, d * slots + k]
-                if len(members) == 2:
-                    row = jnp.where(home, row, metas[at + 1][0, d * slots + k])
-                    col = jnp.where(home, col, metas[at + 1][1, d * slots + k])
-                row = pl.multiple_of(row * tile, tile)
-                col = pl.multiple_of(col * tile, tile)
-                prod = jnp.dot(
-                    tile_buf[i, s, k],
-                    panel_buf[i, pl.ds(col, tile), :],
-                    preferred_element_type=jnp.float32,
-                )
-                acc_ref[pl.ds(row, tile), :] += prod
-            at += len(members)
+            for first in range(0, slots, TOGETHER):
+                prods = []
+                for k in range(first, min(first + TOGETHER, slots)):
+                    row = metas[at][0, d * slots + k]
+                    col = metas[at][1, d * slots + k]
+                    if members == 2:
+                        row = jnp.where(home, row, metas[at + 1][0, d * slots + k])
+                        col = jnp.where(home, col, metas[at + 1][1, d * slots + k])
+                    col = pl.multiple_of(col * tile, tile)
+                    prod = jnp.dot(
+                        tile_buf[i, s, k],
+                        panel_buf[i, pl.ds(col, tile), :],
+                        preferred_element_type=jnp.float32,
+                    )
+                    prods.append((pl.multiple_of(row * tile, tile), prod))
+                for row, prod in prods:
+                    acc_ref[pl.ds(row, tile), :] += prod
+            at += members
     out_ref[...] = acc_ref[:rows, :].astype(out_ref.dtype)
 
 
-def tile_product(named, sets, dtype, before=None):
+def tile_product(named, sets, dtype, before=None, after=()):
     kinds = [kind for kind, _ in named]
     panels = [panel for _, panel in named]
     metas = [meta for members in sets for meta, _ in members]
@@ -203,12 +211,13 @@
     count = len(kinds) * len(sets) * slots
     summed = before is not None
     return pl.pallas_call(
-        functools.partial(tile_kernel, kinds, [[0] * len(m) for m in sets], summed),
+        functools.partial(tile_kernel, kinds, [len(m) for m in sets], summed, len(after)),
         out_shape=jax.ShapeDtypeStruct((rows, width), dtype),
         in_specs=[smem] * len(metas)
         + [hbm] * len(tiles)
         + [anywhere] * len(panels)
-        + [vmem] * summed,
+        + [vmem] * summed
+        + [anywhere] * len(after),
         out_specs=vmem,
         scratch_shapes=[
             pltpu.VMEM((rows + tile, width), jnp.float32),
@@ -224,7 +233,7 @@
             transcendentals=0,
         ),
         name="tile_product",
-    )(*metas, *tiles, *panels, *([before] if summed else []))
+    )(*metas, *tiles, *panels, *([before] if summed else []), *after)
 
 
 def middle_kernel(near_ref, far_ref, w_ref, cot_ref, cot_swap_ref, act_ref, adj_ref):
@@ -290,50 +299,58 @@
     )(near, far, adj, after)
 
 
-def add_kernel(first_ref, second_ref, after_ref, out_ref):
-    out_ref[...] = first_ref[...] + second_ref[...]
-
-
-def add_after(first, second, after):
+def add_kernel(count, *refs):
+    total = refs[0][...].astype(jnp.float32) + refs[1][...].astype(jnp.float32)
+    if count == 4:
+        total = total + (refs[2][...] + refs[3][...])
+    refs[-1][...] = total.astype(refs[-1].dtype)
+
+
+def add_after(values, *after):
     vmem = pl.BlockSpec(memory_space=pltpu.VMEM)
     return pl.pallas_call(
-        add_kernel,
-        out_shape=jax.ShapeDtypeStruct(first.shape, first.dtype),
-        in_specs=[vmem, vmem, pl.BlockSpec(memory_space=pl.ANY)],
+        functools.partial(add_kernel, len(values)),
+        out_shape=jax.ShapeDtypeStruct(values[0].shape, values[0].dtype),
+        in_specs=[vmem] * len(values) + [pl.BlockSpec(memory_space=pl.ANY)] * len(after),
         out_specs=vmem,
-        compiler_params=pltpu.CompilerParams(vmem_limit_bytes=1024 * 1024),
+        compiler_params=pltpu.CompilerParams(vmem_limit_bytes=4 * 1024 * 1024),
         name="add_after",
-    )(first, second, after)
-
-
-def final_kernel(self_ref, one_ref, two_ref, w_ref, out_ref):
+    )(*values, *after)
+
+
+def final_kernel(own_ref, one_ref, two_ref, w_ref, grad_ref, rest_ref, out_ref, grad_out_ref):
     j, _, p = place()
-    half = self_ref.shape[1]
-    near = jnp.where(j == p, self_ref[...], one_ref[...])
+    half = own_ref.shape[1]
+    near_cols = pl.ds(pl.multiple_of(j * half, half), half)
+    far_cols = pl.ds(pl.multiple_of((1 - j) * half, half), half)
+    grad_out_ref[:, near_cols] = grad_ref[...]
+    grad_out_ref[:, far_cols] = rest_ref[...]
+    near = jnp.where(j == p, own_ref[...], one_ref[...])
     far = jnp.where(j == p, one_ref[...], two_ref[...])
-    w_near = w_ref[:, pl.ds(pl.multiple_of(j * half, half), half)]
-    w_far = w_ref[:, pl.ds(pl.multiple_of((1 - j) * half, half), half)]
     dims = (((1,), (1,)), ((), ()))
-    total = lax.dot_general(near, w_near, dims, preferred_element_type=jnp.float32)
-    total += lax.dot_general(far, w_far, dims, preferred_element_type=jnp.float32)
+    total = lax.dot_general(near, w_ref[:, near_cols], dims, preferred_element_type=jnp.float32)
+    total += lax.dot_general(far, w_ref[:, far_cols], dims, preferred_element_type=jnp.float32)
     out_ref[...] = total.astype(out_ref.dtype)
 
 
-def final(own, one, two, weight):
+def final(own, one, two, weight, grad, rest):
     vmem = pl.BlockSpec(memory_space=pltpu.VMEM)
     rows = own.shape[0]
     wide = weight.shape[0]
     return pl.pallas_call(
         final_kernel,
-        out_shape=jax.ShapeDtypeStruct((rows, wide), jnp.bfloat16),
-        in_specs=[vmem] * 4,
-        out_specs=vmem,
+        out_shape=(
+            jax.ShapeDtypeStruct((rows, wide), jnp.bfloat16),
+            jax.ShapeDtypeStruct(weight.shape, jnp.float32),
+        ),
+        in_specs=[vmem] * 6,
+        out_specs=(vmem, vmem),
         compiler_params=pltpu.CompilerParams(vmem_limit_bytes=8 * 1024 * 1024),
         cost_estimate=pl.CostEstimate(
             flops=2 * rows * wide * wide, bytes_accessed=8 * rows * wide, transcendentals=0
         ),
         name="final",
-    )(own, one, two, weight)
+    )(own, one, two, weight, grad, rest)
 
 
 def per_device(node_feats, weight, cotangent, tile_values, tile_coords, tile_counts):
@@ -359,31 +376,41 @@
     def to_home(c, j, z):
         return (c, 1 - j, z) if j == z % 2 else (c, j, z ^ 1)
 
-    def forward_x(c, j, z):
-        return (c + 1, j, z) if j == z % 2 or z % 2 == 0 else (c - 1, j, z)
-
-    def forward_x_cross(c, j, z):
-        to = forward_x(c, j, z)
-        return (to[0], 1 - j, to[2])
+    def to_direct(c, j, z):
+        return (c ^ 1, j, z)
+
+    def to_second(c, j, z):
+        return (c ^ 2, j, z) if shape[0] == 4 else (c + 1 if c % 2 else c - 1, j, z)
+
+    def hand_on(value, direct):
+        return send(direct if shape[0] == 4 else value, to_second)
 
     first = send(own, to_home)
     mine, yours = halves(node_feats)
-    one = send(mine, forward_x)
-    two = send(yours, forward_x_cross)
-    swapped = send(yours, sibling)
-    right = send(pick(mine, swapped), lambda c, j, z: (c - 1, j, z))
-    coords, counts, swapped = lax.optimization_barrier((tile_coords, tile_counts, swapped))
+    feats, feats_other = pick(mine, send(yours, sibling))
+    direct = send(feats, to_direct)
+    coords, counts, feats_later, direct = lax.optimization_barrier(
+        (tile_coords, tile_counts, feats_other, direct)
+    )
+    second = hand_on(feats, direct)
+    far = send(feats_later, lambda c, j, z: (c - 1 if z % 2 else c + 1, j, z))
     meta = slot_blocks(coords[:, 0], counts[0], blocks)
     meta_b = send(meta, to_home)
     meta_far = send(meta, lambda c, j, z: None if j == z % 2 else (c, 1 - j, z ^ 1))
-    first, one, two, right, meta_b, meta_far = lax.optimization_barrier(
-        (first, one, two, right, meta_b, meta_far)
-    )
-    second = send(first, lambda c, j, z: (c, 1 - j, z) if j == z % 2 else None)
+    first, second, far, meta_b, meta_far = lax.optimization_barrier(
+        (first, second, far, meta_b, meta_far)
+    )
+    other_first = send(first, lambda c, j, z: (c, 1 - j, z) if j == z % 2 else None)
 
     set_first = [(meta_b, first)]
-    set_rest = [(meta, own), (meta_far, second)]
-    panels = [("mine", mine), ("swapped", swapped), ("one", one), ("two", two), ("right", right)]
+    set_rest = [(meta, own), (meta_far, other_first)]
+    panels = [
+        ("self", feats),
+        ("near", feats_other),
+        ("direct", direct),
+        ("second", second),
+        ("far", far),
+    ]
     part = tile_product(panels, [set_first], jnp.float32)
     part = tile_product(panels, [set_rest], jnp.bfloat16, part)
 
@@ -396,19 +423,26 @@
     cot, cot_yours = halves(cotangent)
     act, adj = middle(near, far, weight, cot, send(cot_yours, sibling))
 
-    left = send(adj, lambda c, j, z: (c + 1, j, z))
-    right = send(adj, lambda c, j, z: (c - 1, j, z))
-    third = send(adj, lambda c, j, z: (c + 1 if z % 2 else c - 1, j, z ^ 1))
     other = send(adj, lambda c, j, z: (c, j, z ^ 1))
-    back_part = tile_product([("self", adj), ("near", other)], [set_first, set_rest], jnp.float32)
-    far_panels = [("left", left), ("right", right), ("far", third)]
-    back_part = tile_product(far_panels, [set_first, set_rest], jnp.bfloat16, back_part)
+    direct = send(adj, to_direct)
+    adj_later, direct = lax.optimization_barrier((adj, direct))
+    second = hand_on(adj, direct)
+    third = send(adj_later, lambda c, j, z: (c + 1 if z % 2 else c - 1, j, z ^ 1))
+    grad = grad_block(scale, near, far, adj, other)
+    grad_got = send(grad, lambda c, j, z: (c, j, z ^ 1))
+    panels = [("self", adj), ("near", other)]
+    back_part = tile_product(panels, [set_first, set_rest], jnp.float32)
+    panels = [("direct", direct), ("second", second), ("far", third)]
+    back_part = tile_product(
+        panels, [set_first, set_rest], jnp.bfloat16, back_part, [grad_got]
+    )
 
     def deliver(value):
         one = send(value, lambda c, j, z: (c, j, z ^ 1) if j == z % 2 else (c, 1 - j, z))
         two = send(value, lambda c, j, z: None if j == z % 2 else (c, 1 - j, z ^ 1))
         return one, two
 
+    act, back_part = lax.optimization_barrier((act, back_part))
     act_one, act_two = deliver(act)
     act_near = jnp.where(home, act, act_one)
     act_far = jnp.where(home, act_one, act_two)
@@ -418,22 +452,16 @@
 
     back = join(back_part)
     back_one, back_two = deliver(back)
-    input_grad = final(back, back_one, back_two, weight)
-
-    grad = grad_block(scale, near, far, adj, other)
-    grad = add_after(grad, send(grad, lambda c, j, z: (c, j, z ^ 1)), back_part)
+
+    grad = add_after([grad, grad_got], back_part)
     step = 1
     while step < shape[0]:
         flips = [step] if step * 2 >= shape[0] else [step, 2 * step, 3 * step]
         got = [send(grad, lambda c, j, z, s=s: (c ^ s, j, z)) for s in flips]
-        grad = grad + got[0]
-        if len(got) == 3:
-            grad = grad + (got[1] + got[2])
+        grad = add_after([grad, *got], back)
         step *= 2 if len(flips) == 1 else 4
-    rest = send(grad, sibling)
-    weight_grad = jnp.concatenate(
-        [jnp.where(j == 0, grad, rest), jnp.where(j == 0, rest, grad)], axis=1
-    )
+    grad_rest = send(grad, sibling)
+    input_grad, weight_grad = final(back, back_one, back_two, weight, grad, grad_rest)
     return (activated, input_grad, weight_grad)
 
 

time: 95.6 us -> 97 us (1.015)
  waiting for transfers between devices: 38.3 us -> 47.3 us
  starting transfers between devices: 37.3 us -> 33.1 us
  other arithmetic: 2.85 us -> 1.04 us
    ppermute x25, waiting for transfers between devices: 38.3 us -> 47.3 us  [send(): return lax.ppermute(value, AXES, route(shape, move))]
    ppermute x25, starting transfers between devices: 37.3 us -> 33.1 us  [send(): return lax.ppermute(value, AXES, route(shape, move))]
    unnamed x20 -> x10, local copies, waits for them, and re-layouts: 3.09 us -> 1.71 us
    select_n x1, other arithmetic: 1.08 us -> 0.05 us  [per_device(): jnp.where(j == 0, act_near, act_far)]
    pallas_call x7 -> x8, Pallas kernels: 9.95 us -> 9.72 us  [the longest x4 8.35 us: tile_product(): pl.pallas_call(functools.partial(tile_kernel, kinds, [len(m) for m in set...]
  transfers between devices with their start and end apart: 25 -> 25, of which waited for: 13 -> 13; matrix products, arithmetic and copies ran while one was open for 3% -> 2% of each run, Pallas kernels for 9% -> 6%
where the time goes in v5:
time: 97 us; the launch traced here: 96.7 us
  waiting for transfers between devices  47.3 us (49%)
  starting transfers between devices  33.1 us (34%)
  Pallas kernels  12 us (12%)
  local copies, waits for them, and re-layouts  2.41 us (2%)
  other arithmetic  1.04 us (1%)
    ppermute x25, waiting for transfers between devices, send(): return lax.ppermute(value, AXES, route(shape, move))  47.3 us
    ppermute x25, starting transfers between devices, send(): return lax.ppermute(value, AXES, route(shape, move))  33.1 us
    pallas_call x4, Pallas kernels, tile_product(): pl.pallas_call(functools.partial(tile_kernel, kinds, [len(m) for m in set...  8.35 us
  transfers between devices with their start and end apart: 25, of which 13 were waited for; matrix products, arithmetic and copies ran while one was open for 2% of the time, Pallas kernels for 6%

profile of v5, /device:TPU:1, one launch (start us, length us, event | category | flops | bytes accessed | tf_op | source)
XLA Modules:
  0.0 96.7 jit_solution(3463822899595739453)
XLA Ops:
  0.6 2.2 %collective-permute-start.2 = (bf16[5,8,128,128]{3,2,1,0:T(8,128)(2,1)}, bf16[5,8,128,128]{3,2,1,0:T(8,128)(2,1)S(1)}, u32[]{:S(2)}, u32[]{:S(2)}) collective-permute-start(bf16[5,8,128,128]{3,2,1,0:T(8,128)(2,1)} %bitcast.5), channel_id=1, source_target_pairs={{0,4},{1,0},{2,6},{3,2},{4,5},{5,1},{6,7},{7,3},{8,12},{9,8},{10,1... | collective-permute-start | bytes 3932168 | tf_op jit(solution)/shard_map/ppermute | solution.py:365
  2.8 1.0 %copy-done.2 = bf16[1024,256]{1,0:T(8,128)(2,1)S(1)} copy-done((bf16[1024,256]{1,0:T(8,128)(2,1)S(1)}, bf16[1024,256]{1,0:T(8,128)(2,1)}, u32[]{:S(2)}) %copy-start.2) | copy-done | bytes 524312
  3.9 0.1 halves.2
  4.1 1.5 %collective-permute-done.swapped_ref = bf16[1024,128]{1,0:T(8,128)(2,1)S(1)} collective-permute-done((bf16[1024,128]{1,0:T(8,128)(2,1)S(1)}, bf16[1024,128]{1,0:T(8,128)(2,1)S(1)}, u32[]{:S(2)}, u32[]{:S(2)}) %collective-permute-start) | collective-permute-done | bytes 262176 | tf_op jit(solution)/shard_map/ppermute | solution.py:365
  5.6 1.3 %collective-permute-start.1 = (bf16[1024,128]{1,0:T(8,128)(2,1)S(1)}, bf16[1024,128]{1,0:T(8,128)(2,1)S(1)}, u32[]{:S(2)}, u32[]{:S(2)}) collective-permute-start(bf16[1024,128]{1,0:T(8,128)(2,1)S(1)} %get-tuple-element.29.refs_2_.refs_4_), channel_id=1, source_target_pairs={{0,8},{1,9},{2,10},{3,11},{4,12},{5,13},{6,14},{7,15},{8,0},{9,1},... | collective-permute-start | bytes 786440 | tf_op jit(solution)/shard_map/ppermute | solution.py:365
  6.9 6.6 %collective-permute-done.1.refs_4_.refs_6_ = bf16[1024,128]{1,0:T(8,128)(2,1)S(1)} collective-permute-done((bf16[1024,128]{1,0:T(8,128)(2,1)S(1)}, bf16[1024,128]{1,0:T(8,128)(2,1)S(1)}, u32[]{:S(2)}, u32[]{:S(2)}) %collective-permute-start.1) | collective-permute-done | bytes 262176 | tf_op jit(solution)/shard_map/ppermute | solution.py:365
  13.5 1.2 %collective-permute-start.3 = (bf16[1024,128]{1,0:T(8,128)(2,1)S(1)}, bf16[1024,128]{1,0:T(8,128)(2,1)S(1)}, u32[]{:S(2)}, u32[]{:S(2)}) collective-permute-start(bf16[1024,128]{1,0:T(8,128)(2,1)S(1)} %collective-permute-done.1.refs_4_.refs_6_), channel_id=1, source_target_pairs={{0,16},{1,17},{2,18},{3,19},{4,20},{5,21},{6,22},{7,23},{8,24},{9,... | collective-permute-start | bytes 786440 | tf_op jit(solution)/shard_map/ppermute | solution.py:365
  14.7 1.2 %collective-permute-start.4 = (bf16[1024,128]{1,0:T(8,128)(2,1)S(1)}, bf16[1024,128]{1,0:T(8,128)(2,1)S(1)}, u32[]{:S(2)}, u32[]{:S(2)}) collective-permute-start(bf16[1024,128]{1,0:T(8,128)(2,1)S(1)} %get-tuple-element.33.refs_3_.refs_5_), channel_id=1, source_target_pairs={{0,8},{1,25},{2,10},{3,27},{4,12},{5,29},{6,14},{7,31},{8,16},{9,1... | collective-permute-start | bytes 786440 | tf_op jit(solution)/shard_map/ppermute | solution.py:365
  15.9 0.7 copy.12
  16.6 0.7 copy-done.4
  17.3 1.3 %slot_blocks.1.refs_0_.refs_1_ = s32[2,40]{1,0:T(2,128)S(1)} custom-call(s32[2,5,8]{2,1,0:T(8,128)S(1)} %copy.10.coords_ref, s32[5]{0:T(128)S(1)} %bitcast.9), custom_call_target="tpu_custom_call" | custom-call | tf_op jit(solution)/shard_map/slot_blocks/pallas_call | solution.py:111
  18.6 0.7 collective-permute-start.5
  19.4 4.4 %collective-permute-start.6 = (s32[2,40]{1,0:T(2,128)S(1)}, s32[2,40]{1,0:T(2,128)S(1)}, u32[]{:S(2)}, u32[]{:S(2)}) collective-permute-start(s32[2,40]{1,0:T(2,128)S(1)} %slot_blocks.1.refs_0_.refs_1_), channel_id=1, source_target_pairs={{1,4},{3,6},{4,1},{6,3},{9,12},{11,14},{12,9},{14,11},{17,20},{19,... | collective-permute-start | bytes 968 | tf_op jit(solution)/shard_map/ppermute | solution.py:365
  23.8 1.5 %collective-permute-done.6.refs_1_.refs_2_ = s32[2,40]{1,0:T(2,128)S(1)} collective-permute-done((s32[2,40]{1,0:T(2,128)S(1)}, s32[2,40]{1,0:T(2,128)S(1)}, u32[]{:S(2)}, u32[]{:S(2)}) %collective-permute-start.6) | collective-permute-done | bytes 352 | tf_op jit(solution)/shard_map/ppermute | solution.py:365
  25.3 0.7 collective-permute-done.3.refs_5_.refs_7_
  26.0 1.3 %collective-permute-start.7 = (bf16[5,8,128,128]{3,2,1,0:T(8,128)(2,1)S(1)}, bf16[5,8,128,128]{3,2,1,0:T(8,128)(2,1)S(1)}, u32[]{:S(2)}, u32[]{:S(2)}) collective-permute-start(bf16[5,8,128,128]{3,2,1,0:T(8,128)(2,1)S(1)} %collective-permute-done.2.refs_1_.refs_3_), channel_id=1, source_target_pairs={{0,4},{2,6},{5,1},{7,3},{8,12},{10,14},{13,9},{15,11},{16,20},{18,... | collective-permute-start | bytes 3932168 | tf_op jit(solution)/shard_map/ppermute | solution.py:365
  27.2 2.1 %tile_product.4.refs_9_ = f32[1024,128]{1,0:T(8,128)S(1)} custom-call(s32[2,40]{1,0:T(2,128)S(1)} %collective-permute-done.5.refs_0_, bf16[5,8,128,128]{3,2,1,0:T(8,128)(2,1)S(1)} %collective-permute-done.2.refs_1_.refs_3_, bf16[1024,128]{1,0:T(8,128)(2,1)S(1)} %get-tuple-element.29.refs_2_.refs_4_, bf16[1024,128]{1,0:T(8,128)(2,1)S(1)} %get-tuple-element.33.refs_3_.refs_5_, ...), custom_call_target="tpu_custom_call" | custom-call | flops 167772160 | bytes 2621440 | tf_op jit(solution)/shard_map/tile_product/pallas_call | solution.py:213
  29.4 2.2 %collective-permute-done.7.refs_3_.refs_5_ = bf16[5,8,128,128]{3,2,1,0:T(8,128)(2,1)S(1)} collective-permute-done((bf16[5,8,128,128]{3,2,1,0:T(8,128)(2,1)S(1)}, bf16[5,8,128,128]{3,2,1,0:T(8,128)(2,1)S(1)}, u32[]{:S(2)}, u32[]{:S(2)}) %collective-permute-start.7) | collective-permute-done | bytes 1310752 | tf_op jit(solution)/shard_map/ppermute | solution.py:365
  31.6 2.1 %tile_product.5 = bf16[1024,128]{1,0:T(8,128)(2,1)S(1)} custom-call(s32[2,40]{1,0:T(2,128)S(1)} %slot_blocks.1.refs_0_.refs_1_, s32[2,40]{1,0:T(2,128)S(1)} %collective-permute-done.6.refs_1_.refs_2_, bf16[5,8,128,128]{3,2,1,0:T(8,128)(2,1)S(1)} %bitcast.6, bf16[5,8,128,128]{3,2,1,0:T(8,128)(2,1)S(1)} %collective-permute-done.7.refs_3_.refs_5_, ...), custom_call_target="tpu_custom_call" | custom-call | flops 167772160 | bytes 2621440 | tf_op jit(solution)/shard_map/tile_product/pallas_call | solution.py:213
  33.8 2.4 %collective-permute-start.8 = (bf16[1024,128]{1,0:T(8,128)(2,1)S(1)}, bf16[1024,128]{1,0:T(8,128)(2,1)S(1)}, u32[]{:S(2)}, u32[]{:S(2)}) collective-permute-start(bf16[1024,128]{1,0:T(8,128)(2,1)S(1)} %tile_product.5), channel_id=1, source_target_pairs={{0,2},{1,3},{2,0},{3,1},{4,6},{5,7},{6,4},{7,5},{8,10},{9,11},{10,... | collective-permute-start | bytes 786440 | tf_op jit(solution)/shard_map/ppermute | solution.py:365
  36.1 0.1 halves.3
  36.3 0.5 collective-permute-start.10
  36.8 11.4 %collective-permute-done.8 = bf16[1024,128]{1,0:T(8,128)(2,1)S(1)} collective-permute-done((bf16[1024,128]{1,0:T(8,128)(2,1)S(1)}, bf16[1024,128]{1,0:T(8,128)(2,1)S(1)}, u32[]{:S(2)}, u32[]{:S(2)}) %collective-permute-start.8) | collective-permute-done | bytes 262176 | tf_op jit(solution)/shard_map/ppermute | solution.py:365
  48.1 0.1 add_convert_fusion.1.near_ref
  48.2 0.5 collective-permute-start.9
  48.7 1.2 %collective-permute-done.9.far_ref = bf16[1024,128]{1,0:T(8,128)(2,1)S(1)} collective-permute-done((bf16[1024,128]{1,0:T(8,128)(2,1)S(1)}, bf16[1024,128]{1,0:T(8,128)(2,1)S(1)}, u32[]{:S(2)}, u32[]{:S(2)}) %collective-permute-start.9) | collective-permute-done | bytes 262176 | tf_op jit(solution)/shard_map/ppermute | solution.py:365
  49.9 0.4 middle.1
  50.4 7.4 %collective-permute-done.11.refs_6_ = bf16[1024,128]{1,0:T(8,128)(2,1)S(1)} collective-permute-done((bf16[1024,128]{1,0:T(8,128)(2,1)S(1)}, bf16[1024,128]{1,0:T(8,128)(2,1)S(1)}, u32[]{:S(2)}, u32[]{:S(2)}) %collective-permute-start.11) | collective-permute-done | bytes 262176 | tf_op jit(solution)/shard_map/ppermute | solution.py:365
  57.9 0.5 collective-permute-start.12
  58.4 0.3 grad_block.1.refs_0_
  58.7 1.6 %collective-permute-start.15 = (f32[256,128]{1,0:T(8,128)S(1)}, f32[256,128]{1,0:T(8,128)S(1)}, u32[]{:S(2)}, u32[]{:S(2)}) collective-permute-start(f32[256,128]{1,0:T(8,128)S(1)} %grad_block.1.refs_0_), channel_id=1, source_target_pairs={{0,1},{1,0},{2,3},{3,2},{4,5},{5,4},{6,7},{7,6},{8,9},{9,8},{10,11... | collective-permute-start | bytes 393224 | tf_op jit(solution)/shard_map/ppermute | solution.py:365
  60.3 1.8 %tile_product.6.refs_9_ = f32[1024,128]{1,0:T(8,128)S(1)} custom-call(s32[2,40]{1,0:T(2,128)S(1)} %collective-permute-done.5.refs_0_, s32[2,40]{1,0:T(2,128)S(1)} %slot_blocks.1.refs_0_.refs_1_, s32[2,40]{1,0:T(2,128)S(1)} %collective-permute-done.6.refs_1_.refs_2_, bf16[5,8,128,128]{3,2,1,0:T(8,128)(2,1)S(1)} %collective-permute-done.2.refs_1_.refs_3_, ...), custom_call_target="tpu_custom_call" | custom-call | flops 134217728 | bytes 1572864 | tf_op jit(solution)/shard_map/tile_product/pallas_call | solution.py:213
  62.1 5.8 %collective-permute-done.15.refs_10_.refs_1_ = f32[256,128]{1,0:T(8,128)S(1)} collective-permute-done((f32[256,128]{1,0:T(8,128)S(1)}, f32[256,128]{1,0:T(8,128)S(1)}, u32[]{:S(2)}, u32[]{:S(2)}) %collective-permute-start.15) | collective-permute-done | bytes 131104 | tf_op jit(solution)/shard_map/ppermute | solution.py:365
  67.9 2.2 %collective-permute-done.12.refs_7_ = bf16[1024,128]{1,0:T(8,128)(2,1)S(1)} collective-permute-done((bf16[1024,128]{1,0:T(8,128)(2,1)S(1)}, bf16[1024,128]{1,0:T(8,128)(2,1)S(1)}, u32[]{:S(2)}, u32[]{:S(2)}) %collective-permute-start.12) | collective-permute-done | bytes 262176 | tf_op jit(solution)/shard_map/ppermute | solution.py:365
  70.1 2.3 %tile_product.7.refs_2_ = bf16[1024,128]{1,0:T(8,128)(2,1)S(1)} custom-call(s32[2,40]{1,0:T(2,128)S(1)} %collective-permute-done.5.refs_0_, s32[2,40]{1,0:T(2,128)S(1)} %slot_blocks.1.refs_0_.refs_1_, s32[2,40]{1,0:T(2,128)S(1)} %collective-permute-done.6.refs_1_.refs_2_, bf16[5,8,128,128]{3,2,1,0:T(8,128)(2,1)S(1)} %collective-permute-done.2.refs_1_.refs_3_, ...), custom_call_target="tpu_custom_call" | custom-call | flops 201326592 | bytes 2359296 | tf_op jit(solution)/shard_map/tile_product/pallas_call | solution.py:213
  72.5 2.2 %collective-permute-start.16 = (bf16[1024,128]{1,0:T(8,128)(2,1)S(1)}, bf16[1024,128]{1,0:T(8,128)(2,1)S(1)}, u32[]{:S(2)}, u32[]{:S(2)}) collective-permute-start(bf16[1024,128]{1,0:T(8,128)(2,1)S(1)} %get-tuple-element.45), channel_id=1, source_target_pairs={{0,1},{1,5},{2,3},{3,7},{4,0},{5,4},{6,2},{7,6},{8,9},{9,13},{10,1... | collective-permute-start | bytes 786440 | tf_op jit(solution)/shard_map/ppermute | solution.py:365
  74.7 2.8 %collective-permute-start.17 = (bf16[1024,128]{1,0:T(8,128)(2,1)S(1)}, bf16[1024,128]{1,0:T(8,128)(2,1)S(1)}, u32[]{:S(2)}, u32[]{:S(2)}) collective-permute-start(bf16[1024,128]{1,0:T(8,128)(2,1)S(1)} %get-tuple-element.45), channel_id=1, source_target_pairs={{1,4},{3,6},{4,1},{6,3},{9,12},{11,14},{12,9},{14,11},{17,20},{19,... | collective-permute-start | bytes 786440 | tf_op jit(solution)/shard_map/ppermute | solution.py:365
  77.6 2.0 %collective-permute-start.21 = (f32[256,128]{1,0:T(8,128)S(1)}, f32[256,128]{1,0:T(8,128)S(1)}, u32[]{:S(2)}, u32[]{:S(2)}) collective-permute-start(f32[256,128]{1,0:T(8,128)S(1)} %add_after.2.refs_0_), channel_id=1, source_target_pairs={{0,8},{1,9},{2,10},{3,11},{4,12},{5,13},{6,14},{7,15},{8,0},{9,1},... | collective-permute-start | bytes 393224 | tf_op jit(solution)/shard_map/ppermute | solution.py:365
  79.5 1.0 %collective-permute-start.22 = (f32[256,128]{1,0:T(8,128)S(1)}, f32[256,128]{1,0:T(8,128)S(1)}, u32[]{:S(2)}, u32[]{:S(2)}) collective-permute-start(f32[256,128]{1,0:T(8,128)S(1)} %add_after.2.refs_0_), channel_id=1, source_target_pairs={{0,16},{1,17},{2,18},{3,19},{4,20},{5,21},{6,22},{7,23},{8,24},{9,... | collective-permute-start | bytes 393224 | tf_op jit(solution)/shard_map/ppermute | solution.py:365
  80.5 4.1 %collective-permute-done.18 = bf16[1024,128]{1,0:T(8,128)(2,1)S(1)} collective-permute-done((bf16[1024,128]{1,0:T(8,128)(2,1)S(1)}, bf16[1024,128]{1,0:T(8,128)(2,1)S(1)}, u32[]{:S(2)}, u32[]{:S(2)}) %collective-permute-start.18) | collective-permute-done | bytes 262176 | tf_op jit(solution)/shard_map/ppermute | solution.py:365
  84.6 0.8 collective-permute-start.23
  85.5 2.3 %collective-permute-start.19 = (bf16[1024,128]{1,0:T(8,128)(2,1)S(1)}, bf16[1024,128]{1,0:T(8,128)(2,1)S(1)}, u32[]{:S(2)}, u32[]{:S(2)}) collective-permute-start(bf16[1024,128]{1,0:T(8,128)(2,1)S(1)} %add_convert_fusion.refs_4_.own_ref), channel_id=1, source_target_pairs={{0,1},{1,5},{2,3},{3,7},{4,0},{5,4},{6,2},{7,6},{8,9},{9,13},{10,1... | collective-permute-start | bytes 786440 | tf_op jit(solution)/shard_map/ppermute | solution.py:365
  87.8 1.9 %collective-permute-start.20 = (bf16[1024,128]{1,0:T(8,128)(2,1)S(1)}, bf16[1024,128]{1,0:T(8,128)(2,1)S(1)}, u32[]{:S(2)}, u32[]{:S(2)}) collective-permute-start(bf16[1024,128]{1,0:T(8,128)(2,1)S(1)} %add_convert_fusion.refs_4_.own_ref), channel_id=1, source_target_pairs={{1,4},{3,6},{4,1},{6,3},{9,12},{11,14},{12,9},{14,11},{17,20},{19,... | collective-permute-start | bytes 786440 | tf_op jit(solution)/shard_map/ppermute | solution.py:365
  89.7 2.1 %collective-permute-start.24 = (f32[256,128]{1,0:T(8,128)S(1)}, f32[256,128]{1,0:T(8,128)S(1)}, u32[]{:S(2)}, u32[]{:S(2)}) collective-permute-start(f32[256,128]{1,0:T(8,128)S(1)} %add_after.3.grad_ref), channel_id=1, source_target_pairs={{0,4},{1,5},{2,6},{3,7},{4,0},{5,1},{6,2},{7,3},{8,12},{9,13},{10,... | collective-permute-start | bytes 393224 | tf_op jit(solution)/shard_map/ppermute | solution.py:365
  91.9 0.9 pad_maximum_fusion
  92.7 0.1 collective-permute-done.24.rest_ref
  92.8 2.7 %collective-permute-done.20.two_ref = bf16[1024,128]{1,0:T(8,128)(2,1)S(1)} collective-permute-done((bf16[1024,128]{1,0:T(8,128)(2,1)S(1)}, bf16[1024,128]{1,0:T(8,128)(2,1)S(1)}, u32[]{:S(2)}, u32[]{:S(2)}) %collective-permute-start.20) | collective-permute-done | bytes 262176 | tf_op jit(solution)/shard_map/ppermute | solution.py:365
  95.5 1.3 %final.1 = (bf16[1024,256]{1,0:T(8,128)(2,1)}, f32[256,256]{1,0:T(8,128)}) custom-call(bf16[1024,128]{1,0:T(8,128)(2,1)S(1)} %add_convert_fusion.refs_4_.own_ref, bf16[1024,128]{1,0:T(8,128)(2,1)S(1)} %collective-permute-done.19.one_ref, bf16[1024,128]{1,0:T(8,128)(2,1)S(1)} %collective-permute-done.20.two_ref, bf16[256,256]{1,0:T(8,128)(2,1)S(1)} %copy-done.1, ...), custom_call_target="tpu_custom_call" | custom-call | flops 134217728 | bytes 2097152 | tf_op jit(solution)/shard_map/final/pallas_call | solution.py:340
  (31 shorter events, 0.6 us)
Async XLA Ops:
  0.6 25.3 %collective-permute-start.2 = (bf16[5,8,128,128]{3,2,1,0:T(8,128)(2,1)}, bf16[5,8,128,128]{3,2,1,0:T(8,128)(2,1)S(1)}, u32[]{:S(2)}, u32[]{:S(2)}) collective-permute-start(bf16[5,8,128,128]{3,2,1,0:T(8,128)(2,1)} %bitcast.5), channel_id=1, source_target_pairs={{0,4},{1,0},{2,6},{3,2},{4,5},{5,1},{6,7},{7,3},{8,12},{9,8},{10,1... | collective-permute-start | bytes 3932168 | tf_op jit(solution)/shard_map/ppermute | solution.py:365
  2.8 1.0 %copy-start.2 = (bf16[1024,256]{1,0:T(8,128)(2,1)S(1)}, bf16[1024,256]{1,0:T(8,128)(2,1)}, u32[]{:S(2)}) copy-start(bf16[1024,256]{1,0:T(8,128)(2,1)} %x_ref.2) | copy-start | bytes 1572868
  4.0 1.6 %collective-permute-start = (bf16[1024,128]{1,0:T(8,128)(2,1)S(1)}, bf16[1024,128]{1,0:T(8,128)(2,1)S(1)}, u32[]{:S(2)}, u32[]{:S(2)}) collective-permute-start(bf16[1024,128]{1,0:T(8,128)(2,1)S(1)} %get-tuple-element.27), channel_id=1, source_target_pairs={{0,4},{1,5},{2,6},{3,7},{4,0},{5,1},{6,2},{7,3},{8,12},{9,13},{10,... | collective-permute-start | bytes 786440 | tf_op jit(solution)/shard_map/ppermute | solution.py:365
  5.6 7.8 %collective-permute-start.1 = (bf16[1024,128]{1,0:T(8,128)(2,1)S(1)}, bf16[1024,128]{1,0:T(8,128)(2,1)S(1)}, u32[]{:S(2)}, u32[]{:S(2)}) collective-permute-start(bf16[1024,128]{1,0:T(8,128)(2,1)S(1)} %get-tuple-element.29.refs_2_.refs_4_), channel_id=1, source_target_pairs={{0,8},{1,9},{2,10},{3,11},{4,12},{5,13},{6,14},{7,15},{8,0},{9,1},... | collective-permute-start | bytes 786440 | tf_op jit(solution)/shard_map/ppermute | solution.py:365
  13.5 12.5 %collective-permute-start.3 = (bf16[1024,128]{1,0:T(8,128)(2,1)S(1)}, bf16[1024,128]{1,0:T(8,128)(2,1)S(1)}, u32[]{:S(2)}, u32[]{:S(2)}) collective-permute-start(bf16[1024,128]{1,0:T(8,128)(2,1)S(1)} %collective-permute-done.1.refs_4_.refs_6_), channel_id=1, source_target_pairs={{0,16},{1,17},{2,18},{3,19},{4,20},{5,21},{6,22},{7,23},{8,24},{9,... | collective-permute-start | bytes 786440 | tf_op jit(solution)/shard_map/ppermute | solution.py:365
  14.7 11.2 %collective-permute-start.4 = (bf16[1024,128]{1,0:T(8,128)(2,1)S(1)}, bf16[1024,128]{1,0:T(8,128)(2,1)S(1)}, u32[]{:S(2)}, u32[]{:S(2)}) collective-permute-start(bf16[1024,128]{1,0:T(8,128)(2,1)S(1)} %get-tuple-element.33.refs_3_.refs_5_), channel_id=1, source_target_pairs={{0,8},{1,25},{2,10},{3,27},{4,12},{5,29},{6,14},{7,31},{8,16},{9,1... | collective-permute-start | bytes 786440 | tf_op jit(solution)/shard_map/ppermute | solution.py:365
  16.6 0.7 copy-start.4
  18.6 13.0 %copy-start = (bf16[1,5,8,128,128]{4,3,2,1,0:T(8,128)(2,1)S(1)}, bf16[1,5,8,128,128]{4,3,2,1,0:T(8,128)(2,1)}, u32[]{:S(2)}) copy-start(bf16[1,5,8,128,128]{4,3,2,1,0:T(8,128)(2,1)} %param.9) | copy-start | bytes 3932164
  18.6 5.1 %collective-permute-start.5 = (s32[2,40]{1,0:T(2,128)S(1)}, s32[2,40]{1,0:T(2,128)S(1)}, u32[]{:S(2)}, u32[]{:S(2)}) collective-permute-start(s32[2,40]{1,0:T(2,128)S(1)} %slot_blocks.1.refs_0_.refs_1_), channel_id=1, source_target_pairs={{0,4},{1,0},{2,6},{3,2},{4,5},{5,1},{6,7},{7,3},{8,12},{9,8},{10,1... | collective-permute-start | bytes 968 | tf_op jit(solution)/shard_map/ppermute | solution.py:365
  19.4 5.9 %collective-permute-start.6 = (s32[2,40]{1,0:T(2,128)S(1)}, s32[2,40]{1,0:T(2,128)S(1)}, u32[]{:S(2)}, u32[]{:S(2)}) collective-permute-start(s32[2,40]{1,0:T(2,128)S(1)} %slot_blocks.1.refs_0_.refs_1_), channel_id=1, source_target_pairs={{1,4},{3,6},{4,1},{6,3},{9,12},{11,14},{12,9},{14,11},{17,20},{19,... | collective-permute-start | bytes 968 | tf_op jit(solution)/shard_map/ppermute | solution.py:365
  26.0 5.7 %collective-permute-start.7 = (bf16[5,8,128,128]{3,2,1,0:T(8,128)(2,1)S(1)}, bf16[5,8,128,128]{3,2,1,0:T(8,128)(2,1)S(1)}, u32[]{:S(2)}, u32[]{:S(2)}) collective-permute-start(bf16[5,8,128,128]{3,2,1,0:T(8,128)(2,1)S(1)} %collective-permute-done.2.refs_1_.refs_3_), channel_id=1, source_target_pairs={{0,4},{2,6},{5,1},{7,3},{8,12},{10,14},{13,9},{15,11},{16,20},{18,... | collective-permute-start | bytes 3932168 | tf_op jit(solution)/shard_map/ppermute | solution.py:365
  29.4 6.8 %copy-start.3 = (bf16[1024,256]{1,0:T(8,128)(2,1)S(1)}, bf16[1024,256]{1,0:T(8,128)(2,1)}, u32[]{:S(2)}) copy-start(bf16[1024,256]{1,0:T(8,128)(2,1)} %x_ref.3) | copy-start | bytes 1572868
  33.8 16.1 %copy-start.1 = (bf16[256,256]{1,0:T(8,128)(2,1)S(1)}, bf16[256,256]{1,0:T(8,128)(2,1)}, u32[]{:S(2)}) copy-start(bf16[256,256]{1,0:T(8,128)(2,1)} %w_ref.3) | copy-start | bytes 393220
  33.8 14.4 %collective-permute-start.8 = (bf16[1024,128]{1,0:T(8,128)(2,1)S(1)}, bf16[1024,128]{1,0:T(8,128)(2,1)S(1)}, u32[]{:S(2)}, u32[]{:S(2)}) collective-permute-start(bf16[1024,128]{1,0:T(8,128)(2,1)S(1)} %tile_product.5), channel_id=1, source_target_pairs={{0,2},{1,3},{2,0},{3,1},{4,6},{5,7},{6,4},{7,5},{8,10},{9,11},{10,... | collective-permute-start | bytes 786440 | tf_op jit(solution)/shard_map/ppermute | solution.py:365
  36.3 12.5 %collective-permute-start.10 = (bf16[1024,128]{1,0:T(8,128)(2,1)S(1)}, bf16[1024,128]{1,0:T(8,128)(2,1)S(1)}, u32[]{:S(2)}, u32[]{:S(2)}) collective-permute-start(bf16[1024,128]{1,0:T(8,128)(2,1)S(1)} %get-tuple-element.40), channel_id=1, source_target_pairs={{0,4},{1,5},{2,6},{3,7},{4,0},{5,1},{6,2},{7,3},{8,12},{9,13},{10,... | collective-permute-start | bytes 786440 | tf_op jit(solution)/shard_map/ppermute | solution.py:365
  48.2 1.7 %collective-permute-start.9 = (bf16[1024,128]{1,0:T(8,128)(2,1)S(1)}, bf16[1024,128]{1,0:T(8,128)(2,1)S(1)}, u32[]{:S(2)}, u32[]{:S(2)}) collective-permute-start(bf16[1024,128]{1,0:T(8,128)(2,1)S(1)} %add_convert_fusion.1.near_ref), channel_id=1, source_target_pairs={{0,4},{1,5},{2,6},{3,7},{4,0},{5,1},{6,2},{7,3},{8,12},{9,13},{10,... | collective-permute-start | bytes 786440 | tf_op jit(solution)/shard_map/ppermute | solution.py:365
  50.3 7.6 %collective-permute-start.11 = (bf16[1024,128]{1,0:T(8,128)(2,1)S(1)}, bf16[1024,128]{1,0:T(8,128)(2,1)S(1)}, u32[]{:S(2)}, u32[]{:S(2)}) collective-permute-start(bf16[1024,128]{1,0:T(8,128)(2,1)S(1)} %get-tuple-element.44.refs_6_.adj_ref), channel_id=1, source_target_pairs={{0,8},{1,9},{2,10},{3,11},{4,12},{5,13},{6,14},{7,15},{8,0},{9,1},... | collective-permute-start | bytes 786440 | tf_op jit(solution)/shard_map/ppermute | solution.py:365
  50.4 8.0 %collective-permute-start.14 = (bf16[1024,128]{1,0:T(8,128)(2,1)S(1)}, bf16[1024,128]{1,0:T(8,128)(2,1)S(1)}, u32[]{:S(2)}, u32[]{:S(2)}) collective-permute-start(bf16[1024,128]{1,0:T(8,128)(2,1)S(1)} %get-tuple-element.44.refs_6_.adj_ref), channel_id=1, source_target_pairs={{0,1},{1,0},{2,3},{3,2},{4,5},{5,4},{6,7},{7,6},{8,9},{9,8},{10,11... | collective-permute-start | bytes 786440 | tf_op jit(solution)/shard_map/ppermute | solution.py:365
  57.9 12.2 %collective-permute-start.12 = (bf16[1024,128]{1,0:T(8,128)(2,1)S(1)}, bf16[1024,128]{1,0:T(8,128)(2,1)S(1)}, u32[]{:S(2)}, u32[]{:S(2)}) collective-permute-start(bf16[1024,128]{1,0:T(8,128)(2,1)S(1)} %collective-permute-done.11.refs_6_), channel_id=1, source_target_pairs={{0,16},{1,17},{2,18},{3,19},{4,20},{5,21},{6,22},{7,23},{8,24},{9,... | collective-permute-start | bytes 786440 | tf_op jit(solution)/shard_map/ppermute | solution.py:365
  58.4 11.7 %collective-permute-start.13 = (bf16[1024,128]{1,0:T(8,128)(2,1)S(1)}, bf16[1024,128]{1,0:T(8,128)(2,1)S(1)}, u32[]{:S(2)}, u32[]{:S(2)}) collective-permute-start(bf16[1024,128]{1,0:T(8,128)(2,1)S(1)} %get-tuple-element.44.refs_6_.adj_ref), channel_id=1, source_target_pairs={{0,25},{1,8},{2,27},{3,10},{4,29},{5,12},{6,31},{7,14},{8,1},{9,16... | collective-permute-start | bytes 786440 | tf_op jit(solution)/shard_map/ppermute | solution.py:365
  58.7 9.1 %collective-permute-start.15 = (f32[256,128]{1,0:T(8,128)S(1)}, f32[256,128]{1,0:T(8,128)S(1)}, u32[]{:S(2)}, u32[]{:S(2)}) collective-permute-start(f32[256,128]{1,0:T(8,128)S(1)} %grad_block.1.refs_0_), channel_id=1, source_target_pairs={{0,1},{1,0},{2,3},{3,2},{4,5},{5,4},{6,7},{7,6},{8,9},{9,8},{10,11... | collective-permute-start | bytes 393224 | tf_op jit(solution)/shard_map/ppermute | solution.py:365
  72.4 12.2 %collective-permute-start.18 = (bf16[1024,128]{1,0:T(8,128)(2,1)S(1)}, bf16[1024,128]{1,0:T(8,128)(2,1)S(1)}, u32[]{:S(2)}, u32[]{:S(2)}) collective-permute-start(bf16[1024,128]{1,0:T(8,128)(2,1)S(1)} %tile_product.7.refs_2_), channel_id=1, source_target_pairs={{0,2},{1,3},{2,0},{3,1},{4,6},{5,7},{6,4},{7,5},{8,10},{9,11},{10,... | collective-permute-start | bytes 786440 | tf_op jit(solution)/shard_map/ppermute | solution.py:365
  72.5 19.3 %collective-permute-start.16 = (bf16[1024,128]{1,0:T(8,128)(2,1)S(1)}, bf16[1024,128]{1,0:T(8,128)(2,1)S(1)}, u32[]{:S(2)}, u32[]{:S(2)}) collective-permute-start(bf16[1024,128]{1,0:T(8,128)(2,1)S(1)} %get-tuple-element.45), channel_id=1, source_target_pairs={{0,1},{1,5},{2,3},{3,7},{4,0},{5,4},{6,2},{7,6},{8,9},{9,13},{10,1... | collective-permute-start | bytes 786440 | tf_op jit(solution)/shard_map/ppermute | solution.py:365
  74.7 17.1 %collective-permute-start.17 = (bf16[1024,128]{1,0:T(8,128)(2,1)S(1)}, bf16[1024,128]{1,0:T(8,128)(2,1)S(1)}, u32[]{:S(2)}, u32[]{:S(2)}) collective-permute-start(bf16[1024,128]{1,0:T(8,128)(2,1)S(1)} %get-tuple-element.45), channel_id=1, source_target_pairs={{1,4},{3,6},{4,1},{6,3},{9,12},{11,14},{12,9},{14,11},{17,20},{19,... | collective-permute-start | bytes 786440 | tf_op jit(solution)/shard_map/ppermute | solution.py:365
  77.6 7.9 %collective-permute-start.21 = (f32[256,128]{1,0:T(8,128)S(1)}, f32[256,128]{1,0:T(8,128)S(1)}, u32[]{:S(2)}, u32[]{:S(2)}) collective-permute-start(f32[256,128]{1,0:T(8,128)S(1)} %add_after.2.refs_0_), channel_id=1, source_target_pairs={{0,8},{1,9},{2,10},{3,11},{4,12},{5,13},{6,14},{7,15},{8,0},{9,1},... | collective-permute-start | bytes 393224 | tf_op jit(solution)/shard_map/ppermute | solution.py:365
  79.5 8.3 %collective-permute-start.22 = (f32[256,128]{1,0:T(8,128)S(1)}, f32[256,128]{1,0:T(8,128)S(1)}, u32[]{:S(2)}, u32[]{:S(2)}) collective-permute-start(f32[256,128]{1,0:T(8,128)S(1)} %add_after.2.refs_0_), channel_id=1, source_target_pairs={{0,16},{1,17},{2,18},{3,19},{4,20},{5,21},{6,22},{7,23},{8,24},{9,... | collective-permute-start | bytes 393224 | tf_op jit(solution)/shard_map/ppermute | solution.py:365
  84.6 5.1 %collective-permute-start.23 = (f32[256,128]{1,0:T(8,128)S(1)}, f32[256,128]{1,0:T(8,128)S(1)}, u32[]{:S(2)}, u32[]{:S(2)}) collective-permute-start(f32[256,128]{1,0:T(8,128)S(1)} %add_after.2.refs_0_), channel_id=1, source_target_pairs={{0,24},{1,25},{2,26},{3,27},{4,28},{5,29},{6,30},{7,31},{8,16},{9,... | collective-permute-start | bytes 393224 | tf_op jit(solution)/shard_map/ppermute | solution.py:365
  85.5 7.3 %collective-permute-start.19 = (bf16[1024,128]{1,0:T(8,128)(2,1)S(1)}, bf16[1024,128]{1,0:T(8,128)(2,1)S(1)}, u32[]{:S(2)}, u32[]{:S(2)}) collective-permute-start(bf16[1024,128]{1,0:T(8,128)(2,1)S(1)} %add_convert_fusion.refs_4_.own_ref), channel_id=1, source_target_pairs={{0,1},{1,5},{2,3},{3,7},{4,0},{5,4},{6,2},{7,6},{8,9},{9,13},{10,1... | collective-permute-start | bytes 786440 | tf_op jit(solution)/shard_map/ppermute | solution.py:365
  87.8 7.7 %collective-permute-start.20 = (bf16[1024,128]{1,0:T(8,128)(2,1)S(1)}, bf16[1024,128]{1,0:T(8,128)(2,1)S(1)}, u32[]{:S(2)}, u32[]{:S(2)}) collective-permute-start(bf16[1024,128]{1,0:T(8,128)(2,1)S(1)} %add_convert_fusion.refs_4_.own_ref), channel_id=1, source_target_pairs={{1,4},{3,6},{4,1},{6,3},{9,12},{11,14},{12,9},{14,11},{17,20},{19,... | collective-permute-start | bytes 786440 | tf_op jit(solution)/shard_map/ppermute | solution.py:365
  89.7 3.0 %collective-permute-start.24 = (f32[256,128]{1,0:T(8,128)S(1)}, f32[256,128]{1,0:T(8,128)S(1)}, u32[]{:S(2)}, u32[]{:S(2)}) collective-permute-start(f32[256,128]{1,0:T(8,128)S(1)} %add_after.3.grad_ref), channel_id=1, source_target_pairs={{0,4},{1,5},{2,6},{3,7},{4,0},{5,1},{6,2},{7,3},{8,12},{9,13},{10,... | collective-permute-start | bytes 393224 | tf_op jit(solution)/shard_map/ppermute | solution.py:365

commit v6 on v5

--- a/solution.py
+++ b/solution.py
@@ -30,6 +30,35 @@
     return r % 2, z, z % 2
 
 
+def when_of(case):
+    j, z, p = place()
+    home = j == p
+    relay = jnp.logical_and(
+        lax.axis_size("rows") == 8, (lax.axis_index("rows") // 2 + z) % 2 == 1
+    )
+    return {
+        "home": home,
+        "away": jnp.logical_not(home),
+        "relay": relay,
+        "still": jnp.logical_not(relay),
+        "relay home": jnp.logical_and(relay, home),
+        "relay away": jnp.logical_and(relay, jnp.logical_not(home)),
+        "still home": jnp.logical_and(jnp.logical_not(relay), home),
+        "still away": jnp.logical_and(jnp.logical_not(relay), jnp.logical_not(home)),
+    }[case]
+
+
+def start_chosen(choice, make):
+    if len(choice) == 1:
+        make(choice[0][1]).start()
+        return
+    for case, ref in choice:
+
+        @pl.when(when_of(case))
+        def _(ref=ref):
+            make(ref).start()
+
+
 def halves_kernel(x_ref, near_ref, far_ref, sems):
     j, _, _ = place()
     half = near_ref.shape[1]
@@ -58,42 +87,33 @@
     )(value)
 
 
-def pick_kernel(mine_ref, swapped_ref, group_ref, other_ref, sems):
-    j, _, p = place()
-
-    def copies(own, other):
-        return [
-            pltpu.make_async_copy(own, group_ref, sems.at[0]),
-            pltpu.make_async_copy(other, other_ref, sems.at[1]),
-        ]
-
-    @pl.when(j == p)
-    def _():
-        for copy in copies(mine_ref, swapped_ref):
-            copy.start()
-        for copy in copies(mine_ref, swapped_ref):
-            copy.wait()
-
-    @pl.when(j != p)
-    def _():
-        for copy in copies(swapped_ref, mine_ref):
-            copy.start()
-        for copy in copies(swapped_ref, mine_ref):
-            copy.wait()
-
-
-def pick(mine, swapped):
+def pick_kernel(cases, *refs):
+    refs = list(refs)
+    choices = [[(case, refs.pop(0)) for case in each] for each in cases]
+    outs, sems = refs[:-1], refs[-1]
+
+    def copy_to(i):
+        return lambda ref: pltpu.make_async_copy(ref, outs[i], sems.at[i])
+
+    for i, choice in enumerate(choices):
+        start_chosen(choice, copy_to(i))
+    for i, choice in enumerate(choices):
+        copy_to(i)(choice[0][1]).wait()
+
+
+def pick(*choices):
     hbm = pl.BlockSpec(memory_space=pltpu.HBM)
-    shape = jax.ShapeDtypeStruct(mine.shape, mine.dtype)
-    return pl.pallas_call(
-        pick_kernel,
-        out_shape=(shape, shape),
-        in_specs=[hbm, hbm],
-        out_specs=(hbm, hbm),
-        scratch_shapes=[pltpu.SemaphoreType.DMA((2,))],
+    arrays = [array for choice in choices for _, array in choice]
+    shape = jax.ShapeDtypeStruct(arrays[0].shape, arrays[0].dtype)
+    return pl.pallas_call(
+        functools.partial(pick_kernel, [[case for case, _ in choice] for choice in choices]),
+        out_shape=(shape,) * len(choices),
+        in_specs=[hbm] * len(arrays),
+        out_specs=(hbm,) * len(choices),
+        scratch_shapes=[pltpu.SemaphoreType.DMA((len(choices),))],
         compiler_params=pltpu.CompilerParams(vmem_limit_bytes=1024 * 1024),
         name="pick",
-    )(mine, swapped)
+    )(*arrays)
 
 
 def slots_kernel(dead, coords_ref, counts_ref, out_ref):
@@ -130,11 +150,11 @@
     }[kind]
 
 
-def tile_kernel(kinds, sets, summed, waits, *refs):
+def tile_kernel(kinds, cases, sets, summed, waits, *refs):
     refs = list(refs)
     metas = [refs.pop(0) for _ in range(sum(sets))]
     tiles = [refs.pop(0) for _ in range(sum(sets))]
-    panels = [refs.pop(0) for _ in kinds]
+    panels = [[(case, refs.pop(0)) for case in each] for each in cases]
     before = refs.pop(0) if summed else None
     out_ref, acc_ref, tile_buf, panel_buf, tile_sems, panel_sems = refs[waits:]
     slots, tile = tile_buf.shape[2], tile_buf.shape[-1]
@@ -147,24 +167,17 @@
         return pltpu.make_async_copy(ref.at[offsets[i]], tile_buf.at[i, s], tile_sems.at[i, s])
 
     def panel_copy(i):
-        return pltpu.make_async_copy(panels[i], panel_buf.at[i], panel_sems.at[i])
+        return lambda ref: pltpu.make_async_copy(ref, panel_buf.at[i], panel_sems.at[i])
 
     for i in range(len(kinds)):
-        panel_copy(i).start()
+        start_chosen(panels[i], panel_copy(i))
         at = 0
         for s, members in enumerate(sets):
-            if members == 1:
-                tile_copy(tiles[at], i, s).start()
-            else:
-
-                @pl.when(home)
-                def _(ref=tiles[at], i=i, s=s):
-                    tile_copy(ref, i, s).start()
-
-                @pl.when(jnp.logical_not(home))
-                def _(ref=tiles[at + 1], i=i, s=s):
-                    tile_copy(ref, i, s).start()
-
+            cases_of_set = ["home", "away"] if members == 2 else [None]
+            start_chosen(
+                list(zip(cases_of_set, tiles[at : at + members])),
+                lambda ref, i=i, s=s: tile_copy(ref, i, s),
+            )
             at += members
     if summed:
         acc_ref[:rows, :] = before[...]
@@ -172,7 +185,7 @@
         acc_ref[...] = jnp.zeros_like(acc_ref)
     for i in range(len(kinds)):
         d = offsets[i]
-        panel_copy(i).wait()
+        panel_copy(i)(panels[i][0][1]).wait()
         at = 0
         for s, members in enumerate(sets):
             tile_copy(tiles[at], i, s).wait()
@@ -199,7 +212,8 @@
 
 def tile_product(named, sets, dtype, before=None, after=()):
     kinds = [kind for kind, _ in named]
-    panels = [panel for _, panel in named]
+    cases = [[case for case, _ in choice] for _, choice in named]
+    panels = [panel for _, choice in named for _, panel in choice]
     metas = [meta for members in sets for meta, _ in members]
     tiles = [values for members in sets for _, values in members]
     rows, width = panels[0].shape
@@ -211,7 +225,9 @@
     count = len(kinds) * len(sets) * slots
     summed = before is not None
     return pl.pallas_call(
-        functools.partial(tile_kernel, kinds, [len(m) for m in sets], summed, len(after)),
+        functools.partial(
+            tile_kernel, kinds, cases, [len(m) for m in sets], summed, len(after)
+        ),
         out_shape=jax.ShapeDtypeStruct((rows, width), dtype),
         in_specs=[smem] * len(metas)
         + [hbm] * len(tiles)
@@ -278,9 +294,8 @@
     dims = (((0,), (0,)), ((), ()))
     for i, ref in enumerate((near_ref, far_ref)):
         start = pl.multiple_of((j if i == 0 else 1 - j) * half, half)
-        out_ref[pl.ds(start, half), :] = scale * lax.dot_general(
-            ref[...], adj_ref[...], dims, preferred_element_type=jnp.float32
-        )
+        block = lax.dot_general(ref[...], adj_ref[...], dims, preferred_element_type=jnp.float32)
+        out_ref[pl.ds(start, half), :] = (scale * block).astype(out_ref.dtype)
 
 
 def grad_block(scale, near, far, adj, after):
@@ -288,7 +303,7 @@
     rows, width = near.shape
     return pl.pallas_call(
         functools.partial(grad_kernel, scale),
-        out_shape=jax.ShapeDtypeStruct((2 * width, width), jnp.float32),
+        out_shape=jax.ShapeDtypeStruct((2 * width, width), jnp.bfloat16),
         in_specs=[vmem] * 3 + [pl.BlockSpec(memory_space=pl.ANY)],
         out_specs=vmem,
         compiler_params=pltpu.CompilerParams(vmem_limit_bytes=8 * 1024 * 1024),
@@ -300,17 +315,18 @@
 
 
 def add_kernel(count, *refs):
-    total = refs[0][...].astype(jnp.float32) + refs[1][...].astype(jnp.float32)
+    values = [ref[...].astype(jnp.float32) for ref in refs[:count]]
+    total = values[0] + values[1]
     if count == 4:
-        total = total + (refs[2][...] + refs[3][...])
+        total = total + (values[2] + values[3])
     refs[-1][...] = total.astype(refs[-1].dtype)
 
 
-def add_after(values, *after):
+def add_after(values, dtype, *after):
     vmem = pl.BlockSpec(memory_space=pltpu.VMEM)
     return pl.pallas_call(
         functools.partial(add_kernel, len(values)),
-        out_shape=jax.ShapeDtypeStruct(values[0].shape, values[0].dtype),
+        out_shape=jax.ShapeDtypeStruct(values[0].shape, dtype),
         in_specs=[vmem] * len(values) + [pl.BlockSpec(memory_space=pl.ANY)] * len(after),
         out_specs=vmem,
         compiler_params=pltpu.CompilerParams(vmem_limit_bytes=4 * 1024 * 1024),
@@ -376,24 +392,45 @@
     def to_home(c, j, z):
         return (c, 1 - j, z) if j == z % 2 else (c, j, z ^ 1)
 
+    four = shape[0] == 4
+
     def to_direct(c, j, z):
         return (c ^ 1, j, z)
 
     def to_second(c, j, z):
-        return (c ^ 2, j, z) if shape[0] == 4 else (c + 1 if c % 2 else c - 1, j, z)
-
-    def hand_on(value, direct):
-        return send(direct if shape[0] == 4 else value, to_second)
+        return (c ^ 2, j, z) if four else (c + 1 if c % 2 else c - 1, j, z)
+
+    def to_far(c, j, z):
+        return (c ^ 1, j, z) if four else (c - 1 if z % 2 else c + 1, j, z)
+
+    def stage_one(c, j, z):
+        if j == z % 2:
+            return (c ^ 1, j, z)
+        return (c ^ 2, j, z) if four and (c + z) % 2 else None
+
+    def stage_one_cross(c, j, z):
+        to = stage_one(c, j, z)
+        return to and (to[0], 1 - j, z)
 
     first = send(own, to_home)
     mine, yours = halves(node_feats)
-    feats, feats_other = pick(mine, send(yours, sibling))
-    direct = send(feats, to_direct)
-    coords, counts, feats_later, direct = lax.optimization_barrier(
-        (tile_coords, tile_counts, feats_other, direct)
-    )
-    second = hand_on(feats, direct)
-    far = send(feats_later, lambda c, j, z: (c - 1 if z % 2 else c + 1, j, z))
+    one = send(mine, stage_one)
+    two = send(yours, stage_one_cross)
+    swapped = send(yours, sibling)
+    self_choice = [("home", mine), ("away", swapped)]
+    direct_choice = [("home", one), ("away", two)]
+    second, far = pick(
+        direct_choice if four else self_choice,
+        [
+            ("still home", swapped),
+            ("still away", mine),
+            ("relay home", two),
+            ("relay away", one),
+        ],
+    )
+    second = send(second, to_second)
+    far = send(far, to_far)
+    coords, counts, swapped = lax.optimization_barrier((tile_coords, tile_counts, swapped))
     meta = slot_blocks(coords[:, 0], counts[0], blocks)
     meta_b = send(meta, to_home)
     meta_far = send(meta, lambda c, j, z: None if j == z % 2 else (c, 1 - j, z ^ 1))
@@ -405,11 +442,11 @@
     set_first = [(meta_b, first)]
     set_rest = [(meta, own), (meta_far, other_first)]
     panels = [
-        ("self", feats),
-        ("near", feats_other),
-        ("direct", direct),
-        ("second", second),
-        ("far", far),
+        ("self", [("home", mine), ("away", swapped)]),
+        ("near", [("home", swapped), ("away", mine)]),
+        ("direct", direct_choice),
+        ("second", [(None, second)]),
+        ("far", [(None, far)]),
     ]
     part = tile_product(panels, [set_first], jnp.float32)
     part = tile_product(panels, [set_rest], jnp.bfloat16, part)
@@ -419,20 +456,28 @@
         return (value.astype(jnp.float32) + other.astype(jnp.float32)).astype(jnp.bfloat16)
 
     near = join(part)
-    far = send(near, sibling)
+    far_half = send(near, sibling)
     cot, cot_yours = halves(cotangent)
-    act, adj = middle(near, far, weight, cot, send(cot_yours, sibling))
-
-    other = send(adj, lambda c, j, z: (c, j, z ^ 1))
+    act, adj = middle(near, far_half, weight, cot, send(cot_yours, sibling))
+
     direct = send(adj, to_direct)
-    adj_later, direct = lax.optimization_barrier((adj, direct))
-    second = hand_on(adj, direct)
-    third = send(adj_later, lambda c, j, z: (c + 1 if z % 2 else c - 1, j, z ^ 1))
-    grad = grad_block(scale, near, far, adj, other)
+    near_one = send(
+        adj, lambda c, j, z: (c if (c + z) % 2 or not four else c ^ 2, j, z ^ 1)
+    )
+    adj_later, near_one, direct = lax.optimization_barrier((adj, near_one, direct))
+    second = send(direct if four else adj_later, to_second)
+    far = send(near_one, to_far)
+    near_choice = [("still", near_one)]
+    if four:
+        near_two = send(
+            adj_later, lambda c, j, z: None if (c + z) % 2 else (c, j, z ^ 1)
+        )
+        near_choice.append(("relay", near_two))
+    grad = grad_block(scale, near, far_half, adj, direct)
     grad_got = send(grad, lambda c, j, z: (c, j, z ^ 1))
-    panels = [("self", adj), ("near", other)]
+    panels = [("self", [(None, adj)]), ("direct", [(None, direct)])]
     back_part = tile_product(panels, [set_first, set_rest], jnp.float32)
-    panels = [("direct", direct), ("second", second), ("far", third)]
+    panels = [("near", near_choice), ("second", [(None, second)]), ("far", [(None, far)])]
     back_part = tile_product(
         panels, [set_first, set_rest], jnp.bfloat16, back_part, [grad_got]
     )
@@ -453,13 +498,13 @@
     back = join(back_part)
     back_one, back_two = deliver(back)
 
-    grad = add_after([grad, grad_got], back_part)
+    grad = add_after([grad, grad_got], jnp.bfloat16, back_part)
     step = 1
     while step < shape[0]:
         flips = [step] if step * 2 >= shape[0] else [step, 2 * step, 3 * step]
         got = [send(grad, lambda c, j, z, s=s: (c ^ s, j, z)) for s in flips]
-        grad = add_after([grad, *got], back)
         step *= 2 if len(flips) == 1 else 4
+        grad = add_after([grad, *got], jnp.bfloat16 if step < shape[0] else jnp.float32, back)
     grad_rest = send(grad, sibling)
     input_grad, weight_grad = final(back, back_one, back_two, weight, grad, grad_rest)
     return (activated, input_grad, weight_grad)

time: 97 us -> 95.3 us (0.982)
  waiting for transfers between devices: 47.3 us -> 34.4 us
  starting transfers between devices: 33.1 us -> 45.5 us
  local copies, waits for them, and re-layouts: 2.41 us -> 1.08 us
    ppermute x25 -> x27, waiting for transfers between devices: 47.3 us -> 34.4 us  [send(): return lax.ppermute(value, AXES, route(shape, move))]
    ppermute x25 -> x27, starting transfers between devices: 33.1 us -> 45.5 us  [send(): return lax.ppermute(value, AXES, route(shape, move))]
  transfers between devices with their start and end apart: 25 -> 27, of which waited for: 13 -> 14; matrix products, arithmetic and copies ran while one was open for 2% -> 1% of each run, Pallas kernels for 6% -> 6%
where the time goes in v6:
time: 95.3 us; the launch traced here: 95 us
  starting transfers between devices  45.5 us (48%)
  waiting for transfers between devices  34.4 us (36%)
  Pallas kernels  12.1 us (13%)
  local copies, waits for them, and re-layouts  1.08 us (1%)
  other arithmetic  1.04 us (1%)
    ppermute x27, starting transfers between devices, send(): return lax.ppermute(value, AXES, route(shape, move))  45.5 us
    ppermute x27, waiting for transfers between devices, send(): return lax.ppermute(value, AXES, route(shape, move))  34.4 us
    pallas_call x4, Pallas kernels, tile_product(): pl.pallas_call(functools.partial(tile_kernel, kinds, cases, [len(m) for m...  8.39 us
  transfers between devices with their start and end apart: 27, of which 14 were waited for; matrix products, arithmetic and copies ran while one was open for 1% of the time, Pallas kernels for 6%

profile of v6, /device:TPU:1, one launch (start us, length us, event | category | flops | bytes accessed | tf_op | source)
XLA Modules:
  0.0 95.0 jit_solution(12259037820219245198)
XLA Ops:
  0.6 2.2 %collective-permute-start.1 = (bf16[5,8,128,128]{3,2,1,0:T(8,128)(2,1)}, bf16[5,8,128,128]{3,2,1,0:T(8,128)(2,1)S(1)}, u32[]{:S(2)}, u32[]{:S(2)}) collective-permute-start(bf16[5,8,128,128]{3,2,1,0:T(8,128)(2,1)} %bitcast.5), channel_id=1, source_target_pairs={{0,4},{1,0},{2,6},{3,2},{4,5},{5,1},{6,7},{7,3},{8,12},{9,8},{10,1... | collective-permute-start | bytes 3932168 | tf_op jit(solution)/shard_map/ppermute | solution.py:381
  2.8 1.0 %copy-done.2 = bf16[1024,256]{1,0:T(8,128)(2,1)S(1)} copy-done((bf16[1024,256]{1,0:T(8,128)(2,1)S(1)}, bf16[1024,256]{1,0:T(8,128)(2,1)}, u32[]{:S(2)}) %copy-start.2) | copy-done | bytes 524312
  4.0 0.7 collective-permute-start.2
  4.7 1.3 %collective-permute-start.3 = (bf16[1024,128]{1,0:T(8,128)(2,1)S(1)}, bf16[1024,128]{1,0:T(8,128)(2,1)S(1)}, u32[]{:S(2)}, u32[]{:S(2)}) collective-permute-start(bf16[1024,128]{1,0:T(8,128)(2,1)S(1)} %get-tuple-element.26), channel_id=1, source_target_pairs={{0,12},{1,21},{2,14},{3,23},{5,9},{7,11},{8,4},{10,6},{12,24},{13,... | collective-permute-start | bytes 786440 | tf_op jit(solution)/shard_map/ppermute | solution.py:381
  6.0 4.8 %collective-permute-start = (bf16[1024,128]{1,0:T(8,128)(2,1)S(1)}, bf16[1024,128]{1,0:T(8,128)(2,1)S(1)}, u32[]{:S(2)}, u32[]{:S(2)}) collective-permute-start(bf16[1024,128]{1,0:T(8,128)(2,1)S(1)} %get-tuple-element.26), channel_id=1, source_target_pairs={{0,4},{1,5},{2,6},{3,7},{4,0},{5,1},{6,2},{7,3},{8,12},{9,13},{10,... | collective-permute-start | bytes 786440 | tf_op jit(solution)/shard_map/ppermute | solution.py:381
  10.8 2.8 %collective-permute-done.3.refs_1_.refs_4_.refs_7_.refs_9_ = bf16[1024,128]{1,0:T(8,128)(2,1)S(1)} collective-permute-done((bf16[1024,128]{1,0:T(8,128)(2,1)S(1)}, bf16[1024,128]{1,0:T(8,128)(2,1)S(1)}, u32[]{:S(2)}, u32[]{:S(2)}) %collective-permute-start.3) | collective-permute-done | bytes 262176 | tf_op jit(solution)/shard_map/ppermute | solution.py:381
  13.6 1.8 %collective-permute-start.4 = (bf16[1024,128]{1,0:T(8,128)(2,1)S(1)}, bf16[1024,128]{1,0:T(8,128)(2,1)S(1)}, u32[]{:S(2)}, u32[]{:S(2)}) collective-permute-start(bf16[1024,128]{1,0:T(8,128)(2,1)S(1)} %get-tuple-element.30), channel_id=1, source_target_pairs={{0,16},{1,17},{2,18},{3,19},{4,20},{5,21},{6,22},{7,23},{8,24},{9,... | collective-permute-start | bytes 786440 | tf_op jit(solution)/shard_map/ppermute | solution.py:381
  15.5 1.3 %collective-permute-start.5 = (bf16[1024,128]{1,0:T(8,128)(2,1)S(1)}, bf16[1024,128]{1,0:T(8,128)(2,1)S(1)}, u32[]{:S(2)}, u32[]{:S(2)}) collective-permute-start(bf16[1024,128]{1,0:T(8,128)(2,1)S(1)} %get-tuple-element.31), channel_id=1, source_target_pairs={{0,8},{1,9},{2,10},{3,11},{4,12},{5,13},{6,14},{7,15},{8,0},{9,1},... | collective-permute-start | bytes 786440 | tf_op jit(solution)/shard_map/ppermute | solution.py:381
  16.8 1.3 %slot_blocks.1.refs_0_.refs_1_ = s32[2,40]{1,0:T(2,128)S(1)} custom-call(s32[2,5,8]{2,1,0:T(8,128)S(1)} %copy.10.coords_ref, s32[5]{0:T(128)S(1)} %bitcast.9), custom_call_target="tpu_custom_call" | custom-call | tf_op jit(solution)/shard_map/slot_blocks/pallas_call | solution.py:131
  18.1 0.2 collective-permute-start.6
  18.4 4.4 %collective-permute-start.7 = (s32[2,40]{1,0:T(2,128)S(1)}, s32[2,40]{1,0:T(2,128)S(1)}, u32[]{:S(2)}, u32[]{:S(2)}) collective-permute-start(s32[2,40]{1,0:T(2,128)S(1)} %slot_blocks.1.refs_0_.refs_1_), channel_id=1, source_target_pairs={{1,4},{3,6},{4,1},{6,3},{9,12},{11,14},{12,9},{14,11},{17,20},{19,... | collective-permute-start | bytes 968 | tf_op jit(solution)/shard_map/ppermute | solution.py:381
  22.8 1.2 %collective-permute-done.7.refs_1_.refs_2_ = s32[2,40]{1,0:T(2,128)S(1)} collective-permute-done((s32[2,40]{1,0:T(2,128)S(1)}, s32[2,40]{1,0:T(2,128)S(1)}, u32[]{:S(2)}, u32[]{:S(2)}) %collective-permute-start.7) | collective-permute-done | bytes 352 | tf_op jit(solution)/shard_map/ppermute | solution.py:381
  24.0 1.3 %collective-permute-start.8 = (bf16[5,8,128,128]{3,2,1,0:T(8,128)(2,1)S(1)}, bf16[5,8,128,128]{3,2,1,0:T(8,128)(2,1)S(1)}, u32[]{:S(2)}, u32[]{:S(2)}) collective-permute-start(bf16[5,8,128,128]{3,2,1,0:T(8,128)(2,1)S(1)} %collective-permute-done.1.refs_1_.refs_3_), channel_id=1, source_target_pairs={{0,4},{2,6},{5,1},{7,3},{8,12},{10,14},{13,9},{15,11},{16,20},{18,... | collective-permute-start | bytes 3932168 | tf_op jit(solution)/shard_map/ppermute | solution.py:381
  25.3 2.1 %tile_product.4.refs_12_ = f32[1024,128]{1,0:T(8,128)S(1)} custom-call(s32[2,40]{1,0:T(2,128)S(1)} %collective-permute-done.6.refs_0_, bf16[5,8,128,128]{3,2,1,0:T(8,128)(2,1)S(1)} %collective-permute-done.1.refs_1_.refs_3_, bf16[1024,128]{1,0:T(8,128)(2,1)S(1)} %get-tuple-element.29.refs_3_.refs_2_.refs_5_.refs_4_.refs_7_, ...), custom_call_target="tpu_custom_call" | custom-call | flops 167772160 | bytes 2621440 | tf_op jit(solution)/shard_map/tile_product/pallas_call | solution.py:227
  27.5 1.5 %collective-permute-done.8.refs_3_.refs_5_ = bf16[5,8,128,128]{3,2,1,0:T(8,128)(2,1)S(1)} collective-permute-done((bf16[5,8,128,128]{3,2,1,0:T(8,128)(2,1)S(1)}, bf16[5,8,128,128]{3,2,1,0:T(8,128)(2,1)S(1)}, u32[]{:S(2)}, u32[]{:S(2)}) %collective-permute-start.8) | collective-permute-done | bytes 1310752 | tf_op jit(solution)/shard_map/ppermute | solution.py:381
  28.9 2.1 %tile_product.5 = bf16[1024,128]{1,0:T(8,128)(2,1)S(1)} custom-call(s32[2,40]{1,0:T(2,128)S(1)} %slot_blocks.1.refs_0_.refs_1_, s32[2,40]{1,0:T(2,128)S(1)} %collective-permute-done.7.refs_1_.refs_2_, bf16[5,8,128,128]{3,2,1,0:T(8,128)(2,1)S(1)} %bitcast.6, bf16[5,8,128,128]{3,2,1,0:T(8,128)(2,1)S(1)} %collective-permute-done.8.refs_3_.refs_5_, ...), custom_call_target="tpu_custom_call" | custom-call | flops 167772160 | bytes 2621440 | tf_op jit(solution)/shard_map/tile_product/pallas_call | solution.py:227
  31.1 2.4 %collective-permute-start.9 = (bf16[1024,128]{1,0:T(8,128)(2,1)S(1)}, bf16[1024,128]{1,0:T(8,128)(2,1)S(1)}, u32[]{:S(2)}, u32[]{:S(2)}) collective-permute-start(bf16[1024,128]{1,0:T(8,128)(2,1)S(1)} %tile_product.5), channel_id=1, source_target_pairs={{0,2},{1,3},{2,0},{3,1},{4,6},{5,7},{6,4},{7,5},{8,10},{9,11},{10,... | collective-permute-start | bytes 786440 | tf_op jit(solution)/shard_map/ppermute | solution.py:381
  33.6 0.5 collective-permute-start.11
  34.1 11.3 %collective-permute-done.9 = bf16[1024,128]{1,0:T(8,128)(2,1)S(1)} collective-permute-done((bf16[1024,128]{1,0:T(8,128)(2,1)S(1)}, bf16[1024,128]{1,0:T(8,128)(2,1)S(1)}, u32[]{:S(2)}, u32[]{:S(2)}) %collective-permute-start.9) | collective-permute-done | bytes 262176 | tf_op jit(solution)/shard_map/ppermute | solution.py:381
  45.5 1.0 %collective-permute-start.10 = (bf16[1024,128]{1,0:T(8,128)(2,1)S(1)}, bf16[1024,128]{1,0:T(8,128)(2,1)S(1)}, u32[]{:S(2)}, u32[]{:S(2)}) collective-permute-start(bf16[1024,128]{1,0:T(8,128)(2,1)S(1)} %add_convert_fusion.1.near_ref), channel_id=1, source_target_pairs={{0,4},{1,5},{2,6},{3,7},{4,0},{5,1},{6,2},{7,3},{8,12},{9,13},{10,... | collective-permute-start | bytes 786440 | tf_op jit(solution)/shard_map/ppermute | solution.py:381
  46.5 1.2 %collective-permute-done.10.far_ref = bf16[1024,128]{1,0:T(8,128)(2,1)S(1)} collective-permute-done((bf16[1024,128]{1,0:T(8,128)(2,1)S(1)}, bf16[1024,128]{1,0:T(8,128)(2,1)S(1)}, u32[]{:S(2)}, u32[]{:S(2)}) %collective-permute-start.10) | collective-permute-done | bytes 262176 | tf_op jit(solution)/shard_map/ppermute | solution.py:381
  47.7 0.4 middle.1
  48.1 0.7 collective-permute-start.12
  48.8 0.3 collective-permute-start.13
  49.2 6.5 %collective-permute-done.12.refs_6_ = bf16[1024,128]{1,0:T(8,128)(2,1)S(1)} collective-permute-done((bf16[1024,128]{1,0:T(8,128)(2,1)S(1)}, bf16[1024,128]{1,0:T(8,128)(2,1)S(1)}, u32[]{:S(2)}, u32[]{:S(2)}) %collective-permute-start.12) | collective-permute-done | bytes 262176 | tf_op jit(solution)/shard_map/ppermute | solution.py:381
  55.7 0.4 collective-permute-done.13.refs_7_.after_ref
  56.0 2.8 %collective-permute-start.14 = (bf16[1024,128]{1,0:T(8,128)(2,1)S(1)}, bf16[1024,128]{1,0:T(8,128)(2,1)S(1)}, u32[]{:S(2)}, u32[]{:S(2)}) collective-permute-start(bf16[1024,128]{1,0:T(8,128)(2,1)S(1)} %get-tuple-element.43.refs_6_.adj_ref), channel_id=1, source_target_pairs={{0,1},{2,3},{4,5},{6,7},{9,8},{11,10},{13,12},{15,14},{16,17},{18,... | collective-permute-start | bytes 786440 | tf_op jit(solution)/shard_map/ppermute | solution.py:381
  58.9 0.7 collective-permute-start.15
  59.7 0.3 grad_block.1.refs_0_
  60.0 2.2 %collective-permute-start.17 = (bf16[256,128]{1,0:T(8,128)(2,1)S(1)}, bf16[256,128]{1,0:T(8,128)(2,1)S(1)}, u32[]{:S(2)}, u32[]{:S(2)}) collective-permute-start(bf16[256,128]{1,0:T(8,128)(2,1)S(1)} %grad_block.1.refs_0_), channel_id=1, source_target_pairs={{0,1},{1,0},{2,3},{3,2},{4,5},{5,4},{6,7},{7,6},{8,9},{9,8},{10,11... | collective-permute-start | bytes 196616 | tf_op jit(solution)/shard_map/ppermute | solution.py:381
  62.2 1.8 %tile_product.6.refs_10_ = f32[1024,128]{1,0:T(8,128)S(1)} custom-call(s32[2,40]{1,0:T(2,128)S(1)} %collective-permute-done.6.refs_0_, s32[2,40]{1,0:T(2,128)S(1)} %slot_blocks.1.refs_0_.refs_1_, s32[2,40]{1,0:T(2,128)S(1)} %collective-permute-done.7.refs_1_.refs_2_, bf16[5,8,128,128]{3,2,1,0:T(8,128)(2,1)S(1)} %collective-permute-done.1.refs_1_.refs_3_, ...), custom_call_target="tpu_custom_call" | custom-call | flops 134217728 | bytes 1572864 | tf_op jit(solution)/shard_map/tile_product/pallas_call | solution.py:227
  64.0 0.5 collective-permute-done.17.refs_11_.refs_1_
  64.5 0.6 collective-permute-done.15.refs_8_
  65.1 0.2 collective-permute-done.16.refs_9_
  65.3 2.3 %tile_product.7.refs_2_ = bf16[1024,128]{1,0:T(8,128)(2,1)S(1)} custom-call(s32[2,40]{1,0:T(2,128)S(1)} %collective-permute-done.6.refs_0_, s32[2,40]{1,0:T(2,128)S(1)} %slot_blocks.1.refs_0_.refs_1_, s32[2,40]{1,0:T(2,128)S(1)} %collective-permute-done.7.refs_1_.refs_2_, bf16[5,8,128,128]{3,2,1,0:T(8,128)(2,1)S(1)} %collective-permute-done.1.refs_1_.refs_3_, ...), custom_call_target="tpu_custom_call" | custom-call | flops 201326592 | bytes 2359296 | tf_op jit(solution)/shard_map/tile_product/pallas_call | solution.py:227
  67.6 3.5 %collective-permute-start.20 = (bf16[1024,128]{1,0:T(8,128)(2,1)S(1)}, bf16[1024,128]{1,0:T(8,128)(2,1)S(1)}, u32[]{:S(2)}, u32[]{:S(2)}) collective-permute-start(bf16[1024,128]{1,0:T(8,128)(2,1)S(1)} %tile_product.7.refs_2_), channel_id=1, source_target_pairs={{0,2},{1,3},{2,0},{3,1},{4,6},{5,7},{6,4},{7,5},{8,10},{9,11},{10,... | collective-permute-start | bytes 786440 | tf_op jit(solution)/shard_map/ppermute | solution.py:381
  71.1 3.0 %collective-permute-start.18 = (bf16[1024,128]{1,0:T(8,128)(2,1)S(1)}, bf16[1024,128]{1,0:T(8,128)(2,1)S(1)}, u32[]{:S(2)}, u32[]{:S(2)}) collective-permute-start(bf16[1024,128]{1,0:T(8,128)(2,1)S(1)} %get-tuple-element.45), channel_id=1, source_target_pairs={{0,1},{1,5},{2,3},{3,7},{4,0},{5,4},{6,2},{7,6},{8,9},{9,13},{10,1... | collective-permute-start | bytes 786440 | tf_op jit(solution)/shard_map/ppermute | solution.py:381
  74.1 2.5 %collective-permute-start.19 = (bf16[1024,128]{1,0:T(8,128)(2,1)S(1)}, bf16[1024,128]{1,0:T(8,128)(2,1)S(1)}, u32[]{:S(2)}, u32[]{:S(2)}) collective-permute-start(bf16[1024,128]{1,0:T(8,128)(2,1)S(1)} %get-tuple-element.45), channel_id=1, source_target_pairs={{1,4},{3,6},{4,1},{6,3},{9,12},{11,14},{12,9},{14,11},{17,20},{19,... | collective-permute-start | bytes 786440 | tf_op jit(solution)/shard_map/ppermute | solution.py:381
  76.6 0.5 collective-permute-start.23
  77.1 0.5 collective-permute-start.24
  77.7 4.8 %collective-permute-done.20 = bf16[1024,128]{1,0:T(8,128)(2,1)S(1)} collective-permute-done((bf16[1024,128]{1,0:T(8,128)(2,1)S(1)}, bf16[1024,128]{1,0:T(8,128)(2,1)S(1)}, u32[]{:S(2)}, u32[]{:S(2)}) %collective-permute-start.20) | collective-permute-done | bytes 262176 | tf_op jit(solution)/shard_map/ppermute | solution.py:381
  82.4 2.7 %collective-permute-start.25 = (bf16[256,128]{1,0:T(8,128)(2,1)S(1)}, bf16[256,128]{1,0:T(8,128)(2,1)S(1)}, u32[]{:S(2)}, u32[]{:S(2)}) collective-permute-start(bf16[256,128]{1,0:T(8,128)(2,1)S(1)} %add_after.2.refs_0_), channel_id=1, source_target_pairs={{0,24},{1,25},{2,26},{3,27},{4,28},{5,29},{6,30},{7,31},{8,16},{9,... | collective-permute-start | bytes 196616 | tf_op jit(solution)/shard_map/ppermute | solution.py:381
  85.2 0.9 collective-permute-start.21
  86.1 1.9 %collective-permute-start.22 = (bf16[1024,128]{1,0:T(8,128)(2,1)S(1)}, bf16[1024,128]{1,0:T(8,128)(2,1)S(1)}, u32[]{:S(2)}, u32[]{:S(2)}) collective-permute-start(bf16[1024,128]{1,0:T(8,128)(2,1)S(1)} %add_convert_fusion.refs_4_.own_ref), channel_id=1, source_target_pairs={{1,4},{3,6},{4,1},{6,3},{9,12},{11,14},{12,9},{14,11},{17,20},{19,... | collective-permute-start | bytes 786440 | tf_op jit(solution)/shard_map/ppermute | solution.py:381
  88.0 1.3 %collective-permute-start.26 = (f32[256,128]{1,0:T(8,128)S(1)}, f32[256,128]{1,0:T(8,128)S(1)}, u32[]{:S(2)}, u32[]{:S(2)}) collective-permute-start(f32[256,128]{1,0:T(8,128)S(1)} %add_after.3.grad_ref), channel_id=1, source_target_pairs={{0,4},{1,5},{2,6},{3,7},{4,0},{5,1},{6,2},{7,3},{8,12},{9,13},{10,... | collective-permute-start | bytes 393224 | tf_op jit(solution)/shard_map/ppermute | solution.py:381
  89.4 0.9 pad_maximum_fusion
  90.5 3.3 %collective-permute-done.22.two_ref = bf16[1024,128]{1,0:T(8,128)(2,1)S(1)} collective-permute-done((bf16[1024,128]{1,0:T(8,128)(2,1)S(1)}, bf16[1024,128]{1,0:T(8,128)(2,1)S(1)}, u32[]{:S(2)}, u32[]{:S(2)}) %collective-permute-start.22) | collective-permute-done | bytes 262176 | tf_op jit(solution)/shard_map/ppermute | solution.py:381
  93.8 1.3 %final.1 = (bf16[1024,256]{1,0:T(8,128)(2,1)}, f32[256,256]{1,0:T(8,128)}) custom-call(bf16[1024,128]{1,0:T(8,128)(2,1)S(1)} %add_convert_fusion.refs_4_.own_ref, bf16[1024,128]{1,0:T(8,128)(2,1)S(1)} %collective-permute-done.21.one_ref, bf16[1024,128]{1,0:T(8,128)(2,1)S(1)} %collective-permute-done.22.two_ref, bf16[256,256]{1,0:T(8,128)(2,1)S(1)} %copy-done.1, ...), custom_call_target="tpu_custom_call" | custom-call | flops 134217728 | bytes 2097152 | tf_op jit(solution)/shard_map/final/pallas_call | solution.py:356
  (37 shorter events, 1.0 us)
Async XLA Ops:
  0.6 16.1 %copy-start.4 = (s32[1,5]{1,0:T(1,128)S(1)}, s32[1,5]{1,0:T(1,128)}, u32[]{:S(2)}) copy-start(s32[1,5]{1,0:T(1,128)} %param.11) | copy-start | bytes 64
  0.6 23.4 %collective-permute-start.1 = (bf16[5,8,128,128]{3,2,1,0:T(8,128)(2,1)}, bf16[5,8,128,128]{3,2,1,0:T(8,128)(2,1)S(1)}, u32[]{:S(2)}, u32[]{:S(2)}) collective-permute-start(bf16[5,8,128,128]{3,2,1,0:T(8,128)(2,1)} %bitcast.5), channel_id=1, source_target_pairs={{0,4},{1,0},{2,6},{3,2},{4,5},{5,1},{6,7},{7,3},{8,12},{9,8},{10,1... | collective-permute-start | bytes 3932168 | tf_op jit(solution)/shard_map/ppermute | solution.py:381
  2.8 1.0 %copy-start.2 = (bf16[1024,256]{1,0:T(8,128)(2,1)S(1)}, bf16[1024,256]{1,0:T(8,128)(2,1)}, u32[]{:S(2)}) copy-start(bf16[1024,256]{1,0:T(8,128)(2,1)} %x_ref.2) | copy-start | bytes 1572868
  3.9 12.9 %copy-start.5 = (s32[2,1,5,8]{3,1,2,0:T(1,128)S(1)}, s32[2,1,5,8]{3,1,2,0:T(1,128)}, u32[]{:S(2)}) copy-start(s32[2,1,5,8]{3,1,2,0:T(1,128)} %param.10) | copy-start | bytes 964
  4.0 6.8 %collective-permute-start.2 = (bf16[1024,128]{1,0:T(8,128)(2,1)S(1)}, bf16[1024,128]{1,0:T(8,128)(2,1)S(1)}, u32[]{:S(2)}, u32[]{:S(2)}) collective-permute-start(bf16[1024,128]{1,0:T(8,128)(2,1)S(1)} %get-tuple-element.29.refs_3_.refs_2_.refs_5_.refs_4_.refs_7_), channel_id=1, source_target_pairs={{0,8},{1,17},{2,10},{3,19},{5,13},{7,15},{8,0},{10,2},{12,28},{13,... | collective-permute-start | bytes 786440 | tf_op jit(solution)/shard_map/ppermute | solution.py:381
  4.7 8.9 %collective-permute-start.3 = (bf16[1024,128]{1,0:T(8,128)(2,1)S(1)}, bf16[1024,128]{1,0:T(8,128)(2,1)S(1)}, u32[]{:S(2)}, u32[]{:S(2)}) collective-permute-start(bf16[1024,128]{1,0:T(8,128)(2,1)S(1)} %get-tuple-element.26), channel_id=1, source_target_pairs={{0,12},{1,21},{2,14},{3,23},{5,9},{7,11},{8,4},{10,6},{12,24},{13,... | collective-permute-start | bytes 786440 | tf_op jit(solution)/shard_map/ppermute | solution.py:381
  6.0 7.6 %collective-permute-start = (bf16[1024,128]{1,0:T(8,128)(2,1)S(1)}, bf16[1024,128]{1,0:T(8,128)(2,1)S(1)}, u32[]{:S(2)}, u32[]{:S(2)}) collective-permute-start(bf16[1024,128]{1,0:T(8,128)(2,1)S(1)} %get-tuple-element.26), channel_id=1, source_target_pairs={{0,4},{1,5},{2,6},{3,7},{4,0},{5,1},{6,2},{7,3},{8,12},{9,13},{10,... | collective-permute-start | bytes 786440 | tf_op jit(solution)/shard_map/ppermute | solution.py:381
  13.6 10.4 %collective-permute-start.4 = (bf16[1024,128]{1,0:T(8,128)(2,1)S(1)}, bf16[1024,128]{1,0:T(8,128)(2,1)S(1)}, u32[]{:S(2)}, u32[]{:S(2)}) collective-permute-start(bf16[1024,128]{1,0:T(8,128)(2,1)S(1)} %get-tuple-element.30), channel_id=1, source_target_pairs={{0,16},{1,17},{2,18},{3,19},{4,20},{5,21},{6,22},{7,23},{8,24},{9,... | collective-permute-start | bytes 786440 | tf_op jit(solution)/shard_map/ppermute | solution.py:381
  15.5 8.5 %collective-permute-start.5 = (bf16[1024,128]{1,0:T(8,128)(2,1)S(1)}, bf16[1024,128]{1,0:T(8,128)(2,1)S(1)}, u32[]{:S(2)}, u32[]{:S(2)}) collective-permute-start(bf16[1024,128]{1,0:T(8,128)(2,1)S(1)} %get-tuple-element.31), channel_id=1, source_target_pairs={{0,8},{1,9},{2,10},{3,11},{4,12},{5,13},{6,14},{7,15},{8,0},{9,1},... | collective-permute-start | bytes 786440 | tf_op jit(solution)/shard_map/ppermute | solution.py:381
  18.1 10.8 %copy-start = (bf16[1,5,8,128,128]{4,3,2,1,0:T(8,128)(2,1)S(1)}, bf16[1,5,8,128,128]{4,3,2,1,0:T(8,128)(2,1)}, u32[]{:S(2)}) copy-start(bf16[1,5,8,128,128]{4,3,2,1,0:T(8,128)(2,1)} %param.9) | copy-start | bytes 3932164
  18.1 4.7 %collective-permute-start.6 = (s32[2,40]{1,0:T(2,128)S(1)}, s32[2,40]{1,0:T(2,128)S(1)}, u32[]{:S(2)}, u32[]{:S(2)}) collective-permute-start(s32[2,40]{1,0:T(2,128)S(1)} %slot_blocks.1.refs_0_.refs_1_), channel_id=1, source_target_pairs={{0,4},{1,0},{2,6},{3,2},{4,5},{5,1},{6,7},{7,3},{8,12},{9,8},{10,1... | collective-permute-start | bytes 968 | tf_op jit(solution)/shard_map/ppermute | solution.py:381
  18.4 5.6 %collective-permute-start.7 = (s32[2,40]{1,0:T(2,128)S(1)}, s32[2,40]{1,0:T(2,128)S(1)}, u32[]{:S(2)}, u32[]{:S(2)}) collective-permute-start(s32[2,40]{1,0:T(2,128)S(1)} %slot_blocks.1.refs_0_.refs_1_), channel_id=1, source_target_pairs={{1,4},{3,6},{4,1},{6,3},{9,12},{11,14},{12,9},{14,11},{17,20},{19,... | collective-permute-start | bytes 968 | tf_op jit(solution)/shard_map/ppermute | solution.py:381
  24.0 4.9 %collective-permute-start.8 = (bf16[5,8,128,128]{3,2,1,0:T(8,128)(2,1)S(1)}, bf16[5,8,128,128]{3,2,1,0:T(8,128)(2,1)S(1)}, u32[]{:S(2)}, u32[]{:S(2)}) collective-permute-start(bf16[5,8,128,128]{3,2,1,0:T(8,128)(2,1)S(1)} %collective-permute-done.1.refs_1_.refs_3_), channel_id=1, source_target_pairs={{0,4},{2,6},{5,1},{7,3},{8,12},{10,14},{13,9},{15,11},{16,20},{18,... | collective-permute-start | bytes 3932168 | tf_op jit(solution)/shard_map/ppermute | solution.py:381
  27.4 6.0 %copy-start.3 = (bf16[1024,256]{1,0:T(8,128)(2,1)S(1)}, bf16[1024,256]{1,0:T(8,128)(2,1)}, u32[]{:S(2)}) copy-start(bf16[1024,256]{1,0:T(8,128)(2,1)} %x_ref.3) | copy-start | bytes 1572868
  31.1 16.6 %copy-start.1 = (bf16[256,256]{1,0:T(8,128)(2,1)S(1)}, bf16[256,256]{1,0:T(8,128)(2,1)}, u32[]{:S(2)}) copy-start(bf16[256,256]{1,0:T(8,128)(2,1)} %w_ref.3) | copy-start | bytes 393220
  31.1 14.3 %collective-permute-start.9 = (bf16[1024,128]{1,0:T(8,128)(2,1)S(1)}, bf16[1024,128]{1,0:T(8,128)(2,1)S(1)}, u32[]{:S(2)}, u32[]{:S(2)}) collective-permute-start(bf16[1024,128]{1,0:T(8,128)(2,1)S(1)} %tile_product.5), channel_id=1, source_target_pairs={{0,2},{1,3},{2,0},{3,1},{4,6},{5,7},{6,4},{7,5},{8,10},{9,11},{10,... | collective-permute-start | bytes 786440 | tf_op jit(solution)/shard_map/ppermute | solution.py:381
  33.6 12.9 %collective-permute-start.11 = (bf16[1024,128]{1,0:T(8,128)(2,1)S(1)}, bf16[1024,128]{1,0:T(8,128)(2,1)S(1)}, u32[]{:S(2)}, u32[]{:S(2)}) collective-permute-start(bf16[1024,128]{1,0:T(8,128)(2,1)S(1)} %get-tuple-element.39), channel_id=1, source_target_pairs={{0,4},{1,5},{2,6},{3,7},{4,0},{5,1},{6,2},{7,3},{8,12},{9,13},{10,... | collective-permute-start | bytes 786440 | tf_op jit(solution)/shard_map/ppermute | solution.py:381
  45.5 2.2 %collective-permute-start.10 = (bf16[1024,128]{1,0:T(8,128)(2,1)S(1)}, bf16[1024,128]{1,0:T(8,128)(2,1)S(1)}, u32[]{:S(2)}, u32[]{:S(2)}) collective-permute-start(bf16[1024,128]{1,0:T(8,128)(2,1)S(1)} %add_convert_fusion.1.near_ref), channel_id=1, source_target_pairs={{0,4},{1,5},{2,6},{3,7},{4,0},{5,1},{6,2},{7,3},{8,12},{9,13},{10,... | collective-permute-start | bytes 786440 | tf_op jit(solution)/shard_map/ppermute | solution.py:381
  48.1 7.6 %collective-permute-start.12 = (bf16[1024,128]{1,0:T(8,128)(2,1)S(1)}, bf16[1024,128]{1,0:T(8,128)(2,1)S(1)}, u32[]{:S(2)}, u32[]{:S(2)}) collective-permute-start(bf16[1024,128]{1,0:T(8,128)(2,1)S(1)} %get-tuple-element.43.refs_6_.adj_ref), channel_id=1, source_target_pairs={{0,17},{1,0},{2,19},{3,2},{4,21},{5,4},{6,23},{7,6},{8,9},{9,24},{... | collective-permute-start | bytes 786440 | tf_op jit(solution)/shard_map/ppermute | solution.py:381
  48.8 7.2 %collective-permute-start.13 = (bf16[1024,128]{1,0:T(8,128)(2,1)S(1)}, bf16[1024,128]{1,0:T(8,128)(2,1)S(1)}, u32[]{:S(2)}, u32[]{:S(2)}) collective-permute-start(bf16[1024,128]{1,0:T(8,128)(2,1)S(1)} %get-tuple-element.43.refs_6_.adj_ref), channel_id=1, source_target_pairs={{0,8},{1,9},{2,10},{3,11},{4,12},{5,13},{6,14},{7,15},{8,0},{9,1},... | collective-permute-start | bytes 786440 | tf_op jit(solution)/shard_map/ppermute | solution.py:381
  56.0 8.4 %collective-permute-start.14 = (bf16[1024,128]{1,0:T(8,128)(2,1)S(1)}, bf16[1024,128]{1,0:T(8,128)(2,1)S(1)}, u32[]{:S(2)}, u32[]{:S(2)}) collective-permute-start(bf16[1024,128]{1,0:T(8,128)(2,1)S(1)} %get-tuple-element.43.refs_6_.adj_ref), channel_id=1, source_target_pairs={{0,1},{2,3},{4,5},{6,7},{9,8},{11,10},{13,12},{15,14},{16,17},{18,... | collective-permute-start | bytes 786440 | tf_op jit(solution)/shard_map/ppermute | solution.py:381
  58.9 6.2 %collective-permute-start.15 = (bf16[1024,128]{1,0:T(8,128)(2,1)S(1)}, bf16[1024,128]{1,0:T(8,128)(2,1)S(1)}, u32[]{:S(2)}, u32[]{:S(2)}) collective-permute-start(bf16[1024,128]{1,0:T(8,128)(2,1)S(1)} %collective-permute-done.13.refs_7_.after_ref), channel_id=1, source_target_pairs={{0,16},{1,17},{2,18},{3,19},{4,20},{5,21},{6,22},{7,23},{8,24},{9,... | collective-permute-start | bytes 786440 | tf_op jit(solution)/shard_map/ppermute | solution.py:381
  59.5 5.7 %collective-permute-start.16 = (bf16[1024,128]{1,0:T(8,128)(2,1)S(1)}, bf16[1024,128]{1,0:T(8,128)(2,1)S(1)}, u32[]{:S(2)}, u32[]{:S(2)}) collective-permute-start(bf16[1024,128]{1,0:T(8,128)(2,1)S(1)} %collective-permute-done.12.refs_6_), channel_id=1, source_target_pairs={{0,8},{1,9},{2,10},{3,11},{4,12},{5,13},{6,14},{7,15},{8,0},{9,1},... | collective-permute-start | bytes 786440 | tf_op jit(solution)/shard_map/ppermute | solution.py:381
  60.0 4.5 %collective-permute-start.17 = (bf16[256,128]{1,0:T(8,128)(2,1)S(1)}, bf16[256,128]{1,0:T(8,128)(2,1)S(1)}, u32[]{:S(2)}, u32[]{:S(2)}) collective-permute-start(bf16[256,128]{1,0:T(8,128)(2,1)S(1)} %grad_block.1.refs_0_), channel_id=1, source_target_pairs={{0,1},{1,0},{2,3},{3,2},{4,5},{5,4},{6,7},{7,6},{8,9},{9,8},{10,11... | collective-permute-start | bytes 196616 | tf_op jit(solution)/shard_map/ppermute | solution.py:381
  67.6 14.8 %collective-permute-start.20 = (bf16[1024,128]{1,0:T(8,128)(2,1)S(1)}, bf16[1024,128]{1,0:T(8,128)(2,1)S(1)}, u32[]{:S(2)}, u32[]{:S(2)}) collective-permute-start(bf16[1024,128]{1,0:T(8,128)(2,1)S(1)} %tile_product.7.refs_2_), channel_id=1, source_target_pairs={{0,2},{1,3},{2,0},{3,1},{4,6},{5,7},{6,4},{7,5},{8,10},{9,11},{10,... | collective-permute-start | bytes 786440 | tf_op jit(solution)/shard_map/ppermute | solution.py:381
  71.1 18.3 %collective-permute-start.18 = (bf16[1024,128]{1,0:T(8,128)(2,1)S(1)}, bf16[1024,128]{1,0:T(8,128)(2,1)S(1)}, u32[]{:S(2)}, u32[]{:S(2)}) collective-permute-start(bf16[1024,128]{1,0:T(8,128)(2,1)S(1)} %get-tuple-element.45), channel_id=1, source_target_pairs={{0,1},{1,5},{2,3},{3,7},{4,0},{5,4},{6,2},{7,6},{8,9},{9,13},{10,1... | collective-permute-start | bytes 786440 | tf_op jit(solution)/shard_map/ppermute | solution.py:381
  74.1 15.3 %collective-permute-start.19 = (bf16[1024,128]{1,0:T(8,128)(2,1)S(1)}, bf16[1024,128]{1,0:T(8,128)(2,1)S(1)}, u32[]{:S(2)}, u32[]{:S(2)}) collective-permute-start(bf16[1024,128]{1,0:T(8,128)(2,1)S(1)} %get-tuple-element.45), channel_id=1, source_target_pairs={{1,4},{3,6},{4,1},{6,3},{9,12},{11,14},{12,9},{14,11},{17,20},{19,... | collective-permute-start | bytes 786440 | tf_op jit(solution)/shard_map/ppermute | solution.py:381
  76.6 8.5 %collective-permute-start.23 = (bf16[256,128]{1,0:T(8,128)(2,1)S(1)}, bf16[256,128]{1,0:T(8,128)(2,1)S(1)}, u32[]{:S(2)}, u32[]{:S(2)}) collective-permute-start(bf16[256,128]{1,0:T(8,128)(2,1)S(1)} %add_after.2.refs_0_), channel_id=1, source_target_pairs={{0,8},{1,9},{2,10},{3,11},{4,12},{5,13},{6,14},{7,15},{8,0},{9,1},... | collective-permute-start | bytes 196616 | tf_op jit(solution)/shard_map/ppermute | solution.py:381
  77.1 8.9 %collective-permute-start.24 = (bf16[256,128]{1,0:T(8,128)(2,1)S(1)}, bf16[256,128]{1,0:T(8,128)(2,1)S(1)}, u32[]{:S(2)}, u32[]{:S(2)}) collective-permute-start(bf16[256,128]{1,0:T(8,128)(2,1)S(1)} %add_after.2.refs_0_), channel_id=1, source_target_pairs={{0,16},{1,17},{2,18},{3,19},{4,20},{5,21},{6,22},{7,23},{8,24},{9,... | collective-permute-start | bytes 196616 | tf_op jit(solution)/shard_map/ppermute | solution.py:381
  82.4 5.6 %collective-permute-start.25 = (bf16[256,128]{1,0:T(8,128)(2,1)S(1)}, bf16[256,128]{1,0:T(8,128)(2,1)S(1)}, u32[]{:S(2)}, u32[]{:S(2)}) collective-permute-start(bf16[256,128]{1,0:T(8,128)(2,1)S(1)} %add_after.2.refs_0_), channel_id=1, source_target_pairs={{0,24},{1,25},{2,26},{3,27},{4,28},{5,29},{6,30},{7,31},{8,16},{9,... | collective-permute-start | bytes 196616 | tf_op jit(solution)/shard_map/ppermute | solution.py:381
  85.2 5.3 %collective-permute-start.21 = (bf16[1024,128]{1,0:T(8,128)(2,1)S(1)}, bf16[1024,128]{1,0:T(8,128)(2,1)S(1)}, u32[]{:S(2)}, u32[]{:S(2)}) collective-permute-start(bf16[1024,128]{1,0:T(8,128)(2,1)S(1)} %add_convert_fusion.refs_4_.own_ref), channel_id=1, source_target_pairs={{0,1},{1,5},{2,3},{3,7},{4,0},{5,4},{6,2},{7,6},{8,9},{9,13},{10,1... | collective-permute-start | bytes 786440 | tf_op jit(solution)/shard_map/ppermute | solution.py:381
  86.1 7.7 %collective-permute-start.22 = (bf16[1024,128]{1,0:T(8,128)(2,1)S(1)}, bf16[1024,128]{1,0:T(8,128)(2,1)S(1)}, u32[]{:S(2)}, u32[]{:S(2)}) collective-permute-start(bf16[1024,128]{1,0:T(8,128)(2,1)S(1)} %add_convert_fusion.refs_4_.own_ref), channel_id=1, source_target_pairs={{1,4},{3,6},{4,1},{6,3},{9,12},{11,14},{12,9},{14,11},{17,20},{19,... | collective-permute-start | bytes 786440 | tf_op jit(solution)/shard_map/ppermute | solution.py:381
  88.0 2.3 %collective-permute-start.26 = (f32[256,128]{1,0:T(8,128)S(1)}, f32[256,128]{1,0:T(8,128)S(1)}, u32[]{:S(2)}, u32[]{:S(2)}) collective-permute-start(f32[256,128]{1,0:T(8,128)S(1)} %add_after.3.grad_ref), channel_id=1, source_target_pairs={{0,4},{1,5},{2,6},{3,7},{4,0},{5,1},{6,2},{7,3},{8,12},{9,13},{10,... | collective-permute-start | bytes 393224 | tf_op jit(solution)/shard_map/ppermute | solution.py:381

commit v7 on v6

--- a/solution.py
+++ b/solution.py
@@ -8,7 +8,7 @@
 from jax.sharding import PartitionSpec as P
 
 AXES = ("rows", "rep")
-TOGETHER = 4
+WEIGH = 200
 
 
 def route(shape, move):
@@ -150,102 +150,74 @@
     }[kind]
 
 
+def chosen(choice, read):
+    value = read(choice[0][1])
+    for case, ref in choice[1:]:
+        value = jnp.where(when_of(case), read(ref), value)
+    return value
+
+
 def tile_kernel(kinds, cases, sets, summed, waits, *refs):
     refs = list(refs)
-    metas = [refs.pop(0) for _ in range(sum(sets))]
-    tiles = [refs.pop(0) for _ in range(sum(sets))]
+    metas = [[(case, refs.pop(0)) for case in each] for each in sets]
+    tiles = [[(case, refs.pop(0)) for case in each] for each in sets]
     panels = [[(case, refs.pop(0)) for case in each] for each in cases]
     before = refs.pop(0) if summed else None
-    out_ref, acc_ref, tile_buf, panel_buf, tile_sems, panel_sems = refs[waits:]
-    slots, tile = tile_buf.shape[2], tile_buf.shape[-1]
+    out_ref, acc_ref = refs[waits:]
+    _, slots, tile, _ = tiles[0][0][1].shape
     rows = out_ref.shape[0]
-    j, _, p = place()
-    home = j == p
-    offsets = [offset_of(kind) for kind in kinds]
-
-    def tile_copy(ref, i, s):
-        return pltpu.make_async_copy(ref.at[offsets[i]], tile_buf.at[i, s], tile_sems.at[i, s])
-
-    def panel_copy(i):
-        return lambda ref: pltpu.make_async_copy(ref, panel_buf.at[i], panel_sems.at[i])
-
-    for i in range(len(kinds)):
-        start_chosen(panels[i], panel_copy(i))
-        at = 0
-        for s, members in enumerate(sets):
-            cases_of_set = ["home", "away"] if members == 2 else [None]
-            start_chosen(
-                list(zip(cases_of_set, tiles[at : at + members])),
-                lambda ref, i=i, s=s: tile_copy(ref, i, s),
-            )
-            at += members
     if summed:
         acc_ref[:rows, :] = before[...]
     else:
         acc_ref[...] = jnp.zeros_like(acc_ref)
-    for i in range(len(kinds)):
-        d = offsets[i]
-        panel_copy(i)(panels[i][0][1]).wait()
-        at = 0
-        for s, members in enumerate(sets):
-            tile_copy(tiles[at], i, s).wait()
-            for first in range(0, slots, TOGETHER):
-                prods = []
-                for k in range(first, min(first + TOGETHER, slots)):
-                    row = metas[at][0, d * slots + k]
-                    col = metas[at][1, d * slots + k]
-                    if members == 2:
-                        row = jnp.where(home, row, metas[at + 1][0, d * slots + k])
-                        col = jnp.where(home, col, metas[at + 1][1, d * slots + k])
-                    col = pl.multiple_of(col * tile, tile)
-                    prod = jnp.dot(
-                        tile_buf[i, s, k],
-                        panel_buf[i, pl.ds(col, tile), :],
-                        preferred_element_type=jnp.float32,
-                    )
-                    prods.append((pl.multiple_of(row * tile, tile), prod))
-                for row, prod in prods:
-                    acc_ref[pl.ds(row, tile), :] += prod
-            at += members
+    for i, kind in enumerate(kinds):
+        d = offset_of(kind)
+        for s in range(len(sets)):
+            for k in range(slots):
+                row = chosen(metas[s], lambda ref: ref[0, d * slots + k])
+                col = chosen(metas[s], lambda ref: ref[1, d * slots + k])
+                row = pl.multiple_of(row * tile, tile)
+                col = pl.multiple_of(col * tile, tile)
+                acc_ref[pl.ds(row, tile), :] += jnp.dot(
+                    chosen(tiles[s], lambda ref: ref[d, k]),
+                    chosen(panels[i], lambda ref: ref[pl.ds(col, tile), :]),
+                    preferred_element_type=jnp.float32,
+                )
     out_ref[...] = acc_ref[:rows, :].astype(out_ref.dtype)
 
 
-def tile_product(named, sets, dtype, before=None, after=()):
+def tile_product(named, sets, dtype, before=None, after=(), weigh=1):
     kinds = [kind for kind, _ in named]
     cases = [[case for case, _ in choice] for _, choice in named]
     panels = [panel for _, choice in named for _, panel in choice]
-    metas = [meta for members in sets for meta, _ in members]
-    tiles = [values for members in sets for _, values in members]
+    metas = [meta for choice in sets for _, (meta, _) in choice]
+    tiles = [values for choice in sets for _, (_, values) in choice]
     rows, width = panels[0].shape
     _, slots, tile, _ = tiles[0].shape
     smem = pl.BlockSpec(memory_space=pltpu.SMEM)
     vmem = pl.BlockSpec(memory_space=pltpu.VMEM)
-    hbm = pl.BlockSpec(memory_space=pltpu.HBM)
     anywhere = pl.BlockSpec(memory_space=pl.ANY)
     count = len(kinds) * len(sets) * slots
     summed = before is not None
     return pl.pallas_call(
         functools.partial(
-            tile_kernel, kinds, cases, [len(m) for m in sets], summed, len(after)
+            tile_kernel,
+            kinds,
+            cases,
+            [[case for case, _ in choice] for choice in sets],
+            summed,
+            len(after),
         ),
         out_shape=jax.ShapeDtypeStruct((rows, width), dtype),
         in_specs=[smem] * len(metas)
-        + [hbm] * len(tiles)
-        + [anywhere] * len(panels)
-        + [vmem] * summed
+        + [vmem] * (len(tiles) + len(panels) + summed)
         + [anywhere] * len(after),
         out_specs=vmem,
-        scratch_shapes=[
-            pltpu.VMEM((rows + tile, width), jnp.float32),
-            pltpu.VMEM((len(kinds), len(sets), slots, tile, tile), tiles[0].dtype),
-            pltpu.VMEM((len(kinds), rows, width), panels[0].dtype),
-            pltpu.SemaphoreType.DMA((len(kinds), len(sets))),
-            pltpu.SemaphoreType.DMA((len(kinds),)),
-        ],
-        compiler_params=pltpu.CompilerParams(vmem_limit_bytes=8 * 1024 * 1024),
+        scratch_shapes=[pltpu.VMEM((rows + tile, width), jnp.float32)],
+        compiler_params=pltpu.CompilerParams(vmem_limit_bytes=12 * 1024 * 1024),
         cost_estimate=pl.CostEstimate(
-            flops=2 * count * tile * tile * width,
-            bytes_accessed=count * tile * tile * 2 + len(kinds) * rows * width * 2,
+            flops=weigh * 2 * count * tile * tile * width,
+            bytes_accessed=weigh * (count * tile * tile * 2 + len(kinds) * rows * width * 2),
             transcendentals=0,
         ),
         name="tile_product",
@@ -334,39 +306,45 @@
     )(*values, *after)
 
 
-def final_kernel(own_ref, one_ref, two_ref, w_ref, grad_ref, rest_ref, out_ref, grad_out_ref):
+def final_kernel(*refs):
+    back, act, (w_ref, grad_ref, rest_ref), outs = refs[:3], refs[3:6], refs[6:9], refs[9:]
+    out_ref, act_ref, grad_out_ref = outs
     j, _, p = place()
-    half = own_ref.shape[1]
+    half = back[0].shape[1]
     near_cols = pl.ds(pl.multiple_of(j * half, half), half)
     far_cols = pl.ds(pl.multiple_of((1 - j) * half, half), half)
-    grad_out_ref[:, near_cols] = grad_ref[...]
-    grad_out_ref[:, far_cols] = rest_ref[...]
-    near = jnp.where(j == p, own_ref[...], one_ref[...])
-    far = jnp.where(j == p, one_ref[...], two_ref[...])
+
+    def halves_of(parts):
+        own, one, two = parts
+        near = jnp.where(j == p, own[...], one[...])
+        return near, jnp.where(j == p, one[...], two[...])
+
+    near, far = halves_of(back)
     dims = (((1,), (1,)), ((), ()))
     total = lax.dot_general(near, w_ref[:, near_cols], dims, preferred_element_type=jnp.float32)
     total += lax.dot_general(far, w_ref[:, far_cols], dims, preferred_element_type=jnp.float32)
     out_ref[...] = total.astype(out_ref.dtype)
-
-
-def final(own, one, two, weight, grad, rest):
+    act_ref[:, near_cols], act_ref[:, far_cols] = halves_of(act)
+    grad_out_ref[:, near_cols] = grad_ref[...]
+    grad_out_ref[:, far_cols] = rest_ref[...]
+
+
+def final(back, act, weight, grad, rest):
     vmem = pl.BlockSpec(memory_space=pltpu.VMEM)
-    rows = own.shape[0]
+    rows = back[0].shape[0]
     wide = weight.shape[0]
+    whole = jax.ShapeDtypeStruct((rows, wide), jnp.bfloat16)
     return pl.pallas_call(
         final_kernel,
-        out_shape=(
-            jax.ShapeDtypeStruct((rows, wide), jnp.bfloat16),
-            jax.ShapeDtypeStruct(weight.shape, jnp.float32),
-        ),
-        in_specs=[vmem] * 6,
-        out_specs=(vmem, vmem),
+        out_shape=(whole, whole, jax.ShapeDtypeStruct(weight.shape, jnp.float32)),
+        in_specs=[vmem] * 9,
+        out_specs=(vmem,) * 3,
         compiler_params=pltpu.CompilerParams(vmem_limit_bytes=8 * 1024 * 1024),
         cost_estimate=pl.CostEstimate(
             flops=2 * rows * wide * wide, bytes_accessed=8 * rows * wide, transcendentals=0
         ),
         name="final",
-    )(own, one, two, weight, grad, rest)
+    )(*back, *act, weight, grad, rest)
 
 
 def per_device(node_feats, weight, cotangent, tile_values, tile_coords, tile_counts):
@@ -434,13 +412,11 @@
     meta = slot_blocks(coords[:, 0], counts[0], blocks)
     meta_b = send(meta, to_home)
     meta_far = send(meta, lambda c, j, z: None if j == z % 2 else (c, 1 - j, z ^ 1))
-    first, second, far, meta_b, meta_far = lax.optimization_barrier(
-        (first, second, far, meta_b, meta_far)
-    )
+    first, one, two = lax.optimization_barrier((first, one, two))
     other_first = send(first, lambda c, j, z: (c, 1 - j, z) if j == z % 2 else None)
 
-    set_first = [(meta_b, first)]
-    set_rest = [(meta, own), (meta_far, other_first)]
+    set_first = [(None, (meta_b, first))]
+    set_rest = [("home", (meta, own)), ("away", (meta_far, other_first))]
     panels = [
         ("self", [("home", mine), ("away", swapped)]),
         ("near", [("home", swapped), ("away", mine)]),
@@ -448,7 +424,7 @@
         ("second", [(None, second)]),
         ("far", [(None, far)]),
     ]
-    part = tile_product(panels, [set_first], jnp.float32)
+    part = tile_product(panels, [set_first], jnp.float32, weigh=WEIGH)
     part = tile_product(panels, [set_rest], jnp.bfloat16, part)
 
     def join(value):
@@ -466,6 +442,8 @@
     )
     adj_later, near_one, direct = lax.optimization_barrier((adj, near_one, direct))
     second = send(direct if four else adj_later, to_second)
+    grad = grad_block(scale, near, far_half, adj, direct)
+    adj_later, grad = lax.optimization_barrier((adj_later, grad))
     far = send(near_one, to_far)
     near_choice = [("still", near_one)]
     if four:
@@ -473,7 +451,6 @@
             adj_later, lambda c, j, z: None if (c + z) % 2 else (c, j, z ^ 1)
         )
         near_choice.append(("relay", near_two))
-    grad = grad_block(scale, near, far_half, adj, direct)
     grad_got = send(grad, lambda c, j, z: (c, j, z ^ 1))
     panels = [("self", [(None, adj)]), ("direct", [(None, direct)])]
     back_part = tile_product(panels, [set_first, set_rest], jnp.float32)
@@ -487,26 +464,21 @@
         two = send(value, lambda c, j, z: None if j == z % 2 else (c, 1 - j, z ^ 1))
         return one, two
 
-    act, back_part = lax.optimization_barrier((act, back_part))
-    act_one, act_two = deliver(act)
-    act_near = jnp.where(home, act, act_one)
-    act_far = jnp.where(home, act_one, act_two)
-    activated = jnp.concatenate(
-        [jnp.where(j == 0, act_near, act_far), jnp.where(j == 0, act_far, act_near)], axis=1
-    )
-
-    back = join(back_part)
-    back_one, back_two = deliver(back)
-
+    act_later, back_part = lax.optimization_barrier((act, back_part))
+    act_parts = [act, *deliver(act_later)]
     grad = add_after([grad, grad_got], jnp.bfloat16, back_part)
     step = 1
     while step < shape[0]:
-        flips = [step] if step * 2 >= shape[0] else [step, 2 * step, 3 * step]
-        got = [send(grad, lambda c, j, z, s=s: (c ^ s, j, z)) for s in flips]
-        step *= 2 if len(flips) == 1 else 4
-        grad = add_after([grad, *got], jnp.bfloat16 if step < shape[0] else jnp.float32, back)
-    grad_rest = send(grad, sibling)
-    input_grad, weight_grad = final(back, back_one, back_two, weight, grad, grad_rest)
+        got = send(grad, lambda c, j, z, s=step: (c ^ s, j, z))
+        step *= 2
+        if step < shape[0]:
+            grad = add_after([grad, got], jnp.bfloat16)
+    back = add_after([back_part, send(back_part, across)], jnp.bfloat16, got)
+    back_parts = [back, *deliver(back)]
+    grad = add_after([grad, got], jnp.float32, back)
+    input_grad, activated, weight_grad = final(
+        back_parts, act_parts, weight, grad, send(grad, sibling)
+    )
     return (activated, input_grad, weight_grad)
 
 

time: 95.3 us -> 91.4 us (0.959)
  Pallas kernels: 12.1 us -> 9.28 us
  starting transfers between devices: 45.5 us -> 42.7 us
  waiting for transfers between devices: 34.4 us -> 36.7 us
  other arithmetic: 1.04 us -> 0.07 us
    pallas_call x5, Pallas kernels: 9.65 us -> 6.77 us  [the longest x4 5.24 us: tile_product(): pl.pallas_call(functools.partial(tile_kernel, kinds, cases, [[case for ca...]
    ppermute x27 -> x26, starting transfers between devices: 45.5 us -> 42.7 us  [send(): return lax.ppermute(value, AXES, route(shape, move))]
    ppermute x27 -> x26, waiting for transfers between devices: 34.4 us -> 36.7 us  [send(): return lax.ppermute(value, AXES, route(shape, move))]
  transfers between devices with their start and end apart: 27 -> 26, of which waited for: 14 -> 12; matrix products, arithmetic and copies ran while one was open for 1% -> 0% of each run, Pallas kernels for 6% -> 5%
where the time goes in v7:
time: 91.4 us; the launch traced here: 90.8 us
  starting transfers between devices  42.7 us (47%)
  waiting for transfers between devices  36.7 us (40%)
  Pallas kernels  9.28 us (10%)
  local copies, waits for them, and re-layouts  1.08 us (1%)
  between operations  0.93 us (1%)
    ppermute x26, starting transfers between devices, send(): return lax.ppermute(value, AXES, route(shape, move))  42.7 us
    ppermute x26, waiting for transfers between devices, send(): return lax.ppermute(value, AXES, route(shape, move))  36.7 us
    pallas_call x4, Pallas kernels, tile_product(): pl.pallas_call(functools.partial(tile_kernel, kinds, cases, [[case for ca...  5.24 us
  transfers between devices with their start and end apart: 26, of which 12 were waited for; matrix products, arithmetic and copies ran while one was open for 0% of the time, Pallas kernels for 5%

profile of v7, /device:TPU:1, one launch (start us, length us, event | category | flops | bytes accessed | tf_op | source)
XLA Modules:
  0.0 90.8 jit_solution(2024589025508926996)
XLA Ops:
  0.6 2.2 %collective-permute-start.2 = (bf16[5,8,128,128]{3,2,1,0:T(8,128)(2,1)}, bf16[5,8,128,128]{3,2,1,0:T(8,128)(2,1)S(1)}, u32[]{:S(2)}, u32[]{:S(2)}) collective-permute-start(bf16[5,8,128,128]{3,2,1,0:T(8,128)(2,1)} %bitcast.5), channel_id=1, source_target_pairs={{0,4},{1,0},{2,6},{3,2},{4,5},{5,1},{6,7},{7,3},{8,12},{9,8},{10,1... | collective-permute-start | bytes 3932168 | tf_op jit(solution)/shard_map/ppermute | solution.py:359
  2.8 1.0 %copy-done.1 = bf16[1024,256]{1,0:T(8,128)(2,1)S(1)} copy-done((bf16[1024,256]{1,0:T(8,128)(2,1)S(1)}, bf16[1024,256]{1,0:T(8,128)(2,1)}, u32[]{:S(2)}) %copy-start.1) | copy-done | bytes 524312
  3.9 0.1 halves.2
  4.0 0.7 collective-permute-start.3
  4.7 1.3 %collective-permute-start.4 = (bf16[1024,128]{1,0:T(8,128)(2,1)S(1)}, bf16[1024,128]{1,0:T(8,128)(2,1)S(1)}, u32[]{:S(2)}, u32[]{:S(2)}) collective-permute-start(bf16[1024,128]{1,0:T(8,128)(2,1)S(1)} %get-tuple-element.25), channel_id=1, source_target_pairs={{0,12},{1,21},{2,14},{3,23},{5,9},{7,11},{8,4},{10,6},{12,24},{13,... | collective-permute-start | bytes 786440 | tf_op jit(solution)/shard_map/ppermute | solution.py:359
  6.0 4.8 %collective-permute-start = (bf16[1024,128]{1,0:T(8,128)(2,1)S(1)}, bf16[1024,128]{1,0:T(8,128)(2,1)S(1)}, u32[]{:S(2)}, u32[]{:S(2)}) collective-permute-start(bf16[1024,128]{1,0:T(8,128)(2,1)S(1)} %get-tuple-element.25), channel_id=1, source_target_pairs={{0,4},{1,5},{2,6},{3,7},{4,0},{5,1},{6,2},{7,3},{8,12},{9,13},{10,... | collective-permute-start | bytes 786440 | tf_op jit(solution)/shard_map/ppermute | solution.py:359
  10.8 2.8 %collective-permute-done.4.refs_1_.refs_4_.refs_7_.refs_9_ = bf16[1024,128]{1,0:T(8,128)(2,1)S(1)} collective-permute-done((bf16[1024,128]{1,0:T(8,128)(2,1)S(1)}, bf16[1024,128]{1,0:T(8,128)(2,1)S(1)}, u32[]{:S(2)}, u32[]{:S(2)}) %collective-permute-start.4) | collective-permute-done | bytes 262176 | tf_op jit(solution)/shard_map/ppermute | solution.py:359
  13.5 0.1 pick.1
  13.6 1.8 %collective-permute-start.6 = (bf16[1024,128]{1,0:T(8,128)(2,1)S(1)}, bf16[1024,128]{1,0:T(8,128)(2,1)S(1)}, u32[]{:S(2)}, u32[]{:S(2)}) collective-permute-start(bf16[1024,128]{1,0:T(8,128)(2,1)S(1)} %get-tuple-element.31), channel_id=1, source_target_pairs={{0,16},{1,17},{2,18},{3,19},{4,20},{5,21},{6,22},{7,23},{8,24},{9,... | collective-permute-start | bytes 786440 | tf_op jit(solution)/shard_map/ppermute | solution.py:359
  15.5 1.3 %collective-permute-start.7 = (bf16[1024,128]{1,0:T(8,128)(2,1)S(1)}, bf16[1024,128]{1,0:T(8,128)(2,1)S(1)}, u32[]{:S(2)}, u32[]{:S(2)}) collective-permute-start(bf16[1024,128]{1,0:T(8,128)(2,1)S(1)} %get-tuple-element.32), channel_id=1, source_target_pairs={{0,8},{1,9},{2,10},{3,11},{4,12},{5,13},{6,14},{7,15},{8,0},{9,1},... | collective-permute-start | bytes 786440 | tf_op jit(solution)/shard_map/ppermute | solution.py:359
  16.8 1.3 %slot_blocks.1.refs_0_.refs_1_ = s32[2,40]{1,0:T(2,128)S(1)} custom-call(s32[2,5,8]{2,1,0:T(8,128)S(1)} %copy.10.coords_ref, s32[5]{0:T(128)S(1)} %bitcast.9), custom_call_target="tpu_custom_call" | custom-call | tf_op jit(solution)/shard_map/slot_blocks/pallas_call | solution.py:131
  18.1 0.2 collective-permute-start.8
  18.4 4.4 %collective-permute-start.1 = (s32[2,40]{1,0:T(2,128)S(1)}, s32[2,40]{1,0:T(2,128)S(1)}, u32[]{:S(2)}, u32[]{:S(2)}) collective-permute-start(s32[2,40]{1,0:T(2,128)S(1)} %slot_blocks.1.refs_0_.refs_1_), channel_id=1, source_target_pairs={{1,4},{3,6},{4,1},{6,3},{9,12},{11,14},{12,9},{14,11},{17,20},{19,... | collective-permute-start | bytes 968 | tf_op jit(solution)/shard_map/ppermute | solution.py:359
  22.8 1.3 %collective-permute-start.5 = (bf16[5,8,128,128]{3,2,1,0:T(8,128)(2,1)S(1)}, bf16[5,8,128,128]{3,2,1,0:T(8,128)(2,1)S(1)}, u32[]{:S(2)}, u32[]{:S(2)}) collective-permute-start(bf16[5,8,128,128]{3,2,1,0:T(8,128)(2,1)S(1)} %collective-permute-done.2.refs_1_.refs_3_), channel_id=1, source_target_pairs={{0,4},{2,6},{5,1},{7,3},{8,12},{10,14},{13,9},{15,11},{16,20},{18,... | collective-permute-start | bytes 3932168 | tf_op jit(solution)/shard_map/ppermute | solution.py:359
  24.1 1.2 %tile_product.4.refs_12_ = f32[1024,128]{1,0:T(8,128)S(1)} custom-call(s32[2,40]{1,0:T(2,128)S(1)} %collective-permute-done.8.refs_0_, bf16[5,8,128,128]{3,2,1,0:T(8,128)(2,1)S(1)} %collective-permute-done.2.refs_1_.refs_3_, bf16[1024,128]{1,0:T(8,128)(2,1)S(1)} %get-tuple-element.28.refs_3_.refs_2_.refs_5_.refs_4_.refs_7_, ...), custom_call_target="tpu_custom_call" | custom-call | flops 33554432000 | bytes 524288000 | tf_op jit(solution)/shard_map/tile_product/pallas_call | solution.py:202
  25.4 2.3 %collective-permute-done.5.refs_3_.refs_5_ = bf16[5,8,128,128]{3,2,1,0:T(8,128)(2,1)S(1)} collective-permute-done((bf16[5,8,128,128]{3,2,1,0:T(8,128)(2,1)S(1)}, bf16[5,8,128,128]{3,2,1,0:T(8,128)(2,1)S(1)}, u32[]{:S(2)}, u32[]{:S(2)}) %collective-permute-start.5) | collective-permute-done | bytes 1310752 | tf_op jit(solution)/shard_map/ppermute | solution.py:359
  27.7 1.4 %tile_product.5 = bf16[1024,128]{1,0:T(8,128)(2,1)S(1)} custom-call(s32[2,40]{1,0:T(2,128)S(1)} %slot_blocks.1.refs_0_.refs_1_, s32[2,40]{1,0:T(2,128)S(1)} %collective-permute-done.1.refs_1_.refs_2_, bf16[5,8,128,128]{3,2,1,0:T(8,128)(2,1)S(1)} %bitcast.6, bf16[5,8,128,128]{3,2,1,0:T(8,128)(2,1)S(1)} %collective-permute-done.5.refs_3_.refs_5_, ...), custom_call_target="tpu_custom_call" | custom-call | flops 167772160 | bytes 2621440 | tf_op jit(solution)/shard_map/tile_product/pallas_call | solution.py:202
  29.1 2.4 %collective-permute-start.9 = (bf16[1024,128]{1,0:T(8,128)(2,1)S(1)}, bf16[1024,128]{1,0:T(8,128)(2,1)S(1)}, u32[]{:S(2)}, u32[]{:S(2)}) collective-permute-start(bf16[1024,128]{1,0:T(8,128)(2,1)S(1)} %tile_product.5), channel_id=1, source_target_pairs={{0,2},{1,3},{2,0},{3,1},{4,6},{5,7},{6,4},{7,5},{8,10},{9,11},{10,... | collective-permute-start | bytes 786440 | tf_op jit(solution)/shard_map/ppermute | solution.py:359
  31.5 0.1 halves.3
  31.6 0.5 collective-permute-start.11
  32.1 11.3 %collective-permute-done.9 = bf16[1024,128]{1,0:T(8,128)(2,1)S(1)} collective-permute-done((bf16[1024,128]{1,0:T(8,128)(2,1)S(1)}, bf16[1024,128]{1,0:T(8,128)(2,1)S(1)}, u32[]{:S(2)}, u32[]{:S(2)}) %collective-permute-start.9) | collective-permute-done | bytes 262176 | tf_op jit(solution)/shard_map/ppermute | solution.py:359
  43.5 0.1 add_convert_fusion.near_ref
  43.5 0.5 collective-permute-start.10
  44.1 1.2 %collective-permute-done.10.far_ref = bf16[1024,128]{1,0:T(8,128)(2,1)S(1)} collective-permute-done((bf16[1024,128]{1,0:T(8,128)(2,1)S(1)}, bf16[1024,128]{1,0:T(8,128)(2,1)S(1)}, u32[]{:S(2)}, u32[]{:S(2)}) %collective-permute-start.10) | collective-permute-done | bytes 262176 | tf_op jit(solution)/shard_map/ppermute | solution.py:359
  45.2 0.4 middle.1
  45.7 0.3 collective-permute-start.13
  46.0 7.2 %collective-permute-done.12.refs_6_ = bf16[1024,128]{1,0:T(8,128)(2,1)S(1)} collective-permute-done((bf16[1024,128]{1,0:T(8,128)(2,1)S(1)}, bf16[1024,128]{1,0:T(8,128)(2,1)S(1)}, u32[]{:S(2)}, u32[]{:S(2)}) %collective-permute-start.12) | collective-permute-done | bytes 262176 | tf_op jit(solution)/shard_map/ppermute | solution.py:359
  53.2 0.1 collective-permute-done.13.after_ref.refs_7_
  53.2 0.4 collective-permute-start.15
  53.6 0.4 grad_block.1.refs_0_
  54.0 3.1 %collective-permute-start.14 = (bf16[1024,128]{1,0:T(8,128)(2,1)S(1)}, bf16[1024,128]{1,0:T(8,128)(2,1)S(1)}, u32[]{:S(2)}, u32[]{:S(2)}) collective-permute-start(bf16[1024,128]{1,0:T(8,128)(2,1)S(1)} %get-tuple-element.40.adj_ref.refs_6_), channel_id=1, source_target_pairs={{0,1},{2,3},{4,5},{6,7},{9,8},{11,10},{13,12},{15,14},{16,17},{18,... | collective-permute-start | bytes 786440 | tf_op jit(solution)/shard_map/ppermute | solution.py:359
  57.1 1.8 %collective-permute-start.17 = (bf16[256,128]{1,0:T(8,128)(2,1)S(1)}, bf16[256,128]{1,0:T(8,128)(2,1)S(1)}, u32[]{:S(2)}, u32[]{:S(2)}) collective-permute-start(bf16[256,128]{1,0:T(8,128)(2,1)S(1)} %grad_block.1.refs_0_), channel_id=1, source_target_pairs={{0,1},{1,0},{2,3},{3,2},{4,5},{5,4},{6,7},{7,6},{8,9},{9,8},{10,11... | collective-permute-start | bytes 196616 | tf_op jit(solution)/shard_map/ppermute | solution.py:359
  59.0 1.2 %tile_product.6.refs_10_ = f32[1024,128]{1,0:T(8,128)S(1)} custom-call(s32[2,40]{1,0:T(2,128)S(1)} %collective-permute-done.8.refs_0_, s32[2,40]{1,0:T(2,128)S(1)} %slot_blocks.1.refs_0_.refs_1_, s32[2,40]{1,0:T(2,128)S(1)} %collective-permute-done.1.refs_1_.refs_2_, bf16[5,8,128,128]{3,2,1,0:T(8,128)(2,1)S(1)} %collective-permute-done.2.refs_1_.refs_3_, ...), custom_call_target="tpu_custom_call" | custom-call | flops 134217728 | bytes 1572864 | tf_op jit(solution)/shard_map/tile_product/pallas_call | solution.py:202
  60.1 2.1 %collective-permute-done.17.refs_11_.refs_1_ = bf16[256,128]{1,0:T(8,128)(2,1)S(1)} collective-permute-done((bf16[256,128]{1,0:T(8,128)(2,1)S(1)}, bf16[256,128]{1,0:T(8,128)(2,1)S(1)}, u32[]{:S(2)}, u32[]{:S(2)}) %collective-permute-start.17) | collective-permute-done | bytes 65568 | tf_op jit(solution)/shard_map/ppermute | solution.py:359
  62.2 0.6 collective-permute-done.16.refs_9_
  62.8 1.4 %tile_product.7.refs_2_.refs_0_ = bf16[1024,128]{1,0:T(8,128)(2,1)S(1)} custom-call(s32[2,40]{1,0:T(2,128)S(1)} %collective-permute-done.8.refs_0_, s32[2,40]{1,0:T(2,128)S(1)} %slot_blocks.1.refs_0_.refs_1_, s32[2,40]{1,0:T(2,128)S(1)} %collective-permute-done.1.refs_1_.refs_2_, bf16[5,8,128,128]{3,2,1,0:T(8,128)(2,1)S(1)} %collective-permute-done.2.refs_1_.refs_3_, ...), custom_call_target="tpu_custom_call" | custom-call | flops 201326592 | bytes 2359296 | tf_op jit(solution)/shard_map/tile_product/pallas_call | solution.py:202
  64.3 2.7 %collective-permute-start.18 = (bf16[1024,128]{1,0:T(8,128)(2,1)S(1)}, bf16[1024,128]{1,0:T(8,128)(2,1)S(1)}, u32[]{:S(2)}, u32[]{:S(2)}) collective-permute-start(bf16[1024,128]{1,0:T(8,128)(2,1)S(1)} %tile_product.7.refs_2_.refs_0_), channel_id=1, source_target_pairs={{0,2},{1,3},{2,0},{3,1},{4,6},{5,7},{6,4},{7,5},{8,10},{9,11},{10,... | collective-permute-start | bytes 786440 | tf_op jit(solution)/shard_map/ppermute | solution.py:359
  67.0 0.9 collective-permute-start.19
  67.9 2.3 %collective-permute-done.19.refs_1_ = bf16[256,128]{1,0:T(8,128)(2,1)S(1)} collective-permute-done((bf16[256,128]{1,0:T(8,128)(2,1)S(1)}, bf16[256,128]{1,0:T(8,128)(2,1)S(1)}, u32[]{:S(2)}, u32[]{:S(2)}) %collective-permute-start.19) | collective-permute-done | bytes 65568 | tf_op jit(solution)/shard_map/ppermute | solution.py:359
  70.2 1.1 %collective-permute-start.20 = (bf16[256,128]{1,0:T(8,128)(2,1)S(1)}, bf16[256,128]{1,0:T(8,128)(2,1)S(1)}, u32[]{:S(2)}, u32[]{:S(2)}) collective-permute-start(bf16[256,128]{1,0:T(8,128)(2,1)S(1)} %add_after.5.refs_0_), channel_id=1, source_target_pairs={{0,16},{1,17},{2,18},{3,19},{4,20},{5,21},{6,22},{7,23},{8,24},{9,... | collective-permute-start | bytes 196616 | tf_op jit(solution)/shard_map/ppermute | solution.py:359
  71.3 4.4 %collective-permute-start.23 = (bf16[1024,128]{1,0:T(8,128)(2,1)S(1)}, bf16[1024,128]{1,0:T(8,128)(2,1)S(1)}, u32[]{:S(2)}, u32[]{:S(2)}) collective-permute-start(bf16[1024,128]{1,0:T(8,128)(2,1)S(1)} %get-tuple-element.43.refs_3_), channel_id=1, source_target_pairs={{0,1},{1,5},{2,3},{3,7},{4,0},{5,4},{6,2},{7,6},{8,9},{9,13},{10,1... | collective-permute-start | bytes 786440 | tf_op jit(solution)/shard_map/ppermute | solution.py:359
  75.7 3.1 %collective-permute-start.24 = (bf16[1024,128]{1,0:T(8,128)(2,1)S(1)}, bf16[1024,128]{1,0:T(8,128)(2,1)S(1)}, u32[]{:S(2)}, u32[]{:S(2)}) collective-permute-start(bf16[1024,128]{1,0:T(8,128)(2,1)S(1)} %get-tuple-element.43.refs_3_), channel_id=1, source_target_pairs={{1,4},{3,6},{4,1},{6,3},{9,12},{11,14},{12,9},{14,11},{17,20},{19,... | collective-permute-start | bytes 786440 | tf_op jit(solution)/shard_map/ppermute | solution.py:359
  78.9 1.2 %collective-permute-start.21 = (bf16[1024,128]{1,0:T(8,128)(2,1)S(1)}, bf16[1024,128]{1,0:T(8,128)(2,1)S(1)}, u32[]{:S(2)}, u32[]{:S(2)}) collective-permute-start(bf16[1024,128]{1,0:T(8,128)(2,1)S(1)} %add_after.6.refs_2_.refs_0_), channel_id=1, source_target_pairs={{0,1},{1,5},{2,3},{3,7},{4,0},{5,4},{6,2},{7,6},{8,9},{9,13},{10,1... | collective-permute-start | bytes 786440 | tf_op jit(solution)/shard_map/ppermute | solution.py:359
  80.1 2.2 %collective-permute-start.22 = (bf16[1024,128]{1,0:T(8,128)(2,1)S(1)}, bf16[1024,128]{1,0:T(8,128)(2,1)S(1)}, u32[]{:S(2)}, u32[]{:S(2)}) collective-permute-start(bf16[1024,128]{1,0:T(8,128)(2,1)S(1)} %add_after.6.refs_2_.refs_0_), channel_id=1, source_target_pairs={{1,4},{3,6},{4,1},{6,3},{9,12},{11,14},{12,9},{14,11},{17,20},{19,... | collective-permute-start | bytes 786440 | tf_op jit(solution)/shard_map/ppermute | solution.py:359
  82.4 3.4 %collective-permute-done.24.refs_5_ = bf16[1024,128]{1,0:T(8,128)(2,1)S(1)} collective-permute-done((bf16[1024,128]{1,0:T(8,128)(2,1)S(1)}, bf16[1024,128]{1,0:T(8,128)(2,1)S(1)}, u32[]{:S(2)}, u32[]{:S(2)}) %collective-permute-start.24) | collective-permute-done | bytes 262176 | tf_op jit(solution)/shard_map/ppermute | solution.py:359
  85.9 1.1 %collective-permute-done.21.refs_1_ = bf16[1024,128]{1,0:T(8,128)(2,1)S(1)} collective-permute-done((bf16[1024,128]{1,0:T(8,128)(2,1)S(1)}, bf16[1024,128]{1,0:T(8,128)(2,1)S(1)}, u32[]{:S(2)}, u32[]{:S(2)}) %collective-permute-start.21) | collective-permute-done | bytes 262176 | tf_op jit(solution)/shard_map/ppermute | solution.py:359
  87.0 2.3 %collective-permute-done.22.refs_2_ = bf16[1024,128]{1,0:T(8,128)(2,1)S(1)} collective-permute-done((bf16[1024,128]{1,0:T(8,128)(2,1)S(1)}, bf16[1024,128]{1,0:T(8,128)(2,1)S(1)}, u32[]{:S(2)}, u32[]{:S(2)}) %collective-permute-start.22) | collective-permute-done | bytes 262176 | tf_op jit(solution)/shard_map/ppermute | solution.py:359
  89.2 1.5 %final.1 = (bf16[1024,256]{1,0:T(8,128)(2,1)}, bf16[1024,256]{1,0:T(8,128)(2,1)}, f32[256,256]{1,0:T(8,128)}) custom-call(bf16[1024,128]{1,0:T(8,128)(2,1)S(1)} %add_after.6.refs_2_.refs_0_, bf16[1024,128]{1,0:T(8,128)(2,1)S(1)} %collective-permute-done.21.refs_1_, bf16[1024,128]{1,0:T(8,128)(2,1)S(1)} %collective-permute-done.22.refs_2_, ...), custom_call_target="tpu_custom_call" | custom-call | flops 134217728 | bytes 2097152 | tf_op jit(solution)/shard_map/final/pallas_call | solution.py:337
  (34 shorter events, 0.4 us)
Async XLA Ops:
  0.6 16.1 %copy-start.4 = (s32[1,5]{1,0:T(1,128)S(1)}, s32[1,5]{1,0:T(1,128)}, u32[]{:S(2)}) copy-start(s32[1,5]{1,0:T(1,128)} %param.11) | copy-start | bytes 64
  0.6 22.1 %collective-permute-start.2 = (bf16[5,8,128,128]{3,2,1,0:T(8,128)(2,1)}, bf16[5,8,128,128]{3,2,1,0:T(8,128)(2,1)S(1)}, u32[]{:S(2)}, u32[]{:S(2)}) collective-permute-start(bf16[5,8,128,128]{3,2,1,0:T(8,128)(2,1)} %bitcast.5), channel_id=1, source_target_pairs={{0,4},{1,0},{2,6},{3,2},{4,5},{5,1},{6,7},{7,3},{8,12},{9,8},{10,1... | collective-permute-start | bytes 3932168 | tf_op jit(solution)/shard_map/ppermute | solution.py:359
  2.8 1.0 %copy-start.1 = (bf16[1024,256]{1,0:T(8,128)(2,1)S(1)}, bf16[1024,256]{1,0:T(8,128)(2,1)}, u32[]{:S(2)}) copy-start(bf16[1024,256]{1,0:T(8,128)(2,1)} %x_ref.2) | copy-start | bytes 1572868
  3.9 12.9 %copy-start.5 = (s32[2,1,5,8]{3,1,2,0:T(1,128)S(1)}, s32[2,1,5,8]{3,1,2,0:T(1,128)}, u32[]{:S(2)}) copy-start(s32[2,1,5,8]{3,1,2,0:T(1,128)} %param.10) | copy-start | bytes 964
  4.0 6.8 %collective-permute-start.3 = (bf16[1024,128]{1,0:T(8,128)(2,1)S(1)}, bf16[1024,128]{1,0:T(8,128)(2,1)S(1)}, u32[]{:S(2)}, u32[]{:S(2)}) collective-permute-start(bf16[1024,128]{1,0:T(8,128)(2,1)S(1)} %get-tuple-element.28.refs_3_.refs_2_.refs_5_.refs_4_.refs_7_), channel_id=1, source_target_pairs={{0,8},{1,17},{2,10},{3,19},{5,13},{7,15},{8,0},{10,2},{12,28},{13,... | collective-permute-start | bytes 786440 | tf_op jit(solution)/shard_map/ppermute | solution.py:359
  4.7 8.9 %collective-permute-start.4 = (bf16[1024,128]{1,0:T(8,128)(2,1)S(1)}, bf16[1024,128]{1,0:T(8,128)(2,1)S(1)}, u32[]{:S(2)}, u32[]{:S(2)}) collective-permute-start(bf16[1024,128]{1,0:T(8,128)(2,1)S(1)} %get-tuple-element.25), channel_id=1, source_target_pairs={{0,12},{1,21},{2,14},{3,23},{5,9},{7,11},{8,4},{10,6},{12,24},{13,... | collective-permute-start | bytes 786440 | tf_op jit(solution)/shard_map/ppermute | solution.py:359
  6.0 7.6 %collective-permute-start = (bf16[1024,128]{1,0:T(8,128)(2,1)S(1)}, bf16[1024,128]{1,0:T(8,128)(2,1)S(1)}, u32[]{:S(2)}, u32[]{:S(2)}) collective-permute-start(bf16[1024,128]{1,0:T(8,128)(2,1)S(1)} %get-tuple-element.25), channel_id=1, source_target_pairs={{0,4},{1,5},{2,6},{3,7},{4,0},{5,1},{6,2},{7,3},{8,12},{9,13},{10,... | collective-permute-start | bytes 786440 | tf_op jit(solution)/shard_map/ppermute | solution.py:359
  13.6 10.4 %collective-permute-start.6 = (bf16[1024,128]{1,0:T(8,128)(2,1)S(1)}, bf16[1024,128]{1,0:T(8,128)(2,1)S(1)}, u32[]{:S(2)}, u32[]{:S(2)}) collective-permute-start(bf16[1024,128]{1,0:T(8,128)(2,1)S(1)} %get-tuple-element.31), channel_id=1, source_target_pairs={{0,16},{1,17},{2,18},{3,19},{4,20},{5,21},{6,22},{7,23},{8,24},{9,... | collective-permute-start | bytes 786440 | tf_op jit(solution)/shard_map/ppermute | solution.py:359
  15.5 8.6 %collective-permute-start.7 = (bf16[1024,128]{1,0:T(8,128)(2,1)S(1)}, bf16[1024,128]{1,0:T(8,128)(2,1)S(1)}, u32[]{:S(2)}, u32[]{:S(2)}) collective-permute-start(bf16[1024,128]{1,0:T(8,128)(2,1)S(1)} %get-tuple-element.32), channel_id=1, source_target_pairs={{0,8},{1,9},{2,10},{3,11},{4,12},{5,13},{6,14},{7,15},{8,0},{9,1},... | collective-permute-start | bytes 786440 | tf_op jit(solution)/shard_map/ppermute | solution.py:359
  18.1 9.6 %copy-start = (bf16[1,5,8,128,128]{4,3,2,1,0:T(8,128)(2,1)S(1)}, bf16[1,5,8,128,128]{4,3,2,1,0:T(8,128)(2,1)}, u32[]{:S(2)}) copy-start(bf16[1,5,8,128,128]{4,3,2,1,0:T(8,128)(2,1)} %param.9) | copy-start | bytes 3932164
  18.1 6.0 %collective-permute-start.8 = (s32[2,40]{1,0:T(2,128)S(1)}, s32[2,40]{1,0:T(2,128)S(1)}, u32[]{:S(2)}, u32[]{:S(2)}) collective-permute-start(s32[2,40]{1,0:T(2,128)S(1)} %slot_blocks.1.refs_0_.refs_1_), channel_id=1, source_target_pairs={{0,4},{1,0},{2,6},{3,2},{4,5},{5,1},{6,7},{7,3},{8,12},{9,8},{10,1... | collective-permute-start | bytes 968 | tf_op jit(solution)/shard_map/ppermute | solution.py:359
  18.4 7.0 %collective-permute-start.1 = (s32[2,40]{1,0:T(2,128)S(1)}, s32[2,40]{1,0:T(2,128)S(1)}, u32[]{:S(2)}, u32[]{:S(2)}) collective-permute-start(s32[2,40]{1,0:T(2,128)S(1)} %slot_blocks.1.refs_0_.refs_1_), channel_id=1, source_target_pairs={{1,4},{3,6},{4,1},{6,3},{9,12},{11,14},{12,9},{14,11},{17,20},{19,... | collective-permute-start | bytes 968 | tf_op jit(solution)/shard_map/ppermute | solution.py:359
  22.8 4.9 %collective-permute-start.5 = (bf16[5,8,128,128]{3,2,1,0:T(8,128)(2,1)S(1)}, bf16[5,8,128,128]{3,2,1,0:T(8,128)(2,1)S(1)}, u32[]{:S(2)}, u32[]{:S(2)}) collective-permute-start(bf16[5,8,128,128]{3,2,1,0:T(8,128)(2,1)S(1)} %collective-permute-done.2.refs_1_.refs_3_), channel_id=1, source_target_pairs={{0,4},{2,6},{5,1},{7,3},{8,12},{10,14},{13,9},{15,11},{16,20},{18,... | collective-permute-start | bytes 3932168 | tf_op jit(solution)/shard_map/ppermute | solution.py:359
  25.4 6.2 %copy-start.2 = (bf16[1024,256]{1,0:T(8,128)(2,1)S(1)}, bf16[1024,256]{1,0:T(8,128)(2,1)}, u32[]{:S(2)}) copy-start(bf16[1024,256]{1,0:T(8,128)(2,1)} %x_ref.3) | copy-start | bytes 1572868
  29.1 16.1 %copy-start.3 = (bf16[256,256]{1,0:T(8,128)(2,1)S(1)}, bf16[256,256]{1,0:T(8,128)(2,1)}, u32[]{:S(2)}) copy-start(bf16[256,256]{1,0:T(8,128)(2,1)} %refs_6_.1) | copy-start | bytes 393220
  29.1 14.3 %collective-permute-start.9 = (bf16[1024,128]{1,0:T(8,128)(2,1)S(1)}, bf16[1024,128]{1,0:T(8,128)(2,1)S(1)}, u32[]{:S(2)}, u32[]{:S(2)}) collective-permute-start(bf16[1024,128]{1,0:T(8,128)(2,1)S(1)} %tile_product.5), channel_id=1, source_target_pairs={{0,2},{1,3},{2,0},{3,1},{4,6},{5,7},{6,4},{7,5},{8,10},{9,11},{10,... | collective-permute-start | bytes 786440 | tf_op jit(solution)/shard_map/ppermute | solution.py:359
  31.6 12.4 %collective-permute-start.11 = (bf16[1024,128]{1,0:T(8,128)(2,1)S(1)}, bf16[1024,128]{1,0:T(8,128)(2,1)S(1)}, u32[]{:S(2)}, u32[]{:S(2)}) collective-permute-start(bf16[1024,128]{1,0:T(8,128)(2,1)S(1)} %get-tuple-element.34), channel_id=1, source_target_pairs={{0,4},{1,5},{2,6},{3,7},{4,0},{5,1},{6,2},{7,3},{8,12},{9,13},{10,... | collective-permute-start | bytes 786440 | tf_op jit(solution)/shard_map/ppermute | solution.py:359
  43.5 1.7 %collective-permute-start.10 = (bf16[1024,128]{1,0:T(8,128)(2,1)S(1)}, bf16[1024,128]{1,0:T(8,128)(2,1)S(1)}, u32[]{:S(2)}, u32[]{:S(2)}) collective-permute-start(bf16[1024,128]{1,0:T(8,128)(2,1)S(1)} %add_convert_fusion.near_ref), channel_id=1, source_target_pairs={{0,4},{1,5},{2,6},{3,7},{4,0},{5,1},{6,2},{7,3},{8,12},{9,13},{10,... | collective-permute-start | bytes 786440 | tf_op jit(solution)/shard_map/ppermute | solution.py:359
  45.6 7.6 %collective-permute-start.12 = (bf16[1024,128]{1,0:T(8,128)(2,1)S(1)}, bf16[1024,128]{1,0:T(8,128)(2,1)S(1)}, u32[]{:S(2)}, u32[]{:S(2)}) collective-permute-start(bf16[1024,128]{1,0:T(8,128)(2,1)S(1)} %get-tuple-element.40.adj_ref.refs_6_), channel_id=1, source_target_pairs={{0,17},{1,0},{2,19},{3,2},{4,21},{5,4},{6,23},{7,6},{8,9},{9,24},{... | collective-permute-start | bytes 786440 | tf_op jit(solution)/shard_map/ppermute | solution.py:359
  45.7 7.6 %collective-permute-start.13 = (bf16[1024,128]{1,0:T(8,128)(2,1)S(1)}, bf16[1024,128]{1,0:T(8,128)(2,1)S(1)}, u32[]{:S(2)}, u32[]{:S(2)}) collective-permute-start(bf16[1024,128]{1,0:T(8,128)(2,1)S(1)} %get-tuple-element.40.adj_ref.refs_6_), channel_id=1, source_target_pairs={{0,8},{1,9},{2,10},{3,11},{4,12},{5,13},{6,14},{7,15},{8,0},{9,1},... | collective-permute-start | bytes 786440 | tf_op jit(solution)/shard_map/ppermute | solution.py:359
  53.2 9.0 %collective-permute-start.15 = (bf16[1024,128]{1,0:T(8,128)(2,1)S(1)}, bf16[1024,128]{1,0:T(8,128)(2,1)S(1)}, u32[]{:S(2)}, u32[]{:S(2)}) collective-permute-start(bf16[1024,128]{1,0:T(8,128)(2,1)S(1)} %collective-permute-done.13.after_ref.refs_7_), channel_id=1, source_target_pairs={{0,16},{1,17},{2,18},{3,19},{4,20},{5,21},{6,22},{7,23},{8,24},{9,... | collective-permute-start | bytes 786440 | tf_op jit(solution)/shard_map/ppermute | solution.py:359
  54.0 8.2 %collective-permute-start.14 = (bf16[1024,128]{1,0:T(8,128)(2,1)S(1)}, bf16[1024,128]{1,0:T(8,128)(2,1)S(1)}, u32[]{:S(2)}, u32[]{:S(2)}) collective-permute-start(bf16[1024,128]{1,0:T(8,128)(2,1)S(1)} %get-tuple-element.40.adj_ref.refs_6_), channel_id=1, source_target_pairs={{0,1},{2,3},{4,5},{6,7},{9,8},{11,10},{13,12},{15,14},{16,17},{18,... | collective-permute-start | bytes 786440 | tf_op jit(solution)/shard_map/ppermute | solution.py:359
  57.0 5.8 %collective-permute-start.16 = (bf16[1024,128]{1,0:T(8,128)(2,1)S(1)}, bf16[1024,128]{1,0:T(8,128)(2,1)S(1)}, u32[]{:S(2)}, u32[]{:S(2)}) collective-permute-start(bf16[1024,128]{1,0:T(8,128)(2,1)S(1)} %collective-permute-done.12.refs_6_), channel_id=1, source_target_pairs={{0,8},{1,9},{2,10},{3,11},{4,12},{5,13},{6,14},{7,15},{8,0},{9,1},... | collective-permute-start | bytes 786440 | tf_op jit(solution)/shard_map/ppermute | solution.py:359
  57.1 5.1 %collective-permute-start.17 = (bf16[256,128]{1,0:T(8,128)(2,1)S(1)}, bf16[256,128]{1,0:T(8,128)(2,1)S(1)}, u32[]{:S(2)}, u32[]{:S(2)}) collective-permute-start(bf16[256,128]{1,0:T(8,128)(2,1)S(1)} %grad_block.1.refs_0_), channel_id=1, source_target_pairs={{0,1},{1,0},{2,3},{3,2},{4,5},{5,4},{6,7},{7,6},{8,9},{9,8},{10,11... | collective-permute-start | bytes 196616 | tf_op jit(solution)/shard_map/ppermute | solution.py:359
  64.3 14.6 %collective-permute-start.18 = (bf16[1024,128]{1,0:T(8,128)(2,1)S(1)}, bf16[1024,128]{1,0:T(8,128)(2,1)S(1)}, u32[]{:S(2)}, u32[]{:S(2)}) collective-permute-start(bf16[1024,128]{1,0:T(8,128)(2,1)S(1)} %tile_product.7.refs_2_.refs_0_), channel_id=1, source_target_pairs={{0,2},{1,3},{2,0},{3,1},{4,6},{5,7},{6,4},{7,5},{8,10},{9,11},{10,... | collective-permute-start | bytes 786440 | tf_op jit(solution)/shard_map/ppermute | solution.py:359
  67.0 3.2 %collective-permute-start.19 = (bf16[256,128]{1,0:T(8,128)(2,1)S(1)}, bf16[256,128]{1,0:T(8,128)(2,1)S(1)}, u32[]{:S(2)}, u32[]{:S(2)}) collective-permute-start(bf16[256,128]{1,0:T(8,128)(2,1)S(1)} %add_after.4.refs_0_), channel_id=1, source_target_pairs={{0,8},{1,9},{2,10},{3,11},{4,12},{5,13},{6,14},{7,15},{8,0},{9,1},... | collective-permute-start | bytes 196616 | tf_op jit(solution)/shard_map/ppermute | solution.py:359
  70.2 8.6 %collective-permute-start.20 = (bf16[256,128]{1,0:T(8,128)(2,1)S(1)}, bf16[256,128]{1,0:T(8,128)(2,1)S(1)}, u32[]{:S(2)}, u32[]{:S(2)}) collective-permute-start(bf16[256,128]{1,0:T(8,128)(2,1)S(1)} %add_after.5.refs_0_), channel_id=1, source_target_pairs={{0,16},{1,17},{2,18},{3,19},{4,20},{5,21},{6,22},{7,23},{8,24},{9,... | collective-permute-start | bytes 196616 | tf_op jit(solution)/shard_map/ppermute | solution.py:359
  71.3 11.1 %collective-permute-start.23 = (bf16[1024,128]{1,0:T(8,128)(2,1)S(1)}, bf16[1024,128]{1,0:T(8,128)(2,1)S(1)}, u32[]{:S(2)}, u32[]{:S(2)}) collective-permute-start(bf16[1024,128]{1,0:T(8,128)(2,1)S(1)} %get-tuple-element.43.refs_3_), channel_id=1, source_target_pairs={{0,1},{1,5},{2,3},{3,7},{4,0},{5,4},{6,2},{7,6},{8,9},{9,13},{10,1... | collective-permute-start | bytes 786440 | tf_op jit(solution)/shard_map/ppermute | solution.py:359
  75.7 10.2 %collective-permute-start.24 = (bf16[1024,128]{1,0:T(8,128)(2,1)S(1)}, bf16[1024,128]{1,0:T(8,128)(2,1)S(1)}, u32[]{:S(2)}, u32[]{:S(2)}) collective-permute-start(bf16[1024,128]{1,0:T(8,128)(2,1)S(1)} %get-tuple-element.43.refs_3_), channel_id=1, source_target_pairs={{1,4},{3,6},{4,1},{6,3},{9,12},{11,14},{12,9},{14,11},{17,20},{19,... | collective-permute-start | bytes 786440 | tf_op jit(solution)/shard_map/ppermute | solution.py:359
  78.9 8.1 %collective-permute-start.21 = (bf16[1024,128]{1,0:T(8,128)(2,1)S(1)}, bf16[1024,128]{1,0:T(8,128)(2,1)S(1)}, u32[]{:S(2)}, u32[]{:S(2)}) collective-permute-start(bf16[1024,128]{1,0:T(8,128)(2,1)S(1)} %add_after.6.refs_2_.refs_0_), channel_id=1, source_target_pairs={{0,1},{1,5},{2,3},{3,7},{4,0},{5,4},{6,2},{7,6},{8,9},{9,13},{10,1... | collective-permute-start | bytes 786440 | tf_op jit(solution)/shard_map/ppermute | solution.py:359
  80.1 9.1 %collective-permute-start.22 = (bf16[1024,128]{1,0:T(8,128)(2,1)S(1)}, bf16[1024,128]{1,0:T(8,128)(2,1)S(1)}, u32[]{:S(2)}, u32[]{:S(2)}) collective-permute-start(bf16[1024,128]{1,0:T(8,128)(2,1)S(1)} %add_after.6.refs_2_.refs_0_), channel_id=1, source_target_pairs={{1,4},{3,6},{4,1},{6,3},{9,12},{11,14},{12,9},{14,11},{17,20},{19,... | collective-permute-start | bytes 786440 | tf_op jit(solution)/shard_map/ppermute | solution.py:359
  82.3 3.5 %collective-permute-start.25 = (f32[256,128]{1,0:T(8,128)S(1)}, f32[256,128]{1,0:T(8,128)S(1)}, u32[]{:S(2)}, u32[]{:S(2)}) collective-permute-start(f32[256,128]{1,0:T(8,128)S(1)} %add_after.7.refs_7_), channel_id=1, source_target_pairs={{0,4},{1,5},{2,6},{3,7},{4,0},{5,1},{6,2},{7,3},{8,12},{9,13},{10,... | collective-permute-start | bytes 393224 | tf_op jit(solution)/shard_map/ppermute | solution.py:359

commit v8 on v7

--- a/solution.py
+++ b/solution.py
@@ -280,7 +280,9 @@
         out_specs=vmem,
         compiler_params=pltpu.CompilerParams(vmem_limit_bytes=8 * 1024 * 1024),
         cost_estimate=pl.CostEstimate(
-            flops=4 * rows * width * width, bytes_accessed=8 * rows * width, transcendentals=0
+            flops=4 * WEIGH * rows * width * width,
+            bytes_accessed=8 * WEIGH * rows * width,
+            transcendentals=0,
         ),
         name="grad_block",
     )(near, far, adj, after)
@@ -360,6 +362,9 @@
 
     def sibling(c, j, z):
         return (c, 1 - j, z)
+
+    def home_to_sibling(c, j, z):
+        return (c, 1 - j, z) if j == z % 2 else None
 
     def across(c, j, z):
         return (c, j, (z + reps // 2) % reps)
@@ -411,9 +416,9 @@
     coords, counts, swapped = lax.optimization_barrier((tile_coords, tile_counts, swapped))
     meta = slot_blocks(coords[:, 0], counts[0], blocks)
     meta_b = send(meta, to_home)
-    meta_far = send(meta, lambda c, j, z: None if j == z % 2 else (c, 1 - j, z ^ 1))
+    meta_far = send(meta_b, home_to_sibling)
     first, one, two = lax.optimization_barrier((first, one, two))
-    other_first = send(first, lambda c, j, z: (c, 1 - j, z) if j == z % 2 else None)
+    other_first = send(first, home_to_sibling)
 
     set_first = [(None, (meta_b, first))]
     set_rest = [("home", (meta, own)), ("away", (meta_far, other_first))]
@@ -472,8 +477,8 @@
         got = send(grad, lambda c, j, z, s=step: (c ^ s, j, z))
         step *= 2
         if step < shape[0]:
-            grad = add_after([grad, got], jnp.bfloat16)
-    back = add_after([back_part, send(back_part, across)], jnp.bfloat16, got)
+            grad = add_after([grad, got], jnp.float32)
+    back = add_after([back_part, send(back_part, across)], jnp.bfloat16, got, *act_parts[1:])
     back_parts = [back, *deliver(back)]
     grad = add_after([grad, got], jnp.float32, back)
     input_grad, activated, weight_grad = final(

time: 91.4 us -> 93 us (1.018)
  waiting for transfers between devices: 36.7 us -> 45.3 us
  starting transfers between devices: 42.7 us -> 36.2 us
    ppermute x26, waiting for transfers between devices: 36.7 us -> 45.3 us  [send(): return lax.ppermute(value, AXES, route(shape, move))]
    ppermute x26, starting transfers between devices: 42.7 us -> 36.2 us  [send(): return lax.ppermute(value, AXES, route(shape, move))]
  transfers between devices with their start and end apart: 26 -> 26, of which waited for: 12 -> 16; matrix products, arithmetic and copies ran while one was open for 0% -> 0% of each run, Pallas kernels for 5% -> 5%
where the time goes in v8:
time: 93 us; the launch traced here: 92.7 us
  waiting for transfers between devices  45.3 us (49%)
  starting transfers between devices  36.2 us (39%)
  Pallas kernels  9.25 us (10%)
  local copies, waits for them, and re-layouts  1.08 us (1%)
    ppermute x26, waiting for transfers between devices, send(): return lax.ppermute(value, AXES, route(shape, move))  45.3 us
    ppermute x26, starting transfers between devices, send(): return lax.ppermute(value, AXES, route(shape, move))  36.2 us
    pallas_call x4, Pallas kernels, tile_product(): pl.pallas_call(functools.partial(tile_kernel, kinds, cases, [[case for ca...  5.22 us
  transfers between devices with their start and end apart: 26, of which 16 were waited for; matrix products, arithmetic and copies ran while one was open for 0% of the time, Pallas kernels for 5%

profile of v8, /device:TPU:1, one launch (start us, length us, event | category | flops | bytes accessed | tf_op | source)
XLA Modules:
  0.0 92.7 jit_solution(591431614386282153)
XLA Ops:
  0.6 2.2 %collective-permute-start.3 = (bf16[5,8,128,128]{3,2,1,0:T(8,128)(2,1)}, bf16[5,8,128,128]{3,2,1,0:T(8,128)(2,1)S(1)}, u32[]{:S(2)}, u32[]{:S(2)}) collective-permute-start(bf16[5,8,128,128]{3,2,1,0:T(8,128)(2,1)} %bitcast.5), channel_id=1, source_target_pairs={{0,4},{1,0},{2,6},{3,2},{4,5},{5,1},{6,7},{7,3},{8,12},{9,8},{10,1... | collective-permute-start | bytes 3932168 | tf_op jit(solution)/shard_map/ppermute | solution.py:361
  2.8 1.0 %copy-done.1 = bf16[1024,256]{1,0:T(8,128)(2,1)S(1)} copy-done((bf16[1024,256]{1,0:T(8,128)(2,1)S(1)}, bf16[1024,256]{1,0:T(8,128)(2,1)}, u32[]{:S(2)}) %copy-start.1) | copy-done | bytes 524312
  3.9 0.1 halves.2
  4.0 0.7 collective-permute-start.4
  4.7 1.3 %collective-permute-start.5 = (bf16[1024,128]{1,0:T(8,128)(2,1)S(1)}, bf16[1024,128]{1,0:T(8,128)(2,1)S(1)}, u32[]{:S(2)}, u32[]{:S(2)}) collective-permute-start(bf16[1024,128]{1,0:T(8,128)(2,1)S(1)} %get-tuple-element.25), channel_id=1, source_target_pairs={{0,12},{1,21},{2,14},{3,23},{5,9},{7,11},{8,4},{10,6},{12,24},{13,... | collective-permute-start | bytes 786440 | tf_op jit(solution)/shard_map/ppermute | solution.py:361
  6.0 4.8 %collective-permute-start = (bf16[1024,128]{1,0:T(8,128)(2,1)S(1)}, bf16[1024,128]{1,0:T(8,128)(2,1)S(1)}, u32[]{:S(2)}, u32[]{:S(2)}) collective-permute-start(bf16[1024,128]{1,0:T(8,128)(2,1)S(1)} %get-tuple-element.25), channel_id=1, source_target_pairs={{0,4},{1,5},{2,6},{3,7},{4,0},{5,1},{6,2},{7,3},{8,12},{9,13},{10,... | collective-permute-start | bytes 786440 | tf_op jit(solution)/shard_map/ppermute | solution.py:361
  10.8 2.8 %collective-permute-done.5.refs_1_.refs_4_.refs_7_.refs_9_ = bf16[1024,128]{1,0:T(8,128)(2,1)S(1)} collective-permute-done((bf16[1024,128]{1,0:T(8,128)(2,1)S(1)}, bf16[1024,128]{1,0:T(8,128)(2,1)S(1)}, u32[]{:S(2)}, u32[]{:S(2)}) %collective-permute-start.5) | collective-permute-done | bytes 262176 | tf_op jit(solution)/shard_map/ppermute | solution.py:361
  13.6 1.8 %collective-permute-start.7 = (bf16[1024,128]{1,0:T(8,128)(2,1)S(1)}, bf16[1024,128]{1,0:T(8,128)(2,1)S(1)}, u32[]{:S(2)}, u32[]{:S(2)}) collective-permute-start(bf16[1024,128]{1,0:T(8,128)(2,1)S(1)} %get-tuple-element.31), channel_id=1, source_target_pairs={{0,16},{1,17},{2,18},{3,19},{4,20},{5,21},{6,22},{7,23},{8,24},{9,... | collective-permute-start | bytes 786440 | tf_op jit(solution)/shard_map/ppermute | solution.py:361
  15.5 1.3 %collective-permute-start.8 = (bf16[1024,128]{1,0:T(8,128)(2,1)S(1)}, bf16[1024,128]{1,0:T(8,128)(2,1)S(1)}, u32[]{:S(2)}, u32[]{:S(2)}) collective-permute-start(bf16[1024,128]{1,0:T(8,128)(2,1)S(1)} %get-tuple-element.32), channel_id=1, source_target_pairs={{0,8},{1,9},{2,10},{3,11},{4,12},{5,13},{6,14},{7,15},{8,0},{9,1},... | collective-permute-start | bytes 786440 | tf_op jit(solution)/shard_map/ppermute | solution.py:361
  16.8 1.3 %slot_blocks.1.refs_0_.refs_1_ = s32[2,40]{1,0:T(2,128)S(1)} custom-call(s32[2,5,8]{2,1,0:T(8,128)S(1)} %copy.10.coords_ref, s32[5]{0:T(128)S(1)} %bitcast.9), custom_call_target="tpu_custom_call" | custom-call | tf_op jit(solution)/shard_map/slot_blocks/pallas_call | solution.py:131
  18.1 0.2 collective-permute-start.1
  18.4 1.5 %collective-permute-done.1.refs_0_ = s32[2,40]{1,0:T(2,128)S(1)} collective-permute-done((s32[2,40]{1,0:T(2,128)S(1)}, s32[2,40]{1,0:T(2,128)S(1)}, u32[]{:S(2)}, u32[]{:S(2)}) %collective-permute-start.1) | collective-permute-done | bytes 352 | tf_op jit(solution)/shard_map/ppermute | solution.py:361
  19.9 1.3 %collective-permute-start.2 = (s32[2,40]{1,0:T(2,128)S(1)}, s32[2,40]{1,0:T(2,128)S(1)}, u32[]{:S(2)}, u32[]{:S(2)}) collective-permute-start(s32[2,40]{1,0:T(2,128)S(1)} %collective-permute-done.1.refs_0_), channel_id=1, source_target_pairs={{0,4},{2,6},{5,1},{7,3},{8,12},{10,14},{13,9},{15,11},{16,20},{18,... | collective-permute-start | bytes 968 | tf_op jit(solution)/shard_map/ppermute | solution.py:361
  21.2 1.3 %collective-permute-start.6 = (bf16[5,8,128,128]{3,2,1,0:T(8,128)(2,1)S(1)}, bf16[5,8,128,128]{3,2,1,0:T(8,128)(2,1)S(1)}, u32[]{:S(2)}, u32[]{:S(2)}) collective-permute-start(bf16[5,8,128,128]{3,2,1,0:T(8,128)(2,1)S(1)} %collective-permute-done.3.refs_1_.refs_3_), channel_id=1, source_target_pairs={{0,4},{2,6},{5,1},{7,3},{8,12},{10,14},{13,9},{15,11},{16,20},{18,... | collective-permute-start | bytes 3932168 | tf_op jit(solution)/shard_map/ppermute | solution.py:361
  22.5 0.6 collective-permute-done.8.refs_9_.refs_11_
  23.1 1.2 %tile_product.4.refs_12_ = f32[1024,128]{1,0:T(8,128)S(1)} custom-call(s32[2,40]{1,0:T(2,128)S(1)} %collective-permute-done.1.refs_0_, bf16[5,8,128,128]{3,2,1,0:T(8,128)(2,1)S(1)} %collective-permute-done.3.refs_1_.refs_3_, bf16[1024,128]{1,0:T(8,128)(2,1)S(1)} %get-tuple-element.28.refs_3_.refs_2_.refs_5_.refs_4_.refs_7_, ...), custom_call_target="tpu_custom_call" | custom-call | flops 33554432000 | bytes 524288000 | tf_op jit(solution)/shard_map/tile_product/pallas_call | solution.py:202
  24.3 0.4 collective-permute-done.2.refs_1_.refs_2_
  24.7 3.2 %collective-permute-done.6.refs_3_.refs_5_ = bf16[5,8,128,128]{3,2,1,0:T(8,128)(2,1)S(1)} collective-permute-done((bf16[5,8,128,128]{3,2,1,0:T(8,128)(2,1)S(1)}, bf16[5,8,128,128]{3,2,1,0:T(8,128)(2,1)S(1)}, u32[]{:S(2)}, u32[]{:S(2)}) %collective-permute-start.6) | collective-permute-done | bytes 1310752 | tf_op jit(solution)/shard_map/ppermute | solution.py:361
  27.9 1.4 %tile_product.5 = bf16[1024,128]{1,0:T(8,128)(2,1)S(1)} custom-call(s32[2,40]{1,0:T(2,128)S(1)} %slot_blocks.1.refs_0_.refs_1_, s32[2,40]{1,0:T(2,128)S(1)} %collective-permute-done.2.refs_1_.refs_2_, bf16[5,8,128,128]{3,2,1,0:T(8,128)(2,1)S(1)} %bitcast.6, bf16[5,8,128,128]{3,2,1,0:T(8,128)(2,1)S(1)} %collective-permute-done.6.refs_3_.refs_5_, ...), custom_call_target="tpu_custom_call" | custom-call | flops 167772160 | bytes 2621440 | tf_op jit(solution)/shard_map/tile_product/pallas_call | solution.py:202
  29.3 2.4 %collective-permute-start.9 = (bf16[1024,128]{1,0:T(8,128)(2,1)S(1)}, bf16[1024,128]{1,0:T(8,128)(2,1)S(1)}, u32[]{:S(2)}, u32[]{:S(2)}) collective-permute-start(bf16[1024,128]{1,0:T(8,128)(2,1)S(1)} %tile_product.5), channel_id=1, source_target_pairs={{0,2},{1,3},{2,0},{3,1},{4,6},{5,7},{6,4},{7,5},{8,10},{9,11},{10,... | collective-permute-start | bytes 786440 | tf_op jit(solution)/shard_map/ppermute | solution.py:361
  31.7 0.1 halves.3
  31.8 0.5 collective-permute-start.11
  32.3 11.8 %collective-permute-done.9 = bf16[1024,128]{1,0:T(8,128)(2,1)S(1)} collective-permute-done((bf16[1024,128]{1,0:T(8,128)(2,1)S(1)}, bf16[1024,128]{1,0:T(8,128)(2,1)S(1)}, u32[]{:S(2)}, u32[]{:S(2)}) %collective-permute-start.9) | collective-permute-done | bytes 262176 | tf_op jit(solution)/shard_map/ppermute | solution.py:361
  44.2 0.5 collective-permute-start.10
  44.7 1.2 %collective-permute-done.10.far_ref = bf16[1024,128]{1,0:T(8,128)(2,1)S(1)} collective-permute-done((bf16[1024,128]{1,0:T(8,128)(2,1)S(1)}, bf16[1024,128]{1,0:T(8,128)(2,1)S(1)}, u32[]{:S(2)}, u32[]{:S(2)}) %collective-permute-start.10) | collective-permute-done | bytes 262176 | tf_op jit(solution)/shard_map/ppermute | solution.py:361
  45.9 0.4 middle.1
  46.4 7.4 %collective-permute-done.12.refs_6_ = bf16[1024,128]{1,0:T(8,128)(2,1)S(1)} collective-permute-done((bf16[1024,128]{1,0:T(8,128)(2,1)S(1)}, bf16[1024,128]{1,0:T(8,128)(2,1)S(1)}, u32[]{:S(2)}, u32[]{:S(2)}) %collective-permute-start.12) | collective-permute-done | bytes 262176 | tf_op jit(solution)/shard_map/ppermute | solution.py:361
  53.9 0.3 collective-permute-start.15
  54.2 0.4 grad_block.1.refs_0_
  54.6 3.1 %collective-permute-start.14 = (bf16[1024,128]{1,0:T(8,128)(2,1)S(1)}, bf16[1024,128]{1,0:T(8,128)(2,1)S(1)}, u32[]{:S(2)}, u32[]{:S(2)}) collective-permute-start(bf16[1024,128]{1,0:T(8,128)(2,1)S(1)} %get-tuple-element.40.adj_ref.refs_6_), channel_id=1, source_target_pairs={{0,1},{2,3},{4,5},{6,7},{9,8},{11,10},{13,12},{15,14},{16,17},{18,... | collective-permute-start | bytes 786440 | tf_op jit(solution)/shard_map/ppermute | solution.py:361
  57.7 1.3 %collective-permute-start.17 = (bf16[256,128]{1,0:T(8,128)(2,1)S(1)}, bf16[256,128]{1,0:T(8,128)(2,1)S(1)}, u32[]{:S(2)}, u32[]{:S(2)}) collective-permute-start(bf16[256,128]{1,0:T(8,128)(2,1)S(1)} %grad_block.1.refs_0_), channel_id=1, source_target_pairs={{0,1},{1,0},{2,3},{3,2},{4,5},{5,4},{6,7},{7,6},{8,9},{9,8},{10,11... | collective-permute-start | bytes 196616 | tf_op jit(solution)/shard_map/ppermute | solution.py:361
  59.0 1.1 %tile_product.6.refs_10_ = f32[1024,128]{1,0:T(8,128)S(1)} custom-call(s32[2,40]{1,0:T(2,128)S(1)} %collective-permute-done.1.refs_0_, s32[2,40]{1,0:T(2,128)S(1)} %slot_blocks.1.refs_0_.refs_1_, s32[2,40]{1,0:T(2,128)S(1)} %collective-permute-done.2.refs_1_.refs_2_, bf16[5,8,128,128]{3,2,1,0:T(8,128)(2,1)S(1)} %collective-permute-done.3.refs_1_.refs_3_, ...), custom_call_target="tpu_custom_call" | custom-call | flops 134217728 | bytes 1572864 | tf_op jit(solution)/shard_map/tile_product/pallas_call | solution.py:202
  60.1 2.8 %collective-permute-done.17.refs_11_.refs_1_ = bf16[256,128]{1,0:T(8,128)(2,1)S(1)} collective-permute-done((bf16[256,128]{1,0:T(8,128)(2,1)S(1)}, bf16[256,128]{1,0:T(8,128)(2,1)S(1)}, u32[]{:S(2)}, u32[]{:S(2)}) %collective-permute-start.17) | collective-permute-done | bytes 65568 | tf_op jit(solution)/shard_map/ppermute | solution.py:361
  63.0 0.6 collective-permute-done.16.refs_9_
  63.6 1.4 %tile_product.7.refs_2_.refs_0_ = bf16[1024,128]{1,0:T(8,128)(2,1)S(1)} custom-call(s32[2,40]{1,0:T(2,128)S(1)} %collective-permute-done.1.refs_0_, s32[2,40]{1,0:T(2,128)S(1)} %slot_blocks.1.refs_0_.refs_1_, s32[2,40]{1,0:T(2,128)S(1)} %collective-permute-done.2.refs_1_.refs_2_, bf16[5,8,128,128]{3,2,1,0:T(8,128)(2,1)S(1)} %collective-permute-done.3.refs_1_.refs_3_, ...), custom_call_target="tpu_custom_call" | custom-call | flops 201326592 | bytes 2359296 | tf_op jit(solution)/shard_map/tile_product/pallas_call | solution.py:202
  65.0 2.4 %collective-permute-start.18 = (bf16[1024,128]{1,0:T(8,128)(2,1)S(1)}, bf16[1024,128]{1,0:T(8,128)(2,1)S(1)}, u32[]{:S(2)}, u32[]{:S(2)}) collective-permute-start(bf16[1024,128]{1,0:T(8,128)(2,1)S(1)} %tile_product.7.refs_2_.refs_0_), channel_id=1, source_target_pairs={{0,2},{1,3},{2,0},{3,1},{4,6},{5,7},{6,4},{7,5},{8,10},{9,11},{10,... | collective-permute-start | bytes 786440 | tf_op jit(solution)/shard_map/ppermute | solution.py:361
  67.4 3.0 %collective-permute-start.21 = (bf16[1024,128]{1,0:T(8,128)(2,1)S(1)}, bf16[1024,128]{1,0:T(8,128)(2,1)S(1)}, u32[]{:S(2)}, u32[]{:S(2)}) collective-permute-start(bf16[1024,128]{1,0:T(8,128)(2,1)S(1)} %get-tuple-element.43.refs_3_), channel_id=1, source_target_pairs={{0,1},{1,5},{2,3},{3,7},{4,0},{5,4},{6,2},{7,6},{8,9},{9,13},{10,1... | collective-permute-start | bytes 786440 | tf_op jit(solution)/shard_map/ppermute | solution.py:361
  70.4 3.1 %collective-permute-start.22 = (bf16[1024,128]{1,0:T(8,128)(2,1)S(1)}, bf16[1024,128]{1,0:T(8,128)(2,1)S(1)}, u32[]{:S(2)}, u32[]{:S(2)}) collective-permute-start(bf16[1024,128]{1,0:T(8,128)(2,1)S(1)} %get-tuple-element.43.refs_3_), channel_id=1, source_target_pairs={{1,4},{3,6},{4,1},{6,3},{9,12},{11,14},{12,9},{14,11},{17,20},{19,... | collective-permute-start | bytes 786440 | tf_op jit(solution)/shard_map/ppermute | solution.py:361
  73.6 0.3 collective-permute-start.19
  73.8 3.5 %collective-permute-done.19.refs_1_ = bf16[256,128]{1,0:T(8,128)(2,1)S(1)} collective-permute-done((bf16[256,128]{1,0:T(8,128)(2,1)S(1)}, bf16[256,128]{1,0:T(8,128)(2,1)S(1)}, u32[]{:S(2)}, u32[]{:S(2)}) %collective-permute-start.19) | collective-permute-done | bytes 65568 | tf_op jit(solution)/shard_map/ppermute | solution.py:361
  77.4 1.3 %collective-permute-start.20 = (f32[256,128]{1,0:T(8,128)S(1)}, f32[256,128]{1,0:T(8,128)S(1)}, u32[]{:S(2)}, u32[]{:S(2)}) collective-permute-start(f32[256,128]{1,0:T(8,128)S(1)} %add_after.5.refs_0_), channel_id=1, source_target_pairs={{0,16},{1,17},{2,18},{3,19},{4,20},{5,21},{6,22},{7,23},{8,24},{9,... | collective-permute-start | bytes 393224 | tf_op jit(solution)/shard_map/ppermute | solution.py:361
  78.7 3.8 %collective-permute-done.20.refs_2_.refs_1_ = f32[256,128]{1,0:T(8,128)S(1)} collective-permute-done((f32[256,128]{1,0:T(8,128)S(1)}, f32[256,128]{1,0:T(8,128)S(1)}, u32[]{:S(2)}, u32[]{:S(2)}) %collective-permute-start.20) | collective-permute-done | bytes 131104 | tf_op jit(solution)/shard_map/ppermute | solution.py:361
  82.6 0.9 %collective-permute-start.23 = (bf16[1024,128]{1,0:T(8,128)(2,1)S(1)}, bf16[1024,128]{1,0:T(8,128)(2,1)S(1)}, u32[]{:S(2)}, u32[]{:S(2)}) collective-permute-start(bf16[1024,128]{1,0:T(8,128)(2,1)S(1)} %add_after.6.refs_2_.refs_0_), channel_id=1, source_target_pairs={{0,1},{1,5},{2,3},{3,7},{4,0},{5,4},{6,2},{7,6},{8,9},{9,13},{10,1... | collective-permute-start | bytes 786440 | tf_op jit(solution)/shard_map/ppermute | solution.py:361
  83.5 2.0 %collective-permute-start.24 = (bf16[1024,128]{1,0:T(8,128)(2,1)S(1)}, bf16[1024,128]{1,0:T(8,128)(2,1)S(1)}, u32[]{:S(2)}, u32[]{:S(2)}) collective-permute-start(bf16[1024,128]{1,0:T(8,128)(2,1)S(1)} %add_after.6.refs_2_.refs_0_), channel_id=1, source_target_pairs={{1,4},{3,6},{4,1},{6,3},{9,12},{11,14},{12,9},{14,11},{17,20},{19,... | collective-permute-start | bytes 786440 | tf_op jit(solution)/shard_map/ppermute | solution.py:361
  85.6 1.3 %collective-permute-done.25.refs_8_ = f32[256,128]{1,0:T(8,128)S(1)} collective-permute-done((f32[256,128]{1,0:T(8,128)S(1)}, f32[256,128]{1,0:T(8,128)S(1)}, u32[]{:S(2)}, u32[]{:S(2)}) %collective-permute-start.25) | collective-permute-done | bytes 131104 | tf_op jit(solution)/shard_map/ppermute | solution.py:361
  87.0 0.9 collective-permute-done.23.refs_1_
  87.9 3.3 %collective-permute-done.24.refs_2_ = bf16[1024,128]{1,0:T(8,128)(2,1)S(1)} collective-permute-done((bf16[1024,128]{1,0:T(8,128)(2,1)S(1)}, bf16[1024,128]{1,0:T(8,128)(2,1)S(1)}, u32[]{:S(2)}, u32[]{:S(2)}) %collective-permute-start.24) | collective-permute-done | bytes 262176 | tf_op jit(solution)/shard_map/ppermute | solution.py:361
  91.2 1.5 %final.1 = (bf16[1024,256]{1,0:T(8,128)(2,1)}, bf16[1024,256]{1,0:T(8,128)(2,1)}, f32[256,256]{1,0:T(8,128)}) custom-call(bf16[1024,128]{1,0:T(8,128)(2,1)S(1)} %add_after.6.refs_2_.refs_0_, bf16[1024,128]{1,0:T(8,128)(2,1)S(1)} %collective-permute-done.23.refs_1_, bf16[1024,128]{1,0:T(8,128)(2,1)S(1)} %collective-permute-done.24.refs_2_, ...), custom_call_target="tpu_custom_call" | custom-call | flops 134217728 | bytes 2097152 | tf_op jit(solution)/shard_map/final/pallas_call | solution.py:339
  (34 shorter events, 0.7 us)
Async XLA Ops:
  0.6 16.1 %copy-start.4 = (s32[1,5]{1,0:T(1,128)S(1)}, s32[1,5]{1,0:T(1,128)}, u32[]{:S(2)}) copy-start(s32[1,5]{1,0:T(1,128)} %param.11) | copy-start | bytes 64
  0.6 20.5 %collective-permute-start.3 = (bf16[5,8,128,128]{3,2,1,0:T(8,128)(2,1)}, bf16[5,8,128,128]{3,2,1,0:T(8,128)(2,1)S(1)}, u32[]{:S(2)}, u32[]{:S(2)}) collective-permute-start(bf16[5,8,128,128]{3,2,1,0:T(8,128)(2,1)} %bitcast.5), channel_id=1, source_target_pairs={{0,4},{1,0},{2,6},{3,2},{4,5},{5,1},{6,7},{7,3},{8,12},{9,8},{10,1... | collective-permute-start | bytes 3932168 | tf_op jit(solution)/shard_map/ppermute | solution.py:361
  2.8 1.0 %copy-start.1 = (bf16[1024,256]{1,0:T(8,128)(2,1)S(1)}, bf16[1024,256]{1,0:T(8,128)(2,1)}, u32[]{:S(2)}) copy-start(bf16[1024,256]{1,0:T(8,128)(2,1)} %x_ref.2) | copy-start | bytes 1572868
  3.9 12.9 %copy-start.5 = (s32[2,1,5,8]{3,1,2,0:T(1,128)S(1)}, s32[2,1,5,8]{3,1,2,0:T(1,128)}, u32[]{:S(2)}) copy-start(s32[2,1,5,8]{3,1,2,0:T(1,128)} %param.10) | copy-start | bytes 964
  4.0 6.8 %collective-permute-start.4 = (bf16[1024,128]{1,0:T(8,128)(2,1)S(1)}, bf16[1024,128]{1,0:T(8,128)(2,1)S(1)}, u32[]{:S(2)}, u32[]{:S(2)}) collective-permute-start(bf16[1024,128]{1,0:T(8,128)(2,1)S(1)} %get-tuple-element.28.refs_3_.refs_2_.refs_5_.refs_4_.refs_7_), channel_id=1, source_target_pairs={{0,8},{1,17},{2,10},{3,19},{5,13},{7,15},{8,0},{10,2},{12,28},{13,... | collective-permute-start | bytes 786440 | tf_op jit(solution)/shard_map/ppermute | solution.py:361
  4.7 8.9 %collective-permute-start.5 = (bf16[1024,128]{1,0:T(8,128)(2,1)S(1)}, bf16[1024,128]{1,0:T(8,128)(2,1)S(1)}, u32[]{:S(2)}, u32[]{:S(2)}) collective-permute-start(bf16[1024,128]{1,0:T(8,128)(2,1)S(1)} %get-tuple-element.25), channel_id=1, source_target_pairs={{0,12},{1,21},{2,14},{3,23},{5,9},{7,11},{8,4},{10,6},{12,24},{13,... | collective-permute-start | bytes 786440 | tf_op jit(solution)/shard_map/ppermute | solution.py:361
  6.0 7.6 %collective-permute-start = (bf16[1024,128]{1,0:T(8,128)(2,1)S(1)}, bf16[1024,128]{1,0:T(8,128)(2,1)S(1)}, u32[]{:S(2)}, u32[]{:S(2)}) collective-permute-start(bf16[1024,128]{1,0:T(8,128)(2,1)S(1)} %get-tuple-element.25), channel_id=1, source_target_pairs={{0,4},{1,5},{2,6},{3,7},{4,0},{5,1},{6,2},{7,3},{8,12},{9,13},{10,... | collective-permute-start | bytes 786440 | tf_op jit(solution)/shard_map/ppermute | solution.py:361
  13.6 8.8 %collective-permute-start.7 = (bf16[1024,128]{1,0:T(8,128)(2,1)S(1)}, bf16[1024,128]{1,0:T(8,128)(2,1)S(1)}, u32[]{:S(2)}, u32[]{:S(2)}) collective-permute-start(bf16[1024,128]{1,0:T(8,128)(2,1)S(1)} %get-tuple-element.31), channel_id=1, source_target_pairs={{0,16},{1,17},{2,18},{3,19},{4,20},{5,21},{6,22},{7,23},{8,24},{9,... | collective-permute-start | bytes 786440 | tf_op jit(solution)/shard_map/ppermute | solution.py:361
  15.5 7.6 %collective-permute-start.8 = (bf16[1024,128]{1,0:T(8,128)(2,1)S(1)}, bf16[1024,128]{1,0:T(8,128)(2,1)S(1)}, u32[]{:S(2)}, u32[]{:S(2)}) collective-permute-start(bf16[1024,128]{1,0:T(8,128)(2,1)S(1)} %get-tuple-element.32), channel_id=1, source_target_pairs={{0,8},{1,9},{2,10},{3,11},{4,12},{5,13},{6,14},{7,15},{8,0},{9,1},... | collective-permute-start | bytes 786440 | tf_op jit(solution)/shard_map/ppermute | solution.py:361
  18.1 9.8 %copy-start = (bf16[1,5,8,128,128]{4,3,2,1,0:T(8,128)(2,1)S(1)}, bf16[1,5,8,128,128]{4,3,2,1,0:T(8,128)(2,1)}, u32[]{:S(2)}) copy-start(bf16[1,5,8,128,128]{4,3,2,1,0:T(8,128)(2,1)} %param.9) | copy-start | bytes 3932164
  18.1 1.7 %collective-permute-start.1 = (s32[2,40]{1,0:T(2,128)S(1)}, s32[2,40]{1,0:T(2,128)S(1)}, u32[]{:S(2)}, u32[]{:S(2)}) collective-permute-start(s32[2,40]{1,0:T(2,128)S(1)} %slot_blocks.1.refs_0_.refs_1_), channel_id=1, source_target_pairs={{0,4},{1,0},{2,6},{3,2},{4,5},{5,1},{6,7},{7,3},{8,12},{9,8},{10,1... | collective-permute-start | bytes 968 | tf_op jit(solution)/shard_map/ppermute | solution.py:361
  19.9 4.8 %collective-permute-start.2 = (s32[2,40]{1,0:T(2,128)S(1)}, s32[2,40]{1,0:T(2,128)S(1)}, u32[]{:S(2)}, u32[]{:S(2)}) collective-permute-start(s32[2,40]{1,0:T(2,128)S(1)} %collective-permute-done.1.refs_0_), channel_id=1, source_target_pairs={{0,4},{2,6},{5,1},{7,3},{8,12},{10,14},{13,9},{15,11},{16,20},{18,... | collective-permute-start | bytes 968 | tf_op jit(solution)/shard_map/ppermute | solution.py:361
  21.2 6.7 %collective-permute-start.6 = (bf16[5,8,128,128]{3,2,1,0:T(8,128)(2,1)S(1)}, bf16[5,8,128,128]{3,2,1,0:T(8,128)(2,1)S(1)}, u32[]{:S(2)}, u32[]{:S(2)}) collective-permute-start(bf16[5,8,128,128]{3,2,1,0:T(8,128)(2,1)S(1)} %collective-permute-done.3.refs_1_.refs_3_), channel_id=1, source_target_pairs={{0,4},{2,6},{5,1},{7,3},{8,12},{10,14},{13,9},{15,11},{16,20},{18,... | collective-permute-start | bytes 3932168 | tf_op jit(solution)/shard_map/ppermute | solution.py:361
  24.3 7.4 %copy-start.2 = (bf16[1024,256]{1,0:T(8,128)(2,1)S(1)}, bf16[1024,256]{1,0:T(8,128)(2,1)}, u32[]{:S(2)}) copy-start(bf16[1024,256]{1,0:T(8,128)(2,1)} %x_ref.3) | copy-start | bytes 1572868
  29.3 16.6 %copy-start.3 = (bf16[256,256]{1,0:T(8,128)(2,1)S(1)}, bf16[256,256]{1,0:T(8,128)(2,1)}, u32[]{:S(2)}) copy-start(bf16[256,256]{1,0:T(8,128)(2,1)} %refs_6_.1) | copy-start | bytes 393220
  29.3 14.8 %collective-permute-start.9 = (bf16[1024,128]{1,0:T(8,128)(2,1)S(1)}, bf16[1024,128]{1,0:T(8,128)(2,1)S(1)}, u32[]{:S(2)}, u32[]{:S(2)}) collective-permute-start(bf16[1024,128]{1,0:T(8,128)(2,1)S(1)} %tile_product.5), channel_id=1, source_target_pairs={{0,2},{1,3},{2,0},{3,1},{4,6},{5,7},{6,4},{7,5},{8,10},{9,11},{10,... | collective-permute-start | bytes 786440 | tf_op jit(solution)/shard_map/ppermute | solution.py:361
  31.8 12.9 %collective-permute-start.11 = (bf16[1024,128]{1,0:T(8,128)(2,1)S(1)}, bf16[1024,128]{1,0:T(8,128)(2,1)S(1)}, u32[]{:S(2)}, u32[]{:S(2)}) collective-permute-start(bf16[1024,128]{1,0:T(8,128)(2,1)S(1)} %get-tuple-element.34), channel_id=1, source_target_pairs={{0,4},{1,5},{2,6},{3,7},{4,0},{5,1},{6,2},{7,3},{8,12},{9,13},{10,... | collective-permute-start | bytes 786440 | tf_op jit(solution)/shard_map/ppermute | solution.py:361
  44.2 1.7 %collective-permute-start.10 = (bf16[1024,128]{1,0:T(8,128)(2,1)S(1)}, bf16[1024,128]{1,0:T(8,128)(2,1)S(1)}, u32[]{:S(2)}, u32[]{:S(2)}) collective-permute-start(bf16[1024,128]{1,0:T(8,128)(2,1)S(1)} %add_convert_fusion.near_ref), channel_id=1, source_target_pairs={{0,4},{1,5},{2,6},{3,7},{4,0},{5,1},{6,2},{7,3},{8,12},{9,13},{10,... | collective-permute-start | bytes 786440 | tf_op jit(solution)/shard_map/ppermute | solution.py:361
  46.3 7.6 %collective-permute-start.12 = (bf16[1024,128]{1,0:T(8,128)(2,1)S(1)}, bf16[1024,128]{1,0:T(8,128)(2,1)S(1)}, u32[]{:S(2)}, u32[]{:S(2)}) collective-permute-start(bf16[1024,128]{1,0:T(8,128)(2,1)S(1)} %get-tuple-element.40.adj_ref.refs_6_), channel_id=1, source_target_pairs={{0,17},{1,0},{2,19},{3,2},{4,21},{5,4},{6,23},{7,6},{8,9},{9,24},{... | collective-permute-start | bytes 786440 | tf_op jit(solution)/shard_map/ppermute | solution.py:361
  46.3 7.6 %collective-permute-start.13 = (bf16[1024,128]{1,0:T(8,128)(2,1)S(1)}, bf16[1024,128]{1,0:T(8,128)(2,1)S(1)}, u32[]{:S(2)}, u32[]{:S(2)}) collective-permute-start(bf16[1024,128]{1,0:T(8,128)(2,1)S(1)} %get-tuple-element.40.adj_ref.refs_6_), channel_id=1, source_target_pairs={{0,8},{1,9},{2,10},{3,11},{4,12},{5,13},{6,14},{7,15},{8,0},{9,1},... | collective-permute-start | bytes 786440 | tf_op jit(solution)/shard_map/ppermute | solution.py:361
  53.9 9.0 %collective-permute-start.15 = (bf16[1024,128]{1,0:T(8,128)(2,1)S(1)}, bf16[1024,128]{1,0:T(8,128)(2,1)S(1)}, u32[]{:S(2)}, u32[]{:S(2)}) collective-permute-start(bf16[1024,128]{1,0:T(8,128)(2,1)S(1)} %collective-permute-done.13.after_ref.refs_7_), channel_id=1, source_target_pairs={{0,16},{1,17},{2,18},{3,19},{4,20},{5,21},{6,22},{7,23},{8,24},{9,... | collective-permute-start | bytes 786440 | tf_op jit(solution)/shard_map/ppermute | solution.py:361
  54.6 8.4 %collective-permute-start.14 = (bf16[1024,128]{1,0:T(8,128)(2,1)S(1)}, bf16[1024,128]{1,0:T(8,128)(2,1)S(1)}, u32[]{:S(2)}, u32[]{:S(2)}) collective-permute-start(bf16[1024,128]{1,0:T(8,128)(2,1)S(1)} %get-tuple-element.40.adj_ref.refs_6_), channel_id=1, source_target_pairs={{0,1},{2,3},{4,5},{6,7},{9,8},{11,10},{13,12},{15,14},{16,17},{18,... | collective-permute-start | bytes 786440 | tf_op jit(solution)/shard_map/ppermute | solution.py:361
  57.6 5.9 %collective-permute-start.16 = (bf16[1024,128]{1,0:T(8,128)(2,1)S(1)}, bf16[1024,128]{1,0:T(8,128)(2,1)S(1)}, u32[]{:S(2)}, u32[]{:S(2)}) collective-permute-start(bf16[1024,128]{1,0:T(8,128)(2,1)S(1)} %collective-permute-done.12.refs_6_), channel_id=1, source_target_pairs={{0,8},{1,9},{2,10},{3,11},{4,12},{5,13},{6,14},{7,15},{8,0},{9,1},... | collective-permute-start | bytes 786440 | tf_op jit(solution)/shard_map/ppermute | solution.py:361
  57.7 5.2 %collective-permute-start.17 = (bf16[256,128]{1,0:T(8,128)(2,1)S(1)}, bf16[256,128]{1,0:T(8,128)(2,1)S(1)}, u32[]{:S(2)}, u32[]{:S(2)}) collective-permute-start(bf16[256,128]{1,0:T(8,128)(2,1)S(1)} %grad_block.1.refs_0_), channel_id=1, source_target_pairs={{0,1},{1,0},{2,3},{3,2},{4,5},{5,4},{6,7},{7,6},{8,9},{9,8},{10,11... | collective-permute-start | bytes 196616 | tf_op jit(solution)/shard_map/ppermute | solution.py:361
  65.0 17.5 %collective-permute-start.18 = (bf16[1024,128]{1,0:T(8,128)(2,1)S(1)}, bf16[1024,128]{1,0:T(8,128)(2,1)S(1)}, u32[]{:S(2)}, u32[]{:S(2)}) collective-permute-start(bf16[1024,128]{1,0:T(8,128)(2,1)S(1)} %tile_product.7.refs_2_.refs_0_), channel_id=1, source_target_pairs={{0,2},{1,3},{2,0},{3,1},{4,6},{5,7},{6,4},{7,5},{8,10},{9,11},{10,... | collective-permute-start | bytes 786440 | tf_op jit(solution)/shard_map/ppermute | solution.py:361
  67.4 15.1 %collective-permute-start.21 = (bf16[1024,128]{1,0:T(8,128)(2,1)S(1)}, bf16[1024,128]{1,0:T(8,128)(2,1)S(1)}, u32[]{:S(2)}, u32[]{:S(2)}) collective-permute-start(bf16[1024,128]{1,0:T(8,128)(2,1)S(1)} %get-tuple-element.43.refs_3_), channel_id=1, source_target_pairs={{0,1},{1,5},{2,3},{3,7},{4,0},{5,4},{6,2},{7,6},{8,9},{9,13},{10,1... | collective-permute-start | bytes 786440 | tf_op jit(solution)/shard_map/ppermute | solution.py:361
  70.4 12.1 %collective-permute-start.22 = (bf16[1024,128]{1,0:T(8,128)(2,1)S(1)}, bf16[1024,128]{1,0:T(8,128)(2,1)S(1)}, u32[]{:S(2)}, u32[]{:S(2)}) collective-permute-start(bf16[1024,128]{1,0:T(8,128)(2,1)S(1)} %get-tuple-element.43.refs_3_), channel_id=1, source_target_pairs={{1,4},{3,6},{4,1},{6,3},{9,12},{11,14},{12,9},{14,11},{17,20},{19,... | collective-permute-start | bytes 786440 | tf_op jit(solution)/shard_map/ppermute | solution.py:361
  73.6 3.8 %collective-permute-start.19 = (bf16[256,128]{1,0:T(8,128)(2,1)S(1)}, bf16[256,128]{1,0:T(8,128)(2,1)S(1)}, u32[]{:S(2)}, u32[]{:S(2)}) collective-permute-start(bf16[256,128]{1,0:T(8,128)(2,1)S(1)} %add_after.4.refs_0_), channel_id=1, source_target_pairs={{0,8},{1,9},{2,10},{3,11},{4,12},{5,13},{6,14},{7,15},{8,0},{9,1},... | collective-permute-start | bytes 196616 | tf_op jit(solution)/shard_map/ppermute | solution.py:361
  77.4 5.1 %collective-permute-start.20 = (f32[256,128]{1,0:T(8,128)S(1)}, f32[256,128]{1,0:T(8,128)S(1)}, u32[]{:S(2)}, u32[]{:S(2)}) collective-permute-start(f32[256,128]{1,0:T(8,128)S(1)} %add_after.5.refs_0_), channel_id=1, source_target_pairs={{0,16},{1,17},{2,18},{3,19},{4,20},{5,21},{6,22},{7,23},{8,24},{9,... | collective-permute-start | bytes 393224 | tf_op jit(solution)/shard_map/ppermute | solution.py:361
  82.6 5.3 %collective-permute-start.23 = (bf16[1024,128]{1,0:T(8,128)(2,1)S(1)}, bf16[1024,128]{1,0:T(8,128)(2,1)S(1)}, u32[]{:S(2)}, u32[]{:S(2)}) collective-permute-start(bf16[1024,128]{1,0:T(8,128)(2,1)S(1)} %add_after.6.refs_2_.refs_0_), channel_id=1, source_target_pairs={{0,1},{1,5},{2,3},{3,7},{4,0},{5,4},{6,2},{7,6},{8,9},{9,13},{10,1... | collective-permute-start | bytes 786440 | tf_op jit(solution)/shard_map/ppermute | solution.py:361
  83.5 7.7 %collective-permute-start.24 = (bf16[1024,128]{1,0:T(8,128)(2,1)S(1)}, bf16[1024,128]{1,0:T(8,128)(2,1)S(1)}, u32[]{:S(2)}, u32[]{:S(2)}) collective-permute-start(bf16[1024,128]{1,0:T(8,128)(2,1)S(1)} %add_after.6.refs_2_.refs_0_), channel_id=1, source_target_pairs={{1,4},{3,6},{4,1},{6,3},{9,12},{11,14},{12,9},{14,11},{17,20},{19,... | collective-permute-start | bytes 786440 | tf_op jit(solution)/shard_map/ppermute | solution.py:361
  85.6 1.4 %collective-permute-start.25 = (f32[256,128]{1,0:T(8,128)S(1)}, f32[256,128]{1,0:T(8,128)S(1)}, u32[]{:S(2)}, u32[]{:S(2)}) collective-permute-start(f32[256,128]{1,0:T(8,128)S(1)} %add_after.7.refs_7_), channel_id=1, source_target_pairs={{0,4},{1,5},{2,6},{3,7},{4,0},{5,1},{6,2},{7,3},{8,12},{9,13},{10,... | collective-permute-start | bytes 393224 | tf_op jit(solution)/shard_map/ppermute | solution.py:361

commit v9 on v8

--- a/solution.py
+++ b/solution.py
@@ -87,10 +87,10 @@
     )(value)
 
 
-def pick_kernel(cases, *refs):
+def pick_kernel(cases, waits, *refs):
     refs = list(refs)
     choices = [[(case, refs.pop(0)) for case in each] for each in cases]
-    outs, sems = refs[:-1], refs[-1]
+    outs, sems = refs[waits:-1], refs[-1]
 
     def copy_to(i):
         return lambda ref: pltpu.make_async_copy(ref, outs[i], sems.at[i])
@@ -101,19 +101,21 @@
         copy_to(i)(choice[0][1]).wait()
 
 
-def pick(*choices):
+def pick(choices, after):
     hbm = pl.BlockSpec(memory_space=pltpu.HBM)
     arrays = [array for choice in choices for _, array in choice]
     shape = jax.ShapeDtypeStruct(arrays[0].shape, arrays[0].dtype)
     return pl.pallas_call(
-        functools.partial(pick_kernel, [[case for case, _ in choice] for choice in choices]),
+        functools.partial(
+            pick_kernel, [[case for case, _ in choice] for choice in choices], len(after)
+        ),
         out_shape=(shape,) * len(choices),
-        in_specs=[hbm] * len(arrays),
+        in_specs=[hbm] * len(arrays) + [pl.BlockSpec(memory_space=pl.ANY)] * len(after),
         out_specs=(hbm,) * len(choices),
         scratch_shapes=[pltpu.SemaphoreType.DMA((len(choices),))],
         compiler_params=pltpu.CompilerParams(vmem_limit_bytes=1024 * 1024),
         name="pick",
-    )(*arrays)
+    )(*arrays, *after)
 
 
 def slots_kernel(dead, coords_ref, counts_ref, out_ref):
@@ -402,26 +404,25 @@
     swapped = send(yours, sibling)
     self_choice = [("home", mine), ("away", swapped)]
     direct_choice = [("home", one), ("away", two)]
+    meta = slot_blocks(tile_coords[:, 0], tile_counts[0], blocks)
     second, far = pick(
-        direct_choice if four else self_choice,
         [
-            ("still home", swapped),
-            ("still away", mine),
-            ("relay home", two),
-            ("relay away", one),
+            direct_choice if four else self_choice,
+            [
+                ("still home", swapped),
+                ("still away", mine),
+                ("relay home", two),
+                ("relay away", one),
+            ],
         ],
+        [meta],
     )
     second = send(second, to_second)
     far = send(far, to_far)
-    coords, counts, swapped = lax.optimization_barrier((tile_coords, tile_counts, swapped))
-    meta = slot_blocks(coords[:, 0], counts[0], blocks)
     meta_b = send(meta, to_home)
-    meta_far = send(meta_b, home_to_sibling)
     first, one, two = lax.optimization_barrier((first, one, two))
     other_first = send(first, home_to_sibling)
-
     set_first = [(None, (meta_b, first))]
-    set_rest = [("home", (meta, own)), ("away", (meta_far, other_first))]
     panels = [
         ("self", [("home", mine), ("away", swapped)]),
         ("near", [("home", swapped), ("away", mine)]),
@@ -430,6 +431,9 @@
         ("far", [(None, far)]),
     ]
     part = tile_product(panels, [set_first], jnp.float32, weigh=WEIGH)
+    meta_later, part = lax.optimization_barrier((meta_b, part))
+    meta_far = send(meta_later, home_to_sibling)
+    set_rest = [("home", (meta, own)), ("away", (meta_far, other_first))]
     part = tile_product(panels, [set_rest], jnp.bfloat16, part)
 
     def join(value):
@@ -471,16 +475,14 @@
 
     act_later, back_part = lax.optimization_barrier((act, back_part))
     act_parts = [act, *deliver(act_later)]
+    back = add_after([back_part, send(back_part, across)], jnp.bfloat16, *act_parts[1:])
+    back_parts = [back, *deliver(back)]
     grad = add_after([grad, grad_got], jnp.bfloat16, back_part)
     step = 1
     while step < shape[0]:
         got = send(grad, lambda c, j, z, s=step: (c ^ s, j, z))
+        grad = add_after([grad, got], jnp.float32, back)
         step *= 2
-        if step < shape[0]:
-            grad = add_after([grad, got], jnp.float32)
-    back = add_after([back_part, send(back_part, across)], jnp.bfloat16, got, *act_parts[1:])
-    back_parts = [back, *deliver(back)]
-    grad = add_after([grad, got], jnp.float32, back)
     input_grad, activated, weight_grad = final(
         back_parts, act_parts, weight, grad, send(grad, sibling)
     )

time: 93 us -> 94.8 us (1.019)
  the two profiles are of different devices: /device:TPU:1 before, /device:TPU:24 now
where the time goes in v9:
time: 94.8 us; the launch traced here: 94.4 us
  waiting for transfers between devices  54.3 us (57%)
  starting transfers between devices  27.5 us (29%)
  Pallas kernels  9.25 us (10%)
  local copies, waits for them, and re-layouts  2.41 us (3%)
    ppermute x26, waiting for transfers between devices, send(): return lax.ppermute(value, AXES, route(shape, move))  54.3 us
    ppermute x26, starting transfers between devices, send(): return lax.ppermute(value, AXES, route(shape, move))  27.5 us
    pallas_call x4, Pallas kernels, tile_product(): pl.pallas_call(functools.partial(tile_kernel, kinds, cases, [[case for ca...  5.23 us
    unnamed x11, local copies, waits for them, and re-layouts  2.41 us
  transfers between devices with their start and end apart: 26, of which 15 were waited for; matrix products, arithmetic and copies ran while one was open for 1% of the time, Pallas kernels for 5%

profile of v9, /device:TPU:24, one launch (start us, length us, event | category | flops | bytes accessed | tf_op | source)
XLA Modules:
  0.0 94.4 jit_solution(8260050861629100126)
XLA Ops:
  0.6 0.5 collective-permute-start.1
  1.1 1.0 %copy-done.1 = bf16[1024,256]{1,0:T(8,128)(2,1)S(1)} copy-done((bf16[1024,256]{1,0:T(8,128)(2,1)S(1)}, bf16[1024,256]{1,0:T(8,128)(2,1)}, u32[]{:S(2)}) %copy-start.1) | copy-done | bytes 524312
  2.2 0.1 halves.2
  2.3 3.4 %collective-permute-start.2 = (bf16[1024,128]{1,0:T(8,128)(2,1)S(1)}, bf16[1024,128]{1,0:T(8,128)(2,1)S(1)}, u32[]{:S(2)}, u32[]{:S(2)}) collective-permute-start(bf16[1024,128]{1,0:T(8,128)(2,1)S(1)} %get-tuple-element.24.refs_3_.refs_2_.refs_5_.refs_4_.refs_7_), channel_id=1, source_target_pairs={{0,8},{1,17},{2,10},{3,19},{5,13},{7,15},{8,0},{10,2},{12,28},{13,... | collective-permute-start | bytes 786440 | tf_op jit(solution)/shard_map/ppermute | solution.py:363
  5.7 2.8 %collective-permute-start.3 = (bf16[1024,128]{1,0:T(8,128)(2,1)S(1)}, bf16[1024,128]{1,0:T(8,128)(2,1)S(1)}, u32[]{:S(2)}, u32[]{:S(2)}) collective-permute-start(bf16[1024,128]{1,0:T(8,128)(2,1)S(1)} %get-tuple-element.25), channel_id=1, source_target_pairs={{0,12},{1,21},{2,14},{3,23},{5,9},{7,11},{8,4},{10,6},{12,24},{13,... | collective-permute-start | bytes 786440 | tf_op jit(solution)/shard_map/ppermute | solution.py:363
  8.6 0.7 copy.12
  9.3 0.7 copy-done.4
  10.0 1.3 %slot_blocks.1.refs_6_.refs_0_.refs_1_ = s32[2,40]{1,0:T(2,128)S(1)} custom-call(s32[2,5,8]{2,1,0:T(8,128)S(1)} %copy.10.coords_ref, s32[5]{0:T(128)S(1)} %bitcast.9), custom_call_target="tpu_custom_call" | custom-call | tf_op jit(solution)/shard_map/slot_blocks/pallas_call | solution.py:133
  11.3 2.1 %collective-permute-done.3.refs_1_.refs_4_.refs_7_.refs_9_ = bf16[1024,128]{1,0:T(8,128)(2,1)S(1)} collective-permute-done((bf16[1024,128]{1,0:T(8,128)(2,1)S(1)}, bf16[1024,128]{1,0:T(8,128)(2,1)S(1)}, u32[]{:S(2)}, u32[]{:S(2)}) %collective-permute-start.3) | collective-permute-done | bytes 262176 | tf_op jit(solution)/shard_map/ppermute | solution.py:363
  13.4 0.1 pick.1
  13.5 0.6 collective-permute-start.5
  14.2 1.5 %collective-permute-start.6 = (bf16[1024,128]{1,0:T(8,128)(2,1)S(1)}, bf16[1024,128]{1,0:T(8,128)(2,1)S(1)}, u32[]{:S(2)}, u32[]{:S(2)}) collective-permute-start(bf16[1024,128]{1,0:T(8,128)(2,1)S(1)} %get-tuple-element.28), channel_id=1, source_target_pairs={{0,8},{1,9},{2,10},{3,11},{4,12},{5,13},{6,14},{7,15},{8,0},{9,1},... | collective-permute-start | bytes 786440 | tf_op jit(solution)/shard_map/ppermute | solution.py:363
  15.6 1.1 %collective-permute-start = (s32[2,40]{1,0:T(2,128)S(1)}, s32[2,40]{1,0:T(2,128)S(1)}, u32[]{:S(2)}, u32[]{:S(2)}) collective-permute-start(s32[2,40]{1,0:T(2,128)S(1)} %slot_blocks.1.refs_6_.refs_0_.refs_1_), channel_id=1, source_target_pairs={{0,4},{1,0},{2,6},{3,2},{4,5},{5,1},{6,7},{7,3},{8,12},{9,8},{10,1... | collective-permute-start | bytes 968 | tf_op jit(solution)/shard_map/ppermute | solution.py:363
  16.7 1.3 %collective-permute-start.8 = (bf16[5,8,128,128]{3,2,1,0:T(8,128)(2,1)S(1)}, bf16[5,8,128,128]{3,2,1,0:T(8,128)(2,1)S(1)}, u32[]{:S(2)}, u32[]{:S(2)}) collective-permute-start(bf16[5,8,128,128]{3,2,1,0:T(8,128)(2,1)S(1)} %collective-permute-done.1.refs_1_.refs_3_), channel_id=1, source_target_pairs={{0,4},{2,6},{5,1},{7,3},{8,12},{10,14},{13,9},{15,11},{16,20},{18,... | collective-permute-start | bytes 3932168 | tf_op jit(solution)/shard_map/ppermute | solution.py:363
  18.0 3.8 %collective-permute-done.5.refs_8_.refs_10_ = bf16[1024,128]{1,0:T(8,128)(2,1)S(1)} collective-permute-done((bf16[1024,128]{1,0:T(8,128)(2,1)S(1)}, bf16[1024,128]{1,0:T(8,128)(2,1)S(1)}, u32[]{:S(2)}, u32[]{:S(2)}) %collective-permute-start.5) | collective-permute-done | bytes 262176 | tf_op jit(solution)/shard_map/ppermute | solution.py:363
  21.9 0.9 %collective-permute-done.6.refs_9_.refs_11_ = bf16[1024,128]{1,0:T(8,128)(2,1)S(1)} collective-permute-done((bf16[1024,128]{1,0:T(8,128)(2,1)S(1)}, bf16[1024,128]{1,0:T(8,128)(2,1)S(1)}, u32[]{:S(2)}, u32[]{:S(2)}) %collective-permute-start.6) | collective-permute-done | bytes 262176 | tf_op jit(solution)/shard_map/ppermute | solution.py:363
  22.8 1.2 %tile_product.4.refs_12_ = f32[1024,128]{1,0:T(8,128)S(1)} custom-call(s32[2,40]{1,0:T(2,128)S(1)} %collective-permute-done.refs_0_, bf16[5,8,128,128]{3,2,1,0:T(8,128)(2,1)S(1)} %collective-permute-done.1.refs_1_.refs_3_, bf16[1024,128]{1,0:T(8,128)(2,1)S(1)} %get-tuple-element.24.refs_3_.refs_2_.refs_5_.refs_4_.refs_7_, ...), custom_call_target="tpu_custom_call" | custom-call | flops 33554432000 | bytes 524288000 | tf_op jit(solution)/shard_map/tile_product/pallas_call | solution.py:204
  24.1 1.4 %collective-permute-start.7 = (s32[2,40]{1,0:T(2,128)S(1)}, s32[2,40]{1,0:T(2,128)S(1)}, u32[]{:S(2)}, u32[]{:S(2)}) collective-permute-start(s32[2,40]{1,0:T(2,128)S(1)} %collective-permute-done.refs_0_), channel_id=1, source_target_pairs={{0,4},{2,6},{5,1},{7,3},{8,12},{10,14},{13,9},{15,11},{16,20},{18,... | collective-permute-start | bytes 968 | tf_op jit(solution)/shard_map/ppermute | solution.py:363
  25.5 1.7 %collective-permute-done.7.refs_1_.refs_2_ = s32[2,40]{1,0:T(2,128)S(1)} collective-permute-done((s32[2,40]{1,0:T(2,128)S(1)}, s32[2,40]{1,0:T(2,128)S(1)}, u32[]{:S(2)}, u32[]{:S(2)}) %collective-permute-start.7) | collective-permute-done | bytes 352 | tf_op jit(solution)/shard_map/ppermute | solution.py:363
  27.3 1.4 %tile_product.5 = bf16[1024,128]{1,0:T(8,128)(2,1)S(1)} custom-call(s32[2,40]{1,0:T(2,128)S(1)} %slot_blocks.1.refs_6_.refs_0_.refs_1_, s32[2,40]{1,0:T(2,128)S(1)} %collective-permute-done.7.refs_1_.refs_2_, bf16[5,8,128,128]{3,2,1,0:T(8,128)(2,1)S(1)} %bitcast.6, bf16[5,8,128,128]{3,2,1,0:T(8,128)(2,1)S(1)} %collective-permute-done.8.refs_3_.refs_5_, ...), custom_call_target="tpu_custom_call" | custom-call | flops 167772160 | bytes 2621440 | tf_op jit(solution)/shard_map/tile_product/pallas_call | solution.py:204
  28.7 0.4 collective-permute-start.9
  29.1 0.1 halves.3
  29.3 13.3 %collective-permute-done.9 = bf16[1024,128]{1,0:T(8,128)(2,1)S(1)} collective-permute-done((bf16[1024,128]{1,0:T(8,128)(2,1)S(1)}, bf16[1024,128]{1,0:T(8,128)(2,1)S(1)}, u32[]{:S(2)}, u32[]{:S(2)}) %collective-permute-start.9) | collective-permute-done | bytes 262176 | tf_op jit(solution)/shard_map/ppermute | solution.py:363
  42.7 0.1 collective-permute-start.10
  42.8 1.5 %collective-permute-done.10.far_ref = bf16[1024,128]{1,0:T(8,128)(2,1)S(1)} collective-permute-done((bf16[1024,128]{1,0:T(8,128)(2,1)S(1)}, bf16[1024,128]{1,0:T(8,128)(2,1)S(1)}, u32[]{:S(2)}, u32[]{:S(2)}) %collective-permute-start.10) | collective-permute-done | bytes 262176 | tf_op jit(solution)/shard_map/ppermute | solution.py:363
  44.3 0.4 middle.1
  44.8 1.4 %collective-permute-start.13 = (bf16[1024,128]{1,0:T(8,128)(2,1)S(1)}, bf16[1024,128]{1,0:T(8,128)(2,1)S(1)}, u32[]{:S(2)}, u32[]{:S(2)}) collective-permute-start(bf16[1024,128]{1,0:T(8,128)(2,1)S(1)} %get-tuple-element.38.adj_ref.refs_6_), channel_id=1, source_target_pairs={{0,8},{1,9},{2,10},{3,11},{4,12},{5,13},{6,14},{7,15},{8,0},{9,1},... | collective-permute-start | bytes 786440 | tf_op jit(solution)/shard_map/ppermute | solution.py:363
  46.1 7.8 %collective-permute-done.12.refs_6_ = bf16[1024,128]{1,0:T(8,128)(2,1)S(1)} collective-permute-done((bf16[1024,128]{1,0:T(8,128)(2,1)S(1)}, bf16[1024,128]{1,0:T(8,128)(2,1)S(1)}, u32[]{:S(2)}, u32[]{:S(2)}) %collective-permute-start.12) | collective-permute-done | bytes 262176 | tf_op jit(solution)/shard_map/ppermute | solution.py:363
  54.0 1.7 %collective-permute-start.15 = (bf16[1024,128]{1,0:T(8,128)(2,1)S(1)}, bf16[1024,128]{1,0:T(8,128)(2,1)S(1)}, u32[]{:S(2)}, u32[]{:S(2)}) collective-permute-start(bf16[1024,128]{1,0:T(8,128)(2,1)S(1)} %collective-permute-done.13.after_ref.refs_7_), channel_id=1, source_target_pairs={{0,16},{1,17},{2,18},{3,19},{4,20},{5,21},{6,22},{7,23},{8,24},{9,... | collective-permute-start | bytes 786440 | tf_op jit(solution)/shard_map/ppermute | solution.py:363
  55.7 0.4 grad_block.1.refs_0_
  56.1 1.3 %collective-permute-start.14 = (bf16[1024,128]{1,0:T(8,128)(2,1)S(1)}, bf16[1024,128]{1,0:T(8,128)(2,1)S(1)}, u32[]{:S(2)}, u32[]{:S(2)}) collective-permute-start(bf16[1024,128]{1,0:T(8,128)(2,1)S(1)} %get-tuple-element.38.adj_ref.refs_6_), channel_id=1, source_target_pairs={{0,1},{2,3},{4,5},{6,7},{9,8},{11,10},{13,12},{15,14},{16,17},{18,... | collective-permute-start | bytes 786440 | tf_op jit(solution)/shard_map/ppermute | solution.py:363
  57.4 1.9 %collective-permute-start.16 = (bf16[1024,128]{1,0:T(8,128)(2,1)S(1)}, bf16[1024,128]{1,0:T(8,128)(2,1)S(1)}, u32[]{:S(2)}, u32[]{:S(2)}) collective-permute-start(bf16[1024,128]{1,0:T(8,128)(2,1)S(1)} %collective-permute-done.12.refs_6_), channel_id=1, source_target_pairs={{0,8},{1,9},{2,10},{3,11},{4,12},{5,13},{6,14},{7,15},{8,0},{9,1},... | collective-permute-start | bytes 786440 | tf_op jit(solution)/shard_map/ppermute | solution.py:363
  59.3 0.9 collective-permute-start.17
  60.2 1.1 %tile_product.6.refs_10_ = f32[1024,128]{1,0:T(8,128)S(1)} custom-call(s32[2,40]{1,0:T(2,128)S(1)} %collective-permute-done.refs_0_, s32[2,40]{1,0:T(2,128)S(1)} %slot_blocks.1.refs_6_.refs_0_.refs_1_, s32[2,40]{1,0:T(2,128)S(1)} %collective-permute-done.7.refs_1_.refs_2_, bf16[5,8,128,128]{3,2,1,0:T(8,128)(2,1)S(1)} %collective-permute-done.1.refs_1_.refs_3_, ...), custom_call_target="tpu_custom_call" | custom-call | flops 134217728 | bytes 1572864 | tf_op jit(solution)/shard_map/tile_product/pallas_call | solution.py:204
  61.3 5.3 %collective-permute-done.17.refs_11_.refs_1_ = bf16[256,128]{1,0:T(8,128)(2,1)S(1)} collective-permute-done((bf16[256,128]{1,0:T(8,128)(2,1)S(1)}, bf16[256,128]{1,0:T(8,128)(2,1)S(1)}, u32[]{:S(2)}, u32[]{:S(2)}) %collective-permute-start.17) | collective-permute-done | bytes 65568 | tf_op jit(solution)/shard_map/ppermute | solution.py:363
  66.6 1.4 %tile_product.7.refs_0_.refs_2_ = bf16[1024,128]{1,0:T(8,128)(2,1)S(1)} custom-call(s32[2,40]{1,0:T(2,128)S(1)} %collective-permute-done.refs_0_, s32[2,40]{1,0:T(2,128)S(1)} %slot_blocks.1.refs_6_.refs_0_.refs_1_, s32[2,40]{1,0:T(2,128)S(1)} %collective-permute-done.7.refs_1_.refs_2_, bf16[5,8,128,128]{3,2,1,0:T(8,128)(2,1)S(1)} %collective-permute-done.1.refs_1_.refs_3_, ...), custom_call_target="tpu_custom_call" | custom-call | flops 201326592 | bytes 2359296 | tf_op jit(solution)/shard_map/tile_product/pallas_call | solution.py:204
  68.2 2.4 %collective-permute-start.20 = (bf16[1024,128]{1,0:T(8,128)(2,1)S(1)}, bf16[1024,128]{1,0:T(8,128)(2,1)S(1)}, u32[]{:S(2)}, u32[]{:S(2)}) collective-permute-start(bf16[1024,128]{1,0:T(8,128)(2,1)S(1)} %get-tuple-element.41.refs_3_), channel_id=1, source_target_pairs={{1,4},{3,6},{4,1},{6,3},{9,12},{11,14},{12,9},{14,11},{17,20},{19,... | collective-permute-start | bytes 786440 | tf_op jit(solution)/shard_map/ppermute | solution.py:363
  70.7 1.8 %collective-permute-start.23 = (bf16[256,128]{1,0:T(8,128)(2,1)S(1)}, bf16[256,128]{1,0:T(8,128)(2,1)S(1)}, u32[]{:S(2)}, u32[]{:S(2)}) collective-permute-start(bf16[256,128]{1,0:T(8,128)(2,1)S(1)} %add_after.5.refs_0_), channel_id=1, source_target_pairs={{0,8},{1,9},{2,10},{3,11},{4,12},{5,13},{6,14},{7,15},{8,0},{9,1},... | collective-permute-start | bytes 196616 | tf_op jit(solution)/shard_map/ppermute | solution.py:363
  72.4 8.2 %collective-permute-done.18.refs_1_ = bf16[1024,128]{1,0:T(8,128)(2,1)S(1)} collective-permute-done((bf16[1024,128]{1,0:T(8,128)(2,1)S(1)}, bf16[1024,128]{1,0:T(8,128)(2,1)S(1)}, u32[]{:S(2)}, u32[]{:S(2)}) %collective-permute-start.18) | collective-permute-done | bytes 262176 | tf_op jit(solution)/shard_map/ppermute | solution.py:363
  80.6 1.1 %collective-permute-done.19.refs_2_.refs_4_ = bf16[1024,128]{1,0:T(8,128)(2,1)S(1)} collective-permute-done((bf16[1024,128]{1,0:T(8,128)(2,1)S(1)}, bf16[1024,128]{1,0:T(8,128)(2,1)S(1)}, u32[]{:S(2)}, u32[]{:S(2)}) %collective-permute-start.19) | collective-permute-done | bytes 262176 | tf_op jit(solution)/shard_map/ppermute | solution.py:363
  81.8 1.1 %collective-permute-done.20.refs_3_.refs_5_ = bf16[1024,128]{1,0:T(8,128)(2,1)S(1)} collective-permute-done((bf16[1024,128]{1,0:T(8,128)(2,1)S(1)}, bf16[1024,128]{1,0:T(8,128)(2,1)S(1)}, u32[]{:S(2)}, u32[]{:S(2)}) %collective-permute-start.20) | collective-permute-done | bytes 262176 | tf_op jit(solution)/shard_map/ppermute | solution.py:363
  83.0 0.7 collective-permute-start.24
  83.7 1.9 %collective-permute-start.22 = (bf16[1024,128]{1,0:T(8,128)(2,1)S(1)}, bf16[1024,128]{1,0:T(8,128)(2,1)S(1)}, u32[]{:S(2)}, u32[]{:S(2)}) collective-permute-start(bf16[1024,128]{1,0:T(8,128)(2,1)S(1)} %add_after.4.refs_2_.refs_0_), channel_id=1, source_target_pairs={{1,4},{3,6},{4,1},{6,3},{9,12},{11,14},{12,9},{14,11},{17,20},{19,... | collective-permute-start | bytes 786440 | tf_op jit(solution)/shard_map/ppermute | solution.py:363
  85.6 2.4 %collective-permute-done.24.refs_1_ = f32[256,128]{1,0:T(8,128)S(1)} collective-permute-done((f32[256,128]{1,0:T(8,128)S(1)}, f32[256,128]{1,0:T(8,128)S(1)}, u32[]{:S(2)}, u32[]{:S(2)}) %collective-permute-start.24) | collective-permute-done | bytes 131104 | tf_op jit(solution)/shard_map/ppermute | solution.py:363
  88.1 1.3 %collective-permute-done.25.refs_8_ = f32[256,128]{1,0:T(8,128)S(1)} collective-permute-done((f32[256,128]{1,0:T(8,128)S(1)}, f32[256,128]{1,0:T(8,128)S(1)}, u32[]{:S(2)}, u32[]{:S(2)}) %collective-permute-start.25) | collective-permute-done | bytes 131104 | tf_op jit(solution)/shard_map/ppermute | solution.py:363
  89.5 2.1 %collective-permute-done.21.refs_1_ = bf16[1024,128]{1,0:T(8,128)(2,1)S(1)} collective-permute-done((bf16[1024,128]{1,0:T(8,128)(2,1)S(1)}, bf16[1024,128]{1,0:T(8,128)(2,1)S(1)}, u32[]{:S(2)}, u32[]{:S(2)}) %collective-permute-start.21) | collective-permute-done | bytes 262176 | tf_op jit(solution)/shard_map/ppermute | solution.py:363
  91.5 1.4 %collective-permute-done.22.refs_2_ = bf16[1024,128]{1,0:T(8,128)(2,1)S(1)} collective-permute-done((bf16[1024,128]{1,0:T(8,128)(2,1)S(1)}, bf16[1024,128]{1,0:T(8,128)(2,1)S(1)}, u32[]{:S(2)}, u32[]{:S(2)}) %collective-permute-start.22) | collective-permute-done | bytes 262176 | tf_op jit(solution)/shard_map/ppermute | solution.py:363
  92.9 1.5 %final.1 = (bf16[1024,256]{1,0:T(8,128)(2,1)}, bf16[1024,256]{1,0:T(8,128)(2,1)}, f32[256,256]{1,0:T(8,128)}) custom-call(bf16[1024,128]{1,0:T(8,128)(2,1)S(1)} %add_after.4.refs_2_.refs_0_, bf16[1024,128]{1,0:T(8,128)(2,1)S(1)} %collective-permute-done.21.refs_1_, bf16[1024,128]{1,0:T(8,128)(2,1)S(1)} %collective-permute-done.22.refs_2_, ...), custom_call_target="tpu_custom_call" | custom-call | flops 134217728 | bytes 2097152 | tf_op jit(solution)/shard_map/final/pallas_call | solution.py:341
  (32 shorter events, 0.7 us)
Async XLA Ops:
  0.6 16.1 %collective-permute-start.1 = (bf16[5,8,128,128]{3,2,1,0:T(8,128)(2,1)}, bf16[5,8,128,128]{3,2,1,0:T(8,128)(2,1)S(1)}, u32[]{:S(2)}, u32[]{:S(2)}) collective-permute-start(bf16[5,8,128,128]{3,2,1,0:T(8,128)(2,1)} %bitcast.5), channel_id=1, source_target_pairs={{0,4},{1,0},{2,6},{3,2},{4,5},{5,1},{6,7},{7,3},{8,12},{9,8},{10,1... | collective-permute-start | bytes 3932168 | tf_op jit(solution)/shard_map/ppermute | solution.py:363
  1.1 1.0 %copy-start.1 = (bf16[1024,256]{1,0:T(8,128)(2,1)S(1)}, bf16[1024,256]{1,0:T(8,128)(2,1)}, u32[]{:S(2)}) copy-start(bf16[1024,256]{1,0:T(8,128)(2,1)} %x_ref.2) | copy-start | bytes 1572868
  2.3 9.0 %collective-permute-start.2 = (bf16[1024,128]{1,0:T(8,128)(2,1)S(1)}, bf16[1024,128]{1,0:T(8,128)(2,1)S(1)}, u32[]{:S(2)}, u32[]{:S(2)}) collective-permute-start(bf16[1024,128]{1,0:T(8,128)(2,1)S(1)} %get-tuple-element.24.refs_3_.refs_2_.refs_5_.refs_4_.refs_7_), channel_id=1, source_target_pairs={{0,8},{1,17},{2,10},{3,19},{5,13},{7,15},{8,0},{10,2},{12,28},{13,... | collective-permute-start | bytes 786440 | tf_op jit(solution)/shard_map/ppermute | solution.py:363
  5.7 7.7 %collective-permute-start.3 = (bf16[1024,128]{1,0:T(8,128)(2,1)S(1)}, bf16[1024,128]{1,0:T(8,128)(2,1)S(1)}, u32[]{:S(2)}, u32[]{:S(2)}) collective-permute-start(bf16[1024,128]{1,0:T(8,128)(2,1)S(1)} %get-tuple-element.25), channel_id=1, source_target_pairs={{0,12},{1,21},{2,14},{3,23},{5,9},{7,11},{8,4},{10,6},{12,24},{13,... | collective-permute-start | bytes 786440 | tf_op jit(solution)/shard_map/ppermute | solution.py:363
  8.5 4.9 %collective-permute-start.4 = (bf16[1024,128]{1,0:T(8,128)(2,1)S(1)}, bf16[1024,128]{1,0:T(8,128)(2,1)S(1)}, u32[]{:S(2)}, u32[]{:S(2)}) collective-permute-start(bf16[1024,128]{1,0:T(8,128)(2,1)S(1)} %get-tuple-element.25), channel_id=1, source_target_pairs={{0,4},{1,5},{2,6},{3,7},{4,0},{5,1},{6,2},{7,3},{8,12},{9,13},{10,... | collective-permute-start | bytes 786440 | tf_op jit(solution)/shard_map/ppermute | solution.py:363
  9.3 0.7 copy-start.4
  13.5 8.3 %collective-permute-start.5 = (bf16[1024,128]{1,0:T(8,128)(2,1)S(1)}, bf16[1024,128]{1,0:T(8,128)(2,1)S(1)}, u32[]{:S(2)}, u32[]{:S(2)}) collective-permute-start(bf16[1024,128]{1,0:T(8,128)(2,1)S(1)} %get-tuple-element.27), channel_id=1, source_target_pairs={{0,16},{1,17},{2,18},{3,19},{4,20},{5,21},{6,22},{7,23},{8,24},{9,... | collective-permute-start | bytes 786440 | tf_op jit(solution)/shard_map/ppermute | solution.py:363
  14.1 13.1 %copy-start = (bf16[1,5,8,128,128]{4,3,2,1,0:T(8,128)(2,1)S(1)}, bf16[1,5,8,128,128]{4,3,2,1,0:T(8,128)(2,1)}, u32[]{:S(2)}) copy-start(bf16[1,5,8,128,128]{4,3,2,1,0:T(8,128)(2,1)} %param.9) | copy-start | bytes 3932164
  14.2 8.7 %collective-permute-start.6 = (bf16[1024,128]{1,0:T(8,128)(2,1)S(1)}, bf16[1024,128]{1,0:T(8,128)(2,1)S(1)}, u32[]{:S(2)}, u32[]{:S(2)}) collective-permute-start(bf16[1024,128]{1,0:T(8,128)(2,1)S(1)} %get-tuple-element.28), channel_id=1, source_target_pairs={{0,8},{1,9},{2,10},{3,11},{4,12},{5,13},{6,14},{7,15},{8,0},{9,1},... | collective-permute-start | bytes 786440 | tf_op jit(solution)/shard_map/ppermute | solution.py:363
  15.6 2.4 %collective-permute-start = (s32[2,40]{1,0:T(2,128)S(1)}, s32[2,40]{1,0:T(2,128)S(1)}, u32[]{:S(2)}, u32[]{:S(2)}) collective-permute-start(s32[2,40]{1,0:T(2,128)S(1)} %slot_blocks.1.refs_6_.refs_0_.refs_1_), channel_id=1, source_target_pairs={{0,4},{1,0},{2,6},{3,2},{4,5},{5,1},{6,7},{7,3},{8,12},{9,8},{10,1... | collective-permute-start | bytes 968 | tf_op jit(solution)/shard_map/ppermute | solution.py:363
  16.7 10.5 %collective-permute-start.8 = (bf16[5,8,128,128]{3,2,1,0:T(8,128)(2,1)S(1)}, bf16[5,8,128,128]{3,2,1,0:T(8,128)(2,1)S(1)}, u32[]{:S(2)}, u32[]{:S(2)}) collective-permute-start(bf16[5,8,128,128]{3,2,1,0:T(8,128)(2,1)S(1)} %collective-permute-done.1.refs_1_.refs_3_), channel_id=1, source_target_pairs={{0,4},{2,6},{5,1},{7,3},{8,12},{10,14},{13,9},{15,11},{16,20},{18,... | collective-permute-start | bytes 3932168 | tf_op jit(solution)/shard_map/ppermute | solution.py:363
  24.1 5.0 %copy-start.2 = (bf16[1024,256]{1,0:T(8,128)(2,1)S(1)}, bf16[1024,256]{1,0:T(8,128)(2,1)}, u32[]{:S(2)}) copy-start(bf16[1024,256]{1,0:T(8,128)(2,1)} %x_ref.3) | copy-start | bytes 1572868
  24.1 3.2 %collective-permute-start.7 = (s32[2,40]{1,0:T(2,128)S(1)}, s32[2,40]{1,0:T(2,128)S(1)}, u32[]{:S(2)}, u32[]{:S(2)}) collective-permute-start(s32[2,40]{1,0:T(2,128)S(1)} %collective-permute-done.refs_0_), channel_id=1, source_target_pairs={{0,4},{2,6},{5,1},{7,3},{8,12},{10,14},{13,9},{15,11},{16,20},{18,... | collective-permute-start | bytes 968 | tf_op jit(solution)/shard_map/ppermute | solution.py:363
  28.7 15.6 %copy-start.3 = (bf16[256,256]{1,0:T(8,128)(2,1)S(1)}, bf16[256,256]{1,0:T(8,128)(2,1)}, u32[]{:S(2)}) copy-start(bf16[256,256]{1,0:T(8,128)(2,1)} %refs_6_.1) | copy-start | bytes 393220
  28.7 13.9 %collective-permute-start.9 = (bf16[1024,128]{1,0:T(8,128)(2,1)S(1)}, bf16[1024,128]{1,0:T(8,128)(2,1)S(1)}, u32[]{:S(2)}, u32[]{:S(2)}) collective-permute-start(bf16[1024,128]{1,0:T(8,128)(2,1)S(1)} %tile_product.5), channel_id=1, source_target_pairs={{0,2},{1,3},{2,0},{3,1},{4,6},{5,7},{6,4},{7,5},{8,10},{9,11},{10,... | collective-permute-start | bytes 786440 | tf_op jit(solution)/shard_map/ppermute | solution.py:363
  29.2 13.6 %collective-permute-start.11 = (bf16[1024,128]{1,0:T(8,128)(2,1)S(1)}, bf16[1024,128]{1,0:T(8,128)(2,1)S(1)}, u32[]{:S(2)}, u32[]{:S(2)}) collective-permute-start(bf16[1024,128]{1,0:T(8,128)(2,1)S(1)} %get-tuple-element.32), channel_id=1, source_target_pairs={{0,4},{1,5},{2,6},{3,7},{4,0},{5,1},{6,2},{7,3},{8,12},{9,13},{10,... | collective-permute-start | bytes 786440 | tf_op jit(solution)/shard_map/ppermute | solution.py:363
  42.7 1.6 %collective-permute-start.10 = (bf16[1024,128]{1,0:T(8,128)(2,1)S(1)}, bf16[1024,128]{1,0:T(8,128)(2,1)S(1)}, u32[]{:S(2)}, u32[]{:S(2)}) collective-permute-start(bf16[1024,128]{1,0:T(8,128)(2,1)S(1)} %add_convert_fusion.near_ref), channel_id=1, source_target_pairs={{0,4},{1,5},{2,6},{3,7},{4,0},{5,1},{6,2},{7,3},{8,12},{9,13},{10,... | collective-permute-start | bytes 786440 | tf_op jit(solution)/shard_map/ppermute | solution.py:363
  44.7 9.3 %collective-permute-start.12 = (bf16[1024,128]{1,0:T(8,128)(2,1)S(1)}, bf16[1024,128]{1,0:T(8,128)(2,1)S(1)}, u32[]{:S(2)}, u32[]{:S(2)}) collective-permute-start(bf16[1024,128]{1,0:T(8,128)(2,1)S(1)} %get-tuple-element.38.adj_ref.refs_6_), channel_id=1, source_target_pairs={{0,17},{1,0},{2,19},{3,2},{4,21},{5,4},{6,23},{7,6},{8,9},{9,24},{... | collective-permute-start | bytes 786440 | tf_op jit(solution)/shard_map/ppermute | solution.py:363
  44.8 9.2 %collective-permute-start.13 = (bf16[1024,128]{1,0:T(8,128)(2,1)S(1)}, bf16[1024,128]{1,0:T(8,128)(2,1)S(1)}, u32[]{:S(2)}, u32[]{:S(2)}) collective-permute-start(bf16[1024,128]{1,0:T(8,128)(2,1)S(1)} %get-tuple-element.38.adj_ref.refs_6_), channel_id=1, source_target_pairs={{0,8},{1,9},{2,10},{3,11},{4,12},{5,13},{6,14},{7,15},{8,0},{9,1},... | collective-permute-start | bytes 786440 | tf_op jit(solution)/shard_map/ppermute | solution.py:363
  54.0 12.6 %collective-permute-start.15 = (bf16[1024,128]{1,0:T(8,128)(2,1)S(1)}, bf16[1024,128]{1,0:T(8,128)(2,1)S(1)}, u32[]{:S(2)}, u32[]{:S(2)}) collective-permute-start(bf16[1024,128]{1,0:T(8,128)(2,1)S(1)} %collective-permute-done.13.after_ref.refs_7_), channel_id=1, source_target_pairs={{0,16},{1,17},{2,18},{3,19},{4,20},{5,21},{6,22},{7,23},{8,24},{9,... | collective-permute-start | bytes 786440 | tf_op jit(solution)/shard_map/ppermute | solution.py:363
  56.1 10.5 %collective-permute-start.14 = (bf16[1024,128]{1,0:T(8,128)(2,1)S(1)}, bf16[1024,128]{1,0:T(8,128)(2,1)S(1)}, u32[]{:S(2)}, u32[]{:S(2)}) collective-permute-start(bf16[1024,128]{1,0:T(8,128)(2,1)S(1)} %get-tuple-element.38.adj_ref.refs_6_), channel_id=1, source_target_pairs={{0,1},{2,3},{4,5},{6,7},{9,8},{11,10},{13,12},{15,14},{16,17},{18,... | collective-permute-start | bytes 786440 | tf_op jit(solution)/shard_map/ppermute | solution.py:363
  57.4 9.2 %collective-permute-start.16 = (bf16[1024,128]{1,0:T(8,128)(2,1)S(1)}, bf16[1024,128]{1,0:T(8,128)(2,1)S(1)}, u32[]{:S(2)}, u32[]{:S(2)}) collective-permute-start(bf16[1024,128]{1,0:T(8,128)(2,1)S(1)} %collective-permute-done.12.refs_6_), channel_id=1, source_target_pairs={{0,8},{1,9},{2,10},{3,11},{4,12},{5,13},{6,14},{7,15},{8,0},{9,1},... | collective-permute-start | bytes 786440 | tf_op jit(solution)/shard_map/ppermute | solution.py:363
  59.3 7.3 %collective-permute-start.17 = (bf16[256,128]{1,0:T(8,128)(2,1)S(1)}, bf16[256,128]{1,0:T(8,128)(2,1)S(1)}, u32[]{:S(2)}, u32[]{:S(2)}) collective-permute-start(bf16[256,128]{1,0:T(8,128)(2,1)S(1)} %grad_block.1.refs_0_), channel_id=1, source_target_pairs={{0,1},{1,0},{2,3},{3,2},{4,5},{5,4},{6,7},{7,6},{8,9},{9,8},{10,11... | collective-permute-start | bytes 196616 | tf_op jit(solution)/shard_map/ppermute | solution.py:363
  68.1 12.6 %collective-permute-start.18 = (bf16[1024,128]{1,0:T(8,128)(2,1)S(1)}, bf16[1024,128]{1,0:T(8,128)(2,1)S(1)}, u32[]{:S(2)}, u32[]{:S(2)}) collective-permute-start(bf16[1024,128]{1,0:T(8,128)(2,1)S(1)} %tile_product.7.refs_0_.refs_2_), channel_id=1, source_target_pairs={{0,2},{1,3},{2,0},{3,1},{4,6},{5,7},{6,4},{7,5},{8,10},{9,11},{10,... | collective-permute-start | bytes 786440 | tf_op jit(solution)/shard_map/ppermute | solution.py:363
  68.1 13.6 %collective-permute-start.19 = (bf16[1024,128]{1,0:T(8,128)(2,1)S(1)}, bf16[1024,128]{1,0:T(8,128)(2,1)S(1)}, u32[]{:S(2)}, u32[]{:S(2)}) collective-permute-start(bf16[1024,128]{1,0:T(8,128)(2,1)S(1)} %get-tuple-element.41.refs_3_), channel_id=1, source_target_pairs={{0,1},{1,5},{2,3},{3,7},{4,0},{5,4},{6,2},{7,6},{8,9},{9,13},{10,1... | collective-permute-start | bytes 786440 | tf_op jit(solution)/shard_map/ppermute | solution.py:363
  68.2 14.7 %collective-permute-start.20 = (bf16[1024,128]{1,0:T(8,128)(2,1)S(1)}, bf16[1024,128]{1,0:T(8,128)(2,1)S(1)}, u32[]{:S(2)}, u32[]{:S(2)}) collective-permute-start(bf16[1024,128]{1,0:T(8,128)(2,1)S(1)} %get-tuple-element.41.refs_3_), channel_id=1, source_target_pairs={{1,4},{3,6},{4,1},{6,3},{9,12},{11,14},{12,9},{14,11},{17,20},{19,... | collective-permute-start | bytes 786440 | tf_op jit(solution)/shard_map/ppermute | solution.py:363
  70.7 12.3 %collective-permute-start.23 = (bf16[256,128]{1,0:T(8,128)(2,1)S(1)}, bf16[256,128]{1,0:T(8,128)(2,1)S(1)}, u32[]{:S(2)}, u32[]{:S(2)}) collective-permute-start(bf16[256,128]{1,0:T(8,128)(2,1)S(1)} %add_after.5.refs_0_), channel_id=1, source_target_pairs={{0,8},{1,9},{2,10},{3,11},{4,12},{5,13},{6,14},{7,15},{8,0},{9,1},... | collective-permute-start | bytes 196616 | tf_op jit(solution)/shard_map/ppermute | solution.py:363
  83.0 5.0 %collective-permute-start.24 = (f32[256,128]{1,0:T(8,128)S(1)}, f32[256,128]{1,0:T(8,128)S(1)}, u32[]{:S(2)}, u32[]{:S(2)}) collective-permute-start(f32[256,128]{1,0:T(8,128)S(1)} %add_after.6.refs_0_), channel_id=1, source_target_pairs={{0,16},{1,17},{2,18},{3,19},{4,20},{5,21},{6,22},{7,23},{8,24},{9,... | collective-permute-start | bytes 393224 | tf_op jit(solution)/shard_map/ppermute | solution.py:363
  83.7 7.8 %collective-permute-start.21 = (bf16[1024,128]{1,0:T(8,128)(2,1)S(1)}, bf16[1024,128]{1,0:T(8,128)(2,1)S(1)}, u32[]{:S(2)}, u32[]{:S(2)}) collective-permute-start(bf16[1024,128]{1,0:T(8,128)(2,1)S(1)} %add_after.4.refs_2_.refs_0_), channel_id=1, source_target_pairs={{0,1},{1,5},{2,3},{3,7},{4,0},{5,4},{6,2},{7,6},{8,9},{9,13},{10,1... | collective-permute-start | bytes 786440 | tf_op jit(solution)/shard_map/ppermute | solution.py:363
  83.7 9.2 %collective-permute-start.22 = (bf16[1024,128]{1,0:T(8,128)(2,1)S(1)}, bf16[1024,128]{1,0:T(8,128)(2,1)S(1)}, u32[]{:S(2)}, u32[]{:S(2)}) collective-permute-start(bf16[1024,128]{1,0:T(8,128)(2,1)S(1)} %add_after.4.refs_2_.refs_0_), channel_id=1, source_target_pairs={{1,4},{3,6},{4,1},{6,3},{9,12},{11,14},{12,9},{14,11},{17,20},{19,... | collective-permute-start | bytes 786440 | tf_op jit(solution)/shard_map/ppermute | solution.py:363
  88.1 1.4 %collective-permute-start.25 = (f32[256,128]{1,0:T(8,128)S(1)}, f32[256,128]{1,0:T(8,128)S(1)}, u32[]{:S(2)}, u32[]{:S(2)}) collective-permute-start(f32[256,128]{1,0:T(8,128)S(1)} %add_after.7.refs_7_), channel_id=1, source_target_pairs={{0,4},{1,5},{2,6},{3,7},{4,0},{5,1},{6,2},{7,3},{8,12},{9,13},{10,... | collective-permute-start | bytes 393224 | tf_op jit(solution)/shard_map/ppermute | solution.py:363

commit v10 on v9

--- a/solution.py
+++ b/solution.py
@@ -8,7 +8,7 @@
 from jax.sharding import PartitionSpec as P
 
 AXES = ("rows", "rep")
-WEIGH = 200
+WEIGH = 75
 
 
 def route(shape, move):
@@ -310,45 +310,68 @@
     )(*values, *after)
 
 
-def final_kernel(*refs):
-    back, act, (w_ref, grad_ref, rest_ref), outs = refs[:3], refs[3:6], refs[6:9], refs[9:]
-    out_ref, act_ref, grad_out_ref = outs
+def half_columns(half):
+    j, _, _ = place()
+    near = pl.ds(pl.multiple_of(j * half, half), half)
+    return near, pl.ds(pl.multiple_of((1 - j) * half, half), half)
+
+
+def near_and_far(parts):
     j, _, p = place()
-    half = back[0].shape[1]
-    near_cols = pl.ds(pl.multiple_of(j * half, half), half)
-    far_cols = pl.ds(pl.multiple_of((1 - j) * half, half), half)
-
-    def halves_of(parts):
-        own, one, two = parts
-        near = jnp.where(j == p, own[...], one[...])
-        return near, jnp.where(j == p, one[...], two[...])
-
-    near, far = halves_of(back)
+    own, one, two = parts
+    near = jnp.where(j == p, own[...], one[...])
+    return near, jnp.where(j == p, one[...], two[...])
+
+
+def gather_kernel(own_ref, one_ref, two_ref, grad_ref, rest_ref, act_ref, grad_out_ref):
+    near_cols, far_cols = half_columns(own_ref.shape[1])
+    near, far = near_and_far((own_ref, one_ref, two_ref))
+    act_ref[:, near_cols] = near
+    act_ref[:, far_cols] = far
+    grad_out_ref[:, near_cols] = grad_ref[...]
+    grad_out_ref[:, far_cols] = rest_ref[...]
+
+
+def gather_halves(act, grad, rest):
+    vmem = pl.BlockSpec(memory_space=pltpu.VMEM)
+    rows, width = act[0].shape
+    return pl.pallas_call(
+        gather_kernel,
+        out_shape=(
+            jax.ShapeDtypeStruct((rows, 2 * width), act[0].dtype),
+            jax.ShapeDtypeStruct((2 * width, 2 * width), grad.dtype),
+        ),
+        in_specs=[vmem] * 5,
+        out_specs=(vmem, vmem),
+        compiler_params=pltpu.CompilerParams(vmem_limit_bytes=8 * 1024 * 1024),
+        name="gather_halves",
+    )(*act, grad, rest)
+
+
+def final_kernel(own_ref, one_ref, two_ref, w_ref, out_ref):
+    near_cols, far_cols = half_columns(own_ref.shape[1])
+    near, far = near_and_far((own_ref, one_ref, two_ref))
     dims = (((1,), (1,)), ((), ()))
     total = lax.dot_general(near, w_ref[:, near_cols], dims, preferred_element_type=jnp.float32)
     total += lax.dot_general(far, w_ref[:, far_cols], dims, preferred_element_type=jnp.float32)
     out_ref[...] = total.astype(out_ref.dtype)
-    act_ref[:, near_cols], act_ref[:, far_cols] = halves_of(act)
-    grad_out_ref[:, near_cols] = grad_ref[...]
-    grad_out_ref[:, far_cols] = rest_ref[...]
-
-
-def final(back, act, weight, grad, rest):
+
+
+def final(back, weight):
     vmem = pl.BlockSpec(memory_space=pltpu.VMEM)
     rows = back[0].shape[0]
     wide = weight.shape[0]
-    whole = jax.ShapeDtypeStruct((rows, wide), jnp.bfloat16)
     return pl.pallas_call(
         final_kernel,
-        out_shape=(whole, whole, jax.ShapeDtypeStruct(weight.shape, jnp.float32)),
-        in_specs=[vmem] * 9,
-        out_specs=(vmem,) * 3,
+        out_shape=jax.ShapeDtypeStruct((rows, wide), jnp.bfloat16),
+        in_specs=[vmem] * 4,
+        out_specs=vmem,
         compiler_params=pltpu.CompilerParams(vmem_limit_bytes=8 * 1024 * 1024),
         cost_estimate=pl.CostEstimate(
             flops=2 * rows * wide * wide, bytes_accessed=8 * rows * wide, transcendentals=0
         ),
         name="final",
-    )(*back, *act, weight, grad, rest)
+    )(*back, weight)
 
 
 def per_device(node_feats, weight, cotangent, tile_values, tile_coords, tile_counts):
@@ -422,6 +445,8 @@
     meta_b = send(meta, to_home)
     first, one, two = lax.optimization_barrier((first, one, two))
     other_first = send(first, home_to_sibling)
+    meta_later, second, far = lax.optimization_barrier((meta_b, second, far))
+    meta_far = send(meta_later, home_to_sibling)
     set_first = [(None, (meta_b, first))]
     panels = [
         ("self", [("home", mine), ("away", swapped)]),
@@ -431,8 +456,6 @@
         ("far", [(None, far)]),
     ]
     part = tile_product(panels, [set_first], jnp.float32, weigh=WEIGH)
-    meta_later, part = lax.optimization_barrier((meta_b, part))
-    meta_far = send(meta_later, home_to_sibling)
     set_rest = [("home", (meta, own)), ("away", (meta_far, other_first))]
     part = tile_product(panels, [set_rest], jnp.bfloat16, part)
 
@@ -451,16 +474,16 @@
     )
     adj_later, near_one, direct = lax.optimization_barrier((adj, near_one, direct))
     second = send(direct if four else adj_later, to_second)
-    grad = grad_block(scale, near, far_half, adj, direct)
-    adj_later, grad = lax.optimization_barrier((adj_later, grad))
+    grad = grad_block(scale, near, far_half, adj, adj)
+    grad_got = send(grad, lambda c, j, z: (c, j, z ^ 1))
+    adj_soon, grad_got = lax.optimization_barrier((adj, grad_got))
     far = send(near_one, to_far)
     near_choice = [("still", near_one)]
     if four:
         near_two = send(
-            adj_later, lambda c, j, z: None if (c + z) % 2 else (c, j, z ^ 1)
+            adj_soon, lambda c, j, z: None if (c + z) % 2 else (c, j, z ^ 1)
         )
         near_choice.append(("relay", near_two))
-    grad_got = send(grad, lambda c, j, z: (c, j, z ^ 1))
     panels = [("self", [(None, adj)]), ("direct", [(None, direct)])]
     back_part = tile_product(panels, [set_first, set_rest], jnp.float32)
     panels = [("near", near_choice), ("second", [(None, second)]), ("far", [(None, far)])]
@@ -475,17 +498,18 @@
 
     act_later, back_part = lax.optimization_barrier((act, back_part))
     act_parts = [act, *deliver(act_later)]
-    back = add_after([back_part, send(back_part, across)], jnp.bfloat16, *act_parts[1:])
-    back_parts = [back, *deliver(back)]
     grad = add_after([grad, grad_got], jnp.bfloat16, back_part)
     step = 1
     while step < shape[0]:
         got = send(grad, lambda c, j, z, s=step: (c ^ s, j, z))
-        grad = add_after([grad, got], jnp.float32, back)
         step *= 2
-    input_grad, activated, weight_grad = final(
-        back_parts, act_parts, weight, grad, send(grad, sibling)
-    )
+        if step < shape[0]:
+            grad = add_after([grad, got], jnp.bfloat16)
+    back = add_after([back_part, send(back_part, across)], jnp.bfloat16, got)
+    back_parts = [back, *deliver(back)]
+    grad = add_after([grad, got], jnp.float32, back)
+    activated, weight_grad = gather_halves(act_parts, grad, send(grad, sibling))
+    input_grad = final(back_parts, weight)
     return (activated, input_grad, weight_grad)
 
 

time: 94.8 us -> 93.6 us (0.987)
  the two profiles are of different devices: /device:TPU:24 before, /device:TPU:1 now
where the time goes in v10:
time: 93.6 us; the launch traced here: 93.3 us
  starting transfers between devices  43.2 us (46%)
  waiting for transfers between devices  36.7 us (39%)
  Pallas kernels  9.99 us (11%)
  local copies, waits for them, and re-layouts  2.41 us (3%)
    ppermute x26, starting transfers between devices, send(): return lax.ppermute(value, AXES, route(shape, move))  43.2 us
    ppermute x26, waiting for transfers between devices, send(): return lax.ppermute(value, AXES, route(shape, move))  36.7 us
    pallas_call x4, Pallas kernels, tile_product(): pl.pallas_call(functools.partial(tile_kernel, kinds, cases, [[case for ca...  5.23 us
    unnamed x11, local copies, waits for them, and re-layouts  2.4 us
  transfers between devices with their start and end apart: 26, of which 15 were waited for; matrix products, arithmetic and copies ran while one was open for 1% of the time, Pallas kernels for 6%

profile of v10, /device:TPU:1, one launch (start us, length us, event | category | flops | bytes accessed | tf_op | source)
XLA Modules:
  0.0 93.3 jit_solution(8126500716042147054)
XLA Ops:
  0.6 2.2 %collective-permute-start.7 = (bf16[5,8,128,128]{3,2,1,0:T(8,128)(2,1)}, bf16[5,8,128,128]{3,2,1,0:T(8,128)(2,1)S(1)}, u32[]{:S(2)}, u32[]{:S(2)}) collective-permute-start(bf16[5,8,128,128]{3,2,1,0:T(8,128)(2,1)} %bitcast.5), channel_id=1, source_target_pairs={{0,4},{1,0},{2,6},{3,2},{4,5},{5,1},{6,7},{7,3},{8,12},{9,8},{10,1... | collective-permute-start | bytes 3932168 | tf_op jit(solution)/shard_map/ppermute | solution.py:386
  2.8 1.0 %copy-done.1 = bf16[1024,256]{1,0:T(8,128)(2,1)S(1)} copy-done((bf16[1024,256]{1,0:T(8,128)(2,1)S(1)}, bf16[1024,256]{1,0:T(8,128)(2,1)}, u32[]{:S(2)}) %copy-start.1) | copy-done | bytes 524312
  4.0 0.7 collective-permute-start.1
  4.7 1.3 %collective-permute-start.2 = (bf16[1024,128]{1,0:T(8,128)(2,1)S(1)}, bf16[1024,128]{1,0:T(8,128)(2,1)S(1)}, u32[]{:S(2)}, u32[]{:S(2)}) collective-permute-start(bf16[1024,128]{1,0:T(8,128)(2,1)S(1)} %get-tuple-element.24), channel_id=1, source_target_pairs={{0,12},{1,21},{2,14},{3,23},{5,9},{7,11},{8,4},{10,6},{12,24},{13,... | collective-permute-start | bytes 786440 | tf_op jit(solution)/shard_map/ppermute | solution.py:386
  6.0 4.8 %collective-permute-start.3 = (bf16[1024,128]{1,0:T(8,128)(2,1)S(1)}, bf16[1024,128]{1,0:T(8,128)(2,1)S(1)}, u32[]{:S(2)}, u32[]{:S(2)}) collective-permute-start(bf16[1024,128]{1,0:T(8,128)(2,1)S(1)} %get-tuple-element.24), channel_id=1, source_target_pairs={{0,4},{1,5},{2,6},{3,7},{4,0},{5,1},{6,2},{7,3},{8,12},{9,13},{10,... | collective-permute-start | bytes 786440 | tf_op jit(solution)/shard_map/ppermute | solution.py:386
  10.7 0.7 copy.12
  11.4 0.7 copy-done.4
  12.1 1.3 %slot_blocks.1.refs_6_.refs_0_.refs_1_ = s32[2,40]{1,0:T(2,128)S(1)} custom-call(s32[2,5,8]{2,1,0:T(8,128)S(1)} %copy.10.coords_ref, s32[5]{0:T(128)S(1)} %bitcast.9), custom_call_target="tpu_custom_call" | custom-call | tf_op jit(solution)/shard_map/slot_blocks/pallas_call | solution.py:133
  13.6 1.8 %collective-permute-start.4 = (bf16[1024,128]{1,0:T(8,128)(2,1)S(1)}, bf16[1024,128]{1,0:T(8,128)(2,1)S(1)}, u32[]{:S(2)}, u32[]{:S(2)}) collective-permute-start(bf16[1024,128]{1,0:T(8,128)(2,1)S(1)} %get-tuple-element.25), channel_id=1, source_target_pairs={{0,16},{1,17},{2,18},{3,19},{4,20},{5,21},{6,22},{7,23},{8,24},{9,... | collective-permute-start | bytes 786440 | tf_op jit(solution)/shard_map/ppermute | solution.py:386
  15.5 1.3 %collective-permute-start.5 = (bf16[1024,128]{1,0:T(8,128)(2,1)S(1)}, bf16[1024,128]{1,0:T(8,128)(2,1)S(1)}, u32[]{:S(2)}, u32[]{:S(2)}) collective-permute-start(bf16[1024,128]{1,0:T(8,128)(2,1)S(1)} %get-tuple-element.26), channel_id=1, source_target_pairs={{0,8},{1,9},{2,10},{3,11},{4,12},{5,13},{6,14},{7,15},{8,0},{9,1},... | collective-permute-start | bytes 786440 | tf_op jit(solution)/shard_map/ppermute | solution.py:386
  16.7 1.0 %collective-permute-done.7.refs_1_.refs_3_ = bf16[5,8,128,128]{3,2,1,0:T(8,128)(2,1)S(1)} collective-permute-done((bf16[5,8,128,128]{3,2,1,0:T(8,128)(2,1)}, bf16[5,8,128,128]{3,2,1,0:T(8,128)(2,1)S(1)}, u32[]{:S(2)}, u32[]{:S(2)}) %collective-permute-start.7) | collective-permute-done | bytes 1310752 | tf_op jit(solution)/shard_map/ppermute | solution.py:386
  17.7 1.3 %collective-permute-start.8 = (bf16[5,8,128,128]{3,2,1,0:T(8,128)(2,1)S(1)}, bf16[5,8,128,128]{3,2,1,0:T(8,128)(2,1)S(1)}, u32[]{:S(2)}, u32[]{:S(2)}) collective-permute-start(bf16[5,8,128,128]{3,2,1,0:T(8,128)(2,1)S(1)} %collective-permute-done.7.refs_1_.refs_3_), channel_id=1, source_target_pairs={{0,4},{2,6},{5,1},{7,3},{8,12},{10,14},{13,9},{15,11},{16,20},{18,... | collective-permute-start | bytes 3932168 | tf_op jit(solution)/shard_map/ppermute | solution.py:386
  19.0 2.2 %collective-permute-start = (s32[2,40]{1,0:T(2,128)S(1)}, s32[2,40]{1,0:T(2,128)S(1)}, u32[]{:S(2)}, u32[]{:S(2)}) collective-permute-start(s32[2,40]{1,0:T(2,128)S(1)} %slot_blocks.1.refs_6_.refs_0_.refs_1_), channel_id=1, source_target_pairs={{0,4},{1,0},{2,6},{3,2},{4,5},{5,1},{6,7},{7,3},{8,12},{9,8},{10,1... | collective-permute-start | bytes 968 | tf_op jit(solution)/shard_map/ppermute | solution.py:386
  21.2 2.2 %collective-permute-done.refs_0_ = s32[2,40]{1,0:T(2,128)S(1)} collective-permute-done((s32[2,40]{1,0:T(2,128)S(1)}, s32[2,40]{1,0:T(2,128)S(1)}, u32[]{:S(2)}, u32[]{:S(2)}) %collective-permute-start) | collective-permute-done | bytes 352 | tf_op jit(solution)/shard_map/ppermute | solution.py:386
  23.4 1.3 %collective-permute-start.6 = (s32[2,40]{1,0:T(2,128)S(1)}, s32[2,40]{1,0:T(2,128)S(1)}, u32[]{:S(2)}, u32[]{:S(2)}) collective-permute-start(s32[2,40]{1,0:T(2,128)S(1)} %collective-permute-done.refs_0_), channel_id=1, source_target_pairs={{0,4},{2,6},{5,1},{7,3},{8,12},{10,14},{13,9},{15,11},{16,20},{18,... | collective-permute-start | bytes 968 | tf_op jit(solution)/shard_map/ppermute | solution.py:386
  24.7 1.2 %tile_product.4.refs_12_ = f32[1024,128]{1,0:T(8,128)S(1)} custom-call(s32[2,40]{1,0:T(2,128)S(1)} %collective-permute-done.refs_0_, bf16[5,8,128,128]{3,2,1,0:T(8,128)(2,1)S(1)} %collective-permute-done.7.refs_1_.refs_3_, bf16[1024,128]{1,0:T(8,128)(2,1)S(1)} %get-tuple-element.23.refs_3_.refs_2_.refs_5_.refs_4_.refs_7_, ...), custom_call_target="tpu_custom_call" | custom-call | flops 12582912000 | bytes 196608000 | tf_op jit(solution)/shard_map/tile_product/pallas_call | solution.py:204
  25.9 0.5 collective-permute-done.6.refs_1_.refs_2_
  26.5 1.4 %tile_product.5 = bf16[1024,128]{1,0:T(8,128)(2,1)S(1)} custom-call(s32[2,40]{1,0:T(2,128)S(1)} %slot_blocks.1.refs_6_.refs_0_.refs_1_, s32[2,40]{1,0:T(2,128)S(1)} %collective-permute-done.6.refs_1_.refs_2_, bf16[5,8,128,128]{3,2,1,0:T(8,128)(2,1)S(1)} %bitcast.6, bf16[5,8,128,128]{3,2,1,0:T(8,128)(2,1)S(1)} %collective-permute-done.8.refs_3_.refs_5_, ...), custom_call_target="tpu_custom_call" | custom-call | flops 167772160 | bytes 2621440 | tf_op jit(solution)/shard_map/tile_product/pallas_call | solution.py:204
  27.9 2.8 %collective-permute-start.9 = (bf16[1024,128]{1,0:T(8,128)(2,1)S(1)}, bf16[1024,128]{1,0:T(8,128)(2,1)S(1)}, u32[]{:S(2)}, u32[]{:S(2)}) collective-permute-start(bf16[1024,128]{1,0:T(8,128)(2,1)S(1)} %tile_product.5), channel_id=1, source_target_pairs={{0,2},{1,3},{2,0},{3,1},{4,6},{5,7},{6,4},{7,5},{8,10},{9,11},{10,... | collective-permute-start | bytes 786440 | tf_op jit(solution)/shard_map/ppermute | solution.py:386
  30.9 1.0 %collective-permute-start.11 = (bf16[1024,128]{1,0:T(8,128)(2,1)S(1)}, bf16[1024,128]{1,0:T(8,128)(2,1)S(1)}, u32[]{:S(2)}, u32[]{:S(2)}) collective-permute-start(bf16[1024,128]{1,0:T(8,128)(2,1)S(1)} %get-tuple-element.32), channel_id=1, source_target_pairs={{0,4},{1,5},{2,6},{3,7},{4,0},{5,1},{6,2},{7,3},{8,12},{9,13},{10,... | collective-permute-start | bytes 786440 | tf_op jit(solution)/shard_map/ppermute | solution.py:386
  31.9 10.5 %collective-permute-done.9 = bf16[1024,128]{1,0:T(8,128)(2,1)S(1)} collective-permute-done((bf16[1024,128]{1,0:T(8,128)(2,1)S(1)}, bf16[1024,128]{1,0:T(8,128)(2,1)S(1)}, u32[]{:S(2)}, u32[]{:S(2)}) %collective-permute-start.9) | collective-permute-done | bytes 262176 | tf_op jit(solution)/shard_map/ppermute | solution.py:386
  42.4 1.3 %collective-permute-start.10 = (bf16[1024,128]{1,0:T(8,128)(2,1)S(1)}, bf16[1024,128]{1,0:T(8,128)(2,1)S(1)}, u32[]{:S(2)}, u32[]{:S(2)}) collective-permute-start(bf16[1024,128]{1,0:T(8,128)(2,1)S(1)} %add_convert_fusion.near_ref), channel_id=1, source_target_pairs={{0,4},{1,5},{2,6},{3,7},{4,0},{5,1},{6,2},{7,3},{8,12},{9,13},{10,... | collective-permute-start | bytes 786440 | tf_op jit(solution)/shard_map/ppermute | solution.py:386
  43.8 1.2 %collective-permute-done.10.far_ref = bf16[1024,128]{1,0:T(8,128)(2,1)S(1)} collective-permute-done((bf16[1024,128]{1,0:T(8,128)(2,1)S(1)}, bf16[1024,128]{1,0:T(8,128)(2,1)S(1)}, u32[]{:S(2)}, u32[]{:S(2)}) %collective-permute-start.10) | collective-permute-done | bytes 262176 | tf_op jit(solution)/shard_map/ppermute | solution.py:386
  44.9 0.4 middle.1
  45.3 1.4 %collective-permute-start.12 = (bf16[1024,128]{1,0:T(8,128)(2,1)S(1)}, bf16[1024,128]{1,0:T(8,128)(2,1)S(1)}, u32[]{:S(2)}, u32[]{:S(2)}) collective-permute-start(bf16[1024,128]{1,0:T(8,128)(2,1)S(1)} %get-tuple-element.36.adj_ref.after_ref.refs_6_), channel_id=1, source_target_pairs={{0,17},{1,0},{2,19},{3,2},{4,21},{5,4},{6,23},{7,6},{8,9},{9,24},{... | collective-permute-start | bytes 786440 | tf_op jit(solution)/shard_map/ppermute | solution.py:386
  46.7 0.3 grad_block.1.refs_0_
  47.1 2.4 %collective-permute-start.14 = (bf16[256,128]{1,0:T(8,128)(2,1)S(1)}, bf16[256,128]{1,0:T(8,128)(2,1)S(1)}, u32[]{:S(2)}, u32[]{:S(2)}) collective-permute-start(bf16[256,128]{1,0:T(8,128)(2,1)S(1)} %grad_block.1.refs_0_), channel_id=1, source_target_pairs={{0,1},{1,0},{2,3},{3,2},{4,5},{5,4},{6,7},{7,6},{8,9},{9,8},{10,11... | collective-permute-start | bytes 196616 | tf_op jit(solution)/shard_map/ppermute | solution.py:386
  49.5 4.8 %collective-permute-done.14.refs_11_.refs_1_ = bf16[256,128]{1,0:T(8,128)(2,1)S(1)} collective-permute-done((bf16[256,128]{1,0:T(8,128)(2,1)S(1)}, bf16[256,128]{1,0:T(8,128)(2,1)S(1)}, u32[]{:S(2)}, u32[]{:S(2)}) %collective-permute-start.14) | collective-permute-done | bytes 65568 | tf_op jit(solution)/shard_map/ppermute | solution.py:386
  54.3 3.3 %collective-permute-start.15 = (bf16[1024,128]{1,0:T(8,128)(2,1)S(1)}, bf16[1024,128]{1,0:T(8,128)(2,1)S(1)}, u32[]{:S(2)}, u32[]{:S(2)}) collective-permute-start(bf16[1024,128]{1,0:T(8,128)(2,1)S(1)} %get-tuple-element.36.adj_ref.after_ref.refs_6_), channel_id=1, source_target_pairs={{0,1},{2,3},{4,5},{6,7},{9,8},{11,10},{13,12},{15,14},{16,17},{18,... | collective-permute-start | bytes 786440 | tf_op jit(solution)/shard_map/ppermute | solution.py:386
  57.6 0.3 collective-permute-start.16
  58.1 1.1 %tile_product.6.refs_10_ = f32[1024,128]{1,0:T(8,128)S(1)} custom-call(s32[2,40]{1,0:T(2,128)S(1)} %collective-permute-done.refs_0_, s32[2,40]{1,0:T(2,128)S(1)} %slot_blocks.1.refs_6_.refs_0_.refs_1_, s32[2,40]{1,0:T(2,128)S(1)} %collective-permute-done.6.refs_1_.refs_2_, bf16[5,8,128,128]{3,2,1,0:T(8,128)(2,1)S(1)} %collective-permute-done.7.refs_1_.refs_3_, ...), custom_call_target="tpu_custom_call" | custom-call | flops 134217728 | bytes 1572864 | tf_op jit(solution)/shard_map/tile_product/pallas_call | solution.py:204
  59.2 2.7 %collective-permute-done.15.refs_7_ = bf16[1024,128]{1,0:T(8,128)(2,1)S(1)} collective-permute-done((bf16[1024,128]{1,0:T(8,128)(2,1)S(1)}, bf16[1024,128]{1,0:T(8,128)(2,1)S(1)}, u32[]{:S(2)}, u32[]{:S(2)}) %collective-permute-start.15) | collective-permute-done | bytes 262176 | tf_op jit(solution)/shard_map/ppermute | solution.py:386
  61.9 2.0 %collective-permute-done.16.refs_8_ = bf16[1024,128]{1,0:T(8,128)(2,1)S(1)} collective-permute-done((bf16[1024,128]{1,0:T(8,128)(2,1)S(1)}, bf16[1024,128]{1,0:T(8,128)(2,1)S(1)}, u32[]{:S(2)}, u32[]{:S(2)}) %collective-permute-start.16) | collective-permute-done | bytes 262176 | tf_op jit(solution)/shard_map/ppermute | solution.py:386
  64.0 1.4 %tile_product.7.refs_2_.refs_0_ = bf16[1024,128]{1,0:T(8,128)(2,1)S(1)} custom-call(s32[2,40]{1,0:T(2,128)S(1)} %collective-permute-done.refs_0_, s32[2,40]{1,0:T(2,128)S(1)} %slot_blocks.1.refs_6_.refs_0_.refs_1_, s32[2,40]{1,0:T(2,128)S(1)} %collective-permute-done.6.refs_1_.refs_2_, bf16[5,8,128,128]{3,2,1,0:T(8,128)(2,1)S(1)} %collective-permute-done.7.refs_1_.refs_3_, ...), custom_call_target="tpu_custom_call" | custom-call | flops 201326592 | bytes 2359296 | tf_op jit(solution)/shard_map/tile_product/pallas_call | solution.py:204
  65.4 3.2 %collective-permute-start.22 = (bf16[1024,128]{1,0:T(8,128)(2,1)S(1)}, bf16[1024,128]{1,0:T(8,128)(2,1)S(1)}, u32[]{:S(2)}, u32[]{:S(2)}) collective-permute-start(bf16[1024,128]{1,0:T(8,128)(2,1)S(1)} %tile_product.7.refs_2_.refs_0_), channel_id=1, source_target_pairs={{0,2},{1,3},{2,0},{3,1},{4,6},{5,7},{6,4},{7,5},{8,10},{9,11},{10,... | collective-permute-start | bytes 786440 | tf_op jit(solution)/shard_map/ppermute | solution.py:386
  68.9 2.9 %collective-permute-done.20.refs_1_ = bf16[256,128]{1,0:T(8,128)(2,1)S(1)} collective-permute-done((bf16[256,128]{1,0:T(8,128)(2,1)S(1)}, bf16[256,128]{1,0:T(8,128)(2,1)S(1)}, u32[]{:S(2)}, u32[]{:S(2)}) %collective-permute-start.20) | collective-permute-done | bytes 65568 | tf_op jit(solution)/shard_map/ppermute | solution.py:386
  71.8 1.2 %collective-permute-start.21 = (bf16[256,128]{1,0:T(8,128)(2,1)S(1)}, bf16[256,128]{1,0:T(8,128)(2,1)S(1)}, u32[]{:S(2)}, u32[]{:S(2)}) collective-permute-start(bf16[256,128]{1,0:T(8,128)(2,1)S(1)} %add_after.5.refs_0_), channel_id=1, source_target_pairs={{0,16},{1,17},{2,18},{3,19},{4,20},{5,21},{6,22},{7,23},{8,24},{9,... | collective-permute-start | bytes 196616 | tf_op jit(solution)/shard_map/ppermute | solution.py:386
  73.1 4.4 %collective-permute-start.18 = (bf16[1024,128]{1,0:T(8,128)(2,1)S(1)}, bf16[1024,128]{1,0:T(8,128)(2,1)S(1)}, u32[]{:S(2)}, u32[]{:S(2)}) collective-permute-start(bf16[1024,128]{1,0:T(8,128)(2,1)S(1)} %get-tuple-element.39.own_ref), channel_id=1, source_target_pairs={{0,1},{1,5},{2,3},{3,7},{4,0},{5,4},{6,2},{7,6},{8,9},{9,13},{10,1... | collective-permute-start | bytes 786440 | tf_op jit(solution)/shard_map/ppermute | solution.py:386
  77.5 1.9 %collective-permute-start.19 = (bf16[1024,128]{1,0:T(8,128)(2,1)S(1)}, bf16[1024,128]{1,0:T(8,128)(2,1)S(1)}, u32[]{:S(2)}, u32[]{:S(2)}) collective-permute-start(bf16[1024,128]{1,0:T(8,128)(2,1)S(1)} %get-tuple-element.39.own_ref), channel_id=1, source_target_pairs={{1,4},{3,6},{4,1},{6,3},{9,12},{11,14},{12,9},{14,11},{17,20},{19,... | collective-permute-start | bytes 786440 | tf_op jit(solution)/shard_map/ppermute | solution.py:386
  79.4 1.6 %collective-permute-done.22.refs_1_ = bf16[1024,128]{1,0:T(8,128)(2,1)S(1)} collective-permute-done((bf16[1024,128]{1,0:T(8,128)(2,1)S(1)}, bf16[1024,128]{1,0:T(8,128)(2,1)S(1)}, u32[]{:S(2)}, u32[]{:S(2)}) %collective-permute-start.22) | collective-permute-done | bytes 262176 | tf_op jit(solution)/shard_map/ppermute | solution.py:386
  81.1 0.6 collective-permute-start.24
  81.7 1.9 %collective-permute-start.25 = (bf16[1024,128]{1,0:T(8,128)(2,1)S(1)}, bf16[1024,128]{1,0:T(8,128)(2,1)S(1)}, u32[]{:S(2)}, u32[]{:S(2)}) collective-permute-start(bf16[1024,128]{1,0:T(8,128)(2,1)S(1)} %add_after.6.refs_2_.own_ref), channel_id=1, source_target_pairs={{1,4},{3,6},{4,1},{6,3},{9,12},{11,14},{12,9},{14,11},{17,20},{19,... | collective-permute-start | bytes 786440 | tf_op jit(solution)/shard_map/ppermute | solution.py:386
  83.7 1.1 %collective-permute-done.18.one_ref = bf16[1024,128]{1,0:T(8,128)(2,1)S(1)} collective-permute-done((bf16[1024,128]{1,0:T(8,128)(2,1)S(1)}, bf16[1024,128]{1,0:T(8,128)(2,1)S(1)}, u32[]{:S(2)}, u32[]{:S(2)}) %collective-permute-start.18) | collective-permute-done | bytes 262176 | tf_op jit(solution)/shard_map/ppermute | solution.py:386
  84.8 3.2 %collective-permute-done.19.two_ref = bf16[1024,128]{1,0:T(8,128)(2,1)S(1)} collective-permute-done((bf16[1024,128]{1,0:T(8,128)(2,1)S(1)}, bf16[1024,128]{1,0:T(8,128)(2,1)S(1)}, u32[]{:S(2)}, u32[]{:S(2)}) %collective-permute-start.19) | collective-permute-done | bytes 262176 | tf_op jit(solution)/shard_map/ppermute | solution.py:386
  88.0 1.0 %gather_halves.1 = (bf16[1024,256]{1,0:T(8,128)(2,1)}, f32[256,256]{1,0:T(8,128)}) custom-call(bf16[1024,128]{1,0:T(8,128)(2,1)S(1)} %get-tuple-element.39.own_ref, bf16[1024,128]{1,0:T(8,128)(2,1)S(1)} %collective-permute-done.18.one_ref, bf16[1024,128]{1,0:T(8,128)(2,1)S(1)} %collective-permute-done.19.two_ref, f32[256,128]{1,0:T(8,128)S(1)} %add_after.7.grad_ref, ...), custom_call_target="tpu_custom_call" | custom-call | tf_op jit(solution)/shard_map/gather_halves/pallas_call | solution.py:338
  89.1 1.4 %collective-permute-done.24.one_ref = bf16[1024,128]{1,0:T(8,128)(2,1)S(1)} collective-permute-done((bf16[1024,128]{1,0:T(8,128)(2,1)S(1)}, bf16[1024,128]{1,0:T(8,128)(2,1)S(1)}, u32[]{:S(2)}, u32[]{:S(2)}) %collective-permute-start.24) | collective-permute-done | bytes 262176 | tf_op jit(solution)/shard_map/ppermute | solution.py:386
  90.4 1.6 %collective-permute-done.25.two_ref = bf16[1024,128]{1,0:T(8,128)(2,1)S(1)} collective-permute-done((bf16[1024,128]{1,0:T(8,128)(2,1)S(1)}, bf16[1024,128]{1,0:T(8,128)(2,1)S(1)}, u32[]{:S(2)}, u32[]{:S(2)}) %collective-permute-start.25) | collective-permute-done | bytes 262176 | tf_op jit(solution)/shard_map/ppermute | solution.py:386
  92.0 1.2 %final.1 = bf16[1024,256]{1,0:T(8,128)(2,1)} custom-call(bf16[1024,128]{1,0:T(8,128)(2,1)S(1)} %add_after.6.refs_2_.own_ref, bf16[1024,128]{1,0:T(8,128)(2,1)S(1)} %collective-permute-done.24.one_ref, bf16[1024,128]{1,0:T(8,128)(2,1)S(1)} %collective-permute-done.25.two_ref, bf16[256,256]{1,0:T(8,128)(2,1)S(1)} %copy-done.3), custom_call_target="tpu_custom_call" | custom-call | flops 134217728 | bytes 2097152 | tf_op jit(solution)/shard_map/final/pallas_call | solution.py:364
  (33 shorter events, 1.2 us)
Async XLA Ops:
  0.6 17.1 %collective-permute-start.7 = (bf16[5,8,128,128]{3,2,1,0:T(8,128)(2,1)}, bf16[5,8,128,128]{3,2,1,0:T(8,128)(2,1)S(1)}, u32[]{:S(2)}, u32[]{:S(2)}) collective-permute-start(bf16[5,8,128,128]{3,2,1,0:T(8,128)(2,1)} %bitcast.5), channel_id=1, source_target_pairs={{0,4},{1,0},{2,6},{3,2},{4,5},{5,1},{6,7},{7,3},{8,12},{9,8},{10,1... | collective-permute-start | bytes 3932168 | tf_op jit(solution)/shard_map/ppermute | solution.py:386
  2.8 1.0 %copy-start.1 = (bf16[1024,256]{1,0:T(8,128)(2,1)S(1)}, bf16[1024,256]{1,0:T(8,128)(2,1)}, u32[]{:S(2)}) copy-start(bf16[1024,256]{1,0:T(8,128)(2,1)} %x_ref.2) | copy-start | bytes 1572868
  4.0 9.5 %collective-permute-start.1 = (bf16[1024,128]{1,0:T(8,128)(2,1)S(1)}, bf16[1024,128]{1,0:T(8,128)(2,1)S(1)}, u32[]{:S(2)}, u32[]{:S(2)}) collective-permute-start(bf16[1024,128]{1,0:T(8,128)(2,1)S(1)} %get-tuple-element.23.refs_3_.refs_2_.refs_5_.refs_4_.refs_7_), channel_id=1, source_target_pairs={{0,8},{1,17},{2,10},{3,19},{5,13},{7,15},{8,0},{10,2},{12,28},{13,... | collective-permute-start | bytes 786440 | tf_op jit(solution)/shard_map/ppermute | solution.py:386
  4.7 8.9 %collective-permute-start.2 = (bf16[1024,128]{1,0:T(8,128)(2,1)S(1)}, bf16[1024,128]{1,0:T(8,128)(2,1)S(1)}, u32[]{:S(2)}, u32[]{:S(2)}) collective-permute-start(bf16[1024,128]{1,0:T(8,128)(2,1)S(1)} %get-tuple-element.24), channel_id=1, source_target_pairs={{0,12},{1,21},{2,14},{3,23},{5,9},{7,11},{8,4},{10,6},{12,24},{13,... | collective-permute-start | bytes 786440 | tf_op jit(solution)/shard_map/ppermute | solution.py:386
  6.0 7.6 %collective-permute-start.3 = (bf16[1024,128]{1,0:T(8,128)(2,1)S(1)}, bf16[1024,128]{1,0:T(8,128)(2,1)S(1)}, u32[]{:S(2)}, u32[]{:S(2)}) collective-permute-start(bf16[1024,128]{1,0:T(8,128)(2,1)S(1)} %get-tuple-element.24), channel_id=1, source_target_pairs={{0,4},{1,5},{2,6},{3,7},{4,0},{5,1},{6,2},{7,3},{8,12},{9,13},{10,... | collective-permute-start | bytes 786440 | tf_op jit(solution)/shard_map/ppermute | solution.py:386
  11.4 0.7 copy-start.4
  13.6 9.7 %collective-permute-start.4 = (bf16[1024,128]{1,0:T(8,128)(2,1)S(1)}, bf16[1024,128]{1,0:T(8,128)(2,1)S(1)}, u32[]{:S(2)}, u32[]{:S(2)}) collective-permute-start(bf16[1024,128]{1,0:T(8,128)(2,1)S(1)} %get-tuple-element.25), channel_id=1, source_target_pairs={{0,16},{1,17},{2,18},{3,19},{4,20},{5,21},{6,22},{7,23},{8,24},{9,... | collective-permute-start | bytes 786440 | tf_op jit(solution)/shard_map/ppermute | solution.py:386
  15.5 11.0 %copy-start = (bf16[1,5,8,128,128]{4,3,2,1,0:T(8,128)(2,1)S(1)}, bf16[1,5,8,128,128]{4,3,2,1,0:T(8,128)(2,1)}, u32[]{:S(2)}) copy-start(bf16[1,5,8,128,128]{4,3,2,1,0:T(8,128)(2,1)} %param.9) | copy-start | bytes 3932164
  15.5 7.9 %collective-permute-start.5 = (bf16[1024,128]{1,0:T(8,128)(2,1)S(1)}, bf16[1024,128]{1,0:T(8,128)(2,1)S(1)}, u32[]{:S(2)}, u32[]{:S(2)}) collective-permute-start(bf16[1024,128]{1,0:T(8,128)(2,1)S(1)} %get-tuple-element.26), channel_id=1, source_target_pairs={{0,8},{1,9},{2,10},{3,11},{4,12},{5,13},{6,14},{7,15},{8,0},{9,1},... | collective-permute-start | bytes 786440 | tf_op jit(solution)/shard_map/ppermute | solution.py:386
  17.7 8.8 %collective-permute-start.8 = (bf16[5,8,128,128]{3,2,1,0:T(8,128)(2,1)S(1)}, bf16[5,8,128,128]{3,2,1,0:T(8,128)(2,1)S(1)}, u32[]{:S(2)}, u32[]{:S(2)}) collective-permute-start(bf16[5,8,128,128]{3,2,1,0:T(8,128)(2,1)S(1)} %collective-permute-done.7.refs_1_.refs_3_), channel_id=1, source_target_pairs={{0,4},{2,6},{5,1},{7,3},{8,12},{10,14},{13,9},{15,11},{16,20},{18,... | collective-permute-start | bytes 3932168 | tf_op jit(solution)/shard_map/ppermute | solution.py:386
  19.0 4.4 %collective-permute-start = (s32[2,40]{1,0:T(2,128)S(1)}, s32[2,40]{1,0:T(2,128)S(1)}, u32[]{:S(2)}, u32[]{:S(2)}) collective-permute-start(s32[2,40]{1,0:T(2,128)S(1)} %slot_blocks.1.refs_6_.refs_0_.refs_1_), channel_id=1, source_target_pairs={{0,4},{1,0},{2,6},{3,2},{4,5},{5,1},{6,7},{7,3},{8,12},{9,8},{10,1... | collective-permute-start | bytes 968 | tf_op jit(solution)/shard_map/ppermute | solution.py:386
  23.4 3.1 %collective-permute-start.6 = (s32[2,40]{1,0:T(2,128)S(1)}, s32[2,40]{1,0:T(2,128)S(1)}, u32[]{:S(2)}, u32[]{:S(2)}) collective-permute-start(s32[2,40]{1,0:T(2,128)S(1)} %collective-permute-done.refs_0_), channel_id=1, source_target_pairs={{0,4},{2,6},{5,1},{7,3},{8,12},{10,14},{13,9},{15,11},{16,20},{18,... | collective-permute-start | bytes 968 | tf_op jit(solution)/shard_map/ppermute | solution.py:386
  25.9 4.8 %copy-start.2 = (bf16[1024,256]{1,0:T(8,128)(2,1)S(1)}, bf16[1024,256]{1,0:T(8,128)(2,1)}, u32[]{:S(2)}) copy-start(bf16[1024,256]{1,0:T(8,128)(2,1)} %x_ref.3) | copy-start | bytes 1572868
  27.9 17.0 %copy-start.3 = (bf16[256,256]{1,0:T(8,128)(2,1)S(1)}, bf16[256,256]{1,0:T(8,128)(2,1)}, u32[]{:S(2)}) copy-start(bf16[256,256]{1,0:T(8,128)(2,1)} %w_ref.3) | copy-start | bytes 393220
  27.9 14.5 %collective-permute-start.9 = (bf16[1024,128]{1,0:T(8,128)(2,1)S(1)}, bf16[1024,128]{1,0:T(8,128)(2,1)S(1)}, u32[]{:S(2)}, u32[]{:S(2)}) collective-permute-start(bf16[1024,128]{1,0:T(8,128)(2,1)S(1)} %tile_product.5), channel_id=1, source_target_pairs={{0,2},{1,3},{2,0},{3,1},{4,6},{5,7},{6,4},{7,5},{8,10},{9,11},{10,... | collective-permute-start | bytes 786440 | tf_op jit(solution)/shard_map/ppermute | solution.py:386
  30.9 12.9 %collective-permute-start.11 = (bf16[1024,128]{1,0:T(8,128)(2,1)S(1)}, bf16[1024,128]{1,0:T(8,128)(2,1)S(1)}, u32[]{:S(2)}, u32[]{:S(2)}) collective-permute-start(bf16[1024,128]{1,0:T(8,128)(2,1)S(1)} %get-tuple-element.32), channel_id=1, source_target_pairs={{0,4},{1,5},{2,6},{3,7},{4,0},{5,1},{6,2},{7,3},{8,12},{9,13},{10,... | collective-permute-start | bytes 786440 | tf_op jit(solution)/shard_map/ppermute | solution.py:386
  42.4 2.5 %collective-permute-start.10 = (bf16[1024,128]{1,0:T(8,128)(2,1)S(1)}, bf16[1024,128]{1,0:T(8,128)(2,1)S(1)}, u32[]{:S(2)}, u32[]{:S(2)}) collective-permute-start(bf16[1024,128]{1,0:T(8,128)(2,1)S(1)} %add_convert_fusion.near_ref), channel_id=1, source_target_pairs={{0,4},{1,5},{2,6},{3,7},{4,0},{5,1},{6,2},{7,3},{8,12},{9,13},{10,... | collective-permute-start | bytes 786440 | tf_op jit(solution)/shard_map/ppermute | solution.py:386
  45.3 12.3 %collective-permute-start.12 = (bf16[1024,128]{1,0:T(8,128)(2,1)S(1)}, bf16[1024,128]{1,0:T(8,128)(2,1)S(1)}, u32[]{:S(2)}, u32[]{:S(2)}) collective-permute-start(bf16[1024,128]{1,0:T(8,128)(2,1)S(1)} %get-tuple-element.36.adj_ref.after_ref.refs_6_), channel_id=1, source_target_pairs={{0,17},{1,0},{2,19},{3,2},{4,21},{5,4},{6,23},{7,6},{8,9},{9,24},{... | collective-permute-start | bytes 786440 | tf_op jit(solution)/shard_map/ppermute | solution.py:386
  46.7 10.8 %collective-permute-start.13 = (bf16[1024,128]{1,0:T(8,128)(2,1)S(1)}, bf16[1024,128]{1,0:T(8,128)(2,1)S(1)}, u32[]{:S(2)}, u32[]{:S(2)}) collective-permute-start(bf16[1024,128]{1,0:T(8,128)(2,1)S(1)} %get-tuple-element.36.adj_ref.after_ref.refs_6_), channel_id=1, source_target_pairs={{0,8},{1,9},{2,10},{3,11},{4,12},{5,13},{6,14},{7,15},{8,0},{9,1},... | collective-permute-start | bytes 786440 | tf_op jit(solution)/shard_map/ppermute | solution.py:386
  47.1 7.2 %collective-permute-start.14 = (bf16[256,128]{1,0:T(8,128)(2,1)S(1)}, bf16[256,128]{1,0:T(8,128)(2,1)S(1)}, u32[]{:S(2)}, u32[]{:S(2)}) collective-permute-start(bf16[256,128]{1,0:T(8,128)(2,1)S(1)} %grad_block.1.refs_0_), channel_id=1, source_target_pairs={{0,1},{1,0},{2,3},{3,2},{4,5},{5,4},{6,7},{7,6},{8,9},{9,8},{10,11... | collective-permute-start | bytes 196616 | tf_op jit(solution)/shard_map/ppermute | solution.py:386
  54.3 7.7 %collective-permute-start.15 = (bf16[1024,128]{1,0:T(8,128)(2,1)S(1)}, bf16[1024,128]{1,0:T(8,128)(2,1)S(1)}, u32[]{:S(2)}, u32[]{:S(2)}) collective-permute-start(bf16[1024,128]{1,0:T(8,128)(2,1)S(1)} %get-tuple-element.36.adj_ref.after_ref.refs_6_), channel_id=1, source_target_pairs={{0,1},{2,3},{4,5},{6,7},{9,8},{11,10},{13,12},{15,14},{16,17},{18,... | collective-permute-start | bytes 786440 | tf_op jit(solution)/shard_map/ppermute | solution.py:386
  57.6 6.4 %collective-permute-start.16 = (bf16[1024,128]{1,0:T(8,128)(2,1)S(1)}, bf16[1024,128]{1,0:T(8,128)(2,1)S(1)}, u32[]{:S(2)}, u32[]{:S(2)}) collective-permute-start(bf16[1024,128]{1,0:T(8,128)(2,1)S(1)} %collective-permute-done.13.refs_7_), channel_id=1, source_target_pairs={{0,16},{1,17},{2,18},{3,19},{4,20},{5,21},{6,22},{7,23},{8,24},{9,... | collective-permute-start | bytes 786440 | tf_op jit(solution)/shard_map/ppermute | solution.py:386
  57.9 6.1 %collective-permute-start.17 = (bf16[1024,128]{1,0:T(8,128)(2,1)S(1)}, bf16[1024,128]{1,0:T(8,128)(2,1)S(1)}, u32[]{:S(2)}, u32[]{:S(2)}) collective-permute-start(bf16[1024,128]{1,0:T(8,128)(2,1)S(1)} %collective-permute-done.12.refs_6_), channel_id=1, source_target_pairs={{0,8},{1,9},{2,10},{3,11},{4,12},{5,13},{6,14},{7,15},{8,0},{9,1},... | collective-permute-start | bytes 786440 | tf_op jit(solution)/shard_map/ppermute | solution.py:386
  65.4 15.6 %collective-permute-start.22 = (bf16[1024,128]{1,0:T(8,128)(2,1)S(1)}, bf16[1024,128]{1,0:T(8,128)(2,1)S(1)}, u32[]{:S(2)}, u32[]{:S(2)}) collective-permute-start(bf16[1024,128]{1,0:T(8,128)(2,1)S(1)} %tile_product.7.refs_2_.refs_0_), channel_id=1, source_target_pairs={{0,2},{1,3},{2,0},{3,1},{4,6},{5,7},{6,4},{7,5},{8,10},{9,11},{10,... | collective-permute-start | bytes 786440 | tf_op jit(solution)/shard_map/ppermute | solution.py:386
  68.6 3.2 %collective-permute-start.20 = (bf16[256,128]{1,0:T(8,128)(2,1)S(1)}, bf16[256,128]{1,0:T(8,128)(2,1)S(1)}, u32[]{:S(2)}, u32[]{:S(2)}) collective-permute-start(bf16[256,128]{1,0:T(8,128)(2,1)S(1)} %add_after.4.refs_0_), channel_id=1, source_target_pairs={{0,8},{1,9},{2,10},{3,11},{4,12},{5,13},{6,14},{7,15},{8,0},{9,1},... | collective-permute-start | bytes 196616 | tf_op jit(solution)/shard_map/ppermute | solution.py:386
  71.8 7.6 %collective-permute-start.21 = (bf16[256,128]{1,0:T(8,128)(2,1)S(1)}, bf16[256,128]{1,0:T(8,128)(2,1)S(1)}, u32[]{:S(2)}, u32[]{:S(2)}) collective-permute-start(bf16[256,128]{1,0:T(8,128)(2,1)S(1)} %add_after.5.refs_0_), channel_id=1, source_target_pairs={{0,16},{1,17},{2,18},{3,19},{4,20},{5,21},{6,22},{7,23},{8,24},{9,... | collective-permute-start | bytes 196616 | tf_op jit(solution)/shard_map/ppermute | solution.py:386
  73.1 11.7 %collective-permute-start.18 = (bf16[1024,128]{1,0:T(8,128)(2,1)S(1)}, bf16[1024,128]{1,0:T(8,128)(2,1)S(1)}, u32[]{:S(2)}, u32[]{:S(2)}) collective-permute-start(bf16[1024,128]{1,0:T(8,128)(2,1)S(1)} %get-tuple-element.39.own_ref), channel_id=1, source_target_pairs={{0,1},{1,5},{2,3},{3,7},{4,0},{5,4},{6,2},{7,6},{8,9},{9,13},{10,1... | collective-permute-start | bytes 786440 | tf_op jit(solution)/shard_map/ppermute | solution.py:386
  77.5 10.6 %collective-permute-start.19 = (bf16[1024,128]{1,0:T(8,128)(2,1)S(1)}, bf16[1024,128]{1,0:T(8,128)(2,1)S(1)}, u32[]{:S(2)}, u32[]{:S(2)}) collective-permute-start(bf16[1024,128]{1,0:T(8,128)(2,1)S(1)} %get-tuple-element.39.own_ref), channel_id=1, source_target_pairs={{1,4},{3,6},{4,1},{6,3},{9,12},{11,14},{12,9},{14,11},{17,20},{19,... | collective-permute-start | bytes 786440 | tf_op jit(solution)/shard_map/ppermute | solution.py:386
  81.1 9.3 %collective-permute-start.24 = (bf16[1024,128]{1,0:T(8,128)(2,1)S(1)}, bf16[1024,128]{1,0:T(8,128)(2,1)S(1)}, u32[]{:S(2)}, u32[]{:S(2)}) collective-permute-start(bf16[1024,128]{1,0:T(8,128)(2,1)S(1)} %add_after.6.refs_2_.own_ref), channel_id=1, source_target_pairs={{0,1},{1,5},{2,3},{3,7},{4,0},{5,4},{6,2},{7,6},{8,9},{9,13},{10,1... | collective-permute-start | bytes 786440 | tf_op jit(solution)/shard_map/ppermute | solution.py:386
  81.7 10.3 %collective-permute-start.25 = (bf16[1024,128]{1,0:T(8,128)(2,1)S(1)}, bf16[1024,128]{1,0:T(8,128)(2,1)S(1)}, u32[]{:S(2)}, u32[]{:S(2)}) collective-permute-start(bf16[1024,128]{1,0:T(8,128)(2,1)S(1)} %add_after.6.refs_2_.own_ref), channel_id=1, source_target_pairs={{1,4},{3,6},{4,1},{6,3},{9,12},{11,14},{12,9},{14,11},{17,20},{19,... | collective-permute-start | bytes 786440 | tf_op jit(solution)/shard_map/ppermute | solution.py:386
  83.7 4.4 %collective-permute-start.23 = (f32[256,128]{1,0:T(8,128)S(1)}, f32[256,128]{1,0:T(8,128)S(1)}, u32[]{:S(2)}, u32[]{:S(2)}) collective-permute-start(f32[256,128]{1,0:T(8,128)S(1)} %add_after.7.grad_ref), channel_id=1, source_target_pairs={{0,4},{1,5},{2,6},{3,7},{4,0},{5,1},{6,2},{7,3},{8,12},{9,13},{10,... | collective-permute-start | bytes 393224 | tf_op jit(solution)/shard_map/ppermute | solution.py:386

commit v11 on v9

--- a/solution.py
+++ b/solution.py
@@ -8,7 +8,7 @@
 from jax.sharding import PartitionSpec as P
 
 AXES = ("rows", "rep")
-WEIGH = 200
+WEIGH = 75
 
 
 def route(shape, move):
@@ -37,6 +37,8 @@
         lax.axis_size("rows") == 8, (lax.axis_index("rows") // 2 + z) % 2 == 1
     )
     return {
+        "core 0": j == 0,
+        "core 1": j == 1,
         "home": home,
         "away": jnp.logical_not(home),
         "relay": relay,
@@ -85,6 +87,27 @@
         compiler_params=pltpu.CompilerParams(vmem_limit_bytes=1024 * 1024),
         name="halves",
     )(value)
+
+
+def transform_kernel(x_ref, w_ref, near_ref, far_ref):
+    near_cols, far_cols = half_columns(near_ref.shape[1])
+    for cols, out_ref in ((near_cols, near_ref), (far_cols, far_ref)):
+        product = jnp.dot(x_ref[...], w_ref[:, cols], preferred_element_type=jnp.float32)
+        out_ref[...] = product.astype(out_ref.dtype)
+
+
+def transform(feats, weight):
+    rows, width = feats.shape
+    vmem = pl.BlockSpec(memory_space=pltpu.VMEM)
+    part = jax.ShapeDtypeStruct((rows, weight.shape[1] // 2), feats.dtype)
+    return pl.pallas_call(
+        transform_kernel,
+        out_shape=(part, part),
+        in_specs=[vmem, vmem],
+        out_specs=(vmem, vmem),
+        compiler_params=pltpu.CompilerParams(vmem_limit_bytes=8 * 1024 * 1024),
+        name="transform",
+    )(feats, weight)
 
 
 def pick_kernel(cases, waits, *refs):
@@ -226,27 +249,19 @@
     )(*metas, *tiles, *panels, *([before] if summed else []), *after)
 
 
-def middle_kernel(near_ref, far_ref, w_ref, cot_ref, cot_swap_ref, act_ref, adj_ref):
-    j, _, p = place()
-    half = near_ref.shape[1]
-    near = pl.multiple_of(j * half, half)
-    far = pl.multiple_of((1 - j) * half, half)
-    cols = pl.ds(near, half)
-    agg = jnp.dot(
-        near_ref[...], w_ref[pl.ds(near, half), cols], preferred_element_type=jnp.float32
-    )
-    agg += jnp.dot(far_ref[...], w_ref[pl.ds(far, half), cols], preferred_element_type=jnp.float32)
+def middle_kernel(part_ref, zero_ref, one_ref, cot_ref, swap_ref, act_ref, adj_ref):
+    got = chosen([("core 0", zero_ref), ("core 1", one_ref)], lambda ref: ref[...])
+    agg = part_ref[...].astype(jnp.float32) + got.astype(jnp.float32)
     sig = jax.nn.sigmoid(agg)
     act_ref[...] = (agg * sig).astype(act_ref.dtype)
     slope = sig * (1.0 + agg * (1.0 - sig))
-    cot = jnp.where(j == p, cot_ref[...], cot_swap_ref[...])
+    cot = chosen([("home", cot_ref), ("away", swap_ref)], lambda ref: ref[...])
     adj_ref[...] = (cot.astype(jnp.float32) * slope).astype(adj_ref.dtype)
 
 
-def middle(near, far, weight, cot, cot_swap):
+def middle(part, zero, one, cot, cot_swap):
     vmem = pl.BlockSpec(memory_space=pltpu.VMEM)
-    rows, width = near.shape
-    out = jax.ShapeDtypeStruct((rows, width), jnp.bfloat16)
+    out = jax.ShapeDtypeStruct(part.shape, jnp.bfloat16)
     return pl.pallas_call(
         middle_kernel,
         out_shape=(out, out),
@@ -254,40 +269,34 @@
         out_specs=(vmem, vmem),
         compiler_params=pltpu.CompilerParams(vmem_limit_bytes=8 * 1024 * 1024),
         cost_estimate=pl.CostEstimate(
-            flops=4 * rows * width * width,
-            bytes_accessed=10 * rows * width,
-            transcendentals=rows * width,
+            flops=20 * part.size, bytes_accessed=10 * part.size, transcendentals=part.size
         ),
         name="middle",
-    )(near, far, weight, cot, cot_swap)
-
-
-def grad_kernel(scale, near_ref, far_ref, adj_ref, after_ref, out_ref):
-    j, _, _ = place()
-    half = near_ref.shape[1]
+    )(part, zero, one, cot, cot_swap)
+
+
+def grad_kernel(scale, feats_ref, swap_ref, back_ref, out_ref):
+    feats = chosen([("home", feats_ref), ("away", swap_ref)], lambda ref: ref[...])
     dims = (((0,), (0,)), ((), ()))
-    for i, ref in enumerate((near_ref, far_ref)):
-        start = pl.multiple_of((j if i == 0 else 1 - j) * half, half)
-        block = lax.dot_general(ref[...], adj_ref[...], dims, preferred_element_type=jnp.float32)
-        out_ref[pl.ds(start, half), :] = (scale * block).astype(out_ref.dtype)
-
-
-def grad_block(scale, near, far, adj, after):
+    block = lax.dot_general(feats, back_ref[...], dims, preferred_element_type=jnp.float32)
+    out_ref[...] = (scale * block).astype(out_ref.dtype)
+
+
+def grad_block(scale, feats, feats_swap, back):
     vmem = pl.BlockSpec(memory_space=pltpu.VMEM)
-    rows, width = near.shape
+    rows, wide = feats.shape
+    width = back.shape[1]
     return pl.pallas_call(
         functools.partial(grad_kernel, scale),
-        out_shape=jax.ShapeDtypeStruct((2 * width, width), jnp.bfloat16),
-        in_specs=[vmem] * 3 + [pl.BlockSpec(memory_space=pl.ANY)],
+        out_shape=jax.ShapeDtypeStruct((wide, width), jnp.bfloat16),
+        in_specs=[vmem] * 3,
         out_specs=vmem,
         compiler_params=pltpu.CompilerParams(vmem_limit_bytes=8 * 1024 * 1024),
         cost_estimate=pl.CostEstimate(
-            flops=4 * WEIGH * rows * width * width,
-            bytes_accessed=8 * WEIGH * rows * width,
-            transcendentals=0,
+            flops=2 * rows * wide * width, bytes_accessed=8 * rows * width, transcendentals=0
         ),
         name="grad_block",
-    )(near, far, adj, after)
+    )(feats, feats_swap, back)
 
 
 def add_kernel(count, *refs):
@@ -310,25 +319,30 @@
     )(*values, *after)
 
 
+def half_columns(half):
+    j, _, _ = place()
+    near = pl.ds(pl.multiple_of(j * half, half), half)
+    return near, pl.ds(pl.multiple_of((1 - j) * half, half), half)
+
+
 def final_kernel(*refs):
     back, act, (w_ref, grad_ref, rest_ref), outs = refs[:3], refs[3:6], refs[6:9], refs[9:]
     out_ref, act_ref, grad_out_ref = outs
-    j, _, p = place()
-    half = back[0].shape[1]
-    near_cols = pl.ds(pl.multiple_of(j * half, half), half)
-    far_cols = pl.ds(pl.multiple_of((1 - j) * half, half), half)
-
-    def halves_of(parts):
-        own, one, two = parts
-        near = jnp.where(j == p, own[...], one[...])
-        return near, jnp.where(j == p, one[...], two[...])
-
-    near, far = halves_of(back)
+    near_cols, far_cols = half_columns(back[0].shape[1])
+
+    def near_of(parts):
+        return chosen([("home", parts[0]), ("away", parts[1])], lambda ref: ref[...])
+
     dims = (((1,), (1,)), ((), ()))
-    total = lax.dot_general(near, w_ref[:, near_cols], dims, preferred_element_type=jnp.float32)
-    total += lax.dot_general(far, w_ref[:, far_cols], dims, preferred_element_type=jnp.float32)
+    total = lax.dot_general(
+        near_of(back), w_ref[:, near_cols], dims, preferred_element_type=jnp.float32
+    )
+    total += lax.dot_general(
+        back[2][...], w_ref[:, far_cols], dims, preferred_element_type=jnp.float32
+    )
     out_ref[...] = total.astype(out_ref.dtype)
-    act_ref[:, near_cols], act_ref[:, far_cols] = halves_of(act)
+    act_ref[:, near_cols] = near_of(act)
+    act_ref[:, far_cols] = act[2][...]
     grad_out_ref[:, near_cols] = grad_ref[...]
     grad_out_ref[:, far_cols] = rest_ref[...]
 
@@ -398,7 +412,7 @@
         return to and (to[0], 1 - j, z)
 
     first = send(own, to_home)
-    mine, yours = halves(node_feats)
+    mine, yours = transform(node_feats, weight)
     one = send(mine, stage_one)
     two = send(yours, stage_one_cross)
     swapped = send(yours, sibling)
@@ -422,6 +436,8 @@
     meta_b = send(meta, to_home)
     first, one, two = lax.optimization_barrier((first, one, two))
     other_first = send(first, home_to_sibling)
+    meta_later, second, far = lax.optimization_barrier((meta_b, second, far))
+    meta_far = send(meta_later, home_to_sibling)
     set_first = [(None, (meta_b, first))]
     panels = [
         ("self", [("home", mine), ("away", swapped)]),
@@ -431,19 +447,20 @@
         ("far", [(None, far)]),
     ]
     part = tile_product(panels, [set_first], jnp.float32, weigh=WEIGH)
-    meta_later, part = lax.optimization_barrier((meta_b, part))
-    meta_far = send(meta_later, home_to_sibling)
     set_rest = [("home", (meta, own)), ("away", (meta_far, other_first))]
-    part = tile_product(panels, [set_rest], jnp.bfloat16, part)
-
-    def join(value):
-        other = send(value, across)
-        return (value.astype(jnp.float32) + other.astype(jnp.float32)).astype(jnp.bfloat16)
-
-    near = join(part)
-    far_half = send(near, sibling)
     cot, cot_yours = halves(cotangent)
-    act, adj = middle(near, far_half, weight, cot, send(cot_yours, sibling))
+    cot_swap = send(cot_yours, sibling)
+    feats_swap = send(node_feats, sibling)
+    part = tile_product(panels, [set_rest], jnp.bfloat16, part, [cot_swap, feats_swap])
+
+    def core_across(core):
+        return lambda c, j, z: across(c, j, z) if j == core else None
+
+    got_zero = send(part, core_across(0))
+    token = send(got_zero[:16], lambda c, j, z: (c, 1, z) if j == 0 else None)
+    (part_later,) = pick([[(None, part)]], [token])
+    got_one = send(part_later, core_across(1))
+    act, adj = middle(part, got_zero, got_one, cot, cot_swap)
 
     direct = send(adj, to_direct)
     near_one = send(
@@ -451,8 +468,6 @@
     )
     adj_later, near_one, direct = lax.optimization_barrier((adj, near_one, direct))
     second = send(direct if four else adj_later, to_second)
-    grad = grad_block(scale, near, far_half, adj, direct)
-    adj_later, grad = lax.optimization_barrier((adj_later, grad))
     far = send(near_one, to_far)
     near_choice = [("still", near_one)]
     if four:
@@ -460,29 +475,34 @@
             adj_later, lambda c, j, z: None if (c + z) % 2 else (c, j, z ^ 1)
         )
         near_choice.append(("relay", near_two))
-    grad_got = send(grad, lambda c, j, z: (c, j, z ^ 1))
     panels = [("self", [(None, adj)]), ("direct", [(None, direct)])]
     back_part = tile_product(panels, [set_first, set_rest], jnp.float32)
     panels = [("near", near_choice), ("second", [(None, second)]), ("far", [(None, far)])]
-    back_part = tile_product(
-        panels, [set_first, set_rest], jnp.bfloat16, back_part, [grad_got]
-    )
-
-    def deliver(value):
-        one = send(value, lambda c, j, z: (c, j, z ^ 1) if j == z % 2 else (c, 1 - j, z))
-        two = send(value, lambda c, j, z: None if j == z % 2 else (c, 1 - j, z ^ 1))
-        return one, two
-
+    back_part = tile_product(panels, [set_first, set_rest], jnp.bfloat16, back_part)
+
+    def to_other_z(c, j, z):
+        return (c, j, z ^ 1)
+
+    def swap(value, got, after):
+        (payload,) = pick([[("home", got), ("away", value)]], after)
+        return [value, got, send(payload, sibling)]
+
+    grad = grad_block(scale, node_feats, feats_swap, back_part)
+    grad = add_after([grad, send(grad, to_other_z)], jnp.bfloat16)
+    got = send(grad, to_direct)
     act_later, back_part = lax.optimization_barrier((act, back_part))
-    act_parts = [act, *deliver(act_later)]
-    back = add_after([back_part, send(back_part, across)], jnp.bfloat16, *act_parts[1:])
-    back_parts = [back, *deliver(back)]
-    grad = add_after([grad, grad_got], jnp.bfloat16, back_part)
-    step = 1
+    act_got = send(act_later, to_other_z)
+    back = add_after([back_part, send(back_part, across)], jnp.bfloat16, got, act_got)
+    back_got = send(back, to_other_z)
+    back_parts = swap(back, back_got, [])
+    act_parts = swap(act, act_got, [back_got])
+    grad = add_after([grad, got], jnp.bfloat16, back)
+    step = 2
     while step < shape[0]:
         got = send(grad, lambda c, j, z, s=step: (c ^ s, j, z))
-        grad = add_after([grad, got], jnp.float32, back)
+        grad = add_after([grad, got], jnp.float32)
         step *= 2
+    grad = add_after([grad, send(grad, across)], jnp.float32, back_got)
     input_grad, activated, weight_grad = final(
         back_parts, act_parts, weight, grad, send(grad, sibling)
     )

time: 94.8 us -> 103 us (1.086)
  the two profiles are of different devices: /device:TPU:24 before, /device:TPU:1 now
where the time goes in v11:
time: 103 us; the launch traced here: 102 us
  waiting for transfers between devices  54.9 us (53%)
  starting transfers between devices  33.6 us (33%)
  Pallas kernels  9.68 us (9%)
  local copies, waits for them, and re-layouts  3.32 us (3%)
    ppermute x29, waiting for transfers between devices, send(): return lax.ppermute(value, AXES, route(shape, move))  54.9 us
    ppermute x29, starting transfers between devices, send(): return lax.ppermute(value, AXES, route(shape, move))  33.6 us
    pallas_call x4, Pallas kernels, tile_product(): pl.pallas_call(functools.partial(tile_kernel, kinds, cases, [[case for ca...  5.23 us
    unnamed x15, local copies, waits for them, and re-layouts  3.31 us
  transfers between devices with their start and end apart: 29, of which 16 were waited for; matrix products, arithmetic and copies ran while one was open for 1% of the time, Pallas kernels for 5%

profile of v11, /device:TPU:1, one launch (start us, length us, event | category | flops | bytes accessed | tf_op | source)
XLA Modules:
  0.0 102.4 jit_solution(14919794498630423932)
XLA Ops:
  0.6 2.2 %collective-permute-start.7 = (bf16[5,8,128,128]{3,2,1,0:T(8,128)(2,1)}, bf16[5,8,128,128]{3,2,1,0:T(8,128)(2,1)S(1)}, u32[]{:S(2)}, u32[]{:S(2)}) collective-permute-start(bf16[5,8,128,128]{3,2,1,0:T(8,128)(2,1)} %bitcast.5), channel_id=1, source_target_pairs={{0,4},{1,0},{2,6},{3,2},{4,5},{5,1},{6,7},{7,3},{8,12},{9,8},{10,1... | collective-permute-start | bytes 3932168 | tf_op jit(solution)/shard_map/ppermute | solution.py:377
  2.8 1.0 %copy-done.1 = bf16[1024,256]{1,0:T(8,128)(2,1)S(1)} copy-done((bf16[1024,256]{1,0:T(8,128)(2,1)S(1)}, bf16[1024,256]{1,0:T(8,128)(2,1)}, u32[]{:S(2)}) %copy-start.1) | copy-done | bytes 524312
  3.9 0.9 copy-done.4
  4.8 0.4 transform.1
  5.3 1.3 %collective-permute-start.2 = (bf16[1024,128]{1,0:T(8,128)(2,1)S(1)}, bf16[1024,128]{1,0:T(8,128)(2,1)S(1)}, u32[]{:S(2)}, u32[]{:S(2)}) collective-permute-start(bf16[1024,128]{1,0:T(8,128)(2,1)S(1)} %get-tuple-element.24), channel_id=1, source_target_pairs={{0,12},{1,21},{2,14},{3,23},{5,9},{7,11},{8,4},{10,6},{12,24},{13,... | collective-permute-start | bytes 786440 | tf_op jit(solution)/shard_map/ppermute | solution.py:377
  6.6 0.7 collective-permute-start.1
  7.3 0.7 copy.12
  8.0 0.7 copy-done.6
  8.6 1.3 %slot_blocks.1.refs_6_.refs_0_.refs_1_ = s32[2,40]{1,0:T(2,128)S(1)} custom-call(s32[2,5,8]{2,1,0:T(8,128)S(1)} %copy.10.coords_ref, s32[5]{0:T(128)S(1)} %bitcast.9), custom_call_target="tpu_custom_call" | custom-call | tf_op jit(solution)/shard_map/slot_blocks/pallas_call | solution.py:156
  10.0 3.3 %collective-permute-done.2.refs_1_.refs_4_.refs_7_.refs_9_ = bf16[1024,128]{1,0:T(8,128)(2,1)S(1)} collective-permute-done((bf16[1024,128]{1,0:T(8,128)(2,1)S(1)}, bf16[1024,128]{1,0:T(8,128)(2,1)S(1)}, u32[]{:S(2)}, u32[]{:S(2)}) %collective-permute-start.2) | collective-permute-done | bytes 262176 | tf_op jit(solution)/shard_map/ppermute | solution.py:377
  13.4 1.3 %collective-permute-start.4 = (bf16[1024,128]{1,0:T(8,128)(2,1)S(1)}, bf16[1024,128]{1,0:T(8,128)(2,1)S(1)}, u32[]{:S(2)}, u32[]{:S(2)}) collective-permute-start(bf16[1024,128]{1,0:T(8,128)(2,1)S(1)} %get-tuple-element.25), channel_id=1, source_target_pairs={{0,16},{1,17},{2,18},{3,19},{4,20},{5,21},{6,22},{7,23},{8,24},{9,... | collective-permute-start | bytes 786440 | tf_op jit(solution)/shard_map/ppermute | solution.py:377
  14.7 3.8 %collective-permute-start.5 = (bf16[1024,128]{1,0:T(8,128)(2,1)S(1)}, bf16[1024,128]{1,0:T(8,128)(2,1)S(1)}, u32[]{:S(2)}, u32[]{:S(2)}) collective-permute-start(bf16[1024,128]{1,0:T(8,128)(2,1)S(1)} %get-tuple-element.26), channel_id=1, source_target_pairs={{0,8},{1,9},{2,10},{3,11},{4,12},{5,13},{6,14},{7,15},{8,0},{9,1},... | collective-permute-start | bytes 786440 | tf_op jit(solution)/shard_map/ppermute | solution.py:377
  18.5 1.3 %collective-permute-start.8 = (bf16[5,8,128,128]{3,2,1,0:T(8,128)(2,1)S(1)}, bf16[5,8,128,128]{3,2,1,0:T(8,128)(2,1)S(1)}, u32[]{:S(2)}, u32[]{:S(2)}) collective-permute-start(bf16[5,8,128,128]{3,2,1,0:T(8,128)(2,1)S(1)} %collective-permute-done.7.refs_1_.refs_3_), channel_id=1, source_target_pairs={{0,4},{2,6},{5,1},{7,3},{8,12},{10,14},{13,9},{15,11},{16,20},{18,... | collective-permute-start | bytes 3932168 | tf_op jit(solution)/shard_map/ppermute | solution.py:377
  19.8 1.5 %collective-permute-start = (s32[2,40]{1,0:T(2,128)S(1)}, s32[2,40]{1,0:T(2,128)S(1)}, u32[]{:S(2)}, u32[]{:S(2)}) collective-permute-start(s32[2,40]{1,0:T(2,128)S(1)} %slot_blocks.1.refs_6_.refs_0_.refs_1_), channel_id=1, source_target_pairs={{0,4},{1,0},{2,6},{3,2},{4,5},{5,1},{6,7},{7,3},{8,12},{9,8},{10,1... | collective-permute-start | bytes 968 | tf_op jit(solution)/shard_map/ppermute | solution.py:377
  21.5 2.0 %collective-permute-done.refs_0_ = s32[2,40]{1,0:T(2,128)S(1)} collective-permute-done((s32[2,40]{1,0:T(2,128)S(1)}, s32[2,40]{1,0:T(2,128)S(1)}, u32[]{:S(2)}, u32[]{:S(2)}) %collective-permute-start) | collective-permute-done | bytes 352 | tf_op jit(solution)/shard_map/ppermute | solution.py:377
  23.5 1.2 %collective-permute-start.9 = (bf16[1024,128]{1,0:T(8,128)(2,1)S(1)}, bf16[1024,128]{1,0:T(8,128)(2,1)S(1)}, u32[]{:S(2)}, u32[]{:S(2)}) collective-permute-start(bf16[1024,128]{1,0:T(8,128)(2,1)S(1)} %get-tuple-element.31), channel_id=1, source_target_pairs={{0,4},{1,5},{2,6},{3,7},{4,0},{5,1},{6,2},{7,3},{8,12},{9,13},{10,... | collective-permute-start | bytes 786440 | tf_op jit(solution)/shard_map/ppermute | solution.py:377
  24.7 1.3 %collective-permute-start.6 = (s32[2,40]{1,0:T(2,128)S(1)}, s32[2,40]{1,0:T(2,128)S(1)}, u32[]{:S(2)}, u32[]{:S(2)}) collective-permute-start(s32[2,40]{1,0:T(2,128)S(1)} %collective-permute-done.refs_0_), channel_id=1, source_target_pairs={{0,4},{2,6},{5,1},{7,3},{8,12},{10,14},{13,9},{15,11},{16,20},{18,... | collective-permute-start | bytes 968 | tf_op jit(solution)/shard_map/ppermute | solution.py:377
  26.0 1.2 %tile_product.4.refs_12_ = f32[1024,128]{1,0:T(8,128)S(1)} custom-call(s32[2,40]{1,0:T(2,128)S(1)} %collective-permute-done.refs_0_, bf16[5,8,128,128]{3,2,1,0:T(8,128)(2,1)S(1)} %collective-permute-done.7.refs_1_.refs_3_, bf16[1024,128]{1,0:T(8,128)(2,1)S(1)} %get-tuple-element.23.refs_3_.refs_2_.refs_5_.refs_4_.refs_7_, ...), custom_call_target="tpu_custom_call" | custom-call | flops 12582912000 | bytes 196608000 | tf_op jit(solution)/shard_map/tile_product/pallas_call | solution.py:227
  27.2 0.5 collective-permute-done.6.refs_1_.refs_2_
  27.7 1.4 %tile_product.5.refs_0_.part_ref = bf16[1024,128]{1,0:T(8,128)(2,1)S(1)} custom-call(s32[2,40]{1,0:T(2,128)S(1)} %slot_blocks.1.refs_6_.refs_0_.refs_1_, s32[2,40]{1,0:T(2,128)S(1)} %collective-permute-done.6.refs_1_.refs_2_, bf16[5,8,128,128]{3,2,1,0:T(8,128)(2,1)S(1)} %bitcast.6, bf16[5,8,128,128]{3,2,1,0:T(8,128)(2,1)S(1)} %collective-permute-done.8.refs_3_.refs_5_, ...), custom_call_target="tpu_custom_call" | custom-call | flops 167772160 | bytes 2621440 | tf_op jit(solution)/shard_map/tile_product/pallas_call | solution.py:227
  29.1 0.7 collective-permute-start.11
  29.8 1.3 %collective-permute-start.12 = (bf16[16,128]{1,0:T(8,128)(2,1)S(1)}, bf16[16,128]{1,0:T(8,128)(2,1)S(1)}, u32[]{:S(2)}, u32[]{:S(2)}) collective-permute-start(bf16[16,128]{1,0:T(8,128)(2,1)S(1)} %slice.4), channel_id=1, source_target_pairs={{0,4},{1,5},{2,6},{3,7},{8,12},{9,13},{10,14},{11,15},{16,20},{17,... | collective-permute-start | bytes 12296 | tf_op jit(solution)/shard_map/ppermute | solution.py:377
  31.1 12.6 %collective-permute-done.12.refs_1_ = bf16[16,128]{1,0:T(8,128)(2,1)S(1)} collective-permute-done((bf16[16,128]{1,0:T(8,128)(2,1)S(1)}, bf16[16,128]{1,0:T(8,128)(2,1)S(1)}, u32[]{:S(2)}, u32[]{:S(2)}) %collective-permute-start.12) | collective-permute-done | bytes 4128 | tf_op jit(solution)/shard_map/ppermute | solution.py:377
  43.8 1.9 %collective-permute-start.13 = (bf16[1024,128]{1,0:T(8,128)(2,1)S(1)}, bf16[1024,128]{1,0:T(8,128)(2,1)S(1)}, u32[]{:S(2)}, u32[]{:S(2)}) collective-permute-start(bf16[1024,128]{1,0:T(8,128)(2,1)S(1)} %pick.5), channel_id=1, source_target_pairs={{4,6},{5,7},{6,4},{7,5},{12,14},{13,15},{14,12},{15,13},{20,22},{2... | collective-permute-start | bytes 786440 | tf_op jit(solution)/shard_map/ppermute | solution.py:377
  45.7 8.2 %collective-permute-done.13.one_ref = bf16[1024,128]{1,0:T(8,128)(2,1)S(1)} collective-permute-done((bf16[1024,128]{1,0:T(8,128)(2,1)S(1)}, bf16[1024,128]{1,0:T(8,128)(2,1)S(1)}, u32[]{:S(2)}, u32[]{:S(2)}) %collective-permute-start.13) | collective-permute-done | bytes 262176 | tf_op jit(solution)/shard_map/ppermute | solution.py:377
  53.9 0.3 middle.1
  54.2 2.3 %collective-permute-start.15 = (bf16[1024,128]{1,0:T(8,128)(2,1)S(1)}, bf16[1024,128]{1,0:T(8,128)(2,1)S(1)}, u32[]{:S(2)}, u32[]{:S(2)}) collective-permute-start(bf16[1024,128]{1,0:T(8,128)(2,1)S(1)} %get-tuple-element.36.refs_6_), channel_id=1, source_target_pairs={{0,8},{1,9},{2,10},{3,11},{4,12},{5,13},{6,14},{7,15},{8,0},{9,1},... | collective-permute-start | bytes 786440 | tf_op jit(solution)/shard_map/ppermute | solution.py:377
  56.5 4.5 %collective-permute-done.15.refs_7_ = bf16[1024,128]{1,0:T(8,128)(2,1)S(1)} collective-permute-done((bf16[1024,128]{1,0:T(8,128)(2,1)S(1)}, bf16[1024,128]{1,0:T(8,128)(2,1)S(1)}, u32[]{:S(2)}, u32[]{:S(2)}) %collective-permute-start.15) | collective-permute-done | bytes 262176 | tf_op jit(solution)/shard_map/ppermute | solution.py:377
  61.0 1.0 %collective-permute-done.14.refs_6_ = bf16[1024,128]{1,0:T(8,128)(2,1)S(1)} collective-permute-done((bf16[1024,128]{1,0:T(8,128)(2,1)S(1)}, bf16[1024,128]{1,0:T(8,128)(2,1)S(1)}, u32[]{:S(2)}, u32[]{:S(2)}) %collective-permute-start.14) | collective-permute-done | bytes 262176 | tf_op jit(solution)/shard_map/ppermute | solution.py:377
  62.0 5.3 %collective-permute-start.16 = (bf16[1024,128]{1,0:T(8,128)(2,1)S(1)}, bf16[1024,128]{1,0:T(8,128)(2,1)S(1)}, u32[]{:S(2)}, u32[]{:S(2)}) collective-permute-start(bf16[1024,128]{1,0:T(8,128)(2,1)S(1)} %get-tuple-element.36.refs_6_), channel_id=1, source_target_pairs={{0,1},{2,3},{4,5},{6,7},{9,8},{11,10},{13,12},{15,14},{16,17},{18,... | collective-permute-start | bytes 786440 | tf_op jit(solution)/shard_map/ppermute | solution.py:377
  67.7 1.2 %tile_product.6.refs_10_ = f32[1024,128]{1,0:T(8,128)S(1)} custom-call(s32[2,40]{1,0:T(2,128)S(1)} %collective-permute-done.refs_0_, s32[2,40]{1,0:T(2,128)S(1)} %slot_blocks.1.refs_6_.refs_0_.refs_1_, s32[2,40]{1,0:T(2,128)S(1)} %collective-permute-done.6.refs_1_.refs_2_, bf16[5,8,128,128]{3,2,1,0:T(8,128)(2,1)S(1)} %collective-permute-done.7.refs_1_.refs_3_, ...), custom_call_target="tpu_custom_call" | custom-call | flops 134217728 | bytes 1572864 | tf_op jit(solution)/shard_map/tile_product/pallas_call | solution.py:227
  68.8 2.2 %collective-permute-done.16.refs_7_ = bf16[1024,128]{1,0:T(8,128)(2,1)S(1)} collective-permute-done((bf16[1024,128]{1,0:T(8,128)(2,1)S(1)}, bf16[1024,128]{1,0:T(8,128)(2,1)S(1)}, u32[]{:S(2)}, u32[]{:S(2)}) %collective-permute-start.16) | collective-permute-done | bytes 262176 | tf_op jit(solution)/shard_map/ppermute | solution.py:377
  71.0 1.9 %collective-permute-done.18.refs_9_ = bf16[1024,128]{1,0:T(8,128)(2,1)S(1)} collective-permute-done((bf16[1024,128]{1,0:T(8,128)(2,1)S(1)}, bf16[1024,128]{1,0:T(8,128)(2,1)S(1)}, u32[]{:S(2)}, u32[]{:S(2)}) %collective-permute-start.18) | collective-permute-done | bytes 262176 | tf_op jit(solution)/shard_map/ppermute | solution.py:377
  73.0 1.4 %tile_product.7.back_ref.refs_0_ = bf16[1024,128]{1,0:T(8,128)(2,1)S(1)} custom-call(s32[2,40]{1,0:T(2,128)S(1)} %collective-permute-done.refs_0_, s32[2,40]{1,0:T(2,128)S(1)} %slot_blocks.1.refs_6_.refs_0_.refs_1_, s32[2,40]{1,0:T(2,128)S(1)} %collective-permute-done.6.refs_1_.refs_2_, bf16[5,8,128,128]{3,2,1,0:T(8,128)(2,1)S(1)} %collective-permute-done.7.refs_1_.refs_3_, ...), custom_call_target="tpu_custom_call" | custom-call | flops 201326592 | bytes 2359296 | tf_op jit(solution)/shard_map/tile_product/pallas_call | solution.py:227
  74.5 0.9 collective-permute-start.22
  75.3 0.3 grad_block.1.refs_0_
  75.7 0.7 collective-permute-start.20
  76.4 6.9 %collective-permute-done.20.refs_1_ = bf16[256,128]{1,0:T(8,128)(2,1)S(1)} collective-permute-done((bf16[256,128]{1,0:T(8,128)(2,1)S(1)}, bf16[256,128]{1,0:T(8,128)(2,1)S(1)}, u32[]{:S(2)}, u32[]{:S(2)}) %collective-permute-start.20) | collective-permute-done | bytes 65568 | tf_op jit(solution)/shard_map/ppermute | solution.py:377
  83.3 1.0 collective-permute-start.21
  84.3 2.5 %collective-permute-done.21.refs_2_.refs_1_ = bf16[256,128]{1,0:T(8,128)(2,1)S(1)} collective-permute-done((bf16[256,128]{1,0:T(8,128)(2,1)S(1)}, bf16[256,128]{1,0:T(8,128)(2,1)S(1)}, u32[]{:S(2)}, u32[]{:S(2)}) %collective-permute-start.21) | collective-permute-done | bytes 65568 | tf_op jit(solution)/shard_map/ppermute | solution.py:377
  86.9 2.0 %collective-permute-start.23 = (bf16[1024,128]{1,0:T(8,128)(2,1)S(1)}, bf16[1024,128]{1,0:T(8,128)(2,1)S(1)}, u32[]{:S(2)}, u32[]{:S(2)}) collective-permute-start(bf16[1024,128]{1,0:T(8,128)(2,1)S(1)} %add_after.6.refs_1_.refs_2_.refs_0_), channel_id=1, source_target_pairs={{0,1},{1,0},{2,3},{3,2},{4,5},{5,4},{6,7},{7,6},{8,9},{9,8},{10,11... | collective-permute-start | bytes 786440 | tf_op jit(solution)/shard_map/ppermute | solution.py:377
  88.9 1.6 %collective-permute-start.26 = (bf16[256,128]{1,0:T(8,128)(2,1)S(1)}, bf16[256,128]{1,0:T(8,128)(2,1)S(1)}, u32[]{:S(2)}, u32[]{:S(2)}) collective-permute-start(bf16[256,128]{1,0:T(8,128)(2,1)S(1)} %add_after.7.refs_0_), channel_id=1, source_target_pairs={{0,16},{1,17},{2,18},{3,19},{4,20},{5,21},{6,22},{7,23},{8,24},{9,... | collective-permute-start | bytes 196616 | tf_op jit(solution)/shard_map/ppermute | solution.py:377
  90.5 1.7 %collective-permute-done.26.refs_1_ = bf16[256,128]{1,0:T(8,128)(2,1)S(1)} collective-permute-done((bf16[256,128]{1,0:T(8,128)(2,1)S(1)}, bf16[256,128]{1,0:T(8,128)(2,1)S(1)}, u32[]{:S(2)}, u32[]{:S(2)}) %collective-permute-start.26) | collective-permute-done | bytes 65568 | tf_op jit(solution)/shard_map/ppermute | solution.py:377
  92.2 0.3 collective-permute-start.27
  92.8 0.5 collective-permute-start.25
  93.3 6.1 %collective-permute-done.27.refs_1_ = f32[256,128]{1,0:T(8,128)S(1)} collective-permute-done((f32[256,128]{1,0:T(8,128)S(1)}, f32[256,128]{1,0:T(8,128)S(1)}, u32[]{:S(2)}, u32[]{:S(2)}) %collective-permute-start.27) | collective-permute-done | bytes 131104 | tf_op jit(solution)/shard_map/ppermute | solution.py:377
  99.5 1.3 %collective-permute-done.28.refs_8_ = f32[256,128]{1,0:T(8,128)S(1)} collective-permute-done((f32[256,128]{1,0:T(8,128)S(1)}, f32[256,128]{1,0:T(8,128)S(1)}, u32[]{:S(2)}, u32[]{:S(2)}) %collective-permute-start.28) | collective-permute-done | bytes 131104 | tf_op jit(solution)/shard_map/ppermute | solution.py:377
  100.9 1.5 %final.1 = (bf16[1024,256]{1,0:T(8,128)(2,1)}, bf16[1024,256]{1,0:T(8,128)(2,1)}, f32[256,256]{1,0:T(8,128)}) custom-call(bf16[1024,128]{1,0:T(8,128)(2,1)S(1)} %add_after.6.refs_1_.refs_2_.refs_0_, bf16[1024,128]{1,0:T(8,128)(2,1)S(1)} %collective-permute-done.23.refs_0_.refs_2_.refs_1_, bf16[1024,128]{1,0:T(8,128)(2,1)S(1)} %collective-permute-done.24.refs_2_, ...), custom_call_target="tpu_custom_call" | custom-call | flops 134217728 | bytes 2097152 | tf_op jit(solution)/shard_map/final/pallas_call | solution.py:355
  (46 shorter events, 1.3 us)
Async XLA Ops:
  0.6 17.9 %collective-permute-start.7 = (bf16[5,8,128,128]{3,2,1,0:T(8,128)(2,1)}, bf16[5,8,128,128]{3,2,1,0:T(8,128)(2,1)S(1)}, u32[]{:S(2)}, u32[]{:S(2)}) collective-permute-start(bf16[5,8,128,128]{3,2,1,0:T(8,128)(2,1)} %bitcast.5), channel_id=1, source_target_pairs={{0,4},{1,0},{2,6},{3,2},{4,5},{5,1},{6,7},{7,3},{8,12},{9,8},{10,1... | collective-permute-start | bytes 3932168 | tf_op jit(solution)/shard_map/ppermute | solution.py:377
  2.8 1.0 %copy-start.1 = (bf16[1024,256]{1,0:T(8,128)(2,1)S(1)}, bf16[1024,256]{1,0:T(8,128)(2,1)}, u32[]{:S(2)}) copy-start(bf16[1024,256]{1,0:T(8,128)(2,1)} %feats_ref.1) | copy-start | bytes 1572868
  3.9 0.9 copy-start.4
  4.8 16.5 %copy-start.2 = (bf16[1024,256]{1,0:T(8,128)(2,1)S(1)}, bf16[1024,256]{1,0:T(8,128)(2,1)}, u32[]{:S(2)}) copy-start(bf16[1024,256]{1,0:T(8,128)(2,1)} %feats_ref.1) | copy-start | bytes 1572868
  4.8 16.6 %copy-start.3 = (bf16[1024,256]{1,0:T(8,128)(2,1)S(1)}, bf16[1024,256]{1,0:T(8,128)(2,1)}, u32[]{:S(2)}) copy-start(bf16[1024,256]{1,0:T(8,128)(2,1)} %x_ref.3) | copy-start | bytes 1572868
  5.2 4.8 %collective-permute-start.3 = (bf16[1024,128]{1,0:T(8,128)(2,1)S(1)}, bf16[1024,128]{1,0:T(8,128)(2,1)S(1)}, u32[]{:S(2)}, u32[]{:S(2)}) collective-permute-start(bf16[1024,128]{1,0:T(8,128)(2,1)S(1)} %get-tuple-element.24), channel_id=1, source_target_pairs={{0,4},{1,5},{2,6},{3,7},{4,0},{5,1},{6,2},{7,3},{8,12},{9,13},{10,... | collective-permute-start | bytes 786440 | tf_op jit(solution)/shard_map/ppermute | solution.py:377
  5.3 8.0 %collective-permute-start.2 = (bf16[1024,128]{1,0:T(8,128)(2,1)S(1)}, bf16[1024,128]{1,0:T(8,128)(2,1)S(1)}, u32[]{:S(2)}, u32[]{:S(2)}) collective-permute-start(bf16[1024,128]{1,0:T(8,128)(2,1)S(1)} %get-tuple-element.24), channel_id=1, source_target_pairs={{0,12},{1,21},{2,14},{3,23},{5,9},{7,11},{8,4},{10,6},{12,24},{13,... | collective-permute-start | bytes 786440 | tf_op jit(solution)/shard_map/ppermute | solution.py:377
  6.6 6.7 %collective-permute-start.1 = (bf16[1024,128]{1,0:T(8,128)(2,1)S(1)}, bf16[1024,128]{1,0:T(8,128)(2,1)S(1)}, u32[]{:S(2)}, u32[]{:S(2)}) collective-permute-start(bf16[1024,128]{1,0:T(8,128)(2,1)S(1)} %get-tuple-element.23.refs_3_.refs_2_.refs_5_.refs_4_.refs_7_), channel_id=1, source_target_pairs={{0,8},{1,17},{2,10},{3,19},{5,13},{7,15},{8,0},{10,2},{12,28},{13,... | collective-permute-start | bytes 786440 | tf_op jit(solution)/shard_map/ppermute | solution.py:377
  8.0 0.7 copy-start.6
  13.4 11.3 %collective-permute-start.4 = (bf16[1024,128]{1,0:T(8,128)(2,1)S(1)}, bf16[1024,128]{1,0:T(8,128)(2,1)S(1)}, u32[]{:S(2)}, u32[]{:S(2)}) collective-permute-start(bf16[1024,128]{1,0:T(8,128)(2,1)S(1)} %get-tuple-element.25), channel_id=1, source_target_pairs={{0,16},{1,17},{2,18},{3,19},{4,20},{5,21},{6,22},{7,23},{8,24},{9,... | collective-permute-start | bytes 786440 | tf_op jit(solution)/shard_map/ppermute | solution.py:377
  14.7 10.0 %collective-permute-start.5 = (bf16[1024,128]{1,0:T(8,128)(2,1)S(1)}, bf16[1024,128]{1,0:T(8,128)(2,1)S(1)}, u32[]{:S(2)}, u32[]{:S(2)}) collective-permute-start(bf16[1024,128]{1,0:T(8,128)(2,1)S(1)} %get-tuple-element.26), channel_id=1, source_target_pairs={{0,8},{1,9},{2,10},{3,11},{4,12},{5,13},{6,14},{7,15},{8,0},{9,1},... | collective-permute-start | bytes 786440 | tf_op jit(solution)/shard_map/ppermute | solution.py:377
  18.5 9.2 %collective-permute-start.8 = (bf16[5,8,128,128]{3,2,1,0:T(8,128)(2,1)S(1)}, bf16[5,8,128,128]{3,2,1,0:T(8,128)(2,1)S(1)}, u32[]{:S(2)}, u32[]{:S(2)}) collective-permute-start(bf16[5,8,128,128]{3,2,1,0:T(8,128)(2,1)S(1)} %collective-permute-done.7.refs_1_.refs_3_), channel_id=1, source_target_pairs={{0,4},{2,6},{5,1},{7,3},{8,12},{10,14},{13,9},{15,11},{16,20},{18,... | collective-permute-start | bytes 3932168 | tf_op jit(solution)/shard_map/ppermute | solution.py:377
  19.8 3.7 %collective-permute-start = (s32[2,40]{1,0:T(2,128)S(1)}, s32[2,40]{1,0:T(2,128)S(1)}, u32[]{:S(2)}, u32[]{:S(2)}) collective-permute-start(s32[2,40]{1,0:T(2,128)S(1)} %slot_blocks.1.refs_6_.refs_0_.refs_1_), channel_id=1, source_target_pairs={{0,4},{1,0},{2,6},{3,2},{4,5},{5,1},{6,7},{7,3},{8,12},{9,8},{10,1... | collective-permute-start | bytes 968 | tf_op jit(solution)/shard_map/ppermute | solution.py:377
  21.3 5.9 %collective-permute-start.10 = (bf16[1024,256]{1,0:T(8,128)(2,1)S(1)}, bf16[1024,256]{1,0:T(8,128)(2,1)S(1)}, u32[]{:S(2)}, u32[]{:S(2)}) collective-permute-start(bf16[1024,256]{1,0:T(8,128)(2,1)S(1)} %copy-done.2), channel_id=1, source_target_pairs={{0,4},{1,5},{2,6},{3,7},{4,0},{5,1},{6,2},{7,3},{8,12},{9,13},{10,... | collective-permute-start | bytes 1572872 | tf_op jit(solution)/shard_map/ppermute | solution.py:377
  23.5 4.2 %copy-start = (bf16[1,5,8,128,128]{4,3,2,1,0:T(8,128)(2,1)S(1)}, bf16[1,5,8,128,128]{4,3,2,1,0:T(8,128)(2,1)}, u32[]{:S(2)}) copy-start(bf16[1,5,8,128,128]{4,3,2,1,0:T(8,128)(2,1)} %param.9) | copy-start | bytes 3932164
  23.5 3.8 %collective-permute-start.9 = (bf16[1024,128]{1,0:T(8,128)(2,1)S(1)}, bf16[1024,128]{1,0:T(8,128)(2,1)S(1)}, u32[]{:S(2)}, u32[]{:S(2)}) collective-permute-start(bf16[1024,128]{1,0:T(8,128)(2,1)S(1)} %get-tuple-element.31), channel_id=1, source_target_pairs={{0,4},{1,5},{2,6},{3,7},{4,0},{5,1},{6,2},{7,3},{8,12},{9,13},{10,... | collective-permute-start | bytes 786440 | tf_op jit(solution)/shard_map/ppermute | solution.py:377
  24.7 3.0 %collective-permute-start.6 = (s32[2,40]{1,0:T(2,128)S(1)}, s32[2,40]{1,0:T(2,128)S(1)}, u32[]{:S(2)}, u32[]{:S(2)}) collective-permute-start(s32[2,40]{1,0:T(2,128)S(1)} %collective-permute-done.refs_0_), channel_id=1, source_target_pairs={{0,4},{2,6},{5,1},{7,3},{8,12},{10,14},{13,9},{15,11},{16,20},{18,... | collective-permute-start | bytes 968 | tf_op jit(solution)/shard_map/ppermute | solution.py:377
  29.1 0.7 collective-permute-start.11
  29.8 13.9 %collective-permute-start.12 = (bf16[16,128]{1,0:T(8,128)(2,1)S(1)}, bf16[16,128]{1,0:T(8,128)(2,1)S(1)}, u32[]{:S(2)}, u32[]{:S(2)}) collective-permute-start(bf16[16,128]{1,0:T(8,128)(2,1)S(1)} %slice.4), channel_id=1, source_target_pairs={{0,4},{1,5},{2,6},{3,7},{8,12},{9,13},{10,14},{11,15},{16,20},{17,... | collective-permute-start | bytes 12296 | tf_op jit(solution)/shard_map/ppermute | solution.py:377
  43.8 10.1 %collective-permute-start.13 = (bf16[1024,128]{1,0:T(8,128)(2,1)S(1)}, bf16[1024,128]{1,0:T(8,128)(2,1)S(1)}, u32[]{:S(2)}, u32[]{:S(2)}) collective-permute-start(bf16[1024,128]{1,0:T(8,128)(2,1)S(1)} %pick.5), channel_id=1, source_target_pairs={{4,6},{5,7},{6,4},{7,5},{12,14},{13,15},{14,12},{15,13},{20,22},{2... | collective-permute-start | bytes 786440 | tf_op jit(solution)/shard_map/ppermute | solution.py:377
  54.2 6.8 %collective-permute-start.15 = (bf16[1024,128]{1,0:T(8,128)(2,1)S(1)}, bf16[1024,128]{1,0:T(8,128)(2,1)S(1)}, u32[]{:S(2)}, u32[]{:S(2)}) collective-permute-start(bf16[1024,128]{1,0:T(8,128)(2,1)S(1)} %get-tuple-element.36.refs_6_), channel_id=1, source_target_pairs={{0,8},{1,9},{2,10},{3,11},{4,12},{5,13},{6,14},{7,15},{8,0},{9,1},... | collective-permute-start | bytes 786440 | tf_op jit(solution)/shard_map/ppermute | solution.py:377
  56.5 5.5 %collective-permute-start.14 = (bf16[1024,128]{1,0:T(8,128)(2,1)S(1)}, bf16[1024,128]{1,0:T(8,128)(2,1)S(1)}, u32[]{:S(2)}, u32[]{:S(2)}) collective-permute-start(bf16[1024,128]{1,0:T(8,128)(2,1)S(1)} %get-tuple-element.36.refs_6_), channel_id=1, source_target_pairs={{0,17},{1,0},{2,19},{3,2},{4,21},{5,4},{6,23},{7,6},{8,9},{9,24},{... | collective-permute-start | bytes 786440 | tf_op jit(solution)/shard_map/ppermute | solution.py:377
  62.0 9.0 %collective-permute-start.16 = (bf16[1024,128]{1,0:T(8,128)(2,1)S(1)}, bf16[1024,128]{1,0:T(8,128)(2,1)S(1)}, u32[]{:S(2)}, u32[]{:S(2)}) collective-permute-start(bf16[1024,128]{1,0:T(8,128)(2,1)S(1)} %get-tuple-element.36.refs_6_), channel_id=1, source_target_pairs={{0,1},{2,3},{4,5},{6,7},{9,8},{11,10},{13,12},{15,14},{16,17},{18,... | collective-permute-start | bytes 786440 | tf_op jit(solution)/shard_map/ppermute | solution.py:377
  67.3 5.6 %collective-permute-start.18 = (bf16[1024,128]{1,0:T(8,128)(2,1)S(1)}, bf16[1024,128]{1,0:T(8,128)(2,1)S(1)}, u32[]{:S(2)}, u32[]{:S(2)}) collective-permute-start(bf16[1024,128]{1,0:T(8,128)(2,1)S(1)} %collective-permute-done.14.refs_6_), channel_id=1, source_target_pairs={{0,8},{1,9},{2,10},{3,11},{4,12},{5,13},{6,14},{7,15},{8,0},{9,1},... | collective-permute-start | bytes 786440 | tf_op jit(solution)/shard_map/ppermute | solution.py:377
  67.4 5.6 %collective-permute-start.17 = (bf16[1024,128]{1,0:T(8,128)(2,1)S(1)}, bf16[1024,128]{1,0:T(8,128)(2,1)S(1)}, u32[]{:S(2)}, u32[]{:S(2)}) collective-permute-start(bf16[1024,128]{1,0:T(8,128)(2,1)S(1)} %collective-permute-done.15.refs_7_), channel_id=1, source_target_pairs={{0,16},{1,17},{2,18},{3,19},{4,20},{5,21},{6,22},{7,23},{8,24},{9,... | collective-permute-start | bytes 786440 | tf_op jit(solution)/shard_map/ppermute | solution.py:377
  74.5 12.4 %collective-permute-start.22 = (bf16[1024,128]{1,0:T(8,128)(2,1)S(1)}, bf16[1024,128]{1,0:T(8,128)(2,1)S(1)}, u32[]{:S(2)}, u32[]{:S(2)}) collective-permute-start(bf16[1024,128]{1,0:T(8,128)(2,1)S(1)} %get-tuple-element.39.refs_1_.refs_3_), channel_id=1, source_target_pairs={{0,1},{1,0},{2,3},{3,2},{4,5},{5,4},{6,7},{7,6},{8,9},{9,8},{10,11... | collective-permute-start | bytes 786440 | tf_op jit(solution)/shard_map/ppermute | solution.py:377
  75.3 11.5 %collective-permute-start.19 = (bf16[1024,128]{1,0:T(8,128)(2,1)S(1)}, bf16[1024,128]{1,0:T(8,128)(2,1)S(1)}, u32[]{:S(2)}, u32[]{:S(2)}) collective-permute-start(bf16[1024,128]{1,0:T(8,128)(2,1)S(1)} %tile_product.7.back_ref.refs_0_), channel_id=1, source_target_pairs={{0,2},{1,3},{2,0},{3,1},{4,6},{5,7},{6,4},{7,5},{8,10},{9,11},{10,... | collective-permute-start | bytes 786440 | tf_op jit(solution)/shard_map/ppermute | solution.py:377
  75.7 7.6 %collective-permute-start.20 = (bf16[256,128]{1,0:T(8,128)(2,1)S(1)}, bf16[256,128]{1,0:T(8,128)(2,1)S(1)}, u32[]{:S(2)}, u32[]{:S(2)}) collective-permute-start(bf16[256,128]{1,0:T(8,128)(2,1)S(1)} %grad_block.1.refs_0_), channel_id=1, source_target_pairs={{0,1},{1,0},{2,3},{3,2},{4,5},{5,4},{6,7},{7,6},{8,9},{9,8},{10,11... | collective-permute-start | bytes 196616 | tf_op jit(solution)/shard_map/ppermute | solution.py:377
  83.3 3.5 %collective-permute-start.21 = (bf16[256,128]{1,0:T(8,128)(2,1)S(1)}, bf16[256,128]{1,0:T(8,128)(2,1)S(1)}, u32[]{:S(2)}, u32[]{:S(2)}) collective-permute-start(bf16[256,128]{1,0:T(8,128)(2,1)S(1)} %add_after.5.refs_0_), channel_id=1, source_target_pairs={{0,8},{1,9},{2,10},{3,11},{4,12},{5,13},{6,14},{7,15},{8,0},{9,1},... | collective-permute-start | bytes 196616 | tf_op jit(solution)/shard_map/ppermute | solution.py:377
  86.9 5.7 %collective-permute-start.23 = (bf16[1024,128]{1,0:T(8,128)(2,1)S(1)}, bf16[1024,128]{1,0:T(8,128)(2,1)S(1)}, u32[]{:S(2)}, u32[]{:S(2)}) collective-permute-start(bf16[1024,128]{1,0:T(8,128)(2,1)S(1)} %add_after.6.refs_1_.refs_2_.refs_0_), channel_id=1, source_target_pairs={{0,1},{1,0},{2,3},{3,2},{4,5},{5,4},{6,7},{7,6},{8,9},{9,8},{10,11... | collective-permute-start | bytes 786440 | tf_op jit(solution)/shard_map/ppermute | solution.py:377
  88.9 3.3 %collective-permute-start.26 = (bf16[256,128]{1,0:T(8,128)(2,1)S(1)}, bf16[256,128]{1,0:T(8,128)(2,1)S(1)}, u32[]{:S(2)}, u32[]{:S(2)}) collective-permute-start(bf16[256,128]{1,0:T(8,128)(2,1)S(1)} %add_after.7.refs_0_), channel_id=1, source_target_pairs={{0,16},{1,17},{2,18},{3,19},{4,20},{5,21},{6,22},{7,23},{8,24},{9,... | collective-permute-start | bytes 196616 | tf_op jit(solution)/shard_map/ppermute | solution.py:377
  92.2 8.7 %copy-start.5 = (bf16[256,256]{1,0:T(8,128)(2,1)S(1)}, bf16[256,256]{1,0:T(8,128)(2,1)}, u32[]{:S(2)}) copy-start(bf16[256,256]{1,0:T(8,128)(2,1)} %refs_6_.1) | copy-start | bytes 393220
  92.2 7.2 %collective-permute-start.27 = (f32[256,128]{1,0:T(8,128)S(1)}, f32[256,128]{1,0:T(8,128)S(1)}, u32[]{:S(2)}, u32[]{:S(2)}) collective-permute-start(f32[256,128]{1,0:T(8,128)S(1)} %add_after.8.refs_0_), channel_id=1, source_target_pairs={{0,2},{1,3},{2,0},{3,1},{4,6},{5,7},{6,4},{7,5},{8,10},{9,11},{10,... | collective-permute-start | bytes 393224 | tf_op jit(solution)/shard_map/ppermute | solution.py:377
  92.7 8.2 %collective-permute-start.24 = (bf16[1024,128]{1,0:T(8,128)(2,1)S(1)}, bf16[1024,128]{1,0:T(8,128)(2,1)S(1)}, u32[]{:S(2)}, u32[]{:S(2)}) collective-permute-start(bf16[1024,128]{1,0:T(8,128)(2,1)S(1)} %pick.6), channel_id=1, source_target_pairs={{0,4},{1,5},{2,6},{3,7},{4,0},{5,1},{6,2},{7,3},{8,12},{9,13},{10,... | collective-permute-start | bytes 786440 | tf_op jit(solution)/shard_map/ppermute | solution.py:377
  92.8 8.1 %collective-permute-start.25 = (bf16[1024,128]{1,0:T(8,128)(2,1)S(1)}, bf16[1024,128]{1,0:T(8,128)(2,1)S(1)}, u32[]{:S(2)}, u32[]{:S(2)}) collective-permute-start(bf16[1024,128]{1,0:T(8,128)(2,1)S(1)} %pick.7), channel_id=1, source_target_pairs={{0,4},{1,5},{2,6},{3,7},{4,0},{5,1},{6,2},{7,3},{8,12},{9,13},{10,... | collective-permute-start | bytes 786440 | tf_op jit(solution)/shard_map/ppermute | solution.py:377
  99.4 1.4 %collective-permute-start.28 = (f32[256,128]{1,0:T(8,128)S(1)}, f32[256,128]{1,0:T(8,128)S(1)}, u32[]{:S(2)}, u32[]{:S(2)}) collective-permute-start(f32[256,128]{1,0:T(8,128)S(1)} %add_after.9.refs_7_), channel_id=1, source_target_pairs={{0,4},{1,5},{2,6},{3,7},{4,0},{5,1},{6,2},{7,3},{8,12},{9,13},{10,... | collective-permute-start | bytes 393224 | tf_op jit(solution)/shard_map/ppermute | solution.py:377

commit v12 on v10

--- a/solution.py
+++ b/solution.py
@@ -421,7 +421,9 @@
         return to and (to[0], 1 - j, z)
 
     first = send(own, to_home)
-    mine, yours = halves(node_feats)
+    half = node_feats.shape[1] // 2
+    mine = lax.dynamic_slice_in_dim(node_feats, j * half, half, 1)
+    yours = lax.dynamic_slice_in_dim(node_feats, (1 - j) * half, half, 1)
     one = send(mine, stage_one)
     two = send(yours, stage_one_cross)
     swapped = send(yours, sibling)
@@ -443,9 +445,9 @@
     second = send(second, to_second)
     far = send(far, to_far)
     meta_b = send(meta, to_home)
-    first, one, two = lax.optimization_barrier((first, one, two))
+    first, meta_b = lax.optimization_barrier((first, meta_b))
     other_first = send(first, home_to_sibling)
-    meta_later, second, far = lax.optimization_barrier((meta_b, second, far))
+    meta_later, second = lax.optimization_barrier((meta_b, second))
     meta_far = send(meta_later, home_to_sibling)
     set_first = [(None, (meta_b, first))]
     panels = [
@@ -474,16 +476,16 @@
     )
     adj_later, near_one, direct = lax.optimization_barrier((adj, near_one, direct))
     second = send(direct if four else adj_later, to_second)
-    grad = grad_block(scale, near, far_half, adj, adj)
-    grad_got = send(grad, lambda c, j, z: (c, j, z ^ 1))
-    adj_soon, grad_got = lax.optimization_barrier((adj, grad_got))
+    grad = grad_block(scale, near, far_half, adj, direct)
+    adj_later, grad = lax.optimization_barrier((adj_later, grad))
     far = send(near_one, to_far)
     near_choice = [("still", near_one)]
     if four:
         near_two = send(
-            adj_soon, lambda c, j, z: None if (c + z) % 2 else (c, j, z ^ 1)
+            adj_later, lambda c, j, z: None if (c + z) % 2 else (c, j, z ^ 1)
         )
         near_choice.append(("relay", near_two))
+    grad_got = send(grad, lambda c, j, z: (c, j, z ^ 1))
     panels = [("self", [(None, adj)]), ("direct", [(None, direct)])]
     back_part = tile_product(panels, [set_first, set_rest], jnp.float32)
     panels = [("near", near_choice), ("second", [(None, second)]), ("far", [(None, far)])]

time: 93.6 us -> 91 us (0.972)
  waiting for transfers between devices: 36.7 us -> 34.7 us
  starting transfers between devices: 43.2 us -> 41.8 us
    ppermute x26, waiting for transfers between devices: 36.7 us -> 34.7 us  [send(): return lax.ppermute(value, AXES, route(shape, move))]
    ppermute x26, starting transfers between devices: 43.2 us -> 41.8 us  [send(): return lax.ppermute(value, AXES, route(shape, move))]
    dynamic_slice x0 -> x1, local copies, waits for them, and re-layouts: none -> 1.06 us  [per_device(): yours = lax.dynamic_slice_in_dim(node_feats, (1 - j) * half, half, 1)]
    unnamed x11 -> x9, local copies, waits for them, and re-layouts: 2.4 us -> 1.36 us
  transfers between devices with their start and end apart: 26 -> 26, of which waited for: 15 -> 16; matrix products, arithmetic and copies ran while one was open for 1% -> 2% of each run, Pallas kernels for 6% -> 6%
where the time goes in v12:
time: 91 us; the launch traced here: 89.7 us
  starting transfers between devices  41.8 us (46%)
  waiting for transfers between devices  34.7 us (38%)
  Pallas kernels  9.9 us (11%)
  local copies, waits for them, and re-layouts  2.43 us (3%)
    ppermute x26, starting transfers between devices, send(): return lax.ppermute(value, AXES, route(shape, move))  41.8 us
    ppermute x26, waiting for transfers between devices, send(): return lax.ppermute(value, AXES, route(shape, move))  34.7 us
    pallas_call x4, Pallas kernels, tile_product(): pl.pallas_call(functools.partial(tile_kernel, kinds, cases, [[case for ca...  5.25 us
  transfers between devices with their start and end apart: 26, of which 16 were waited for; matrix products, arithmetic and copies ran while one was open for 2% of the time, Pallas kernels for 6%

profile of v12, /device:TPU:1, one launch (start us, length us, event | category | flops | bytes accessed | tf_op | source)
XLA Modules:
  0.0 89.7 jit_solution(1241070176150169353)
XLA Ops:
  0.6 2.2 %collective-permute-start = (bf16[5,8,128,128]{3,2,1,0:T(8,128)(2,1)}, bf16[5,8,128,128]{3,2,1,0:T(8,128)(2,1)S(1)}, u32[]{:S(2)}, u32[]{:S(2)}) collective-permute-start(bf16[5,8,128,128]{3,2,1,0:T(8,128)(2,1)} %bitcast.5), channel_id=1, source_target_pairs={{0,4},{1,0},{2,6},{3,2},{4,5},{5,1},{6,7},{7,3},{8,12},{9,8},{10,1... | collective-permute-start | bytes 3932168 | tf_op jit(solution)/shard_map/ppermute | solution.py:386
  2.8 1.1 %constant_dynamic-slice_fusion = (bf16[1024,128]{1,0:T(8,128)(2,1)S(1)}, bf16[1024,128]{1,0:T(8,128)(2,1)S(1)}) fusion(bf16[1024,256]{1,0:T(8,128)(2,1)} %param.6, s32[]{:T(128)S(6)} %select_n.15, s32[]{:T(128)S(6)} %select_n.14), kind=kLoop, calls=%fused_computation.2 | loop fusion | bytes 1048584 | tf_op jit(solution)/shard_map/dynamic_slice | solution.py:426
  3.9 0.7 collective-permute-start.2
  4.6 1.3 %collective-permute-start.3 = (bf16[1024,128]{1,0:T(8,128)(2,1)S(1)}, bf16[1024,128]{1,0:T(8,128)(2,1)S(1)}, u32[]{:S(2)}, u32[]{:S(2)}) collective-permute-start(bf16[1024,128]{1,0:T(8,128)(2,1)S(1)} %get-tuple-element.41), channel_id=1, source_target_pairs={{0,12},{1,21},{2,14},{3,23},{5,9},{7,11},{8,4},{10,6},{12,24},{13,... | collective-permute-start | bytes 786440 | tf_op jit(solution)/shard_map/ppermute | solution.py:386
  5.9 4.8 %collective-permute-start.4 = (bf16[1024,128]{1,0:T(8,128)(2,1)S(1)}, bf16[1024,128]{1,0:T(8,128)(2,1)S(1)}, u32[]{:S(2)}, u32[]{:S(2)}) collective-permute-start(bf16[1024,128]{1,0:T(8,128)(2,1)S(1)} %get-tuple-element.41), channel_id=1, source_target_pairs={{0,4},{1,5},{2,6},{3,7},{4,0},{5,1},{6,2},{7,3},{8,12},{9,13},{10,... | collective-permute-start | bytes 786440 | tf_op jit(solution)/shard_map/ppermute | solution.py:386
  10.6 0.7 copy.12
  11.3 0.7 copy-done.3
  12.0 1.3 %slot_blocks.1.refs_6_.refs_0_.refs_1_ = s32[2,40]{1,0:T(2,128)S(1)} custom-call(s32[2,5,8]{2,1,0:T(8,128)S(1)} %copy.10.coords_ref, s32[5]{0:T(128)S(1)} %bitcast.9), custom_call_target="tpu_custom_call" | custom-call | tf_op jit(solution)/shard_map/slot_blocks/pallas_call | solution.py:133
  13.6 1.8 %collective-permute-start.5 = (bf16[1024,128]{1,0:T(8,128)(2,1)S(1)}, bf16[1024,128]{1,0:T(8,128)(2,1)S(1)}, u32[]{:S(2)}, u32[]{:S(2)}) collective-permute-start(bf16[1024,128]{1,0:T(8,128)(2,1)S(1)} %get-tuple-element.23), channel_id=1, source_target_pairs={{0,16},{1,17},{2,18},{3,19},{4,20},{5,21},{6,22},{7,23},{8,24},{9,... | collective-permute-start | bytes 786440 | tf_op jit(solution)/shard_map/ppermute | solution.py:386
  15.4 1.2 %collective-permute-start.8 = (bf16[1024,128]{1,0:T(8,128)(2,1)S(1)}, bf16[1024,128]{1,0:T(8,128)(2,1)S(1)}, u32[]{:S(2)}, u32[]{:S(2)}) collective-permute-start(bf16[1024,128]{1,0:T(8,128)(2,1)S(1)} %get-tuple-element.27), channel_id=1, source_target_pairs={{0,8},{1,9},{2,10},{3,11},{4,12},{5,13},{6,14},{7,15},{8,0},{9,1},... | collective-permute-start | bytes 786440 | tf_op jit(solution)/shard_map/ppermute | solution.py:386
  16.8 1.5 %collective-permute-done.1.refs_0_ = s32[2,40]{1,0:T(2,128)S(1)} collective-permute-done((s32[2,40]{1,0:T(2,128)S(1)}, s32[2,40]{1,0:T(2,128)S(1)}, u32[]{:S(2)}, u32[]{:S(2)}) %collective-permute-start.1) | collective-permute-done | bytes 352 | tf_op jit(solution)/shard_map/ppermute | solution.py:386
  18.3 1.3 %collective-permute-start.7 = (bf16[5,8,128,128]{3,2,1,0:T(8,128)(2,1)S(1)}, bf16[5,8,128,128]{3,2,1,0:T(8,128)(2,1)S(1)}, u32[]{:S(2)}, u32[]{:S(2)}) collective-permute-start(bf16[5,8,128,128]{3,2,1,0:T(8,128)(2,1)S(1)} %collective-permute-done.refs_1_.refs_3_), channel_id=1, source_target_pairs={{0,4},{2,6},{5,1},{7,3},{8,12},{10,14},{13,9},{15,11},{16,20},{18,... | collective-permute-start | bytes 3932168 | tf_op jit(solution)/shard_map/ppermute | solution.py:386
  19.6 1.9 %collective-permute-done.5.refs_8_.refs_10_ = bf16[1024,128]{1,0:T(8,128)(2,1)S(1)} collective-permute-done((bf16[1024,128]{1,0:T(8,128)(2,1)S(1)}, bf16[1024,128]{1,0:T(8,128)(2,1)S(1)}, u32[]{:S(2)}, u32[]{:S(2)}) %collective-permute-start.5) | collective-permute-done | bytes 262176 | tf_op jit(solution)/shard_map/ppermute | solution.py:386
  21.5 1.3 %collective-permute-start.6 = (s32[2,40]{1,0:T(2,128)S(1)}, s32[2,40]{1,0:T(2,128)S(1)}, u32[]{:S(2)}, u32[]{:S(2)}) collective-permute-start(s32[2,40]{1,0:T(2,128)S(1)} %collective-permute-done.1.refs_0_), channel_id=1, source_target_pairs={{0,4},{2,6},{5,1},{7,3},{8,12},{10,14},{13,9},{15,11},{16,20},{18,... | collective-permute-start | bytes 968 | tf_op jit(solution)/shard_map/ppermute | solution.py:386
  22.8 0.3 collective-permute-done.8.refs_9_.refs_11_
  23.0 1.2 %tile_product.4.refs_12_ = f32[1024,128]{1,0:T(8,128)S(1)} custom-call(s32[2,40]{1,0:T(2,128)S(1)} %collective-permute-done.1.refs_0_, bf16[5,8,128,128]{3,2,1,0:T(8,128)(2,1)S(1)} %collective-permute-done.refs_1_.refs_3_, bf16[1024,128]{1,0:T(8,128)(2,1)S(1)} %get-tuple-element.42.refs_3_.refs_2_.refs_5_.refs_4_.refs_7_, ...), custom_call_target="tpu_custom_call" | custom-call | flops 12582912000 | bytes 196608000 | tf_op jit(solution)/shard_map/tile_product/pallas_call | solution.py:204
  24.3 0.8 collective-permute-done.6.refs_1_.refs_2_
  25.0 1.4 %tile_product.5 = bf16[1024,128]{1,0:T(8,128)(2,1)S(1)} custom-call(s32[2,40]{1,0:T(2,128)S(1)} %slot_blocks.1.refs_6_.refs_0_.refs_1_, s32[2,40]{1,0:T(2,128)S(1)} %collective-permute-done.6.refs_1_.refs_2_, bf16[5,8,128,128]{3,2,1,0:T(8,128)(2,1)S(1)} %bitcast.6, bf16[5,8,128,128]{3,2,1,0:T(8,128)(2,1)S(1)} %collective-permute-done.7.refs_3_.refs_5_, ...), custom_call_target="tpu_custom_call" | custom-call | flops 167772160 | bytes 2621440 | tf_op jit(solution)/shard_map/tile_product/pallas_call | solution.py:204
  26.5 2.4 %collective-permute-start.9 = (bf16[1024,128]{1,0:T(8,128)(2,1)S(1)}, bf16[1024,128]{1,0:T(8,128)(2,1)S(1)}, u32[]{:S(2)}, u32[]{:S(2)}) collective-permute-start(bf16[1024,128]{1,0:T(8,128)(2,1)S(1)} %tile_product.5), channel_id=1, source_target_pairs={{0,2},{1,3},{2,0},{3,1},{4,6},{5,7},{6,4},{7,5},{8,10},{9,11},{10,... | collective-permute-start | bytes 786440 | tf_op jit(solution)/shard_map/ppermute | solution.py:386
  29.0 0.8 collective-permute-start.11
  29.7 10.9 %collective-permute-done.9 = bf16[1024,128]{1,0:T(8,128)(2,1)S(1)} collective-permute-done((bf16[1024,128]{1,0:T(8,128)(2,1)S(1)}, bf16[1024,128]{1,0:T(8,128)(2,1)S(1)}, u32[]{:S(2)}, u32[]{:S(2)}) %collective-permute-start.9) | collective-permute-done | bytes 262176 | tf_op jit(solution)/shard_map/ppermute | solution.py:386
  40.7 1.2 %collective-permute-start.10 = (bf16[1024,128]{1,0:T(8,128)(2,1)S(1)}, bf16[1024,128]{1,0:T(8,128)(2,1)S(1)}, u32[]{:S(2)}, u32[]{:S(2)}) collective-permute-start(bf16[1024,128]{1,0:T(8,128)(2,1)S(1)} %add_convert_fusion.near_ref), channel_id=1, source_target_pairs={{0,4},{1,5},{2,6},{3,7},{4,0},{5,1},{6,2},{7,3},{8,12},{9,13},{10,... | collective-permute-start | bytes 786440 | tf_op jit(solution)/shard_map/ppermute | solution.py:386
  41.9 1.2 %collective-permute-done.10.far_ref = bf16[1024,128]{1,0:T(8,128)(2,1)S(1)} collective-permute-done((bf16[1024,128]{1,0:T(8,128)(2,1)S(1)}, bf16[1024,128]{1,0:T(8,128)(2,1)S(1)}, u32[]{:S(2)}, u32[]{:S(2)}) %collective-permute-start.10) | collective-permute-done | bytes 262176 | tf_op jit(solution)/shard_map/ppermute | solution.py:386
  43.1 0.4 middle.1
  43.5 1.8 %collective-permute-start.12 = (bf16[1024,128]{1,0:T(8,128)(2,1)S(1)}, bf16[1024,128]{1,0:T(8,128)(2,1)S(1)}, u32[]{:S(2)}, u32[]{:S(2)}) collective-permute-start(bf16[1024,128]{1,0:T(8,128)(2,1)S(1)} %get-tuple-element.35.adj_ref.refs_6_), channel_id=1, source_target_pairs={{0,17},{1,0},{2,19},{3,2},{4,21},{5,4},{6,23},{7,6},{8,9},{9,24},{... | collective-permute-start | bytes 786440 | tf_op jit(solution)/shard_map/ppermute | solution.py:386
  45.4 5.7 %collective-permute-done.12.refs_6_ = bf16[1024,128]{1,0:T(8,128)(2,1)S(1)} collective-permute-done((bf16[1024,128]{1,0:T(8,128)(2,1)S(1)}, bf16[1024,128]{1,0:T(8,128)(2,1)S(1)}, u32[]{:S(2)}, u32[]{:S(2)}) %collective-permute-start.12) | collective-permute-done | bytes 262176 | tf_op jit(solution)/shard_map/ppermute | solution.py:386
  51.0 1.4 %collective-permute-done.13.after_ref.refs_7_ = bf16[1024,128]{1,0:T(8,128)(2,1)S(1)} collective-permute-done((bf16[1024,128]{1,0:T(8,128)(2,1)S(1)}, bf16[1024,128]{1,0:T(8,128)(2,1)S(1)}, u32[]{:S(2)}, u32[]{:S(2)}) %collective-permute-start.13) | collective-permute-done | bytes 262176 | tf_op jit(solution)/shard_map/ppermute | solution.py:386
  52.4 0.2 collective-permute-start.15
  52.6 0.3 grad_block.1.refs_0_
  53.0 3.2 %collective-permute-start.14 = (bf16[1024,128]{1,0:T(8,128)(2,1)S(1)}, bf16[1024,128]{1,0:T(8,128)(2,1)S(1)}, u32[]{:S(2)}, u32[]{:S(2)}) collective-permute-start(bf16[1024,128]{1,0:T(8,128)(2,1)S(1)} %get-tuple-element.35.adj_ref.refs_6_), channel_id=1, source_target_pairs={{0,1},{2,3},{4,5},{6,7},{9,8},{11,10},{13,12},{15,14},{16,17},{18,... | collective-permute-start | bytes 786440 | tf_op jit(solution)/shard_map/ppermute | solution.py:386
  56.3 1.5 %collective-permute-start.17 = (bf16[256,128]{1,0:T(8,128)(2,1)S(1)}, bf16[256,128]{1,0:T(8,128)(2,1)S(1)}, u32[]{:S(2)}, u32[]{:S(2)}) collective-permute-start(bf16[256,128]{1,0:T(8,128)(2,1)S(1)} %grad_block.1.refs_0_), channel_id=1, source_target_pairs={{0,1},{1,0},{2,3},{3,2},{4,5},{5,4},{6,7},{7,6},{8,9},{9,8},{10,11... | collective-permute-start | bytes 196616 | tf_op jit(solution)/shard_map/ppermute | solution.py:386
  57.8 1.2 %tile_product.6.refs_10_ = f32[1024,128]{1,0:T(8,128)S(1)} custom-call(s32[2,40]{1,0:T(2,128)S(1)} %collective-permute-done.1.refs_0_, s32[2,40]{1,0:T(2,128)S(1)} %slot_blocks.1.refs_6_.refs_0_.refs_1_, s32[2,40]{1,0:T(2,128)S(1)} %collective-permute-done.6.refs_1_.refs_2_, bf16[5,8,128,128]{3,2,1,0:T(8,128)(2,1)S(1)} %collective-permute-done.refs_1_.refs_3_, ...), custom_call_target="tpu_custom_call" | custom-call | flops 134217728 | bytes 1572864 | tf_op jit(solution)/shard_map/tile_product/pallas_call | solution.py:204
  59.0 2.6 %collective-permute-done.17.refs_11_.refs_1_ = bf16[256,128]{1,0:T(8,128)(2,1)S(1)} collective-permute-done((bf16[256,128]{1,0:T(8,128)(2,1)S(1)}, bf16[256,128]{1,0:T(8,128)(2,1)S(1)}, u32[]{:S(2)}, u32[]{:S(2)}) %collective-permute-start.17) | collective-permute-done | bytes 65568 | tf_op jit(solution)/shard_map/ppermute | solution.py:386
  61.6 0.6 collective-permute-done.16.refs_9_
  62.2 1.5 %tile_product.7.refs_2_.refs_0_ = bf16[1024,128]{1,0:T(8,128)(2,1)S(1)} custom-call(s32[2,40]{1,0:T(2,128)S(1)} %collective-permute-done.1.refs_0_, s32[2,40]{1,0:T(2,128)S(1)} %slot_blocks.1.refs_6_.refs_0_.refs_1_, s32[2,40]{1,0:T(2,128)S(1)} %collective-permute-done.6.refs_1_.refs_2_, bf16[5,8,128,128]{3,2,1,0:T(8,128)(2,1)S(1)} %collective-permute-done.refs_1_.refs_3_, ...), custom_call_target="tpu_custom_call" | custom-call | flops 201326592 | bytes 2359296 | tf_op jit(solution)/shard_map/tile_product/pallas_call | solution.py:204
  63.6 3.3 %collective-permute-start.22 = (bf16[1024,128]{1,0:T(8,128)(2,1)S(1)}, bf16[1024,128]{1,0:T(8,128)(2,1)S(1)}, u32[]{:S(2)}, u32[]{:S(2)}) collective-permute-start(bf16[1024,128]{1,0:T(8,128)(2,1)S(1)} %tile_product.7.refs_2_.refs_0_), channel_id=1, source_target_pairs={{0,2},{1,3},{2,0},{3,1},{4,6},{5,7},{6,4},{7,5},{8,10},{9,11},{10,... | collective-permute-start | bytes 786440 | tf_op jit(solution)/shard_map/ppermute | solution.py:386
  67.0 0.6 collective-permute-start.20
  67.6 2.6 %collective-permute-done.20.refs_1_ = bf16[256,128]{1,0:T(8,128)(2,1)S(1)} collective-permute-done((bf16[256,128]{1,0:T(8,128)(2,1)S(1)}, bf16[256,128]{1,0:T(8,128)(2,1)S(1)}, u32[]{:S(2)}, u32[]{:S(2)}) %collective-permute-start.20) | collective-permute-done | bytes 65568 | tf_op jit(solution)/shard_map/ppermute | solution.py:386
  70.2 0.5 collective-permute-start.21
  70.6 4.0 %collective-permute-start.18 = (bf16[1024,128]{1,0:T(8,128)(2,1)S(1)}, bf16[1024,128]{1,0:T(8,128)(2,1)S(1)}, u32[]{:S(2)}, u32[]{:S(2)}) collective-permute-start(bf16[1024,128]{1,0:T(8,128)(2,1)S(1)} %get-tuple-element.37.own_ref), channel_id=1, source_target_pairs={{0,1},{1,5},{2,3},{3,7},{4,0},{5,4},{6,2},{7,6},{8,9},{9,13},{10,1... | collective-permute-start | bytes 786440 | tf_op jit(solution)/shard_map/ppermute | solution.py:386
  74.6 3.1 %collective-permute-start.19 = (bf16[1024,128]{1,0:T(8,128)(2,1)S(1)}, bf16[1024,128]{1,0:T(8,128)(2,1)S(1)}, u32[]{:S(2)}, u32[]{:S(2)}) collective-permute-start(bf16[1024,128]{1,0:T(8,128)(2,1)S(1)} %get-tuple-element.37.own_ref), channel_id=1, source_target_pairs={{1,4},{3,6},{4,1},{6,3},{9,12},{11,14},{12,9},{14,11},{17,20},{19,... | collective-permute-start | bytes 786440 | tf_op jit(solution)/shard_map/ppermute | solution.py:386
  78.0 2.1 %collective-permute-start.24 = (bf16[1024,128]{1,0:T(8,128)(2,1)S(1)}, bf16[1024,128]{1,0:T(8,128)(2,1)S(1)}, u32[]{:S(2)}, u32[]{:S(2)}) collective-permute-start(bf16[1024,128]{1,0:T(8,128)(2,1)S(1)} %add_after.6.refs_2_.own_ref), channel_id=1, source_target_pairs={{0,1},{1,5},{2,3},{3,7},{4,0},{5,4},{6,2},{7,6},{8,9},{9,13},{10,1... | collective-permute-start | bytes 786440 | tf_op jit(solution)/shard_map/ppermute | solution.py:386
  80.1 2.2 %collective-permute-start.25 = (bf16[1024,128]{1,0:T(8,128)(2,1)S(1)}, bf16[1024,128]{1,0:T(8,128)(2,1)S(1)}, u32[]{:S(2)}, u32[]{:S(2)}) collective-permute-start(bf16[1024,128]{1,0:T(8,128)(2,1)S(1)} %add_after.6.refs_2_.own_ref), channel_id=1, source_target_pairs={{1,4},{3,6},{4,1},{6,3},{9,12},{11,14},{12,9},{14,11},{17,20},{19,... | collective-permute-start | bytes 786440 | tf_op jit(solution)/shard_map/ppermute | solution.py:386
  82.4 2.7 %collective-permute-done.19.two_ref = bf16[1024,128]{1,0:T(8,128)(2,1)S(1)} collective-permute-done((bf16[1024,128]{1,0:T(8,128)(2,1)S(1)}, bf16[1024,128]{1,0:T(8,128)(2,1)S(1)}, u32[]{:S(2)}, u32[]{:S(2)}) %collective-permute-start.19) | collective-permute-done | bytes 262176 | tf_op jit(solution)/shard_map/ppermute | solution.py:386
  85.1 1.0 %gather_halves.1 = (bf16[1024,256]{1,0:T(8,128)(2,1)}, f32[256,256]{1,0:T(8,128)}) custom-call(bf16[1024,128]{1,0:T(8,128)(2,1)S(1)} %get-tuple-element.37.own_ref, bf16[1024,128]{1,0:T(8,128)(2,1)S(1)} %collective-permute-done.18.one_ref, bf16[1024,128]{1,0:T(8,128)(2,1)S(1)} %collective-permute-done.19.two_ref, f32[256,128]{1,0:T(8,128)S(1)} %add_after.7.grad_ref, ...), custom_call_target="tpu_custom_call" | custom-call | tf_op jit(solution)/shard_map/gather_halves/pallas_call | solution.py:338
  86.1 0.2 collective-permute-done.24.one_ref
  86.3 2.2 %collective-permute-done.25.two_ref = bf16[1024,128]{1,0:T(8,128)(2,1)S(1)} collective-permute-done((bf16[1024,128]{1,0:T(8,128)(2,1)S(1)}, bf16[1024,128]{1,0:T(8,128)(2,1)S(1)}, u32[]{:S(2)}, u32[]{:S(2)}) %collective-permute-start.25) | collective-permute-done | bytes 262176 | tf_op jit(solution)/shard_map/ppermute | solution.py:386
  88.5 1.2 %final.1 = bf16[1024,256]{1,0:T(8,128)(2,1)} custom-call(bf16[1024,128]{1,0:T(8,128)(2,1)S(1)} %add_after.6.refs_2_.own_ref, bf16[1024,128]{1,0:T(8,128)(2,1)S(1)} %collective-permute-done.24.one_ref, bf16[1024,128]{1,0:T(8,128)(2,1)S(1)} %collective-permute-done.25.two_ref, bf16[256,256]{1,0:T(8,128)(2,1)S(1)} %copy-done.2), custom_call_target="tpu_custom_call" | custom-call | flops 134217728 | bytes 2097152 | tf_op jit(solution)/shard_map/final/pallas_call | solution.py:364
  (31 shorter events, 1.2 us)
Async XLA Ops:
  0.6 17.7 %collective-permute-start = (bf16[5,8,128,128]{3,2,1,0:T(8,128)(2,1)}, bf16[5,8,128,128]{3,2,1,0:T(8,128)(2,1)S(1)}, u32[]{:S(2)}, u32[]{:S(2)}) collective-permute-start(bf16[5,8,128,128]{3,2,1,0:T(8,128)(2,1)} %bitcast.5), channel_id=1, source_target_pairs={{0,4},{1,0},{2,6},{3,2},{4,5},{5,1},{6,7},{7,3},{8,12},{9,8},{10,1... | collective-permute-start | bytes 3932168 | tf_op jit(solution)/shard_map/ppermute | solution.py:386
  3.9 9.5 %collective-permute-start.2 = (bf16[1024,128]{1,0:T(8,128)(2,1)S(1)}, bf16[1024,128]{1,0:T(8,128)(2,1)S(1)}, u32[]{:S(2)}, u32[]{:S(2)}) collective-permute-start(bf16[1024,128]{1,0:T(8,128)(2,1)S(1)} %get-tuple-element.42.refs_3_.refs_2_.refs_5_.refs_4_.refs_7_), channel_id=1, source_target_pairs={{0,8},{1,17},{2,10},{3,19},{5,13},{7,15},{8,0},{10,2},{12,28},{13,... | collective-permute-start | bytes 786440 | tf_op jit(solution)/shard_map/ppermute | solution.py:386
  4.6 8.9 %collective-permute-start.3 = (bf16[1024,128]{1,0:T(8,128)(2,1)S(1)}, bf16[1024,128]{1,0:T(8,128)(2,1)S(1)}, u32[]{:S(2)}, u32[]{:S(2)}) collective-permute-start(bf16[1024,128]{1,0:T(8,128)(2,1)S(1)} %get-tuple-element.41), channel_id=1, source_target_pairs={{0,12},{1,21},{2,14},{3,23},{5,9},{7,11},{8,4},{10,6},{12,24},{13,... | collective-permute-start | bytes 786440 | tf_op jit(solution)/shard_map/ppermute | solution.py:386
  5.9 7.6 %collective-permute-start.4 = (bf16[1024,128]{1,0:T(8,128)(2,1)S(1)}, bf16[1024,128]{1,0:T(8,128)(2,1)S(1)}, u32[]{:S(2)}, u32[]{:S(2)}) collective-permute-start(bf16[1024,128]{1,0:T(8,128)(2,1)S(1)} %get-tuple-element.41), channel_id=1, source_target_pairs={{0,4},{1,5},{2,6},{3,7},{4,0},{5,1},{6,2},{7,3},{8,12},{9,13},{10,... | collective-permute-start | bytes 786440 | tf_op jit(solution)/shard_map/ppermute | solution.py:386
  11.3 0.7 copy-start.3
  13.6 7.9 %collective-permute-start.5 = (bf16[1024,128]{1,0:T(8,128)(2,1)S(1)}, bf16[1024,128]{1,0:T(8,128)(2,1)S(1)}, u32[]{:S(2)}, u32[]{:S(2)}) collective-permute-start(bf16[1024,128]{1,0:T(8,128)(2,1)S(1)} %get-tuple-element.23), channel_id=1, source_target_pairs={{0,16},{1,17},{2,18},{3,19},{4,20},{5,21},{6,22},{7,23},{8,24},{9,... | collective-permute-start | bytes 786440 | tf_op jit(solution)/shard_map/ppermute | solution.py:386
  15.4 9.7 %copy-start = (bf16[1,5,8,128,128]{4,3,2,1,0:T(8,128)(2,1)S(1)}, bf16[1,5,8,128,128]{4,3,2,1,0:T(8,128)(2,1)}, u32[]{:S(2)}) copy-start(bf16[1,5,8,128,128]{4,3,2,1,0:T(8,128)(2,1)} %param.9) | copy-start | bytes 3932164
  15.4 7.6 %collective-permute-start.8 = (bf16[1024,128]{1,0:T(8,128)(2,1)S(1)}, bf16[1024,128]{1,0:T(8,128)(2,1)S(1)}, u32[]{:S(2)}, u32[]{:S(2)}) collective-permute-start(bf16[1024,128]{1,0:T(8,128)(2,1)S(1)} %get-tuple-element.27), channel_id=1, source_target_pairs={{0,8},{1,9},{2,10},{3,11},{4,12},{5,13},{6,14},{7,15},{8,0},{9,1},... | collective-permute-start | bytes 786440 | tf_op jit(solution)/shard_map/ppermute | solution.py:386
  16.6 1.7 %collective-permute-start.1 = (s32[2,40]{1,0:T(2,128)S(1)}, s32[2,40]{1,0:T(2,128)S(1)}, u32[]{:S(2)}, u32[]{:S(2)}) collective-permute-start(s32[2,40]{1,0:T(2,128)S(1)} %slot_blocks.1.refs_6_.refs_0_.refs_1_), channel_id=1, source_target_pairs={{0,4},{1,0},{2,6},{3,2},{4,5},{5,1},{6,7},{7,3},{8,12},{9,8},{10,1... | collective-permute-start | bytes 968 | tf_op jit(solution)/shard_map/ppermute | solution.py:386
  18.3 6.7 %collective-permute-start.7 = (bf16[5,8,128,128]{3,2,1,0:T(8,128)(2,1)S(1)}, bf16[5,8,128,128]{3,2,1,0:T(8,128)(2,1)S(1)}, u32[]{:S(2)}, u32[]{:S(2)}) collective-permute-start(bf16[5,8,128,128]{3,2,1,0:T(8,128)(2,1)S(1)} %collective-permute-done.refs_1_.refs_3_), channel_id=1, source_target_pairs={{0,4},{2,6},{5,1},{7,3},{8,12},{10,14},{13,9},{15,11},{16,20},{18,... | collective-permute-start | bytes 3932168 | tf_op jit(solution)/shard_map/ppermute | solution.py:386
  21.5 3.6 %collective-permute-start.6 = (s32[2,40]{1,0:T(2,128)S(1)}, s32[2,40]{1,0:T(2,128)S(1)}, u32[]{:S(2)}, u32[]{:S(2)}) collective-permute-start(s32[2,40]{1,0:T(2,128)S(1)} %collective-permute-done.1.refs_0_), channel_id=1, source_target_pairs={{0,4},{2,6},{5,1},{7,3},{8,12},{10,14},{13,9},{15,11},{16,20},{18,... | collective-permute-start | bytes 968 | tf_op jit(solution)/shard_map/ppermute | solution.py:386
  24.3 4.6 %copy-start.1 = (bf16[1024,256]{1,0:T(8,128)(2,1)S(1)}, bf16[1024,256]{1,0:T(8,128)(2,1)}, u32[]{:S(2)}) copy-start(bf16[1024,256]{1,0:T(8,128)(2,1)} %x_ref.1) | copy-start | bytes 1572868
  26.5 16.6 %copy-start.2 = (bf16[256,256]{1,0:T(8,128)(2,1)S(1)}, bf16[256,256]{1,0:T(8,128)(2,1)}, u32[]{:S(2)}) copy-start(bf16[256,256]{1,0:T(8,128)(2,1)} %w_ref.3) | copy-start | bytes 393220
  26.5 14.1 %collective-permute-start.9 = (bf16[1024,128]{1,0:T(8,128)(2,1)S(1)}, bf16[1024,128]{1,0:T(8,128)(2,1)S(1)}, u32[]{:S(2)}, u32[]{:S(2)}) collective-permute-start(bf16[1024,128]{1,0:T(8,128)(2,1)S(1)} %tile_product.5), channel_id=1, source_target_pairs={{0,2},{1,3},{2,0},{3,1},{4,6},{5,7},{6,4},{7,5},{8,10},{9,11},{10,... | collective-permute-start | bytes 786440 | tf_op jit(solution)/shard_map/ppermute | solution.py:386
  29.0 12.9 %collective-permute-start.11 = (bf16[1024,128]{1,0:T(8,128)(2,1)S(1)}, bf16[1024,128]{1,0:T(8,128)(2,1)S(1)}, u32[]{:S(2)}, u32[]{:S(2)}) collective-permute-start(bf16[1024,128]{1,0:T(8,128)(2,1)S(1)} %get-tuple-element.29), channel_id=1, source_target_pairs={{0,4},{1,5},{2,6},{3,7},{4,0},{5,1},{6,2},{7,3},{8,12},{9,13},{10,... | collective-permute-start | bytes 786440 | tf_op jit(solution)/shard_map/ppermute | solution.py:386
  40.7 2.4 %collective-permute-start.10 = (bf16[1024,128]{1,0:T(8,128)(2,1)S(1)}, bf16[1024,128]{1,0:T(8,128)(2,1)S(1)}, u32[]{:S(2)}, u32[]{:S(2)}) collective-permute-start(bf16[1024,128]{1,0:T(8,128)(2,1)S(1)} %add_convert_fusion.near_ref), channel_id=1, source_target_pairs={{0,4},{1,5},{2,6},{3,7},{4,0},{5,1},{6,2},{7,3},{8,12},{9,13},{10,... | collective-permute-start | bytes 786440 | tf_op jit(solution)/shard_map/ppermute | solution.py:386
  43.5 7.6 %collective-permute-start.12 = (bf16[1024,128]{1,0:T(8,128)(2,1)S(1)}, bf16[1024,128]{1,0:T(8,128)(2,1)S(1)}, u32[]{:S(2)}, u32[]{:S(2)}) collective-permute-start(bf16[1024,128]{1,0:T(8,128)(2,1)S(1)} %get-tuple-element.35.adj_ref.refs_6_), channel_id=1, source_target_pairs={{0,17},{1,0},{2,19},{3,2},{4,21},{5,4},{6,23},{7,6},{8,9},{9,24},{... | collective-permute-start | bytes 786440 | tf_op jit(solution)/shard_map/ppermute | solution.py:386
  45.2 7.2 %collective-permute-start.13 = (bf16[1024,128]{1,0:T(8,128)(2,1)S(1)}, bf16[1024,128]{1,0:T(8,128)(2,1)S(1)}, u32[]{:S(2)}, u32[]{:S(2)}) collective-permute-start(bf16[1024,128]{1,0:T(8,128)(2,1)S(1)} %get-tuple-element.35.adj_ref.refs_6_), channel_id=1, source_target_pairs={{0,8},{1,9},{2,10},{3,11},{4,12},{5,13},{6,14},{7,15},{8,0},{9,1},... | collective-permute-start | bytes 786440 | tf_op jit(solution)/shard_map/ppermute | solution.py:386
  52.4 9.1 %collective-permute-start.15 = (bf16[1024,128]{1,0:T(8,128)(2,1)S(1)}, bf16[1024,128]{1,0:T(8,128)(2,1)S(1)}, u32[]{:S(2)}, u32[]{:S(2)}) collective-permute-start(bf16[1024,128]{1,0:T(8,128)(2,1)S(1)} %collective-permute-done.13.after_ref.refs_7_), channel_id=1, source_target_pairs={{0,16},{1,17},{2,18},{3,19},{4,20},{5,21},{6,22},{7,23},{8,24},{9,... | collective-permute-start | bytes 786440 | tf_op jit(solution)/shard_map/ppermute | solution.py:386
  53.0 8.6 %collective-permute-start.14 = (bf16[1024,128]{1,0:T(8,128)(2,1)S(1)}, bf16[1024,128]{1,0:T(8,128)(2,1)S(1)}, u32[]{:S(2)}, u32[]{:S(2)}) collective-permute-start(bf16[1024,128]{1,0:T(8,128)(2,1)S(1)} %get-tuple-element.35.adj_ref.refs_6_), channel_id=1, source_target_pairs={{0,1},{2,3},{4,5},{6,7},{9,8},{11,10},{13,12},{15,14},{16,17},{18,... | collective-permute-start | bytes 786440 | tf_op jit(solution)/shard_map/ppermute | solution.py:386
  56.2 6.0 %collective-permute-start.16 = (bf16[1024,128]{1,0:T(8,128)(2,1)S(1)}, bf16[1024,128]{1,0:T(8,128)(2,1)S(1)}, u32[]{:S(2)}, u32[]{:S(2)}) collective-permute-start(bf16[1024,128]{1,0:T(8,128)(2,1)S(1)} %collective-permute-done.12.refs_6_), channel_id=1, source_target_pairs={{0,8},{1,9},{2,10},{3,11},{4,12},{5,13},{6,14},{7,15},{8,0},{9,1},... | collective-permute-start | bytes 786440 | tf_op jit(solution)/shard_map/ppermute | solution.py:386
  56.3 5.3 %collective-permute-start.17 = (bf16[256,128]{1,0:T(8,128)(2,1)S(1)}, bf16[256,128]{1,0:T(8,128)(2,1)S(1)}, u32[]{:S(2)}, u32[]{:S(2)}) collective-permute-start(bf16[256,128]{1,0:T(8,128)(2,1)S(1)} %grad_block.1.refs_0_), channel_id=1, source_target_pairs={{0,1},{1,0},{2,3},{3,2},{4,5},{5,4},{6,7},{7,6},{8,9},{9,8},{10,11... | collective-permute-start | bytes 196616 | tf_op jit(solution)/shard_map/ppermute | solution.py:386
  63.6 14.3 %collective-permute-start.22 = (bf16[1024,128]{1,0:T(8,128)(2,1)S(1)}, bf16[1024,128]{1,0:T(8,128)(2,1)S(1)}, u32[]{:S(2)}, u32[]{:S(2)}) collective-permute-start(bf16[1024,128]{1,0:T(8,128)(2,1)S(1)} %tile_product.7.refs_2_.refs_0_), channel_id=1, source_target_pairs={{0,2},{1,3},{2,0},{3,1},{4,6},{5,7},{6,4},{7,5},{8,10},{9,11},{10,... | collective-permute-start | bytes 786440 | tf_op jit(solution)/shard_map/ppermute | solution.py:386
  67.0 3.2 %collective-permute-start.20 = (bf16[256,128]{1,0:T(8,128)(2,1)S(1)}, bf16[256,128]{1,0:T(8,128)(2,1)S(1)}, u32[]{:S(2)}, u32[]{:S(2)}) collective-permute-start(bf16[256,128]{1,0:T(8,128)(2,1)S(1)} %add_after.4.refs_0_), channel_id=1, source_target_pairs={{0,8},{1,9},{2,10},{3,11},{4,12},{5,13},{6,14},{7,15},{8,0},{9,1},... | collective-permute-start | bytes 196616 | tf_op jit(solution)/shard_map/ppermute | solution.py:386
  70.2 7.6 %collective-permute-start.21 = (bf16[256,128]{1,0:T(8,128)(2,1)S(1)}, bf16[256,128]{1,0:T(8,128)(2,1)S(1)}, u32[]{:S(2)}, u32[]{:S(2)}) collective-permute-start(bf16[256,128]{1,0:T(8,128)(2,1)S(1)} %add_after.5.refs_0_), channel_id=1, source_target_pairs={{0,16},{1,17},{2,18},{3,19},{4,20},{5,21},{6,22},{7,23},{8,24},{9,... | collective-permute-start | bytes 196616 | tf_op jit(solution)/shard_map/ppermute | solution.py:386
  70.6 11.7 %collective-permute-start.18 = (bf16[1024,128]{1,0:T(8,128)(2,1)S(1)}, bf16[1024,128]{1,0:T(8,128)(2,1)S(1)}, u32[]{:S(2)}, u32[]{:S(2)}) collective-permute-start(bf16[1024,128]{1,0:T(8,128)(2,1)S(1)} %get-tuple-element.37.own_ref), channel_id=1, source_target_pairs={{0,1},{1,5},{2,3},{3,7},{4,0},{5,4},{6,2},{7,6},{8,9},{9,13},{10,1... | collective-permute-start | bytes 786440 | tf_op jit(solution)/shard_map/ppermute | solution.py:386
  74.6 10.4 %collective-permute-start.19 = (bf16[1024,128]{1,0:T(8,128)(2,1)S(1)}, bf16[1024,128]{1,0:T(8,128)(2,1)S(1)}, u32[]{:S(2)}, u32[]{:S(2)}) collective-permute-start(bf16[1024,128]{1,0:T(8,128)(2,1)S(1)} %get-tuple-element.37.own_ref), channel_id=1, source_target_pairs={{1,4},{3,6},{4,1},{6,3},{9,12},{11,14},{12,9},{14,11},{17,20},{19,... | collective-permute-start | bytes 786440 | tf_op jit(solution)/shard_map/ppermute | solution.py:386
  78.0 8.3 %collective-permute-start.24 = (bf16[1024,128]{1,0:T(8,128)(2,1)S(1)}, bf16[1024,128]{1,0:T(8,128)(2,1)S(1)}, u32[]{:S(2)}, u32[]{:S(2)}) collective-permute-start(bf16[1024,128]{1,0:T(8,128)(2,1)S(1)} %add_after.6.refs_2_.own_ref), channel_id=1, source_target_pairs={{0,1},{1,5},{2,3},{3,7},{4,0},{5,4},{6,2},{7,6},{8,9},{9,13},{10,1... | collective-permute-start | bytes 786440 | tf_op jit(solution)/shard_map/ppermute | solution.py:386
  80.1 8.4 %collective-permute-start.25 = (bf16[1024,128]{1,0:T(8,128)(2,1)S(1)}, bf16[1024,128]{1,0:T(8,128)(2,1)S(1)}, u32[]{:S(2)}, u32[]{:S(2)}) collective-permute-start(bf16[1024,128]{1,0:T(8,128)(2,1)S(1)} %add_after.6.refs_2_.own_ref), channel_id=1, source_target_pairs={{1,4},{3,6},{4,1},{6,3},{9,12},{11,14},{12,9},{14,11},{17,20},{19,... | collective-permute-start | bytes 786440 | tf_op jit(solution)/shard_map/ppermute | solution.py:386
  82.3 2.8 %collective-permute-start.23 = (f32[256,128]{1,0:T(8,128)S(1)}, f32[256,128]{1,0:T(8,128)S(1)}, u32[]{:S(2)}, u32[]{:S(2)}) collective-permute-start(f32[256,128]{1,0:T(8,128)S(1)} %add_after.7.grad_ref), channel_id=1, source_target_pairs={{0,4},{1,5},{2,6},{3,7},{4,0},{5,1},{6,2},{7,3},{8,12},{9,13},{10,... | collective-permute-start | bytes 393224 | tf_op jit(solution)/shard_map/ppermute | solution.py:386

commit v13 on v12

--- a/solution.py
+++ b/solution.py
@@ -194,7 +194,7 @@
     panels = [panel for _, choice in named for _, panel in choice]
     metas = [meta for choice in sets for _, (meta, _) in choice]
     tiles = [values for choice in sets for _, (_, values) in choice]
-    rows, width = panels[0].shape
+    rows, width = panels[0].shape if before is None else before.shape
     _, slots, tile, _ = tiles[0].shape
     smem = pl.BlockSpec(memory_space=pltpu.SMEM)
     vmem = pl.BlockSpec(memory_space=pltpu.VMEM)
@@ -226,7 +226,7 @@
     )(*metas, *tiles, *panels, *([before] if summed else []), *after)
 
 
-def middle_kernel(near_ref, far_ref, w_ref, cot_ref, cot_swap_ref, act_ref, adj_ref):
+def middle_kernel(near_ref, far_ref, w_ref, cot_ref, cot_swap_ref, act_ref, *adj_refs):
     j, _, p = place()
     half = near_ref.shape[1]
     near = pl.multiple_of(j * half, half)
@@ -240,18 +240,24 @@
     act_ref[...] = (agg * sig).astype(act_ref.dtype)
     slope = sig * (1.0 + agg * (1.0 - sig))
     cot = jnp.where(j == p, cot_ref[...], cot_swap_ref[...])
-    adj_ref[...] = (cot.astype(jnp.float32) * slope).astype(adj_ref.dtype)
+    adj = (cot.astype(jnp.float32) * slope).astype(act_ref.dtype)
+    rows = adj.shape[0]
+    for ref in adj_refs:
+        ref[:rows, :] = adj
+        if ref.shape[0] > rows:
+            ref[rows:, :] = jnp.zeros((ref.shape[0] - rows, ref.shape[1]), ref.dtype)
 
 
 def middle(near, far, weight, cot, cot_swap):
     vmem = pl.BlockSpec(memory_space=pltpu.VMEM)
     rows, width = near.shape
     out = jax.ShapeDtypeStruct((rows, width), jnp.bfloat16)
+    longer = tuple(jax.ShapeDtypeStruct((rows + n, width), jnp.bfloat16) for n in (32, 16))
     return pl.pallas_call(
         middle_kernel,
-        out_shape=(out, out),
+        out_shape=(out, out) + longer,
         in_specs=[vmem] * 5,
-        out_specs=(vmem, vmem),
+        out_specs=(vmem,) * 4,
         compiler_params=pltpu.CompilerParams(vmem_limit_bytes=8 * 1024 * 1024),
         cost_estimate=pl.CostEstimate(
             flops=4 * rows * width * width,
@@ -468,14 +474,16 @@
     near = join(part)
     far_half = send(near, sibling)
     cot, cot_yours = halves(cotangent)
-    act, adj = middle(near, far_half, weight, cot, send(cot_yours, sibling))
-
-    direct = send(adj, to_direct)
+    act, adj, adj_longer, adj_long = middle(
+        near, far_half, weight, cot, send(cot_yours, sibling)
+    )
+
+    direct = send(adj_longer, to_direct)
     near_one = send(
-        adj, lambda c, j, z: (c if (c + z) % 2 or not four else c ^ 2, j, z ^ 1)
+        adj_long, lambda c, j, z: (c if (c + z) % 2 or not four else c ^ 2, j, z ^ 1)
     )
     adj_later, near_one, direct = lax.optimization_barrier((adj, near_one, direct))
-    second = send(direct if four else adj_later, to_second)
+    second = send(direct if four else adj_longer, to_second)
     grad = grad_block(scale, near, far_half, adj, direct)
     adj_later, grad = lax.optimization_barrier((adj_later, grad))
     far = send(near_one, to_far)
@@ -488,7 +496,7 @@
     grad_got = send(grad, lambda c, j, z: (c, j, z ^ 1))
     panels = [("self", [(None, adj)]), ("direct", [(None, direct)])]
     back_part = tile_product(panels, [set_first, set_rest], jnp.float32)
-    panels = [("near", near_choice), ("second", [(None, second)]), ("far", [(None, far)])]
+    panels = [("second", [(None, second)]), ("far", [(None, far)]), ("near", near_choice)]
     back_part = tile_product(
         panels, [set_first, set_rest], jnp.bfloat16, back_part, [grad_got]
     )
@@ -509,7 +517,7 @@
             grad = add_after([grad, got], jnp.bfloat16)
     back = add_after([back_part, send(back_part, across)], jnp.bfloat16, got)
     back_parts = [back, *deliver(back)]
-    grad = add_after([grad, got], jnp.float32, back)
+    grad = add_after([grad, got], jnp.float32, back, *act_parts[1:])
     activated, weight_grad = gather_halves(act_parts, grad, send(grad, sibling))
     input_grad = final(back_parts, weight)
     return (activated, input_grad, weight_grad)

time: 91 us -> 88.6 us (0.974); the launches traced: 89.7 us -> 88.3 us
  starting transfers between devices: 41.8 us -> 40.7 us
    ppermute x26, starting transfers between devices: 41.8 us -> 40.7 us  [send(): return lax.ppermute(value, AXES, route(shape, move))]
  transfers between devices with their start and end apart: 26 -> 26, of which waited for: 16 -> 12; matrix products, arithmetic and copies ran while one was open for 2% -> 2% of each run, Pallas kernels for 6% -> 6%
where the time goes in v13:
time: 88.6 us; the launch traced here: 88.3 us
  starting transfers between devices  40.7 us (46%)
  waiting for transfers between devices  34.3 us (39%)
  Pallas kernels  9.96 us (11%)
  local copies, waits for them, and re-layouts  2.43 us (3%)
    ppermute x26, starting transfers between devices, send(): return lax.ppermute(value, AXES, route(shape, move))  40.7 us
    ppermute x26, waiting for transfers between devices, send(): return lax.ppermute(value, AXES, route(shape, move))  34.3 us
    pallas_call x4, Pallas kernels, tile_product(): pl.pallas_call(functools.partial(tile_kernel, kinds, cases, [[case for ca...  5.32 us
  transfers between devices with their start and end apart: 26, of which 12 were waited for; matrix products, arithmetic and copies ran while one was open for 2% of the time, Pallas kernels for 6%

profile of v13, /device:TPU:1, one launch (start us, length us, event | category | flops | bytes accessed | tf_op | source)
XLA Modules:
  0.0 88.3 jit_solution(11056788327540997070)
XLA Ops:
  0.6 2.2 %collective-permute-start = (bf16[5,8,128,128]{3,2,1,0:T(8,128)(2,1)}, bf16[5,8,128,128]{3,2,1,0:T(8,128)(2,1)S(1)}, u32[]{:S(2)}, u32[]{:S(2)}) collective-permute-start(bf16[5,8,128,128]{3,2,1,0:T(8,128)(2,1)} %bitcast.5), channel_id=1, source_target_pairs={{0,4},{1,0},{2,6},{3,2},{4,5},{5,1},{6,7},{7,3},{8,12},{9,8},{10,1... | collective-permute-start | bytes 3932168 | tf_op jit(solution)/shard_map/ppermute | solution.py:392
  2.8 1.1 %constant_dynamic-slice_fusion = (bf16[1024,128]{1,0:T(8,128)(2,1)S(1)}, bf16[1024,128]{1,0:T(8,128)(2,1)S(1)}) fusion(bf16[1024,256]{1,0:T(8,128)(2,1)} %param.6, s32[]{:T(128)S(6)} %select_n.15, s32[]{:T(128)S(6)} %select_n.14), kind=kLoop, calls=%fused_computation.2 | loop fusion | bytes 1048584 | tf_op jit(solution)/shard_map/dynamic_slice | solution.py:432
  3.9 0.7 collective-permute-start.2
  4.6 1.3 %collective-permute-start.3 = (bf16[1024,128]{1,0:T(8,128)(2,1)S(1)}, bf16[1024,128]{1,0:T(8,128)(2,1)S(1)}, u32[]{:S(2)}, u32[]{:S(2)}) collective-permute-start(bf16[1024,128]{1,0:T(8,128)(2,1)S(1)} %get-tuple-element.45), channel_id=1, source_target_pairs={{0,12},{1,21},{2,14},{3,23},{5,9},{7,11},{8,4},{10,6},{12,24},{13,... | collective-permute-start | bytes 786440 | tf_op jit(solution)/shard_map/ppermute | solution.py:392
  5.9 4.8 %collective-permute-start.4 = (bf16[1024,128]{1,0:T(8,128)(2,1)S(1)}, bf16[1024,128]{1,0:T(8,128)(2,1)S(1)}, u32[]{:S(2)}, u32[]{:S(2)}) collective-permute-start(bf16[1024,128]{1,0:T(8,128)(2,1)S(1)} %get-tuple-element.45), channel_id=1, source_target_pairs={{0,4},{1,5},{2,6},{3,7},{4,0},{5,1},{6,2},{7,3},{8,12},{9,13},{10,... | collective-permute-start | bytes 786440 | tf_op jit(solution)/shard_map/ppermute | solution.py:392
  10.6 0.7 copy.12
  11.3 0.7 copy-done.3
  12.0 1.3 %slot_blocks.1.refs_6_.refs_0_.refs_1_ = s32[2,40]{1,0:T(2,128)S(1)} custom-call(s32[2,5,8]{2,1,0:T(8,128)S(1)} %copy.10.coords_ref, s32[5]{0:T(128)S(1)} %bitcast.9), custom_call_target="tpu_custom_call" | custom-call | tf_op jit(solution)/shard_map/slot_blocks/pallas_call | solution.py:133
  13.4 0.1 collective-permute-done.3.refs_1_.refs_4_.refs_7_.refs_9_
  13.6 1.8 %collective-permute-start.5 = (bf16[1024,128]{1,0:T(8,128)(2,1)S(1)}, bf16[1024,128]{1,0:T(8,128)(2,1)S(1)}, u32[]{:S(2)}, u32[]{:S(2)}) collective-permute-start(bf16[1024,128]{1,0:T(8,128)(2,1)S(1)} %get-tuple-element.25), channel_id=1, source_target_pairs={{0,16},{1,17},{2,18},{3,19},{4,20},{5,21},{6,22},{7,23},{8,24},{9,... | collective-permute-start | bytes 786440 | tf_op jit(solution)/shard_map/ppermute | solution.py:392
  15.4 1.2 %collective-permute-start.8 = (bf16[1024,128]{1,0:T(8,128)(2,1)S(1)}, bf16[1024,128]{1,0:T(8,128)(2,1)S(1)}, u32[]{:S(2)}, u32[]{:S(2)}) collective-permute-start(bf16[1024,128]{1,0:T(8,128)(2,1)S(1)} %get-tuple-element.29), channel_id=1, source_target_pairs={{0,8},{1,9},{2,10},{3,11},{4,12},{5,13},{6,14},{7,15},{8,0},{9,1},... | collective-permute-start | bytes 786440 | tf_op jit(solution)/shard_map/ppermute | solution.py:392
  16.6 0.2 collective-permute-start.1
  16.8 1.5 %collective-permute-done.1.refs_0_ = s32[2,40]{1,0:T(2,128)S(1)} collective-permute-done((s32[2,40]{1,0:T(2,128)S(1)}, s32[2,40]{1,0:T(2,128)S(1)}, u32[]{:S(2)}, u32[]{:S(2)}) %collective-permute-start.1) | collective-permute-done | bytes 352 | tf_op jit(solution)/shard_map/ppermute | solution.py:392
  18.3 1.3 %collective-permute-start.7 = (bf16[5,8,128,128]{3,2,1,0:T(8,128)(2,1)S(1)}, bf16[5,8,128,128]{3,2,1,0:T(8,128)(2,1)S(1)}, u32[]{:S(2)}, u32[]{:S(2)}) collective-permute-start(bf16[5,8,128,128]{3,2,1,0:T(8,128)(2,1)S(1)} %collective-permute-done.refs_1_.refs_3_), channel_id=1, source_target_pairs={{0,4},{2,6},{5,1},{7,3},{8,12},{10,14},{13,9},{15,11},{16,20},{18,... | collective-permute-start | bytes 3932168 | tf_op jit(solution)/shard_map/ppermute | solution.py:392
  19.6 1.9 %collective-permute-done.5.refs_8_.refs_10_ = bf16[1024,128]{1,0:T(8,128)(2,1)S(1)} collective-permute-done((bf16[1024,128]{1,0:T(8,128)(2,1)S(1)}, bf16[1024,128]{1,0:T(8,128)(2,1)S(1)}, u32[]{:S(2)}, u32[]{:S(2)}) %collective-permute-start.5) | collective-permute-done | bytes 262176 | tf_op jit(solution)/shard_map/ppermute | solution.py:392
  21.5 1.3 %collective-permute-start.6 = (s32[2,40]{1,0:T(2,128)S(1)}, s32[2,40]{1,0:T(2,128)S(1)}, u32[]{:S(2)}, u32[]{:S(2)}) collective-permute-start(s32[2,40]{1,0:T(2,128)S(1)} %collective-permute-done.1.refs_0_), channel_id=1, source_target_pairs={{0,4},{2,6},{5,1},{7,3},{8,12},{10,14},{13,9},{15,11},{16,20},{18,... | collective-permute-start | bytes 968 | tf_op jit(solution)/shard_map/ppermute | solution.py:392
  22.8 0.3 collective-permute-done.8.refs_9_.refs_11_
  23.0 1.2 %tile_product.4.refs_12_ = f32[1024,128]{1,0:T(8,128)S(1)} custom-call(s32[2,40]{1,0:T(2,128)S(1)} %collective-permute-done.1.refs_0_, bf16[5,8,128,128]{3,2,1,0:T(8,128)(2,1)S(1)} %collective-permute-done.refs_1_.refs_3_, bf16[1024,128]{1,0:T(8,128)(2,1)S(1)} %get-tuple-element.46.refs_3_.refs_2_.refs_5_.refs_4_.refs_7_, ...), custom_call_target="tpu_custom_call" | custom-call | flops 12582912000 | bytes 196608000 | tf_op jit(solution)/shard_map/tile_product/pallas_call | solution.py:204
  24.3 0.8 collective-permute-done.6.refs_1_.refs_2_
  25.0 1.4 %tile_product.5 = bf16[1024,128]{1,0:T(8,128)(2,1)S(1)} custom-call(s32[2,40]{1,0:T(2,128)S(1)} %slot_blocks.1.refs_6_.refs_0_.refs_1_, s32[2,40]{1,0:T(2,128)S(1)} %collective-permute-done.6.refs_1_.refs_2_, bf16[5,8,128,128]{3,2,1,0:T(8,128)(2,1)S(1)} %bitcast.6, bf16[5,8,128,128]{3,2,1,0:T(8,128)(2,1)S(1)} %collective-permute-done.7.refs_3_.refs_5_, ...), custom_call_target="tpu_custom_call" | custom-call | flops 167772160 | bytes 2621440 | tf_op jit(solution)/shard_map/tile_product/pallas_call | solution.py:204
  26.5 2.4 %collective-permute-start.9 = (bf16[1024,128]{1,0:T(8,128)(2,1)S(1)}, bf16[1024,128]{1,0:T(8,128)(2,1)S(1)}, u32[]{:S(2)}, u32[]{:S(2)}) collective-permute-start(bf16[1024,128]{1,0:T(8,128)(2,1)S(1)} %tile_product.5), channel_id=1, source_target_pairs={{0,2},{1,3},{2,0},{3,1},{4,6},{5,7},{6,4},{7,5},{8,10},{9,11},{10,... | collective-permute-start | bytes 786440 | tf_op jit(solution)/shard_map/ppermute | solution.py:392
  28.9 0.1 halves.1
  29.0 0.8 collective-permute-start.11
  29.7 10.9 %collective-permute-done.9 = bf16[1024,128]{1,0:T(8,128)(2,1)S(1)} collective-permute-done((bf16[1024,128]{1,0:T(8,128)(2,1)S(1)}, bf16[1024,128]{1,0:T(8,128)(2,1)S(1)}, u32[]{:S(2)}, u32[]{:S(2)}) %collective-permute-start.9) | collective-permute-done | bytes 262176 | tf_op jit(solution)/shard_map/ppermute | solution.py:392
  40.7 1.2 %collective-permute-start.10 = (bf16[1024,128]{1,0:T(8,128)(2,1)S(1)}, bf16[1024,128]{1,0:T(8,128)(2,1)S(1)}, u32[]{:S(2)}, u32[]{:S(2)}) collective-permute-start(bf16[1024,128]{1,0:T(8,128)(2,1)S(1)} %add_convert_fusion.near_ref), channel_id=1, source_target_pairs={{0,4},{1,5},{2,6},{3,7},{4,0},{5,1},{6,2},{7,3},{8,12},{9,13},{10,... | collective-permute-start | bytes 786440 | tf_op jit(solution)/shard_map/ppermute | solution.py:392
  41.9 1.2 %collective-permute-done.10.far_ref = bf16[1024,128]{1,0:T(8,128)(2,1)S(1)} collective-permute-done((bf16[1024,128]{1,0:T(8,128)(2,1)S(1)}, bf16[1024,128]{1,0:T(8,128)(2,1)S(1)}, u32[]{:S(2)}, u32[]{:S(2)}) %collective-permute-start.10) | collective-permute-done | bytes 262176 | tf_op jit(solution)/shard_map/ppermute | solution.py:392
  43.1 0.4 middle.1
  43.5 1.8 %collective-permute-start.13 = (bf16[1056,128]{1,0:T(8,128)(2,1)S(1)}, bf16[1056,128]{1,0:T(8,128)(2,1)S(1)}, u32[]{:S(2)}, u32[]{:S(2)}) collective-permute-start(bf16[1056,128]{1,0:T(8,128)(2,1)S(1)} %get-tuple-element.35), channel_id=1, source_target_pairs={{0,8},{1,9},{2,10},{3,11},{4,12},{5,13},{6,14},{7,15},{8,0},{9,1},... | collective-permute-start | bytes 811016 | tf_op jit(solution)/shard_map/ppermute | solution.py:392
  45.3 7.3 %collective-permute-done.12.refs_8_ = bf16[1040,128]{1,0:T(8,128)(2,1)S(1)} collective-permute-done((bf16[1040,128]{1,0:T(8,128)(2,1)S(1)}, bf16[1040,128]{1,0:T(8,128)(2,1)S(1)}, u32[]{:S(2)}, u32[]{:S(2)}) %collective-permute-start.12) | collective-permute-done | bytes 266272 | tf_op jit(solution)/shard_map/ppermute | solution.py:392
  52.6 0.3 collective-permute-start.14
  52.9 1.9 %collective-permute-start.15 = (bf16[1040,128]{1,0:T(8,128)(2,1)S(1)}, bf16[1040,128]{1,0:T(8,128)(2,1)S(1)}, u32[]{:S(2)}, u32[]{:S(2)}) collective-permute-start(bf16[1040,128]{1,0:T(8,128)(2,1)S(1)} %collective-permute-done.12.refs_8_), channel_id=1, source_target_pairs={{0,8},{1,9},{2,10},{3,11},{4,12},{5,13},{6,14},{7,15},{8,0},{9,1},... | collective-permute-start | bytes 798728 | tf_op jit(solution)/shard_map/ppermute | solution.py:392
  54.8 0.3 grad_block.1.refs_0_
  55.1 1.4 %collective-permute-start.16 = (bf16[1024,128]{1,0:T(8,128)(2,1)S(1)}, bf16[1024,128]{1,0:T(8,128)(2,1)S(1)}, u32[]{:S(2)}, u32[]{:S(2)}) collective-permute-start(bf16[1024,128]{1,0:T(8,128)(2,1)S(1)} %get-tuple-element.39.adj_ref.refs_6_), channel_id=1, source_target_pairs={{0,1},{2,3},{4,5},{6,7},{9,8},{11,10},{13,12},{15,14},{16,17},{18,... | collective-permute-start | bytes 786440 | tf_op jit(solution)/shard_map/ppermute | solution.py:392
  56.6 1.2 %tile_product.6.refs_10_ = f32[1024,128]{1,0:T(8,128)S(1)} custom-call(s32[2,40]{1,0:T(2,128)S(1)} %collective-permute-done.1.refs_0_, s32[2,40]{1,0:T(2,128)S(1)} %slot_blocks.1.refs_6_.refs_0_.refs_1_, s32[2,40]{1,0:T(2,128)S(1)} %collective-permute-done.6.refs_1_.refs_2_, bf16[5,8,128,128]{3,2,1,0:T(8,128)(2,1)S(1)} %collective-permute-done.refs_1_.refs_3_, ...), custom_call_target="tpu_custom_call" | custom-call | flops 134217728 | bytes 1572864 | tf_op jit(solution)/shard_map/tile_product/pallas_call | solution.py:204
  57.8 3.6 %collective-permute-done.17.refs_11_.refs_1_ = bf16[256,128]{1,0:T(8,128)(2,1)S(1)} collective-permute-done((bf16[256,128]{1,0:T(8,128)(2,1)S(1)}, bf16[256,128]{1,0:T(8,128)(2,1)S(1)}, u32[]{:S(2)}, u32[]{:S(2)}) %collective-permute-start.17) | collective-permute-done | bytes 65568 | tf_op jit(solution)/shard_map/ppermute | solution.py:392
  61.4 1.5 %tile_product.7.refs_2_.refs_0_ = bf16[1024,128]{1,0:T(8,128)(2,1)S(1)} custom-call(s32[2,40]{1,0:T(2,128)S(1)} %collective-permute-done.1.refs_0_, s32[2,40]{1,0:T(2,128)S(1)} %slot_blocks.1.refs_6_.refs_0_.refs_1_, s32[2,40]{1,0:T(2,128)S(1)} %collective-permute-done.6.refs_1_.refs_2_, bf16[5,8,128,128]{3,2,1,0:T(8,128)(2,1)S(1)} %collective-permute-done.refs_1_.refs_3_, ...), custom_call_target="tpu_custom_call" | custom-call | flops 201326592 | bytes 2359296 | tf_op jit(solution)/shard_map/tile_product/pallas_call | solution.py:204
  63.0 3.2 %collective-permute-start.22 = (bf16[1024,128]{1,0:T(8,128)(2,1)S(1)}, bf16[1024,128]{1,0:T(8,128)(2,1)S(1)}, u32[]{:S(2)}, u32[]{:S(2)}) collective-permute-start(bf16[1024,128]{1,0:T(8,128)(2,1)S(1)} %tile_product.7.refs_2_.refs_0_), channel_id=1, source_target_pairs={{0,2},{1,3},{2,0},{3,1},{4,6},{5,7},{6,4},{7,5},{8,10},{9,11},{10,... | collective-permute-start | bytes 786440 | tf_op jit(solution)/shard_map/ppermute | solution.py:392
  66.2 2.1 %collective-permute-start.20 = (bf16[256,128]{1,0:T(8,128)(2,1)S(1)}, bf16[256,128]{1,0:T(8,128)(2,1)S(1)}, u32[]{:S(2)}, u32[]{:S(2)}) collective-permute-start(bf16[256,128]{1,0:T(8,128)(2,1)S(1)} %add_after.4.refs_0_), channel_id=1, source_target_pairs={{0,8},{1,9},{2,10},{3,11},{4,12},{5,13},{6,14},{7,15},{8,0},{9,1},... | collective-permute-start | bytes 196616 | tf_op jit(solution)/shard_map/ppermute | solution.py:392
  68.3 2.9 %collective-permute-start.18 = (bf16[1024,128]{1,0:T(8,128)(2,1)S(1)}, bf16[1024,128]{1,0:T(8,128)(2,1)S(1)}, u32[]{:S(2)}, u32[]{:S(2)}) collective-permute-start(bf16[1024,128]{1,0:T(8,128)(2,1)S(1)} %get-tuple-element.41.own_ref), channel_id=1, source_target_pairs={{0,1},{1,5},{2,3},{3,7},{4,0},{5,4},{6,2},{7,6},{8,9},{9,13},{10,1... | collective-permute-start | bytes 786440 | tf_op jit(solution)/shard_map/ppermute | solution.py:392
  71.2 2.4 %collective-permute-start.19 = (bf16[1024,128]{1,0:T(8,128)(2,1)S(1)}, bf16[1024,128]{1,0:T(8,128)(2,1)S(1)}, u32[]{:S(2)}, u32[]{:S(2)}) collective-permute-start(bf16[1024,128]{1,0:T(8,128)(2,1)S(1)} %get-tuple-element.41.own_ref), channel_id=1, source_target_pairs={{1,4},{3,6},{4,1},{6,3},{9,12},{11,14},{12,9},{14,11},{17,20},{19,... | collective-permute-start | bytes 786440 | tf_op jit(solution)/shard_map/ppermute | solution.py:392
  73.6 0.4 collective-permute-start.21
  74.0 3.2 %collective-permute-done.21.refs_2_.refs_1_ = bf16[256,128]{1,0:T(8,128)(2,1)S(1)} collective-permute-done((bf16[256,128]{1,0:T(8,128)(2,1)S(1)}, bf16[256,128]{1,0:T(8,128)(2,1)S(1)}, u32[]{:S(2)}, u32[]{:S(2)}) %collective-permute-start.21) | collective-permute-done | bytes 65568 | tf_op jit(solution)/shard_map/ppermute | solution.py:392
  77.3 1.9 %collective-permute-start.24 = (bf16[1024,128]{1,0:T(8,128)(2,1)S(1)}, bf16[1024,128]{1,0:T(8,128)(2,1)S(1)}, u32[]{:S(2)}, u32[]{:S(2)}) collective-permute-start(bf16[1024,128]{1,0:T(8,128)(2,1)S(1)} %add_after.6.refs_2_.own_ref), channel_id=1, source_target_pairs={{0,1},{1,5},{2,3},{3,7},{4,0},{5,4},{6,2},{7,6},{8,9},{9,13},{10,1... | collective-permute-start | bytes 786440 | tf_op jit(solution)/shard_map/ppermute | solution.py:392
  79.2 3.1 %collective-permute-start.25 = (bf16[1024,128]{1,0:T(8,128)(2,1)S(1)}, bf16[1024,128]{1,0:T(8,128)(2,1)S(1)}, u32[]{:S(2)}, u32[]{:S(2)}) collective-permute-start(bf16[1024,128]{1,0:T(8,128)(2,1)S(1)} %add_after.6.refs_2_.own_ref), channel_id=1, source_target_pairs={{1,4},{3,6},{4,1},{6,3},{9,12},{11,14},{12,9},{14,11},{17,20},{19,... | collective-permute-start | bytes 786440 | tf_op jit(solution)/shard_map/ppermute | solution.py:392
  82.4 1.3 %collective-permute-done.23.rest_ref = f32[256,128]{1,0:T(8,128)S(1)} collective-permute-done((f32[256,128]{1,0:T(8,128)S(1)}, f32[256,128]{1,0:T(8,128)S(1)}, u32[]{:S(2)}, u32[]{:S(2)}) %collective-permute-start.23) | collective-permute-done | bytes 131104 | tf_op jit(solution)/shard_map/ppermute | solution.py:392
  83.7 1.0 %gather_halves.1 = (bf16[1024,256]{1,0:T(8,128)(2,1)}, f32[256,256]{1,0:T(8,128)}) custom-call(bf16[1024,128]{1,0:T(8,128)(2,1)S(1)} %get-tuple-element.41.own_ref, bf16[1024,128]{1,0:T(8,128)(2,1)S(1)} %collective-permute-done.18.refs_3_.one_ref, bf16[1024,128]{1,0:T(8,128)(2,1)S(1)} %collective-permute-done.19.refs_4_.two_ref, ...), custom_call_target="tpu_custom_call" | custom-call | tf_op jit(solution)/shard_map/gather_halves/pallas_call | solution.py:344
  84.8 2.3 %collective-permute-done.25.two_ref = bf16[1024,128]{1,0:T(8,128)(2,1)S(1)} collective-permute-done((bf16[1024,128]{1,0:T(8,128)(2,1)S(1)}, bf16[1024,128]{1,0:T(8,128)(2,1)S(1)}, u32[]{:S(2)}, u32[]{:S(2)}) %collective-permute-start.25) | collective-permute-done | bytes 262176 | tf_op jit(solution)/shard_map/ppermute | solution.py:392
  87.0 1.2 %final.1 = bf16[1024,256]{1,0:T(8,128)(2,1)} custom-call(bf16[1024,128]{1,0:T(8,128)(2,1)S(1)} %add_after.6.refs_2_.own_ref, bf16[1024,128]{1,0:T(8,128)(2,1)S(1)} %collective-permute-done.24.one_ref, bf16[1024,128]{1,0:T(8,128)(2,1)S(1)} %collective-permute-done.25.two_ref, bf16[256,256]{1,0:T(8,128)(2,1)S(1)} %copy-done.2), custom_call_target="tpu_custom_call" | custom-call | flops 134217728 | bytes 2097152 | tf_op jit(solution)/shard_map/final/pallas_call | solution.py:370
  (31 shorter events, 0.5 us)
Async XLA Ops:
  0.6 17.7 %collective-permute-start = (bf16[5,8,128,128]{3,2,1,0:T(8,128)(2,1)}, bf16[5,8,128,128]{3,2,1,0:T(8,128)(2,1)S(1)}, u32[]{:S(2)}, u32[]{:S(2)}) collective-permute-start(bf16[5,8,128,128]{3,2,1,0:T(8,128)(2,1)} %bitcast.5), channel_id=1, source_target_pairs={{0,4},{1,0},{2,6},{3,2},{4,5},{5,1},{6,7},{7,3},{8,12},{9,8},{10,1... | collective-permute-start | bytes 3932168 | tf_op jit(solution)/shard_map/ppermute | solution.py:392
  3.9 9.5 %collective-permute-start.2 = (bf16[1024,128]{1,0:T(8,128)(2,1)S(1)}, bf16[1024,128]{1,0:T(8,128)(2,1)S(1)}, u32[]{:S(2)}, u32[]{:S(2)}) collective-permute-start(bf16[1024,128]{1,0:T(8,128)(2,1)S(1)} %get-tuple-element.46.refs_3_.refs_2_.refs_5_.refs_4_.refs_7_), channel_id=1, source_target_pairs={{0,8},{1,17},{2,10},{3,19},{5,13},{7,15},{8,0},{10,2},{12,28},{13,... | collective-permute-start | bytes 786440 | tf_op jit(solution)/shard_map/ppermute | solution.py:392
  4.6 8.9 %collective-permute-start.3 = (bf16[1024,128]{1,0:T(8,128)(2,1)S(1)}, bf16[1024,128]{1,0:T(8,128)(2,1)S(1)}, u32[]{:S(2)}, u32[]{:S(2)}) collective-permute-start(bf16[1024,128]{1,0:T(8,128)(2,1)S(1)} %get-tuple-element.45), channel_id=1, source_target_pairs={{0,12},{1,21},{2,14},{3,23},{5,9},{7,11},{8,4},{10,6},{12,24},{13,... | collective-permute-start | bytes 786440 | tf_op jit(solution)/shard_map/ppermute | solution.py:392
  5.9 7.6 %collective-permute-start.4 = (bf16[1024,128]{1,0:T(8,128)(2,1)S(1)}, bf16[1024,128]{1,0:T(8,128)(2,1)S(1)}, u32[]{:S(2)}, u32[]{:S(2)}) collective-permute-start(bf16[1024,128]{1,0:T(8,128)(2,1)S(1)} %get-tuple-element.45), channel_id=1, source_target_pairs={{0,4},{1,5},{2,6},{3,7},{4,0},{5,1},{6,2},{7,3},{8,12},{9,13},{10,... | collective-permute-start | bytes 786440 | tf_op jit(solution)/shard_map/ppermute | solution.py:392
  11.3 0.7 copy-start.3
  13.6 7.9 %collective-permute-start.5 = (bf16[1024,128]{1,0:T(8,128)(2,1)S(1)}, bf16[1024,128]{1,0:T(8,128)(2,1)S(1)}, u32[]{:S(2)}, u32[]{:S(2)}) collective-permute-start(bf16[1024,128]{1,0:T(8,128)(2,1)S(1)} %get-tuple-element.25), channel_id=1, source_target_pairs={{0,16},{1,17},{2,18},{3,19},{4,20},{5,21},{6,22},{7,23},{8,24},{9,... | collective-permute-start | bytes 786440 | tf_op jit(solution)/shard_map/ppermute | solution.py:392
  15.4 9.7 %copy-start = (bf16[1,5,8,128,128]{4,3,2,1,0:T(8,128)(2,1)S(1)}, bf16[1,5,8,128,128]{4,3,2,1,0:T(8,128)(2,1)}, u32[]{:S(2)}) copy-start(bf16[1,5,8,128,128]{4,3,2,1,0:T(8,128)(2,1)} %param.9) | copy-start | bytes 3932164
  15.4 7.6 %collective-permute-start.8 = (bf16[1024,128]{1,0:T(8,128)(2,1)S(1)}, bf16[1024,128]{1,0:T(8,128)(2,1)S(1)}, u32[]{:S(2)}, u32[]{:S(2)}) collective-permute-start(bf16[1024,128]{1,0:T(8,128)(2,1)S(1)} %get-tuple-element.29), channel_id=1, source_target_pairs={{0,8},{1,9},{2,10},{3,11},{4,12},{5,13},{6,14},{7,15},{8,0},{9,1},... | collective-permute-start | bytes 786440 | tf_op jit(solution)/shard_map/ppermute | solution.py:392
  16.6 1.7 %collective-permute-start.1 = (s32[2,40]{1,0:T(2,128)S(1)}, s32[2,40]{1,0:T(2,128)S(1)}, u32[]{:S(2)}, u32[]{:S(2)}) collective-permute-start(s32[2,40]{1,0:T(2,128)S(1)} %slot_blocks.1.refs_6_.refs_0_.refs_1_), channel_id=1, source_target_pairs={{0,4},{1,0},{2,6},{3,2},{4,5},{5,1},{6,7},{7,3},{8,12},{9,8},{10,1... | collective-permute-start | bytes 968 | tf_op jit(solution)/shard_map/ppermute | solution.py:392
  18.3 6.7 %collective-permute-start.7 = (bf16[5,8,128,128]{3,2,1,0:T(8,128)(2,1)S(1)}, bf16[5,8,128,128]{3,2,1,0:T(8,128)(2,1)S(1)}, u32[]{:S(2)}, u32[]{:S(2)}) collective-permute-start(bf16[5,8,128,128]{3,2,1,0:T(8,128)(2,1)S(1)} %collective-permute-done.refs_1_.refs_3_), channel_id=1, source_target_pairs={{0,4},{2,6},{5,1},{7,3},{8,12},{10,14},{13,9},{15,11},{16,20},{18,... | collective-permute-start | bytes 3932168 | tf_op jit(solution)/shard_map/ppermute | solution.py:392
  21.5 3.6 %collective-permute-start.6 = (s32[2,40]{1,0:T(2,128)S(1)}, s32[2,40]{1,0:T(2,128)S(1)}, u32[]{:S(2)}, u32[]{:S(2)}) collective-permute-start(s32[2,40]{1,0:T(2,128)S(1)} %collective-permute-done.1.refs_0_), channel_id=1, source_target_pairs={{0,4},{2,6},{5,1},{7,3},{8,12},{10,14},{13,9},{15,11},{16,20},{18,... | collective-permute-start | bytes 968 | tf_op jit(solution)/shard_map/ppermute | solution.py:392
  24.3 4.6 %copy-start.1 = (bf16[1024,256]{1,0:T(8,128)(2,1)S(1)}, bf16[1024,256]{1,0:T(8,128)(2,1)}, u32[]{:S(2)}) copy-start(bf16[1024,256]{1,0:T(8,128)(2,1)} %x_ref.1) | copy-start | bytes 1572868
  26.5 16.6 %copy-start.2 = (bf16[256,256]{1,0:T(8,128)(2,1)S(1)}, bf16[256,256]{1,0:T(8,128)(2,1)}, u32[]{:S(2)}) copy-start(bf16[256,256]{1,0:T(8,128)(2,1)} %w_ref.3) | copy-start | bytes 393220
  26.5 14.1 %collective-permute-start.9 = (bf16[1024,128]{1,0:T(8,128)(2,1)S(1)}, bf16[1024,128]{1,0:T(8,128)(2,1)S(1)}, u32[]{:S(2)}, u32[]{:S(2)}) collective-permute-start(bf16[1024,128]{1,0:T(8,128)(2,1)S(1)} %tile_product.5), channel_id=1, source_target_pairs={{0,2},{1,3},{2,0},{3,1},{4,6},{5,7},{6,4},{7,5},{8,10},{9,11},{10,... | collective-permute-start | bytes 786440 | tf_op jit(solution)/shard_map/ppermute | solution.py:392
  29.0 12.9 %collective-permute-start.11 = (bf16[1024,128]{1,0:T(8,128)(2,1)S(1)}, bf16[1024,128]{1,0:T(8,128)(2,1)S(1)}, u32[]{:S(2)}, u32[]{:S(2)}) collective-permute-start(bf16[1024,128]{1,0:T(8,128)(2,1)S(1)} %get-tuple-element.31), channel_id=1, source_target_pairs={{0,4},{1,5},{2,6},{3,7},{4,0},{5,1},{6,2},{7,3},{8,12},{9,13},{10,... | collective-permute-start | bytes 786440 | tf_op jit(solution)/shard_map/ppermute | solution.py:392
  40.7 2.4 %collective-permute-start.10 = (bf16[1024,128]{1,0:T(8,128)(2,1)S(1)}, bf16[1024,128]{1,0:T(8,128)(2,1)S(1)}, u32[]{:S(2)}, u32[]{:S(2)}) collective-permute-start(bf16[1024,128]{1,0:T(8,128)(2,1)S(1)} %add_convert_fusion.near_ref), channel_id=1, source_target_pairs={{0,4},{1,5},{2,6},{3,7},{4,0},{5,1},{6,2},{7,3},{8,12},{9,13},{10,... | collective-permute-start | bytes 786440 | tf_op jit(solution)/shard_map/ppermute | solution.py:392
  43.5 9.1 %collective-permute-start.13 = (bf16[1056,128]{1,0:T(8,128)(2,1)S(1)}, bf16[1056,128]{1,0:T(8,128)(2,1)S(1)}, u32[]{:S(2)}, u32[]{:S(2)}) collective-permute-start(bf16[1056,128]{1,0:T(8,128)(2,1)S(1)} %get-tuple-element.35), channel_id=1, source_target_pairs={{0,8},{1,9},{2,10},{3,11},{4,12},{5,13},{6,14},{7,15},{8,0},{9,1},... | collective-permute-start | bytes 811016 | tf_op jit(solution)/shard_map/ppermute | solution.py:392
  45.3 7.3 %collective-permute-start.12 = (bf16[1040,128]{1,0:T(8,128)(2,1)S(1)}, bf16[1040,128]{1,0:T(8,128)(2,1)S(1)}, u32[]{:S(2)}, u32[]{:S(2)}) collective-permute-start(bf16[1040,128]{1,0:T(8,128)(2,1)S(1)} %get-tuple-element.34), channel_id=1, source_target_pairs={{0,17},{1,0},{2,19},{3,2},{4,21},{5,4},{6,23},{7,6},{8,9},{9,24},{... | collective-permute-start | bytes 798728 | tf_op jit(solution)/shard_map/ppermute | solution.py:392
  52.6 8.9 %collective-permute-start.14 = (bf16[1056,128]{1,0:T(8,128)(2,1)S(1)}, bf16[1056,128]{1,0:T(8,128)(2,1)S(1)}, u32[]{:S(2)}, u32[]{:S(2)}) collective-permute-start(bf16[1056,128]{1,0:T(8,128)(2,1)S(1)} %collective-permute-done.13.after_ref.refs_7_), channel_id=1, source_target_pairs={{0,16},{1,17},{2,18},{3,19},{4,20},{5,21},{6,22},{7,23},{8,24},{9,... | collective-permute-start | bytes 811016 | tf_op jit(solution)/shard_map/ppermute | solution.py:392
  52.9 8.6 %collective-permute-start.15 = (bf16[1040,128]{1,0:T(8,128)(2,1)S(1)}, bf16[1040,128]{1,0:T(8,128)(2,1)S(1)}, u32[]{:S(2)}, u32[]{:S(2)}) collective-permute-start(bf16[1040,128]{1,0:T(8,128)(2,1)S(1)} %collective-permute-done.12.refs_8_), channel_id=1, source_target_pairs={{0,8},{1,9},{2,10},{3,11},{4,12},{5,13},{6,14},{7,15},{8,0},{9,1},... | collective-permute-start | bytes 798728 | tf_op jit(solution)/shard_map/ppermute | solution.py:392
  55.1 6.3 %collective-permute-start.16 = (bf16[1024,128]{1,0:T(8,128)(2,1)S(1)}, bf16[1024,128]{1,0:T(8,128)(2,1)S(1)}, u32[]{:S(2)}, u32[]{:S(2)}) collective-permute-start(bf16[1024,128]{1,0:T(8,128)(2,1)S(1)} %get-tuple-element.39.adj_ref.refs_6_), channel_id=1, source_target_pairs={{0,1},{2,3},{4,5},{6,7},{9,8},{11,10},{13,12},{15,14},{16,17},{18,... | collective-permute-start | bytes 786440 | tf_op jit(solution)/shard_map/ppermute | solution.py:392
  56.6 4.9 %collective-permute-start.17 = (bf16[256,128]{1,0:T(8,128)(2,1)S(1)}, bf16[256,128]{1,0:T(8,128)(2,1)S(1)}, u32[]{:S(2)}, u32[]{:S(2)}) collective-permute-start(bf16[256,128]{1,0:T(8,128)(2,1)S(1)} %grad_block.1.refs_0_), channel_id=1, source_target_pairs={{0,1},{1,0},{2,3},{3,2},{4,5},{5,4},{6,7},{7,6},{8,9},{9,8},{10,11... | collective-permute-start | bytes 196616 | tf_op jit(solution)/shard_map/ppermute | solution.py:392
  63.0 14.3 %collective-permute-start.22 = (bf16[1024,128]{1,0:T(8,128)(2,1)S(1)}, bf16[1024,128]{1,0:T(8,128)(2,1)S(1)}, u32[]{:S(2)}, u32[]{:S(2)}) collective-permute-start(bf16[1024,128]{1,0:T(8,128)(2,1)S(1)} %tile_product.7.refs_2_.refs_0_), channel_id=1, source_target_pairs={{0,2},{1,3},{2,0},{3,1},{4,6},{5,7},{6,4},{7,5},{8,10},{9,11},{10,... | collective-permute-start | bytes 786440 | tf_op jit(solution)/shard_map/ppermute | solution.py:392
  66.2 7.4 %collective-permute-start.20 = (bf16[256,128]{1,0:T(8,128)(2,1)S(1)}, bf16[256,128]{1,0:T(8,128)(2,1)S(1)}, u32[]{:S(2)}, u32[]{:S(2)}) collective-permute-start(bf16[256,128]{1,0:T(8,128)(2,1)S(1)} %add_after.4.refs_0_), channel_id=1, source_target_pairs={{0,8},{1,9},{2,10},{3,11},{4,12},{5,13},{6,14},{7,15},{8,0},{9,1},... | collective-permute-start | bytes 196616 | tf_op jit(solution)/shard_map/ppermute | solution.py:392
  68.3 14.0 %collective-permute-start.18 = (bf16[1024,128]{1,0:T(8,128)(2,1)S(1)}, bf16[1024,128]{1,0:T(8,128)(2,1)S(1)}, u32[]{:S(2)}, u32[]{:S(2)}) collective-permute-start(bf16[1024,128]{1,0:T(8,128)(2,1)S(1)} %get-tuple-element.41.own_ref), channel_id=1, source_target_pairs={{0,1},{1,5},{2,3},{3,7},{4,0},{5,4},{6,2},{7,6},{8,9},{9,13},{10,1... | collective-permute-start | bytes 786440 | tf_op jit(solution)/shard_map/ppermute | solution.py:392
  71.2 11.1 %collective-permute-start.19 = (bf16[1024,128]{1,0:T(8,128)(2,1)S(1)}, bf16[1024,128]{1,0:T(8,128)(2,1)S(1)}, u32[]{:S(2)}, u32[]{:S(2)}) collective-permute-start(bf16[1024,128]{1,0:T(8,128)(2,1)S(1)} %get-tuple-element.41.own_ref), channel_id=1, source_target_pairs={{1,4},{3,6},{4,1},{6,3},{9,12},{11,14},{12,9},{14,11},{17,20},{19,... | collective-permute-start | bytes 786440 | tf_op jit(solution)/shard_map/ppermute | solution.py:392
  73.6 3.6 %collective-permute-start.21 = (bf16[256,128]{1,0:T(8,128)(2,1)S(1)}, bf16[256,128]{1,0:T(8,128)(2,1)S(1)}, u32[]{:S(2)}, u32[]{:S(2)}) collective-permute-start(bf16[256,128]{1,0:T(8,128)(2,1)S(1)} %add_after.5.refs_0_), channel_id=1, source_target_pairs={{0,16},{1,17},{2,18},{3,19},{4,20},{5,21},{6,22},{7,23},{8,24},{9,... | collective-permute-start | bytes 196616 | tf_op jit(solution)/shard_map/ppermute | solution.py:392
  77.3 7.4 %collective-permute-start.24 = (bf16[1024,128]{1,0:T(8,128)(2,1)S(1)}, bf16[1024,128]{1,0:T(8,128)(2,1)S(1)}, u32[]{:S(2)}, u32[]{:S(2)}) collective-permute-start(bf16[1024,128]{1,0:T(8,128)(2,1)S(1)} %add_after.6.refs_2_.own_ref), channel_id=1, source_target_pairs={{0,1},{1,5},{2,3},{3,7},{4,0},{5,4},{6,2},{7,6},{8,9},{9,13},{10,1... | collective-permute-start | bytes 786440 | tf_op jit(solution)/shard_map/ppermute | solution.py:392
  79.2 7.8 %collective-permute-start.25 = (bf16[1024,128]{1,0:T(8,128)(2,1)S(1)}, bf16[1024,128]{1,0:T(8,128)(2,1)S(1)}, u32[]{:S(2)}, u32[]{:S(2)}) collective-permute-start(bf16[1024,128]{1,0:T(8,128)(2,1)S(1)} %add_after.6.refs_2_.own_ref), channel_id=1, source_target_pairs={{1,4},{3,6},{4,1},{6,3},{9,12},{11,14},{12,9},{14,11},{17,20},{19,... | collective-permute-start | bytes 786440 | tf_op jit(solution)/shard_map/ppermute | solution.py:392
  82.3 1.4 %collective-permute-start.23 = (f32[256,128]{1,0:T(8,128)S(1)}, f32[256,128]{1,0:T(8,128)S(1)}, u32[]{:S(2)}, u32[]{:S(2)}) collective-permute-start(f32[256,128]{1,0:T(8,128)S(1)} %add_after.7.grad_ref), channel_id=1, source_target_pairs={{0,4},{1,5},{2,6},{3,7},{4,0},{5,1},{6,2},{7,3},{8,12},{9,13},{10,... | collective-permute-start | bytes 393224 | tf_op jit(solution)/shard_map/ppermute | solution.py:392

commit v14 on v13

--- a/solution.py
+++ b/solution.py
@@ -268,7 +268,7 @@
     )(near, far, weight, cot, cot_swap)
 
 
-def grad_kernel(scale, near_ref, far_ref, adj_ref, after_ref, out_ref):
+def grad_kernel(scale, near_ref, far_ref, adj_ref, out_ref):
     j, _, _ = place()
     half = near_ref.shape[1]
     dims = (((0,), (0,)), ((), ()))
@@ -278,13 +278,13 @@
         out_ref[pl.ds(start, half), :] = (scale * block).astype(out_ref.dtype)
 
 
-def grad_block(scale, near, far, adj, after):
+def grad_block(scale, near, far, adj):
     vmem = pl.BlockSpec(memory_space=pltpu.VMEM)
     rows, width = near.shape
     return pl.pallas_call(
         functools.partial(grad_kernel, scale),
         out_shape=jax.ShapeDtypeStruct((2 * width, width), jnp.bfloat16),
-        in_specs=[vmem] * 3 + [pl.BlockSpec(memory_space=pl.ANY)],
+        in_specs=[vmem] * 3,
         out_specs=vmem,
         compiler_params=pltpu.CompilerParams(vmem_limit_bytes=8 * 1024 * 1024),
         cost_estimate=pl.CostEstimate(
@@ -293,7 +293,7 @@
             transcendentals=0,
         ),
         name="grad_block",
-    )(near, far, adj, after)
+    )(near, far, adj)
 
 
 def add_kernel(count, *refs):
@@ -482,10 +482,10 @@
     near_one = send(
         adj_long, lambda c, j, z: (c if (c + z) % 2 or not four else c ^ 2, j, z ^ 1)
     )
-    adj_later, near_one, direct = lax.optimization_barrier((adj, near_one, direct))
     second = send(direct if four else adj_longer, to_second)
-    grad = grad_block(scale, near, far_half, adj, direct)
-    adj_later, grad = lax.optimization_barrier((adj_later, grad))
+    grad = grad_block(scale, near, far_half, adj)
+    grad_got = send(grad, lambda c, j, z: (c, j, z ^ 1))
+    adj_later, grad_got = lax.optimization_barrier((adj, grad_got))
     far = send(near_one, to_far)
     near_choice = [("still", near_one)]
     if four:
@@ -493,13 +493,10 @@
             adj_later, lambda c, j, z: None if (c + z) % 2 else (c, j, z ^ 1)
         )
         near_choice.append(("relay", near_two))
-    grad_got = send(grad, lambda c, j, z: (c, j, z ^ 1))
     panels = [("self", [(None, adj)]), ("direct", [(None, direct)])]
     back_part = tile_product(panels, [set_first, set_rest], jnp.float32)
     panels = [("second", [(None, second)]), ("far", [(None, far)]), ("near", near_choice)]
-    back_part = tile_product(
-        panels, [set_first, set_rest], jnp.bfloat16, back_part, [grad_got]
-    )
+    back_part = tile_product(panels, [set_first, set_rest], jnp.bfloat16, back_part)
 
     def deliver(value):
         one = send(value, lambda c, j, z: (c, j, z ^ 1) if j == z % 2 else (c, 1 - j, z))

time: 88.6 us -> 87.6 us (0.989)
  waiting for transfers between devices: 34.3 us -> 31.9 us
  starting transfers between devices: 40.7 us -> 42.1 us
    ppermute x26, waiting for transfers between devices: 34.3 us -> 31.9 us  [send(): return lax.ppermute(value, AXES, route(shape, move))]
    ppermute x26, starting transfers between devices: 40.7 us -> 42.1 us  [send(): return lax.ppermute(value, AXES, route(shape, move))]
  transfers between devices with their start and end apart: 26 -> 26, of which waited for: 12 -> 13; matrix products, arithmetic and copies ran while one was open for 2% -> 2% of each run, Pallas kernels for 6% -> 6%
where the time goes in v14:
time: 87.6 us; the launch traced here: 87.3 us
  starting transfers between devices  42.1 us (48%)
  waiting for transfers between devices  31.9 us (36%)
  Pallas kernels  9.96 us (11%)
  local copies, waits for them, and re-layouts  2.43 us (3%)
    ppermute x26, starting transfers between devices, send(): return lax.ppermute(value, AXES, route(shape, move))  42.1 us
    ppermute x26, waiting for transfers between devices, send(): return lax.ppermute(value, AXES, route(shape, move))  31.9 us
    pallas_call x4, Pallas kernels, tile_product(): pl.pallas_call(functools.partial(tile_kernel, kinds, cases, [[case for ca...  5.32 us
  transfers between devices with their start and end apart: 26, of which 13 were waited for; matrix products, arithmetic and copies ran while one was open for 2% of the time, Pallas kernels for 6%

profile of v14, /device:TPU:1, one launch (start us, length us, event | category | flops | bytes accessed | tf_op | source)
XLA Modules:
  0.0 87.3 jit_solution(7578973696031653392)
XLA Ops:
  0.6 2.2 %collective-permute-start = (bf16[5,8,128,128]{3,2,1,0:T(8,128)(2,1)}, bf16[5,8,128,128]{3,2,1,0:T(8,128)(2,1)S(1)}, u32[]{:S(2)}, u32[]{:S(2)}) collective-permute-start(bf16[5,8,128,128]{3,2,1,0:T(8,128)(2,1)} %bitcast.5), channel_id=1, source_target_pairs={{0,4},{1,0},{2,6},{3,2},{4,5},{5,1},{6,7},{7,3},{8,12},{9,8},{10,1... | collective-permute-start | bytes 3932168 | tf_op jit(solution)/shard_map/ppermute | solution.py:392
  2.8 1.1 %constant_dynamic-slice_fusion = (bf16[1024,128]{1,0:T(8,128)(2,1)S(1)}, bf16[1024,128]{1,0:T(8,128)(2,1)S(1)}) fusion(bf16[1024,256]{1,0:T(8,128)(2,1)} %param.6, s32[]{:T(128)S(6)} %select_n.15, s32[]{:T(128)S(6)} %select_n.14), kind=kLoop, calls=%fused_computation.2 | loop fusion | bytes 1048584 | tf_op jit(solution)/shard_map/dynamic_slice | solution.py:432
  3.9 0.7 collective-permute-start.2
  4.6 1.3 %collective-permute-start.3 = (bf16[1024,128]{1,0:T(8,128)(2,1)S(1)}, bf16[1024,128]{1,0:T(8,128)(2,1)S(1)}, u32[]{:S(2)}, u32[]{:S(2)}) collective-permute-start(bf16[1024,128]{1,0:T(8,128)(2,1)S(1)} %get-tuple-element.39), channel_id=1, source_target_pairs={{0,12},{1,21},{2,14},{3,23},{5,9},{7,11},{8,4},{10,6},{12,24},{13,... | collective-permute-start | bytes 786440 | tf_op jit(solution)/shard_map/ppermute | solution.py:392
  5.9 4.8 %collective-permute-start.4 = (bf16[1024,128]{1,0:T(8,128)(2,1)S(1)}, bf16[1024,128]{1,0:T(8,128)(2,1)S(1)}, u32[]{:S(2)}, u32[]{:S(2)}) collective-permute-start(bf16[1024,128]{1,0:T(8,128)(2,1)S(1)} %get-tuple-element.39), channel_id=1, source_target_pairs={{0,4},{1,5},{2,6},{3,7},{4,0},{5,1},{6,2},{7,3},{8,12},{9,13},{10,... | collective-permute-start | bytes 786440 | tf_op jit(solution)/shard_map/ppermute | solution.py:392
  10.6 0.7 copy.12
  11.3 0.7 copy-done.3
  12.0 1.3 %slot_blocks.1.refs_6_.refs_0_.refs_1_ = s32[2,40]{1,0:T(2,128)S(1)} custom-call(s32[2,5,8]{2,1,0:T(8,128)S(1)} %copy.10.coords_ref, s32[5]{0:T(128)S(1)} %bitcast.9), custom_call_target="tpu_custom_call" | custom-call | tf_op jit(solution)/shard_map/slot_blocks/pallas_call | solution.py:133
  13.6 1.8 %collective-permute-start.5 = (bf16[1024,128]{1,0:T(8,128)(2,1)S(1)}, bf16[1024,128]{1,0:T(8,128)(2,1)S(1)}, u32[]{:S(2)}, u32[]{:S(2)}) collective-permute-start(bf16[1024,128]{1,0:T(8,128)(2,1)S(1)} %get-tuple-element.22), channel_id=1, source_target_pairs={{0,16},{1,17},{2,18},{3,19},{4,20},{5,21},{6,22},{7,23},{8,24},{9,... | collective-permute-start | bytes 786440 | tf_op jit(solution)/shard_map/ppermute | solution.py:392
  15.4 1.2 %collective-permute-start.8 = (bf16[1024,128]{1,0:T(8,128)(2,1)S(1)}, bf16[1024,128]{1,0:T(8,128)(2,1)S(1)}, u32[]{:S(2)}, u32[]{:S(2)}) collective-permute-start(bf16[1024,128]{1,0:T(8,128)(2,1)S(1)} %get-tuple-element.26), channel_id=1, source_target_pairs={{0,8},{1,9},{2,10},{3,11},{4,12},{5,13},{6,14},{7,15},{8,0},{9,1},... | collective-permute-start | bytes 786440 | tf_op jit(solution)/shard_map/ppermute | solution.py:392
  16.6 0.2 collective-permute-start.1
  16.8 1.5 %collective-permute-done.1.refs_0_ = s32[2,40]{1,0:T(2,128)S(1)} collective-permute-done((s32[2,40]{1,0:T(2,128)S(1)}, s32[2,40]{1,0:T(2,128)S(1)}, u32[]{:S(2)}, u32[]{:S(2)}) %collective-permute-start.1) | collective-permute-done | bytes 352 | tf_op jit(solution)/shard_map/ppermute | solution.py:392
  18.3 1.3 %collective-permute-start.7 = (bf16[5,8,128,128]{3,2,1,0:T(8,128)(2,1)S(1)}, bf16[5,8,128,128]{3,2,1,0:T(8,128)(2,1)S(1)}, u32[]{:S(2)}, u32[]{:S(2)}) collective-permute-start(bf16[5,8,128,128]{3,2,1,0:T(8,128)(2,1)S(1)} %collective-permute-done.refs_1_.refs_3_), channel_id=1, source_target_pairs={{0,4},{2,6},{5,1},{7,3},{8,12},{10,14},{13,9},{15,11},{16,20},{18,... | collective-permute-start | bytes 3932168 | tf_op jit(solution)/shard_map/ppermute | solution.py:392
  19.6 1.9 %collective-permute-done.5.refs_8_.refs_10_ = bf16[1024,128]{1,0:T(8,128)(2,1)S(1)} collective-permute-done((bf16[1024,128]{1,0:T(8,128)(2,1)S(1)}, bf16[1024,128]{1,0:T(8,128)(2,1)S(1)}, u32[]{:S(2)}, u32[]{:S(2)}) %collective-permute-start.5) | collective-permute-done | bytes 262176 | tf_op jit(solution)/shard_map/ppermute | solution.py:392
  21.5 1.3 %collective-permute-start.6 = (s32[2,40]{1,0:T(2,128)S(1)}, s32[2,40]{1,0:T(2,128)S(1)}, u32[]{:S(2)}, u32[]{:S(2)}) collective-permute-start(s32[2,40]{1,0:T(2,128)S(1)} %collective-permute-done.1.refs_0_), channel_id=1, source_target_pairs={{0,4},{2,6},{5,1},{7,3},{8,12},{10,14},{13,9},{15,11},{16,20},{18,... | collective-permute-start | bytes 968 | tf_op jit(solution)/shard_map/ppermute | solution.py:392
  22.8 0.3 collective-permute-done.8.refs_9_.refs_11_
  23.0 1.2 %tile_product.4.refs_12_ = f32[1024,128]{1,0:T(8,128)S(1)} custom-call(s32[2,40]{1,0:T(2,128)S(1)} %collective-permute-done.1.refs_0_, bf16[5,8,128,128]{3,2,1,0:T(8,128)(2,1)S(1)} %collective-permute-done.refs_1_.refs_3_, bf16[1024,128]{1,0:T(8,128)(2,1)S(1)} %get-tuple-element.40.refs_3_.refs_2_.refs_5_.refs_4_.refs_7_, ...), custom_call_target="tpu_custom_call" | custom-call | flops 12582912000 | bytes 196608000 | tf_op jit(solution)/shard_map/tile_product/pallas_call | solution.py:204
  24.3 0.8 collective-permute-done.6.refs_1_.refs_2_
  25.0 1.4 %tile_product.5 = bf16[1024,128]{1,0:T(8,128)(2,1)S(1)} custom-call(s32[2,40]{1,0:T(2,128)S(1)} %slot_blocks.1.refs_6_.refs_0_.refs_1_, s32[2,40]{1,0:T(2,128)S(1)} %collective-permute-done.6.refs_1_.refs_2_, bf16[5,8,128,128]{3,2,1,0:T(8,128)(2,1)S(1)} %bitcast.6, bf16[5,8,128,128]{3,2,1,0:T(8,128)(2,1)S(1)} %collective-permute-done.7.refs_3_.refs_5_, ...), custom_call_target="tpu_custom_call" | custom-call | flops 167772160 | bytes 2621440 | tf_op jit(solution)/shard_map/tile_product/pallas_call | solution.py:204
  26.5 2.4 %collective-permute-start.9 = (bf16[1024,128]{1,0:T(8,128)(2,1)S(1)}, bf16[1024,128]{1,0:T(8,128)(2,1)S(1)}, u32[]{:S(2)}, u32[]{:S(2)}) collective-permute-start(bf16[1024,128]{1,0:T(8,128)(2,1)S(1)} %tile_product.5), channel_id=1, source_target_pairs={{0,2},{1,3},{2,0},{3,1},{4,6},{5,7},{6,4},{7,5},{8,10},{9,11},{10,... | collective-permute-start | bytes 786440 | tf_op jit(solution)/shard_map/ppermute | solution.py:392
  29.0 0.8 collective-permute-start.11
  29.7 10.9 %collective-permute-done.9 = bf16[1024,128]{1,0:T(8,128)(2,1)S(1)} collective-permute-done((bf16[1024,128]{1,0:T(8,128)(2,1)S(1)}, bf16[1024,128]{1,0:T(8,128)(2,1)S(1)}, u32[]{:S(2)}, u32[]{:S(2)}) %collective-permute-start.9) | collective-permute-done | bytes 262176 | tf_op jit(solution)/shard_map/ppermute | solution.py:392
  40.7 1.2 %collective-permute-start.10 = (bf16[1024,128]{1,0:T(8,128)(2,1)S(1)}, bf16[1024,128]{1,0:T(8,128)(2,1)S(1)}, u32[]{:S(2)}, u32[]{:S(2)}) collective-permute-start(bf16[1024,128]{1,0:T(8,128)(2,1)S(1)} %add_convert_fusion.near_ref), channel_id=1, source_target_pairs={{0,4},{1,5},{2,6},{3,7},{4,0},{5,1},{6,2},{7,3},{8,12},{9,13},{10,... | collective-permute-start | bytes 786440 | tf_op jit(solution)/shard_map/ppermute | solution.py:392
  41.9 1.2 %collective-permute-done.10.far_ref = bf16[1024,128]{1,0:T(8,128)(2,1)S(1)} collective-permute-done((bf16[1024,128]{1,0:T(8,128)(2,1)S(1)}, bf16[1024,128]{1,0:T(8,128)(2,1)S(1)}, u32[]{:S(2)}, u32[]{:S(2)}) %collective-permute-start.10) | collective-permute-done | bytes 262176 | tf_op jit(solution)/shard_map/ppermute | solution.py:392
  43.1 0.4 middle.1
  43.5 1.8 %collective-permute-start.12 = (bf16[1056,128]{1,0:T(8,128)(2,1)S(1)}, bf16[1056,128]{1,0:T(8,128)(2,1)S(1)}, u32[]{:S(2)}, u32[]{:S(2)}) collective-permute-start(bf16[1056,128]{1,0:T(8,128)(2,1)S(1)} %get-tuple-element.30), channel_id=1, source_target_pairs={{0,8},{1,9},{2,10},{3,11},{4,12},{5,13},{6,14},{7,15},{8,0},{9,1},... | collective-permute-start | bytes 811016 | tf_op jit(solution)/shard_map/ppermute | solution.py:392
  45.3 0.3 grad_block.1.refs_0_
  45.7 1.5 %collective-permute-start.16 = (bf16[256,128]{1,0:T(8,128)(2,1)S(1)}, bf16[256,128]{1,0:T(8,128)(2,1)S(1)}, u32[]{:S(2)}, u32[]{:S(2)}) collective-permute-start(bf16[256,128]{1,0:T(8,128)(2,1)S(1)} %grad_block.1.refs_0_), channel_id=1, source_target_pairs={{0,1},{1,0},{2,3},{3,2},{4,5},{5,4},{6,7},{7,6},{8,9},{9,8},{10,11... | collective-permute-start | bytes 196616 | tf_op jit(solution)/shard_map/ppermute | solution.py:392
  47.2 4.7 %collective-permute-done.12.refs_7_ = bf16[1056,128]{1,0:T(8,128)(2,1)S(1)} collective-permute-done((bf16[1056,128]{1,0:T(8,128)(2,1)S(1)}, bf16[1056,128]{1,0:T(8,128)(2,1)S(1)}, u32[]{:S(2)}, u32[]{:S(2)}) %collective-permute-start.12) | collective-permute-done | bytes 270368 | tf_op jit(solution)/shard_map/ppermute | solution.py:392
  51.9 1.0 %collective-permute-start.13 = (bf16[1056,128]{1,0:T(8,128)(2,1)S(1)}, bf16[1056,128]{1,0:T(8,128)(2,1)S(1)}, u32[]{:S(2)}, u32[]{:S(2)}) collective-permute-start(bf16[1056,128]{1,0:T(8,128)(2,1)S(1)} %collective-permute-done.12.refs_7_), channel_id=1, source_target_pairs={{0,16},{1,17},{2,18},{3,19},{4,20},{5,21},{6,22},{7,23},{8,24},{9,... | collective-permute-start | bytes 811016 | tf_op jit(solution)/shard_map/ppermute | solution.py:392
  52.8 1.1 %collective-permute-start.15 = (bf16[1040,128]{1,0:T(8,128)(2,1)S(1)}, bf16[1040,128]{1,0:T(8,128)(2,1)S(1)}, u32[]{:S(2)}, u32[]{:S(2)}) collective-permute-start(bf16[1040,128]{1,0:T(8,128)(2,1)S(1)} %collective-permute-done.14.refs_8_), channel_id=1, source_target_pairs={{0,8},{1,9},{2,10},{3,11},{4,12},{5,13},{6,14},{7,15},{8,0},{9,1},... | collective-permute-start | bytes 798728 | tf_op jit(solution)/shard_map/ppermute | solution.py:392
  53.9 0.1 collective-permute-done.16.refs_1_
  54.0 2.2 %collective-permute-start.17 = (bf16[1024,128]{1,0:T(8,128)(2,1)S(1)}, bf16[1024,128]{1,0:T(8,128)(2,1)S(1)}, u32[]{:S(2)}, u32[]{:S(2)}) collective-permute-start(bf16[1024,128]{1,0:T(8,128)(2,1)S(1)} %get-tuple-element.33.adj_ref.refs_6_), channel_id=1, source_target_pairs={{0,1},{2,3},{4,5},{6,7},{9,8},{11,10},{13,12},{15,14},{16,17},{18,... | collective-permute-start | bytes 786440 | tf_op jit(solution)/shard_map/ppermute | solution.py:392
  56.2 1.2 %tile_product.6.refs_10_ = f32[1024,128]{1,0:T(8,128)S(1)} custom-call(s32[2,40]{1,0:T(2,128)S(1)} %collective-permute-done.1.refs_0_, s32[2,40]{1,0:T(2,128)S(1)} %slot_blocks.1.refs_6_.refs_0_.refs_1_, s32[2,40]{1,0:T(2,128)S(1)} %collective-permute-done.6.refs_1_.refs_2_, bf16[5,8,128,128]{3,2,1,0:T(8,128)(2,1)S(1)} %collective-permute-done.refs_1_.refs_3_, ...), custom_call_target="tpu_custom_call" | custom-call | flops 134217728 | bytes 1572864 | tf_op jit(solution)/shard_map/tile_product/pallas_call | solution.py:204
  57.4 3.2 %collective-permute-done.17.refs_9_ = bf16[1024,128]{1,0:T(8,128)(2,1)S(1)} collective-permute-done((bf16[1024,128]{1,0:T(8,128)(2,1)S(1)}, bf16[1024,128]{1,0:T(8,128)(2,1)S(1)}, u32[]{:S(2)}, u32[]{:S(2)}) %collective-permute-start.17) | collective-permute-done | bytes 262176 | tf_op jit(solution)/shard_map/ppermute | solution.py:392
  60.6 1.5 %tile_product.7.refs_2_.refs_0_ = bf16[1024,128]{1,0:T(8,128)(2,1)S(1)} custom-call(s32[2,40]{1,0:T(2,128)S(1)} %collective-permute-done.1.refs_0_, s32[2,40]{1,0:T(2,128)S(1)} %slot_blocks.1.refs_6_.refs_0_.refs_1_, s32[2,40]{1,0:T(2,128)S(1)} %collective-permute-done.6.refs_1_.refs_2_, bf16[5,8,128,128]{3,2,1,0:T(8,128)(2,1)S(1)} %collective-permute-done.refs_1_.refs_3_, ...), custom_call_target="tpu_custom_call" | custom-call | flops 201326592 | bytes 2359296 | tf_op jit(solution)/shard_map/tile_product/pallas_call | solution.py:204
  62.1 3.2 %collective-permute-start.22 = (bf16[1024,128]{1,0:T(8,128)(2,1)S(1)}, bf16[1024,128]{1,0:T(8,128)(2,1)S(1)}, u32[]{:S(2)}, u32[]{:S(2)}) collective-permute-start(bf16[1024,128]{1,0:T(8,128)(2,1)S(1)} %tile_product.7.refs_2_.refs_0_), channel_id=1, source_target_pairs={{0,2},{1,3},{2,0},{3,1},{4,6},{5,7},{6,4},{7,5},{8,10},{9,11},{10,... | collective-permute-start | bytes 786440 | tf_op jit(solution)/shard_map/ppermute | solution.py:392
  65.3 0.3 collective-permute-start.20
  65.6 3.3 %collective-permute-start.18 = (bf16[1024,128]{1,0:T(8,128)(2,1)S(1)}, bf16[1024,128]{1,0:T(8,128)(2,1)S(1)}, u32[]{:S(2)}, u32[]{:S(2)}) collective-permute-start(bf16[1024,128]{1,0:T(8,128)(2,1)S(1)} %get-tuple-element.34.own_ref), channel_id=1, source_target_pairs={{0,1},{1,5},{2,3},{3,7},{4,0},{5,4},{6,2},{7,6},{8,9},{9,13},{10,1... | collective-permute-start | bytes 786440 | tf_op jit(solution)/shard_map/ppermute | solution.py:392
  68.9 3.0 %collective-permute-start.19 = (bf16[1024,128]{1,0:T(8,128)(2,1)S(1)}, bf16[1024,128]{1,0:T(8,128)(2,1)S(1)}, u32[]{:S(2)}, u32[]{:S(2)}) collective-permute-start(bf16[1024,128]{1,0:T(8,128)(2,1)S(1)} %get-tuple-element.34.own_ref), channel_id=1, source_target_pairs={{1,4},{3,6},{4,1},{6,3},{9,12},{11,14},{12,9},{14,11},{17,20},{19,... | collective-permute-start | bytes 786440 | tf_op jit(solution)/shard_map/ppermute | solution.py:392
  71.9 0.6 collective-permute-start.21
  72.5 3.0 %collective-permute-done.21.refs_2_.refs_1_ = bf16[256,128]{1,0:T(8,128)(2,1)S(1)} collective-permute-done((bf16[256,128]{1,0:T(8,128)(2,1)S(1)}, bf16[256,128]{1,0:T(8,128)(2,1)S(1)}, u32[]{:S(2)}, u32[]{:S(2)}) %collective-permute-start.21) | collective-permute-done | bytes 65568 | tf_op jit(solution)/shard_map/ppermute | solution.py:392
  75.6 2.8 %collective-permute-start.24 = (bf16[1024,128]{1,0:T(8,128)(2,1)S(1)}, bf16[1024,128]{1,0:T(8,128)(2,1)S(1)}, u32[]{:S(2)}, u32[]{:S(2)}) collective-permute-start(bf16[1024,128]{1,0:T(8,128)(2,1)S(1)} %add_after.6.refs_2_.own_ref), channel_id=1, source_target_pairs={{0,1},{1,5},{2,3},{3,7},{4,0},{5,4},{6,2},{7,6},{8,9},{9,13},{10,1... | collective-permute-start | bytes 786440 | tf_op jit(solution)/shard_map/ppermute | solution.py:392
  78.4 2.2 %collective-permute-start.25 = (bf16[1024,128]{1,0:T(8,128)(2,1)S(1)}, bf16[1024,128]{1,0:T(8,128)(2,1)S(1)}, u32[]{:S(2)}, u32[]{:S(2)}) collective-permute-start(bf16[1024,128]{1,0:T(8,128)(2,1)S(1)} %add_after.6.refs_2_.own_ref), channel_id=1, source_target_pairs={{1,4},{3,6},{4,1},{6,3},{9,12},{11,14},{12,9},{14,11},{17,20},{19,... | collective-permute-start | bytes 786440 | tf_op jit(solution)/shard_map/ppermute | solution.py:392
  80.7 1.3 %collective-permute-done.23.rest_ref = f32[256,128]{1,0:T(8,128)S(1)} collective-permute-done((f32[256,128]{1,0:T(8,128)S(1)}, f32[256,128]{1,0:T(8,128)S(1)}, u32[]{:S(2)}, u32[]{:S(2)}) %collective-permute-start.23) | collective-permute-done | bytes 131104 | tf_op jit(solution)/shard_map/ppermute | solution.py:392
  82.1 1.0 %gather_halves.1 = (bf16[1024,256]{1,0:T(8,128)(2,1)}, f32[256,256]{1,0:T(8,128)}) custom-call(bf16[1024,128]{1,0:T(8,128)(2,1)S(1)} %get-tuple-element.34.own_ref, bf16[1024,128]{1,0:T(8,128)(2,1)S(1)} %collective-permute-done.18.refs_3_.one_ref, bf16[1024,128]{1,0:T(8,128)(2,1)S(1)} %collective-permute-done.19.refs_4_.two_ref, ...), custom_call_target="tpu_custom_call" | custom-call | tf_op jit(solution)/shard_map/gather_halves/pallas_call | solution.py:344
  83.1 3.0 %collective-permute-done.25.two_ref = bf16[1024,128]{1,0:T(8,128)(2,1)S(1)} collective-permute-done((bf16[1024,128]{1,0:T(8,128)(2,1)S(1)}, bf16[1024,128]{1,0:T(8,128)(2,1)S(1)}, u32[]{:S(2)}, u32[]{:S(2)}) %collective-permute-start.25) | collective-permute-done | bytes 262176 | tf_op jit(solution)/shard_map/ppermute | solution.py:392
  86.1 1.2 %final.1 = bf16[1024,256]{1,0:T(8,128)(2,1)} custom-call(bf16[1024,128]{1,0:T(8,128)(2,1)S(1)} %add_after.6.refs_2_.own_ref, bf16[1024,128]{1,0:T(8,128)(2,1)S(1)} %collective-permute-done.24.one_ref, bf16[1024,128]{1,0:T(8,128)(2,1)S(1)} %collective-permute-done.25.two_ref, bf16[256,256]{1,0:T(8,128)(2,1)S(1)} %copy-done.2), custom_call_target="tpu_custom_call" | custom-call | flops 134217728 | bytes 2097152 | tf_op jit(solution)/shard_map/final/pallas_call | solution.py:370
  (31 shorter events, 0.6 us)
Async XLA Ops:
  0.6 17.7 %collective-permute-start = (bf16[5,8,128,128]{3,2,1,0:T(8,128)(2,1)}, bf16[5,8,128,128]{3,2,1,0:T(8,128)(2,1)S(1)}, u32[]{:S(2)}, u32[]{:S(2)}) collective-permute-start(bf16[5,8,128,128]{3,2,1,0:T(8,128)(2,1)} %bitcast.5), channel_id=1, source_target_pairs={{0,4},{1,0},{2,6},{3,2},{4,5},{5,1},{6,7},{7,3},{8,12},{9,8},{10,1... | collective-permute-start | bytes 3932168 | tf_op jit(solution)/shard_map/ppermute | solution.py:392
  3.9 9.5 %collective-permute-start.2 = (bf16[1024,128]{1,0:T(8,128)(2,1)S(1)}, bf16[1024,128]{1,0:T(8,128)(2,1)S(1)}, u32[]{:S(2)}, u32[]{:S(2)}) collective-permute-start(bf16[1024,128]{1,0:T(8,128)(2,1)S(1)} %get-tuple-element.40.refs_3_.refs_2_.refs_5_.refs_4_.refs_7_), channel_id=1, source_target_pairs={{0,8},{1,17},{2,10},{3,19},{5,13},{7,15},{8,0},{10,2},{12,28},{13,... | collective-permute-start | bytes 786440 | tf_op jit(solution)/shard_map/ppermute | solution.py:392
  4.6 8.9 %collective-permute-start.3 = (bf16[1024,128]{1,0:T(8,128)(2,1)S(1)}, bf16[1024,128]{1,0:T(8,128)(2,1)S(1)}, u32[]{:S(2)}, u32[]{:S(2)}) collective-permute-start(bf16[1024,128]{1,0:T(8,128)(2,1)S(1)} %get-tuple-element.39), channel_id=1, source_target_pairs={{0,12},{1,21},{2,14},{3,23},{5,9},{7,11},{8,4},{10,6},{12,24},{13,... | collective-permute-start | bytes 786440 | tf_op jit(solution)/shard_map/ppermute | solution.py:392
  5.9 7.6 %collective-permute-start.4 = (bf16[1024,128]{1,0:T(8,128)(2,1)S(1)}, bf16[1024,128]{1,0:T(8,128)(2,1)S(1)}, u32[]{:S(2)}, u32[]{:S(2)}) collective-permute-start(bf16[1024,128]{1,0:T(8,128)(2,1)S(1)} %get-tuple-element.39), channel_id=1, source_target_pairs={{0,4},{1,5},{2,6},{3,7},{4,0},{5,1},{6,2},{7,3},{8,12},{9,13},{10,... | collective-permute-start | bytes 786440 | tf_op jit(solution)/shard_map/ppermute | solution.py:392
  11.3 0.7 copy-start.3
  13.6 7.9 %collective-permute-start.5 = (bf16[1024,128]{1,0:T(8,128)(2,1)S(1)}, bf16[1024,128]{1,0:T(8,128)(2,1)S(1)}, u32[]{:S(2)}, u32[]{:S(2)}) collective-permute-start(bf16[1024,128]{1,0:T(8,128)(2,1)S(1)} %get-tuple-element.22), channel_id=1, source_target_pairs={{0,16},{1,17},{2,18},{3,19},{4,20},{5,21},{6,22},{7,23},{8,24},{9,... | collective-permute-start | bytes 786440 | tf_op jit(solution)/shard_map/ppermute | solution.py:392
  15.4 9.7 %copy-start = (bf16[1,5,8,128,128]{4,3,2,1,0:T(8,128)(2,1)S(1)}, bf16[1,5,8,128,128]{4,3,2,1,0:T(8,128)(2,1)}, u32[]{:S(2)}) copy-start(bf16[1,5,8,128,128]{4,3,2,1,0:T(8,128)(2,1)} %param.9) | copy-start | bytes 3932164
  15.4 7.6 %collective-permute-start.8 = (bf16[1024,128]{1,0:T(8,128)(2,1)S(1)}, bf16[1024,128]{1,0:T(8,128)(2,1)S(1)}, u32[]{:S(2)}, u32[]{:S(2)}) collective-permute-start(bf16[1024,128]{1,0:T(8,128)(2,1)S(1)} %get-tuple-element.26), channel_id=1, source_target_pairs={{0,8},{1,9},{2,10},{3,11},{4,12},{5,13},{6,14},{7,15},{8,0},{9,1},... | collective-permute-start | bytes 786440 | tf_op jit(solution)/shard_map/ppermute | solution.py:392
  16.6 1.7 %collective-permute-start.1 = (s32[2,40]{1,0:T(2,128)S(1)}, s32[2,40]{1,0:T(2,128)S(1)}, u32[]{:S(2)}, u32[]{:S(2)}) collective-permute-start(s32[2,40]{1,0:T(2,128)S(1)} %slot_blocks.1.refs_6_.refs_0_.refs_1_), channel_id=1, source_target_pairs={{0,4},{1,0},{2,6},{3,2},{4,5},{5,1},{6,7},{7,3},{8,12},{9,8},{10,1... | collective-permute-start | bytes 968 | tf_op jit(solution)/shard_map/ppermute | solution.py:392
  18.3 6.7 %collective-permute-start.7 = (bf16[5,8,128,128]{3,2,1,0:T(8,128)(2,1)S(1)}, bf16[5,8,128,128]{3,2,1,0:T(8,128)(2,1)S(1)}, u32[]{:S(2)}, u32[]{:S(2)}) collective-permute-start(bf16[5,8,128,128]{3,2,1,0:T(8,128)(2,1)S(1)} %collective-permute-done.refs_1_.refs_3_), channel_id=1, source_target_pairs={{0,4},{2,6},{5,1},{7,3},{8,12},{10,14},{13,9},{15,11},{16,20},{18,... | collective-permute-start | bytes 3932168 | tf_op jit(solution)/shard_map/ppermute | solution.py:392
  21.5 3.6 %collective-permute-start.6 = (s32[2,40]{1,0:T(2,128)S(1)}, s32[2,40]{1,0:T(2,128)S(1)}, u32[]{:S(2)}, u32[]{:S(2)}) collective-permute-start(s32[2,40]{1,0:T(2,128)S(1)} %collective-permute-done.1.refs_0_), channel_id=1, source_target_pairs={{0,4},{2,6},{5,1},{7,3},{8,12},{10,14},{13,9},{15,11},{16,20},{18,... | collective-permute-start | bytes 968 | tf_op jit(solution)/shard_map/ppermute | solution.py:392
  24.3 4.6 %copy-start.1 = (bf16[1024,256]{1,0:T(8,128)(2,1)S(1)}, bf16[1024,256]{1,0:T(8,128)(2,1)}, u32[]{:S(2)}) copy-start(bf16[1024,256]{1,0:T(8,128)(2,1)} %x_ref.1) | copy-start | bytes 1572868
  26.5 16.6 %copy-start.2 = (bf16[256,256]{1,0:T(8,128)(2,1)S(1)}, bf16[256,256]{1,0:T(8,128)(2,1)}, u32[]{:S(2)}) copy-start(bf16[256,256]{1,0:T(8,128)(2,1)} %w_ref.3) | copy-start | bytes 393220
  26.5 14.1 %collective-permute-start.9 = (bf16[1024,128]{1,0:T(8,128)(2,1)S(1)}, bf16[1024,128]{1,0:T(8,128)(2,1)S(1)}, u32[]{:S(2)}, u32[]{:S(2)}) collective-permute-start(bf16[1024,128]{1,0:T(8,128)(2,1)S(1)} %tile_product.5), channel_id=1, source_target_pairs={{0,2},{1,3},{2,0},{3,1},{4,6},{5,7},{6,4},{7,5},{8,10},{9,11},{10,... | collective-permute-start | bytes 786440 | tf_op jit(solution)/shard_map/ppermute | solution.py:392
  29.0 12.9 %collective-permute-start.11 = (bf16[1024,128]{1,0:T(8,128)(2,1)S(1)}, bf16[1024,128]{1,0:T(8,128)(2,1)S(1)}, u32[]{:S(2)}, u32[]{:S(2)}) collective-permute-start(bf16[1024,128]{1,0:T(8,128)(2,1)S(1)} %get-tuple-element.28), channel_id=1, source_target_pairs={{0,4},{1,5},{2,6},{3,7},{4,0},{5,1},{6,2},{7,3},{8,12},{9,13},{10,... | collective-permute-start | bytes 786440 | tf_op jit(solution)/shard_map/ppermute | solution.py:392
  40.7 2.4 %collective-permute-start.10 = (bf16[1024,128]{1,0:T(8,128)(2,1)S(1)}, bf16[1024,128]{1,0:T(8,128)(2,1)S(1)}, u32[]{:S(2)}, u32[]{:S(2)}) collective-permute-start(bf16[1024,128]{1,0:T(8,128)(2,1)S(1)} %add_convert_fusion.near_ref), channel_id=1, source_target_pairs={{0,4},{1,5},{2,6},{3,7},{4,0},{5,1},{6,2},{7,3},{8,12},{9,13},{10,... | collective-permute-start | bytes 786440 | tf_op jit(solution)/shard_map/ppermute | solution.py:392
  43.5 8.4 %collective-permute-start.12 = (bf16[1056,128]{1,0:T(8,128)(2,1)S(1)}, bf16[1056,128]{1,0:T(8,128)(2,1)S(1)}, u32[]{:S(2)}, u32[]{:S(2)}) collective-permute-start(bf16[1056,128]{1,0:T(8,128)(2,1)S(1)} %get-tuple-element.30), channel_id=1, source_target_pairs={{0,8},{1,9},{2,10},{3,11},{4,12},{5,13},{6,14},{7,15},{8,0},{9,1},... | collective-permute-start | bytes 811016 | tf_op jit(solution)/shard_map/ppermute | solution.py:392
  45.3 7.5 %collective-permute-start.14 = (bf16[1040,128]{1,0:T(8,128)(2,1)S(1)}, bf16[1040,128]{1,0:T(8,128)(2,1)S(1)}, u32[]{:S(2)}, u32[]{:S(2)}) collective-permute-start(bf16[1040,128]{1,0:T(8,128)(2,1)S(1)} %get-tuple-element.31), channel_id=1, source_target_pairs={{0,17},{1,0},{2,19},{3,2},{4,21},{5,4},{6,23},{7,6},{8,9},{9,24},{... | collective-permute-start | bytes 798728 | tf_op jit(solution)/shard_map/ppermute | solution.py:392
  45.7 8.3 %collective-permute-start.16 = (bf16[256,128]{1,0:T(8,128)(2,1)S(1)}, bf16[256,128]{1,0:T(8,128)(2,1)S(1)}, u32[]{:S(2)}, u32[]{:S(2)}) collective-permute-start(bf16[256,128]{1,0:T(8,128)(2,1)S(1)} %grad_block.1.refs_0_), channel_id=1, source_target_pairs={{0,1},{1,0},{2,3},{3,2},{4,5},{5,4},{6,7},{7,6},{8,9},{9,8},{10,11... | collective-permute-start | bytes 196616 | tf_op jit(solution)/shard_map/ppermute | solution.py:392
  51.9 8.8 %collective-permute-start.13 = (bf16[1056,128]{1,0:T(8,128)(2,1)S(1)}, bf16[1056,128]{1,0:T(8,128)(2,1)S(1)}, u32[]{:S(2)}, u32[]{:S(2)}) collective-permute-start(bf16[1056,128]{1,0:T(8,128)(2,1)S(1)} %collective-permute-done.12.refs_7_), channel_id=1, source_target_pairs={{0,16},{1,17},{2,18},{3,19},{4,20},{5,21},{6,22},{7,23},{8,24},{9,... | collective-permute-start | bytes 811016 | tf_op jit(solution)/shard_map/ppermute | solution.py:392
  52.8 7.8 %collective-permute-start.15 = (bf16[1040,128]{1,0:T(8,128)(2,1)S(1)}, bf16[1040,128]{1,0:T(8,128)(2,1)S(1)}, u32[]{:S(2)}, u32[]{:S(2)}) collective-permute-start(bf16[1040,128]{1,0:T(8,128)(2,1)S(1)} %collective-permute-done.14.refs_8_), channel_id=1, source_target_pairs={{0,8},{1,9},{2,10},{3,11},{4,12},{5,13},{6,14},{7,15},{8,0},{9,1},... | collective-permute-start | bytes 798728 | tf_op jit(solution)/shard_map/ppermute | solution.py:392
  54.0 6.6 %collective-permute-start.17 = (bf16[1024,128]{1,0:T(8,128)(2,1)S(1)}, bf16[1024,128]{1,0:T(8,128)(2,1)S(1)}, u32[]{:S(2)}, u32[]{:S(2)}) collective-permute-start(bf16[1024,128]{1,0:T(8,128)(2,1)S(1)} %get-tuple-element.33.adj_ref.refs_6_), channel_id=1, source_target_pairs={{0,1},{2,3},{4,5},{6,7},{9,8},{11,10},{13,12},{15,14},{16,17},{18,... | collective-permute-start | bytes 786440 | tf_op jit(solution)/shard_map/ppermute | solution.py:392
  62.1 13.4 %collective-permute-start.22 = (bf16[1024,128]{1,0:T(8,128)(2,1)S(1)}, bf16[1024,128]{1,0:T(8,128)(2,1)S(1)}, u32[]{:S(2)}, u32[]{:S(2)}) collective-permute-start(bf16[1024,128]{1,0:T(8,128)(2,1)S(1)} %tile_product.7.refs_2_.refs_0_), channel_id=1, source_target_pairs={{0,2},{1,3},{2,0},{3,1},{4,6},{5,7},{6,4},{7,5},{8,10},{9,11},{10,... | collective-permute-start | bytes 786440 | tf_op jit(solution)/shard_map/ppermute | solution.py:392
  65.3 6.6 %collective-permute-start.20 = (bf16[256,128]{1,0:T(8,128)(2,1)S(1)}, bf16[256,128]{1,0:T(8,128)(2,1)S(1)}, u32[]{:S(2)}, u32[]{:S(2)}) collective-permute-start(bf16[256,128]{1,0:T(8,128)(2,1)S(1)} %add_after.4.refs_0_), channel_id=1, source_target_pairs={{0,8},{1,9},{2,10},{3,11},{4,12},{5,13},{6,14},{7,15},{8,0},{9,1},... | collective-permute-start | bytes 196616 | tf_op jit(solution)/shard_map/ppermute | solution.py:392
  65.6 15.0 %collective-permute-start.18 = (bf16[1024,128]{1,0:T(8,128)(2,1)S(1)}, bf16[1024,128]{1,0:T(8,128)(2,1)S(1)}, u32[]{:S(2)}, u32[]{:S(2)}) collective-permute-start(bf16[1024,128]{1,0:T(8,128)(2,1)S(1)} %get-tuple-element.34.own_ref), channel_id=1, source_target_pairs={{0,1},{1,5},{2,3},{3,7},{4,0},{5,4},{6,2},{7,6},{8,9},{9,13},{10,1... | collective-permute-start | bytes 786440 | tf_op jit(solution)/shard_map/ppermute | solution.py:392
  68.9 11.7 %collective-permute-start.19 = (bf16[1024,128]{1,0:T(8,128)(2,1)S(1)}, bf16[1024,128]{1,0:T(8,128)(2,1)S(1)}, u32[]{:S(2)}, u32[]{:S(2)}) collective-permute-start(bf16[1024,128]{1,0:T(8,128)(2,1)S(1)} %get-tuple-element.34.own_ref), channel_id=1, source_target_pairs={{1,4},{3,6},{4,1},{6,3},{9,12},{11,14},{12,9},{14,11},{17,20},{19,... | collective-permute-start | bytes 786440 | tf_op jit(solution)/shard_map/ppermute | solution.py:392
  71.9 3.6 %collective-permute-start.21 = (bf16[256,128]{1,0:T(8,128)(2,1)S(1)}, bf16[256,128]{1,0:T(8,128)(2,1)S(1)}, u32[]{:S(2)}, u32[]{:S(2)}) collective-permute-start(bf16[256,128]{1,0:T(8,128)(2,1)S(1)} %add_after.5.refs_0_), channel_id=1, source_target_pairs={{0,16},{1,17},{2,18},{3,19},{4,20},{5,21},{6,22},{7,23},{8,24},{9,... | collective-permute-start | bytes 196616 | tf_op jit(solution)/shard_map/ppermute | solution.py:392
  75.6 7.5 %collective-permute-start.24 = (bf16[1024,128]{1,0:T(8,128)(2,1)S(1)}, bf16[1024,128]{1,0:T(8,128)(2,1)S(1)}, u32[]{:S(2)}, u32[]{:S(2)}) collective-permute-start(bf16[1024,128]{1,0:T(8,128)(2,1)S(1)} %add_after.6.refs_2_.own_ref), channel_id=1, source_target_pairs={{0,1},{1,5},{2,3},{3,7},{4,0},{5,4},{6,2},{7,6},{8,9},{9,13},{10,1... | collective-permute-start | bytes 786440 | tf_op jit(solution)/shard_map/ppermute | solution.py:392
  78.4 7.7 %collective-permute-start.25 = (bf16[1024,128]{1,0:T(8,128)(2,1)S(1)}, bf16[1024,128]{1,0:T(8,128)(2,1)S(1)}, u32[]{:S(2)}, u32[]{:S(2)}) collective-permute-start(bf16[1024,128]{1,0:T(8,128)(2,1)S(1)} %add_after.6.refs_2_.own_ref), channel_id=1, source_target_pairs={{1,4},{3,6},{4,1},{6,3},{9,12},{11,14},{12,9},{14,11},{17,20},{19,... | collective-permute-start | bytes 786440 | tf_op jit(solution)/shard_map/ppermute | solution.py:392
  80.6 1.4 %collective-permute-start.23 = (f32[256,128]{1,0:T(8,128)S(1)}, f32[256,128]{1,0:T(8,128)S(1)}, u32[]{:S(2)}, u32[]{:S(2)}) collective-permute-start(f32[256,128]{1,0:T(8,128)S(1)} %add_after.7.grad_ref), channel_id=1, source_target_pairs={{0,4},{1,5},{2,6},{3,7},{4,0},{5,1},{6,2},{7,3},{8,12},{9,13},{10,... | collective-permute-start | bytes 393224 | tf_op jit(solution)/shard_map/ppermute | solution.py:392

commit v15 on v14

--- a/solution.py
+++ b/solution.py
@@ -440,10 +440,10 @@
         [
             direct_choice if four else self_choice,
             [
+                ("relay home", two),
+                ("relay away", one),
                 ("still home", swapped),
                 ("still away", mine),
-                ("relay home", two),
-                ("relay away", one),
             ],
         ],
         [meta],
@@ -451,17 +451,16 @@
     second = send(second, to_second)
     far = send(far, to_far)
     meta_b = send(meta, to_home)
-    first, meta_b = lax.optimization_barrier((first, meta_b))
+    meta_far = send(meta_b, home_to_sibling)
+    first, meta_far = lax.optimization_barrier((first, meta_far))
     other_first = send(first, home_to_sibling)
-    meta_later, second = lax.optimization_barrier((meta_b, second))
-    meta_far = send(meta_later, home_to_sibling)
     set_first = [(None, (meta_b, first))]
     panels = [
-        ("self", [("home", mine), ("away", swapped)]),
-        ("near", [("home", swapped), ("away", mine)]),
         ("direct", direct_choice),
         ("second", [(None, second)]),
         ("far", [(None, far)]),
+        ("self", [("home", mine), ("away", swapped)]),
+        ("near", [("home", swapped), ("away", mine)]),
     ]
     part = tile_product(panels, [set_first], jnp.float32, weigh=WEIGH)
     set_rest = [("home", (meta, own)), ("away", (meta_far, other_first))]

time: 87.6 us -> 88.3 us (level)
  waiting for transfers between devices: 31.9 us -> 35.2 us
  starting transfers between devices: 42.1 us -> 39.3 us
    ppermute x26, waiting for transfers between devices: 31.9 us -> 35.2 us  [send(): return lax.ppermute(value, AXES, route(shape, move))]
    ppermute x26, starting transfers between devices: 42.1 us -> 39.3 us  [send(): return lax.ppermute(value, AXES, route(shape, move))]
  transfers between devices with their start and end apart: 26 -> 26, of which waited for: 13 -> 12; matrix products, arithmetic and copies ran while one was open for 2% -> 2% of each run, Pallas kernels for 6% -> 6%
where the time goes in v15:
time: 88.3 us; the launch traced here: 88 us
  starting transfers between devices  39.3 us (45%)
  waiting for transfers between devices  35.2 us (40%)
  Pallas kernels  10 us (11%)
  local copies, waits for them, and re-layouts  2.43 us (3%)
    ppermute x26, starting transfers between devices, send(): return lax.ppermute(value, AXES, route(shape, move))  39.3 us
    ppermute x26, waiting for transfers between devices, send(): return lax.ppermute(value, AXES, route(shape, move))  35.2 us
    pallas_call x4, Pallas kernels, tile_product(): pl.pallas_call(functools.partial(tile_kernel, kinds, cases, [[case for ca...  5.4 us
  transfers between devices with their start and end apart: 26, of which 12 were waited for; matrix products, arithmetic and copies ran while one was open for 2% of the time, Pallas kernels for 6%

profile of v15, /device:TPU:1, one launch (start us, length us, event | category | flops | bytes accessed | tf_op | source)
XLA Modules:
  0.0 88.0 jit_solution(10248185956034101542)
XLA Ops:
  0.6 2.2 %collective-permute-start = (bf16[5,8,128,128]{3,2,1,0:T(8,128)(2,1)}, bf16[5,8,128,128]{3,2,1,0:T(8,128)(2,1)S(1)}, u32[]{:S(2)}, u32[]{:S(2)}) collective-permute-start(bf16[5,8,128,128]{3,2,1,0:T(8,128)(2,1)} %bitcast.5), channel_id=1, source_target_pairs={{0,4},{1,0},{2,6},{3,2},{4,5},{5,1},{6,7},{7,3},{8,12},{9,8},{10,1... | collective-permute-start | bytes 3932168 | tf_op jit(solution)/shard_map/ppermute | solution.py:392
  2.8 1.1 %constant_dynamic-slice_fusion = (bf16[1024,128]{1,0:T(8,128)(2,1)S(1)}, bf16[1024,128]{1,0:T(8,128)(2,1)S(1)}) fusion(bf16[1024,256]{1,0:T(8,128)(2,1)} %param.6, s32[]{:T(128)S(6)} %select_n.15, s32[]{:T(128)S(6)} %select_n.14), kind=kLoop, calls=%fused_computation.2 | loop fusion | bytes 1048584 | tf_op jit(solution)/shard_map/dynamic_slice | solution.py:432
  3.9 0.7 collective-permute-start.4
  4.6 1.3 %collective-permute-start.5 = (bf16[1024,128]{1,0:T(8,128)(2,1)S(1)}, bf16[1024,128]{1,0:T(8,128)(2,1)S(1)}, u32[]{:S(2)}, u32[]{:S(2)}) collective-permute-start(bf16[1024,128]{1,0:T(8,128)(2,1)S(1)} %get-tuple-element.35), channel_id=1, source_target_pairs={{0,12},{1,21},{2,14},{3,23},{5,9},{7,11},{8,4},{10,6},{12,24},{13,... | collective-permute-start | bytes 786440 | tf_op jit(solution)/shard_map/ppermute | solution.py:392
  5.9 4.8 %collective-permute-start.6 = (bf16[1024,128]{1,0:T(8,128)(2,1)S(1)}, bf16[1024,128]{1,0:T(8,128)(2,1)S(1)}, u32[]{:S(2)}, u32[]{:S(2)}) collective-permute-start(bf16[1024,128]{1,0:T(8,128)(2,1)S(1)} %get-tuple-element.35), channel_id=1, source_target_pairs={{0,4},{1,5},{2,6},{3,7},{4,0},{5,1},{6,2},{7,3},{8,12},{9,13},{10,... | collective-permute-start | bytes 786440 | tf_op jit(solution)/shard_map/ppermute | solution.py:392
  10.6 0.7 copy.12
  11.3 0.7 copy-done.3
  12.0 1.3 %slot_blocks.1.refs_6_.refs_0_.refs_1_ = s32[2,40]{1,0:T(2,128)S(1)} custom-call(s32[2,5,8]{2,1,0:T(8,128)S(1)} %copy.10.coords_ref, s32[5]{0:T(128)S(1)} %bitcast.9), custom_call_target="tpu_custom_call" | custom-call | tf_op jit(solution)/shard_map/slot_blocks/pallas_call | solution.py:133
  13.6 1.8 %collective-permute-start.7 = (bf16[1024,128]{1,0:T(8,128)(2,1)S(1)}, bf16[1024,128]{1,0:T(8,128)(2,1)S(1)}, u32[]{:S(2)}, u32[]{:S(2)}) collective-permute-start(bf16[1024,128]{1,0:T(8,128)(2,1)S(1)} %get-tuple-element.21), channel_id=1, source_target_pairs={{0,16},{1,17},{2,18},{3,19},{4,20},{5,21},{6,22},{7,23},{8,24},{9,... | collective-permute-start | bytes 786440 | tf_op jit(solution)/shard_map/ppermute | solution.py:392
  15.4 1.2 %collective-permute-start.8 = (bf16[1024,128]{1,0:T(8,128)(2,1)S(1)}, bf16[1024,128]{1,0:T(8,128)(2,1)S(1)}, u32[]{:S(2)}, u32[]{:S(2)}) collective-permute-start(bf16[1024,128]{1,0:T(8,128)(2,1)S(1)} %get-tuple-element.22), channel_id=1, source_target_pairs={{0,8},{1,9},{2,10},{3,11},{4,12},{5,13},{6,14},{7,15},{8,0},{9,1},... | collective-permute-start | bytes 786440 | tf_op jit(solution)/shard_map/ppermute | solution.py:392
  16.6 0.2 collective-permute-start.1
  16.8 1.5 %collective-permute-done.1.refs_0_ = s32[2,40]{1,0:T(2,128)S(1)} collective-permute-done((s32[2,40]{1,0:T(2,128)S(1)}, s32[2,40]{1,0:T(2,128)S(1)}, u32[]{:S(2)}, u32[]{:S(2)}) %collective-permute-start.1) | collective-permute-done | bytes 352 | tf_op jit(solution)/shard_map/ppermute | solution.py:392
  18.3 1.3 %collective-permute-start.2 = (s32[2,40]{1,0:T(2,128)S(1)}, s32[2,40]{1,0:T(2,128)S(1)}, u32[]{:S(2)}, u32[]{:S(2)}) collective-permute-start(s32[2,40]{1,0:T(2,128)S(1)} %collective-permute-done.1.refs_0_), channel_id=1, source_target_pairs={{0,4},{2,6},{5,1},{7,3},{8,12},{10,14},{13,9},{15,11},{16,20},{18,... | collective-permute-start | bytes 968 | tf_op jit(solution)/shard_map/ppermute | solution.py:392
  19.6 3.5 %collective-permute-done.2.refs_1_.refs_2_ = s32[2,40]{1,0:T(2,128)S(1)} collective-permute-done((s32[2,40]{1,0:T(2,128)S(1)}, s32[2,40]{1,0:T(2,128)S(1)}, u32[]{:S(2)}, u32[]{:S(2)}) %collective-permute-start.2) | collective-permute-done | bytes 352 | tf_op jit(solution)/shard_map/ppermute | solution.py:392
  23.1 1.3 %collective-permute-start.3 = (bf16[5,8,128,128]{3,2,1,0:T(8,128)(2,1)S(1)}, bf16[5,8,128,128]{3,2,1,0:T(8,128)(2,1)S(1)}, u32[]{:S(2)}, u32[]{:S(2)}) collective-permute-start(bf16[5,8,128,128]{3,2,1,0:T(8,128)(2,1)S(1)} %collective-permute-done.refs_1_.refs_3_), channel_id=1, source_target_pairs={{0,4},{2,6},{5,1},{7,3},{8,12},{10,14},{13,9},{15,11},{16,20},{18,... | collective-permute-start | bytes 3932168 | tf_op jit(solution)/shard_map/ppermute | solution.py:392
  24.5 1.3 %tile_product.4.refs_12_ = f32[1024,128]{1,0:T(8,128)S(1)} custom-call(s32[2,40]{1,0:T(2,128)S(1)} %collective-permute-done.1.refs_0_, bf16[5,8,128,128]{3,2,1,0:T(8,128)(2,1)S(1)} %collective-permute-done.refs_1_.refs_3_, bf16[1024,128]{1,0:T(8,128)(2,1)S(1)} %collective-permute-done.4.refs_0_.refs_3_.refs_2_.refs_4_, ...), custom_call_target="tpu_custom_call" | custom-call | flops 12582912000 | bytes 196608000 | tf_op jit(solution)/shard_map/tile_product/pallas_call | solution.py:204
  25.7 2.3 %collective-permute-done.3.refs_3_.refs_5_ = bf16[5,8,128,128]{3,2,1,0:T(8,128)(2,1)S(1)} collective-permute-done((bf16[5,8,128,128]{3,2,1,0:T(8,128)(2,1)S(1)}, bf16[5,8,128,128]{3,2,1,0:T(8,128)(2,1)S(1)}, u32[]{:S(2)}, u32[]{:S(2)}) %collective-permute-start.3) | collective-permute-done | bytes 1310752 | tf_op jit(solution)/shard_map/ppermute | solution.py:392
  28.1 1.5 %tile_product.5 = bf16[1024,128]{1,0:T(8,128)(2,1)S(1)} custom-call(s32[2,40]{1,0:T(2,128)S(1)} %slot_blocks.1.refs_6_.refs_0_.refs_1_, s32[2,40]{1,0:T(2,128)S(1)} %collective-permute-done.2.refs_1_.refs_2_, bf16[5,8,128,128]{3,2,1,0:T(8,128)(2,1)S(1)} %bitcast.6, bf16[5,8,128,128]{3,2,1,0:T(8,128)(2,1)S(1)} %collective-permute-done.3.refs_3_.refs_5_, ...), custom_call_target="tpu_custom_call" | custom-call | flops 167772160 | bytes 2621440 | tf_op jit(solution)/shard_map/tile_product/pallas_call | solution.py:204
  29.6 2.4 %collective-permute-start.9 = (bf16[1024,128]{1,0:T(8,128)(2,1)S(1)}, bf16[1024,128]{1,0:T(8,128)(2,1)S(1)}, u32[]{:S(2)}, u32[]{:S(2)}) collective-permute-start(bf16[1024,128]{1,0:T(8,128)(2,1)S(1)} %tile_product.5), channel_id=1, source_target_pairs={{0,2},{1,3},{2,0},{3,1},{4,6},{5,7},{6,4},{7,5},{8,10},{9,11},{10,... | collective-permute-start | bytes 786440 | tf_op jit(solution)/shard_map/ppermute | solution.py:392
  31.9 0.1 halves.1
  32.1 0.5 collective-permute-start.11
  32.5 11.8 %collective-permute-done.9 = bf16[1024,128]{1,0:T(8,128)(2,1)S(1)} collective-permute-done((bf16[1024,128]{1,0:T(8,128)(2,1)S(1)}, bf16[1024,128]{1,0:T(8,128)(2,1)S(1)}, u32[]{:S(2)}, u32[]{:S(2)}) %collective-permute-start.9) | collective-permute-done | bytes 262176 | tf_op jit(solution)/shard_map/ppermute | solution.py:392
  44.4 0.5 collective-permute-start.10
  44.9 1.2 %collective-permute-done.10.far_ref = bf16[1024,128]{1,0:T(8,128)(2,1)S(1)} collective-permute-done((bf16[1024,128]{1,0:T(8,128)(2,1)S(1)}, bf16[1024,128]{1,0:T(8,128)(2,1)S(1)}, u32[]{:S(2)}, u32[]{:S(2)}) %collective-permute-start.10) | collective-permute-done | bytes 262176 | tf_op jit(solution)/shard_map/ppermute | solution.py:392
  46.1 0.4 middle.1
  46.6 0.3 collective-permute-start.14
  46.9 0.3 grad_block.1.refs_0_
  47.2 1.3 %collective-permute-start.16 = (bf16[256,128]{1,0:T(8,128)(2,1)S(1)}, bf16[256,128]{1,0:T(8,128)(2,1)S(1)}, u32[]{:S(2)}, u32[]{:S(2)}) collective-permute-start(bf16[256,128]{1,0:T(8,128)(2,1)S(1)} %grad_block.1.refs_0_), channel_id=1, source_target_pairs={{0,1},{1,0},{2,3},{3,2},{4,5},{5,4},{6,7},{7,6},{8,9},{9,8},{10,11... | collective-permute-start | bytes 196616 | tf_op jit(solution)/shard_map/ppermute | solution.py:392
  48.5 5.7 %collective-permute-done.12.refs_7_ = bf16[1056,128]{1,0:T(8,128)(2,1)S(1)} collective-permute-done((bf16[1056,128]{1,0:T(8,128)(2,1)S(1)}, bf16[1056,128]{1,0:T(8,128)(2,1)S(1)}, u32[]{:S(2)}, u32[]{:S(2)}) %collective-permute-start.12) | collective-permute-done | bytes 270368 | tf_op jit(solution)/shard_map/ppermute | solution.py:392
  54.2 0.2 collective-permute-start.13
  54.5 1.7 %collective-permute-start.15 = (bf16[1040,128]{1,0:T(8,128)(2,1)S(1)}, bf16[1040,128]{1,0:T(8,128)(2,1)S(1)}, u32[]{:S(2)}, u32[]{:S(2)}) collective-permute-start(bf16[1040,128]{1,0:T(8,128)(2,1)S(1)} %collective-permute-done.14.refs_8_), channel_id=1, source_target_pairs={{0,8},{1,9},{2,10},{3,11},{4,12},{5,13},{6,14},{7,15},{8,0},{9,1},... | collective-permute-start | bytes 798728 | tf_op jit(solution)/shard_map/ppermute | solution.py:392
  56.2 1.3 %collective-permute-start.17 = (bf16[1024,128]{1,0:T(8,128)(2,1)S(1)}, bf16[1024,128]{1,0:T(8,128)(2,1)S(1)}, u32[]{:S(2)}, u32[]{:S(2)}) collective-permute-start(bf16[1024,128]{1,0:T(8,128)(2,1)S(1)} %get-tuple-element.29.adj_ref.refs_6_), channel_id=1, source_target_pairs={{0,1},{2,3},{4,5},{6,7},{9,8},{11,10},{13,12},{15,14},{16,17},{18,... | collective-permute-start | bytes 786440 | tf_op jit(solution)/shard_map/ppermute | solution.py:392
  57.5 1.2 %tile_product.6.refs_10_ = f32[1024,128]{1,0:T(8,128)S(1)} custom-call(s32[2,40]{1,0:T(2,128)S(1)} %collective-permute-done.1.refs_0_, s32[2,40]{1,0:T(2,128)S(1)} %slot_blocks.1.refs_6_.refs_0_.refs_1_, s32[2,40]{1,0:T(2,128)S(1)} %collective-permute-done.2.refs_1_.refs_2_, bf16[5,8,128,128]{3,2,1,0:T(8,128)(2,1)S(1)} %collective-permute-done.refs_1_.refs_3_, ...), custom_call_target="tpu_custom_call" | custom-call | flops 134217728 | bytes 1572864 | tf_op jit(solution)/shard_map/tile_product/pallas_call | solution.py:204
  58.7 2.1 %collective-permute-done.17.refs_9_ = bf16[1024,128]{1,0:T(8,128)(2,1)S(1)} collective-permute-done((bf16[1024,128]{1,0:T(8,128)(2,1)S(1)}, bf16[1024,128]{1,0:T(8,128)(2,1)S(1)}, u32[]{:S(2)}, u32[]{:S(2)}) %collective-permute-start.17) | collective-permute-done | bytes 262176 | tf_op jit(solution)/shard_map/ppermute | solution.py:392
  60.8 0.2 collective-permute-done.13.refs_6_
  61.0 1.5 %tile_product.7.refs_2_.refs_0_ = bf16[1024,128]{1,0:T(8,128)(2,1)S(1)} custom-call(s32[2,40]{1,0:T(2,128)S(1)} %collective-permute-done.1.refs_0_, s32[2,40]{1,0:T(2,128)S(1)} %slot_blocks.1.refs_6_.refs_0_.refs_1_, s32[2,40]{1,0:T(2,128)S(1)} %collective-permute-done.2.refs_1_.refs_2_, bf16[5,8,128,128]{3,2,1,0:T(8,128)(2,1)S(1)} %collective-permute-done.refs_1_.refs_3_, ...), custom_call_target="tpu_custom_call" | custom-call | flops 201326592 | bytes 2359296 | tf_op jit(solution)/shard_map/tile_product/pallas_call | solution.py:204
  62.5 3.4 %collective-permute-start.22 = (bf16[1024,128]{1,0:T(8,128)(2,1)S(1)}, bf16[1024,128]{1,0:T(8,128)(2,1)S(1)}, u32[]{:S(2)}, u32[]{:S(2)}) collective-permute-start(bf16[1024,128]{1,0:T(8,128)(2,1)S(1)} %tile_product.7.refs_2_.refs_0_), channel_id=1, source_target_pairs={{0,2},{1,3},{2,0},{3,1},{4,6},{5,7},{6,4},{7,5},{8,10},{9,11},{10,... | collective-permute-start | bytes 786440 | tf_op jit(solution)/shard_map/ppermute | solution.py:392
  66.0 2.3 %collective-permute-start.20 = (bf16[256,128]{1,0:T(8,128)(2,1)S(1)}, bf16[256,128]{1,0:T(8,128)(2,1)S(1)}, u32[]{:S(2)}, u32[]{:S(2)}) collective-permute-start(bf16[256,128]{1,0:T(8,128)(2,1)S(1)} %add_after.4.refs_0_), channel_id=1, source_target_pairs={{0,8},{1,9},{2,10},{3,11},{4,12},{5,13},{6,14},{7,15},{8,0},{9,1},... | collective-permute-start | bytes 196616 | tf_op jit(solution)/shard_map/ppermute | solution.py:392
  68.3 2.7 %collective-permute-start.18 = (bf16[1024,128]{1,0:T(8,128)(2,1)S(1)}, bf16[1024,128]{1,0:T(8,128)(2,1)S(1)}, u32[]{:S(2)}, u32[]{:S(2)}) collective-permute-start(bf16[1024,128]{1,0:T(8,128)(2,1)S(1)} %get-tuple-element.30.own_ref), channel_id=1, source_target_pairs={{0,1},{1,5},{2,3},{3,7},{4,0},{5,4},{6,2},{7,6},{8,9},{9,13},{10,1... | collective-permute-start | bytes 786440 | tf_op jit(solution)/shard_map/ppermute | solution.py:392
  71.0 2.1 %collective-permute-start.19 = (bf16[1024,128]{1,0:T(8,128)(2,1)S(1)}, bf16[1024,128]{1,0:T(8,128)(2,1)S(1)}, u32[]{:S(2)}, u32[]{:S(2)}) collective-permute-start(bf16[1024,128]{1,0:T(8,128)(2,1)S(1)} %get-tuple-element.30.own_ref), channel_id=1, source_target_pairs={{1,4},{3,6},{4,1},{6,3},{9,12},{11,14},{12,9},{14,11},{17,20},{19,... | collective-permute-start | bytes 786440 | tf_op jit(solution)/shard_map/ppermute | solution.py:392
  73.1 0.7 collective-permute-start.21
  73.9 2.9 %collective-permute-done.21.refs_2_.refs_1_ = bf16[256,128]{1,0:T(8,128)(2,1)S(1)} collective-permute-done((bf16[256,128]{1,0:T(8,128)(2,1)S(1)}, bf16[256,128]{1,0:T(8,128)(2,1)S(1)}, u32[]{:S(2)}, u32[]{:S(2)}) %collective-permute-start.21) | collective-permute-done | bytes 65568 | tf_op jit(solution)/shard_map/ppermute | solution.py:392
  76.8 2.2 %collective-permute-start.24 = (bf16[1024,128]{1,0:T(8,128)(2,1)S(1)}, bf16[1024,128]{1,0:T(8,128)(2,1)S(1)}, u32[]{:S(2)}, u32[]{:S(2)}) collective-permute-start(bf16[1024,128]{1,0:T(8,128)(2,1)S(1)} %add_after.6.refs_2_.own_ref), channel_id=1, source_target_pairs={{0,1},{1,5},{2,3},{3,7},{4,0},{5,4},{6,2},{7,6},{8,9},{9,13},{10,1... | collective-permute-start | bytes 786440 | tf_op jit(solution)/shard_map/ppermute | solution.py:392
  79.0 2.7 %collective-permute-start.25 = (bf16[1024,128]{1,0:T(8,128)(2,1)S(1)}, bf16[1024,128]{1,0:T(8,128)(2,1)S(1)}, u32[]{:S(2)}, u32[]{:S(2)}) collective-permute-start(bf16[1024,128]{1,0:T(8,128)(2,1)S(1)} %add_after.6.refs_2_.own_ref), channel_id=1, source_target_pairs={{1,4},{3,6},{4,1},{6,3},{9,12},{11,14},{12,9},{14,11},{17,20},{19,... | collective-permute-start | bytes 786440 | tf_op jit(solution)/shard_map/ppermute | solution.py:392
  81.9 1.3 %collective-permute-done.23.rest_ref = f32[256,128]{1,0:T(8,128)S(1)} collective-permute-done((f32[256,128]{1,0:T(8,128)S(1)}, f32[256,128]{1,0:T(8,128)S(1)}, u32[]{:S(2)}, u32[]{:S(2)}) %collective-permute-start.23) | collective-permute-done | bytes 131104 | tf_op jit(solution)/shard_map/ppermute | solution.py:392
  83.2 1.0 %gather_halves.1 = (bf16[1024,256]{1,0:T(8,128)(2,1)}, f32[256,256]{1,0:T(8,128)}) custom-call(bf16[1024,128]{1,0:T(8,128)(2,1)S(1)} %get-tuple-element.30.own_ref, bf16[1024,128]{1,0:T(8,128)(2,1)S(1)} %collective-permute-done.18.refs_3_.one_ref, bf16[1024,128]{1,0:T(8,128)(2,1)S(1)} %collective-permute-done.19.refs_4_.two_ref, ...), custom_call_target="tpu_custom_call" | custom-call | tf_op jit(solution)/shard_map/gather_halves/pallas_call | solution.py:344
  84.3 2.4 %collective-permute-done.25.two_ref = bf16[1024,128]{1,0:T(8,128)(2,1)S(1)} collective-permute-done((bf16[1024,128]{1,0:T(8,128)(2,1)S(1)}, bf16[1024,128]{1,0:T(8,128)(2,1)S(1)}, u32[]{:S(2)}, u32[]{:S(2)}) %collective-permute-start.25) | collective-permute-done | bytes 262176 | tf_op jit(solution)/shard_map/ppermute | solution.py:392
  86.7 1.2 %final.1 = bf16[1024,256]{1,0:T(8,128)(2,1)} custom-call(bf16[1024,128]{1,0:T(8,128)(2,1)S(1)} %add_after.6.refs_2_.own_ref, bf16[1024,128]{1,0:T(8,128)(2,1)S(1)} %collective-permute-done.24.one_ref, bf16[1024,128]{1,0:T(8,128)(2,1)S(1)} %collective-permute-done.25.two_ref, bf16[256,256]{1,0:T(8,128)(2,1)S(1)} %copy-done.2), custom_call_target="tpu_custom_call" | custom-call | flops 134217728 | bytes 2097152 | tf_op jit(solution)/shard_map/final/pallas_call | solution.py:370
  (31 shorter events, 0.6 us)
Async XLA Ops:
  0.6 22.5 %collective-permute-start = (bf16[5,8,128,128]{3,2,1,0:T(8,128)(2,1)}, bf16[5,8,128,128]{3,2,1,0:T(8,128)(2,1)S(1)}, u32[]{:S(2)}, u32[]{:S(2)}) collective-permute-start(bf16[5,8,128,128]{3,2,1,0:T(8,128)(2,1)} %bitcast.5), channel_id=1, source_target_pairs={{0,4},{1,0},{2,6},{3,2},{4,5},{5,1},{6,7},{7,3},{8,12},{9,8},{10,1... | collective-permute-start | bytes 3932168 | tf_op jit(solution)/shard_map/ppermute | solution.py:392
  3.9 9.5 %collective-permute-start.4 = (bf16[1024,128]{1,0:T(8,128)(2,1)S(1)}, bf16[1024,128]{1,0:T(8,128)(2,1)S(1)}, u32[]{:S(2)}, u32[]{:S(2)}) collective-permute-start(bf16[1024,128]{1,0:T(8,128)(2,1)S(1)} %get-tuple-element.36.refs_5_.refs_6_.refs_9_.refs_8_.refs_11_), channel_id=1, source_target_pairs={{0,8},{1,17},{2,10},{3,19},{5,13},{7,15},{8,0},{10,2},{12,28},{13,... | collective-permute-start | bytes 786440 | tf_op jit(solution)/shard_map/ppermute | solution.py:392
  4.6 8.9 %collective-permute-start.5 = (bf16[1024,128]{1,0:T(8,128)(2,1)S(1)}, bf16[1024,128]{1,0:T(8,128)(2,1)S(1)}, u32[]{:S(2)}, u32[]{:S(2)}) collective-permute-start(bf16[1024,128]{1,0:T(8,128)(2,1)S(1)} %get-tuple-element.35), channel_id=1, source_target_pairs={{0,12},{1,21},{2,14},{3,23},{5,9},{7,11},{8,4},{10,6},{12,24},{13,... | collective-permute-start | bytes 786440 | tf_op jit(solution)/shard_map/ppermute | solution.py:392
  5.9 7.6 %collective-permute-start.6 = (bf16[1024,128]{1,0:T(8,128)(2,1)S(1)}, bf16[1024,128]{1,0:T(8,128)(2,1)S(1)}, u32[]{:S(2)}, u32[]{:S(2)}) collective-permute-start(bf16[1024,128]{1,0:T(8,128)(2,1)S(1)} %get-tuple-element.35), channel_id=1, source_target_pairs={{0,4},{1,5},{2,6},{3,7},{4,0},{5,1},{6,2},{7,3},{8,12},{9,13},{10,... | collective-permute-start | bytes 786440 | tf_op jit(solution)/shard_map/ppermute | solution.py:392
  11.3 0.7 copy-start.3
  13.6 10.9 %collective-permute-start.7 = (bf16[1024,128]{1,0:T(8,128)(2,1)S(1)}, bf16[1024,128]{1,0:T(8,128)(2,1)S(1)}, u32[]{:S(2)}, u32[]{:S(2)}) collective-permute-start(bf16[1024,128]{1,0:T(8,128)(2,1)S(1)} %get-tuple-element.21), channel_id=1, source_target_pairs={{0,16},{1,17},{2,18},{3,19},{4,20},{5,21},{6,22},{7,23},{8,24},{9,... | collective-permute-start | bytes 786440 | tf_op jit(solution)/shard_map/ppermute | solution.py:392
  15.4 12.7 %copy-start = (bf16[1,5,8,128,128]{4,3,2,1,0:T(8,128)(2,1)S(1)}, bf16[1,5,8,128,128]{4,3,2,1,0:T(8,128)(2,1)}, u32[]{:S(2)}) copy-start(bf16[1,5,8,128,128]{4,3,2,1,0:T(8,128)(2,1)} %param.9) | copy-start | bytes 3932164
  15.4 9.1 %collective-permute-start.8 = (bf16[1024,128]{1,0:T(8,128)(2,1)S(1)}, bf16[1024,128]{1,0:T(8,128)(2,1)S(1)}, u32[]{:S(2)}, u32[]{:S(2)}) collective-permute-start(bf16[1024,128]{1,0:T(8,128)(2,1)S(1)} %get-tuple-element.22), channel_id=1, source_target_pairs={{0,8},{1,9},{2,10},{3,11},{4,12},{5,13},{6,14},{7,15},{8,0},{9,1},... | collective-permute-start | bytes 786440 | tf_op jit(solution)/shard_map/ppermute | solution.py:392
  16.6 1.7 %collective-permute-start.1 = (s32[2,40]{1,0:T(2,128)S(1)}, s32[2,40]{1,0:T(2,128)S(1)}, u32[]{:S(2)}, u32[]{:S(2)}) collective-permute-start(s32[2,40]{1,0:T(2,128)S(1)} %slot_blocks.1.refs_6_.refs_0_.refs_1_), channel_id=1, source_target_pairs={{0,4},{1,0},{2,6},{3,2},{4,5},{5,1},{6,7},{7,3},{8,12},{9,8},{10,1... | collective-permute-start | bytes 968 | tf_op jit(solution)/shard_map/ppermute | solution.py:392
  18.3 4.8 %collective-permute-start.2 = (s32[2,40]{1,0:T(2,128)S(1)}, s32[2,40]{1,0:T(2,128)S(1)}, u32[]{:S(2)}, u32[]{:S(2)}) collective-permute-start(s32[2,40]{1,0:T(2,128)S(1)} %collective-permute-done.1.refs_0_), channel_id=1, source_target_pairs={{0,4},{2,6},{5,1},{7,3},{8,12},{10,14},{13,9},{15,11},{16,20},{18,... | collective-permute-start | bytes 968 | tf_op jit(solution)/shard_map/ppermute | solution.py:392
  23.1 4.9 %collective-permute-start.3 = (bf16[5,8,128,128]{3,2,1,0:T(8,128)(2,1)S(1)}, bf16[5,8,128,128]{3,2,1,0:T(8,128)(2,1)S(1)}, u32[]{:S(2)}, u32[]{:S(2)}) collective-permute-start(bf16[5,8,128,128]{3,2,1,0:T(8,128)(2,1)S(1)} %collective-permute-done.refs_1_.refs_3_), channel_id=1, source_target_pairs={{0,4},{2,6},{5,1},{7,3},{8,12},{10,14},{13,9},{15,11},{16,20},{18,... | collective-permute-start | bytes 3932168 | tf_op jit(solution)/shard_map/ppermute | solution.py:392
  25.7 6.2 %copy-start.1 = (bf16[1024,256]{1,0:T(8,128)(2,1)S(1)}, bf16[1024,256]{1,0:T(8,128)(2,1)}, u32[]{:S(2)}) copy-start(bf16[1024,256]{1,0:T(8,128)(2,1)} %x_ref.1) | copy-start | bytes 1572868
  29.5 16.6 %copy-start.2 = (bf16[256,256]{1,0:T(8,128)(2,1)S(1)}, bf16[256,256]{1,0:T(8,128)(2,1)}, u32[]{:S(2)}) copy-start(bf16[256,256]{1,0:T(8,128)(2,1)} %w_ref.3) | copy-start | bytes 393220
  29.6 14.8 %collective-permute-start.9 = (bf16[1024,128]{1,0:T(8,128)(2,1)S(1)}, bf16[1024,128]{1,0:T(8,128)(2,1)S(1)}, u32[]{:S(2)}, u32[]{:S(2)}) collective-permute-start(bf16[1024,128]{1,0:T(8,128)(2,1)S(1)} %tile_product.5), channel_id=1, source_target_pairs={{0,2},{1,3},{2,0},{3,1},{4,6},{5,7},{6,4},{7,5},{8,10},{9,11},{10,... | collective-permute-start | bytes 786440 | tf_op jit(solution)/shard_map/ppermute | solution.py:392
  32.1 12.9 %collective-permute-start.11 = (bf16[1024,128]{1,0:T(8,128)(2,1)S(1)}, bf16[1024,128]{1,0:T(8,128)(2,1)S(1)}, u32[]{:S(2)}, u32[]{:S(2)}) collective-permute-start(bf16[1024,128]{1,0:T(8,128)(2,1)S(1)} %get-tuple-element.24), channel_id=1, source_target_pairs={{0,4},{1,5},{2,6},{3,7},{4,0},{5,1},{6,2},{7,3},{8,12},{9,13},{10,... | collective-permute-start | bytes 786440 | tf_op jit(solution)/shard_map/ppermute | solution.py:392
  44.4 1.7 %collective-permute-start.10 = (bf16[1024,128]{1,0:T(8,128)(2,1)S(1)}, bf16[1024,128]{1,0:T(8,128)(2,1)S(1)}, u32[]{:S(2)}, u32[]{:S(2)}) collective-permute-start(bf16[1024,128]{1,0:T(8,128)(2,1)S(1)} %add_convert_fusion.near_ref), channel_id=1, source_target_pairs={{0,4},{1,5},{2,6},{3,7},{4,0},{5,1},{6,2},{7,3},{8,12},{9,13},{10,... | collective-permute-start | bytes 786440 | tf_op jit(solution)/shard_map/ppermute | solution.py:392
  46.5 7.8 %collective-permute-start.12 = (bf16[1056,128]{1,0:T(8,128)(2,1)S(1)}, bf16[1056,128]{1,0:T(8,128)(2,1)S(1)}, u32[]{:S(2)}, u32[]{:S(2)}) collective-permute-start(bf16[1056,128]{1,0:T(8,128)(2,1)S(1)} %get-tuple-element.26), channel_id=1, source_target_pairs={{0,8},{1,9},{2,10},{3,11},{4,12},{5,13},{6,14},{7,15},{8,0},{9,1},... | collective-permute-start | bytes 811016 | tf_op jit(solution)/shard_map/ppermute | solution.py:392
  46.6 7.9 %collective-permute-start.14 = (bf16[1040,128]{1,0:T(8,128)(2,1)S(1)}, bf16[1040,128]{1,0:T(8,128)(2,1)S(1)}, u32[]{:S(2)}, u32[]{:S(2)}) collective-permute-start(bf16[1040,128]{1,0:T(8,128)(2,1)S(1)} %get-tuple-element.27), channel_id=1, source_target_pairs={{0,17},{1,0},{2,19},{3,2},{4,21},{5,4},{6,23},{7,6},{8,9},{9,24},{... | collective-permute-start | bytes 798728 | tf_op jit(solution)/shard_map/ppermute | solution.py:392
  47.2 9.0 %collective-permute-start.16 = (bf16[256,128]{1,0:T(8,128)(2,1)S(1)}, bf16[256,128]{1,0:T(8,128)(2,1)S(1)}, u32[]{:S(2)}, u32[]{:S(2)}) collective-permute-start(bf16[256,128]{1,0:T(8,128)(2,1)S(1)} %grad_block.1.refs_0_), channel_id=1, source_target_pairs={{0,1},{1,0},{2,3},{3,2},{4,5},{5,4},{6,7},{7,6},{8,9},{9,8},{10,11... | collective-permute-start | bytes 196616 | tf_op jit(solution)/shard_map/ppermute | solution.py:392
  54.2 6.8 %collective-permute-start.13 = (bf16[1056,128]{1,0:T(8,128)(2,1)S(1)}, bf16[1056,128]{1,0:T(8,128)(2,1)S(1)}, u32[]{:S(2)}, u32[]{:S(2)}) collective-permute-start(bf16[1056,128]{1,0:T(8,128)(2,1)S(1)} %collective-permute-done.12.refs_7_), channel_id=1, source_target_pairs={{0,16},{1,17},{2,18},{3,19},{4,20},{5,21},{6,22},{7,23},{8,24},{9,... | collective-permute-start | bytes 811016 | tf_op jit(solution)/shard_map/ppermute | solution.py:392
  54.5 6.4 %collective-permute-start.15 = (bf16[1040,128]{1,0:T(8,128)(2,1)S(1)}, bf16[1040,128]{1,0:T(8,128)(2,1)S(1)}, u32[]{:S(2)}, u32[]{:S(2)}) collective-permute-start(bf16[1040,128]{1,0:T(8,128)(2,1)S(1)} %collective-permute-done.14.refs_8_), channel_id=1, source_target_pairs={{0,8},{1,9},{2,10},{3,11},{4,12},{5,13},{6,14},{7,15},{8,0},{9,1},... | collective-permute-start | bytes 798728 | tf_op jit(solution)/shard_map/ppermute | solution.py:392
  56.2 4.6 %collective-permute-start.17 = (bf16[1024,128]{1,0:T(8,128)(2,1)S(1)}, bf16[1024,128]{1,0:T(8,128)(2,1)S(1)}, u32[]{:S(2)}, u32[]{:S(2)}) collective-permute-start(bf16[1024,128]{1,0:T(8,128)(2,1)S(1)} %get-tuple-element.29.adj_ref.refs_6_), channel_id=1, source_target_pairs={{0,1},{2,3},{4,5},{6,7},{9,8},{11,10},{13,12},{15,14},{16,17},{18,... | collective-permute-start | bytes 786440 | tf_op jit(solution)/shard_map/ppermute | solution.py:392
  62.5 14.2 %collective-permute-start.22 = (bf16[1024,128]{1,0:T(8,128)(2,1)S(1)}, bf16[1024,128]{1,0:T(8,128)(2,1)S(1)}, u32[]{:S(2)}, u32[]{:S(2)}) collective-permute-start(bf16[1024,128]{1,0:T(8,128)(2,1)S(1)} %tile_product.7.refs_2_.refs_0_), channel_id=1, source_target_pairs={{0,2},{1,3},{2,0},{3,1},{4,6},{5,7},{6,4},{7,5},{8,10},{9,11},{10,... | collective-permute-start | bytes 786440 | tf_op jit(solution)/shard_map/ppermute | solution.py:392
  66.0 7.1 %collective-permute-start.20 = (bf16[256,128]{1,0:T(8,128)(2,1)S(1)}, bf16[256,128]{1,0:T(8,128)(2,1)S(1)}, u32[]{:S(2)}, u32[]{:S(2)}) collective-permute-start(bf16[256,128]{1,0:T(8,128)(2,1)S(1)} %add_after.4.refs_0_), channel_id=1, source_target_pairs={{0,8},{1,9},{2,10},{3,11},{4,12},{5,13},{6,14},{7,15},{8,0},{9,1},... | collective-permute-start | bytes 196616 | tf_op jit(solution)/shard_map/ppermute | solution.py:392
  68.3 13.5 %collective-permute-start.18 = (bf16[1024,128]{1,0:T(8,128)(2,1)S(1)}, bf16[1024,128]{1,0:T(8,128)(2,1)S(1)}, u32[]{:S(2)}, u32[]{:S(2)}) collective-permute-start(bf16[1024,128]{1,0:T(8,128)(2,1)S(1)} %get-tuple-element.30.own_ref), channel_id=1, source_target_pairs={{0,1},{1,5},{2,3},{3,7},{4,0},{5,4},{6,2},{7,6},{8,9},{9,13},{10,1... | collective-permute-start | bytes 786440 | tf_op jit(solution)/shard_map/ppermute | solution.py:392
  71.0 10.8 %collective-permute-start.19 = (bf16[1024,128]{1,0:T(8,128)(2,1)S(1)}, bf16[1024,128]{1,0:T(8,128)(2,1)S(1)}, u32[]{:S(2)}, u32[]{:S(2)}) collective-permute-start(bf16[1024,128]{1,0:T(8,128)(2,1)S(1)} %get-tuple-element.30.own_ref), channel_id=1, source_target_pairs={{1,4},{3,6},{4,1},{6,3},{9,12},{11,14},{12,9},{14,11},{17,20},{19,... | collective-permute-start | bytes 786440 | tf_op jit(solution)/shard_map/ppermute | solution.py:392
  73.1 3.6 %collective-permute-start.21 = (bf16[256,128]{1,0:T(8,128)(2,1)S(1)}, bf16[256,128]{1,0:T(8,128)(2,1)S(1)}, u32[]{:S(2)}, u32[]{:S(2)}) collective-permute-start(bf16[256,128]{1,0:T(8,128)(2,1)S(1)} %add_after.5.refs_0_), channel_id=1, source_target_pairs={{0,16},{1,17},{2,18},{3,19},{4,20},{5,21},{6,22},{7,23},{8,24},{9,... | collective-permute-start | bytes 196616 | tf_op jit(solution)/shard_map/ppermute | solution.py:392
  76.8 7.4 %collective-permute-start.24 = (bf16[1024,128]{1,0:T(8,128)(2,1)S(1)}, bf16[1024,128]{1,0:T(8,128)(2,1)S(1)}, u32[]{:S(2)}, u32[]{:S(2)}) collective-permute-start(bf16[1024,128]{1,0:T(8,128)(2,1)S(1)} %add_after.6.refs_2_.own_ref), channel_id=1, source_target_pairs={{0,1},{1,5},{2,3},{3,7},{4,0},{5,4},{6,2},{7,6},{8,9},{9,13},{10,1... | collective-permute-start | bytes 786440 | tf_op jit(solution)/shard_map/ppermute | solution.py:392
  79.0 7.7 %collective-permute-start.25 = (bf16[1024,128]{1,0:T(8,128)(2,1)S(1)}, bf16[1024,128]{1,0:T(8,128)(2,1)S(1)}, u32[]{:S(2)}, u32[]{:S(2)}) collective-permute-start(bf16[1024,128]{1,0:T(8,128)(2,1)S(1)} %add_after.6.refs_2_.own_ref), channel_id=1, source_target_pairs={{1,4},{3,6},{4,1},{6,3},{9,12},{11,14},{12,9},{14,11},{17,20},{19,... | collective-permute-start | bytes 786440 | tf_op jit(solution)/shard_map/ppermute | solution.py:392
  81.8 1.4 %collective-permute-start.23 = (f32[256,128]{1,0:T(8,128)S(1)}, f32[256,128]{1,0:T(8,128)S(1)}, u32[]{:S(2)}, u32[]{:S(2)}) collective-permute-start(f32[256,128]{1,0:T(8,128)S(1)} %add_after.7.grad_ref), channel_id=1, source_target_pairs={{0,4},{1,5},{2,6},{3,7},{4,0},{5,1},{6,2},{7,3},{8,12},{9,13},{10,... | collective-permute-start | bytes 393224 | tf_op jit(solution)/shard_map/ppermute | solution.py:392

commit v16 on v14

--- a/solution.py
+++ b/solution.py
@@ -8,6 +8,8 @@
 from jax.sharding import PartitionSpec as P
 
 AXES = ("rows", "rep")
+TOGETHER = 2
+ROWS = 256
 WEIGH = 75
 
 
@@ -175,16 +177,20 @@
     for i, kind in enumerate(kinds):
         d = offset_of(kind)
         for s in range(len(sets)):
-            for k in range(slots):
-                row = chosen(metas[s], lambda ref: ref[0, d * slots + k])
-                col = chosen(metas[s], lambda ref: ref[1, d * slots + k])
-                row = pl.multiple_of(row * tile, tile)
-                col = pl.multiple_of(col * tile, tile)
-                acc_ref[pl.ds(row, tile), :] += jnp.dot(
-                    chosen(tiles[s], lambda ref: ref[d, k]),
-                    chosen(panels[i], lambda ref: ref[pl.ds(col, tile), :]),
-                    preferred_element_type=jnp.float32,
-                )
+            for first in range(0, slots, TOGETHER):
+                prods = []
+                for k in range(first, min(first + TOGETHER, slots)):
+                    row = chosen(metas[s], lambda ref: ref[0, d * slots + k])
+                    col = chosen(metas[s], lambda ref: ref[1, d * slots + k])
+                    col = pl.multiple_of(col * tile, tile)
+                    prod = jnp.dot(
+                        chosen(tiles[s], lambda ref: ref[d, k]),
+                        chosen(panels[i], lambda ref: ref[pl.ds(col, tile), :]),
+                        preferred_element_type=jnp.float32,
+                    )
+                    prods.append((pl.multiple_of(row * tile, tile), prod))
+                for row, prod in prods:
+                    acc_ref[pl.ds(row, tile), :] += prod
     out_ref[...] = acc_ref[:rows, :].astype(out_ref.dtype)
 
 
@@ -228,24 +234,23 @@
 
 def middle_kernel(near_ref, far_ref, w_ref, cot_ref, cot_swap_ref, act_ref, *adj_refs):
     j, _, p = place()
-    half = near_ref.shape[1]
-    near = pl.multiple_of(j * half, half)
-    far = pl.multiple_of((1 - j) * half, half)
-    cols = pl.ds(near, half)
-    agg = jnp.dot(
-        near_ref[...], w_ref[pl.ds(near, half), cols], preferred_element_type=jnp.float32
-    )
-    agg += jnp.dot(far_ref[...], w_ref[pl.ds(far, half), cols], preferred_element_type=jnp.float32)
-    sig = jax.nn.sigmoid(agg)
-    act_ref[...] = (agg * sig).astype(act_ref.dtype)
-    slope = sig * (1.0 + agg * (1.0 - sig))
-    cot = jnp.where(j == p, cot_ref[...], cot_swap_ref[...])
-    adj = (cot.astype(jnp.float32) * slope).astype(act_ref.dtype)
-    rows = adj.shape[0]
+    near_cols, far_cols = half_columns(near_ref.shape[1])
+    weight = jnp.concatenate([w_ref[near_cols, near_cols], w_ref[far_cols, near_cols]], axis=0)
+    count = near_ref.shape[0]
+    for start in range(0, count, ROWS):
+        rows = pl.ds(start, ROWS)
+        both = jnp.concatenate([near_ref[rows, :], far_ref[rows, :]], axis=1)
+        agg = jnp.dot(both, weight, preferred_element_type=jnp.float32)
+        sig = jax.nn.sigmoid(agg)
+        act_ref[rows, :] = (agg * sig).astype(act_ref.dtype)
+        slope = sig * (1.0 + agg * (1.0 - sig))
+        cot = jnp.where(j == p, cot_ref[rows, :], cot_swap_ref[rows, :])
+        adj = (cot.astype(jnp.float32) * slope).astype(act_ref.dtype)
+        for ref in adj_refs:
+            ref[rows, :] = adj
     for ref in adj_refs:
-        ref[:rows, :] = adj
-        if ref.shape[0] > rows:
-            ref[rows:, :] = jnp.zeros((ref.shape[0] - rows, ref.shape[1]), ref.dtype)
+        if ref.shape[0] > count:
+            ref[count:, :] = jnp.zeros((ref.shape[0] - count, ref.shape[1]), ref.dtype)
 
 
 def middle(near, far, weight, cot, cot_swap):
@@ -355,12 +360,20 @@
 
 
 def final_kernel(own_ref, one_ref, two_ref, w_ref, out_ref):
+    j, _, p = place()
     near_cols, far_cols = half_columns(own_ref.shape[1])
-    near, far = near_and_far((own_ref, one_ref, two_ref))
-    dims = (((1,), (1,)), ((), ()))
-    total = lax.dot_general(near, w_ref[:, near_cols], dims, preferred_element_type=jnp.float32)
-    total += lax.dot_general(far, w_ref[:, far_cols], dims, preferred_element_type=jnp.float32)
-    out_ref[...] = total.astype(out_ref.dtype)
+    weight = jnp.concatenate([w_ref[:, near_cols], w_ref[:, far_cols]], axis=1)
+    for start in range(0, own_ref.shape[0], ROWS):
+        rows = pl.ds(start, ROWS)
+        own, one, two = own_ref[rows, :], one_ref[rows, :], two_ref[rows, :]
+        near, far = jnp.where(j == p, own, one), jnp.where(j == p, one, two)
+        product = lax.dot_general(
+            jnp.concatenate([near, far], axis=1),
+            weight,
+            (((1,), (1,)), ((), ())),
+            preferred_element_type=jnp.float32,
+        )
+        out_ref[rows, :] = product.astype(out_ref.dtype)
 
 
 def final(back, weight):

time: 87.6 us -> 87.5 us (level)
  no operation moved by 1% of the time
where the time goes in v16:
time: 87.5 us; the launch traced here: 87.2 us
  starting transfers between devices  42.1 us (48%)
  waiting for transfers between devices  31.9 us (36%)
  Pallas kernels  9.85 us (11%)
  local copies, waits for them, and re-layouts  2.43 us (3%)
    ppermute x26, starting transfers between devices, send(): return lax.ppermute(value, AXES, route(shape, move))  42.1 us
    ppermute x26, waiting for transfers between devices, send(): return lax.ppermute(value, AXES, route(shape, move))  31.9 us
    pallas_call x4, Pallas kernels, tile_product(): pl.pallas_call(functools.partial(tile_kernel, kinds, cases, [[case for ca...  5.31 us
  transfers between devices with their start and end apart: 26, of which 13 were waited for; matrix products, arithmetic and copies ran while one was open for 2% of the time, Pallas kernels for 6%

profile of v16, /device:TPU:1, one launch (start us, length us, event | category | flops | bytes accessed | tf_op | source)
XLA Modules:
  0.0 87.2 jit_solution(11657772239306222142)
XLA Ops:
  0.6 2.2 %collective-permute-start = (bf16[5,8,128,128]{3,2,1,0:T(8,128)(2,1)}, bf16[5,8,128,128]{3,2,1,0:T(8,128)(2,1)S(1)}, u32[]{:S(2)}, u32[]{:S(2)}) collective-permute-start(bf16[5,8,128,128]{3,2,1,0:T(8,128)(2,1)} %bitcast.5), channel_id=1, source_target_pairs={{0,4},{1,0},{2,6},{3,2},{4,5},{5,1},{6,7},{7,3},{8,12},{9,8},{10,1... | collective-permute-start | bytes 3932168 | tf_op jit(solution)/shard_map/ppermute | solution.py:405
  2.8 1.1 %constant_dynamic-slice_fusion = (bf16[1024,128]{1,0:T(8,128)(2,1)S(1)}, bf16[1024,128]{1,0:T(8,128)(2,1)S(1)}) fusion(bf16[1024,256]{1,0:T(8,128)(2,1)} %param.6, s32[]{:T(128)S(6)} %select_n.15, s32[]{:T(128)S(6)} %select_n.14), kind=kLoop, calls=%fused_computation.2 | loop fusion | bytes 1048584 | tf_op jit(solution)/shard_map/dynamic_slice | solution.py:445
  3.9 0.7 collective-permute-start.2
  4.6 1.3 %collective-permute-start.3 = (bf16[1024,128]{1,0:T(8,128)(2,1)S(1)}, bf16[1024,128]{1,0:T(8,128)(2,1)S(1)}, u32[]{:S(2)}, u32[]{:S(2)}) collective-permute-start(bf16[1024,128]{1,0:T(8,128)(2,1)S(1)} %get-tuple-element.39), channel_id=1, source_target_pairs={{0,12},{1,21},{2,14},{3,23},{5,9},{7,11},{8,4},{10,6},{12,24},{13,... | collective-permute-start | bytes 786440 | tf_op jit(solution)/shard_map/ppermute | solution.py:405
  5.9 4.8 %collective-permute-start.4 = (bf16[1024,128]{1,0:T(8,128)(2,1)S(1)}, bf16[1024,128]{1,0:T(8,128)(2,1)S(1)}, u32[]{:S(2)}, u32[]{:S(2)}) collective-permute-start(bf16[1024,128]{1,0:T(8,128)(2,1)S(1)} %get-tuple-element.39), channel_id=1, source_target_pairs={{0,4},{1,5},{2,6},{3,7},{4,0},{5,1},{6,2},{7,3},{8,12},{9,13},{10,... | collective-permute-start | bytes 786440 | tf_op jit(solution)/shard_map/ppermute | solution.py:405
  10.6 0.7 copy.12
  11.3 0.7 copy-done.3
  12.0 1.3 %slot_blocks.1.refs_6_.refs_0_.refs_1_ = s32[2,40]{1,0:T(2,128)S(1)} custom-call(s32[2,5,8]{2,1,0:T(8,128)S(1)} %copy.10.coords_ref, s32[5]{0:T(128)S(1)} %bitcast.9), custom_call_target="tpu_custom_call" | custom-call | tf_op jit(solution)/shard_map/slot_blocks/pallas_call | solution.py:135
  13.6 1.8 %collective-permute-start.5 = (bf16[1024,128]{1,0:T(8,128)(2,1)S(1)}, bf16[1024,128]{1,0:T(8,128)(2,1)S(1)}, u32[]{:S(2)}, u32[]{:S(2)}) collective-permute-start(bf16[1024,128]{1,0:T(8,128)(2,1)S(1)} %get-tuple-element.22), channel_id=1, source_target_pairs={{0,16},{1,17},{2,18},{3,19},{4,20},{5,21},{6,22},{7,23},{8,24},{9,... | collective-permute-start | bytes 786440 | tf_op jit(solution)/shard_map/ppermute | solution.py:405
  15.4 1.2 %collective-permute-start.8 = (bf16[1024,128]{1,0:T(8,128)(2,1)S(1)}, bf16[1024,128]{1,0:T(8,128)(2,1)S(1)}, u32[]{:S(2)}, u32[]{:S(2)}) collective-permute-start(bf16[1024,128]{1,0:T(8,128)(2,1)S(1)} %get-tuple-element.26), channel_id=1, source_target_pairs={{0,8},{1,9},{2,10},{3,11},{4,12},{5,13},{6,14},{7,15},{8,0},{9,1},... | collective-permute-start | bytes 786440 | tf_op jit(solution)/shard_map/ppermute | solution.py:405
  16.6 0.2 collective-permute-start.1
  16.8 1.5 %collective-permute-done.1.refs_0_ = s32[2,40]{1,0:T(2,128)S(1)} collective-permute-done((s32[2,40]{1,0:T(2,128)S(1)}, s32[2,40]{1,0:T(2,128)S(1)}, u32[]{:S(2)}, u32[]{:S(2)}) %collective-permute-start.1) | collective-permute-done | bytes 352 | tf_op jit(solution)/shard_map/ppermute | solution.py:405
  18.3 1.3 %collective-permute-start.7 = (bf16[5,8,128,128]{3,2,1,0:T(8,128)(2,1)S(1)}, bf16[5,8,128,128]{3,2,1,0:T(8,128)(2,1)S(1)}, u32[]{:S(2)}, u32[]{:S(2)}) collective-permute-start(bf16[5,8,128,128]{3,2,1,0:T(8,128)(2,1)S(1)} %collective-permute-done.refs_1_.refs_3_), channel_id=1, source_target_pairs={{0,4},{2,6},{5,1},{7,3},{8,12},{10,14},{13,9},{15,11},{16,20},{18,... | collective-permute-start | bytes 3932168 | tf_op jit(solution)/shard_map/ppermute | solution.py:405
  19.6 1.9 %collective-permute-done.5.refs_8_.refs_10_ = bf16[1024,128]{1,0:T(8,128)(2,1)S(1)} collective-permute-done((bf16[1024,128]{1,0:T(8,128)(2,1)S(1)}, bf16[1024,128]{1,0:T(8,128)(2,1)S(1)}, u32[]{:S(2)}, u32[]{:S(2)}) %collective-permute-start.5) | collective-permute-done | bytes 262176 | tf_op jit(solution)/shard_map/ppermute | solution.py:405
  21.5 1.3 %collective-permute-start.6 = (s32[2,40]{1,0:T(2,128)S(1)}, s32[2,40]{1,0:T(2,128)S(1)}, u32[]{:S(2)}, u32[]{:S(2)}) collective-permute-start(s32[2,40]{1,0:T(2,128)S(1)} %collective-permute-done.1.refs_0_), channel_id=1, source_target_pairs={{0,4},{2,6},{5,1},{7,3},{8,12},{10,14},{13,9},{15,11},{16,20},{18,... | collective-permute-start | bytes 968 | tf_op jit(solution)/shard_map/ppermute | solution.py:405
  22.8 0.3 collective-permute-done.8.refs_9_.refs_11_
  23.0 1.2 %tile_product.4.refs_12_ = f32[1024,128]{1,0:T(8,128)S(1)} custom-call(s32[2,40]{1,0:T(2,128)S(1)} %collective-permute-done.1.refs_0_, bf16[5,8,128,128]{3,2,1,0:T(8,128)(2,1)S(1)} %collective-permute-done.refs_1_.refs_3_, bf16[1024,128]{1,0:T(8,128)(2,1)S(1)} %get-tuple-element.40.refs_3_.refs_2_.refs_5_.refs_4_.refs_7_, ...), custom_call_target="tpu_custom_call" | custom-call | flops 12582912000 | bytes 196608000 | tf_op jit(solution)/shard_map/tile_product/pallas_call | solution.py:210
  24.3 0.8 collective-permute-done.6.refs_1_.refs_2_
  25.0 1.4 %tile_product.5 = bf16[1024,128]{1,0:T(8,128)(2,1)S(1)} custom-call(s32[2,40]{1,0:T(2,128)S(1)} %slot_blocks.1.refs_6_.refs_0_.refs_1_, s32[2,40]{1,0:T(2,128)S(1)} %collective-permute-done.6.refs_1_.refs_2_, bf16[5,8,128,128]{3,2,1,0:T(8,128)(2,1)S(1)} %bitcast.6, bf16[5,8,128,128]{3,2,1,0:T(8,128)(2,1)S(1)} %collective-permute-done.7.refs_3_.refs_5_, ...), custom_call_target="tpu_custom_call" | custom-call | flops 167772160 | bytes 2621440 | tf_op jit(solution)/shard_map/tile_product/pallas_call | solution.py:210
  26.5 2.4 %collective-permute-start.9 = (bf16[1024,128]{1,0:T(8,128)(2,1)S(1)}, bf16[1024,128]{1,0:T(8,128)(2,1)S(1)}, u32[]{:S(2)}, u32[]{:S(2)}) collective-permute-start(bf16[1024,128]{1,0:T(8,128)(2,1)S(1)} %tile_product.5), channel_id=1, source_target_pairs={{0,2},{1,3},{2,0},{3,1},{4,6},{5,7},{6,4},{7,5},{8,10},{9,11},{10,... | collective-permute-start | bytes 786440 | tf_op jit(solution)/shard_map/ppermute | solution.py:405
  29.0 0.8 collective-permute-start.11
  29.7 10.9 %collective-permute-done.9 = bf16[1024,128]{1,0:T(8,128)(2,1)S(1)} collective-permute-done((bf16[1024,128]{1,0:T(8,128)(2,1)S(1)}, bf16[1024,128]{1,0:T(8,128)(2,1)S(1)}, u32[]{:S(2)}, u32[]{:S(2)}) %collective-permute-start.9) | collective-permute-done | bytes 262176 | tf_op jit(solution)/shard_map/ppermute | solution.py:405
  40.7 1.2 %collective-permute-start.10 = (bf16[1024,128]{1,0:T(8,128)(2,1)S(1)}, bf16[1024,128]{1,0:T(8,128)(2,1)S(1)}, u32[]{:S(2)}, u32[]{:S(2)}) collective-permute-start(bf16[1024,128]{1,0:T(8,128)(2,1)S(1)} %add_convert_fusion.near_ref), channel_id=1, source_target_pairs={{0,4},{1,5},{2,6},{3,7},{4,0},{5,1},{6,2},{7,3},{8,12},{9,13},{10,... | collective-permute-start | bytes 786440 | tf_op jit(solution)/shard_map/ppermute | solution.py:405
  41.9 1.2 %collective-permute-done.10.far_ref = bf16[1024,128]{1,0:T(8,128)(2,1)S(1)} collective-permute-done((bf16[1024,128]{1,0:T(8,128)(2,1)S(1)}, bf16[1024,128]{1,0:T(8,128)(2,1)S(1)}, u32[]{:S(2)}, u32[]{:S(2)}) %collective-permute-start.10) | collective-permute-done | bytes 262176 | tf_op jit(solution)/shard_map/ppermute | solution.py:405
  43.1 0.4 middle.1
  43.5 1.8 %collective-permute-start.12 = (bf16[1056,128]{1,0:T(8,128)(2,1)S(1)}, bf16[1056,128]{1,0:T(8,128)(2,1)S(1)}, u32[]{:S(2)}, u32[]{:S(2)}) collective-permute-start(bf16[1056,128]{1,0:T(8,128)(2,1)S(1)} %get-tuple-element.30), channel_id=1, source_target_pairs={{0,8},{1,9},{2,10},{3,11},{4,12},{5,13},{6,14},{7,15},{8,0},{9,1},... | collective-permute-start | bytes 811016 | tf_op jit(solution)/shard_map/ppermute | solution.py:405
  45.3 0.3 grad_block.1.refs_0_
  45.7 1.5 %collective-permute-start.16 = (bf16[256,128]{1,0:T(8,128)(2,1)S(1)}, bf16[256,128]{1,0:T(8,128)(2,1)S(1)}, u32[]{:S(2)}, u32[]{:S(2)}) collective-permute-start(bf16[256,128]{1,0:T(8,128)(2,1)S(1)} %grad_block.1.refs_0_), channel_id=1, source_target_pairs={{0,1},{1,0},{2,3},{3,2},{4,5},{5,4},{6,7},{7,6},{8,9},{9,8},{10,11... | collective-permute-start | bytes 196616 | tf_op jit(solution)/shard_map/ppermute | solution.py:405
  47.2 4.7 %collective-permute-done.12.refs_7_ = bf16[1056,128]{1,0:T(8,128)(2,1)S(1)} collective-permute-done((bf16[1056,128]{1,0:T(8,128)(2,1)S(1)}, bf16[1056,128]{1,0:T(8,128)(2,1)S(1)}, u32[]{:S(2)}, u32[]{:S(2)}) %collective-permute-start.12) | collective-permute-done | bytes 270368 | tf_op jit(solution)/shard_map/ppermute | solution.py:405
  51.9 0.9 %collective-permute-start.13 = (bf16[1056,128]{1,0:T(8,128)(2,1)S(1)}, bf16[1056,128]{1,0:T(8,128)(2,1)S(1)}, u32[]{:S(2)}, u32[]{:S(2)}) collective-permute-start(bf16[1056,128]{1,0:T(8,128)(2,1)S(1)} %collective-permute-done.12.refs_7_), channel_id=1, source_target_pairs={{0,16},{1,17},{2,18},{3,19},{4,20},{5,21},{6,22},{7,23},{8,24},{9,... | collective-permute-start | bytes 811016 | tf_op jit(solution)/shard_map/ppermute | solution.py:405
  52.8 1.1 %collective-permute-start.15 = (bf16[1040,128]{1,0:T(8,128)(2,1)S(1)}, bf16[1040,128]{1,0:T(8,128)(2,1)S(1)}, u32[]{:S(2)}, u32[]{:S(2)}) collective-permute-start(bf16[1040,128]{1,0:T(8,128)(2,1)S(1)} %collective-permute-done.14.refs_8_), channel_id=1, source_target_pairs={{0,8},{1,9},{2,10},{3,11},{4,12},{5,13},{6,14},{7,15},{8,0},{9,1},... | collective-permute-start | bytes 798728 | tf_op jit(solution)/shard_map/ppermute | solution.py:405
  53.9 0.1 collective-permute-done.16.refs_1_
  54.0 2.2 %collective-permute-start.17 = (bf16[1024,128]{1,0:T(8,128)(2,1)S(1)}, bf16[1024,128]{1,0:T(8,128)(2,1)S(1)}, u32[]{:S(2)}, u32[]{:S(2)}) collective-permute-start(bf16[1024,128]{1,0:T(8,128)(2,1)S(1)} %get-tuple-element.33.adj_ref.refs_6_), channel_id=1, source_target_pairs={{0,1},{2,3},{4,5},{6,7},{9,8},{11,10},{13,12},{15,14},{16,17},{18,... | collective-permute-start | bytes 786440 | tf_op jit(solution)/shard_map/ppermute | solution.py:405
  56.2 1.2 %tile_product.6.refs_10_ = f32[1024,128]{1,0:T(8,128)S(1)} custom-call(s32[2,40]{1,0:T(2,128)S(1)} %collective-permute-done.1.refs_0_, s32[2,40]{1,0:T(2,128)S(1)} %slot_blocks.1.refs_6_.refs_0_.refs_1_, s32[2,40]{1,0:T(2,128)S(1)} %collective-permute-done.6.refs_1_.refs_2_, bf16[5,8,128,128]{3,2,1,0:T(8,128)(2,1)S(1)} %collective-permute-done.refs_1_.refs_3_, ...), custom_call_target="tpu_custom_call" | custom-call | flops 134217728 | bytes 1572864 | tf_op jit(solution)/shard_map/tile_product/pallas_call | solution.py:210
  57.4 3.2 %collective-permute-done.17.refs_9_ = bf16[1024,128]{1,0:T(8,128)(2,1)S(1)} collective-permute-done((bf16[1024,128]{1,0:T(8,128)(2,1)S(1)}, bf16[1024,128]{1,0:T(8,128)(2,1)S(1)}, u32[]{:S(2)}, u32[]{:S(2)}) %collective-permute-start.17) | collective-permute-done | bytes 262176 | tf_op jit(solution)/shard_map/ppermute | solution.py:405
  60.6 1.5 %tile_product.7.refs_2_.refs_0_ = bf16[1024,128]{1,0:T(8,128)(2,1)S(1)} custom-call(s32[2,40]{1,0:T(2,128)S(1)} %collective-permute-done.1.refs_0_, s32[2,40]{1,0:T(2,128)S(1)} %slot_blocks.1.refs_6_.refs_0_.refs_1_, s32[2,40]{1,0:T(2,128)S(1)} %collective-permute-done.6.refs_1_.refs_2_, bf16[5,8,128,128]{3,2,1,0:T(8,128)(2,1)S(1)} %collective-permute-done.refs_1_.refs_3_, ...), custom_call_target="tpu_custom_call" | custom-call | flops 201326592 | bytes 2359296 | tf_op jit(solution)/shard_map/tile_product/pallas_call | solution.py:210
  62.1 3.1 %collective-permute-start.22 = (bf16[1024,128]{1,0:T(8,128)(2,1)S(1)}, bf16[1024,128]{1,0:T(8,128)(2,1)S(1)}, u32[]{:S(2)}, u32[]{:S(2)}) collective-permute-start(bf16[1024,128]{1,0:T(8,128)(2,1)S(1)} %tile_product.7.refs_2_.refs_0_), channel_id=1, source_target_pairs={{0,2},{1,3},{2,0},{3,1},{4,6},{5,7},{6,4},{7,5},{8,10},{9,11},{10,... | collective-permute-start | bytes 786440 | tf_op jit(solution)/shard_map/ppermute | solution.py:405
  65.3 0.3 collective-permute-start.20
  65.6 3.3 %collective-permute-start.18 = (bf16[1024,128]{1,0:T(8,128)(2,1)S(1)}, bf16[1024,128]{1,0:T(8,128)(2,1)S(1)}, u32[]{:S(2)}, u32[]{:S(2)}) collective-permute-start(bf16[1024,128]{1,0:T(8,128)(2,1)S(1)} %get-tuple-element.34.own_ref), channel_id=1, source_target_pairs={{0,1},{1,5},{2,3},{3,7},{4,0},{5,4},{6,2},{7,6},{8,9},{9,13},{10,1... | collective-permute-start | bytes 786440 | tf_op jit(solution)/shard_map/ppermute | solution.py:405
  68.9 3.0 %collective-permute-start.19 = (bf16[1024,128]{1,0:T(8,128)(2,1)S(1)}, bf16[1024,128]{1,0:T(8,128)(2,1)S(1)}, u32[]{:S(2)}, u32[]{:S(2)}) collective-permute-start(bf16[1024,128]{1,0:T(8,128)(2,1)S(1)} %get-tuple-element.34.own_ref), channel_id=1, source_target_pairs={{1,4},{3,6},{4,1},{6,3},{9,12},{11,14},{12,9},{14,11},{17,20},{19,... | collective-permute-start | bytes 786440 | tf_op jit(solution)/shard_map/ppermute | solution.py:405
  71.9 0.6 collective-permute-start.21
  72.5 3.0 %collective-permute-done.21.refs_2_.refs_1_ = bf16[256,128]{1,0:T(8,128)(2,1)S(1)} collective-permute-done((bf16[256,128]{1,0:T(8,128)(2,1)S(1)}, bf16[256,128]{1,0:T(8,128)(2,1)S(1)}, u32[]{:S(2)}, u32[]{:S(2)}) %collective-permute-start.21) | collective-permute-done | bytes 65568 | tf_op jit(solution)/shard_map/ppermute | solution.py:405
  75.6 2.8 %collective-permute-start.24 = (bf16[1024,128]{1,0:T(8,128)(2,1)S(1)}, bf16[1024,128]{1,0:T(8,128)(2,1)S(1)}, u32[]{:S(2)}, u32[]{:S(2)}) collective-permute-start(bf16[1024,128]{1,0:T(8,128)(2,1)S(1)} %add_after.6.refs_2_.own_ref), channel_id=1, source_target_pairs={{0,1},{1,5},{2,3},{3,7},{4,0},{5,4},{6,2},{7,6},{8,9},{9,13},{10,1... | collective-permute-start | bytes 786440 | tf_op jit(solution)/shard_map/ppermute | solution.py:405
  78.4 2.2 %collective-permute-start.25 = (bf16[1024,128]{1,0:T(8,128)(2,1)S(1)}, bf16[1024,128]{1,0:T(8,128)(2,1)S(1)}, u32[]{:S(2)}, u32[]{:S(2)}) collective-permute-start(bf16[1024,128]{1,0:T(8,128)(2,1)S(1)} %add_after.6.refs_2_.own_ref), channel_id=1, source_target_pairs={{1,4},{3,6},{4,1},{6,3},{9,12},{11,14},{12,9},{14,11},{17,20},{19,... | collective-permute-start | bytes 786440 | tf_op jit(solution)/shard_map/ppermute | solution.py:405
  80.7 1.3 %collective-permute-done.23.rest_ref = f32[256,128]{1,0:T(8,128)S(1)} collective-permute-done((f32[256,128]{1,0:T(8,128)S(1)}, f32[256,128]{1,0:T(8,128)S(1)}, u32[]{:S(2)}, u32[]{:S(2)}) %collective-permute-start.23) | collective-permute-done | bytes 131104 | tf_op jit(solution)/shard_map/ppermute | solution.py:405
  82.1 1.0 %gather_halves.1 = (bf16[1024,256]{1,0:T(8,128)(2,1)}, f32[256,256]{1,0:T(8,128)}) custom-call(bf16[1024,128]{1,0:T(8,128)(2,1)S(1)} %get-tuple-element.34.own_ref, bf16[1024,128]{1,0:T(8,128)(2,1)S(1)} %collective-permute-done.18.refs_3_.one_ref, bf16[1024,128]{1,0:T(8,128)(2,1)S(1)} %collective-permute-done.19.refs_4_.two_ref, ...), custom_call_target="tpu_custom_call" | custom-call | tf_op jit(solution)/shard_map/gather_halves/pallas_call | solution.py:349
  83.1 3.0 %collective-permute-done.25.two_ref = bf16[1024,128]{1,0:T(8,128)(2,1)S(1)} collective-permute-done((bf16[1024,128]{1,0:T(8,128)(2,1)S(1)}, bf16[1024,128]{1,0:T(8,128)(2,1)S(1)}, u32[]{:S(2)}, u32[]{:S(2)}) %collective-permute-start.25) | collective-permute-done | bytes 262176 | tf_op jit(solution)/shard_map/ppermute | solution.py:405
  86.1 1.1 %final.1 = bf16[1024,256]{1,0:T(8,128)(2,1)} custom-call(bf16[1024,128]{1,0:T(8,128)(2,1)S(1)} %add_after.6.refs_2_.own_ref, bf16[1024,128]{1,0:T(8,128)(2,1)S(1)} %collective-permute-done.24.one_ref, bf16[1024,128]{1,0:T(8,128)(2,1)S(1)} %collective-permute-done.25.two_ref, bf16[256,256]{1,0:T(8,128)(2,1)S(1)} %copy-done.2), custom_call_target="tpu_custom_call" | custom-call | flops 134217728 | bytes 2097152 | tf_op jit(solution)/shard_map/final/pallas_call | solution.py:383
  (31 shorter events, 0.6 us)
Async XLA Ops:
  0.6 17.7 %collective-permute-start = (bf16[5,8,128,128]{3,2,1,0:T(8,128)(2,1)}, bf16[5,8,128,128]{3,2,1,0:T(8,128)(2,1)S(1)}, u32[]{:S(2)}, u32[]{:S(2)}) collective-permute-start(bf16[5,8,128,128]{3,2,1,0:T(8,128)(2,1)} %bitcast.5), channel_id=1, source_target_pairs={{0,4},{1,0},{2,6},{3,2},{4,5},{5,1},{6,7},{7,3},{8,12},{9,8},{10,1... | collective-permute-start | bytes 3932168 | tf_op jit(solution)/shard_map/ppermute | solution.py:405
  3.9 9.5 %collective-permute-start.2 = (bf16[1024,128]{1,0:T(8,128)(2,1)S(1)}, bf16[1024,128]{1,0:T(8,128)(2,1)S(1)}, u32[]{:S(2)}, u32[]{:S(2)}) collective-permute-start(bf16[1024,128]{1,0:T(8,128)(2,1)S(1)} %get-tuple-element.40.refs_3_.refs_2_.refs_5_.refs_4_.refs_7_), channel_id=1, source_target_pairs={{0,8},{1,17},{2,10},{3,19},{5,13},{7,15},{8,0},{10,2},{12,28},{13,... | collective-permute-start | bytes 786440 | tf_op jit(solution)/shard_map/ppermute | solution.py:405
  4.6 8.9 %collective-permute-start.3 = (bf16[1024,128]{1,0:T(8,128)(2,1)S(1)}, bf16[1024,128]{1,0:T(8,128)(2,1)S(1)}, u32[]{:S(2)}, u32[]{:S(2)}) collective-permute-start(bf16[1024,128]{1,0:T(8,128)(2,1)S(1)} %get-tuple-element.39), channel_id=1, source_target_pairs={{0,12},{1,21},{2,14},{3,23},{5,9},{7,11},{8,4},{10,6},{12,24},{13,... | collective-permute-start | bytes 786440 | tf_op jit(solution)/shard_map/ppermute | solution.py:405
  5.9 7.6 %collective-permute-start.4 = (bf16[1024,128]{1,0:T(8,128)(2,1)S(1)}, bf16[1024,128]{1,0:T(8,128)(2,1)S(1)}, u32[]{:S(2)}, u32[]{:S(2)}) collective-permute-start(bf16[1024,128]{1,0:T(8,128)(2,1)S(1)} %get-tuple-element.39), channel_id=1, source_target_pairs={{0,4},{1,5},{2,6},{3,7},{4,0},{5,1},{6,2},{7,3},{8,12},{9,13},{10,... | collective-permute-start | bytes 786440 | tf_op jit(solution)/shard_map/ppermute | solution.py:405
  11.3 0.7 copy-start.3
  13.6 7.9 %collective-permute-start.5 = (bf16[1024,128]{1,0:T(8,128)(2,1)S(1)}, bf16[1024,128]{1,0:T(8,128)(2,1)S(1)}, u32[]{:S(2)}, u32[]{:S(2)}) collective-permute-start(bf16[1024,128]{1,0:T(8,128)(2,1)S(1)} %get-tuple-element.22), channel_id=1, source_target_pairs={{0,16},{1,17},{2,18},{3,19},{4,20},{5,21},{6,22},{7,23},{8,24},{9,... | collective-permute-start | bytes 786440 | tf_op jit(solution)/shard_map/ppermute | solution.py:405
  15.4 9.7 %copy-start = (bf16[1,5,8,128,128]{4,3,2,1,0:T(8,128)(2,1)S(1)}, bf16[1,5,8,128,128]{4,3,2,1,0:T(8,128)(2,1)}, u32[]{:S(2)}) copy-start(bf16[1,5,8,128,128]{4,3,2,1,0:T(8,128)(2,1)} %param.9) | copy-start | bytes 3932164
  15.4 7.6 %collective-permute-start.8 = (bf16[1024,128]{1,0:T(8,128)(2,1)S(1)}, bf16[1024,128]{1,0:T(8,128)(2,1)S(1)}, u32[]{:S(2)}, u32[]{:S(2)}) collective-permute-start(bf16[1024,128]{1,0:T(8,128)(2,1)S(1)} %get-tuple-element.26), channel_id=1, source_target_pairs={{0,8},{1,9},{2,10},{3,11},{4,12},{5,13},{6,14},{7,15},{8,0},{9,1},... | collective-permute-start | bytes 786440 | tf_op jit(solution)/shard_map/ppermute | solution.py:405
  16.6 1.7 %collective-permute-start.1 = (s32[2,40]{1,0:T(2,128)S(1)}, s32[2,40]{1,0:T(2,128)S(1)}, u32[]{:S(2)}, u32[]{:S(2)}) collective-permute-start(s32[2,40]{1,0:T(2,128)S(1)} %slot_blocks.1.refs_6_.refs_0_.refs_1_), channel_id=1, source_target_pairs={{0,4},{1,0},{2,6},{3,2},{4,5},{5,1},{6,7},{7,3},{8,12},{9,8},{10,1... | collective-permute-start | bytes 968 | tf_op jit(solution)/shard_map/ppermute | solution.py:405
  18.3 6.7 %collective-permute-start.7 = (bf16[5,8,128,128]{3,2,1,0:T(8,128)(2,1)S(1)}, bf16[5,8,128,128]{3,2,1,0:T(8,128)(2,1)S(1)}, u32[]{:S(2)}, u32[]{:S(2)}) collective-permute-start(bf16[5,8,128,128]{3,2,1,0:T(8,128)(2,1)S(1)} %collective-permute-done.refs_1_.refs_3_), channel_id=1, source_target_pairs={{0,4},{2,6},{5,1},{7,3},{8,12},{10,14},{13,9},{15,11},{16,20},{18,... | collective-permute-start | bytes 3932168 | tf_op jit(solution)/shard_map/ppermute | solution.py:405
  21.5 3.6 %collective-permute-start.6 = (s32[2,40]{1,0:T(2,128)S(1)}, s32[2,40]{1,0:T(2,128)S(1)}, u32[]{:S(2)}, u32[]{:S(2)}) collective-permute-start(s32[2,40]{1,0:T(2,128)S(1)} %collective-permute-done.1.refs_0_), channel_id=1, source_target_pairs={{0,4},{2,6},{5,1},{7,3},{8,12},{10,14},{13,9},{15,11},{16,20},{18,... | collective-permute-start | bytes 968 | tf_op jit(solution)/shard_map/ppermute | solution.py:405
  24.3 4.6 %copy-start.1 = (bf16[1024,256]{1,0:T(8,128)(2,1)S(1)}, bf16[1024,256]{1,0:T(8,128)(2,1)}, u32[]{:S(2)}) copy-start(bf16[1024,256]{1,0:T(8,128)(2,1)} %x_ref.1) | copy-start | bytes 1572868
  26.5 16.6 %copy-start.2 = (bf16[256,256]{1,0:T(8,128)(2,1)S(1)}, bf16[256,256]{1,0:T(8,128)(2,1)}, u32[]{:S(2)}) copy-start(bf16[256,256]{1,0:T(8,128)(2,1)} %w_ref.3) | copy-start | bytes 393220
  26.5 14.1 %collective-permute-start.9 = (bf16[1024,128]{1,0:T(8,128)(2,1)S(1)}, bf16[1024,128]{1,0:T(8,128)(2,1)S(1)}, u32[]{:S(2)}, u32[]{:S(2)}) collective-permute-start(bf16[1024,128]{1,0:T(8,128)(2,1)S(1)} %tile_product.5), channel_id=1, source_target_pairs={{0,2},{1,3},{2,0},{3,1},{4,6},{5,7},{6,4},{7,5},{8,10},{9,11},{10,... | collective-permute-start | bytes 786440 | tf_op jit(solution)/shard_map/ppermute | solution.py:405
  29.0 12.9 %collective-permute-start.11 = (bf16[1024,128]{1,0:T(8,128)(2,1)S(1)}, bf16[1024,128]{1,0:T(8,128)(2,1)S(1)}, u32[]{:S(2)}, u32[]{:S(2)}) collective-permute-start(bf16[1024,128]{1,0:T(8,128)(2,1)S(1)} %get-tuple-element.28), channel_id=1, source_target_pairs={{0,4},{1,5},{2,6},{3,7},{4,0},{5,1},{6,2},{7,3},{8,12},{9,13},{10,... | collective-permute-start | bytes 786440 | tf_op jit(solution)/shard_map/ppermute | solution.py:405
  40.7 2.4 %collective-permute-start.10 = (bf16[1024,128]{1,0:T(8,128)(2,1)S(1)}, bf16[1024,128]{1,0:T(8,128)(2,1)S(1)}, u32[]{:S(2)}, u32[]{:S(2)}) collective-permute-start(bf16[1024,128]{1,0:T(8,128)(2,1)S(1)} %add_convert_fusion.near_ref), channel_id=1, source_target_pairs={{0,4},{1,5},{2,6},{3,7},{4,0},{5,1},{6,2},{7,3},{8,12},{9,13},{10,... | collective-permute-start | bytes 786440 | tf_op jit(solution)/shard_map/ppermute | solution.py:405
  43.5 8.4 %collective-permute-start.12 = (bf16[1056,128]{1,0:T(8,128)(2,1)S(1)}, bf16[1056,128]{1,0:T(8,128)(2,1)S(1)}, u32[]{:S(2)}, u32[]{:S(2)}) collective-permute-start(bf16[1056,128]{1,0:T(8,128)(2,1)S(1)} %get-tuple-element.30), channel_id=1, source_target_pairs={{0,8},{1,9},{2,10},{3,11},{4,12},{5,13},{6,14},{7,15},{8,0},{9,1},... | collective-permute-start | bytes 811016 | tf_op jit(solution)/shard_map/ppermute | solution.py:405
  45.3 7.5 %collective-permute-start.14 = (bf16[1040,128]{1,0:T(8,128)(2,1)S(1)}, bf16[1040,128]{1,0:T(8,128)(2,1)S(1)}, u32[]{:S(2)}, u32[]{:S(2)}) collective-permute-start(bf16[1040,128]{1,0:T(8,128)(2,1)S(1)} %get-tuple-element.31), channel_id=1, source_target_pairs={{0,17},{1,0},{2,19},{3,2},{4,21},{5,4},{6,23},{7,6},{8,9},{9,24},{... | collective-permute-start | bytes 798728 | tf_op jit(solution)/shard_map/ppermute | solution.py:405
  45.7 8.3 %collective-permute-start.16 = (bf16[256,128]{1,0:T(8,128)(2,1)S(1)}, bf16[256,128]{1,0:T(8,128)(2,1)S(1)}, u32[]{:S(2)}, u32[]{:S(2)}) collective-permute-start(bf16[256,128]{1,0:T(8,128)(2,1)S(1)} %grad_block.1.refs_0_), channel_id=1, source_target_pairs={{0,1},{1,0},{2,3},{3,2},{4,5},{5,4},{6,7},{7,6},{8,9},{9,8},{10,11... | collective-permute-start | bytes 196616 | tf_op jit(solution)/shard_map/ppermute | solution.py:405
  51.9 8.8 %collective-permute-start.13 = (bf16[1056,128]{1,0:T(8,128)(2,1)S(1)}, bf16[1056,128]{1,0:T(8,128)(2,1)S(1)}, u32[]{:S(2)}, u32[]{:S(2)}) collective-permute-start(bf16[1056,128]{1,0:T(8,128)(2,1)S(1)} %collective-permute-done.12.refs_7_), channel_id=1, source_target_pairs={{0,16},{1,17},{2,18},{3,19},{4,20},{5,21},{6,22},{7,23},{8,24},{9,... | collective-permute-start | bytes 811016 | tf_op jit(solution)/shard_map/ppermute | solution.py:405
  52.8 7.8 %collective-permute-start.15 = (bf16[1040,128]{1,0:T(8,128)(2,1)S(1)}, bf16[1040,128]{1,0:T(8,128)(2,1)S(1)}, u32[]{:S(2)}, u32[]{:S(2)}) collective-permute-start(bf16[1040,128]{1,0:T(8,128)(2,1)S(1)} %collective-permute-done.14.refs_8_), channel_id=1, source_target_pairs={{0,8},{1,9},{2,10},{3,11},{4,12},{5,13},{6,14},{7,15},{8,0},{9,1},... | collective-permute-start | bytes 798728 | tf_op jit(solution)/shard_map/ppermute | solution.py:405
  54.0 6.6 %collective-permute-start.17 = (bf16[1024,128]{1,0:T(8,128)(2,1)S(1)}, bf16[1024,128]{1,0:T(8,128)(2,1)S(1)}, u32[]{:S(2)}, u32[]{:S(2)}) collective-permute-start(bf16[1024,128]{1,0:T(8,128)(2,1)S(1)} %get-tuple-element.33.adj_ref.refs_6_), channel_id=1, source_target_pairs={{0,1},{2,3},{4,5},{6,7},{9,8},{11,10},{13,12},{15,14},{16,17},{18,... | collective-permute-start | bytes 786440 | tf_op jit(solution)/shard_map/ppermute | solution.py:405
  62.1 13.4 %collective-permute-start.22 = (bf16[1024,128]{1,0:T(8,128)(2,1)S(1)}, bf16[1024,128]{1,0:T(8,128)(2,1)S(1)}, u32[]{:S(2)}, u32[]{:S(2)}) collective-permute-start(bf16[1024,128]{1,0:T(8,128)(2,1)S(1)} %tile_product.7.refs_2_.refs_0_), channel_id=1, source_target_pairs={{0,2},{1,3},{2,0},{3,1},{4,6},{5,7},{6,4},{7,5},{8,10},{9,11},{10,... | collective-permute-start | bytes 786440 | tf_op jit(solution)/shard_map/ppermute | solution.py:405
  65.3 6.6 %collective-permute-start.20 = (bf16[256,128]{1,0:T(8,128)(2,1)S(1)}, bf16[256,128]{1,0:T(8,128)(2,1)S(1)}, u32[]{:S(2)}, u32[]{:S(2)}) collective-permute-start(bf16[256,128]{1,0:T(8,128)(2,1)S(1)} %add_after.4.refs_0_), channel_id=1, source_target_pairs={{0,8},{1,9},{2,10},{3,11},{4,12},{5,13},{6,14},{7,15},{8,0},{9,1},... | collective-permute-start | bytes 196616 | tf_op jit(solution)/shard_map/ppermute | solution.py:405
  65.6 15.0 %collective-permute-start.18 = (bf16[1024,128]{1,0:T(8,128)(2,1)S(1)}, bf16[1024,128]{1,0:T(8,128)(2,1)S(1)}, u32[]{:S(2)}, u32[]{:S(2)}) collective-permute-start(bf16[1024,128]{1,0:T(8,128)(2,1)S(1)} %get-tuple-element.34.own_ref), channel_id=1, source_target_pairs={{0,1},{1,5},{2,3},{3,7},{4,0},{5,4},{6,2},{7,6},{8,9},{9,13},{10,1... | collective-permute-start | bytes 786440 | tf_op jit(solution)/shard_map/ppermute | solution.py:405
  68.9 11.7 %collective-permute-start.19 = (bf16[1024,128]{1,0:T(8,128)(2,1)S(1)}, bf16[1024,128]{1,0:T(8,128)(2,1)S(1)}, u32[]{:S(2)}, u32[]{:S(2)}) collective-permute-start(bf16[1024,128]{1,0:T(8,128)(2,1)S(1)} %get-tuple-element.34.own_ref), channel_id=1, source_target_pairs={{1,4},{3,6},{4,1},{6,3},{9,12},{11,14},{12,9},{14,11},{17,20},{19,... | collective-permute-start | bytes 786440 | tf_op jit(solution)/shard_map/ppermute | solution.py:405
  71.9 3.6 %collective-permute-start.21 = (bf16[256,128]{1,0:T(8,128)(2,1)S(1)}, bf16[256,128]{1,0:T(8,128)(2,1)S(1)}, u32[]{:S(2)}, u32[]{:S(2)}) collective-permute-start(bf16[256,128]{1,0:T(8,128)(2,1)S(1)} %add_after.5.refs_0_), channel_id=1, source_target_pairs={{0,16},{1,17},{2,18},{3,19},{4,20},{5,21},{6,22},{7,23},{8,24},{9,... | collective-permute-start | bytes 196616 | tf_op jit(solution)/shard_map/ppermute | solution.py:405
  75.6 7.5 %collective-permute-start.24 = (bf16[1024,128]{1,0:T(8,128)(2,1)S(1)}, bf16[1024,128]{1,0:T(8,128)(2,1)S(1)}, u32[]{:S(2)}, u32[]{:S(2)}) collective-permute-start(bf16[1024,128]{1,0:T(8,128)(2,1)S(1)} %add_after.6.refs_2_.own_ref), channel_id=1, source_target_pairs={{0,1},{1,5},{2,3},{3,7},{4,0},{5,4},{6,2},{7,6},{8,9},{9,13},{10,1... | collective-permute-start | bytes 786440 | tf_op jit(solution)/shard_map/ppermute | solution.py:405
  78.4 7.7 %collective-permute-start.25 = (bf16[1024,128]{1,0:T(8,128)(2,1)S(1)}, bf16[1024,128]{1,0:T(8,128)(2,1)S(1)}, u32[]{:S(2)}, u32[]{:S(2)}) collective-permute-start(bf16[1024,128]{1,0:T(8,128)(2,1)S(1)} %add_after.6.refs_2_.own_ref), channel_id=1, source_target_pairs={{1,4},{3,6},{4,1},{6,3},{9,12},{11,14},{12,9},{14,11},{17,20},{19,... | collective-permute-start | bytes 786440 | tf_op jit(solution)/shard_map/ppermute | solution.py:405
  80.6 1.4 %collective-permute-start.23 = (f32[256,128]{1,0:T(8,128)S(1)}, f32[256,128]{1,0:T(8,128)S(1)}, u32[]{:S(2)}, u32[]{:S(2)}) collective-permute-start(f32[256,128]{1,0:T(8,128)S(1)} %add_after.7.grad_ref), channel_id=1, source_target_pairs={{0,4},{1,5},{2,6},{3,7},{4,0},{5,1},{6,2},{7,3},{8,12},{9,13},{10,... | collective-permute-start | bytes 393224 | tf_op jit(solution)/shard_map/ppermute | solution.py:405

commit v17 on v16

--- a/solution.py
+++ b/solution.py
@@ -497,13 +497,11 @@
     )
     second = send(direct if four else adj_longer, to_second)
     grad = grad_block(scale, near, far_half, adj)
-    grad_got = send(grad, lambda c, j, z: (c, j, z ^ 1))
-    adj_later, grad_got = lax.optimization_barrier((adj, grad_got))
     far = send(near_one, to_far)
     near_choice = [("still", near_one)]
     if four:
         near_two = send(
-            adj_later, lambda c, j, z: None if (c + z) % 2 else (c, j, z ^ 1)
+            adj, lambda c, j, z: None if (c + z) % 2 else (c, j, z ^ 1)
         )
         near_choice.append(("relay", near_two))
     panels = [("self", [(None, adj)]), ("direct", [(None, direct)])]
@@ -518,7 +516,9 @@
 
     act_later, back_part = lax.optimization_barrier((act, back_part))
     act_parts = [act, *deliver(act_later)]
-    grad = add_after([grad, grad_got], jnp.bfloat16, back_part)
+    grad, back_part = lax.optimization_barrier((grad, back_part))
+    grad_got = send(grad, lambda c, j, z: (c, j, z ^ 1))
+    grad = add_after([grad, grad_got], jnp.bfloat16)
     step = 1
     while step < shape[0]:
         got = send(grad, lambda c, j, z, s=step: (c ^ s, j, z))

time: 87.5 us -> 91.1 us (1.041)
  starting transfers between devices: 42.1 us -> 47.1 us
  waiting for transfers between devices: 31.9 us -> 30.5 us
    ppermute x26, starting transfers between devices: 42.1 us -> 47.1 us  [send(): return lax.ppermute(value, AXES, route(shape, move))]
    ppermute x26, waiting for transfers between devices: 31.9 us -> 30.5 us  [send(): return lax.ppermute(value, AXES, route(shape, move))]
  transfers between devices with their start and end apart: 26 -> 26, of which waited for: 13 -> 14; matrix products, arithmetic and copies ran while one was open for 2% -> 2% of each run, Pallas kernels for 6% -> 6%
where the time goes in v17:
time: 91.1 us; the launch traced here: 90.8 us
  starting transfers between devices  47.1 us (52%)
  waiting for transfers between devices  30.5 us (33%)
  Pallas kernels  9.86 us (11%)
  local copies, waits for them, and re-layouts  2.43 us (3%)
    ppermute x26, starting transfers between devices, send(): return lax.ppermute(value, AXES, route(shape, move))  47.1 us
    ppermute x26, waiting for transfers between devices, send(): return lax.ppermute(value, AXES, route(shape, move))  30.5 us
    pallas_call x4, Pallas kernels, tile_product(): pl.pallas_call(functools.partial(tile_kernel, kinds, cases, [[case for ca...  5.31 us
  transfers between devices with their start and end apart: 26, of which 14 were waited for; matrix products, arithmetic and copies ran while one was open for 2% of the time, Pallas kernels for 6%

profile of v17, /device:TPU:1, one launch (start us, length us, event | category | flops | bytes accessed | tf_op | source)
XLA Modules:
  0.0 90.8 jit_solution(11446037296572922059)
XLA Ops:
  0.6 2.2 %collective-permute-start = (bf16[5,8,128,128]{3,2,1,0:T(8,128)(2,1)}, bf16[5,8,128,128]{3,2,1,0:T(8,128)(2,1)S(1)}, u32[]{:S(2)}, u32[]{:S(2)}) collective-permute-start(bf16[5,8,128,128]{3,2,1,0:T(8,128)(2,1)} %bitcast.5), channel_id=1, source_target_pairs={{0,4},{1,0},{2,6},{3,2},{4,5},{5,1},{6,7},{7,3},{8,12},{9,8},{10,1... | collective-permute-start | bytes 3932168 | tf_op jit(solution)/shard_map/ppermute | solution.py:405
  2.8 1.1 %constant_dynamic-slice_fusion = (bf16[1024,128]{1,0:T(8,128)(2,1)S(1)}, bf16[1024,128]{1,0:T(8,128)(2,1)S(1)}) fusion(bf16[1024,256]{1,0:T(8,128)(2,1)} %param.6, s32[]{:T(128)S(6)} %select_n.15, s32[]{:T(128)S(6)} %select_n.14), kind=kLoop, calls=%fused_computation.2 | loop fusion | bytes 1048584 | tf_op jit(solution)/shard_map/dynamic_slice | solution.py:445
  3.9 0.7 collective-permute-start.2
  4.6 1.3 %collective-permute-start.3 = (bf16[1024,128]{1,0:T(8,128)(2,1)S(1)}, bf16[1024,128]{1,0:T(8,128)(2,1)S(1)}, u32[]{:S(2)}, u32[]{:S(2)}) collective-permute-start(bf16[1024,128]{1,0:T(8,128)(2,1)S(1)} %get-tuple-element.39), channel_id=1, source_target_pairs={{0,12},{1,21},{2,14},{3,23},{5,9},{7,11},{8,4},{10,6},{12,24},{13,... | collective-permute-start | bytes 786440 | tf_op jit(solution)/shard_map/ppermute | solution.py:405
  5.9 4.8 %collective-permute-start.4 = (bf16[1024,128]{1,0:T(8,128)(2,1)S(1)}, bf16[1024,128]{1,0:T(8,128)(2,1)S(1)}, u32[]{:S(2)}, u32[]{:S(2)}) collective-permute-start(bf16[1024,128]{1,0:T(8,128)(2,1)S(1)} %get-tuple-element.39), channel_id=1, source_target_pairs={{0,4},{1,5},{2,6},{3,7},{4,0},{5,1},{6,2},{7,3},{8,12},{9,13},{10,... | collective-permute-start | bytes 786440 | tf_op jit(solution)/shard_map/ppermute | solution.py:405
  10.6 0.7 copy.12
  11.3 0.7 copy-done.3
  12.0 1.3 %slot_blocks.1.refs_6_.refs_0_.refs_1_ = s32[2,40]{1,0:T(2,128)S(1)} custom-call(s32[2,5,8]{2,1,0:T(8,128)S(1)} %copy.10.coords_ref, s32[5]{0:T(128)S(1)} %bitcast.9), custom_call_target="tpu_custom_call" | custom-call | tf_op jit(solution)/shard_map/slot_blocks/pallas_call | solution.py:135
  13.6 1.8 %collective-permute-start.5 = (bf16[1024,128]{1,0:T(8,128)(2,1)S(1)}, bf16[1024,128]{1,0:T(8,128)(2,1)S(1)}, u32[]{:S(2)}, u32[]{:S(2)}) collective-permute-start(bf16[1024,128]{1,0:T(8,128)(2,1)S(1)} %get-tuple-element.22), channel_id=1, source_target_pairs={{0,16},{1,17},{2,18},{3,19},{4,20},{5,21},{6,22},{7,23},{8,24},{9,... | collective-permute-start | bytes 786440 | tf_op jit(solution)/shard_map/ppermute | solution.py:405
  15.4 1.2 %collective-permute-start.8 = (bf16[1024,128]{1,0:T(8,128)(2,1)S(1)}, bf16[1024,128]{1,0:T(8,128)(2,1)S(1)}, u32[]{:S(2)}, u32[]{:S(2)}) collective-permute-start(bf16[1024,128]{1,0:T(8,128)(2,1)S(1)} %get-tuple-element.26), channel_id=1, source_target_pairs={{0,8},{1,9},{2,10},{3,11},{4,12},{5,13},{6,14},{7,15},{8,0},{9,1},... | collective-permute-start | bytes 786440 | tf_op jit(solution)/shard_map/ppermute | solution.py:405
  16.6 0.2 collective-permute-start.1
  16.8 1.5 %collective-permute-done.1.refs_0_ = s32[2,40]{1,0:T(2,128)S(1)} collective-permute-done((s32[2,40]{1,0:T(2,128)S(1)}, s32[2,40]{1,0:T(2,128)S(1)}, u32[]{:S(2)}, u32[]{:S(2)}) %collective-permute-start.1) | collective-permute-done | bytes 352 | tf_op jit(solution)/shard_map/ppermute | solution.py:405
  18.3 1.3 %collective-permute-start.7 = (bf16[5,8,128,128]{3,2,1,0:T(8,128)(2,1)S(1)}, bf16[5,8,128,128]{3,2,1,0:T(8,128)(2,1)S(1)}, u32[]{:S(2)}, u32[]{:S(2)}) collective-permute-start(bf16[5,8,128,128]{3,2,1,0:T(8,128)(2,1)S(1)} %collective-permute-done.refs_1_.refs_3_), channel_id=1, source_target_pairs={{0,4},{2,6},{5,1},{7,3},{8,12},{10,14},{13,9},{15,11},{16,20},{18,... | collective-permute-start | bytes 3932168 | tf_op jit(solution)/shard_map/ppermute | solution.py:405
  19.6 1.9 %collective-permute-done.5.refs_8_.refs_10_ = bf16[1024,128]{1,0:T(8,128)(2,1)S(1)} collective-permute-done((bf16[1024,128]{1,0:T(8,128)(2,1)S(1)}, bf16[1024,128]{1,0:T(8,128)(2,1)S(1)}, u32[]{:S(2)}, u32[]{:S(2)}) %collective-permute-start.5) | collective-permute-done | bytes 262176 | tf_op jit(solution)/shard_map/ppermute | solution.py:405
  21.5 1.3 %collective-permute-start.6 = (s32[2,40]{1,0:T(2,128)S(1)}, s32[2,40]{1,0:T(2,128)S(1)}, u32[]{:S(2)}, u32[]{:S(2)}) collective-permute-start(s32[2,40]{1,0:T(2,128)S(1)} %collective-permute-done.1.refs_0_), channel_id=1, source_target_pairs={{0,4},{2,6},{5,1},{7,3},{8,12},{10,14},{13,9},{15,11},{16,20},{18,... | collective-permute-start | bytes 968 | tf_op jit(solution)/shard_map/ppermute | solution.py:405
  22.8 0.3 collective-permute-done.8.refs_9_.refs_11_
  23.0 1.2 %tile_product.4.refs_12_ = f32[1024,128]{1,0:T(8,128)S(1)} custom-call(s32[2,40]{1,0:T(2,128)S(1)} %collective-permute-done.1.refs_0_, bf16[5,8,128,128]{3,2,1,0:T(8,128)(2,1)S(1)} %collective-permute-done.refs_1_.refs_3_, bf16[1024,128]{1,0:T(8,128)(2,1)S(1)} %get-tuple-element.40.refs_3_.refs_2_.refs_5_.refs_4_.refs_7_, ...), custom_call_target="tpu_custom_call" | custom-call | flops 12582912000 | bytes 196608000 | tf_op jit(solution)/shard_map/tile_product/pallas_call | solution.py:210
  24.3 0.8 collective-permute-done.6.refs_1_.refs_2_
  25.0 1.4 %tile_product.5 = bf16[1024,128]{1,0:T(8,128)(2,1)S(1)} custom-call(s32[2,40]{1,0:T(2,128)S(1)} %slot_blocks.1.refs_6_.refs_0_.refs_1_, s32[2,40]{1,0:T(2,128)S(1)} %collective-permute-done.6.refs_1_.refs_2_, bf16[5,8,128,128]{3,2,1,0:T(8,128)(2,1)S(1)} %bitcast.6, bf16[5,8,128,128]{3,2,1,0:T(8,128)(2,1)S(1)} %collective-permute-done.7.refs_3_.refs_5_, ...), custom_call_target="tpu_custom_call" | custom-call | flops 167772160 | bytes 2621440 | tf_op jit(solution)/shard_map/tile_product/pallas_call | solution.py:210
  26.5 2.4 %collective-permute-start.9 = (bf16[1024,128]{1,0:T(8,128)(2,1)S(1)}, bf16[1024,128]{1,0:T(8,128)(2,1)S(1)}, u32[]{:S(2)}, u32[]{:S(2)}) collective-permute-start(bf16[1024,128]{1,0:T(8,128)(2,1)S(1)} %tile_product.5), channel_id=1, source_target_pairs={{0,2},{1,3},{2,0},{3,1},{4,6},{5,7},{6,4},{7,5},{8,10},{9,11},{10,... | collective-permute-start | bytes 786440 | tf_op jit(solution)/shard_map/ppermute | solution.py:405
  28.9 0.1 halves.1
  29.0 0.8 collective-permute-start.11
  29.7 10.9 %collective-permute-done.9 = bf16[1024,128]{1,0:T(8,128)(2,1)S(1)} collective-permute-done((bf16[1024,128]{1,0:T(8,128)(2,1)S(1)}, bf16[1024,128]{1,0:T(8,128)(2,1)S(1)}, u32[]{:S(2)}, u32[]{:S(2)}) %collective-permute-start.9) | collective-permute-done | bytes 262176 | tf_op jit(solution)/shard_map/ppermute | solution.py:405
  40.7 1.2 %collective-permute-start.10 = (bf16[1024,128]{1,0:T(8,128)(2,1)S(1)}, bf16[1024,128]{1,0:T(8,128)(2,1)S(1)}, u32[]{:S(2)}, u32[]{:S(2)}) collective-permute-start(bf16[1024,128]{1,0:T(8,128)(2,1)S(1)} %add_convert_fusion.near_ref), channel_id=1, source_target_pairs={{0,4},{1,5},{2,6},{3,7},{4,0},{5,1},{6,2},{7,3},{8,12},{9,13},{10,... | collective-permute-start | bytes 786440 | tf_op jit(solution)/shard_map/ppermute | solution.py:405
  41.9 1.2 %collective-permute-done.10.far_ref = bf16[1024,128]{1,0:T(8,128)(2,1)S(1)} collective-permute-done((bf16[1024,128]{1,0:T(8,128)(2,1)S(1)}, bf16[1024,128]{1,0:T(8,128)(2,1)S(1)}, u32[]{:S(2)}, u32[]{:S(2)}) %collective-permute-start.10) | collective-permute-done | bytes 262176 | tf_op jit(solution)/shard_map/ppermute | solution.py:405
  43.1 0.4 middle.1
  43.5 1.8 %collective-permute-start.12 = (bf16[1056,128]{1,0:T(8,128)(2,1)S(1)}, bf16[1056,128]{1,0:T(8,128)(2,1)S(1)}, u32[]{:S(2)}, u32[]{:S(2)}) collective-permute-start(bf16[1056,128]{1,0:T(8,128)(2,1)S(1)} %get-tuple-element.30), channel_id=1, source_target_pairs={{0,8},{1,9},{2,10},{3,11},{4,12},{5,13},{6,14},{7,15},{8,0},{9,1},... | collective-permute-start | bytes 811016 | tf_op jit(solution)/shard_map/ppermute | solution.py:405
  45.3 3.4 %collective-permute-start.16 = (bf16[1024,128]{1,0:T(8,128)(2,1)S(1)}, bf16[1024,128]{1,0:T(8,128)(2,1)S(1)}, u32[]{:S(2)}, u32[]{:S(2)}) collective-permute-start(bf16[1024,128]{1,0:T(8,128)(2,1)S(1)} %get-tuple-element.32.refs_6_.adj_ref), channel_id=1, source_target_pairs={{0,1},{2,3},{4,5},{6,7},{9,8},{11,10},{13,12},{15,14},{16,17},{18,... | collective-permute-start | bytes 786440 | tf_op jit(solution)/shard_map/ppermute | solution.py:405
  48.7 3.9 %collective-permute-done.14.refs_8_ = bf16[1040,128]{1,0:T(8,128)(2,1)S(1)} collective-permute-done((bf16[1040,128]{1,0:T(8,128)(2,1)S(1)}, bf16[1040,128]{1,0:T(8,128)(2,1)S(1)}, u32[]{:S(2)}, u32[]{:S(2)}) %collective-permute-start.14) | collective-permute-done | bytes 266272 | tf_op jit(solution)/shard_map/ppermute | solution.py:405
  52.6 1.3 %collective-permute-start.15 = (bf16[1040,128]{1,0:T(8,128)(2,1)S(1)}, bf16[1040,128]{1,0:T(8,128)(2,1)S(1)}, u32[]{:S(2)}, u32[]{:S(2)}) collective-permute-start(bf16[1040,128]{1,0:T(8,128)(2,1)S(1)} %collective-permute-done.14.refs_8_), channel_id=1, source_target_pairs={{0,8},{1,9},{2,10},{3,11},{4,12},{5,13},{6,14},{7,15},{8,0},{9,1},... | collective-permute-start | bytes 798728 | tf_op jit(solution)/shard_map/ppermute | solution.py:405
  53.9 0.9 collective-permute-start.13
  54.8 0.3 grad_block.1.refs_0_
  55.1 1.2 %tile_product.6.refs_10_ = f32[1024,128]{1,0:T(8,128)S(1)} custom-call(s32[2,40]{1,0:T(2,128)S(1)} %collective-permute-done.1.refs_0_, s32[2,40]{1,0:T(2,128)S(1)} %slot_blocks.1.refs_6_.refs_0_.refs_1_, s32[2,40]{1,0:T(2,128)S(1)} %collective-permute-done.6.refs_1_.refs_2_, bf16[5,8,128,128]{3,2,1,0:T(8,128)(2,1)S(1)} %collective-permute-done.refs_1_.refs_3_, ...), custom_call_target="tpu_custom_call" | custom-call | flops 134217728 | bytes 1572864 | tf_op jit(solution)/shard_map/tile_product/pallas_call | solution.py:210
  56.3 2.6 %collective-permute-done.15.refs_7_ = bf16[1040,128]{1,0:T(8,128)(2,1)S(1)} collective-permute-done((bf16[1040,128]{1,0:T(8,128)(2,1)S(1)}, bf16[1040,128]{1,0:T(8,128)(2,1)S(1)}, u32[]{:S(2)}, u32[]{:S(2)}) %collective-permute-start.15) | collective-permute-done | bytes 266272 | tf_op jit(solution)/shard_map/ppermute | solution.py:405
  58.9 0.6 collective-permute-done.13.refs_6_
  59.6 1.5 %tile_product.7.refs_0_ = bf16[1024,128]{1,0:T(8,128)(2,1)S(1)} custom-call(s32[2,40]{1,0:T(2,128)S(1)} %collective-permute-done.1.refs_0_, s32[2,40]{1,0:T(2,128)S(1)} %slot_blocks.1.refs_6_.refs_0_.refs_1_, s32[2,40]{1,0:T(2,128)S(1)} %collective-permute-done.6.refs_1_.refs_2_, bf16[5,8,128,128]{3,2,1,0:T(8,128)(2,1)S(1)} %collective-permute-done.refs_1_.refs_3_, ...), custom_call_target="tpu_custom_call" | custom-call | flops 201326592 | bytes 2359296 | tf_op jit(solution)/shard_map/tile_product/pallas_call | solution.py:210
  61.1 2.1 %collective-permute-start.22 = (bf16[1024,128]{1,0:T(8,128)(2,1)S(1)}, bf16[1024,128]{1,0:T(8,128)(2,1)S(1)}, u32[]{:S(2)}, u32[]{:S(2)}) collective-permute-start(bf16[1024,128]{1,0:T(8,128)(2,1)S(1)} %tile_product.7.refs_0_), channel_id=1, source_target_pairs={{0,2},{1,3},{2,0},{3,1},{4,6},{5,7},{6,4},{7,5},{8,10},{9,11},{10,... | collective-permute-start | bytes 786440 | tf_op jit(solution)/shard_map/ppermute | solution.py:405
  63.3 4.1 %collective-permute-start.17 = (bf16[1024,128]{1,0:T(8,128)(2,1)S(1)}, bf16[1024,128]{1,0:T(8,128)(2,1)S(1)}, u32[]{:S(2)}, u32[]{:S(2)}) collective-permute-start(bf16[1024,128]{1,0:T(8,128)(2,1)S(1)} %get-tuple-element.33.own_ref), channel_id=1, source_target_pairs={{0,1},{1,5},{2,3},{3,7},{4,0},{5,4},{6,2},{7,6},{8,9},{9,13},{10,1... | collective-permute-start | bytes 786440 | tf_op jit(solution)/shard_map/ppermute | solution.py:405
  67.4 1.8 %collective-permute-start.20 = (bf16[256,128]{1,0:T(8,128)(2,1)S(1)}, bf16[256,128]{1,0:T(8,128)(2,1)S(1)}, u32[]{:S(2)}, u32[]{:S(2)}) collective-permute-start(bf16[256,128]{1,0:T(8,128)(2,1)S(1)} %add_after.4.refs_0_), channel_id=1, source_target_pairs={{0,8},{1,9},{2,10},{3,11},{4,12},{5,13},{6,14},{7,15},{8,0},{9,1},... | collective-permute-start | bytes 196616 | tf_op jit(solution)/shard_map/ppermute | solution.py:405
  69.2 6.7 %collective-permute-start.18 = (bf16[1024,128]{1,0:T(8,128)(2,1)S(1)}, bf16[1024,128]{1,0:T(8,128)(2,1)S(1)}, u32[]{:S(2)}, u32[]{:S(2)}) collective-permute-start(bf16[1024,128]{1,0:T(8,128)(2,1)S(1)} %get-tuple-element.33.own_ref), channel_id=1, source_target_pairs={{1,4},{3,6},{4,1},{6,3},{9,12},{11,14},{12,9},{14,11},{17,20},{19,... | collective-permute-start | bytes 786440 | tf_op jit(solution)/shard_map/ppermute | solution.py:405
  75.9 0.8 collective-permute-start.21
  76.7 2.4 %collective-permute-done.21.refs_2_.refs_1_ = bf16[256,128]{1,0:T(8,128)(2,1)S(1)} collective-permute-done((bf16[256,128]{1,0:T(8,128)(2,1)S(1)}, bf16[256,128]{1,0:T(8,128)(2,1)S(1)}, u32[]{:S(2)}, u32[]{:S(2)}) %collective-permute-start.21) | collective-permute-done | bytes 65568 | tf_op jit(solution)/shard_map/ppermute | solution.py:405
  79.1 2.9 %collective-permute-start.24 = (bf16[1024,128]{1,0:T(8,128)(2,1)S(1)}, bf16[1024,128]{1,0:T(8,128)(2,1)S(1)}, u32[]{:S(2)}, u32[]{:S(2)}) collective-permute-start(bf16[1024,128]{1,0:T(8,128)(2,1)S(1)} %add_after.6.refs_2_.own_ref), channel_id=1, source_target_pairs={{0,1},{1,5},{2,3},{3,7},{4,0},{5,4},{6,2},{7,6},{8,9},{9,13},{10,1... | collective-permute-start | bytes 786440 | tf_op jit(solution)/shard_map/ppermute | solution.py:405
  82.0 2.2 %collective-permute-start.25 = (bf16[1024,128]{1,0:T(8,128)(2,1)S(1)}, bf16[1024,128]{1,0:T(8,128)(2,1)S(1)}, u32[]{:S(2)}, u32[]{:S(2)}) collective-permute-start(bf16[1024,128]{1,0:T(8,128)(2,1)S(1)} %add_after.6.refs_2_.own_ref), channel_id=1, source_target_pairs={{1,4},{3,6},{4,1},{6,3},{9,12},{11,14},{12,9},{14,11},{17,20},{19,... | collective-permute-start | bytes 786440 | tf_op jit(solution)/shard_map/ppermute | solution.py:405
  84.3 1.3 %collective-permute-done.23.rest_ref = f32[256,128]{1,0:T(8,128)S(1)} collective-permute-done((f32[256,128]{1,0:T(8,128)S(1)}, f32[256,128]{1,0:T(8,128)S(1)}, u32[]{:S(2)}, u32[]{:S(2)}) %collective-permute-start.23) | collective-permute-done | bytes 131104 | tf_op jit(solution)/shard_map/ppermute | solution.py:405
  85.6 1.0 %gather_halves.1 = (bf16[1024,256]{1,0:T(8,128)(2,1)}, f32[256,256]{1,0:T(8,128)}) custom-call(bf16[1024,128]{1,0:T(8,128)(2,1)S(1)} %get-tuple-element.33.own_ref, bf16[1024,128]{1,0:T(8,128)(2,1)S(1)} %collective-permute-done.17.refs_3_.one_ref, bf16[1024,128]{1,0:T(8,128)(2,1)S(1)} %collective-permute-done.18.refs_4_.two_ref, ...), custom_call_target="tpu_custom_call" | custom-call | tf_op jit(solution)/shard_map/gather_halves/pallas_call | solution.py:349
  86.7 3.0 %collective-permute-done.25.two_ref = bf16[1024,128]{1,0:T(8,128)(2,1)S(1)} collective-permute-done((bf16[1024,128]{1,0:T(8,128)(2,1)S(1)}, bf16[1024,128]{1,0:T(8,128)(2,1)S(1)}, u32[]{:S(2)}, u32[]{:S(2)}) %collective-permute-start.25) | collective-permute-done | bytes 262176 | tf_op jit(solution)/shard_map/ppermute | solution.py:405
  89.7 1.1 %final.1 = bf16[1024,256]{1,0:T(8,128)(2,1)} custom-call(bf16[1024,128]{1,0:T(8,128)(2,1)S(1)} %add_after.6.refs_2_.own_ref, bf16[1024,128]{1,0:T(8,128)(2,1)S(1)} %collective-permute-done.24.one_ref, bf16[1024,128]{1,0:T(8,128)(2,1)S(1)} %collective-permute-done.25.two_ref, bf16[256,256]{1,0:T(8,128)(2,1)S(1)} %copy-done.2), custom_call_target="tpu_custom_call" | custom-call | flops 134217728 | bytes 2097152 | tf_op jit(solution)/shard_map/final/pallas_call | solution.py:383
  (31 shorter events, 0.6 us)
Async XLA Ops:
  0.6 17.7 %collective-permute-start = (bf16[5,8,128,128]{3,2,1,0:T(8,128)(2,1)}, bf16[5,8,128,128]{3,2,1,0:T(8,128)(2,1)S(1)}, u32[]{:S(2)}, u32[]{:S(2)}) collective-permute-start(bf16[5,8,128,128]{3,2,1,0:T(8,128)(2,1)} %bitcast.5), channel_id=1, source_target_pairs={{0,4},{1,0},{2,6},{3,2},{4,5},{5,1},{6,7},{7,3},{8,12},{9,8},{10,1... | collective-permute-start | bytes 3932168 | tf_op jit(solution)/shard_map/ppermute | solution.py:405
  3.9 9.5 %collective-permute-start.2 = (bf16[1024,128]{1,0:T(8,128)(2,1)S(1)}, bf16[1024,128]{1,0:T(8,128)(2,1)S(1)}, u32[]{:S(2)}, u32[]{:S(2)}) collective-permute-start(bf16[1024,128]{1,0:T(8,128)(2,1)S(1)} %get-tuple-element.40.refs_3_.refs_2_.refs_5_.refs_4_.refs_7_), channel_id=1, source_target_pairs={{0,8},{1,17},{2,10},{3,19},{5,13},{7,15},{8,0},{10,2},{12,28},{13,... | collective-permute-start | bytes 786440 | tf_op jit(solution)/shard_map/ppermute | solution.py:405
  4.6 8.9 %collective-permute-start.3 = (bf16[1024,128]{1,0:T(8,128)(2,1)S(1)}, bf16[1024,128]{1,0:T(8,128)(2,1)S(1)}, u32[]{:S(2)}, u32[]{:S(2)}) collective-permute-start(bf16[1024,128]{1,0:T(8,128)(2,1)S(1)} %get-tuple-element.39), channel_id=1, source_target_pairs={{0,12},{1,21},{2,14},{3,23},{5,9},{7,11},{8,4},{10,6},{12,24},{13,... | collective-permute-start | bytes 786440 | tf_op jit(solution)/shard_map/ppermute | solution.py:405
  5.9 7.6 %collective-permute-start.4 = (bf16[1024,128]{1,0:T(8,128)(2,1)S(1)}, bf16[1024,128]{1,0:T(8,128)(2,1)S(1)}, u32[]{:S(2)}, u32[]{:S(2)}) collective-permute-start(bf16[1024,128]{1,0:T(8,128)(2,1)S(1)} %get-tuple-element.39), channel_id=1, source_target_pairs={{0,4},{1,5},{2,6},{3,7},{4,0},{5,1},{6,2},{7,3},{8,12},{9,13},{10,... | collective-permute-start | bytes 786440 | tf_op jit(solution)/shard_map/ppermute | solution.py:405
  11.3 0.7 copy-start.3
  13.6 7.9 %collective-permute-start.5 = (bf16[1024,128]{1,0:T(8,128)(2,1)S(1)}, bf16[1024,128]{1,0:T(8,128)(2,1)S(1)}, u32[]{:S(2)}, u32[]{:S(2)}) collective-permute-start(bf16[1024,128]{1,0:T(8,128)(2,1)S(1)} %get-tuple-element.22), channel_id=1, source_target_pairs={{0,16},{1,17},{2,18},{3,19},{4,20},{5,21},{6,22},{7,23},{8,24},{9,... | collective-permute-start | bytes 786440 | tf_op jit(solution)/shard_map/ppermute | solution.py:405
  15.4 9.7 %copy-start = (bf16[1,5,8,128,128]{4,3,2,1,0:T(8,128)(2,1)S(1)}, bf16[1,5,8,128,128]{4,3,2,1,0:T(8,128)(2,1)}, u32[]{:S(2)}) copy-start(bf16[1,5,8,128,128]{4,3,2,1,0:T(8,128)(2,1)} %param.9) | copy-start | bytes 3932164
  15.4 7.6 %collective-permute-start.8 = (bf16[1024,128]{1,0:T(8,128)(2,1)S(1)}, bf16[1024,128]{1,0:T(8,128)(2,1)S(1)}, u32[]{:S(2)}, u32[]{:S(2)}) collective-permute-start(bf16[1024,128]{1,0:T(8,128)(2,1)S(1)} %get-tuple-element.26), channel_id=1, source_target_pairs={{0,8},{1,9},{2,10},{3,11},{4,12},{5,13},{6,14},{7,15},{8,0},{9,1},... | collective-permute-start | bytes 786440 | tf_op jit(solution)/shard_map/ppermute | solution.py:405
  16.6 1.7 %collective-permute-start.1 = (s32[2,40]{1,0:T(2,128)S(1)}, s32[2,40]{1,0:T(2,128)S(1)}, u32[]{:S(2)}, u32[]{:S(2)}) collective-permute-start(s32[2,40]{1,0:T(2,128)S(1)} %slot_blocks.1.refs_6_.refs_0_.refs_1_), channel_id=1, source_target_pairs={{0,4},{1,0},{2,6},{3,2},{4,5},{5,1},{6,7},{7,3},{8,12},{9,8},{10,1... | collective-permute-start | bytes 968 | tf_op jit(solution)/shard_map/ppermute | solution.py:405
  18.3 6.7 %collective-permute-start.7 = (bf16[5,8,128,128]{3,2,1,0:T(8,128)(2,1)S(1)}, bf16[5,8,128,128]{3,2,1,0:T(8,128)(2,1)S(1)}, u32[]{:S(2)}, u32[]{:S(2)}) collective-permute-start(bf16[5,8,128,128]{3,2,1,0:T(8,128)(2,1)S(1)} %collective-permute-done.refs_1_.refs_3_), channel_id=1, source_target_pairs={{0,4},{2,6},{5,1},{7,3},{8,12},{10,14},{13,9},{15,11},{16,20},{18,... | collective-permute-start | bytes 3932168 | tf_op jit(solution)/shard_map/ppermute | solution.py:405
  21.5 3.6 %collective-permute-start.6 = (s32[2,40]{1,0:T(2,128)S(1)}, s32[2,40]{1,0:T(2,128)S(1)}, u32[]{:S(2)}, u32[]{:S(2)}) collective-permute-start(s32[2,40]{1,0:T(2,128)S(1)} %collective-permute-done.1.refs_0_), channel_id=1, source_target_pairs={{0,4},{2,6},{5,1},{7,3},{8,12},{10,14},{13,9},{15,11},{16,20},{18,... | collective-permute-start | bytes 968 | tf_op jit(solution)/shard_map/ppermute | solution.py:405
  24.3 4.6 %copy-start.1 = (bf16[1024,256]{1,0:T(8,128)(2,1)S(1)}, bf16[1024,256]{1,0:T(8,128)(2,1)}, u32[]{:S(2)}) copy-start(bf16[1024,256]{1,0:T(8,128)(2,1)} %x_ref.1) | copy-start | bytes 1572868
  26.5 16.6 %copy-start.2 = (bf16[256,256]{1,0:T(8,128)(2,1)S(1)}, bf16[256,256]{1,0:T(8,128)(2,1)}, u32[]{:S(2)}) copy-start(bf16[256,256]{1,0:T(8,128)(2,1)} %w_ref.3) | copy-start | bytes 393220
  26.5 14.1 %collective-permute-start.9 = (bf16[1024,128]{1,0:T(8,128)(2,1)S(1)}, bf16[1024,128]{1,0:T(8,128)(2,1)S(1)}, u32[]{:S(2)}, u32[]{:S(2)}) collective-permute-start(bf16[1024,128]{1,0:T(8,128)(2,1)S(1)} %tile_product.5), channel_id=1, source_target_pairs={{0,2},{1,3},{2,0},{3,1},{4,6},{5,7},{6,4},{7,5},{8,10},{9,11},{10,... | collective-permute-start | bytes 786440 | tf_op jit(solution)/shard_map/ppermute | solution.py:405
  29.0 12.9 %collective-permute-start.11 = (bf16[1024,128]{1,0:T(8,128)(2,1)S(1)}, bf16[1024,128]{1,0:T(8,128)(2,1)S(1)}, u32[]{:S(2)}, u32[]{:S(2)}) collective-permute-start(bf16[1024,128]{1,0:T(8,128)(2,1)S(1)} %get-tuple-element.28), channel_id=1, source_target_pairs={{0,4},{1,5},{2,6},{3,7},{4,0},{5,1},{6,2},{7,3},{8,12},{9,13},{10,... | collective-permute-start | bytes 786440 | tf_op jit(solution)/shard_map/ppermute | solution.py:405
  40.7 2.4 %collective-permute-start.10 = (bf16[1024,128]{1,0:T(8,128)(2,1)S(1)}, bf16[1024,128]{1,0:T(8,128)(2,1)S(1)}, u32[]{:S(2)}, u32[]{:S(2)}) collective-permute-start(bf16[1024,128]{1,0:T(8,128)(2,1)S(1)} %add_convert_fusion.near_ref), channel_id=1, source_target_pairs={{0,4},{1,5},{2,6},{3,7},{4,0},{5,1},{6,2},{7,3},{8,12},{9,13},{10,... | collective-permute-start | bytes 786440 | tf_op jit(solution)/shard_map/ppermute | solution.py:405
  43.5 10.4 %collective-permute-start.12 = (bf16[1056,128]{1,0:T(8,128)(2,1)S(1)}, bf16[1056,128]{1,0:T(8,128)(2,1)S(1)}, u32[]{:S(2)}, u32[]{:S(2)}) collective-permute-start(bf16[1056,128]{1,0:T(8,128)(2,1)S(1)} %get-tuple-element.30), channel_id=1, source_target_pairs={{0,8},{1,9},{2,10},{3,11},{4,12},{5,13},{6,14},{7,15},{8,0},{9,1},... | collective-permute-start | bytes 811016 | tf_op jit(solution)/shard_map/ppermute | solution.py:405
  45.3 7.3 %collective-permute-start.14 = (bf16[1040,128]{1,0:T(8,128)(2,1)S(1)}, bf16[1040,128]{1,0:T(8,128)(2,1)S(1)}, u32[]{:S(2)}, u32[]{:S(2)}) collective-permute-start(bf16[1040,128]{1,0:T(8,128)(2,1)S(1)} %get-tuple-element.31), channel_id=1, source_target_pairs={{0,17},{1,0},{2,19},{3,2},{4,21},{5,4},{6,23},{7,6},{8,9},{9,24},{... | collective-permute-start | bytes 798728 | tf_op jit(solution)/shard_map/ppermute | solution.py:405
  45.3 11.0 %collective-permute-start.16 = (bf16[1024,128]{1,0:T(8,128)(2,1)S(1)}, bf16[1024,128]{1,0:T(8,128)(2,1)S(1)}, u32[]{:S(2)}, u32[]{:S(2)}) collective-permute-start(bf16[1024,128]{1,0:T(8,128)(2,1)S(1)} %get-tuple-element.32.refs_6_.adj_ref), channel_id=1, source_target_pairs={{0,1},{2,3},{4,5},{6,7},{9,8},{11,10},{13,12},{15,14},{16,17},{18,... | collective-permute-start | bytes 786440 | tf_op jit(solution)/shard_map/ppermute | solution.py:405
  52.6 6.3 %collective-permute-start.15 = (bf16[1040,128]{1,0:T(8,128)(2,1)S(1)}, bf16[1040,128]{1,0:T(8,128)(2,1)S(1)}, u32[]{:S(2)}, u32[]{:S(2)}) collective-permute-start(bf16[1040,128]{1,0:T(8,128)(2,1)S(1)} %collective-permute-done.14.refs_8_), channel_id=1, source_target_pairs={{0,8},{1,9},{2,10},{3,11},{4,12},{5,13},{6,14},{7,15},{8,0},{9,1},... | collective-permute-start | bytes 798728 | tf_op jit(solution)/shard_map/ppermute | solution.py:405
  53.9 5.7 %collective-permute-start.13 = (bf16[1056,128]{1,0:T(8,128)(2,1)S(1)}, bf16[1056,128]{1,0:T(8,128)(2,1)S(1)}, u32[]{:S(2)}, u32[]{:S(2)}) collective-permute-start(bf16[1056,128]{1,0:T(8,128)(2,1)S(1)} %collective-permute-done.12.refs_7_), channel_id=1, source_target_pairs={{0,16},{1,17},{2,18},{3,19},{4,20},{5,21},{6,22},{7,23},{8,24},{9,... | collective-permute-start | bytes 811016 | tf_op jit(solution)/shard_map/ppermute | solution.py:405
  61.1 18.0 %collective-permute-start.22 = (bf16[1024,128]{1,0:T(8,128)(2,1)S(1)}, bf16[1024,128]{1,0:T(8,128)(2,1)S(1)}, u32[]{:S(2)}, u32[]{:S(2)}) collective-permute-start(bf16[1024,128]{1,0:T(8,128)(2,1)S(1)} %tile_product.7.refs_0_), channel_id=1, source_target_pairs={{0,2},{1,3},{2,0},{3,1},{4,6},{5,7},{6,4},{7,5},{8,10},{9,11},{10,... | collective-permute-start | bytes 786440 | tf_op jit(solution)/shard_map/ppermute | solution.py:405
  63.2 4.1 %collective-permute-start.19 = (bf16[256,128]{1,0:T(8,128)(2,1)S(1)}, bf16[256,128]{1,0:T(8,128)(2,1)S(1)}, u32[]{:S(2)}, u32[]{:S(2)}) collective-permute-start(bf16[256,128]{1,0:T(8,128)(2,1)S(1)} %grad_block.1.refs_0_), channel_id=1, source_target_pairs={{0,1},{1,0},{2,3},{3,2},{4,5},{5,4},{6,7},{7,6},{8,9},{9,8},{10,11... | collective-permute-start | bytes 196616 | tf_op jit(solution)/shard_map/ppermute | solution.py:405
  63.3 20.9 %collective-permute-start.17 = (bf16[1024,128]{1,0:T(8,128)(2,1)S(1)}, bf16[1024,128]{1,0:T(8,128)(2,1)S(1)}, u32[]{:S(2)}, u32[]{:S(2)}) collective-permute-start(bf16[1024,128]{1,0:T(8,128)(2,1)S(1)} %get-tuple-element.33.own_ref), channel_id=1, source_target_pairs={{0,1},{1,5},{2,3},{3,7},{4,0},{5,4},{6,2},{7,6},{8,9},{9,13},{10,1... | collective-permute-start | bytes 786440 | tf_op jit(solution)/shard_map/ppermute | solution.py:405
  67.4 8.5 %collective-permute-start.20 = (bf16[256,128]{1,0:T(8,128)(2,1)S(1)}, bf16[256,128]{1,0:T(8,128)(2,1)S(1)}, u32[]{:S(2)}, u32[]{:S(2)}) collective-permute-start(bf16[256,128]{1,0:T(8,128)(2,1)S(1)} %add_after.4.refs_0_), channel_id=1, source_target_pairs={{0,8},{1,9},{2,10},{3,11},{4,12},{5,13},{6,14},{7,15},{8,0},{9,1},... | collective-permute-start | bytes 196616 | tf_op jit(solution)/shard_map/ppermute | solution.py:405
  69.2 15.0 %collective-permute-start.18 = (bf16[1024,128]{1,0:T(8,128)(2,1)S(1)}, bf16[1024,128]{1,0:T(8,128)(2,1)S(1)}, u32[]{:S(2)}, u32[]{:S(2)}) collective-permute-start(bf16[1024,128]{1,0:T(8,128)(2,1)S(1)} %get-tuple-element.33.own_ref), channel_id=1, source_target_pairs={{1,4},{3,6},{4,1},{6,3},{9,12},{11,14},{12,9},{14,11},{17,20},{19,... | collective-permute-start | bytes 786440 | tf_op jit(solution)/shard_map/ppermute | solution.py:405
  75.9 3.2 %collective-permute-start.21 = (bf16[256,128]{1,0:T(8,128)(2,1)S(1)}, bf16[256,128]{1,0:T(8,128)(2,1)S(1)}, u32[]{:S(2)}, u32[]{:S(2)}) collective-permute-start(bf16[256,128]{1,0:T(8,128)(2,1)S(1)} %add_after.5.refs_0_), channel_id=1, source_target_pairs={{0,16},{1,17},{2,18},{3,19},{4,20},{5,21},{6,22},{7,23},{8,24},{9,... | collective-permute-start | bytes 196616 | tf_op jit(solution)/shard_map/ppermute | solution.py:405
  79.1 7.5 %collective-permute-start.24 = (bf16[1024,128]{1,0:T(8,128)(2,1)S(1)}, bf16[1024,128]{1,0:T(8,128)(2,1)S(1)}, u32[]{:S(2)}, u32[]{:S(2)}) collective-permute-start(bf16[1024,128]{1,0:T(8,128)(2,1)S(1)} %add_after.6.refs_2_.own_ref), channel_id=1, source_target_pairs={{0,1},{1,5},{2,3},{3,7},{4,0},{5,4},{6,2},{7,6},{8,9},{9,13},{10,1... | collective-permute-start | bytes 786440 | tf_op jit(solution)/shard_map/ppermute | solution.py:405
  82.0 7.7 %collective-permute-start.25 = (bf16[1024,128]{1,0:T(8,128)(2,1)S(1)}, bf16[1024,128]{1,0:T(8,128)(2,1)S(1)}, u32[]{:S(2)}, u32[]{:S(2)}) collective-permute-start(bf16[1024,128]{1,0:T(8,128)(2,1)S(1)} %add_after.6.refs_2_.own_ref), channel_id=1, source_target_pairs={{1,4},{3,6},{4,1},{6,3},{9,12},{11,14},{12,9},{14,11},{17,20},{19,... | collective-permute-start | bytes 786440 | tf_op jit(solution)/shard_map/ppermute | solution.py:405
  84.2 1.4 %collective-permute-start.23 = (f32[256,128]{1,0:T(8,128)S(1)}, f32[256,128]{1,0:T(8,128)S(1)}, u32[]{:S(2)}, u32[]{:S(2)}) collective-permute-start(f32[256,128]{1,0:T(8,128)S(1)} %add_after.7.grad_ref), channel_id=1, source_target_pairs={{0,4},{1,5},{2,6},{3,7},{4,0},{5,1},{6,2},{7,3},{8,12},{9,13},{10,... | collective-permute-start | bytes 393224 | tf_op jit(solution)/shard_map/ppermute | solution.py:405

commit v18 on v17

--- a/solution.py
+++ b/solution.py
@@ -507,7 +507,10 @@
     panels = [("self", [(None, adj)]), ("direct", [(None, direct)])]
     back_part = tile_product(panels, [set_first, set_rest], jnp.float32)
     panels = [("second", [(None, second)]), ("far", [(None, far)]), ("near", near_choice)]
-    back_part = tile_product(panels, [set_first, set_rest], jnp.bfloat16, back_part)
+    grad_got = send(grad, lambda c, j, z: (c, j, z ^ 1))
+    back_part = tile_product(
+        panels, [set_first, set_rest], jnp.bfloat16, back_part, [grad_got]
+    )
 
     def deliver(value):
         one = send(value, lambda c, j, z: (c, j, z ^ 1) if j == z % 2 else (c, 1 - j, z))
@@ -516,9 +519,7 @@
 
     act_later, back_part = lax.optimization_barrier((act, back_part))
     act_parts = [act, *deliver(act_later)]
-    grad, back_part = lax.optimization_barrier((grad, back_part))
-    grad_got = send(grad, lambda c, j, z: (c, j, z ^ 1))
-    grad = add_after([grad, grad_got], jnp.bfloat16)
+    grad = add_after([grad, grad_got], jnp.bfloat16, back_part)
     step = 1
     while step < shape[0]:
         got = send(grad, lambda c, j, z, s=step: (c ^ s, j, z))

time: 91.1 us -> 85.8 us (0.942)
  starting transfers between devices: 47.1 us -> 40.6 us
  waiting for transfers between devices: 30.5 us -> 31.7 us
    ppermute x26, starting transfers between devices: 47.1 us -> 40.6 us  [send(): return lax.ppermute(value, AXES, route(shape, move))]
    ppermute x26, waiting for transfers between devices: 30.5 us -> 31.7 us  [send(): return lax.ppermute(value, AXES, route(shape, move))]
  transfers between devices with their start and end apart: 26 -> 26, of which waited for: 14 -> 15; matrix products, arithmetic and copies ran while one was open for 2% -> 2% of each run, Pallas kernels for 6% -> 6%
where the time goes in v18:
time: 85.8 us; the launch traced here: 85.5 us
  starting transfers between devices  40.6 us (47%)
  waiting for transfers between devices  31.7 us (37%)
  Pallas kernels  9.85 us (11%)
  local copies, waits for them, and re-layouts  2.43 us (3%)
  between operations  0.87 us (1%)
    ppermute x26, starting transfers between devices, send(): return lax.ppermute(value, AXES, route(shape, move))  40.6 us
    ppermute x26, waiting for transfers between devices, send(): return lax.ppermute(value, AXES, route(shape, move))  31.7 us
    pallas_call x4, Pallas kernels, tile_product(): pl.pallas_call(functools.partial(tile_kernel, kinds, cases, [[case for ca...  5.3 us
  transfers between devices with their start and end apart: 26, of which 15 were waited for; matrix products, arithmetic and copies ran while one was open for 2% of the time, Pallas kernels for 6%

profile of v18, /device:TPU:1, one launch (start us, length us, event | category | flops | bytes accessed | tf_op | source)
XLA Modules:
  0.0 85.5 jit_solution(5859280441110808858)
XLA Ops:
  0.6 2.2 %collective-permute-start = (bf16[5,8,128,128]{3,2,1,0:T(8,128)(2,1)}, bf16[5,8,128,128]{3,2,1,0:T(8,128)(2,1)S(1)}, u32[]{:S(2)}, u32[]{:S(2)}) collective-permute-start(bf16[5,8,128,128]{3,2,1,0:T(8,128)(2,1)} %bitcast.5), channel_id=1, source_target_pairs={{0,4},{1,0},{2,6},{3,2},{4,5},{5,1},{6,7},{7,3},{8,12},{9,8},{10,1... | collective-permute-start | bytes 3932168 | tf_op jit(solution)/shard_map/ppermute | solution.py:405
  2.8 1.1 %constant_dynamic-slice_fusion = (bf16[1024,128]{1,0:T(8,128)(2,1)S(1)}, bf16[1024,128]{1,0:T(8,128)(2,1)S(1)}) fusion(bf16[1024,256]{1,0:T(8,128)(2,1)} %param.6, s32[]{:T(128)S(6)} %select_n.15, s32[]{:T(128)S(6)} %select_n.14), kind=kLoop, calls=%fused_computation.2 | loop fusion | bytes 1048584 | tf_op jit(solution)/shard_map/dynamic_slice | solution.py:445
  3.9 0.7 collective-permute-start.2
  4.6 1.3 %collective-permute-start.3 = (bf16[1024,128]{1,0:T(8,128)(2,1)S(1)}, bf16[1024,128]{1,0:T(8,128)(2,1)S(1)}, u32[]{:S(2)}, u32[]{:S(2)}) collective-permute-start(bf16[1024,128]{1,0:T(8,128)(2,1)S(1)} %get-tuple-element.35), channel_id=1, source_target_pairs={{0,12},{1,21},{2,14},{3,23},{5,9},{7,11},{8,4},{10,6},{12,24},{13,... | collective-permute-start | bytes 786440 | tf_op jit(solution)/shard_map/ppermute | solution.py:405
  5.9 4.8 %collective-permute-start.4 = (bf16[1024,128]{1,0:T(8,128)(2,1)S(1)}, bf16[1024,128]{1,0:T(8,128)(2,1)S(1)}, u32[]{:S(2)}, u32[]{:S(2)}) collective-permute-start(bf16[1024,128]{1,0:T(8,128)(2,1)S(1)} %get-tuple-element.35), channel_id=1, source_target_pairs={{0,4},{1,5},{2,6},{3,7},{4,0},{5,1},{6,2},{7,3},{8,12},{9,13},{10,... | collective-permute-start | bytes 786440 | tf_op jit(solution)/shard_map/ppermute | solution.py:405
  10.6 0.7 copy.12
  11.3 0.7 copy-done.3
  12.0 1.3 %slot_blocks.1.refs_6_.refs_0_.refs_1_ = s32[2,40]{1,0:T(2,128)S(1)} custom-call(s32[2,5,8]{2,1,0:T(8,128)S(1)} %copy.10.coords_ref, s32[5]{0:T(128)S(1)} %bitcast.9), custom_call_target="tpu_custom_call" | custom-call | tf_op jit(solution)/shard_map/slot_blocks/pallas_call | solution.py:135
  13.6 1.8 %collective-permute-start.5 = (bf16[1024,128]{1,0:T(8,128)(2,1)S(1)}, bf16[1024,128]{1,0:T(8,128)(2,1)S(1)}, u32[]{:S(2)}, u32[]{:S(2)}) collective-permute-start(bf16[1024,128]{1,0:T(8,128)(2,1)S(1)} %get-tuple-element.20), channel_id=1, source_target_pairs={{0,16},{1,17},{2,18},{3,19},{4,20},{5,21},{6,22},{7,23},{8,24},{9,... | collective-permute-start | bytes 786440 | tf_op jit(solution)/shard_map/ppermute | solution.py:405
  15.4 1.2 %collective-permute-start.8 = (bf16[1024,128]{1,0:T(8,128)(2,1)S(1)}, bf16[1024,128]{1,0:T(8,128)(2,1)S(1)}, u32[]{:S(2)}, u32[]{:S(2)}) collective-permute-start(bf16[1024,128]{1,0:T(8,128)(2,1)S(1)} %get-tuple-element.24), channel_id=1, source_target_pairs={{0,8},{1,9},{2,10},{3,11},{4,12},{5,13},{6,14},{7,15},{8,0},{9,1},... | collective-permute-start | bytes 786440 | tf_op jit(solution)/shard_map/ppermute | solution.py:405
  16.8 1.5 %collective-permute-done.1.refs_0_ = s32[2,40]{1,0:T(2,128)S(1)} collective-permute-done((s32[2,40]{1,0:T(2,128)S(1)}, s32[2,40]{1,0:T(2,128)S(1)}, u32[]{:S(2)}, u32[]{:S(2)}) %collective-permute-start.1) | collective-permute-done | bytes 352 | tf_op jit(solution)/shard_map/ppermute | solution.py:405
  18.3 1.3 %collective-permute-start.7 = (bf16[5,8,128,128]{3,2,1,0:T(8,128)(2,1)S(1)}, bf16[5,8,128,128]{3,2,1,0:T(8,128)(2,1)S(1)}, u32[]{:S(2)}, u32[]{:S(2)}) collective-permute-start(bf16[5,8,128,128]{3,2,1,0:T(8,128)(2,1)S(1)} %collective-permute-done.refs_1_.refs_3_), channel_id=1, source_target_pairs={{0,4},{2,6},{5,1},{7,3},{8,12},{10,14},{13,9},{15,11},{16,20},{18,... | collective-permute-start | bytes 3932168 | tf_op jit(solution)/shard_map/ppermute | solution.py:405
  19.6 1.9 %collective-permute-done.5.refs_8_.refs_10_ = bf16[1024,128]{1,0:T(8,128)(2,1)S(1)} collective-permute-done((bf16[1024,128]{1,0:T(8,128)(2,1)S(1)}, bf16[1024,128]{1,0:T(8,128)(2,1)S(1)}, u32[]{:S(2)}, u32[]{:S(2)}) %collective-permute-start.5) | collective-permute-done | bytes 262176 | tf_op jit(solution)/shard_map/ppermute | solution.py:405
  21.5 1.3 %collective-permute-start.6 = (s32[2,40]{1,0:T(2,128)S(1)}, s32[2,40]{1,0:T(2,128)S(1)}, u32[]{:S(2)}, u32[]{:S(2)}) collective-permute-start(s32[2,40]{1,0:T(2,128)S(1)} %collective-permute-done.1.refs_0_), channel_id=1, source_target_pairs={{0,4},{2,6},{5,1},{7,3},{8,12},{10,14},{13,9},{15,11},{16,20},{18,... | collective-permute-start | bytes 968 | tf_op jit(solution)/shard_map/ppermute | solution.py:405
  22.8 0.3 collective-permute-done.8.refs_9_.refs_11_
  23.0 1.2 %tile_product.4.refs_12_ = f32[1024,128]{1,0:T(8,128)S(1)} custom-call(s32[2,40]{1,0:T(2,128)S(1)} %collective-permute-done.1.refs_0_, bf16[5,8,128,128]{3,2,1,0:T(8,128)(2,1)S(1)} %collective-permute-done.refs_1_.refs_3_, bf16[1024,128]{1,0:T(8,128)(2,1)S(1)} %get-tuple-element.36.refs_3_.refs_2_.refs_5_.refs_4_.refs_7_, ...), custom_call_target="tpu_custom_call" | custom-call | flops 12582912000 | bytes 196608000 | tf_op jit(solution)/shard_map/tile_product/pallas_call | solution.py:210
  24.3 0.8 collective-permute-done.6.refs_1_.refs_2_
  25.0 1.4 %tile_product.5 = bf16[1024,128]{1,0:T(8,128)(2,1)S(1)} custom-call(s32[2,40]{1,0:T(2,128)S(1)} %slot_blocks.1.refs_6_.refs_0_.refs_1_, s32[2,40]{1,0:T(2,128)S(1)} %collective-permute-done.6.refs_1_.refs_2_, bf16[5,8,128,128]{3,2,1,0:T(8,128)(2,1)S(1)} %bitcast.6, bf16[5,8,128,128]{3,2,1,0:T(8,128)(2,1)S(1)} %collective-permute-done.7.refs_3_.refs_5_, ...), custom_call_target="tpu_custom_call" | custom-call | flops 167772160 | bytes 2621440 | tf_op jit(solution)/shard_map/tile_product/pallas_call | solution.py:210
  26.5 2.4 %collective-permute-start.9 = (bf16[1024,128]{1,0:T(8,128)(2,1)S(1)}, bf16[1024,128]{1,0:T(8,128)(2,1)S(1)}, u32[]{:S(2)}, u32[]{:S(2)}) collective-permute-start(bf16[1024,128]{1,0:T(8,128)(2,1)S(1)} %tile_product.5), channel_id=1, source_target_pairs={{0,2},{1,3},{2,0},{3,1},{4,6},{5,7},{6,4},{7,5},{8,10},{9,11},{10,... | collective-permute-start | bytes 786440 | tf_op jit(solution)/shard_map/ppermute | solution.py:405
  29.0 0.8 collective-permute-start.11
  29.7 10.9 %collective-permute-done.9 = bf16[1024,128]{1,0:T(8,128)(2,1)S(1)} collective-permute-done((bf16[1024,128]{1,0:T(8,128)(2,1)S(1)}, bf16[1024,128]{1,0:T(8,128)(2,1)S(1)}, u32[]{:S(2)}, u32[]{:S(2)}) %collective-permute-start.9) | collective-permute-done | bytes 262176 | tf_op jit(solution)/shard_map/ppermute | solution.py:405
  40.7 1.2 %collective-permute-start.10 = (bf16[1024,128]{1,0:T(8,128)(2,1)S(1)}, bf16[1024,128]{1,0:T(8,128)(2,1)S(1)}, u32[]{:S(2)}, u32[]{:S(2)}) collective-permute-start(bf16[1024,128]{1,0:T(8,128)(2,1)S(1)} %add_convert_fusion.near_ref), channel_id=1, source_target_pairs={{0,4},{1,5},{2,6},{3,7},{4,0},{5,1},{6,2},{7,3},{8,12},{9,13},{10,... | collective-permute-start | bytes 786440 | tf_op jit(solution)/shard_map/ppermute | solution.py:405
  41.9 1.2 %collective-permute-done.10.far_ref = bf16[1024,128]{1,0:T(8,128)(2,1)S(1)} collective-permute-done((bf16[1024,128]{1,0:T(8,128)(2,1)S(1)}, bf16[1024,128]{1,0:T(8,128)(2,1)S(1)}, u32[]{:S(2)}, u32[]{:S(2)}) %collective-permute-start.10) | collective-permute-done | bytes 262176 | tf_op jit(solution)/shard_map/ppermute | solution.py:405
  43.1 0.4 middle.1
  43.5 1.8 %collective-permute-start.12 = (bf16[1056,128]{1,0:T(8,128)(2,1)S(1)}, bf16[1056,128]{1,0:T(8,128)(2,1)S(1)}, u32[]{:S(2)}, u32[]{:S(2)}) collective-permute-start(bf16[1056,128]{1,0:T(8,128)(2,1)S(1)} %get-tuple-element.28), channel_id=1, source_target_pairs={{0,8},{1,9},{2,10},{3,11},{4,12},{5,13},{6,14},{7,15},{8,0},{9,1},... | collective-permute-start | bytes 811016 | tf_op jit(solution)/shard_map/ppermute | solution.py:405
  45.3 3.4 %collective-permute-start.16 = (bf16[1024,128]{1,0:T(8,128)(2,1)S(1)}, bf16[1024,128]{1,0:T(8,128)(2,1)S(1)}, u32[]{:S(2)}, u32[]{:S(2)}) collective-permute-start(bf16[1024,128]{1,0:T(8,128)(2,1)S(1)} %get-tuple-element.30.refs_6_.adj_ref), channel_id=1, source_target_pairs={{0,1},{2,3},{4,5},{6,7},{9,8},{11,10},{13,12},{15,14},{16,17},{18,... | collective-permute-start | bytes 786440 | tf_op jit(solution)/shard_map/ppermute | solution.py:405
  48.7 3.9 %collective-permute-done.14.refs_8_ = bf16[1040,128]{1,0:T(8,128)(2,1)S(1)} collective-permute-done((bf16[1040,128]{1,0:T(8,128)(2,1)S(1)}, bf16[1040,128]{1,0:T(8,128)(2,1)S(1)}, u32[]{:S(2)}, u32[]{:S(2)}) %collective-permute-start.14) | collective-permute-done | bytes 266272 | tf_op jit(solution)/shard_map/ppermute | solution.py:405
  52.6 1.3 %collective-permute-start.15 = (bf16[1040,128]{1,0:T(8,128)(2,1)S(1)}, bf16[1040,128]{1,0:T(8,128)(2,1)S(1)}, u32[]{:S(2)}, u32[]{:S(2)}) collective-permute-start(bf16[1040,128]{1,0:T(8,128)(2,1)S(1)} %collective-permute-done.14.refs_8_), channel_id=1, source_target_pairs={{0,8},{1,9},{2,10},{3,11},{4,12},{5,13},{6,14},{7,15},{8,0},{9,1},... | collective-permute-start | bytes 798728 | tf_op jit(solution)/shard_map/ppermute | solution.py:405
  53.9 0.9 %collective-permute-start.13 = (bf16[1056,128]{1,0:T(8,128)(2,1)S(1)}, bf16[1056,128]{1,0:T(8,128)(2,1)S(1)}, u32[]{:S(2)}, u32[]{:S(2)}) collective-permute-start(bf16[1056,128]{1,0:T(8,128)(2,1)S(1)} %collective-permute-done.12.refs_7_), channel_id=1, source_target_pairs={{0,16},{1,17},{2,18},{3,19},{4,20},{5,21},{6,22},{7,23},{8,24},{9,... | collective-permute-start | bytes 811016 | tf_op jit(solution)/shard_map/ppermute | solution.py:405
  54.8 0.3 grad_block.1.refs_0_
  55.2 1.2 %tile_product.6.refs_10_ = f32[1024,128]{1,0:T(8,128)S(1)} custom-call(s32[2,40]{1,0:T(2,128)S(1)} %collective-permute-done.1.refs_0_, s32[2,40]{1,0:T(2,128)S(1)} %slot_blocks.1.refs_6_.refs_0_.refs_1_, s32[2,40]{1,0:T(2,128)S(1)} %collective-permute-done.6.refs_1_.refs_2_, bf16[5,8,128,128]{3,2,1,0:T(8,128)(2,1)S(1)} %collective-permute-done.refs_1_.refs_3_, ...), custom_call_target="tpu_custom_call" | custom-call | flops 134217728 | bytes 1572864 | tf_op jit(solution)/shard_map/tile_product/pallas_call | solution.py:210
  56.3 2.2 %collective-permute-done.17.refs_11_.refs_1_ = bf16[256,128]{1,0:T(8,128)(2,1)S(1)} collective-permute-done((bf16[256,128]{1,0:T(8,128)(2,1)S(1)}, bf16[256,128]{1,0:T(8,128)(2,1)S(1)}, u32[]{:S(2)}, u32[]{:S(2)}) %collective-permute-start.17) | collective-permute-done | bytes 65568 | tf_op jit(solution)/shard_map/ppermute | solution.py:405
  58.6 0.3 collective-permute-done.15.refs_7_
  58.9 0.6 collective-permute-done.13.refs_6_
  59.6 1.5 %tile_product.7.refs_2_.refs_0_ = bf16[1024,128]{1,0:T(8,128)(2,1)S(1)} custom-call(s32[2,40]{1,0:T(2,128)S(1)} %collective-permute-done.1.refs_0_, s32[2,40]{1,0:T(2,128)S(1)} %slot_blocks.1.refs_6_.refs_0_.refs_1_, s32[2,40]{1,0:T(2,128)S(1)} %collective-permute-done.6.refs_1_.refs_2_, bf16[5,8,128,128]{3,2,1,0:T(8,128)(2,1)S(1)} %collective-permute-done.refs_1_.refs_3_, ...), custom_call_target="tpu_custom_call" | custom-call | flops 201326592 | bytes 2359296 | tf_op jit(solution)/shard_map/tile_product/pallas_call | solution.py:210
  61.1 2.1 %collective-permute-start.22 = (bf16[1024,128]{1,0:T(8,128)(2,1)S(1)}, bf16[1024,128]{1,0:T(8,128)(2,1)S(1)}, u32[]{:S(2)}, u32[]{:S(2)}) collective-permute-start(bf16[1024,128]{1,0:T(8,128)(2,1)S(1)} %tile_product.7.refs_2_.refs_0_), channel_id=1, source_target_pairs={{0,2},{1,3},{2,0},{3,1},{4,6},{5,7},{6,4},{7,5},{8,10},{9,11},{10,... | collective-permute-start | bytes 786440 | tf_op jit(solution)/shard_map/ppermute | solution.py:405
  63.2 0.3 collective-permute-start.20
  63.6 3.5 %collective-permute-start.18 = (bf16[1024,128]{1,0:T(8,128)(2,1)S(1)}, bf16[1024,128]{1,0:T(8,128)(2,1)S(1)}, u32[]{:S(2)}, u32[]{:S(2)}) collective-permute-start(bf16[1024,128]{1,0:T(8,128)(2,1)S(1)} %get-tuple-element.31.own_ref), channel_id=1, source_target_pairs={{0,1},{1,5},{2,3},{3,7},{4,0},{5,4},{6,2},{7,6},{8,9},{9,13},{10,1... | collective-permute-start | bytes 786440 | tf_op jit(solution)/shard_map/ppermute | solution.py:405
  67.1 3.9 %collective-permute-start.19 = (bf16[1024,128]{1,0:T(8,128)(2,1)S(1)}, bf16[1024,128]{1,0:T(8,128)(2,1)S(1)}, u32[]{:S(2)}, u32[]{:S(2)}) collective-permute-start(bf16[1024,128]{1,0:T(8,128)(2,1)S(1)} %get-tuple-element.31.own_ref), channel_id=1, source_target_pairs={{1,4},{3,6},{4,1},{6,3},{9,12},{11,14},{12,9},{14,11},{17,20},{19,... | collective-permute-start | bytes 786440 | tf_op jit(solution)/shard_map/ppermute | solution.py:405
  71.0 0.7 collective-permute-start.21
  71.7 3.0 %collective-permute-done.21.refs_2_.refs_1_ = bf16[256,128]{1,0:T(8,128)(2,1)S(1)} collective-permute-done((bf16[256,128]{1,0:T(8,128)(2,1)S(1)}, bf16[256,128]{1,0:T(8,128)(2,1)S(1)}, u32[]{:S(2)}, u32[]{:S(2)}) %collective-permute-start.21) | collective-permute-done | bytes 65568 | tf_op jit(solution)/shard_map/ppermute | solution.py:405
  74.7 0.3 collective-permute-done.22.refs_1_
  75.1 1.5 %collective-permute-start.24 = (bf16[1024,128]{1,0:T(8,128)(2,1)S(1)}, bf16[1024,128]{1,0:T(8,128)(2,1)S(1)}, u32[]{:S(2)}, u32[]{:S(2)}) collective-permute-start(bf16[1024,128]{1,0:T(8,128)(2,1)S(1)} %add_after.6.refs_2_.own_ref), channel_id=1, source_target_pairs={{0,1},{1,5},{2,3},{3,7},{4,0},{5,4},{6,2},{7,6},{8,9},{9,13},{10,1... | collective-permute-start | bytes 786440 | tf_op jit(solution)/shard_map/ppermute | solution.py:405
  76.6 1.9 %collective-permute-start.25 = (bf16[1024,128]{1,0:T(8,128)(2,1)S(1)}, bf16[1024,128]{1,0:T(8,128)(2,1)S(1)}, u32[]{:S(2)}, u32[]{:S(2)}) collective-permute-start(bf16[1024,128]{1,0:T(8,128)(2,1)S(1)} %add_after.6.refs_2_.own_ref), channel_id=1, source_target_pairs={{1,4},{3,6},{4,1},{6,3},{9,12},{11,14},{12,9},{14,11},{17,20},{19,... | collective-permute-start | bytes 786440 | tf_op jit(solution)/shard_map/ppermute | solution.py:405
  78.7 1.3 %collective-permute-done.23.rest_ref = f32[256,128]{1,0:T(8,128)S(1)} collective-permute-done((f32[256,128]{1,0:T(8,128)S(1)}, f32[256,128]{1,0:T(8,128)S(1)}, u32[]{:S(2)}, u32[]{:S(2)}) %collective-permute-start.23) | collective-permute-done | bytes 131104 | tf_op jit(solution)/shard_map/ppermute | solution.py:405
  80.0 1.0 %gather_halves.1 = (bf16[1024,256]{1,0:T(8,128)(2,1)}, f32[256,256]{1,0:T(8,128)}) custom-call(bf16[1024,128]{1,0:T(8,128)(2,1)S(1)} %get-tuple-element.31.own_ref, bf16[1024,128]{1,0:T(8,128)(2,1)S(1)} %collective-permute-done.18.refs_3_.one_ref, bf16[1024,128]{1,0:T(8,128)(2,1)S(1)} %collective-permute-done.19.refs_4_.two_ref, ...), custom_call_target="tpu_custom_call" | custom-call | tf_op jit(solution)/shard_map/gather_halves/pallas_call | solution.py:349
  81.0 3.3 %collective-permute-done.25.two_ref = bf16[1024,128]{1,0:T(8,128)(2,1)S(1)} collective-permute-done((bf16[1024,128]{1,0:T(8,128)(2,1)S(1)}, bf16[1024,128]{1,0:T(8,128)(2,1)S(1)}, u32[]{:S(2)}, u32[]{:S(2)}) %collective-permute-start.25) | collective-permute-done | bytes 262176 | tf_op jit(solution)/shard_map/ppermute | solution.py:405
  84.3 1.2 %final.1 = bf16[1024,256]{1,0:T(8,128)(2,1)} custom-call(bf16[1024,128]{1,0:T(8,128)(2,1)S(1)} %add_after.6.refs_2_.own_ref, bf16[1024,128]{1,0:T(8,128)(2,1)S(1)} %collective-permute-done.24.one_ref, bf16[1024,128]{1,0:T(8,128)(2,1)S(1)} %collective-permute-done.25.two_ref, bf16[256,256]{1,0:T(8,128)(2,1)S(1)} %copy-done.2), custom_call_target="tpu_custom_call" | custom-call | flops 134217728 | bytes 2097152 | tf_op jit(solution)/shard_map/final/pallas_call | solution.py:383
  (31 shorter events, 0.9 us)
Async XLA Ops:
  0.6 17.7 %collective-permute-start = (bf16[5,8,128,128]{3,2,1,0:T(8,128)(2,1)}, bf16[5,8,128,128]{3,2,1,0:T(8,128)(2,1)S(1)}, u32[]{:S(2)}, u32[]{:S(2)}) collective-permute-start(bf16[5,8,128,128]{3,2,1,0:T(8,128)(2,1)} %bitcast.5), channel_id=1, source_target_pairs={{0,4},{1,0},{2,6},{3,2},{4,5},{5,1},{6,7},{7,3},{8,12},{9,8},{10,1... | collective-permute-start | bytes 3932168 | tf_op jit(solution)/shard_map/ppermute | solution.py:405
  3.9 9.5 %collective-permute-start.2 = (bf16[1024,128]{1,0:T(8,128)(2,1)S(1)}, bf16[1024,128]{1,0:T(8,128)(2,1)S(1)}, u32[]{:S(2)}, u32[]{:S(2)}) collective-permute-start(bf16[1024,128]{1,0:T(8,128)(2,1)S(1)} %get-tuple-element.36.refs_3_.refs_2_.refs_5_.refs_4_.refs_7_), channel_id=1, source_target_pairs={{0,8},{1,17},{2,10},{3,19},{5,13},{7,15},{8,0},{10,2},{12,28},{13,... | collective-permute-start | bytes 786440 | tf_op jit(solution)/shard_map/ppermute | solution.py:405
  4.6 8.9 %collective-permute-start.3 = (bf16[1024,128]{1,0:T(8,128)(2,1)S(1)}, bf16[1024,128]{1,0:T(8,128)(2,1)S(1)}, u32[]{:S(2)}, u32[]{:S(2)}) collective-permute-start(bf16[1024,128]{1,0:T(8,128)(2,1)S(1)} %get-tuple-element.35), channel_id=1, source_target_pairs={{0,12},{1,21},{2,14},{3,23},{5,9},{7,11},{8,4},{10,6},{12,24},{13,... | collective-permute-start | bytes 786440 | tf_op jit(solution)/shard_map/ppermute | solution.py:405
  5.9 7.6 %collective-permute-start.4 = (bf16[1024,128]{1,0:T(8,128)(2,1)S(1)}, bf16[1024,128]{1,0:T(8,128)(2,1)S(1)}, u32[]{:S(2)}, u32[]{:S(2)}) collective-permute-start(bf16[1024,128]{1,0:T(8,128)(2,1)S(1)} %get-tuple-element.35), channel_id=1, source_target_pairs={{0,4},{1,5},{2,6},{3,7},{4,0},{5,1},{6,2},{7,3},{8,12},{9,13},{10,... | collective-permute-start | bytes 786440 | tf_op jit(solution)/shard_map/ppermute | solution.py:405
  11.3 0.7 copy-start.3
  13.6 7.9 %collective-permute-start.5 = (bf16[1024,128]{1,0:T(8,128)(2,1)S(1)}, bf16[1024,128]{1,0:T(8,128)(2,1)S(1)}, u32[]{:S(2)}, u32[]{:S(2)}) collective-permute-start(bf16[1024,128]{1,0:T(8,128)(2,1)S(1)} %get-tuple-element.20), channel_id=1, source_target_pairs={{0,16},{1,17},{2,18},{3,19},{4,20},{5,21},{6,22},{7,23},{8,24},{9,... | collective-permute-start | bytes 786440 | tf_op jit(solution)/shard_map/ppermute | solution.py:405
  15.4 9.7 %copy-start = (bf16[1,5,8,128,128]{4,3,2,1,0:T(8,128)(2,1)S(1)}, bf16[1,5,8,128,128]{4,3,2,1,0:T(8,128)(2,1)}, u32[]{:S(2)}) copy-start(bf16[1,5,8,128,128]{4,3,2,1,0:T(8,128)(2,1)} %param.9) | copy-start | bytes 3932164
  15.4 7.6 %collective-permute-start.8 = (bf16[1024,128]{1,0:T(8,128)(2,1)S(1)}, bf16[1024,128]{1,0:T(8,128)(2,1)S(1)}, u32[]{:S(2)}, u32[]{:S(2)}) collective-permute-start(bf16[1024,128]{1,0:T(8,128)(2,1)S(1)} %get-tuple-element.24), channel_id=1, source_target_pairs={{0,8},{1,9},{2,10},{3,11},{4,12},{5,13},{6,14},{7,15},{8,0},{9,1},... | collective-permute-start | bytes 786440 | tf_op jit(solution)/shard_map/ppermute | solution.py:405
  16.6 1.7 %collective-permute-start.1 = (s32[2,40]{1,0:T(2,128)S(1)}, s32[2,40]{1,0:T(2,128)S(1)}, u32[]{:S(2)}, u32[]{:S(2)}) collective-permute-start(s32[2,40]{1,0:T(2,128)S(1)} %slot_blocks.1.refs_6_.refs_0_.refs_1_), channel_id=1, source_target_pairs={{0,4},{1,0},{2,6},{3,2},{4,5},{5,1},{6,7},{7,3},{8,12},{9,8},{10,1... | collective-permute-start | bytes 968 | tf_op jit(solution)/shard_map/ppermute | solution.py:405
  18.3 6.7 %collective-permute-start.7 = (bf16[5,8,128,128]{3,2,1,0:T(8,128)(2,1)S(1)}, bf16[5,8,128,128]{3,2,1,0:T(8,128)(2,1)S(1)}, u32[]{:S(2)}, u32[]{:S(2)}) collective-permute-start(bf16[5,8,128,128]{3,2,1,0:T(8,128)(2,1)S(1)} %collective-permute-done.refs_1_.refs_3_), channel_id=1, source_target_pairs={{0,4},{2,6},{5,1},{7,3},{8,12},{10,14},{13,9},{15,11},{16,20},{18,... | collective-permute-start | bytes 3932168 | tf_op jit(solution)/shard_map/ppermute | solution.py:405
  21.5 3.6 %collective-permute-start.6 = (s32[2,40]{1,0:T(2,128)S(1)}, s32[2,40]{1,0:T(2,128)S(1)}, u32[]{:S(2)}, u32[]{:S(2)}) collective-permute-start(s32[2,40]{1,0:T(2,128)S(1)} %collective-permute-done.1.refs_0_), channel_id=1, source_target_pairs={{0,4},{2,6},{5,1},{7,3},{8,12},{10,14},{13,9},{15,11},{16,20},{18,... | collective-permute-start | bytes 968 | tf_op jit(solution)/shard_map/ppermute | solution.py:405
  24.3 4.6 %copy-start.1 = (bf16[1024,256]{1,0:T(8,128)(2,1)S(1)}, bf16[1024,256]{1,0:T(8,128)(2,1)}, u32[]{:S(2)}) copy-start(bf16[1024,256]{1,0:T(8,128)(2,1)} %x_ref.1) | copy-start | bytes 1572868
  26.5 16.6 %copy-start.2 = (bf16[256,256]{1,0:T(8,128)(2,1)S(1)}, bf16[256,256]{1,0:T(8,128)(2,1)}, u32[]{:S(2)}) copy-start(bf16[256,256]{1,0:T(8,128)(2,1)} %w_ref.3) | copy-start | bytes 393220
  26.5 14.1 %collective-permute-start.9 = (bf16[1024,128]{1,0:T(8,128)(2,1)S(1)}, bf16[1024,128]{1,0:T(8,128)(2,1)S(1)}, u32[]{:S(2)}, u32[]{:S(2)}) collective-permute-start(bf16[1024,128]{1,0:T(8,128)(2,1)S(1)} %tile_product.5), channel_id=1, source_target_pairs={{0,2},{1,3},{2,0},{3,1},{4,6},{5,7},{6,4},{7,5},{8,10},{9,11},{10,... | collective-permute-start | bytes 786440 | tf_op jit(solution)/shard_map/ppermute | solution.py:405
  29.0 12.9 %collective-permute-start.11 = (bf16[1024,128]{1,0:T(8,128)(2,1)S(1)}, bf16[1024,128]{1,0:T(8,128)(2,1)S(1)}, u32[]{:S(2)}, u32[]{:S(2)}) collective-permute-start(bf16[1024,128]{1,0:T(8,128)(2,1)S(1)} %get-tuple-element.26), channel_id=1, source_target_pairs={{0,4},{1,5},{2,6},{3,7},{4,0},{5,1},{6,2},{7,3},{8,12},{9,13},{10,... | collective-permute-start | bytes 786440 | tf_op jit(solution)/shard_map/ppermute | solution.py:405
  40.7 2.4 %collective-permute-start.10 = (bf16[1024,128]{1,0:T(8,128)(2,1)S(1)}, bf16[1024,128]{1,0:T(8,128)(2,1)S(1)}, u32[]{:S(2)}, u32[]{:S(2)}) collective-permute-start(bf16[1024,128]{1,0:T(8,128)(2,1)S(1)} %add_convert_fusion.near_ref), channel_id=1, source_target_pairs={{0,4},{1,5},{2,6},{3,7},{4,0},{5,1},{6,2},{7,3},{8,12},{9,13},{10,... | collective-permute-start | bytes 786440 | tf_op jit(solution)/shard_map/ppermute | solution.py:405
  43.5 10.4 %collective-permute-start.12 = (bf16[1056,128]{1,0:T(8,128)(2,1)S(1)}, bf16[1056,128]{1,0:T(8,128)(2,1)S(1)}, u32[]{:S(2)}, u32[]{:S(2)}) collective-permute-start(bf16[1056,128]{1,0:T(8,128)(2,1)S(1)} %get-tuple-element.28), channel_id=1, source_target_pairs={{0,8},{1,9},{2,10},{3,11},{4,12},{5,13},{6,14},{7,15},{8,0},{9,1},... | collective-permute-start | bytes 811016 | tf_op jit(solution)/shard_map/ppermute | solution.py:405
  45.3 7.3 %collective-permute-start.14 = (bf16[1040,128]{1,0:T(8,128)(2,1)S(1)}, bf16[1040,128]{1,0:T(8,128)(2,1)S(1)}, u32[]{:S(2)}, u32[]{:S(2)}) collective-permute-start(bf16[1040,128]{1,0:T(8,128)(2,1)S(1)} %get-tuple-element.29), channel_id=1, source_target_pairs={{0,17},{1,0},{2,19},{3,2},{4,21},{5,4},{6,23},{7,6},{8,9},{9,24},{... | collective-permute-start | bytes 798728 | tf_op jit(solution)/shard_map/ppermute | solution.py:405
  45.3 13.3 %collective-permute-start.16 = (bf16[1024,128]{1,0:T(8,128)(2,1)S(1)}, bf16[1024,128]{1,0:T(8,128)(2,1)S(1)}, u32[]{:S(2)}, u32[]{:S(2)}) collective-permute-start(bf16[1024,128]{1,0:T(8,128)(2,1)S(1)} %get-tuple-element.30.refs_6_.adj_ref), channel_id=1, source_target_pairs={{0,1},{2,3},{4,5},{6,7},{9,8},{11,10},{13,12},{15,14},{16,17},{18,... | collective-permute-start | bytes 786440 | tf_op jit(solution)/shard_map/ppermute | solution.py:405
  52.6 6.3 %collective-permute-start.15 = (bf16[1040,128]{1,0:T(8,128)(2,1)S(1)}, bf16[1040,128]{1,0:T(8,128)(2,1)S(1)}, u32[]{:S(2)}, u32[]{:S(2)}) collective-permute-start(bf16[1040,128]{1,0:T(8,128)(2,1)S(1)} %collective-permute-done.14.refs_8_), channel_id=1, source_target_pairs={{0,8},{1,9},{2,10},{3,11},{4,12},{5,13},{6,14},{7,15},{8,0},{9,1},... | collective-permute-start | bytes 798728 | tf_op jit(solution)/shard_map/ppermute | solution.py:405
  53.9 5.7 %collective-permute-start.13 = (bf16[1056,128]{1,0:T(8,128)(2,1)S(1)}, bf16[1056,128]{1,0:T(8,128)(2,1)S(1)}, u32[]{:S(2)}, u32[]{:S(2)}) collective-permute-start(bf16[1056,128]{1,0:T(8,128)(2,1)S(1)} %collective-permute-done.12.refs_7_), channel_id=1, source_target_pairs={{0,16},{1,17},{2,18},{3,19},{4,20},{5,21},{6,22},{7,23},{8,24},{9,... | collective-permute-start | bytes 811016 | tf_op jit(solution)/shard_map/ppermute | solution.py:405
  55.1 3.5 %collective-permute-start.17 = (bf16[256,128]{1,0:T(8,128)(2,1)S(1)}, bf16[256,128]{1,0:T(8,128)(2,1)S(1)}, u32[]{:S(2)}, u32[]{:S(2)}) collective-permute-start(bf16[256,128]{1,0:T(8,128)(2,1)S(1)} %grad_block.1.refs_0_), channel_id=1, source_target_pairs={{0,1},{1,0},{2,3},{3,2},{4,5},{5,4},{6,7},{7,6},{8,9},{9,8},{10,11... | collective-permute-start | bytes 196616 | tf_op jit(solution)/shard_map/ppermute | solution.py:405
  61.1 14.0 %collective-permute-start.22 = (bf16[1024,128]{1,0:T(8,128)(2,1)S(1)}, bf16[1024,128]{1,0:T(8,128)(2,1)S(1)}, u32[]{:S(2)}, u32[]{:S(2)}) collective-permute-start(bf16[1024,128]{1,0:T(8,128)(2,1)S(1)} %tile_product.7.refs_2_.refs_0_), channel_id=1, source_target_pairs={{0,2},{1,3},{2,0},{3,1},{4,6},{5,7},{6,4},{7,5},{8,10},{9,11},{10,... | collective-permute-start | bytes 786440 | tf_op jit(solution)/shard_map/ppermute | solution.py:405
  63.2 7.7 %collective-permute-start.20 = (bf16[256,128]{1,0:T(8,128)(2,1)S(1)}, bf16[256,128]{1,0:T(8,128)(2,1)S(1)}, u32[]{:S(2)}, u32[]{:S(2)}) collective-permute-start(bf16[256,128]{1,0:T(8,128)(2,1)S(1)} %add_after.4.refs_0_), channel_id=1, source_target_pairs={{0,8},{1,9},{2,10},{3,11},{4,12},{5,13},{6,14},{7,15},{8,0},{9,1},... | collective-permute-start | bytes 196616 | tf_op jit(solution)/shard_map/ppermute | solution.py:405
  63.6 15.0 %collective-permute-start.18 = (bf16[1024,128]{1,0:T(8,128)(2,1)S(1)}, bf16[1024,128]{1,0:T(8,128)(2,1)S(1)}, u32[]{:S(2)}, u32[]{:S(2)}) collective-permute-start(bf16[1024,128]{1,0:T(8,128)(2,1)S(1)} %get-tuple-element.31.own_ref), channel_id=1, source_target_pairs={{0,1},{1,5},{2,3},{3,7},{4,0},{5,4},{6,2},{7,6},{8,9},{9,13},{10,1... | collective-permute-start | bytes 786440 | tf_op jit(solution)/shard_map/ppermute | solution.py:405
  67.1 11.5 %collective-permute-start.19 = (bf16[1024,128]{1,0:T(8,128)(2,1)S(1)}, bf16[1024,128]{1,0:T(8,128)(2,1)S(1)}, u32[]{:S(2)}, u32[]{:S(2)}) collective-permute-start(bf16[1024,128]{1,0:T(8,128)(2,1)S(1)} %get-tuple-element.31.own_ref), channel_id=1, source_target_pairs={{1,4},{3,6},{4,1},{6,3},{9,12},{11,14},{12,9},{14,11},{17,20},{19,... | collective-permute-start | bytes 786440 | tf_op jit(solution)/shard_map/ppermute | solution.py:405
  71.0 3.7 %collective-permute-start.21 = (bf16[256,128]{1,0:T(8,128)(2,1)S(1)}, bf16[256,128]{1,0:T(8,128)(2,1)S(1)}, u32[]{:S(2)}, u32[]{:S(2)}) collective-permute-start(bf16[256,128]{1,0:T(8,128)(2,1)S(1)} %add_after.5.refs_0_), channel_id=1, source_target_pairs={{0,16},{1,17},{2,18},{3,19},{4,20},{5,21},{6,22},{7,23},{8,24},{9,... | collective-permute-start | bytes 196616 | tf_op jit(solution)/shard_map/ppermute | solution.py:405
  75.1 5.9 %collective-permute-start.24 = (bf16[1024,128]{1,0:T(8,128)(2,1)S(1)}, bf16[1024,128]{1,0:T(8,128)(2,1)S(1)}, u32[]{:S(2)}, u32[]{:S(2)}) collective-permute-start(bf16[1024,128]{1,0:T(8,128)(2,1)S(1)} %add_after.6.refs_2_.own_ref), channel_id=1, source_target_pairs={{0,1},{1,5},{2,3},{3,7},{4,0},{5,4},{6,2},{7,6},{8,9},{9,13},{10,1... | collective-permute-start | bytes 786440 | tf_op jit(solution)/shard_map/ppermute | solution.py:405
  76.6 7.7 %collective-permute-start.25 = (bf16[1024,128]{1,0:T(8,128)(2,1)S(1)}, bf16[1024,128]{1,0:T(8,128)(2,1)S(1)}, u32[]{:S(2)}, u32[]{:S(2)}) collective-permute-start(bf16[1024,128]{1,0:T(8,128)(2,1)S(1)} %add_after.6.refs_2_.own_ref), channel_id=1, source_target_pairs={{1,4},{3,6},{4,1},{6,3},{9,12},{11,14},{12,9},{14,11},{17,20},{19,... | collective-permute-start | bytes 786440 | tf_op jit(solution)/shard_map/ppermute | solution.py:405
  78.6 1.4 %collective-permute-start.23 = (f32[256,128]{1,0:T(8,128)S(1)}, f32[256,128]{1,0:T(8,128)S(1)}, u32[]{:S(2)}, u32[]{:S(2)}) collective-permute-start(f32[256,128]{1,0:T(8,128)S(1)} %add_after.7.grad_ref), channel_id=1, source_target_pairs={{0,4},{1,5},{2,6},{3,7},{4,0},{5,1},{6,2},{7,3},{8,12},{9,13},{10,... | collective-permute-start | bytes 393224 | tf_op jit(solution)/shard_map/ppermute | solution.py:405

commit v19 on v18

--- a/solution.py
+++ b/solution.py
@@ -10,7 +10,7 @@
 AXES = ("rows", "rep")
 TOGETHER = 2
 ROWS = 256
-WEIGH = 75
+WEIGH = 180
 
 
 def route(shape, move):
@@ -469,16 +469,16 @@
     meta_later, second = lax.optimization_barrier((meta_b, second))
     meta_far = send(meta_later, home_to_sibling)
     set_first = [(None, (meta_b, first))]
-    panels = [
+    set_rest = [("home", (meta, own)), ("away", (meta_far, other_first))]
+    early = [
         ("self", [("home", mine), ("away", swapped)]),
         ("near", [("home", swapped), ("away", mine)]),
         ("direct", direct_choice),
-        ("second", [(None, second)]),
-        ("far", [(None, far)]),
     ]
-    part = tile_product(panels, [set_first], jnp.float32, weigh=WEIGH)
-    set_rest = [("home", (meta, own)), ("away", (meta_far, other_first))]
-    part = tile_product(panels, [set_rest], jnp.bfloat16, part)
+    late = [("second", [(None, second)]), ("far", [(None, far)])]
+    part = tile_product(early, [set_first], jnp.float32)
+    part = tile_product(late, [set_first], jnp.float32, part, weigh=WEIGH)
+    part = tile_product(early + late, [set_rest], jnp.bfloat16, part)
 
     def join(value):
         other = send(value, across)

time: 85.8 us -> 86.7 us (1.010)
  waiting for transfers between devices: 31.7 us -> 29.9 us
  starting transfers between devices: 40.6 us -> 42.4 us
    ppermute x26, starting transfers between devices: 40.6 us -> 42.4 us  [send(): return lax.ppermute(value, AXES, route(shape, move))]
    ppermute x26, waiting for transfers between devices: 31.7 us -> 29.9 us  [send(): return lax.ppermute(value, AXES, route(shape, move))]
    pallas_call x4 -> x5, Pallas kernels: 5.3 us -> 6.04 us  [tile_product(): pl.pallas_call(functools.partial(tile_kernel, kinds, cases, [[case for ca...]
  transfers between devices with their start and end apart: 26 -> 26, of which waited for: 15 -> 14; matrix products, arithmetic and copies ran while one was open for 2% -> 2% of each run, Pallas kernels for 6% -> 7%
where the time goes in v19:
time: 86.7 us; the launch traced here: 86.4 us
  starting transfers between devices  42.4 us (49%)
  waiting for transfers between devices  29.9 us (34%)
  Pallas kernels  10.6 us (12%)
  local copies, waits for them, and re-layouts  2.54 us (3%)
  between operations  0.89 us (1%)
    ppermute x26, starting transfers between devices, send(): return lax.ppermute(value, AXES, route(shape, move))  42.4 us
    ppermute x26, waiting for transfers between devices, send(): return lax.ppermute(value, AXES, route(shape, move))  29.9 us
    pallas_call x5, Pallas kernels, tile_product(): pl.pallas_call(functools.partial(tile_kernel, kinds, cases, [[case for ca...  6.04 us
  transfers between devices with their start and end apart: 26, of which 14 were waited for; matrix products, arithmetic and copies ran while one was open for 2% of the time, Pallas kernels for 7%

profile of v19, /device:TPU:1, one launch (start us, length us, event | category | flops | bytes accessed | tf_op | source)
XLA Modules:
  0.0 86.4 jit_solution(17888826683951828306)
XLA Ops:
  0.6 2.2 %collective-permute-start = (bf16[5,8,128,128]{3,2,1,0:T(8,128)(2,1)}, bf16[5,8,128,128]{3,2,1,0:T(8,128)(2,1)S(1)}, u32[]{:S(2)}, u32[]{:S(2)}) collective-permute-start(bf16[5,8,128,128]{3,2,1,0:T(8,128)(2,1)} %bitcast.5), channel_id=1, source_target_pairs={{0,4},{1,0},{2,6},{3,2},{4,5},{5,1},{6,7},{7,3},{8,12},{9,8},{10,1... | collective-permute-start | bytes 3932168 | tf_op jit(solution)/shard_map/ppermute | solution.py:405
  2.8 1.1 %constant_dynamic-slice_fusion = (bf16[1024,128]{1,0:T(8,128)(2,1)S(1)}, bf16[1024,128]{1,0:T(8,128)(2,1)S(1)}) fusion(bf16[1024,256]{1,0:T(8,128)(2,1)} %param.6, s32[]{:T(128)S(6)} %select_n.15, s32[]{:T(128)S(6)} %select_n.14), kind=kLoop, calls=%fused_computation.2 | loop fusion | bytes 1048584 | tf_op jit(solution)/shard_map/dynamic_slice | solution.py:445
  3.9 0.7 collective-permute-start.2
  4.6 1.3 %collective-permute-start.3 = (bf16[1024,128]{1,0:T(8,128)(2,1)S(1)}, bf16[1024,128]{1,0:T(8,128)(2,1)S(1)}, u32[]{:S(2)}, u32[]{:S(2)}) collective-permute-start(bf16[1024,128]{1,0:T(8,128)(2,1)S(1)} %get-tuple-element.35), channel_id=1, source_target_pairs={{0,12},{1,21},{2,14},{3,23},{5,9},{7,11},{8,4},{10,6},{12,24},{13,... | collective-permute-start | bytes 786440 | tf_op jit(solution)/shard_map/ppermute | solution.py:405
  5.9 4.8 %collective-permute-start.4 = (bf16[1024,128]{1,0:T(8,128)(2,1)S(1)}, bf16[1024,128]{1,0:T(8,128)(2,1)S(1)}, u32[]{:S(2)}, u32[]{:S(2)}) collective-permute-start(bf16[1024,128]{1,0:T(8,128)(2,1)S(1)} %get-tuple-element.35), channel_id=1, source_target_pairs={{0,4},{1,5},{2,6},{3,7},{4,0},{5,1},{6,2},{7,3},{8,12},{9,13},{10,... | collective-permute-start | bytes 786440 | tf_op jit(solution)/shard_map/ppermute | solution.py:405
  10.6 0.7 copy.12
  11.3 0.7 copy-done.3
  12.0 1.3 %slot_blocks.1.refs_6_.refs_0_.refs_1_ = s32[2,40]{1,0:T(2,128)S(1)} custom-call(s32[2,5,8]{2,1,0:T(8,128)S(1)} %copy.10.coords_ref, s32[5]{0:T(128)S(1)} %bitcast.9), custom_call_target="tpu_custom_call" | custom-call | tf_op jit(solution)/shard_map/slot_blocks/pallas_call | solution.py:135
  13.6 1.8 %collective-permute-start.5 = (bf16[1024,128]{1,0:T(8,128)(2,1)S(1)}, bf16[1024,128]{1,0:T(8,128)(2,1)S(1)}, u32[]{:S(2)}, u32[]{:S(2)}) collective-permute-start(bf16[1024,128]{1,0:T(8,128)(2,1)S(1)} %get-tuple-element.20), channel_id=1, source_target_pairs={{0,16},{1,17},{2,18},{3,19},{4,20},{5,21},{6,22},{7,23},{8,24},{9,... | collective-permute-start | bytes 786440 | tf_op jit(solution)/shard_map/ppermute | solution.py:405
  15.4 1.2 %collective-permute-start.8 = (bf16[1024,128]{1,0:T(8,128)(2,1)S(1)}, bf16[1024,128]{1,0:T(8,128)(2,1)S(1)}, u32[]{:S(2)}, u32[]{:S(2)}) collective-permute-start(bf16[1024,128]{1,0:T(8,128)(2,1)S(1)} %get-tuple-element.24), channel_id=1, source_target_pairs={{0,8},{1,9},{2,10},{3,11},{4,12},{5,13},{6,14},{7,15},{8,0},{9,1},... | collective-permute-start | bytes 786440 | tf_op jit(solution)/shard_map/ppermute | solution.py:405
  16.8 1.5 %collective-permute-done.1.refs_0_ = s32[2,40]{1,0:T(2,128)S(1)} collective-permute-done((s32[2,40]{1,0:T(2,128)S(1)}, s32[2,40]{1,0:T(2,128)S(1)}, u32[]{:S(2)}, u32[]{:S(2)}) %collective-permute-start.1) | collective-permute-done | bytes 352 | tf_op jit(solution)/shard_map/ppermute | solution.py:405
  18.3 1.3 %collective-permute-start.7 = (bf16[5,8,128,128]{3,2,1,0:T(8,128)(2,1)S(1)}, bf16[5,8,128,128]{3,2,1,0:T(8,128)(2,1)S(1)}, u32[]{:S(2)}, u32[]{:S(2)}) collective-permute-start(bf16[5,8,128,128]{3,2,1,0:T(8,128)(2,1)S(1)} %collective-permute-done.refs_1_.refs_3_), channel_id=1, source_target_pairs={{0,4},{2,6},{5,1},{7,3},{8,12},{10,14},{13,9},{15,11},{16,20},{18,... | collective-permute-start | bytes 3932168 | tf_op jit(solution)/shard_map/ppermute | solution.py:405
  19.6 1.9 %collective-permute-done.5.refs_2_.refs_10_ = bf16[1024,128]{1,0:T(8,128)(2,1)S(1)} collective-permute-done((bf16[1024,128]{1,0:T(8,128)(2,1)S(1)}, bf16[1024,128]{1,0:T(8,128)(2,1)S(1)}, u32[]{:S(2)}, u32[]{:S(2)}) %collective-permute-start.5) | collective-permute-done | bytes 262176 | tf_op jit(solution)/shard_map/ppermute | solution.py:405
  21.5 1.3 %collective-permute-start.6 = (s32[2,40]{1,0:T(2,128)S(1)}, s32[2,40]{1,0:T(2,128)S(1)}, u32[]{:S(2)}, u32[]{:S(2)}) collective-permute-start(s32[2,40]{1,0:T(2,128)S(1)} %collective-permute-done.1.refs_0_), channel_id=1, source_target_pairs={{0,4},{2,6},{5,1},{7,3},{8,12},{10,14},{13,9},{15,11},{16,20},{18,... | collective-permute-start | bytes 968 | tf_op jit(solution)/shard_map/ppermute | solution.py:405
  22.8 1.1 %tile_product.5.refs_4_ = f32[1024,128]{1,0:T(8,128)S(1)} custom-call(s32[2,40]{1,0:T(2,128)S(1)} %collective-permute-done.1.refs_0_, bf16[5,8,128,128]{3,2,1,0:T(8,128)(2,1)S(1)} %collective-permute-done.refs_1_.refs_3_, bf16[1024,128]{1,0:T(8,128)(2,1)S(1)} %get-tuple-element.36.refs_3_.refs_2_.refs_5_.refs_4_.refs_7_, ...), custom_call_target="tpu_custom_call" | custom-call | flops 100663296 | bytes 1572864 | tf_op jit(solution)/shard_map/tile_product/pallas_call | solution.py:210
  23.9 0.9 %tile_product.6.refs_12_ = f32[1024,128]{1,0:T(8,128)S(1)} custom-call(s32[2,40]{1,0:T(2,128)S(1)} %collective-permute-done.1.refs_0_, bf16[5,8,128,128]{3,2,1,0:T(8,128)(2,1)S(1)} %collective-permute-done.refs_1_.refs_3_, bf16[1024,128]{1,0:T(8,128)(2,1)S(1)} %collective-permute-done.5.refs_2_.refs_10_, ...), custom_call_target="tpu_custom_call" | custom-call | flops 12079595520 | bytes 188743680 | tf_op jit(solution)/shard_map/tile_product/pallas_call | solution.py:210
  24.8 0.3 collective-permute-done.6.refs_1_.refs_2_
  25.1 1.4 %tile_product.7 = bf16[1024,128]{1,0:T(8,128)(2,1)S(1)} custom-call(s32[2,40]{1,0:T(2,128)S(1)} %slot_blocks.1.refs_6_.refs_0_.refs_1_, s32[2,40]{1,0:T(2,128)S(1)} %collective-permute-done.6.refs_1_.refs_2_, bf16[5,8,128,128]{3,2,1,0:T(8,128)(2,1)S(1)} %bitcast.6, bf16[5,8,128,128]{3,2,1,0:T(8,128)(2,1)S(1)} %collective-permute-done.7.refs_3_.refs_5_, ...), custom_call_target="tpu_custom_call" | custom-call | flops 167772160 | bytes 2621440 | tf_op jit(solution)/shard_map/tile_product/pallas_call | solution.py:210
  26.6 2.5 %collective-permute-start.9 = (bf16[1024,128]{1,0:T(8,128)(2,1)S(1)}, bf16[1024,128]{1,0:T(8,128)(2,1)S(1)}, u32[]{:S(2)}, u32[]{:S(2)}) collective-permute-start(bf16[1024,128]{1,0:T(8,128)(2,1)S(1)} %tile_product.7), channel_id=1, source_target_pairs={{0,2},{1,3},{2,0},{3,1},{4,6},{5,7},{6,4},{7,5},{8,10},{9,11},{10,... | collective-permute-start | bytes 786440 | tf_op jit(solution)/shard_map/ppermute | solution.py:405
  29.2 1.6 %collective-permute-start.11 = (bf16[1024,128]{1,0:T(8,128)(2,1)S(1)}, bf16[1024,128]{1,0:T(8,128)(2,1)S(1)}, u32[]{:S(2)}, u32[]{:S(2)}) collective-permute-start(bf16[1024,128]{1,0:T(8,128)(2,1)S(1)} %get-tuple-element.26), channel_id=1, source_target_pairs={{0,4},{1,5},{2,6},{3,7},{4,0},{5,1},{6,2},{7,3},{8,12},{9,13},{10,... | collective-permute-start | bytes 786440 | tf_op jit(solution)/shard_map/ppermute | solution.py:405
  30.8 9.1 %collective-permute-done.9 = bf16[1024,128]{1,0:T(8,128)(2,1)S(1)} collective-permute-done((bf16[1024,128]{1,0:T(8,128)(2,1)S(1)}, bf16[1024,128]{1,0:T(8,128)(2,1)S(1)}, u32[]{:S(2)}, u32[]{:S(2)}) %collective-permute-start.9) | collective-permute-done | bytes 262176 | tf_op jit(solution)/shard_map/ppermute | solution.py:405
  40.0 2.1 %collective-permute-start.10 = (bf16[1024,128]{1,0:T(8,128)(2,1)S(1)}, bf16[1024,128]{1,0:T(8,128)(2,1)S(1)}, u32[]{:S(2)}, u32[]{:S(2)}) collective-permute-start(bf16[1024,128]{1,0:T(8,128)(2,1)S(1)} %add_convert_fusion.near_ref), channel_id=1, source_target_pairs={{0,4},{1,5},{2,6},{3,7},{4,0},{5,1},{6,2},{7,3},{8,12},{9,13},{10,... | collective-permute-start | bytes 786440 | tf_op jit(solution)/shard_map/ppermute | solution.py:405
  42.1 1.2 %collective-permute-done.10.far_ref = bf16[1024,128]{1,0:T(8,128)(2,1)S(1)} collective-permute-done((bf16[1024,128]{1,0:T(8,128)(2,1)S(1)}, bf16[1024,128]{1,0:T(8,128)(2,1)S(1)}, u32[]{:S(2)}, u32[]{:S(2)}) %collective-permute-start.10) | collective-permute-done | bytes 262176 | tf_op jit(solution)/shard_map/ppermute | solution.py:405
  43.2 0.4 middle.1
  43.6 2.6 %collective-permute-start.12 = (bf16[1056,128]{1,0:T(8,128)(2,1)S(1)}, bf16[1056,128]{1,0:T(8,128)(2,1)S(1)}, u32[]{:S(2)}, u32[]{:S(2)}) collective-permute-start(bf16[1056,128]{1,0:T(8,128)(2,1)S(1)} %get-tuple-element.28), channel_id=1, source_target_pairs={{0,8},{1,9},{2,10},{3,11},{4,12},{5,13},{6,14},{7,15},{8,0},{9,1},... | collective-permute-start | bytes 811016 | tf_op jit(solution)/shard_map/ppermute | solution.py:405
  46.2 3.4 %collective-permute-start.16 = (bf16[1024,128]{1,0:T(8,128)(2,1)S(1)}, bf16[1024,128]{1,0:T(8,128)(2,1)S(1)}, u32[]{:S(2)}, u32[]{:S(2)}) collective-permute-start(bf16[1024,128]{1,0:T(8,128)(2,1)S(1)} %get-tuple-element.30.refs_6_.adj_ref), channel_id=1, source_target_pairs={{0,1},{2,3},{4,5},{6,7},{9,8},{11,10},{13,12},{15,14},{16,17},{18,... | collective-permute-start | bytes 786440 | tf_op jit(solution)/shard_map/ppermute | solution.py:405
  49.6 3.9 %collective-permute-done.14.refs_8_ = bf16[1040,128]{1,0:T(8,128)(2,1)S(1)} collective-permute-done((bf16[1040,128]{1,0:T(8,128)(2,1)S(1)}, bf16[1040,128]{1,0:T(8,128)(2,1)S(1)}, u32[]{:S(2)}, u32[]{:S(2)}) %collective-permute-start.14) | collective-permute-done | bytes 266272 | tf_op jit(solution)/shard_map/ppermute | solution.py:405
  53.5 1.3 %collective-permute-start.15 = (bf16[1040,128]{1,0:T(8,128)(2,1)S(1)}, bf16[1040,128]{1,0:T(8,128)(2,1)S(1)}, u32[]{:S(2)}, u32[]{:S(2)}) collective-permute-start(bf16[1040,128]{1,0:T(8,128)(2,1)S(1)} %collective-permute-done.14.refs_8_), channel_id=1, source_target_pairs={{0,8},{1,9},{2,10},{3,11},{4,12},{5,13},{6,14},{7,15},{8,0},{9,1},... | collective-permute-start | bytes 798728 | tf_op jit(solution)/shard_map/ppermute | solution.py:405
  54.8 0.6 collective-permute-start.13
  55.4 0.3 grad_block.1.refs_0_
  55.8 1.2 %tile_product.8.refs_10_ = f32[1024,128]{1,0:T(8,128)S(1)} custom-call(s32[2,40]{1,0:T(2,128)S(1)} %collective-permute-done.1.refs_0_, s32[2,40]{1,0:T(2,128)S(1)} %slot_blocks.1.refs_6_.refs_0_.refs_1_, s32[2,40]{1,0:T(2,128)S(1)} %collective-permute-done.6.refs_1_.refs_2_, bf16[5,8,128,128]{3,2,1,0:T(8,128)(2,1)S(1)} %collective-permute-done.refs_1_.refs_3_, ...), custom_call_target="tpu_custom_call" | custom-call | flops 134217728 | bytes 1572864 | tf_op jit(solution)/shard_map/tile_product/pallas_call | solution.py:210
  57.0 2.2 %collective-permute-done.17.refs_11_.refs_1_ = bf16[256,128]{1,0:T(8,128)(2,1)S(1)} collective-permute-done((bf16[256,128]{1,0:T(8,128)(2,1)S(1)}, bf16[256,128]{1,0:T(8,128)(2,1)S(1)}, u32[]{:S(2)}, u32[]{:S(2)}) %collective-permute-start.17) | collective-permute-done | bytes 65568 | tf_op jit(solution)/shard_map/ppermute | solution.py:405
  59.2 0.6 collective-permute-done.15.refs_7_
  59.8 0.7 collective-permute-done.13.refs_6_
  60.5 1.5 %tile_product.9.refs_2_.refs_0_ = bf16[1024,128]{1,0:T(8,128)(2,1)S(1)} custom-call(s32[2,40]{1,0:T(2,128)S(1)} %collective-permute-done.1.refs_0_, s32[2,40]{1,0:T(2,128)S(1)} %slot_blocks.1.refs_6_.refs_0_.refs_1_, s32[2,40]{1,0:T(2,128)S(1)} %collective-permute-done.6.refs_1_.refs_2_, bf16[5,8,128,128]{3,2,1,0:T(8,128)(2,1)S(1)} %collective-permute-done.refs_1_.refs_3_, ...), custom_call_target="tpu_custom_call" | custom-call | flops 201326592 | bytes 2359296 | tf_op jit(solution)/shard_map/tile_product/pallas_call | solution.py:210
  62.0 1.8 %collective-permute-start.22 = (bf16[1024,128]{1,0:T(8,128)(2,1)S(1)}, bf16[1024,128]{1,0:T(8,128)(2,1)S(1)}, u32[]{:S(2)}, u32[]{:S(2)}) collective-permute-start(bf16[1024,128]{1,0:T(8,128)(2,1)S(1)} %tile_product.9.refs_2_.refs_0_), channel_id=1, source_target_pairs={{0,2},{1,3},{2,0},{3,1},{4,6},{5,7},{6,4},{7,5},{8,10},{9,11},{10,... | collective-permute-start | bytes 786440 | tf_op jit(solution)/shard_map/ppermute | solution.py:405
  63.8 0.3 collective-permute-start.20
  64.2 3.5 %collective-permute-start.18 = (bf16[1024,128]{1,0:T(8,128)(2,1)S(1)}, bf16[1024,128]{1,0:T(8,128)(2,1)S(1)}, u32[]{:S(2)}, u32[]{:S(2)}) collective-permute-start(bf16[1024,128]{1,0:T(8,128)(2,1)S(1)} %get-tuple-element.31.own_ref), channel_id=1, source_target_pairs={{0,1},{1,5},{2,3},{3,7},{4,0},{5,4},{6,2},{7,6},{8,9},{9,13},{10,1... | collective-permute-start | bytes 786440 | tf_op jit(solution)/shard_map/ppermute | solution.py:405
  67.7 4.0 %collective-permute-start.19 = (bf16[1024,128]{1,0:T(8,128)(2,1)S(1)}, bf16[1024,128]{1,0:T(8,128)(2,1)S(1)}, u32[]{:S(2)}, u32[]{:S(2)}) collective-permute-start(bf16[1024,128]{1,0:T(8,128)(2,1)S(1)} %get-tuple-element.31.own_ref), channel_id=1, source_target_pairs={{1,4},{3,6},{4,1},{6,3},{9,12},{11,14},{12,9},{14,11},{17,20},{19,... | collective-permute-start | bytes 786440 | tf_op jit(solution)/shard_map/ppermute | solution.py:405
  71.8 0.5 collective-permute-start.21
  72.3 3.3 %collective-permute-done.21.refs_2_.refs_1_ = bf16[256,128]{1,0:T(8,128)(2,1)S(1)} collective-permute-done((bf16[256,128]{1,0:T(8,128)(2,1)S(1)}, bf16[256,128]{1,0:T(8,128)(2,1)S(1)}, u32[]{:S(2)}, u32[]{:S(2)}) %collective-permute-start.21) | collective-permute-done | bytes 65568 | tf_op jit(solution)/shard_map/ppermute | solution.py:405
  75.6 0.6 collective-permute-done.22.refs_1_
  76.3 1.2 %collective-permute-start.24 = (bf16[1024,128]{1,0:T(8,128)(2,1)S(1)}, bf16[1024,128]{1,0:T(8,128)(2,1)S(1)}, u32[]{:S(2)}, u32[]{:S(2)}) collective-permute-start(bf16[1024,128]{1,0:T(8,128)(2,1)S(1)} %add_after.6.refs_2_.own_ref), channel_id=1, source_target_pairs={{0,1},{1,5},{2,3},{3,7},{4,0},{5,4},{6,2},{7,6},{8,9},{9,13},{10,1... | collective-permute-start | bytes 786440 | tf_op jit(solution)/shard_map/ppermute | solution.py:405
  77.5 1.9 %collective-permute-start.25 = (bf16[1024,128]{1,0:T(8,128)(2,1)S(1)}, bf16[1024,128]{1,0:T(8,128)(2,1)S(1)}, u32[]{:S(2)}, u32[]{:S(2)}) collective-permute-start(bf16[1024,128]{1,0:T(8,128)(2,1)S(1)} %add_after.6.refs_2_.own_ref), channel_id=1, source_target_pairs={{1,4},{3,6},{4,1},{6,3},{9,12},{11,14},{12,9},{14,11},{17,20},{19,... | collective-permute-start | bytes 786440 | tf_op jit(solution)/shard_map/ppermute | solution.py:405
  79.6 1.3 %collective-permute-done.23.rest_ref = f32[256,128]{1,0:T(8,128)S(1)} collective-permute-done((f32[256,128]{1,0:T(8,128)S(1)}, f32[256,128]{1,0:T(8,128)S(1)}, u32[]{:S(2)}, u32[]{:S(2)}) %collective-permute-start.23) | collective-permute-done | bytes 131104 | tf_op jit(solution)/shard_map/ppermute | solution.py:405
  80.9 1.0 %gather_halves.1 = (bf16[1024,256]{1,0:T(8,128)(2,1)}, f32[256,256]{1,0:T(8,128)}) custom-call(bf16[1024,128]{1,0:T(8,128)(2,1)S(1)} %get-tuple-element.31.own_ref, bf16[1024,128]{1,0:T(8,128)(2,1)S(1)} %collective-permute-done.18.refs_3_.one_ref, bf16[1024,128]{1,0:T(8,128)(2,1)S(1)} %collective-permute-done.19.refs_4_.two_ref, ...), custom_call_target="tpu_custom_call" | custom-call | tf_op jit(solution)/shard_map/gather_halves/pallas_call | solution.py:349
  81.9 3.3 %collective-permute-done.25.two_ref = bf16[1024,128]{1,0:T(8,128)(2,1)S(1)} collective-permute-done((bf16[1024,128]{1,0:T(8,128)(2,1)S(1)}, bf16[1024,128]{1,0:T(8,128)(2,1)S(1)}, u32[]{:S(2)}, u32[]{:S(2)}) %collective-permute-start.25) | collective-permute-done | bytes 262176 | tf_op jit(solution)/shard_map/ppermute | solution.py:405
  85.2 1.2 %final.1 = bf16[1024,256]{1,0:T(8,128)(2,1)} custom-call(bf16[1024,128]{1,0:T(8,128)(2,1)S(1)} %add_after.6.refs_2_.own_ref, bf16[1024,128]{1,0:T(8,128)(2,1)S(1)} %collective-permute-done.24.one_ref, bf16[1024,128]{1,0:T(8,128)(2,1)S(1)} %collective-permute-done.25.two_ref, bf16[256,256]{1,0:T(8,128)(2,1)S(1)} %copy-done.2), custom_call_target="tpu_custom_call" | custom-call | flops 134217728 | bytes 2097152 | tf_op jit(solution)/shard_map/final/pallas_call | solution.py:383
  (32 shorter events, 1.0 us)
Async XLA Ops:
  0.6 17.7 %collective-permute-start = (bf16[5,8,128,128]{3,2,1,0:T(8,128)(2,1)}, bf16[5,8,128,128]{3,2,1,0:T(8,128)(2,1)S(1)}, u32[]{:S(2)}, u32[]{:S(2)}) collective-permute-start(bf16[5,8,128,128]{3,2,1,0:T(8,128)(2,1)} %bitcast.5), channel_id=1, source_target_pairs={{0,4},{1,0},{2,6},{3,2},{4,5},{5,1},{6,7},{7,3},{8,12},{9,8},{10,1... | collective-permute-start | bytes 3932168 | tf_op jit(solution)/shard_map/ppermute | solution.py:405
  3.9 9.5 %collective-permute-start.2 = (bf16[1024,128]{1,0:T(8,128)(2,1)S(1)}, bf16[1024,128]{1,0:T(8,128)(2,1)S(1)}, u32[]{:S(2)}, u32[]{:S(2)}) collective-permute-start(bf16[1024,128]{1,0:T(8,128)(2,1)S(1)} %get-tuple-element.36.refs_3_.refs_2_.refs_5_.refs_4_.refs_7_), channel_id=1, source_target_pairs={{0,8},{1,17},{2,10},{3,19},{5,13},{7,15},{8,0},{10,2},{12,28},{13,... | collective-permute-start | bytes 786440 | tf_op jit(solution)/shard_map/ppermute | solution.py:405
  4.6 8.9 %collective-permute-start.3 = (bf16[1024,128]{1,0:T(8,128)(2,1)S(1)}, bf16[1024,128]{1,0:T(8,128)(2,1)S(1)}, u32[]{:S(2)}, u32[]{:S(2)}) collective-permute-start(bf16[1024,128]{1,0:T(8,128)(2,1)S(1)} %get-tuple-element.35), channel_id=1, source_target_pairs={{0,12},{1,21},{2,14},{3,23},{5,9},{7,11},{8,4},{10,6},{12,24},{13,... | collective-permute-start | bytes 786440 | tf_op jit(solution)/shard_map/ppermute | solution.py:405
  5.9 7.6 %collective-permute-start.4 = (bf16[1024,128]{1,0:T(8,128)(2,1)S(1)}, bf16[1024,128]{1,0:T(8,128)(2,1)S(1)}, u32[]{:S(2)}, u32[]{:S(2)}) collective-permute-start(bf16[1024,128]{1,0:T(8,128)(2,1)S(1)} %get-tuple-element.35), channel_id=1, source_target_pairs={{0,4},{1,5},{2,6},{3,7},{4,0},{5,1},{6,2},{7,3},{8,12},{9,13},{10,... | collective-permute-start | bytes 786440 | tf_op jit(solution)/shard_map/ppermute | solution.py:405
  11.3 0.7 copy-start.3
  13.6 7.9 %collective-permute-start.5 = (bf16[1024,128]{1,0:T(8,128)(2,1)S(1)}, bf16[1024,128]{1,0:T(8,128)(2,1)S(1)}, u32[]{:S(2)}, u32[]{:S(2)}) collective-permute-start(bf16[1024,128]{1,0:T(8,128)(2,1)S(1)} %get-tuple-element.20), channel_id=1, source_target_pairs={{0,16},{1,17},{2,18},{3,19},{4,20},{5,21},{6,22},{7,23},{8,24},{9,... | collective-permute-start | bytes 786440 | tf_op jit(solution)/shard_map/ppermute | solution.py:405
  15.4 8.5 %collective-permute-start.8 = (bf16[1024,128]{1,0:T(8,128)(2,1)S(1)}, bf16[1024,128]{1,0:T(8,128)(2,1)S(1)}, u32[]{:S(2)}, u32[]{:S(2)}) collective-permute-start(bf16[1024,128]{1,0:T(8,128)(2,1)S(1)} %get-tuple-element.24), channel_id=1, source_target_pairs={{0,8},{1,9},{2,10},{3,11},{4,12},{5,13},{6,14},{7,15},{8,0},{9,1},... | collective-permute-start | bytes 786440 | tf_op jit(solution)/shard_map/ppermute | solution.py:405
  16.6 1.7 %collective-permute-start.1 = (s32[2,40]{1,0:T(2,128)S(1)}, s32[2,40]{1,0:T(2,128)S(1)}, u32[]{:S(2)}, u32[]{:S(2)}) collective-permute-start(s32[2,40]{1,0:T(2,128)S(1)} %slot_blocks.1.refs_6_.refs_0_.refs_1_), channel_id=1, source_target_pairs={{0,4},{1,0},{2,6},{3,2},{4,5},{5,1},{6,7},{7,3},{8,12},{9,8},{10,1... | collective-permute-start | bytes 968 | tf_op jit(solution)/shard_map/ppermute | solution.py:405
  18.3 6.7 %collective-permute-start.7 = (bf16[5,8,128,128]{3,2,1,0:T(8,128)(2,1)S(1)}, bf16[5,8,128,128]{3,2,1,0:T(8,128)(2,1)S(1)}, u32[]{:S(2)}, u32[]{:S(2)}) collective-permute-start(bf16[5,8,128,128]{3,2,1,0:T(8,128)(2,1)S(1)} %collective-permute-done.refs_1_.refs_3_), channel_id=1, source_target_pairs={{0,4},{2,6},{5,1},{7,3},{8,12},{10,14},{13,9},{15,11},{16,20},{18,... | collective-permute-start | bytes 3932168 | tf_op jit(solution)/shard_map/ppermute | solution.py:405
  21.5 3.6 %collective-permute-start.6 = (s32[2,40]{1,0:T(2,128)S(1)}, s32[2,40]{1,0:T(2,128)S(1)}, u32[]{:S(2)}, u32[]{:S(2)}) collective-permute-start(s32[2,40]{1,0:T(2,128)S(1)} %collective-permute-done.1.refs_0_), channel_id=1, source_target_pairs={{0,4},{2,6},{5,1},{7,3},{8,12},{10,14},{13,9},{15,11},{16,20},{18,... | collective-permute-start | bytes 968 | tf_op jit(solution)/shard_map/ppermute | solution.py:405
  23.8 1.3 %copy-start = (bf16[1,5,8,128,128]{4,3,2,1,0:T(8,128)(2,1)S(1)}, bf16[1,5,8,128,128]{4,3,2,1,0:T(8,128)(2,1)}, u32[]{:S(2)}) copy-start(bf16[1,5,8,128,128]{4,3,2,1,0:T(8,128)(2,1)} %param.9) | copy-start | bytes 3932164
  24.8 4.3 %copy-start.1 = (bf16[1024,256]{1,0:T(8,128)(2,1)S(1)}, bf16[1024,256]{1,0:T(8,128)(2,1)}, u32[]{:S(2)}) copy-start(bf16[1024,256]{1,0:T(8,128)(2,1)} %x_ref.1) | copy-start | bytes 1572868
  26.6 16.7 %copy-start.2 = (bf16[256,256]{1,0:T(8,128)(2,1)S(1)}, bf16[256,256]{1,0:T(8,128)(2,1)}, u32[]{:S(2)}) copy-start(bf16[256,256]{1,0:T(8,128)(2,1)} %w_ref.3) | copy-start | bytes 393220
  26.6 13.3 %collective-permute-start.9 = (bf16[1024,128]{1,0:T(8,128)(2,1)S(1)}, bf16[1024,128]{1,0:T(8,128)(2,1)S(1)}, u32[]{:S(2)}, u32[]{:S(2)}) collective-permute-start(bf16[1024,128]{1,0:T(8,128)(2,1)S(1)} %tile_product.7), channel_id=1, source_target_pairs={{0,2},{1,3},{2,0},{3,1},{4,6},{5,7},{6,4},{7,5},{8,10},{9,11},{10,... | collective-permute-start | bytes 786440 | tf_op jit(solution)/shard_map/ppermute | solution.py:405
  29.2 12.9 %collective-permute-start.11 = (bf16[1024,128]{1,0:T(8,128)(2,1)S(1)}, bf16[1024,128]{1,0:T(8,128)(2,1)S(1)}, u32[]{:S(2)}, u32[]{:S(2)}) collective-permute-start(bf16[1024,128]{1,0:T(8,128)(2,1)S(1)} %get-tuple-element.26), channel_id=1, source_target_pairs={{0,4},{1,5},{2,6},{3,7},{4,0},{5,1},{6,2},{7,3},{8,12},{9,13},{10,... | collective-permute-start | bytes 786440 | tf_op jit(solution)/shard_map/ppermute | solution.py:405
  40.0 3.3 %collective-permute-start.10 = (bf16[1024,128]{1,0:T(8,128)(2,1)S(1)}, bf16[1024,128]{1,0:T(8,128)(2,1)S(1)}, u32[]{:S(2)}, u32[]{:S(2)}) collective-permute-start(bf16[1024,128]{1,0:T(8,128)(2,1)S(1)} %add_convert_fusion.near_ref), channel_id=1, source_target_pairs={{0,4},{1,5},{2,6},{3,7},{4,0},{5,1},{6,2},{7,3},{8,12},{9,13},{10,... | collective-permute-start | bytes 786440 | tf_op jit(solution)/shard_map/ppermute | solution.py:405
  43.6 11.2 %collective-permute-start.12 = (bf16[1056,128]{1,0:T(8,128)(2,1)S(1)}, bf16[1056,128]{1,0:T(8,128)(2,1)S(1)}, u32[]{:S(2)}, u32[]{:S(2)}) collective-permute-start(bf16[1056,128]{1,0:T(8,128)(2,1)S(1)} %get-tuple-element.28), channel_id=1, source_target_pairs={{0,8},{1,9},{2,10},{3,11},{4,12},{5,13},{6,14},{7,15},{8,0},{9,1},... | collective-permute-start | bytes 811016 | tf_op jit(solution)/shard_map/ppermute | solution.py:405
  46.2 7.3 %collective-permute-start.14 = (bf16[1040,128]{1,0:T(8,128)(2,1)S(1)}, bf16[1040,128]{1,0:T(8,128)(2,1)S(1)}, u32[]{:S(2)}, u32[]{:S(2)}) collective-permute-start(bf16[1040,128]{1,0:T(8,128)(2,1)S(1)} %get-tuple-element.29), channel_id=1, source_target_pairs={{0,17},{1,0},{2,19},{3,2},{4,21},{5,4},{6,23},{7,6},{8,9},{9,24},{... | collective-permute-start | bytes 798728 | tf_op jit(solution)/shard_map/ppermute | solution.py:405
  46.2 13.0 %collective-permute-start.16 = (bf16[1024,128]{1,0:T(8,128)(2,1)S(1)}, bf16[1024,128]{1,0:T(8,128)(2,1)S(1)}, u32[]{:S(2)}, u32[]{:S(2)}) collective-permute-start(bf16[1024,128]{1,0:T(8,128)(2,1)S(1)} %get-tuple-element.30.refs_6_.adj_ref), channel_id=1, source_target_pairs={{0,1},{2,3},{4,5},{6,7},{9,8},{11,10},{13,12},{15,14},{16,17},{18,... | collective-permute-start | bytes 786440 | tf_op jit(solution)/shard_map/ppermute | solution.py:405
  53.5 6.3 %collective-permute-start.15 = (bf16[1040,128]{1,0:T(8,128)(2,1)S(1)}, bf16[1040,128]{1,0:T(8,128)(2,1)S(1)}, u32[]{:S(2)}, u32[]{:S(2)}) collective-permute-start(bf16[1040,128]{1,0:T(8,128)(2,1)S(1)} %collective-permute-done.14.refs_8_), channel_id=1, source_target_pairs={{0,8},{1,9},{2,10},{3,11},{4,12},{5,13},{6,14},{7,15},{8,0},{9,1},... | collective-permute-start | bytes 798728 | tf_op jit(solution)/shard_map/ppermute | solution.py:405
  54.8 5.7 %collective-permute-start.13 = (bf16[1056,128]{1,0:T(8,128)(2,1)S(1)}, bf16[1056,128]{1,0:T(8,128)(2,1)S(1)}, u32[]{:S(2)}, u32[]{:S(2)}) collective-permute-start(bf16[1056,128]{1,0:T(8,128)(2,1)S(1)} %collective-permute-done.12.refs_7_), channel_id=1, source_target_pairs={{0,16},{1,17},{2,18},{3,19},{4,20},{5,21},{6,22},{7,23},{8,24},{9,... | collective-permute-start | bytes 811016 | tf_op jit(solution)/shard_map/ppermute | solution.py:405
  55.8 3.5 %collective-permute-start.17 = (bf16[256,128]{1,0:T(8,128)(2,1)S(1)}, bf16[256,128]{1,0:T(8,128)(2,1)S(1)}, u32[]{:S(2)}, u32[]{:S(2)}) collective-permute-start(bf16[256,128]{1,0:T(8,128)(2,1)S(1)} %grad_block.1.refs_0_), channel_id=1, source_target_pairs={{0,1},{1,0},{2,3},{3,2},{4,5},{5,4},{6,7},{7,6},{8,9},{9,8},{10,11... | collective-permute-start | bytes 196616 | tf_op jit(solution)/shard_map/ppermute | solution.py:405
  62.0 14.2 %collective-permute-start.22 = (bf16[1024,128]{1,0:T(8,128)(2,1)S(1)}, bf16[1024,128]{1,0:T(8,128)(2,1)S(1)}, u32[]{:S(2)}, u32[]{:S(2)}) collective-permute-start(bf16[1024,128]{1,0:T(8,128)(2,1)S(1)} %tile_product.9.refs_2_.refs_0_), channel_id=1, source_target_pairs={{0,2},{1,3},{2,0},{3,1},{4,6},{5,7},{6,4},{7,5},{8,10},{9,11},{10,... | collective-permute-start | bytes 786440 | tf_op jit(solution)/shard_map/ppermute | solution.py:405
  63.8 7.9 %collective-permute-start.20 = (bf16[256,128]{1,0:T(8,128)(2,1)S(1)}, bf16[256,128]{1,0:T(8,128)(2,1)S(1)}, u32[]{:S(2)}, u32[]{:S(2)}) collective-permute-start(bf16[256,128]{1,0:T(8,128)(2,1)S(1)} %add_after.4.refs_0_), channel_id=1, source_target_pairs={{0,8},{1,9},{2,10},{3,11},{4,12},{5,13},{6,14},{7,15},{8,0},{9,1},... | collective-permute-start | bytes 196616 | tf_op jit(solution)/shard_map/ppermute | solution.py:405
  64.2 15.3 %collective-permute-start.18 = (bf16[1024,128]{1,0:T(8,128)(2,1)S(1)}, bf16[1024,128]{1,0:T(8,128)(2,1)S(1)}, u32[]{:S(2)}, u32[]{:S(2)}) collective-permute-start(bf16[1024,128]{1,0:T(8,128)(2,1)S(1)} %get-tuple-element.31.own_ref), channel_id=1, source_target_pairs={{0,1},{1,5},{2,3},{3,7},{4,0},{5,4},{6,2},{7,6},{8,9},{9,13},{10,1... | collective-permute-start | bytes 786440 | tf_op jit(solution)/shard_map/ppermute | solution.py:405
  67.7 11.8 %collective-permute-start.19 = (bf16[1024,128]{1,0:T(8,128)(2,1)S(1)}, bf16[1024,128]{1,0:T(8,128)(2,1)S(1)}, u32[]{:S(2)}, u32[]{:S(2)}) collective-permute-start(bf16[1024,128]{1,0:T(8,128)(2,1)S(1)} %get-tuple-element.31.own_ref), channel_id=1, source_target_pairs={{1,4},{3,6},{4,1},{6,3},{9,12},{11,14},{12,9},{14,11},{17,20},{19,... | collective-permute-start | bytes 786440 | tf_op jit(solution)/shard_map/ppermute | solution.py:405
  71.8 3.9 %collective-permute-start.21 = (bf16[256,128]{1,0:T(8,128)(2,1)S(1)}, bf16[256,128]{1,0:T(8,128)(2,1)S(1)}, u32[]{:S(2)}, u32[]{:S(2)}) collective-permute-start(bf16[256,128]{1,0:T(8,128)(2,1)S(1)} %add_after.5.refs_0_), channel_id=1, source_target_pairs={{0,16},{1,17},{2,18},{3,19},{4,20},{5,21},{6,22},{7,23},{8,24},{9,... | collective-permute-start | bytes 196616 | tf_op jit(solution)/shard_map/ppermute | solution.py:405
  76.3 5.6 %collective-permute-start.24 = (bf16[1024,128]{1,0:T(8,128)(2,1)S(1)}, bf16[1024,128]{1,0:T(8,128)(2,1)S(1)}, u32[]{:S(2)}, u32[]{:S(2)}) collective-permute-start(bf16[1024,128]{1,0:T(8,128)(2,1)S(1)} %add_after.6.refs_2_.own_ref), channel_id=1, source_target_pairs={{0,1},{1,5},{2,3},{3,7},{4,0},{5,4},{6,2},{7,6},{8,9},{9,13},{10,1... | collective-permute-start | bytes 786440 | tf_op jit(solution)/shard_map/ppermute | solution.py:405
  77.5 7.7 %collective-permute-start.25 = (bf16[1024,128]{1,0:T(8,128)(2,1)S(1)}, bf16[1024,128]{1,0:T(8,128)(2,1)S(1)}, u32[]{:S(2)}, u32[]{:S(2)}) collective-permute-start(bf16[1024,128]{1,0:T(8,128)(2,1)S(1)} %add_after.6.refs_2_.own_ref), channel_id=1, source_target_pairs={{1,4},{3,6},{4,1},{6,3},{9,12},{11,14},{12,9},{14,11},{17,20},{19,... | collective-permute-start | bytes 786440 | tf_op jit(solution)/shard_map/ppermute | solution.py:405
  79.5 1.4 %collective-permute-start.23 = (f32[256,128]{1,0:T(8,128)S(1)}, f32[256,128]{1,0:T(8,128)S(1)}, u32[]{:S(2)}, u32[]{:S(2)}) collective-permute-start(f32[256,128]{1,0:T(8,128)S(1)} %add_after.7.grad_ref), channel_id=1, source_target_pairs={{0,4},{1,5},{2,6},{3,7},{4,0},{5,1},{6,2},{7,3},{8,12},{9,13},{10,... | collective-permute-start | bytes 393224 | tf_op jit(solution)/shard_map/ppermute | solution.py:405

commit v20 on v18

--- a/solution.py
+++ b/solution.py
@@ -517,9 +517,9 @@
         two = send(value, lambda c, j, z: None if j == z % 2 else (c, 1 - j, z ^ 1))
         return one, two
 
-    act_later, back_part = lax.optimization_barrier((act, back_part))
+    act_later, direct = lax.optimization_barrier((act, direct))
     act_parts = [act, *deliver(act_later)]
-    grad = add_after([grad, grad_got], jnp.bfloat16, back_part)
+    grad = add_after([grad, grad_got], jnp.bfloat16, back_part, *act_parts[1:])
     step = 1
     while step < shape[0]:
         got = send(grad, lambda c, j, z, s=step: (c ^ s, j, z))

time: 85.8 us -> 89.5 us (1.043)
  starting transfers between devices: 40.6 us -> 42.6 us
  waiting for transfers between devices: 31.7 us -> 33.4 us
    ppermute x26, starting transfers between devices: 40.6 us -> 42.6 us  [send(): return lax.ppermute(value, AXES, route(shape, move))]
    ppermute x26, waiting for transfers between devices: 31.7 us -> 33.4 us  [send(): return lax.ppermute(value, AXES, route(shape, move))]
  transfers between devices with their start and end apart: 26 -> 26, of which waited for: 15 -> 15; matrix products, arithmetic and copies ran while one was open for 2% -> 2% of each run, Pallas kernels for 6% -> 8%
where the time goes in v20:
time: 89.5 us; the launch traced here: 89.2 us
  starting transfers between devices  42.6 us (48%)
  waiting for transfers between devices  33.4 us (37%)
  Pallas kernels  9.86 us (11%)
  local copies, waits for them, and re-layouts  2.43 us (3%)
    ppermute x26, starting transfers between devices, send(): return lax.ppermute(value, AXES, route(shape, move))  42.6 us
    ppermute x26, waiting for transfers between devices, send(): return lax.ppermute(value, AXES, route(shape, move))  33.4 us
    pallas_call x4, Pallas kernels, tile_product(): pl.pallas_call(functools.partial(tile_kernel, kinds, cases, [[case for ca...  5.3 us
  transfers between devices with their start and end apart: 26, of which 15 were waited for; matrix products, arithmetic and copies ran while one was open for 2% of the time, Pallas kernels for 8%

profile of v20, /device:TPU:1, one launch (start us, length us, event | category | flops | bytes accessed | tf_op | source)
XLA Modules:
  0.0 89.2 jit_solution(700994637842684288)
XLA Ops:
  0.6 2.2 %collective-permute-start = (bf16[5,8,128,128]{3,2,1,0:T(8,128)(2,1)}, bf16[5,8,128,128]{3,2,1,0:T(8,128)(2,1)S(1)}, u32[]{:S(2)}, u32[]{:S(2)}) collective-permute-start(bf16[5,8,128,128]{3,2,1,0:T(8,128)(2,1)} %bitcast.5), channel_id=1, source_target_pairs={{0,4},{1,0},{2,6},{3,2},{4,5},{5,1},{6,7},{7,3},{8,12},{9,8},{10,1... | collective-permute-start | bytes 3932168 | tf_op jit(solution)/shard_map/ppermute | solution.py:405
  2.8 1.1 %constant_dynamic-slice_fusion = (bf16[1024,128]{1,0:T(8,128)(2,1)S(1)}, bf16[1024,128]{1,0:T(8,128)(2,1)S(1)}) fusion(bf16[1024,256]{1,0:T(8,128)(2,1)} %param.6, s32[]{:T(128)S(6)} %select_n.15, s32[]{:T(128)S(6)} %select_n.14), kind=kLoop, calls=%fused_computation.2 | loop fusion | bytes 1048584 | tf_op jit(solution)/shard_map/dynamic_slice | solution.py:445
  3.9 0.7 collective-permute-start.2
  4.6 1.3 %collective-permute-start.3 = (bf16[1024,128]{1,0:T(8,128)(2,1)S(1)}, bf16[1024,128]{1,0:T(8,128)(2,1)S(1)}, u32[]{:S(2)}, u32[]{:S(2)}) collective-permute-start(bf16[1024,128]{1,0:T(8,128)(2,1)S(1)} %get-tuple-element.33), channel_id=1, source_target_pairs={{0,12},{1,21},{2,14},{3,23},{5,9},{7,11},{8,4},{10,6},{12,24},{13,... | collective-permute-start | bytes 786440 | tf_op jit(solution)/shard_map/ppermute | solution.py:405
  5.9 4.8 %collective-permute-start.4 = (bf16[1024,128]{1,0:T(8,128)(2,1)S(1)}, bf16[1024,128]{1,0:T(8,128)(2,1)S(1)}, u32[]{:S(2)}, u32[]{:S(2)}) collective-permute-start(bf16[1024,128]{1,0:T(8,128)(2,1)S(1)} %get-tuple-element.33), channel_id=1, source_target_pairs={{0,4},{1,5},{2,6},{3,7},{4,0},{5,1},{6,2},{7,3},{8,12},{9,13},{10,... | collective-permute-start | bytes 786440 | tf_op jit(solution)/shard_map/ppermute | solution.py:405
  10.6 0.7 copy.12
  11.3 0.7 copy-done.3
  12.0 1.3 %slot_blocks.1.refs_6_.refs_0_.refs_1_ = s32[2,40]{1,0:T(2,128)S(1)} custom-call(s32[2,5,8]{2,1,0:T(8,128)S(1)} %copy.10.coords_ref, s32[5]{0:T(128)S(1)} %bitcast.9), custom_call_target="tpu_custom_call" | custom-call | tf_op jit(solution)/shard_map/slot_blocks/pallas_call | solution.py:135
  13.6 1.8 %collective-permute-start.5 = (bf16[1024,128]{1,0:T(8,128)(2,1)S(1)}, bf16[1024,128]{1,0:T(8,128)(2,1)S(1)}, u32[]{:S(2)}, u32[]{:S(2)}) collective-permute-start(bf16[1024,128]{1,0:T(8,128)(2,1)S(1)} %get-tuple-element.19), channel_id=1, source_target_pairs={{0,16},{1,17},{2,18},{3,19},{4,20},{5,21},{6,22},{7,23},{8,24},{9,... | collective-permute-start | bytes 786440 | tf_op jit(solution)/shard_map/ppermute | solution.py:405
  15.4 1.2 %collective-permute-start.8 = (bf16[1024,128]{1,0:T(8,128)(2,1)S(1)}, bf16[1024,128]{1,0:T(8,128)(2,1)S(1)}, u32[]{:S(2)}, u32[]{:S(2)}) collective-permute-start(bf16[1024,128]{1,0:T(8,128)(2,1)S(1)} %get-tuple-element.23), channel_id=1, source_target_pairs={{0,8},{1,9},{2,10},{3,11},{4,12},{5,13},{6,14},{7,15},{8,0},{9,1},... | collective-permute-start | bytes 786440 | tf_op jit(solution)/shard_map/ppermute | solution.py:405
  16.6 0.2 collective-permute-start.1
  16.8 1.5 %collective-permute-done.1.refs_0_ = s32[2,40]{1,0:T(2,128)S(1)} collective-permute-done((s32[2,40]{1,0:T(2,128)S(1)}, s32[2,40]{1,0:T(2,128)S(1)}, u32[]{:S(2)}, u32[]{:S(2)}) %collective-permute-start.1) | collective-permute-done | bytes 352 | tf_op jit(solution)/shard_map/ppermute | solution.py:405
  18.3 1.3 %collective-permute-start.7 = (bf16[5,8,128,128]{3,2,1,0:T(8,128)(2,1)S(1)}, bf16[5,8,128,128]{3,2,1,0:T(8,128)(2,1)S(1)}, u32[]{:S(2)}, u32[]{:S(2)}) collective-permute-start(bf16[5,8,128,128]{3,2,1,0:T(8,128)(2,1)S(1)} %collective-permute-done.refs_1_.refs_3_), channel_id=1, source_target_pairs={{0,4},{2,6},{5,1},{7,3},{8,12},{10,14},{13,9},{15,11},{16,20},{18,... | collective-permute-start | bytes 3932168 | tf_op jit(solution)/shard_map/ppermute | solution.py:405
  19.6 1.9 %collective-permute-done.5.refs_8_.refs_10_ = bf16[1024,128]{1,0:T(8,128)(2,1)S(1)} collective-permute-done((bf16[1024,128]{1,0:T(8,128)(2,1)S(1)}, bf16[1024,128]{1,0:T(8,128)(2,1)S(1)}, u32[]{:S(2)}, u32[]{:S(2)}) %collective-permute-start.5) | collective-permute-done | bytes 262176 | tf_op jit(solution)/shard_map/ppermute | solution.py:405
  21.5 1.3 %collective-permute-start.6 = (s32[2,40]{1,0:T(2,128)S(1)}, s32[2,40]{1,0:T(2,128)S(1)}, u32[]{:S(2)}, u32[]{:S(2)}) collective-permute-start(s32[2,40]{1,0:T(2,128)S(1)} %collective-permute-done.1.refs_0_), channel_id=1, source_target_pairs={{0,4},{2,6},{5,1},{7,3},{8,12},{10,14},{13,9},{15,11},{16,20},{18,... | collective-permute-start | bytes 968 | tf_op jit(solution)/shard_map/ppermute | solution.py:405
  22.8 0.3 collective-permute-done.8.refs_9_.refs_11_
  23.0 1.2 %tile_product.4.refs_12_ = f32[1024,128]{1,0:T(8,128)S(1)} custom-call(s32[2,40]{1,0:T(2,128)S(1)} %collective-permute-done.1.refs_0_, bf16[5,8,128,128]{3,2,1,0:T(8,128)(2,1)S(1)} %collective-permute-done.refs_1_.refs_3_, bf16[1024,128]{1,0:T(8,128)(2,1)S(1)} %get-tuple-element.34.refs_3_.refs_2_.refs_5_.refs_4_.refs_7_, ...), custom_call_target="tpu_custom_call" | custom-call | flops 12582912000 | bytes 196608000 | tf_op jit(solution)/shard_map/tile_product/pallas_call | solution.py:210
  24.3 0.8 collective-permute-done.6.refs_1_.refs_2_
  25.0 1.4 %tile_product.5 = bf16[1024,128]{1,0:T(8,128)(2,1)S(1)} custom-call(s32[2,40]{1,0:T(2,128)S(1)} %slot_blocks.1.refs_6_.refs_0_.refs_1_, s32[2,40]{1,0:T(2,128)S(1)} %collective-permute-done.6.refs_1_.refs_2_, bf16[5,8,128,128]{3,2,1,0:T(8,128)(2,1)S(1)} %bitcast.6, bf16[5,8,128,128]{3,2,1,0:T(8,128)(2,1)S(1)} %collective-permute-done.7.refs_3_.refs_5_, ...), custom_call_target="tpu_custom_call" | custom-call | flops 167772160 | bytes 2621440 | tf_op jit(solution)/shard_map/tile_product/pallas_call | solution.py:210
  26.5 2.4 %collective-permute-start.9 = (bf16[1024,128]{1,0:T(8,128)(2,1)S(1)}, bf16[1024,128]{1,0:T(8,128)(2,1)S(1)}, u32[]{:S(2)}, u32[]{:S(2)}) collective-permute-start(bf16[1024,128]{1,0:T(8,128)(2,1)S(1)} %tile_product.5), channel_id=1, source_target_pairs={{0,2},{1,3},{2,0},{3,1},{4,6},{5,7},{6,4},{7,5},{8,10},{9,11},{10,... | collective-permute-start | bytes 786440 | tf_op jit(solution)/shard_map/ppermute | solution.py:405
  29.0 0.8 collective-permute-start.11
  29.7 10.9 %collective-permute-done.9 = bf16[1024,128]{1,0:T(8,128)(2,1)S(1)} collective-permute-done((bf16[1024,128]{1,0:T(8,128)(2,1)S(1)}, bf16[1024,128]{1,0:T(8,128)(2,1)S(1)}, u32[]{:S(2)}, u32[]{:S(2)}) %collective-permute-start.9) | collective-permute-done | bytes 262176 | tf_op jit(solution)/shard_map/ppermute | solution.py:405
  40.7 1.2 %collective-permute-start.10 = (bf16[1024,128]{1,0:T(8,128)(2,1)S(1)}, bf16[1024,128]{1,0:T(8,128)(2,1)S(1)}, u32[]{:S(2)}, u32[]{:S(2)}) collective-permute-start(bf16[1024,128]{1,0:T(8,128)(2,1)S(1)} %add_convert_fusion.near_ref), channel_id=1, source_target_pairs={{0,4},{1,5},{2,6},{3,7},{4,0},{5,1},{6,2},{7,3},{8,12},{9,13},{10,... | collective-permute-start | bytes 786440 | tf_op jit(solution)/shard_map/ppermute | solution.py:405
  41.9 1.2 %collective-permute-done.10.far_ref = bf16[1024,128]{1,0:T(8,128)(2,1)S(1)} collective-permute-done((bf16[1024,128]{1,0:T(8,128)(2,1)S(1)}, bf16[1024,128]{1,0:T(8,128)(2,1)S(1)}, u32[]{:S(2)}, u32[]{:S(2)}) %collective-permute-start.10) | collective-permute-done | bytes 262176 | tf_op jit(solution)/shard_map/ppermute | solution.py:405
  43.1 0.4 middle.1
  43.5 1.8 %collective-permute-start.12 = (bf16[1056,128]{1,0:T(8,128)(2,1)S(1)}, bf16[1056,128]{1,0:T(8,128)(2,1)S(1)}, u32[]{:S(2)}, u32[]{:S(2)}) collective-permute-start(bf16[1056,128]{1,0:T(8,128)(2,1)S(1)} %get-tuple-element.27), channel_id=1, source_target_pairs={{0,8},{1,9},{2,10},{3,11},{4,12},{5,13},{6,14},{7,15},{8,0},{9,1},... | collective-permute-start | bytes 811016 | tf_op jit(solution)/shard_map/ppermute | solution.py:405
  45.3 3.4 %collective-permute-start.19 = (bf16[1024,128]{1,0:T(8,128)(2,1)S(1)}, bf16[1024,128]{1,0:T(8,128)(2,1)S(1)}, u32[]{:S(2)}, u32[]{:S(2)}) collective-permute-start(bf16[1024,128]{1,0:T(8,128)(2,1)S(1)} %get-tuple-element.29.adj_ref.refs_6_), channel_id=1, source_target_pairs={{0,1},{2,3},{4,5},{6,7},{9,8},{11,10},{13,12},{15,14},{16,17},{18,... | collective-permute-start | bytes 786440 | tf_op jit(solution)/shard_map/ppermute | solution.py:405
  48.7 3.9 %collective-permute-done.17.refs_8_ = bf16[1040,128]{1,0:T(8,128)(2,1)S(1)} collective-permute-done((bf16[1040,128]{1,0:T(8,128)(2,1)S(1)}, bf16[1040,128]{1,0:T(8,128)(2,1)S(1)}, u32[]{:S(2)}, u32[]{:S(2)}) %collective-permute-start.17) | collective-permute-done | bytes 266272 | tf_op jit(solution)/shard_map/ppermute | solution.py:405
  52.6 1.3 %collective-permute-start.18 = (bf16[1040,128]{1,0:T(8,128)(2,1)S(1)}, bf16[1040,128]{1,0:T(8,128)(2,1)S(1)}, u32[]{:S(2)}, u32[]{:S(2)}) collective-permute-start(bf16[1040,128]{1,0:T(8,128)(2,1)S(1)} %collective-permute-done.17.refs_8_), channel_id=1, source_target_pairs={{0,8},{1,9},{2,10},{3,11},{4,12},{5,13},{6,14},{7,15},{8,0},{9,1},... | collective-permute-start | bytes 798728 | tf_op jit(solution)/shard_map/ppermute | solution.py:405
  53.9 0.9 collective-permute-start.16
  54.8 0.3 grad_block.1.refs_0_
  55.2 3.3 %collective-permute-start.13 = (bf16[1024,128]{1,0:T(8,128)(2,1)S(1)}, bf16[1024,128]{1,0:T(8,128)(2,1)S(1)}, u32[]{:S(2)}, u32[]{:S(2)}) collective-permute-start(bf16[1024,128]{1,0:T(8,128)(2,1)S(1)} %get-tuple-element.28.own_ref), channel_id=1, source_target_pairs={{0,1},{1,5},{2,3},{3,7},{4,0},{5,4},{6,2},{7,6},{8,9},{9,13},{10,1... | collective-permute-start | bytes 786440 | tf_op jit(solution)/shard_map/ppermute | solution.py:405
  58.6 5.6 %collective-permute-start.14 = (bf16[1024,128]{1,0:T(8,128)(2,1)S(1)}, bf16[1024,128]{1,0:T(8,128)(2,1)S(1)}, u32[]{:S(2)}, u32[]{:S(2)}) collective-permute-start(bf16[1024,128]{1,0:T(8,128)(2,1)S(1)} %get-tuple-element.28.own_ref), channel_id=1, source_target_pairs={{1,4},{3,6},{4,1},{6,3},{9,12},{11,14},{12,9},{14,11},{17,20},{19,... | collective-permute-start | bytes 786440 | tf_op jit(solution)/shard_map/ppermute | solution.py:405
  64.2 1.2 %tile_product.6.refs_10_ = f32[1024,128]{1,0:T(8,128)S(1)} custom-call(s32[2,40]{1,0:T(2,128)S(1)} %collective-permute-done.1.refs_0_, s32[2,40]{1,0:T(2,128)S(1)} %slot_blocks.1.refs_6_.refs_0_.refs_1_, s32[2,40]{1,0:T(2,128)S(1)} %collective-permute-done.6.refs_1_.refs_2_, bf16[5,8,128,128]{3,2,1,0:T(8,128)(2,1)S(1)} %collective-permute-done.refs_1_.refs_3_, ...), custom_call_target="tpu_custom_call" | custom-call | flops 134217728 | bytes 1572864 | tf_op jit(solution)/shard_map/tile_product/pallas_call | solution.py:210
  65.4 1.5 %tile_product.7.refs_2_.refs_0_ = bf16[1024,128]{1,0:T(8,128)(2,1)S(1)} custom-call(s32[2,40]{1,0:T(2,128)S(1)} %collective-permute-done.1.refs_0_, s32[2,40]{1,0:T(2,128)S(1)} %slot_blocks.1.refs_6_.refs_0_.refs_1_, s32[2,40]{1,0:T(2,128)S(1)} %collective-permute-done.6.refs_1_.refs_2_, bf16[5,8,128,128]{3,2,1,0:T(8,128)(2,1)S(1)} %collective-permute-done.refs_1_.refs_3_, ...), custom_call_target="tpu_custom_call" | custom-call | flops 201326592 | bytes 2359296 | tf_op jit(solution)/shard_map/tile_product/pallas_call | solution.py:210
  66.9 1.9 %collective-permute-start.22 = (bf16[1024,128]{1,0:T(8,128)(2,1)S(1)}, bf16[1024,128]{1,0:T(8,128)(2,1)S(1)}, u32[]{:S(2)}, u32[]{:S(2)}) collective-permute-start(bf16[1024,128]{1,0:T(8,128)(2,1)S(1)} %tile_product.7.refs_2_.refs_0_), channel_id=1, source_target_pairs={{0,2},{1,3},{2,0},{3,1},{4,6},{5,7},{6,4},{7,5},{8,10},{9,11},{10,... | collective-permute-start | bytes 786440 | tf_op jit(solution)/shard_map/ppermute | solution.py:405
  68.8 1.7 %collective-permute-start.20 = (bf16[256,128]{1,0:T(8,128)(2,1)S(1)}, bf16[256,128]{1,0:T(8,128)(2,1)S(1)}, u32[]{:S(2)}, u32[]{:S(2)}) collective-permute-start(bf16[256,128]{1,0:T(8,128)(2,1)S(1)} %add_after.4.refs_0_), channel_id=1, source_target_pairs={{0,8},{1,9},{2,10},{3,11},{4,12},{5,13},{6,14},{7,15},{8,0},{9,1},... | collective-permute-start | bytes 196616 | tf_op jit(solution)/shard_map/ppermute | solution.py:405
  70.6 2.0 %collective-permute-done.20.refs_1_ = bf16[256,128]{1,0:T(8,128)(2,1)S(1)} collective-permute-done((bf16[256,128]{1,0:T(8,128)(2,1)S(1)}, bf16[256,128]{1,0:T(8,128)(2,1)S(1)}, u32[]{:S(2)}, u32[]{:S(2)}) %collective-permute-start.20) | collective-permute-done | bytes 65568 | tf_op jit(solution)/shard_map/ppermute | solution.py:405
  72.5 1.1 %collective-permute-start.21 = (bf16[256,128]{1,0:T(8,128)(2,1)S(1)}, bf16[256,128]{1,0:T(8,128)(2,1)S(1)}, u32[]{:S(2)}, u32[]{:S(2)}) collective-permute-start(bf16[256,128]{1,0:T(8,128)(2,1)S(1)} %add_after.5.refs_0_), channel_id=1, source_target_pairs={{0,16},{1,17},{2,18},{3,19},{4,20},{5,21},{6,22},{7,23},{8,24},{9,... | collective-permute-start | bytes 196616 | tf_op jit(solution)/shard_map/ppermute | solution.py:405
  73.6 3.0 %collective-permute-done.21.refs_2_.refs_1_ = bf16[256,128]{1,0:T(8,128)(2,1)S(1)} collective-permute-done((bf16[256,128]{1,0:T(8,128)(2,1)S(1)}, bf16[256,128]{1,0:T(8,128)(2,1)S(1)}, u32[]{:S(2)}, u32[]{:S(2)}) %collective-permute-start.21) | collective-permute-done | bytes 65568 | tf_op jit(solution)/shard_map/ppermute | solution.py:405
  76.6 3.3 %collective-permute-done.22.refs_1_ = bf16[1024,128]{1,0:T(8,128)(2,1)S(1)} collective-permute-done((bf16[1024,128]{1,0:T(8,128)(2,1)S(1)}, bf16[1024,128]{1,0:T(8,128)(2,1)S(1)}, u32[]{:S(2)}, u32[]{:S(2)}) %collective-permute-start.22) | collective-permute-done | bytes 262176 | tf_op jit(solution)/shard_map/ppermute | solution.py:405
  79.9 0.5 collective-permute-start.24
  80.4 1.9 %collective-permute-start.25 = (bf16[1024,128]{1,0:T(8,128)(2,1)S(1)}, bf16[1024,128]{1,0:T(8,128)(2,1)S(1)}, u32[]{:S(2)}, u32[]{:S(2)}) collective-permute-start(bf16[1024,128]{1,0:T(8,128)(2,1)S(1)} %add_after.6.refs_2_.own_ref), channel_id=1, source_target_pairs={{1,4},{3,6},{4,1},{6,3},{9,12},{11,14},{12,9},{14,11},{17,20},{19,... | collective-permute-start | bytes 786440 | tf_op jit(solution)/shard_map/ppermute | solution.py:405
  82.4 1.3 %collective-permute-done.23.rest_ref = f32[256,128]{1,0:T(8,128)S(1)} collective-permute-done((f32[256,128]{1,0:T(8,128)S(1)}, f32[256,128]{1,0:T(8,128)S(1)}, u32[]{:S(2)}, u32[]{:S(2)}) %collective-permute-start.23) | collective-permute-done | bytes 131104 | tf_op jit(solution)/shard_map/ppermute | solution.py:405
  83.7 1.0 %gather_halves.1 = (bf16[1024,256]{1,0:T(8,128)(2,1)}, f32[256,256]{1,0:T(8,128)}) custom-call(bf16[1024,128]{1,0:T(8,128)(2,1)S(1)} %get-tuple-element.28.own_ref, bf16[1024,128]{1,0:T(8,128)(2,1)S(1)} %collective-permute-done.13.refs_3_.one_ref, bf16[1024,128]{1,0:T(8,128)(2,1)S(1)} %collective-permute-done.14.refs_4_.two_ref, ...), custom_call_target="tpu_custom_call" | custom-call | tf_op jit(solution)/shard_map/gather_halves/pallas_call | solution.py:349
  84.8 0.4 collective-permute-done.24.one_ref
  85.2 2.9 %collective-permute-done.25.two_ref = bf16[1024,128]{1,0:T(8,128)(2,1)S(1)} collective-permute-done((bf16[1024,128]{1,0:T(8,128)(2,1)S(1)}, bf16[1024,128]{1,0:T(8,128)(2,1)S(1)}, u32[]{:S(2)}, u32[]{:S(2)}) %collective-permute-start.25) | collective-permute-done | bytes 262176 | tf_op jit(solution)/shard_map/ppermute | solution.py:405
  88.0 1.1 %final.1 = bf16[1024,256]{1,0:T(8,128)(2,1)} custom-call(bf16[1024,128]{1,0:T(8,128)(2,1)S(1)} %add_after.6.refs_2_.own_ref, bf16[1024,128]{1,0:T(8,128)(2,1)S(1)} %collective-permute-done.24.one_ref, bf16[1024,128]{1,0:T(8,128)(2,1)S(1)} %collective-permute-done.25.two_ref, bf16[256,256]{1,0:T(8,128)(2,1)S(1)} %copy-done.2), custom_call_target="tpu_custom_call" | custom-call | flops 134217728 | bytes 2097152 | tf_op jit(solution)/shard_map/final/pallas_call | solution.py:383
  (31 shorter events, 0.8 us)
Async XLA Ops:
  0.6 17.7 %collective-permute-start = (bf16[5,8,128,128]{3,2,1,0:T(8,128)(2,1)}, bf16[5,8,128,128]{3,2,1,0:T(8,128)(2,1)S(1)}, u32[]{:S(2)}, u32[]{:S(2)}) collective-permute-start(bf16[5,8,128,128]{3,2,1,0:T(8,128)(2,1)} %bitcast.5), channel_id=1, source_target_pairs={{0,4},{1,0},{2,6},{3,2},{4,5},{5,1},{6,7},{7,3},{8,12},{9,8},{10,1... | collective-permute-start | bytes 3932168 | tf_op jit(solution)/shard_map/ppermute | solution.py:405
  3.9 9.5 %collective-permute-start.2 = (bf16[1024,128]{1,0:T(8,128)(2,1)S(1)}, bf16[1024,128]{1,0:T(8,128)(2,1)S(1)}, u32[]{:S(2)}, u32[]{:S(2)}) collective-permute-start(bf16[1024,128]{1,0:T(8,128)(2,1)S(1)} %get-tuple-element.34.refs_3_.refs_2_.refs_5_.refs_4_.refs_7_), channel_id=1, source_target_pairs={{0,8},{1,17},{2,10},{3,19},{5,13},{7,15},{8,0},{10,2},{12,28},{13,... | collective-permute-start | bytes 786440 | tf_op jit(solution)/shard_map/ppermute | solution.py:405
  4.6 8.9 %collective-permute-start.3 = (bf16[1024,128]{1,0:T(8,128)(2,1)S(1)}, bf16[1024,128]{1,0:T(8,128)(2,1)S(1)}, u32[]{:S(2)}, u32[]{:S(2)}) collective-permute-start(bf16[1024,128]{1,0:T(8,128)(2,1)S(1)} %get-tuple-element.33), channel_id=1, source_target_pairs={{0,12},{1,21},{2,14},{3,23},{5,9},{7,11},{8,4},{10,6},{12,24},{13,... | collective-permute-start | bytes 786440 | tf_op jit(solution)/shard_map/ppermute | solution.py:405
  5.9 7.6 %collective-permute-start.4 = (bf16[1024,128]{1,0:T(8,128)(2,1)S(1)}, bf16[1024,128]{1,0:T(8,128)(2,1)S(1)}, u32[]{:S(2)}, u32[]{:S(2)}) collective-permute-start(bf16[1024,128]{1,0:T(8,128)(2,1)S(1)} %get-tuple-element.33), channel_id=1, source_target_pairs={{0,4},{1,5},{2,6},{3,7},{4,0},{5,1},{6,2},{7,3},{8,12},{9,13},{10,... | collective-permute-start | bytes 786440 | tf_op jit(solution)/shard_map/ppermute | solution.py:405
  11.3 0.7 copy-start.3
  13.6 7.9 %collective-permute-start.5 = (bf16[1024,128]{1,0:T(8,128)(2,1)S(1)}, bf16[1024,128]{1,0:T(8,128)(2,1)S(1)}, u32[]{:S(2)}, u32[]{:S(2)}) collective-permute-start(bf16[1024,128]{1,0:T(8,128)(2,1)S(1)} %get-tuple-element.19), channel_id=1, source_target_pairs={{0,16},{1,17},{2,18},{3,19},{4,20},{5,21},{6,22},{7,23},{8,24},{9,... | collective-permute-start | bytes 786440 | tf_op jit(solution)/shard_map/ppermute | solution.py:405
  15.4 9.7 %copy-start = (bf16[1,5,8,128,128]{4,3,2,1,0:T(8,128)(2,1)S(1)}, bf16[1,5,8,128,128]{4,3,2,1,0:T(8,128)(2,1)}, u32[]{:S(2)}) copy-start(bf16[1,5,8,128,128]{4,3,2,1,0:T(8,128)(2,1)} %param.9) | copy-start | bytes 3932164
  15.4 7.6 %collective-permute-start.8 = (bf16[1024,128]{1,0:T(8,128)(2,1)S(1)}, bf16[1024,128]{1,0:T(8,128)(2,1)S(1)}, u32[]{:S(2)}, u32[]{:S(2)}) collective-permute-start(bf16[1024,128]{1,0:T(8,128)(2,1)S(1)} %get-tuple-element.23), channel_id=1, source_target_pairs={{0,8},{1,9},{2,10},{3,11},{4,12},{5,13},{6,14},{7,15},{8,0},{9,1},... | collective-permute-start | bytes 786440 | tf_op jit(solution)/shard_map/ppermute | solution.py:405
  16.6 1.7 %collective-permute-start.1 = (s32[2,40]{1,0:T(2,128)S(1)}, s32[2,40]{1,0:T(2,128)S(1)}, u32[]{:S(2)}, u32[]{:S(2)}) collective-permute-start(s32[2,40]{1,0:T(2,128)S(1)} %slot_blocks.1.refs_6_.refs_0_.refs_1_), channel_id=1, source_target_pairs={{0,4},{1,0},{2,6},{3,2},{4,5},{5,1},{6,7},{7,3},{8,12},{9,8},{10,1... | collective-permute-start | bytes 968 | tf_op jit(solution)/shard_map/ppermute | solution.py:405
  18.3 6.7 %collective-permute-start.7 = (bf16[5,8,128,128]{3,2,1,0:T(8,128)(2,1)S(1)}, bf16[5,8,128,128]{3,2,1,0:T(8,128)(2,1)S(1)}, u32[]{:S(2)}, u32[]{:S(2)}) collective-permute-start(bf16[5,8,128,128]{3,2,1,0:T(8,128)(2,1)S(1)} %collective-permute-done.refs_1_.refs_3_), channel_id=1, source_target_pairs={{0,4},{2,6},{5,1},{7,3},{8,12},{10,14},{13,9},{15,11},{16,20},{18,... | collective-permute-start | bytes 3932168 | tf_op jit(solution)/shard_map/ppermute | solution.py:405
  21.5 3.6 %collective-permute-start.6 = (s32[2,40]{1,0:T(2,128)S(1)}, s32[2,40]{1,0:T(2,128)S(1)}, u32[]{:S(2)}, u32[]{:S(2)}) collective-permute-start(s32[2,40]{1,0:T(2,128)S(1)} %collective-permute-done.1.refs_0_), channel_id=1, source_target_pairs={{0,4},{2,6},{5,1},{7,3},{8,12},{10,14},{13,9},{15,11},{16,20},{18,... | collective-permute-start | bytes 968 | tf_op jit(solution)/shard_map/ppermute | solution.py:405
  24.3 4.6 %copy-start.1 = (bf16[1024,256]{1,0:T(8,128)(2,1)S(1)}, bf16[1024,256]{1,0:T(8,128)(2,1)}, u32[]{:S(2)}) copy-start(bf16[1024,256]{1,0:T(8,128)(2,1)} %x_ref.1) | copy-start | bytes 1572868
  26.5 16.6 %copy-start.2 = (bf16[256,256]{1,0:T(8,128)(2,1)S(1)}, bf16[256,256]{1,0:T(8,128)(2,1)}, u32[]{:S(2)}) copy-start(bf16[256,256]{1,0:T(8,128)(2,1)} %w_ref.3) | copy-start | bytes 393220
  26.5 14.1 %collective-permute-start.9 = (bf16[1024,128]{1,0:T(8,128)(2,1)S(1)}, bf16[1024,128]{1,0:T(8,128)(2,1)S(1)}, u32[]{:S(2)}, u32[]{:S(2)}) collective-permute-start(bf16[1024,128]{1,0:T(8,128)(2,1)S(1)} %tile_product.5), channel_id=1, source_target_pairs={{0,2},{1,3},{2,0},{3,1},{4,6},{5,7},{6,4},{7,5},{8,10},{9,11},{10,... | collective-permute-start | bytes 786440 | tf_op jit(solution)/shard_map/ppermute | solution.py:405
  29.0 12.9 %collective-permute-start.11 = (bf16[1024,128]{1,0:T(8,128)(2,1)S(1)}, bf16[1024,128]{1,0:T(8,128)(2,1)S(1)}, u32[]{:S(2)}, u32[]{:S(2)}) collective-permute-start(bf16[1024,128]{1,0:T(8,128)(2,1)S(1)} %get-tuple-element.25), channel_id=1, source_target_pairs={{0,4},{1,5},{2,6},{3,7},{4,0},{5,1},{6,2},{7,3},{8,12},{9,13},{10,... | collective-permute-start | bytes 786440 | tf_op jit(solution)/shard_map/ppermute | solution.py:405
  40.7 2.4 %collective-permute-start.10 = (bf16[1024,128]{1,0:T(8,128)(2,1)S(1)}, bf16[1024,128]{1,0:T(8,128)(2,1)S(1)}, u32[]{:S(2)}, u32[]{:S(2)}) collective-permute-start(bf16[1024,128]{1,0:T(8,128)(2,1)S(1)} %add_convert_fusion.near_ref), channel_id=1, source_target_pairs={{0,4},{1,5},{2,6},{3,7},{4,0},{5,1},{6,2},{7,3},{8,12},{9,13},{10,... | collective-permute-start | bytes 786440 | tf_op jit(solution)/shard_map/ppermute | solution.py:405
  43.5 10.4 %collective-permute-start.12 = (bf16[1056,128]{1,0:T(8,128)(2,1)S(1)}, bf16[1056,128]{1,0:T(8,128)(2,1)S(1)}, u32[]{:S(2)}, u32[]{:S(2)}) collective-permute-start(bf16[1056,128]{1,0:T(8,128)(2,1)S(1)} %get-tuple-element.27), channel_id=1, source_target_pairs={{0,8},{1,9},{2,10},{3,11},{4,12},{5,13},{6,14},{7,15},{8,0},{9,1},... | collective-permute-start | bytes 811016 | tf_op jit(solution)/shard_map/ppermute | solution.py:405
  45.3 7.3 %collective-permute-start.17 = (bf16[1040,128]{1,0:T(8,128)(2,1)S(1)}, bf16[1040,128]{1,0:T(8,128)(2,1)S(1)}, u32[]{:S(2)}, u32[]{:S(2)}) collective-permute-start(bf16[1040,128]{1,0:T(8,128)(2,1)S(1)} %get-tuple-element.30), channel_id=1, source_target_pairs={{0,17},{1,0},{2,19},{3,2},{4,21},{5,4},{6,23},{7,6},{8,9},{9,24},{... | collective-permute-start | bytes 798728 | tf_op jit(solution)/shard_map/ppermute | solution.py:405
  45.3 20.0 %collective-permute-start.19 = (bf16[1024,128]{1,0:T(8,128)(2,1)S(1)}, bf16[1024,128]{1,0:T(8,128)(2,1)S(1)}, u32[]{:S(2)}, u32[]{:S(2)}) collective-permute-start(bf16[1024,128]{1,0:T(8,128)(2,1)S(1)} %get-tuple-element.29.adj_ref.refs_6_), channel_id=1, source_target_pairs={{0,1},{2,3},{4,5},{6,7},{9,8},{11,10},{13,12},{15,14},{16,17},{18,... | collective-permute-start | bytes 786440 | tf_op jit(solution)/shard_map/ppermute | solution.py:405
  52.6 12.8 %collective-permute-start.18 = (bf16[1040,128]{1,0:T(8,128)(2,1)S(1)}, bf16[1040,128]{1,0:T(8,128)(2,1)S(1)}, u32[]{:S(2)}, u32[]{:S(2)}) collective-permute-start(bf16[1040,128]{1,0:T(8,128)(2,1)S(1)} %collective-permute-done.17.refs_8_), channel_id=1, source_target_pairs={{0,8},{1,9},{2,10},{3,11},{4,12},{5,13},{6,14},{7,15},{8,0},{9,1},... | collective-permute-start | bytes 798728 | tf_op jit(solution)/shard_map/ppermute | solution.py:405
  53.9 11.5 %collective-permute-start.16 = (bf16[1056,128]{1,0:T(8,128)(2,1)S(1)}, bf16[1056,128]{1,0:T(8,128)(2,1)S(1)}, u32[]{:S(2)}, u32[]{:S(2)}) collective-permute-start(bf16[1056,128]{1,0:T(8,128)(2,1)S(1)} %collective-permute-done.12.refs_7_), channel_id=1, source_target_pairs={{0,16},{1,17},{2,18},{3,19},{4,20},{5,21},{6,22},{7,23},{8,24},{9,... | collective-permute-start | bytes 811016 | tf_op jit(solution)/shard_map/ppermute | solution.py:405
  55.1 3.5 %collective-permute-start.15 = (bf16[256,128]{1,0:T(8,128)(2,1)S(1)}, bf16[256,128]{1,0:T(8,128)(2,1)S(1)}, u32[]{:S(2)}, u32[]{:S(2)}) collective-permute-start(bf16[256,128]{1,0:T(8,128)(2,1)S(1)} %grad_block.1.refs_0_), channel_id=1, source_target_pairs={{0,1},{1,0},{2,3},{3,2},{4,5},{5,4},{6,7},{7,6},{8,9},{9,8},{10,11... | collective-permute-start | bytes 196616 | tf_op jit(solution)/shard_map/ppermute | solution.py:405
  55.2 13.6 %collective-permute-start.13 = (bf16[1024,128]{1,0:T(8,128)(2,1)S(1)}, bf16[1024,128]{1,0:T(8,128)(2,1)S(1)}, u32[]{:S(2)}, u32[]{:S(2)}) collective-permute-start(bf16[1024,128]{1,0:T(8,128)(2,1)S(1)} %get-tuple-element.28.own_ref), channel_id=1, source_target_pairs={{0,1},{1,5},{2,3},{3,7},{4,0},{5,4},{6,2},{7,6},{8,9},{9,13},{10,1... | collective-permute-start | bytes 786440 | tf_op jit(solution)/shard_map/ppermute | solution.py:405
  58.6 10.2 %collective-permute-start.14 = (bf16[1024,128]{1,0:T(8,128)(2,1)S(1)}, bf16[1024,128]{1,0:T(8,128)(2,1)S(1)}, u32[]{:S(2)}, u32[]{:S(2)}) collective-permute-start(bf16[1024,128]{1,0:T(8,128)(2,1)S(1)} %get-tuple-element.28.own_ref), channel_id=1, source_target_pairs={{1,4},{3,6},{4,1},{6,3},{9,12},{11,14},{12,9},{14,11},{17,20},{19,... | collective-permute-start | bytes 786440 | tf_op jit(solution)/shard_map/ppermute | solution.py:405
  66.9 12.9 %collective-permute-start.22 = (bf16[1024,128]{1,0:T(8,128)(2,1)S(1)}, bf16[1024,128]{1,0:T(8,128)(2,1)S(1)}, u32[]{:S(2)}, u32[]{:S(2)}) collective-permute-start(bf16[1024,128]{1,0:T(8,128)(2,1)S(1)} %tile_product.7.refs_2_.refs_0_), channel_id=1, source_target_pairs={{0,2},{1,3},{2,0},{3,1},{4,6},{5,7},{6,4},{7,5},{8,10},{9,11},{10,... | collective-permute-start | bytes 786440 | tf_op jit(solution)/shard_map/ppermute | solution.py:405
  68.8 3.7 %collective-permute-start.20 = (bf16[256,128]{1,0:T(8,128)(2,1)S(1)}, bf16[256,128]{1,0:T(8,128)(2,1)S(1)}, u32[]{:S(2)}, u32[]{:S(2)}) collective-permute-start(bf16[256,128]{1,0:T(8,128)(2,1)S(1)} %add_after.4.refs_0_), channel_id=1, source_target_pairs={{0,8},{1,9},{2,10},{3,11},{4,12},{5,13},{6,14},{7,15},{8,0},{9,1},... | collective-permute-start | bytes 196616 | tf_op jit(solution)/shard_map/ppermute | solution.py:405
  72.5 4.1 %collective-permute-start.21 = (bf16[256,128]{1,0:T(8,128)(2,1)S(1)}, bf16[256,128]{1,0:T(8,128)(2,1)S(1)}, u32[]{:S(2)}, u32[]{:S(2)}) collective-permute-start(bf16[256,128]{1,0:T(8,128)(2,1)S(1)} %add_after.5.refs_0_), channel_id=1, source_target_pairs={{0,16},{1,17},{2,18},{3,19},{4,20},{5,21},{6,22},{7,23},{8,24},{9,... | collective-permute-start | bytes 196616 | tf_op jit(solution)/shard_map/ppermute | solution.py:405
  79.9 5.3 %collective-permute-start.24 = (bf16[1024,128]{1,0:T(8,128)(2,1)S(1)}, bf16[1024,128]{1,0:T(8,128)(2,1)S(1)}, u32[]{:S(2)}, u32[]{:S(2)}) collective-permute-start(bf16[1024,128]{1,0:T(8,128)(2,1)S(1)} %add_after.6.refs_2_.own_ref), channel_id=1, source_target_pairs={{0,1},{1,5},{2,3},{3,7},{4,0},{5,4},{6,2},{7,6},{8,9},{9,13},{10,1... | collective-permute-start | bytes 786440 | tf_op jit(solution)/shard_map/ppermute | solution.py:405
  80.4 7.7 %collective-permute-start.25 = (bf16[1024,128]{1,0:T(8,128)(2,1)S(1)}, bf16[1024,128]{1,0:T(8,128)(2,1)S(1)}, u32[]{:S(2)}, u32[]{:S(2)}) collective-permute-start(bf16[1024,128]{1,0:T(8,128)(2,1)S(1)} %add_after.6.refs_2_.own_ref), channel_id=1, source_target_pairs={{1,4},{3,6},{4,1},{6,3},{9,12},{11,14},{12,9},{14,11},{17,20},{19,... | collective-permute-start | bytes 786440 | tf_op jit(solution)/shard_map/ppermute | solution.py:405
  82.3 1.4 %collective-permute-start.23 = (f32[256,128]{1,0:T(8,128)S(1)}, f32[256,128]{1,0:T(8,128)S(1)}, u32[]{:S(2)}, u32[]{:S(2)}) collective-permute-start(f32[256,128]{1,0:T(8,128)S(1)} %add_after.7.grad_ref), channel_id=1, source_target_pairs={{0,4},{1,5},{2,6},{3,7},{4,0},{5,1},{6,2},{7,3},{8,12},{9,13},{10,... | collective-permute-start | bytes 393224 | tf_op jit(solution)/shard_map/ppermute | solution.py:405

commit v21 on v18

--- a/solution.py
+++ b/solution.py
@@ -491,11 +491,11 @@
         near, far_half, weight, cot, send(cot_yours, sibling)
     )
 
-    direct = send(adj_longer, to_direct)
+    direct = send(adj_long, to_direct)
     near_one = send(
-        adj_long, lambda c, j, z: (c if (c + z) % 2 or not four else c ^ 2, j, z ^ 1)
+        adj_longer, lambda c, j, z: (c if (c + z) % 2 or not four else c ^ 2, j, z ^ 1)
     )
-    second = send(direct if four else adj_longer, to_second)
+    second = send(direct if four else adj_long, to_second)
     grad = grad_block(scale, near, far_half, adj)
     far = send(near_one, to_far)
     near_choice = [("still", near_one)]

time: 85.8 us -> 85.7 us (level)
  no operation moved by 1% of the time
where the time goes in v21:
time: 85.7 us; the launch traced here: 85.4 us
  starting transfers between devices  40.7 us (47%)
  waiting for transfers between devices  31.6 us (37%)
  Pallas kernels  9.76 us (11%)
  local copies, waits for them, and re-layouts  2.43 us (3%)
  between operations  0.86 us (1%)
    ppermute x26, starting transfers between devices, send(): return lax.ppermute(value, AXES, route(shape, move))  40.7 us
    ppermute x26, waiting for transfers between devices, send(): return lax.ppermute(value, AXES, route(shape, move))  31.6 us
    pallas_call x4, Pallas kernels, tile_product(): pl.pallas_call(functools.partial(tile_kernel, kinds, cases, [[case for ca...  5.22 us
  transfers between devices with their start and end apart: 26, of which 15 were waited for; matrix products, arithmetic and copies ran while one was open for 2% of the time, Pallas kernels for 6%

profile of v21, /device:TPU:1, one launch (start us, length us, event | category | flops | bytes accessed | tf_op | source)
XLA Modules:
  0.0 85.4 jit_solution(2194181778272580867)
XLA Ops:
  0.6 2.2 %collective-permute-start = (bf16[5,8,128,128]{3,2,1,0:T(8,128)(2,1)}, bf16[5,8,128,128]{3,2,1,0:T(8,128)(2,1)S(1)}, u32[]{:S(2)}, u32[]{:S(2)}) collective-permute-start(bf16[5,8,128,128]{3,2,1,0:T(8,128)(2,1)} %bitcast.5), channel_id=1, source_target_pairs={{0,4},{1,0},{2,6},{3,2},{4,5},{5,1},{6,7},{7,3},{8,12},{9,8},{10,1... | collective-permute-start | bytes 3932168 | tf_op jit(solution)/shard_map/ppermute | solution.py:405
  2.8 1.1 %constant_dynamic-slice_fusion = (bf16[1024,128]{1,0:T(8,128)(2,1)S(1)}, bf16[1024,128]{1,0:T(8,128)(2,1)S(1)}) fusion(bf16[1024,256]{1,0:T(8,128)(2,1)} %param.6, s32[]{:T(128)S(6)} %select_n.15, s32[]{:T(128)S(6)} %select_n.14), kind=kLoop, calls=%fused_computation.2 | loop fusion | bytes 1048584 | tf_op jit(solution)/shard_map/dynamic_slice | solution.py:445
  3.9 0.7 collective-permute-start.2
  4.6 1.3 %collective-permute-start.3 = (bf16[1024,128]{1,0:T(8,128)(2,1)S(1)}, bf16[1024,128]{1,0:T(8,128)(2,1)S(1)}, u32[]{:S(2)}, u32[]{:S(2)}) collective-permute-start(bf16[1024,128]{1,0:T(8,128)(2,1)S(1)} %get-tuple-element.35), channel_id=1, source_target_pairs={{0,12},{1,21},{2,14},{3,23},{5,9},{7,11},{8,4},{10,6},{12,24},{13,... | collective-permute-start | bytes 786440 | tf_op jit(solution)/shard_map/ppermute | solution.py:405
  5.9 4.8 %collective-permute-start.4 = (bf16[1024,128]{1,0:T(8,128)(2,1)S(1)}, bf16[1024,128]{1,0:T(8,128)(2,1)S(1)}, u32[]{:S(2)}, u32[]{:S(2)}) collective-permute-start(bf16[1024,128]{1,0:T(8,128)(2,1)S(1)} %get-tuple-element.35), channel_id=1, source_target_pairs={{0,4},{1,5},{2,6},{3,7},{4,0},{5,1},{6,2},{7,3},{8,12},{9,13},{10,... | collective-permute-start | bytes 786440 | tf_op jit(solution)/shard_map/ppermute | solution.py:405
  10.6 0.7 copy.12
  11.3 0.7 copy-done.3
  12.0 1.3 %slot_blocks.1.refs_6_.refs_0_.refs_1_ = s32[2,40]{1,0:T(2,128)S(1)} custom-call(s32[2,5,8]{2,1,0:T(8,128)S(1)} %copy.10.coords_ref, s32[5]{0:T(128)S(1)} %bitcast.9), custom_call_target="tpu_custom_call" | custom-call | tf_op jit(solution)/shard_map/slot_blocks/pallas_call | solution.py:135
  13.6 1.8 %collective-permute-start.5 = (bf16[1024,128]{1,0:T(8,128)(2,1)S(1)}, bf16[1024,128]{1,0:T(8,128)(2,1)S(1)}, u32[]{:S(2)}, u32[]{:S(2)}) collective-permute-start(bf16[1024,128]{1,0:T(8,128)(2,1)S(1)} %get-tuple-element.20), channel_id=1, source_target_pairs={{0,16},{1,17},{2,18},{3,19},{4,20},{5,21},{6,22},{7,23},{8,24},{9,... | collective-permute-start | bytes 786440 | tf_op jit(solution)/shard_map/ppermute | solution.py:405
  15.4 1.2 %collective-permute-start.8 = (bf16[1024,128]{1,0:T(8,128)(2,1)S(1)}, bf16[1024,128]{1,0:T(8,128)(2,1)S(1)}, u32[]{:S(2)}, u32[]{:S(2)}) collective-permute-start(bf16[1024,128]{1,0:T(8,128)(2,1)S(1)} %get-tuple-element.24), channel_id=1, source_target_pairs={{0,8},{1,9},{2,10},{3,11},{4,12},{5,13},{6,14},{7,15},{8,0},{9,1},... | collective-permute-start | bytes 786440 | tf_op jit(solution)/shard_map/ppermute | solution.py:405
  16.8 1.5 %collective-permute-done.1.refs_0_ = s32[2,40]{1,0:T(2,128)S(1)} collective-permute-done((s32[2,40]{1,0:T(2,128)S(1)}, s32[2,40]{1,0:T(2,128)S(1)}, u32[]{:S(2)}, u32[]{:S(2)}) %collective-permute-start.1) | collective-permute-done | bytes 352 | tf_op jit(solution)/shard_map/ppermute | solution.py:405
  18.3 1.3 %collective-permute-start.7 = (bf16[5,8,128,128]{3,2,1,0:T(8,128)(2,1)S(1)}, bf16[5,8,128,128]{3,2,1,0:T(8,128)(2,1)S(1)}, u32[]{:S(2)}, u32[]{:S(2)}) collective-permute-start(bf16[5,8,128,128]{3,2,1,0:T(8,128)(2,1)S(1)} %collective-permute-done.refs_1_.refs_3_), channel_id=1, source_target_pairs={{0,4},{2,6},{5,1},{7,3},{8,12},{10,14},{13,9},{15,11},{16,20},{18,... | collective-permute-start | bytes 3932168 | tf_op jit(solution)/shard_map/ppermute | solution.py:405
  19.6 1.9 %collective-permute-done.5.refs_8_.refs_10_ = bf16[1024,128]{1,0:T(8,128)(2,1)S(1)} collective-permute-done((bf16[1024,128]{1,0:T(8,128)(2,1)S(1)}, bf16[1024,128]{1,0:T(8,128)(2,1)S(1)}, u32[]{:S(2)}, u32[]{:S(2)}) %collective-permute-start.5) | collective-permute-done | bytes 262176 | tf_op jit(solution)/shard_map/ppermute | solution.py:405
  21.5 1.3 %collective-permute-start.6 = (s32[2,40]{1,0:T(2,128)S(1)}, s32[2,40]{1,0:T(2,128)S(1)}, u32[]{:S(2)}, u32[]{:S(2)}) collective-permute-start(s32[2,40]{1,0:T(2,128)S(1)} %collective-permute-done.1.refs_0_), channel_id=1, source_target_pairs={{0,4},{2,6},{5,1},{7,3},{8,12},{10,14},{13,9},{15,11},{16,20},{18,... | collective-permute-start | bytes 968 | tf_op jit(solution)/shard_map/ppermute | solution.py:405
  22.8 0.3 collective-permute-done.8.refs_9_.refs_11_
  23.0 1.2 %tile_product.4.refs_12_ = f32[1024,128]{1,0:T(8,128)S(1)} custom-call(s32[2,40]{1,0:T(2,128)S(1)} %collective-permute-done.1.refs_0_, bf16[5,8,128,128]{3,2,1,0:T(8,128)(2,1)S(1)} %collective-permute-done.refs_1_.refs_3_, bf16[1024,128]{1,0:T(8,128)(2,1)S(1)} %get-tuple-element.36.refs_3_.refs_2_.refs_5_.refs_4_.refs_7_, ...), custom_call_target="tpu_custom_call" | custom-call | flops 12582912000 | bytes 196608000 | tf_op jit(solution)/shard_map/tile_product/pallas_call | solution.py:210
  24.3 0.8 collective-permute-done.6.refs_1_.refs_2_
  25.0 1.4 %tile_product.5 = bf16[1024,128]{1,0:T(8,128)(2,1)S(1)} custom-call(s32[2,40]{1,0:T(2,128)S(1)} %slot_blocks.1.refs_6_.refs_0_.refs_1_, s32[2,40]{1,0:T(2,128)S(1)} %collective-permute-done.6.refs_1_.refs_2_, bf16[5,8,128,128]{3,2,1,0:T(8,128)(2,1)S(1)} %bitcast.6, bf16[5,8,128,128]{3,2,1,0:T(8,128)(2,1)S(1)} %collective-permute-done.7.refs_3_.refs_5_, ...), custom_call_target="tpu_custom_call" | custom-call | flops 167772160 | bytes 2621440 | tf_op jit(solution)/shard_map/tile_product/pallas_call | solution.py:210
  26.5 2.4 %collective-permute-start.9 = (bf16[1024,128]{1,0:T(8,128)(2,1)S(1)}, bf16[1024,128]{1,0:T(8,128)(2,1)S(1)}, u32[]{:S(2)}, u32[]{:S(2)}) collective-permute-start(bf16[1024,128]{1,0:T(8,128)(2,1)S(1)} %tile_product.5), channel_id=1, source_target_pairs={{0,2},{1,3},{2,0},{3,1},{4,6},{5,7},{6,4},{7,5},{8,10},{9,11},{10,... | collective-permute-start | bytes 786440 | tf_op jit(solution)/shard_map/ppermute | solution.py:405
  29.0 0.8 collective-permute-start.11
  29.8 10.8 %collective-permute-done.9 = bf16[1024,128]{1,0:T(8,128)(2,1)S(1)} collective-permute-done((bf16[1024,128]{1,0:T(8,128)(2,1)S(1)}, bf16[1024,128]{1,0:T(8,128)(2,1)S(1)}, u32[]{:S(2)}, u32[]{:S(2)}) %collective-permute-start.9) | collective-permute-done | bytes 262176 | tf_op jit(solution)/shard_map/ppermute | solution.py:405
  40.7 1.2 %collective-permute-start.10 = (bf16[1024,128]{1,0:T(8,128)(2,1)S(1)}, bf16[1024,128]{1,0:T(8,128)(2,1)S(1)}, u32[]{:S(2)}, u32[]{:S(2)}) collective-permute-start(bf16[1024,128]{1,0:T(8,128)(2,1)S(1)} %add_convert_fusion.near_ref), channel_id=1, source_target_pairs={{0,4},{1,5},{2,6},{3,7},{4,0},{5,1},{6,2},{7,3},{8,12},{9,13},{10,... | collective-permute-start | bytes 786440 | tf_op jit(solution)/shard_map/ppermute | solution.py:405
  41.9 1.2 %collective-permute-done.10.far_ref = bf16[1024,128]{1,0:T(8,128)(2,1)S(1)} collective-permute-done((bf16[1024,128]{1,0:T(8,128)(2,1)S(1)}, bf16[1024,128]{1,0:T(8,128)(2,1)S(1)}, u32[]{:S(2)}, u32[]{:S(2)}) %collective-permute-start.10) | collective-permute-done | bytes 262176 | tf_op jit(solution)/shard_map/ppermute | solution.py:405
  43.1 0.4 middle.1
  43.5 1.8 %collective-permute-start.14 = (bf16[1056,128]{1,0:T(8,128)(2,1)S(1)}, bf16[1056,128]{1,0:T(8,128)(2,1)S(1)}, u32[]{:S(2)}, u32[]{:S(2)}) collective-permute-start(bf16[1056,128]{1,0:T(8,128)(2,1)S(1)} %get-tuple-element.29), channel_id=1, source_target_pairs={{0,17},{1,0},{2,19},{3,2},{4,21},{5,4},{6,23},{7,6},{8,9},{9,24},{... | collective-permute-start | bytes 811016 | tf_op jit(solution)/shard_map/ppermute | solution.py:405
  45.4 3.3 %collective-permute-start.16 = (bf16[1024,128]{1,0:T(8,128)(2,1)S(1)}, bf16[1024,128]{1,0:T(8,128)(2,1)S(1)}, u32[]{:S(2)}, u32[]{:S(2)}) collective-permute-start(bf16[1024,128]{1,0:T(8,128)(2,1)S(1)} %get-tuple-element.30.refs_6_.adj_ref), channel_id=1, source_target_pairs={{0,1},{2,3},{4,5},{6,7},{9,8},{11,10},{13,12},{15,14},{16,17},{18,... | collective-permute-start | bytes 786440 | tf_op jit(solution)/shard_map/ppermute | solution.py:405
  48.7 3.8 %collective-permute-done.12.refs_7_ = bf16[1040,128]{1,0:T(8,128)(2,1)S(1)} collective-permute-done((bf16[1040,128]{1,0:T(8,128)(2,1)S(1)}, bf16[1040,128]{1,0:T(8,128)(2,1)S(1)}, u32[]{:S(2)}, u32[]{:S(2)}) %collective-permute-start.12) | collective-permute-done | bytes 266272 | tf_op jit(solution)/shard_map/ppermute | solution.py:405
  52.5 0.2 collective-permute-start.13
  52.7 1.2 %collective-permute-start.15 = (bf16[1056,128]{1,0:T(8,128)(2,1)S(1)}, bf16[1056,128]{1,0:T(8,128)(2,1)S(1)}, u32[]{:S(2)}, u32[]{:S(2)}) collective-permute-start(bf16[1056,128]{1,0:T(8,128)(2,1)S(1)} %collective-permute-done.14.refs_8_), channel_id=1, source_target_pairs={{0,8},{1,9},{2,10},{3,11},{4,12},{5,13},{6,14},{7,15},{8,0},{9,1},... | collective-permute-start | bytes 811016 | tf_op jit(solution)/shard_map/ppermute | solution.py:405
  53.9 0.3 grad_block.1.refs_0_
  54.2 1.4 %collective-permute-start.17 = (bf16[256,128]{1,0:T(8,128)(2,1)S(1)}, bf16[256,128]{1,0:T(8,128)(2,1)S(1)}, u32[]{:S(2)}, u32[]{:S(2)}) collective-permute-start(bf16[256,128]{1,0:T(8,128)(2,1)S(1)} %grad_block.1.refs_0_), channel_id=1, source_target_pairs={{0,1},{1,0},{2,3},{3,2},{4,5},{5,4},{6,7},{7,6},{8,9},{9,8},{10,11... | collective-permute-start | bytes 196616 | tf_op jit(solution)/shard_map/ppermute | solution.py:405
  55.6 1.1 %tile_product.6.refs_10_ = f32[1024,128]{1,0:T(8,128)S(1)} custom-call(s32[2,40]{1,0:T(2,128)S(1)} %collective-permute-done.1.refs_0_, s32[2,40]{1,0:T(2,128)S(1)} %slot_blocks.1.refs_6_.refs_0_.refs_1_, s32[2,40]{1,0:T(2,128)S(1)} %collective-permute-done.6.refs_1_.refs_2_, bf16[5,8,128,128]{3,2,1,0:T(8,128)(2,1)S(1)} %collective-permute-done.refs_1_.refs_3_, ...), custom_call_target="tpu_custom_call" | custom-call | flops 134217728 | bytes 1572864 | tf_op jit(solution)/shard_map/tile_product/pallas_call | solution.py:210
  56.8 1.0 %collective-permute-done.17.refs_11_.refs_1_ = bf16[256,128]{1,0:T(8,128)(2,1)S(1)} collective-permute-done((bf16[256,128]{1,0:T(8,128)(2,1)S(1)}, bf16[256,128]{1,0:T(8,128)(2,1)S(1)}, u32[]{:S(2)}, u32[]{:S(2)}) %collective-permute-start.17) | collective-permute-done | bytes 65568 | tf_op jit(solution)/shard_map/ppermute | solution.py:405
  57.7 1.1 %collective-permute-done.13.refs_6_ = bf16[1040,128]{1,0:T(8,128)(2,1)S(1)} collective-permute-done((bf16[1040,128]{1,0:T(8,128)(2,1)S(1)}, bf16[1040,128]{1,0:T(8,128)(2,1)S(1)}, u32[]{:S(2)}, u32[]{:S(2)}) %collective-permute-start.13) | collective-permute-done | bytes 266272 | tf_op jit(solution)/shard_map/ppermute | solution.py:405
  59.0 1.5 %tile_product.7.refs_2_.refs_0_ = bf16[1024,128]{1,0:T(8,128)(2,1)S(1)} custom-call(s32[2,40]{1,0:T(2,128)S(1)} %collective-permute-done.1.refs_0_, s32[2,40]{1,0:T(2,128)S(1)} %slot_blocks.1.refs_6_.refs_0_.refs_1_, s32[2,40]{1,0:T(2,128)S(1)} %collective-permute-done.6.refs_1_.refs_2_, bf16[5,8,128,128]{3,2,1,0:T(8,128)(2,1)S(1)} %collective-permute-done.refs_1_.refs_3_, ...), custom_call_target="tpu_custom_call" | custom-call | flops 201326592 | bytes 2359296 | tf_op jit(solution)/shard_map/tile_product/pallas_call | solution.py:210
  60.5 3.0 %collective-permute-start.22 = (bf16[1024,128]{1,0:T(8,128)(2,1)S(1)}, bf16[1024,128]{1,0:T(8,128)(2,1)S(1)}, u32[]{:S(2)}, u32[]{:S(2)}) collective-permute-start(bf16[1024,128]{1,0:T(8,128)(2,1)S(1)} %tile_product.7.refs_2_.refs_0_), channel_id=1, source_target_pairs={{0,2},{1,3},{2,0},{3,1},{4,6},{5,7},{6,4},{7,5},{8,10},{9,11},{10,... | collective-permute-start | bytes 786440 | tf_op jit(solution)/shard_map/ppermute | solution.py:405
  63.5 0.7 collective-permute-start.20
  64.2 2.8 %collective-permute-start.18 = (bf16[1024,128]{1,0:T(8,128)(2,1)S(1)}, bf16[1024,128]{1,0:T(8,128)(2,1)S(1)}, u32[]{:S(2)}, u32[]{:S(2)}) collective-permute-start(bf16[1024,128]{1,0:T(8,128)(2,1)S(1)} %get-tuple-element.31.own_ref), channel_id=1, source_target_pairs={{0,1},{1,5},{2,3},{3,7},{4,0},{5,4},{6,2},{7,6},{8,9},{9,13},{10,1... | collective-permute-start | bytes 786440 | tf_op jit(solution)/shard_map/ppermute | solution.py:405
  67.0 2.5 %collective-permute-start.19 = (bf16[1024,128]{1,0:T(8,128)(2,1)S(1)}, bf16[1024,128]{1,0:T(8,128)(2,1)S(1)}, u32[]{:S(2)}, u32[]{:S(2)}) collective-permute-start(bf16[1024,128]{1,0:T(8,128)(2,1)S(1)} %get-tuple-element.31.own_ref), channel_id=1, source_target_pairs={{1,4},{3,6},{4,1},{6,3},{9,12},{11,14},{12,9},{14,11},{17,20},{19,... | collective-permute-start | bytes 786440 | tf_op jit(solution)/shard_map/ppermute | solution.py:405
  69.5 1.0 %collective-permute-start.21 = (bf16[256,128]{1,0:T(8,128)(2,1)S(1)}, bf16[256,128]{1,0:T(8,128)(2,1)S(1)}, u32[]{:S(2)}, u32[]{:S(2)}) collective-permute-start(bf16[256,128]{1,0:T(8,128)(2,1)S(1)} %add_after.5.refs_0_), channel_id=1, source_target_pairs={{0,16},{1,17},{2,18},{3,19},{4,20},{5,21},{6,22},{7,23},{8,24},{9,... | collective-permute-start | bytes 196616 | tf_op jit(solution)/shard_map/ppermute | solution.py:405
  70.5 2.5 %collective-permute-done.21.refs_2_.refs_1_ = bf16[256,128]{1,0:T(8,128)(2,1)S(1)} collective-permute-done((bf16[256,128]{1,0:T(8,128)(2,1)S(1)}, bf16[256,128]{1,0:T(8,128)(2,1)S(1)}, u32[]{:S(2)}, u32[]{:S(2)}) %collective-permute-start.21) | collective-permute-done | bytes 65568 | tf_op jit(solution)/shard_map/ppermute | solution.py:405
  73.0 2.1 %collective-permute-done.22.refs_1_ = bf16[1024,128]{1,0:T(8,128)(2,1)S(1)} collective-permute-done((bf16[1024,128]{1,0:T(8,128)(2,1)S(1)}, bf16[1024,128]{1,0:T(8,128)(2,1)S(1)}, u32[]{:S(2)}, u32[]{:S(2)}) %collective-permute-start.22) | collective-permute-done | bytes 262176 | tf_op jit(solution)/shard_map/ppermute | solution.py:405
  75.1 1.5 %collective-permute-start.24 = (bf16[1024,128]{1,0:T(8,128)(2,1)S(1)}, bf16[1024,128]{1,0:T(8,128)(2,1)S(1)}, u32[]{:S(2)}, u32[]{:S(2)}) collective-permute-start(bf16[1024,128]{1,0:T(8,128)(2,1)S(1)} %add_after.6.refs_2_.own_ref), channel_id=1, source_target_pairs={{0,1},{1,5},{2,3},{3,7},{4,0},{5,4},{6,2},{7,6},{8,9},{9,13},{10,1... | collective-permute-start | bytes 786440 | tf_op jit(solution)/shard_map/ppermute | solution.py:405
  76.6 2.1 %collective-permute-start.25 = (bf16[1024,128]{1,0:T(8,128)(2,1)S(1)}, bf16[1024,128]{1,0:T(8,128)(2,1)S(1)}, u32[]{:S(2)}, u32[]{:S(2)}) collective-permute-start(bf16[1024,128]{1,0:T(8,128)(2,1)S(1)} %add_after.6.refs_2_.own_ref), channel_id=1, source_target_pairs={{1,4},{3,6},{4,1},{6,3},{9,12},{11,14},{12,9},{14,11},{17,20},{19,... | collective-permute-start | bytes 786440 | tf_op jit(solution)/shard_map/ppermute | solution.py:405
  78.8 1.3 %collective-permute-done.23.rest_ref = f32[256,128]{1,0:T(8,128)S(1)} collective-permute-done((f32[256,128]{1,0:T(8,128)S(1)}, f32[256,128]{1,0:T(8,128)S(1)}, u32[]{:S(2)}, u32[]{:S(2)}) %collective-permute-start.23) | collective-permute-done | bytes 131104 | tf_op jit(solution)/shard_map/ppermute | solution.py:405
  80.2 1.0 %gather_halves.1 = (bf16[1024,256]{1,0:T(8,128)(2,1)}, f32[256,256]{1,0:T(8,128)}) custom-call(bf16[1024,128]{1,0:T(8,128)(2,1)S(1)} %get-tuple-element.31.own_ref, bf16[1024,128]{1,0:T(8,128)(2,1)S(1)} %collective-permute-done.18.refs_3_.one_ref, bf16[1024,128]{1,0:T(8,128)(2,1)S(1)} %collective-permute-done.19.refs_4_.two_ref, ...), custom_call_target="tpu_custom_call" | custom-call | tf_op jit(solution)/shard_map/gather_halves/pallas_call | solution.py:349
  81.2 3.1 %collective-permute-done.25.two_ref = bf16[1024,128]{1,0:T(8,128)(2,1)S(1)} collective-permute-done((bf16[1024,128]{1,0:T(8,128)(2,1)S(1)}, bf16[1024,128]{1,0:T(8,128)(2,1)S(1)}, u32[]{:S(2)}, u32[]{:S(2)}) %collective-permute-start.25) | collective-permute-done | bytes 262176 | tf_op jit(solution)/shard_map/ppermute | solution.py:405
  84.3 1.1 %final.1 = bf16[1024,256]{1,0:T(8,128)(2,1)} custom-call(bf16[1024,128]{1,0:T(8,128)(2,1)S(1)} %add_after.6.refs_2_.own_ref, bf16[1024,128]{1,0:T(8,128)(2,1)S(1)} %collective-permute-done.24.one_ref, bf16[1024,128]{1,0:T(8,128)(2,1)S(1)} %collective-permute-done.25.two_ref, bf16[256,256]{1,0:T(8,128)(2,1)S(1)} %copy-done.2), custom_call_target="tpu_custom_call" | custom-call | flops 134217728 | bytes 2097152 | tf_op jit(solution)/shard_map/final/pallas_call | solution.py:383
  (31 shorter events, 1.1 us)
Async XLA Ops:
  0.6 17.7 %collective-permute-start = (bf16[5,8,128,128]{3,2,1,0:T(8,128)(2,1)}, bf16[5,8,128,128]{3,2,1,0:T(8,128)(2,1)S(1)}, u32[]{:S(2)}, u32[]{:S(2)}) collective-permute-start(bf16[5,8,128,128]{3,2,1,0:T(8,128)(2,1)} %bitcast.5), channel_id=1, source_target_pairs={{0,4},{1,0},{2,6},{3,2},{4,5},{5,1},{6,7},{7,3},{8,12},{9,8},{10,1... | collective-permute-start | bytes 3932168 | tf_op jit(solution)/shard_map/ppermute | solution.py:405
  3.9 9.5 %collective-permute-start.2 = (bf16[1024,128]{1,0:T(8,128)(2,1)S(1)}, bf16[1024,128]{1,0:T(8,128)(2,1)S(1)}, u32[]{:S(2)}, u32[]{:S(2)}) collective-permute-start(bf16[1024,128]{1,0:T(8,128)(2,1)S(1)} %get-tuple-element.36.refs_3_.refs_2_.refs_5_.refs_4_.refs_7_), channel_id=1, source_target_pairs={{0,8},{1,17},{2,10},{3,19},{5,13},{7,15},{8,0},{10,2},{12,28},{13,... | collective-permute-start | bytes 786440 | tf_op jit(solution)/shard_map/ppermute | solution.py:405
  4.6 8.9 %collective-permute-start.3 = (bf16[1024,128]{1,0:T(8,128)(2,1)S(1)}, bf16[1024,128]{1,0:T(8,128)(2,1)S(1)}, u32[]{:S(2)}, u32[]{:S(2)}) collective-permute-start(bf16[1024,128]{1,0:T(8,128)(2,1)S(1)} %get-tuple-element.35), channel_id=1, source_target_pairs={{0,12},{1,21},{2,14},{3,23},{5,9},{7,11},{8,4},{10,6},{12,24},{13,... | collective-permute-start | bytes 786440 | tf_op jit(solution)/shard_map/ppermute | solution.py:405
  5.9 7.6 %collective-permute-start.4 = (bf16[1024,128]{1,0:T(8,128)(2,1)S(1)}, bf16[1024,128]{1,0:T(8,128)(2,1)S(1)}, u32[]{:S(2)}, u32[]{:S(2)}) collective-permute-start(bf16[1024,128]{1,0:T(8,128)(2,1)S(1)} %get-tuple-element.35), channel_id=1, source_target_pairs={{0,4},{1,5},{2,6},{3,7},{4,0},{5,1},{6,2},{7,3},{8,12},{9,13},{10,... | collective-permute-start | bytes 786440 | tf_op jit(solution)/shard_map/ppermute | solution.py:405
  11.3 0.7 copy-start.3
  13.6 7.9 %collective-permute-start.5 = (bf16[1024,128]{1,0:T(8,128)(2,1)S(1)}, bf16[1024,128]{1,0:T(8,128)(2,1)S(1)}, u32[]{:S(2)}, u32[]{:S(2)}) collective-permute-start(bf16[1024,128]{1,0:T(8,128)(2,1)S(1)} %get-tuple-element.20), channel_id=1, source_target_pairs={{0,16},{1,17},{2,18},{3,19},{4,20},{5,21},{6,22},{7,23},{8,24},{9,... | collective-permute-start | bytes 786440 | tf_op jit(solution)/shard_map/ppermute | solution.py:405
  15.4 9.7 %copy-start = (bf16[1,5,8,128,128]{4,3,2,1,0:T(8,128)(2,1)S(1)}, bf16[1,5,8,128,128]{4,3,2,1,0:T(8,128)(2,1)}, u32[]{:S(2)}) copy-start(bf16[1,5,8,128,128]{4,3,2,1,0:T(8,128)(2,1)} %param.9) | copy-start | bytes 3932164
  15.4 7.6 %collective-permute-start.8 = (bf16[1024,128]{1,0:T(8,128)(2,1)S(1)}, bf16[1024,128]{1,0:T(8,128)(2,1)S(1)}, u32[]{:S(2)}, u32[]{:S(2)}) collective-permute-start(bf16[1024,128]{1,0:T(8,128)(2,1)S(1)} %get-tuple-element.24), channel_id=1, source_target_pairs={{0,8},{1,9},{2,10},{3,11},{4,12},{5,13},{6,14},{7,15},{8,0},{9,1},... | collective-permute-start | bytes 786440 | tf_op jit(solution)/shard_map/ppermute | solution.py:405
  16.6 1.7 %collective-permute-start.1 = (s32[2,40]{1,0:T(2,128)S(1)}, s32[2,40]{1,0:T(2,128)S(1)}, u32[]{:S(2)}, u32[]{:S(2)}) collective-permute-start(s32[2,40]{1,0:T(2,128)S(1)} %slot_blocks.1.refs_6_.refs_0_.refs_1_), channel_id=1, source_target_pairs={{0,4},{1,0},{2,6},{3,2},{4,5},{5,1},{6,7},{7,3},{8,12},{9,8},{10,1... | collective-permute-start | bytes 968 | tf_op jit(solution)/shard_map/ppermute | solution.py:405
  18.3 6.7 %collective-permute-start.7 = (bf16[5,8,128,128]{3,2,1,0:T(8,128)(2,1)S(1)}, bf16[5,8,128,128]{3,2,1,0:T(8,128)(2,1)S(1)}, u32[]{:S(2)}, u32[]{:S(2)}) collective-permute-start(bf16[5,8,128,128]{3,2,1,0:T(8,128)(2,1)S(1)} %collective-permute-done.refs_1_.refs_3_), channel_id=1, source_target_pairs={{0,4},{2,6},{5,1},{7,3},{8,12},{10,14},{13,9},{15,11},{16,20},{18,... | collective-permute-start | bytes 3932168 | tf_op jit(solution)/shard_map/ppermute | solution.py:405
  21.5 3.6 %collective-permute-start.6 = (s32[2,40]{1,0:T(2,128)S(1)}, s32[2,40]{1,0:T(2,128)S(1)}, u32[]{:S(2)}, u32[]{:S(2)}) collective-permute-start(s32[2,40]{1,0:T(2,128)S(1)} %collective-permute-done.1.refs_0_), channel_id=1, source_target_pairs={{0,4},{2,6},{5,1},{7,3},{8,12},{10,14},{13,9},{15,11},{16,20},{18,... | collective-permute-start | bytes 968 | tf_op jit(solution)/shard_map/ppermute | solution.py:405
  24.3 4.6 %copy-start.1 = (bf16[1024,256]{1,0:T(8,128)(2,1)S(1)}, bf16[1024,256]{1,0:T(8,128)(2,1)}, u32[]{:S(2)}) copy-start(bf16[1024,256]{1,0:T(8,128)(2,1)} %x_ref.1) | copy-start | bytes 1572868
  26.5 16.6 %copy-start.2 = (bf16[256,256]{1,0:T(8,128)(2,1)S(1)}, bf16[256,256]{1,0:T(8,128)(2,1)}, u32[]{:S(2)}) copy-start(bf16[256,256]{1,0:T(8,128)(2,1)} %w_ref.3) | copy-start | bytes 393220
  26.5 14.1 %collective-permute-start.9 = (bf16[1024,128]{1,0:T(8,128)(2,1)S(1)}, bf16[1024,128]{1,0:T(8,128)(2,1)S(1)}, u32[]{:S(2)}, u32[]{:S(2)}) collective-permute-start(bf16[1024,128]{1,0:T(8,128)(2,1)S(1)} %tile_product.5), channel_id=1, source_target_pairs={{0,2},{1,3},{2,0},{3,1},{4,6},{5,7},{6,4},{7,5},{8,10},{9,11},{10,... | collective-permute-start | bytes 786440 | tf_op jit(solution)/shard_map/ppermute | solution.py:405
  29.0 13.0 %collective-permute-start.11 = (bf16[1024,128]{1,0:T(8,128)(2,1)S(1)}, bf16[1024,128]{1,0:T(8,128)(2,1)S(1)}, u32[]{:S(2)}, u32[]{:S(2)}) collective-permute-start(bf16[1024,128]{1,0:T(8,128)(2,1)S(1)} %get-tuple-element.26), channel_id=1, source_target_pairs={{0,4},{1,5},{2,6},{3,7},{4,0},{5,1},{6,2},{7,3},{8,12},{9,13},{10,... | collective-permute-start | bytes 786440 | tf_op jit(solution)/shard_map/ppermute | solution.py:405
  40.7 2.4 %collective-permute-start.10 = (bf16[1024,128]{1,0:T(8,128)(2,1)S(1)}, bf16[1024,128]{1,0:T(8,128)(2,1)S(1)}, u32[]{:S(2)}, u32[]{:S(2)}) collective-permute-start(bf16[1024,128]{1,0:T(8,128)(2,1)S(1)} %add_convert_fusion.near_ref), channel_id=1, source_target_pairs={{0,4},{1,5},{2,6},{3,7},{4,0},{5,1},{6,2},{7,3},{8,12},{9,13},{10,... | collective-permute-start | bytes 786440 | tf_op jit(solution)/shard_map/ppermute | solution.py:405
  43.5 9.2 %collective-permute-start.14 = (bf16[1056,128]{1,0:T(8,128)(2,1)S(1)}, bf16[1056,128]{1,0:T(8,128)(2,1)S(1)}, u32[]{:S(2)}, u32[]{:S(2)}) collective-permute-start(bf16[1056,128]{1,0:T(8,128)(2,1)S(1)} %get-tuple-element.29), channel_id=1, source_target_pairs={{0,17},{1,0},{2,19},{3,2},{4,21},{5,4},{6,23},{7,6},{8,9},{9,24},{... | collective-permute-start | bytes 811016 | tf_op jit(solution)/shard_map/ppermute | solution.py:405
  45.2 7.3 %collective-permute-start.12 = (bf16[1040,128]{1,0:T(8,128)(2,1)S(1)}, bf16[1040,128]{1,0:T(8,128)(2,1)S(1)}, u32[]{:S(2)}, u32[]{:S(2)}) collective-permute-start(bf16[1040,128]{1,0:T(8,128)(2,1)S(1)} %get-tuple-element.28), channel_id=1, source_target_pairs={{0,8},{1,9},{2,10},{3,11},{4,12},{5,13},{6,14},{7,15},{8,0},{9,1},... | collective-permute-start | bytes 798728 | tf_op jit(solution)/shard_map/ppermute | solution.py:405
  45.4 12.4 %collective-permute-start.16 = (bf16[1024,128]{1,0:T(8,128)(2,1)S(1)}, bf16[1024,128]{1,0:T(8,128)(2,1)S(1)}, u32[]{:S(2)}, u32[]{:S(2)}) collective-permute-start(bf16[1024,128]{1,0:T(8,128)(2,1)S(1)} %get-tuple-element.30.refs_6_.adj_ref), channel_id=1, source_target_pairs={{0,1},{2,3},{4,5},{6,7},{9,8},{11,10},{13,12},{15,14},{16,17},{18,... | collective-permute-start | bytes 786440 | tf_op jit(solution)/shard_map/ppermute | solution.py:405
  52.5 6.4 %collective-permute-start.13 = (bf16[1040,128]{1,0:T(8,128)(2,1)S(1)}, bf16[1040,128]{1,0:T(8,128)(2,1)S(1)}, u32[]{:S(2)}, u32[]{:S(2)}) collective-permute-start(bf16[1040,128]{1,0:T(8,128)(2,1)S(1)} %collective-permute-done.12.refs_7_), channel_id=1, source_target_pairs={{0,16},{1,17},{2,18},{3,19},{4,20},{5,21},{6,22},{7,23},{8,24},{9,... | collective-permute-start | bytes 798728 | tf_op jit(solution)/shard_map/ppermute | solution.py:405
  52.7 6.3 %collective-permute-start.15 = (bf16[1056,128]{1,0:T(8,128)(2,1)S(1)}, bf16[1056,128]{1,0:T(8,128)(2,1)S(1)}, u32[]{:S(2)}, u32[]{:S(2)}) collective-permute-start(bf16[1056,128]{1,0:T(8,128)(2,1)S(1)} %collective-permute-done.14.refs_8_), channel_id=1, source_target_pairs={{0,8},{1,9},{2,10},{3,11},{4,12},{5,13},{6,14},{7,15},{8,0},{9,1},... | collective-permute-start | bytes 811016 | tf_op jit(solution)/shard_map/ppermute | solution.py:405
  54.2 3.5 %collective-permute-start.17 = (bf16[256,128]{1,0:T(8,128)(2,1)S(1)}, bf16[256,128]{1,0:T(8,128)(2,1)S(1)}, u32[]{:S(2)}, u32[]{:S(2)}) collective-permute-start(bf16[256,128]{1,0:T(8,128)(2,1)S(1)} %grad_block.1.refs_0_), channel_id=1, source_target_pairs={{0,1},{1,0},{2,3},{3,2},{4,5},{5,4},{6,7},{7,6},{8,9},{9,8},{10,11... | collective-permute-start | bytes 196616 | tf_op jit(solution)/shard_map/ppermute | solution.py:405
  60.5 14.6 %collective-permute-start.22 = (bf16[1024,128]{1,0:T(8,128)(2,1)S(1)}, bf16[1024,128]{1,0:T(8,128)(2,1)S(1)}, u32[]{:S(2)}, u32[]{:S(2)}) collective-permute-start(bf16[1024,128]{1,0:T(8,128)(2,1)S(1)} %tile_product.7.refs_2_.refs_0_), channel_id=1, source_target_pairs={{0,2},{1,3},{2,0},{3,1},{4,6},{5,7},{6,4},{7,5},{8,10},{9,11},{10,... | collective-permute-start | bytes 786440 | tf_op jit(solution)/shard_map/ppermute | solution.py:405
  63.5 6.0 %collective-permute-start.20 = (bf16[256,128]{1,0:T(8,128)(2,1)S(1)}, bf16[256,128]{1,0:T(8,128)(2,1)S(1)}, u32[]{:S(2)}, u32[]{:S(2)}) collective-permute-start(bf16[256,128]{1,0:T(8,128)(2,1)S(1)} %add_after.4.refs_0_), channel_id=1, source_target_pairs={{0,8},{1,9},{2,10},{3,11},{4,12},{5,13},{6,14},{7,15},{8,0},{9,1},... | collective-permute-start | bytes 196616 | tf_op jit(solution)/shard_map/ppermute | solution.py:405
  64.2 14.5 %collective-permute-start.18 = (bf16[1024,128]{1,0:T(8,128)(2,1)S(1)}, bf16[1024,128]{1,0:T(8,128)(2,1)S(1)}, u32[]{:S(2)}, u32[]{:S(2)}) collective-permute-start(bf16[1024,128]{1,0:T(8,128)(2,1)S(1)} %get-tuple-element.31.own_ref), channel_id=1, source_target_pairs={{0,1},{1,5},{2,3},{3,7},{4,0},{5,4},{6,2},{7,6},{8,9},{9,13},{10,1... | collective-permute-start | bytes 786440 | tf_op jit(solution)/shard_map/ppermute | solution.py:405
  67.0 11.7 %collective-permute-start.19 = (bf16[1024,128]{1,0:T(8,128)(2,1)S(1)}, bf16[1024,128]{1,0:T(8,128)(2,1)S(1)}, u32[]{:S(2)}, u32[]{:S(2)}) collective-permute-start(bf16[1024,128]{1,0:T(8,128)(2,1)S(1)} %get-tuple-element.31.own_ref), channel_id=1, source_target_pairs={{1,4},{3,6},{4,1},{6,3},{9,12},{11,14},{12,9},{14,11},{17,20},{19,... | collective-permute-start | bytes 786440 | tf_op jit(solution)/shard_map/ppermute | solution.py:405
  69.5 3.5 %collective-permute-start.21 = (bf16[256,128]{1,0:T(8,128)(2,1)S(1)}, bf16[256,128]{1,0:T(8,128)(2,1)S(1)}, u32[]{:S(2)}, u32[]{:S(2)}) collective-permute-start(bf16[256,128]{1,0:T(8,128)(2,1)S(1)} %add_after.5.refs_0_), channel_id=1, source_target_pairs={{0,16},{1,17},{2,18},{3,19},{4,20},{5,21},{6,22},{7,23},{8,24},{9,... | collective-permute-start | bytes 196616 | tf_op jit(solution)/shard_map/ppermute | solution.py:405
  75.1 6.1 %collective-permute-start.24 = (bf16[1024,128]{1,0:T(8,128)(2,1)S(1)}, bf16[1024,128]{1,0:T(8,128)(2,1)S(1)}, u32[]{:S(2)}, u32[]{:S(2)}) collective-permute-start(bf16[1024,128]{1,0:T(8,128)(2,1)S(1)} %add_after.6.refs_2_.own_ref), channel_id=1, source_target_pairs={{0,1},{1,5},{2,3},{3,7},{4,0},{5,4},{6,2},{7,6},{8,9},{9,13},{10,1... | collective-permute-start | bytes 786440 | tf_op jit(solution)/shard_map/ppermute | solution.py:405
  76.6 7.7 %collective-permute-start.25 = (bf16[1024,128]{1,0:T(8,128)(2,1)S(1)}, bf16[1024,128]{1,0:T(8,128)(2,1)S(1)}, u32[]{:S(2)}, u32[]{:S(2)}) collective-permute-start(bf16[1024,128]{1,0:T(8,128)(2,1)S(1)} %add_after.6.refs_2_.own_ref), channel_id=1, source_target_pairs={{1,4},{3,6},{4,1},{6,3},{9,12},{11,14},{12,9},{14,11},{17,20},{19,... | collective-permute-start | bytes 786440 | tf_op jit(solution)/shard_map/ppermute | solution.py:405
  78.8 1.4 %collective-permute-start.23 = (f32[256,128]{1,0:T(8,128)S(1)}, f32[256,128]{1,0:T(8,128)S(1)}, u32[]{:S(2)}, u32[]{:S(2)}) collective-permute-start(f32[256,128]{1,0:T(8,128)S(1)} %add_after.7.grad_ref), channel_id=1, source_target_pairs={{0,4},{1,5},{2,6},{3,7},{4,0},{5,1},{6,2},{7,3},{8,12},{9,13},{10,... | collective-permute-start | bytes 393224 | tf_op jit(solution)/shard_map/ppermute | solution.py:405

commit v22 on v18

--- a/solution.py
+++ b/solution.py
@@ -517,8 +517,6 @@
         two = send(value, lambda c, j, z: None if j == z % 2 else (c, 1 - j, z ^ 1))
         return one, two
 
-    act_later, back_part = lax.optimization_barrier((act, back_part))
-    act_parts = [act, *deliver(act_later)]
     grad = add_after([grad, grad_got], jnp.bfloat16, back_part)
     step = 1
     while step < shape[0]:
@@ -526,6 +524,9 @@
         step *= 2
         if step < shape[0]:
             grad = add_after([grad, got], jnp.bfloat16)
+        if step == 2:
+            act_later, grad = lax.optimization_barrier((act, grad))
+    act_parts = [act, *deliver(act_later)]
     back = add_after([back_part, send(back_part, across)], jnp.bfloat16, got)
     back_parts = [back, *deliver(back)]
     grad = add_after([grad, got], jnp.float32, back, *act_parts[1:])

time: 85.8 us -> 87.4 us (1.019)
  no operation moved by 1% of the time
where the time goes in v22:
time: 87.4 us; the launch traced here: 87.1 us
  starting transfers between devices  41.4 us (47%)
  waiting for transfers between devices  32.5 us (37%)
  Pallas kernels  9.86 us (11%)
  local copies, waits for them, and re-layouts  2.43 us (3%)
    ppermute x26, starting transfers between devices, send(): return lax.ppermute(value, AXES, route(shape, move))  41.4 us
    ppermute x26, waiting for transfers between devices, send(): return lax.ppermute(value, AXES, route(shape, move))  32.5 us
    pallas_call x4, Pallas kernels, tile_product(): pl.pallas_call(functools.partial(tile_kernel, kinds, cases, [[case for ca...  5.31 us
  transfers between devices with their start and end apart: 26, of which 15 were waited for; matrix products, arithmetic and copies ran while one was open for 2% of the time, Pallas kernels for 6%

profile of v22, /device:TPU:1, one launch (start us, length us, event | category | flops | bytes accessed | tf_op | source)
XLA Modules:
  0.0 87.1 jit_solution(16526442644769774541)
XLA Ops:
  0.6 2.2 %collective-permute-start = (bf16[5,8,128,128]{3,2,1,0:T(8,128)(2,1)}, bf16[5,8,128,128]{3,2,1,0:T(8,128)(2,1)S(1)}, u32[]{:S(2)}, u32[]{:S(2)}) collective-permute-start(bf16[5,8,128,128]{3,2,1,0:T(8,128)(2,1)} %bitcast.5), channel_id=1, source_target_pairs={{0,4},{1,0},{2,6},{3,2},{4,5},{5,1},{6,7},{7,3},{8,12},{9,8},{10,1... | collective-permute-start | bytes 3932168 | tf_op jit(solution)/shard_map/ppermute | solution.py:405
  2.8 1.1 %constant_dynamic-slice_fusion = (bf16[1024,128]{1,0:T(8,128)(2,1)S(1)}, bf16[1024,128]{1,0:T(8,128)(2,1)S(1)}) fusion(bf16[1024,256]{1,0:T(8,128)(2,1)} %param.6, s32[]{:T(128)S(6)} %select_n.15, s32[]{:T(128)S(6)} %select_n.14), kind=kLoop, calls=%fused_computation.2 | loop fusion | bytes 1048584 | tf_op jit(solution)/shard_map/dynamic_slice | solution.py:445
  3.9 0.7 collective-permute-start.2
  4.6 1.3 %collective-permute-start.3 = (bf16[1024,128]{1,0:T(8,128)(2,1)S(1)}, bf16[1024,128]{1,0:T(8,128)(2,1)S(1)}, u32[]{:S(2)}, u32[]{:S(2)}) collective-permute-start(bf16[1024,128]{1,0:T(8,128)(2,1)S(1)} %get-tuple-element.35), channel_id=1, source_target_pairs={{0,12},{1,21},{2,14},{3,23},{5,9},{7,11},{8,4},{10,6},{12,24},{13,... | collective-permute-start | bytes 786440 | tf_op jit(solution)/shard_map/ppermute | solution.py:405
  5.9 4.8 %collective-permute-start.4 = (bf16[1024,128]{1,0:T(8,128)(2,1)S(1)}, bf16[1024,128]{1,0:T(8,128)(2,1)S(1)}, u32[]{:S(2)}, u32[]{:S(2)}) collective-permute-start(bf16[1024,128]{1,0:T(8,128)(2,1)S(1)} %get-tuple-element.35), channel_id=1, source_target_pairs={{0,4},{1,5},{2,6},{3,7},{4,0},{5,1},{6,2},{7,3},{8,12},{9,13},{10,... | collective-permute-start | bytes 786440 | tf_op jit(solution)/shard_map/ppermute | solution.py:405
  10.6 0.7 copy.12
  11.3 0.7 copy-done.3
  12.0 1.3 %slot_blocks.1.refs_6_.refs_0_.refs_1_ = s32[2,40]{1,0:T(2,128)S(1)} custom-call(s32[2,5,8]{2,1,0:T(8,128)S(1)} %copy.10.coords_ref, s32[5]{0:T(128)S(1)} %bitcast.9), custom_call_target="tpu_custom_call" | custom-call | tf_op jit(solution)/shard_map/slot_blocks/pallas_call | solution.py:135
  13.6 1.8 %collective-permute-start.5 = (bf16[1024,128]{1,0:T(8,128)(2,1)S(1)}, bf16[1024,128]{1,0:T(8,128)(2,1)S(1)}, u32[]{:S(2)}, u32[]{:S(2)}) collective-permute-start(bf16[1024,128]{1,0:T(8,128)(2,1)S(1)} %get-tuple-element.20), channel_id=1, source_target_pairs={{0,16},{1,17},{2,18},{3,19},{4,20},{5,21},{6,22},{7,23},{8,24},{9,... | collective-permute-start | bytes 786440 | tf_op jit(solution)/shard_map/ppermute | solution.py:405
  15.4 1.2 %collective-permute-start.8 = (bf16[1024,128]{1,0:T(8,128)(2,1)S(1)}, bf16[1024,128]{1,0:T(8,128)(2,1)S(1)}, u32[]{:S(2)}, u32[]{:S(2)}) collective-permute-start(bf16[1024,128]{1,0:T(8,128)(2,1)S(1)} %get-tuple-element.24), channel_id=1, source_target_pairs={{0,8},{1,9},{2,10},{3,11},{4,12},{5,13},{6,14},{7,15},{8,0},{9,1},... | collective-permute-start | bytes 786440 | tf_op jit(solution)/shard_map/ppermute | solution.py:405
  16.8 1.5 %collective-permute-done.1.refs_0_ = s32[2,40]{1,0:T(2,128)S(1)} collective-permute-done((s32[2,40]{1,0:T(2,128)S(1)}, s32[2,40]{1,0:T(2,128)S(1)}, u32[]{:S(2)}, u32[]{:S(2)}) %collective-permute-start.1) | collective-permute-done | bytes 352 | tf_op jit(solution)/shard_map/ppermute | solution.py:405
  18.3 1.3 %collective-permute-start.7 = (bf16[5,8,128,128]{3,2,1,0:T(8,128)(2,1)S(1)}, bf16[5,8,128,128]{3,2,1,0:T(8,128)(2,1)S(1)}, u32[]{:S(2)}, u32[]{:S(2)}) collective-permute-start(bf16[5,8,128,128]{3,2,1,0:T(8,128)(2,1)S(1)} %collective-permute-done.refs_1_.refs_3_), channel_id=1, source_target_pairs={{0,4},{2,6},{5,1},{7,3},{8,12},{10,14},{13,9},{15,11},{16,20},{18,... | collective-permute-start | bytes 3932168 | tf_op jit(solution)/shard_map/ppermute | solution.py:405
  19.6 1.9 %collective-permute-done.5.refs_8_.refs_10_ = bf16[1024,128]{1,0:T(8,128)(2,1)S(1)} collective-permute-done((bf16[1024,128]{1,0:T(8,128)(2,1)S(1)}, bf16[1024,128]{1,0:T(8,128)(2,1)S(1)}, u32[]{:S(2)}, u32[]{:S(2)}) %collective-permute-start.5) | collective-permute-done | bytes 262176 | tf_op jit(solution)/shard_map/ppermute | solution.py:405
  21.5 1.3 %collective-permute-start.6 = (s32[2,40]{1,0:T(2,128)S(1)}, s32[2,40]{1,0:T(2,128)S(1)}, u32[]{:S(2)}, u32[]{:S(2)}) collective-permute-start(s32[2,40]{1,0:T(2,128)S(1)} %collective-permute-done.1.refs_0_), channel_id=1, source_target_pairs={{0,4},{2,6},{5,1},{7,3},{8,12},{10,14},{13,9},{15,11},{16,20},{18,... | collective-permute-start | bytes 968 | tf_op jit(solution)/shard_map/ppermute | solution.py:405
  22.8 0.3 collective-permute-done.8.refs_9_.refs_11_
  23.0 1.2 %tile_product.4.refs_12_ = f32[1024,128]{1,0:T(8,128)S(1)} custom-call(s32[2,40]{1,0:T(2,128)S(1)} %collective-permute-done.1.refs_0_, bf16[5,8,128,128]{3,2,1,0:T(8,128)(2,1)S(1)} %collective-permute-done.refs_1_.refs_3_, bf16[1024,128]{1,0:T(8,128)(2,1)S(1)} %get-tuple-element.36.refs_3_.refs_2_.refs_5_.refs_4_.refs_7_, ...), custom_call_target="tpu_custom_call" | custom-call | flops 12582912000 | bytes 196608000 | tf_op jit(solution)/shard_map/tile_product/pallas_call | solution.py:210
  24.3 0.8 collective-permute-done.6.refs_1_.refs_2_
  25.0 1.4 %tile_product.5 = bf16[1024,128]{1,0:T(8,128)(2,1)S(1)} custom-call(s32[2,40]{1,0:T(2,128)S(1)} %slot_blocks.1.refs_6_.refs_0_.refs_1_, s32[2,40]{1,0:T(2,128)S(1)} %collective-permute-done.6.refs_1_.refs_2_, bf16[5,8,128,128]{3,2,1,0:T(8,128)(2,1)S(1)} %bitcast.6, bf16[5,8,128,128]{3,2,1,0:T(8,128)(2,1)S(1)} %collective-permute-done.7.refs_3_.refs_5_, ...), custom_call_target="tpu_custom_call" | custom-call | flops 167772160 | bytes 2621440 | tf_op jit(solution)/shard_map/tile_product/pallas_call | solution.py:210
  26.5 2.4 %collective-permute-start.9 = (bf16[1024,128]{1,0:T(8,128)(2,1)S(1)}, bf16[1024,128]{1,0:T(8,128)(2,1)S(1)}, u32[]{:S(2)}, u32[]{:S(2)}) collective-permute-start(bf16[1024,128]{1,0:T(8,128)(2,1)S(1)} %tile_product.5), channel_id=1, source_target_pairs={{0,2},{1,3},{2,0},{3,1},{4,6},{5,7},{6,4},{7,5},{8,10},{9,11},{10,... | collective-permute-start | bytes 786440 | tf_op jit(solution)/shard_map/ppermute | solution.py:405
  29.0 0.8 collective-permute-start.11
  29.7 10.9 %collective-permute-done.9 = bf16[1024,128]{1,0:T(8,128)(2,1)S(1)} collective-permute-done((bf16[1024,128]{1,0:T(8,128)(2,1)S(1)}, bf16[1024,128]{1,0:T(8,128)(2,1)S(1)}, u32[]{:S(2)}, u32[]{:S(2)}) %collective-permute-start.9) | collective-permute-done | bytes 262176 | tf_op jit(solution)/shard_map/ppermute | solution.py:405
  40.7 1.2 %collective-permute-start.10 = (bf16[1024,128]{1,0:T(8,128)(2,1)S(1)}, bf16[1024,128]{1,0:T(8,128)(2,1)S(1)}, u32[]{:S(2)}, u32[]{:S(2)}) collective-permute-start(bf16[1024,128]{1,0:T(8,128)(2,1)S(1)} %add_convert_fusion.near_ref), channel_id=1, source_target_pairs={{0,4},{1,5},{2,6},{3,7},{4,0},{5,1},{6,2},{7,3},{8,12},{9,13},{10,... | collective-permute-start | bytes 786440 | tf_op jit(solution)/shard_map/ppermute | solution.py:405
  41.9 1.2 %collective-permute-done.10.far_ref = bf16[1024,128]{1,0:T(8,128)(2,1)S(1)} collective-permute-done((bf16[1024,128]{1,0:T(8,128)(2,1)S(1)}, bf16[1024,128]{1,0:T(8,128)(2,1)S(1)}, u32[]{:S(2)}, u32[]{:S(2)}) %collective-permute-start.10) | collective-permute-done | bytes 262176 | tf_op jit(solution)/shard_map/ppermute | solution.py:405
  43.1 0.4 middle.1
  43.5 1.8 %collective-permute-start.13 = (bf16[1056,128]{1,0:T(8,128)(2,1)S(1)}, bf16[1056,128]{1,0:T(8,128)(2,1)S(1)}, u32[]{:S(2)}, u32[]{:S(2)}) collective-permute-start(bf16[1056,128]{1,0:T(8,128)(2,1)S(1)} %get-tuple-element.29), channel_id=1, source_target_pairs={{0,8},{1,9},{2,10},{3,11},{4,12},{5,13},{6,14},{7,15},{8,0},{9,1},... | collective-permute-start | bytes 811016 | tf_op jit(solution)/shard_map/ppermute | solution.py:405
  45.3 3.4 %collective-permute-start.17 = (bf16[1024,128]{1,0:T(8,128)(2,1)S(1)}, bf16[1024,128]{1,0:T(8,128)(2,1)S(1)}, u32[]{:S(2)}, u32[]{:S(2)}) collective-permute-start(bf16[1024,128]{1,0:T(8,128)(2,1)S(1)} %get-tuple-element.28.adj_ref.refs_6_), channel_id=1, source_target_pairs={{0,1},{2,3},{4,5},{6,7},{9,8},{11,10},{13,12},{15,14},{16,17},{18,... | collective-permute-start | bytes 786440 | tf_op jit(solution)/shard_map/ppermute | solution.py:405
  48.7 3.9 %collective-permute-done.15.refs_8_ = bf16[1040,128]{1,0:T(8,128)(2,1)S(1)} collective-permute-done((bf16[1040,128]{1,0:T(8,128)(2,1)S(1)}, bf16[1040,128]{1,0:T(8,128)(2,1)S(1)}, u32[]{:S(2)}, u32[]{:S(2)}) %collective-permute-start.15) | collective-permute-done | bytes 266272 | tf_op jit(solution)/shard_map/ppermute | solution.py:405
  52.6 1.3 %collective-permute-start.16 = (bf16[1040,128]{1,0:T(8,128)(2,1)S(1)}, bf16[1040,128]{1,0:T(8,128)(2,1)S(1)}, u32[]{:S(2)}, u32[]{:S(2)}) collective-permute-start(bf16[1040,128]{1,0:T(8,128)(2,1)S(1)} %collective-permute-done.15.refs_8_), channel_id=1, source_target_pairs={{0,8},{1,9},{2,10},{3,11},{4,12},{5,13},{6,14},{7,15},{8,0},{9,1},... | collective-permute-start | bytes 798728 | tf_op jit(solution)/shard_map/ppermute | solution.py:405
  53.9 0.9 %collective-permute-start.14 = (bf16[1056,128]{1,0:T(8,128)(2,1)S(1)}, bf16[1056,128]{1,0:T(8,128)(2,1)S(1)}, u32[]{:S(2)}, u32[]{:S(2)}) collective-permute-start(bf16[1056,128]{1,0:T(8,128)(2,1)S(1)} %collective-permute-done.13.refs_7_), channel_id=1, source_target_pairs={{0,16},{1,17},{2,18},{3,19},{4,20},{5,21},{6,22},{7,23},{8,24},{9,... | collective-permute-start | bytes 811016 | tf_op jit(solution)/shard_map/ppermute | solution.py:405
  54.8 0.3 grad_block.1.refs_0_
  55.2 1.2 %tile_product.6.refs_10_ = f32[1024,128]{1,0:T(8,128)S(1)} custom-call(s32[2,40]{1,0:T(2,128)S(1)} %collective-permute-done.1.refs_0_, s32[2,40]{1,0:T(2,128)S(1)} %slot_blocks.1.refs_6_.refs_0_.refs_1_, s32[2,40]{1,0:T(2,128)S(1)} %collective-permute-done.6.refs_1_.refs_2_, bf16[5,8,128,128]{3,2,1,0:T(8,128)(2,1)S(1)} %collective-permute-done.refs_1_.refs_3_, ...), custom_call_target="tpu_custom_call" | custom-call | flops 134217728 | bytes 1572864 | tf_op jit(solution)/shard_map/tile_product/pallas_call | solution.py:210
  56.4 2.2 %collective-permute-done.12.refs_11_.refs_1_ = bf16[256,128]{1,0:T(8,128)(2,1)S(1)} collective-permute-done((bf16[256,128]{1,0:T(8,128)(2,1)S(1)}, bf16[256,128]{1,0:T(8,128)(2,1)S(1)}, u32[]{:S(2)}, u32[]{:S(2)}) %collective-permute-start.12) | collective-permute-done | bytes 65568 | tf_op jit(solution)/shard_map/ppermute | solution.py:405
  58.6 0.3 collective-permute-done.16.refs_7_
  58.9 0.6 collective-permute-done.14.refs_6_
  59.6 1.5 %tile_product.7.refs_2_.refs_0_ = bf16[1024,128]{1,0:T(8,128)(2,1)S(1)} custom-call(s32[2,40]{1,0:T(2,128)S(1)} %collective-permute-done.1.refs_0_, s32[2,40]{1,0:T(2,128)S(1)} %slot_blocks.1.refs_6_.refs_0_.refs_1_, s32[2,40]{1,0:T(2,128)S(1)} %collective-permute-done.6.refs_1_.refs_2_, bf16[5,8,128,128]{3,2,1,0:T(8,128)(2,1)S(1)} %collective-permute-done.refs_1_.refs_3_, ...), custom_call_target="tpu_custom_call" | custom-call | flops 201326592 | bytes 2359296 | tf_op jit(solution)/shard_map/tile_product/pallas_call | solution.py:210
  61.1 2.1 %collective-permute-start.22 = (bf16[1024,128]{1,0:T(8,128)(2,1)S(1)}, bf16[1024,128]{1,0:T(8,128)(2,1)S(1)}, u32[]{:S(2)}, u32[]{:S(2)}) collective-permute-start(bf16[1024,128]{1,0:T(8,128)(2,1)S(1)} %tile_product.7.refs_2_.refs_0_), channel_id=1, source_target_pairs={{0,2},{1,3},{2,0},{3,1},{4,6},{5,7},{6,4},{7,5},{8,10},{9,11},{10,... | collective-permute-start | bytes 786440 | tf_op jit(solution)/shard_map/ppermute | solution.py:405
  63.2 0.3 collective-permute-start.18
  63.6 2.8 %collective-permute-done.18.refs_1_ = bf16[256,128]{1,0:T(8,128)(2,1)S(1)} collective-permute-done((bf16[256,128]{1,0:T(8,128)(2,1)S(1)}, bf16[256,128]{1,0:T(8,128)(2,1)S(1)}, u32[]{:S(2)}, u32[]{:S(2)}) %collective-permute-start.18) | collective-permute-done | bytes 65568 | tf_op jit(solution)/shard_map/ppermute | solution.py:405
  66.4 4.7 %collective-permute-start.19 = (bf16[1024,128]{1,0:T(8,128)(2,1)S(1)}, bf16[1024,128]{1,0:T(8,128)(2,1)S(1)}, u32[]{:S(2)}, u32[]{:S(2)}) collective-permute-start(bf16[1024,128]{1,0:T(8,128)(2,1)S(1)} %get-tuple-element.31.own_ref), channel_id=1, source_target_pairs={{0,1},{1,5},{2,3},{3,7},{4,0},{5,4},{6,2},{7,6},{8,9},{9,13},{10,1... | collective-permute-start | bytes 786440 | tf_op jit(solution)/shard_map/ppermute | solution.py:405
  71.1 2.2 %collective-permute-start.20 = (bf16[1024,128]{1,0:T(8,128)(2,1)S(1)}, bf16[1024,128]{1,0:T(8,128)(2,1)S(1)}, u32[]{:S(2)}, u32[]{:S(2)}) collective-permute-start(bf16[1024,128]{1,0:T(8,128)(2,1)S(1)} %get-tuple-element.31.own_ref), channel_id=1, source_target_pairs={{1,4},{3,6},{4,1},{6,3},{9,12},{11,14},{12,9},{14,11},{17,20},{19,... | collective-permute-start | bytes 786440 | tf_op jit(solution)/shard_map/ppermute | solution.py:405
  73.3 1.1 %collective-permute-start.21 = (bf16[256,128]{1,0:T(8,128)(2,1)S(1)}, bf16[256,128]{1,0:T(8,128)(2,1)S(1)}, u32[]{:S(2)}, u32[]{:S(2)}) collective-permute-start(bf16[256,128]{1,0:T(8,128)(2,1)S(1)} %add_after.5.refs_0_), channel_id=1, source_target_pairs={{0,16},{1,17},{2,18},{3,19},{4,20},{5,21},{6,22},{7,23},{8,24},{9,... | collective-permute-start | bytes 196616 | tf_op jit(solution)/shard_map/ppermute | solution.py:405
  74.4 2.4 %collective-permute-done.21.refs_2_.refs_1_ = bf16[256,128]{1,0:T(8,128)(2,1)S(1)} collective-permute-done((bf16[256,128]{1,0:T(8,128)(2,1)S(1)}, bf16[256,128]{1,0:T(8,128)(2,1)S(1)}, u32[]{:S(2)}, u32[]{:S(2)}) %collective-permute-start.21) | collective-permute-done | bytes 65568 | tf_op jit(solution)/shard_map/ppermute | solution.py:405
  76.9 0.4 collective-permute-start.24
  77.3 3.9 %collective-permute-start.25 = (bf16[1024,128]{1,0:T(8,128)(2,1)S(1)}, bf16[1024,128]{1,0:T(8,128)(2,1)S(1)}, u32[]{:S(2)}, u32[]{:S(2)}) collective-permute-start(bf16[1024,128]{1,0:T(8,128)(2,1)S(1)} %add_after.6.refs_2_.own_ref), channel_id=1, source_target_pairs={{1,4},{3,6},{4,1},{6,3},{9,12},{11,14},{12,9},{14,11},{17,20},{19,... | collective-permute-start | bytes 786440 | tf_op jit(solution)/shard_map/ppermute | solution.py:405
  81.3 1.3 %collective-permute-done.23.rest_ref = f32[256,128]{1,0:T(8,128)S(1)} collective-permute-done((f32[256,128]{1,0:T(8,128)S(1)}, f32[256,128]{1,0:T(8,128)S(1)}, u32[]{:S(2)}, u32[]{:S(2)}) %collective-permute-start.23) | collective-permute-done | bytes 131104 | tf_op jit(solution)/shard_map/ppermute | solution.py:405
  82.6 1.0 %gather_halves.1 = (bf16[1024,256]{1,0:T(8,128)(2,1)}, f32[256,256]{1,0:T(8,128)}) custom-call(bf16[1024,128]{1,0:T(8,128)(2,1)S(1)} %get-tuple-element.31.own_ref, bf16[1024,128]{1,0:T(8,128)(2,1)S(1)} %collective-permute-done.19.refs_3_.one_ref, bf16[1024,128]{1,0:T(8,128)(2,1)S(1)} %collective-permute-done.20.refs_4_.two_ref, ...), custom_call_target="tpu_custom_call" | custom-call | tf_op jit(solution)/shard_map/gather_halves/pallas_call | solution.py:349
  83.7 2.3 %collective-permute-done.25.two_ref = bf16[1024,128]{1,0:T(8,128)(2,1)S(1)} collective-permute-done((bf16[1024,128]{1,0:T(8,128)(2,1)S(1)}, bf16[1024,128]{1,0:T(8,128)(2,1)S(1)}, u32[]{:S(2)}, u32[]{:S(2)}) %collective-permute-start.25) | collective-permute-done | bytes 262176 | tf_op jit(solution)/shard_map/ppermute | solution.py:405
  85.9 1.1 %final.1 = bf16[1024,256]{1,0:T(8,128)(2,1)} custom-call(bf16[1024,128]{1,0:T(8,128)(2,1)S(1)} %add_after.6.refs_2_.own_ref, bf16[1024,128]{1,0:T(8,128)(2,1)S(1)} %collective-permute-done.24.one_ref, bf16[1024,128]{1,0:T(8,128)(2,1)S(1)} %collective-permute-done.25.two_ref, bf16[256,256]{1,0:T(8,128)(2,1)S(1)} %copy-done.2), custom_call_target="tpu_custom_call" | custom-call | flops 134217728 | bytes 2097152 | tf_op jit(solution)/shard_map/final/pallas_call | solution.py:383
  (31 shorter events, 0.9 us)
Async XLA Ops:
  0.6 17.7 %collective-permute-start = (bf16[5,8,128,128]{3,2,1,0:T(8,128)(2,1)}, bf16[5,8,128,128]{3,2,1,0:T(8,128)(2,1)S(1)}, u32[]{:S(2)}, u32[]{:S(2)}) collective-permute-start(bf16[5,8,128,128]{3,2,1,0:T(8,128)(2,1)} %bitcast.5), channel_id=1, source_target_pairs={{0,4},{1,0},{2,6},{3,2},{4,5},{5,1},{6,7},{7,3},{8,12},{9,8},{10,1... | collective-permute-start | bytes 3932168 | tf_op jit(solution)/shard_map/ppermute | solution.py:405
  3.9 9.5 %collective-permute-start.2 = (bf16[1024,128]{1,0:T(8,128)(2,1)S(1)}, bf16[1024,128]{1,0:T(8,128)(2,1)S(1)}, u32[]{:S(2)}, u32[]{:S(2)}) collective-permute-start(bf16[1024,128]{1,0:T(8,128)(2,1)S(1)} %get-tuple-element.36.refs_3_.refs_2_.refs_5_.refs_4_.refs_7_), channel_id=1, source_target_pairs={{0,8},{1,17},{2,10},{3,19},{5,13},{7,15},{8,0},{10,2},{12,28},{13,... | collective-permute-start | bytes 786440 | tf_op jit(solution)/shard_map/ppermute | solution.py:405
  4.6 8.9 %collective-permute-start.3 = (bf16[1024,128]{1,0:T(8,128)(2,1)S(1)}, bf16[1024,128]{1,0:T(8,128)(2,1)S(1)}, u32[]{:S(2)}, u32[]{:S(2)}) collective-permute-start(bf16[1024,128]{1,0:T(8,128)(2,1)S(1)} %get-tuple-element.35), channel_id=1, source_target_pairs={{0,12},{1,21},{2,14},{3,23},{5,9},{7,11},{8,4},{10,6},{12,24},{13,... | collective-permute-start | bytes 786440 | tf_op jit(solution)/shard_map/ppermute | solution.py:405
  5.9 7.6 %collective-permute-start.4 = (bf16[1024,128]{1,0:T(8,128)(2,1)S(1)}, bf16[1024,128]{1,0:T(8,128)(2,1)S(1)}, u32[]{:S(2)}, u32[]{:S(2)}) collective-permute-start(bf16[1024,128]{1,0:T(8,128)(2,1)S(1)} %get-tuple-element.35), channel_id=1, source_target_pairs={{0,4},{1,5},{2,6},{3,7},{4,0},{5,1},{6,2},{7,3},{8,12},{9,13},{10,... | collective-permute-start | bytes 786440 | tf_op jit(solution)/shard_map/ppermute | solution.py:405
  11.3 0.7 copy-start.3
  13.6 7.9 %collective-permute-start.5 = (bf16[1024,128]{1,0:T(8,128)(2,1)S(1)}, bf16[1024,128]{1,0:T(8,128)(2,1)S(1)}, u32[]{:S(2)}, u32[]{:S(2)}) collective-permute-start(bf16[1024,128]{1,0:T(8,128)(2,1)S(1)} %get-tuple-element.20), channel_id=1, source_target_pairs={{0,16},{1,17},{2,18},{3,19},{4,20},{5,21},{6,22},{7,23},{8,24},{9,... | collective-permute-start | bytes 786440 | tf_op jit(solution)/shard_map/ppermute | solution.py:405
  15.4 9.7 %copy-start = (bf16[1,5,8,128,128]{4,3,2,1,0:T(8,128)(2,1)S(1)}, bf16[1,5,8,128,128]{4,3,2,1,0:T(8,128)(2,1)}, u32[]{:S(2)}) copy-start(bf16[1,5,8,128,128]{4,3,2,1,0:T(8,128)(2,1)} %param.9) | copy-start | bytes 3932164
  15.4 7.6 %collective-permute-start.8 = (bf16[1024,128]{1,0:T(8,128)(2,1)S(1)}, bf16[1024,128]{1,0:T(8,128)(2,1)S(1)}, u32[]{:S(2)}, u32[]{:S(2)}) collective-permute-start(bf16[1024,128]{1,0:T(8,128)(2,1)S(1)} %get-tuple-element.24), channel_id=1, source_target_pairs={{0,8},{1,9},{2,10},{3,11},{4,12},{5,13},{6,14},{7,15},{8,0},{9,1},... | collective-permute-start | bytes 786440 | tf_op jit(solution)/shard_map/ppermute | solution.py:405
  16.6 1.7 %collective-permute-start.1 = (s32[2,40]{1,0:T(2,128)S(1)}, s32[2,40]{1,0:T(2,128)S(1)}, u32[]{:S(2)}, u32[]{:S(2)}) collective-permute-start(s32[2,40]{1,0:T(2,128)S(1)} %slot_blocks.1.refs_6_.refs_0_.refs_1_), channel_id=1, source_target_pairs={{0,4},{1,0},{2,6},{3,2},{4,5},{5,1},{6,7},{7,3},{8,12},{9,8},{10,1... | collective-permute-start | bytes 968 | tf_op jit(solution)/shard_map/ppermute | solution.py:405
  18.3 6.7 %collective-permute-start.7 = (bf16[5,8,128,128]{3,2,1,0:T(8,128)(2,1)S(1)}, bf16[5,8,128,128]{3,2,1,0:T(8,128)(2,1)S(1)}, u32[]{:S(2)}, u32[]{:S(2)}) collective-permute-start(bf16[5,8,128,128]{3,2,1,0:T(8,128)(2,1)S(1)} %collective-permute-done.refs_1_.refs_3_), channel_id=1, source_target_pairs={{0,4},{2,6},{5,1},{7,3},{8,12},{10,14},{13,9},{15,11},{16,20},{18,... | collective-permute-start | bytes 3932168 | tf_op jit(solution)/shard_map/ppermute | solution.py:405
  21.5 3.6 %collective-permute-start.6 = (s32[2,40]{1,0:T(2,128)S(1)}, s32[2,40]{1,0:T(2,128)S(1)}, u32[]{:S(2)}, u32[]{:S(2)}) collective-permute-start(s32[2,40]{1,0:T(2,128)S(1)} %collective-permute-done.1.refs_0_), channel_id=1, source_target_pairs={{0,4},{2,6},{5,1},{7,3},{8,12},{10,14},{13,9},{15,11},{16,20},{18,... | collective-permute-start | bytes 968 | tf_op jit(solution)/shard_map/ppermute | solution.py:405
  24.3 4.6 %copy-start.1 = (bf16[1024,256]{1,0:T(8,128)(2,1)S(1)}, bf16[1024,256]{1,0:T(8,128)(2,1)}, u32[]{:S(2)}) copy-start(bf16[1024,256]{1,0:T(8,128)(2,1)} %x_ref.1) | copy-start | bytes 1572868
  26.5 16.6 %copy-start.2 = (bf16[256,256]{1,0:T(8,128)(2,1)S(1)}, bf16[256,256]{1,0:T(8,128)(2,1)}, u32[]{:S(2)}) copy-start(bf16[256,256]{1,0:T(8,128)(2,1)} %w_ref.3) | copy-start | bytes 393220
  26.5 14.1 %collective-permute-start.9 = (bf16[1024,128]{1,0:T(8,128)(2,1)S(1)}, bf16[1024,128]{1,0:T(8,128)(2,1)S(1)}, u32[]{:S(2)}, u32[]{:S(2)}) collective-permute-start(bf16[1024,128]{1,0:T(8,128)(2,1)S(1)} %tile_product.5), channel_id=1, source_target_pairs={{0,2},{1,3},{2,0},{3,1},{4,6},{5,7},{6,4},{7,5},{8,10},{9,11},{10,... | collective-permute-start | bytes 786440 | tf_op jit(solution)/shard_map/ppermute | solution.py:405
  29.0 12.9 %collective-permute-start.11 = (bf16[1024,128]{1,0:T(8,128)(2,1)S(1)}, bf16[1024,128]{1,0:T(8,128)(2,1)S(1)}, u32[]{:S(2)}, u32[]{:S(2)}) collective-permute-start(bf16[1024,128]{1,0:T(8,128)(2,1)S(1)} %get-tuple-element.26), channel_id=1, source_target_pairs={{0,4},{1,5},{2,6},{3,7},{4,0},{5,1},{6,2},{7,3},{8,12},{9,13},{10,... | collective-permute-start | bytes 786440 | tf_op jit(solution)/shard_map/ppermute | solution.py:405
  40.7 2.4 %collective-permute-start.10 = (bf16[1024,128]{1,0:T(8,128)(2,1)S(1)}, bf16[1024,128]{1,0:T(8,128)(2,1)S(1)}, u32[]{:S(2)}, u32[]{:S(2)}) collective-permute-start(bf16[1024,128]{1,0:T(8,128)(2,1)S(1)} %add_convert_fusion.near_ref), channel_id=1, source_target_pairs={{0,4},{1,5},{2,6},{3,7},{4,0},{5,1},{6,2},{7,3},{8,12},{9,13},{10,... | collective-permute-start | bytes 786440 | tf_op jit(solution)/shard_map/ppermute | solution.py:405
  43.5 10.4 %collective-permute-start.13 = (bf16[1056,128]{1,0:T(8,128)(2,1)S(1)}, bf16[1056,128]{1,0:T(8,128)(2,1)S(1)}, u32[]{:S(2)}, u32[]{:S(2)}) collective-permute-start(bf16[1056,128]{1,0:T(8,128)(2,1)S(1)} %get-tuple-element.29), channel_id=1, source_target_pairs={{0,8},{1,9},{2,10},{3,11},{4,12},{5,13},{6,14},{7,15},{8,0},{9,1},... | collective-permute-start | bytes 811016 | tf_op jit(solution)/shard_map/ppermute | solution.py:405
  45.3 7.3 %collective-permute-start.15 = (bf16[1040,128]{1,0:T(8,128)(2,1)S(1)}, bf16[1040,128]{1,0:T(8,128)(2,1)S(1)}, u32[]{:S(2)}, u32[]{:S(2)}) collective-permute-start(bf16[1040,128]{1,0:T(8,128)(2,1)S(1)} %get-tuple-element.30), channel_id=1, source_target_pairs={{0,17},{1,0},{2,19},{3,2},{4,21},{5,4},{6,23},{7,6},{8,9},{9,24},{... | collective-permute-start | bytes 798728 | tf_op jit(solution)/shard_map/ppermute | solution.py:405
  45.3 13.3 %collective-permute-start.17 = (bf16[1024,128]{1,0:T(8,128)(2,1)S(1)}, bf16[1024,128]{1,0:T(8,128)(2,1)S(1)}, u32[]{:S(2)}, u32[]{:S(2)}) collective-permute-start(bf16[1024,128]{1,0:T(8,128)(2,1)S(1)} %get-tuple-element.28.adj_ref.refs_6_), channel_id=1, source_target_pairs={{0,1},{2,3},{4,5},{6,7},{9,8},{11,10},{13,12},{15,14},{16,17},{18,... | collective-permute-start | bytes 786440 | tf_op jit(solution)/shard_map/ppermute | solution.py:405
  52.6 6.3 %collective-permute-start.16 = (bf16[1040,128]{1,0:T(8,128)(2,1)S(1)}, bf16[1040,128]{1,0:T(8,128)(2,1)S(1)}, u32[]{:S(2)}, u32[]{:S(2)}) collective-permute-start(bf16[1040,128]{1,0:T(8,128)(2,1)S(1)} %collective-permute-done.15.refs_8_), channel_id=1, source_target_pairs={{0,8},{1,9},{2,10},{3,11},{4,12},{5,13},{6,14},{7,15},{8,0},{9,1},... | collective-permute-start | bytes 798728 | tf_op jit(solution)/shard_map/ppermute | solution.py:405
  53.9 5.7 %collective-permute-start.14 = (bf16[1056,128]{1,0:T(8,128)(2,1)S(1)}, bf16[1056,128]{1,0:T(8,128)(2,1)S(1)}, u32[]{:S(2)}, u32[]{:S(2)}) collective-permute-start(bf16[1056,128]{1,0:T(8,128)(2,1)S(1)} %collective-permute-done.13.refs_7_), channel_id=1, source_target_pairs={{0,16},{1,17},{2,18},{3,19},{4,20},{5,21},{6,22},{7,23},{8,24},{9,... | collective-permute-start | bytes 811016 | tf_op jit(solution)/shard_map/ppermute | solution.py:405
  55.1 3.5 %collective-permute-start.12 = (bf16[256,128]{1,0:T(8,128)(2,1)S(1)}, bf16[256,128]{1,0:T(8,128)(2,1)S(1)}, u32[]{:S(2)}, u32[]{:S(2)}) collective-permute-start(bf16[256,128]{1,0:T(8,128)(2,1)S(1)} %grad_block.1.refs_0_), channel_id=1, source_target_pairs={{0,1},{1,0},{2,3},{3,2},{4,5},{5,4},{6,7},{7,6},{8,9},{9,8},{10,11... | collective-permute-start | bytes 196616 | tf_op jit(solution)/shard_map/ppermute | solution.py:405
  61.1 15.7 %collective-permute-start.22 = (bf16[1024,128]{1,0:T(8,128)(2,1)S(1)}, bf16[1024,128]{1,0:T(8,128)(2,1)S(1)}, u32[]{:S(2)}, u32[]{:S(2)}) collective-permute-start(bf16[1024,128]{1,0:T(8,128)(2,1)S(1)} %tile_product.7.refs_2_.refs_0_), channel_id=1, source_target_pairs={{0,2},{1,3},{2,0},{3,1},{4,6},{5,7},{6,4},{7,5},{8,10},{9,11},{10,... | collective-permute-start | bytes 786440 | tf_op jit(solution)/shard_map/ppermute | solution.py:405
  63.2 3.2 %collective-permute-start.18 = (bf16[256,128]{1,0:T(8,128)(2,1)S(1)}, bf16[256,128]{1,0:T(8,128)(2,1)S(1)}, u32[]{:S(2)}, u32[]{:S(2)}) collective-permute-start(bf16[256,128]{1,0:T(8,128)(2,1)S(1)} %add_after.4.refs_0_), channel_id=1, source_target_pairs={{0,8},{1,9},{2,10},{3,11},{4,12},{5,13},{6,14},{7,15},{8,0},{9,1},... | collective-permute-start | bytes 196616 | tf_op jit(solution)/shard_map/ppermute | solution.py:405
  66.4 14.8 %collective-permute-start.19 = (bf16[1024,128]{1,0:T(8,128)(2,1)S(1)}, bf16[1024,128]{1,0:T(8,128)(2,1)S(1)}, u32[]{:S(2)}, u32[]{:S(2)}) collective-permute-start(bf16[1024,128]{1,0:T(8,128)(2,1)S(1)} %get-tuple-element.31.own_ref), channel_id=1, source_target_pairs={{0,1},{1,5},{2,3},{3,7},{4,0},{5,4},{6,2},{7,6},{8,9},{9,13},{10,1... | collective-permute-start | bytes 786440 | tf_op jit(solution)/shard_map/ppermute | solution.py:405
  71.1 10.1 %collective-permute-start.20 = (bf16[1024,128]{1,0:T(8,128)(2,1)S(1)}, bf16[1024,128]{1,0:T(8,128)(2,1)S(1)}, u32[]{:S(2)}, u32[]{:S(2)}) collective-permute-start(bf16[1024,128]{1,0:T(8,128)(2,1)S(1)} %get-tuple-element.31.own_ref), channel_id=1, source_target_pairs={{1,4},{3,6},{4,1},{6,3},{9,12},{11,14},{12,9},{14,11},{17,20},{19,... | collective-permute-start | bytes 786440 | tf_op jit(solution)/shard_map/ppermute | solution.py:405
  73.3 3.5 %collective-permute-start.21 = (bf16[256,128]{1,0:T(8,128)(2,1)S(1)}, bf16[256,128]{1,0:T(8,128)(2,1)S(1)}, u32[]{:S(2)}, u32[]{:S(2)}) collective-permute-start(bf16[256,128]{1,0:T(8,128)(2,1)S(1)} %add_after.5.refs_0_), channel_id=1, source_target_pairs={{0,16},{1,17},{2,18},{3,19},{4,20},{5,21},{6,22},{7,23},{8,24},{9,... | collective-permute-start | bytes 196616 | tf_op jit(solution)/shard_map/ppermute | solution.py:405
  76.9 6.8 %collective-permute-start.24 = (bf16[1024,128]{1,0:T(8,128)(2,1)S(1)}, bf16[1024,128]{1,0:T(8,128)(2,1)S(1)}, u32[]{:S(2)}, u32[]{:S(2)}) collective-permute-start(bf16[1024,128]{1,0:T(8,128)(2,1)S(1)} %add_after.6.refs_2_.own_ref), channel_id=1, source_target_pairs={{0,1},{1,5},{2,3},{3,7},{4,0},{5,4},{6,2},{7,6},{8,9},{9,13},{10,1... | collective-permute-start | bytes 786440 | tf_op jit(solution)/shard_map/ppermute | solution.py:405
  77.3 8.6 %collective-permute-start.25 = (bf16[1024,128]{1,0:T(8,128)(2,1)S(1)}, bf16[1024,128]{1,0:T(8,128)(2,1)S(1)}, u32[]{:S(2)}, u32[]{:S(2)}) collective-permute-start(bf16[1024,128]{1,0:T(8,128)(2,1)S(1)} %add_after.6.refs_2_.own_ref), channel_id=1, source_target_pairs={{1,4},{3,6},{4,1},{6,3},{9,12},{11,14},{12,9},{14,11},{17,20},{19,... | collective-permute-start | bytes 786440 | tf_op jit(solution)/shard_map/ppermute | solution.py:405
  81.2 1.4 %collective-permute-start.23 = (f32[256,128]{1,0:T(8,128)S(1)}, f32[256,128]{1,0:T(8,128)S(1)}, u32[]{:S(2)}, u32[]{:S(2)}) collective-permute-start(f32[256,128]{1,0:T(8,128)S(1)} %add_after.7.grad_ref), channel_id=1, source_target_pairs={{0,4},{1,5},{2,6},{3,7},{4,0},{5,1},{6,2},{7,3},{8,12},{9,13},{10,... | collective-permute-start | bytes 393224 | tf_op jit(solution)/shard_map/ppermute | solution.py:405
